TPU v7x, 32 devices: a whole 2x2x4 slice. The times are simulated.
32 devices in a mesh: sec: 2 (over y), dp: 4 (over x, core), tp: 4 (over z).
Axes of the slice: x: 2, y: 2, z: 4, core: 2. Of those that a mesh axis runs over, the one named last changes fastest.
Arguments:
- latents: bfloat16 [32, 64, 1280], P(('dp', 'tp')), may hold values from -6 to 6
- timesteps: int32 [32], P(('dp', 'tp')), may hold values from 0 to 24
- prompt_ids: int32 [32], P(('dp', 'tp')), may hold values from 0 to 63
- prompt_table: bfloat16 [64, 1280], replicated, may hold values from -6 to 6
- gains: float32 [2, 1280], replicated, may hold values from 0.5 to 1.5
- w_in: bfloat16 [2, 1280, 5120], P('sec', None, 'tp'), may hold values from -0.15625 to 0.15625
- w_out: bfloat16 [2, 1280, 5120], P('sec', None, 'tp'), may hold values from -0.078125 to 0.078125
Outputs:
- grad_in: float32 [1280, 5120], P(('sec', 'dp'), 'tp')
- grad_out: float32 [1280, 5120], P(('sec', 'dp'), 'tp')
All inputs are finite; a program needn't handle non-finite values.
Results may differ from a plain program's by a relative error of at most 0.03.
Values may be sent and summed in bfloat16 or wider, within the bound.
No kernel may reach another device: no remote copies, remote signals or barrier semaphores. Data moves between devices by JAX's collectives and lax.ppermute only.
A program may use at most 64 MiB of HBM per device.

v0:
```python
import math

import jax
import jax.numpy as jnp
from jax import lax
from jax.sharding import PartitionSpec as P

STEPS = 50


EPS = 1e-06


def shifted(value, axis, steps):
    count = lax.axis_size(axis)
    leading, last = (max(0, -steps), min(count, count - steps))
    return lax.ppermute(value, axis, [(source, source + steps) for source in range(leading, last)])


def gelu_slope(value):
    return 0.5 * (1.0 + lax.erf(value / math.sqrt(2.0))) + value * jnp.exp(
        -0.5 * value * value
    ) / math.sqrt(2.0 * math.pi)


def normed(rows, gain):
    scale = lax.rsqrt(jnp.mean(rows * rows, axis=-1, keepdims=True) + EPS)
    return ((rows * scale * gain).astype(jnp.bfloat16), scale)


def score_of(pooled, text):
    unit_img = pooled * lax.rsqrt(jnp.mean(pooled * pooled, axis=-1, keepdims=True) + EPS)
    unit_txt = text * lax.rsqrt(jnp.mean(text * text, axis=-1, keepdims=True) + EPS)
    return 100.0 * jnp.sum(unit_img * unit_txt, axis=-1) / pooled.shape[-1]


def collect(piece):
    return lax.all_gather(piece, "tp", axis=0, tiled=True)


def reduce_rows(term_fn, local_rows):
    return lax.psum_scatter(
        term_fn(jnp.int32(0), local_rows * lax.axis_size("tp")).astype(jnp.bfloat16),
        "tp",
        scatter_dimension=0,
        tiled=True,
    ).astype(jnp.float32)


def guarded(active, compute, empty):
    return lax.cond(active, compute, empty)


def forward(rows, gain, weight_in, weight_out, active):
    count, tokens, width = rows.shape
    hidden = weight_in.shape[1]
    local_rows = count * tokens
    whole = collect(rows).reshape(-1, width)
    total_rows = whole.shape[0]

    def compute():
        xn, unused = normed(whole.astype(jnp.float32), gain)
        hp = jnp.dot(xn, weight_in, preferred_element_type=jnp.float32)
        return (xn, hp, jax.nn.gelu(hp, approximate=False).astype(jnp.bfloat16))

    def skip():
        return (
            jnp.zeros((total_rows, width), jnp.bfloat16),
            jnp.zeros((total_rows, hidden), jnp.float32),
            jnp.zeros((total_rows, hidden), jnp.bfloat16),
        )

    xn, hp, act = guarded(active, compute, skip)

    def term(start, size):

        def term_product():
            return lax.dot_general(
                act, weight_out, (((1,), (1,)), ((), ())), preferred_element_type=jnp.float32
            )

        return guarded(active, term_product, lambda: jnp.zeros((size, width), jnp.float32))

    mixed = reduce_rows(term, local_rows)
    return (mixed.reshape(count, tokens, width), xn, hp, act)


def reward_back(arrived, mix1, hp1, ids, prompt_table, gain, weight_in, weight_out, active):
    count, tokens, width = arrived.shape
    hidden = weight_in.shape[1]
    local_rows = count * tokens
    seen = arrived.astype(jnp.float32)
    pooled = jnp.mean(seen + mix1, axis=1)
    onehot = (ids[:, None] == jnp.arange(prompt_table.shape[0], dtype=jnp.int32)[None, :]).astype(
        jnp.bfloat16
    )
    text = jnp.dot(onehot, prompt_table, preferred_element_type=jnp.float32)
    g_pooled = jax.grad(lambda p: -jnp.sum(score_of(p, text)))(pooled)
    g_mean = g_pooled / tokens
    all_tok = collect(g_mean.astype(jnp.bfloat16))
    total_rows = hp1.shape[0]

    def grad_hidden():
        g_h = jnp.dot(all_tok, weight_out, preferred_element_type=jnp.float32)
        slope = gelu_slope(hp1).reshape(-1, tokens, hidden)
        return (g_h[:, None, :] * slope).reshape(total_rows, hidden).astype(jnp.bfloat16)

    g_hp1 = guarded(active, grad_hidden, lambda: jnp.zeros((total_rows, hidden), jnp.bfloat16))

    def back_term(start, size):

        def back_product():
            return lax.dot_general(
                g_hp1, weight_in, (((1,), (1,)), ((), ())), preferred_element_type=jnp.float32
            )

        return guarded(active, back_product, lambda: jnp.zeros((size, width), jnp.float32))

    g_xn = reduce_rows(back_term, local_rows)
    flat_seen = seen.reshape(local_rows, width)
    scale1 = lax.rsqrt(jnp.mean(flat_seen * flat_seen, axis=-1, keepdims=True) + EPS)
    weighted = gain * g_xn
    g_norm = scale1 * weighted - flat_seen * scale1**3 * jnp.mean(
        flat_seen * weighted, axis=-1, keepdims=True
    )
    return (g_mean[:, None, :] + g_norm.reshape(count, tokens, width)).astype(jnp.bfloat16)


def weight_terms(g_all, xn0, hp0, act0, weight_out):
    contract_first = (((0,), (0,)), ((), ()))
    grad_w_out = lax.dot_general(g_all, act0, contract_first, preferred_element_type=jnp.float32)
    g_hp0 = (
        jnp.dot(g_all, weight_out, preferred_element_type=jnp.float32) * gelu_slope(hp0)
    ).astype(jnp.bfloat16)
    grad_w_in = lax.dot_general(xn0, g_hp0, contract_first, preferred_element_type=jnp.float32)
    return (grad_w_in, grad_w_out)


def on_device(latents, timesteps, prompt_ids, prompt_table, gains, w_in, w_out):
    count, tokens, width = latents.shape
    hidden = w_in.shape[2]
    segment = lax.axis_index("sec")
    diffusing = segment == 0
    scoring = segment == 1
    weight_in = w_in[0]
    weight_out = w_out[0]
    theta = math.pi / 2.0 * (timesteps.astype(jnp.float32) + 1.0) / (STEPS + 1.0)
    alpha = jnp.cos(theta)[:, None, None]
    sigma = jnp.sin(theta)[:, None, None]
    eps_mix, xn0, hp0, act0 = forward(latents, gains[0], weight_in, weight_out, diffusing)
    base = latents.astype(jnp.float32)
    images = ((base - sigma * (base + eps_mix)) / alpha).astype(jnp.bfloat16)
    arrived = shifted(images, "sec", 1)
    mix1, xn1, hp1, act1 = forward(arrived, gains[1], weight_in, weight_out, scoring)
    g_images = reward_back(
        arrived, mix1, hp1, prompt_ids, prompt_table, gains[1], weight_in, weight_out, scoring
    )
    returned = shifted(g_images, "sec", -1)
    g_eps = (-(sigma / alpha) * returned.astype(jnp.float32)).astype(jnp.bfloat16)
    g_all = collect(g_eps).reshape(-1, width)

    def no_terms():
        return (jnp.zeros((width, hidden), jnp.float32), jnp.zeros((width, hidden), jnp.float32))

    grad_w_in, grad_w_out = lax.cond(
        diffusing, lambda: weight_terms(g_all, xn0, hp0, act0, weight_out), no_terms
    )
    grad_in, grad_out = (
        lax.psum_scatter(
            grad_w_in.astype(jnp.bfloat16), ("sec", "dp"), scatter_dimension=0, tiled=True
        ).astype(jnp.float32),
        lax.psum_scatter(
            grad_w_out.astype(jnp.bfloat16), ("sec", "dp"), scatter_dimension=0, tiled=True
        ).astype(jnp.float32),
    )
    return (grad_in, grad_out)


def solution(mesh):
    in_specs = (
        P(("dp", "tp"), None, None),
        P(("dp", "tp")),
        P(("dp", "tp")),
        P(),
        P(),
        P("sec", None, "tp"),
        P("sec", None, "tp"),
    )
    out_specs = (P(("sec", "dp"), "tp"), P(("sec", "dp"), "tp"))
    return jax.shard_map(
        on_device, mesh=mesh, in_specs=in_specs, out_specs=out_specs, check_vma=False
    )
```

profile of v0, /device:TPU:0, one launch (start us, length us, event | category | flops | bytes accessed | tf_op | source)
XLA Modules:
  0.0 409.3 jit_solution(1710735596105612729)
XLA Ops:
  7.2 0.0 all-gather.5.cloned.1.call-start
  7.2 0.7 all-gather.5.cloned.1.call-update
  7.9 0.0 reduce-scatter.6.cloned.1.call-start
  8.0 37.0 %all-gather.5.cloned.1.call-done = bf16[8,64,1280]{2,1,0:T(8,128)(2,1)} async-done(((bf16[2,64,1280]{2,1,0:T(8,128)(2,1)}), bf16[8,64,1280]{2,1,0:T(8,128)(2,1)}) %all-gather.5.cloned.1.call-update) | async-done | bytes 1310736 | tf_op jit(solution)/shard_map/all_gather | solution.py:38
  45.0 15.3 %conditional.7 = (bf16[512,1280]{1,0:T(8,128)(2,1)}, f32[512,1280]{1,0:T(8,128)S(1)}, bf16[512,1280]{1,0:T(8,128)(2,1)}) conditional(s32[]{:T(128)} %convert_element_type.98, () %tuple.58, (bf16[8,64,1280]{2,1,0:T(8,128)(2,1)}, f32[2,1280]{1,0:T(2,128)}, bf16[1280,1280]{1,0:T(8,128)(2,1)}) %tuple.118), branch_computations={%region_1.2_spmd, %region_2.4_spmd} | conditional | flops 1724908032 | bytes 12479512 | solution.py:51
  45.0 1.6 multiply_reduce_fusion
  46.7 0.1 rsqrt.47
  46.7 0.7 slice_reduce_fusion
  47.5 2.7 fusion.20
  50.2 10.1 %fusion.18 = (bf16[512,1280]{1,0:T(8,128)(2,1)}, f32[512,1280]{1,0:T(8,128)S(1)}) fusion(bf16[512,1280]{1,0:T(8,128)(2,1)} %fusion.20, bf16[1280,1280]{1,0:T(8,128)(2,1)} %get-tuple-element.58), kind=kOutput, calls=%fused_computation.23 | convolution fusion | flops 1720320000 | bytes 8519680 | tf_op jit(solution)/shard_map/cond/branch_1_fun/dot_general | solution.py:63
  60.3 1.5 copy-done.6
  61.8 4.2 %conditional.8 = (bf16[512,1280]{1,0:T(8,128)(2,1)S(1)}) conditional(s32[]{:T(128)} %convert_element_type.98, () %tuple.57, (bf16[512,1280]{1,0:T(8,128)(2,1)}, bf16[1280,1280]{1,0:T(8,128)(2,1)}) %tuple.113), branch_computations={%region_4.0_spmd, %region_5.0_spmd} | conditional | flops 1677721600 | bytes 5898248 | solution.py:51
  61.8 4.2 %fusion.59 = bf16[512,1280]{1,0:T(8,128)(2,1)S(1)} fusion(bf16[512,1280]{1,0:T(8,128)(2,1)} %get-tuple-element.59, bf16[1280,1280]{1,0:T(8,128)(2,1)} %get-tuple-element.60), kind=kOutput, calls=%fused_computation.111 | convolution fusion | flops 1677721600 | bytes 5898240 | tf_op jit(solution)/shard_map/cond/branch_1_fun/dot_general | solution.py:78
  66.0 1.0 copy-done.2
  67.1 0.0 reduce-scatter.6.cloned.1.call-update
  67.1 0.0 all-gather.7.cloned.1.call-start
  67.2 29.4 %reduce-scatter.6.cloned.1.call-done = bf16[128,1280]{1,0:T(8,128)(2,1)} async-done(((bf16[512,1280]{1,0:T(8,128)(2,1)}), bf16[128,1280]{1,0:T(8,128)(2,1)}) %reduce-scatter.6.cloned.1.call-update) | async-done | bytes 327696 | tf_op jit(solution)/shard_map/reduce_scatter | solution.py:42
  96.6 1.2 fusion.47
  97.8 3.4 collective-permute-start
  101.2 6.8 %collective-permute-done = bf16[2,64,1280]{2,1,0:T(8,128)(2,1)S(1)} collective-permute-done((bf16[2,64,1280]{2,1,0:T(8,128)(2,1)S(1)}, bf16[2,64,1280]{2,1,0:T(8,128)(2,1)S(1)}, u32[]{:S(2)}, u32[]{:S(2)}) %collective-permute-start) | collective-permute-done | bytes 327712 | tf_op jit(solution)/shard_map/ppermute | solution.py:17
  107.9 0.7 copy-done.4
  108.7 0.0 all-gather.7.cloned.1.call-update
  108.7 0.0 reduce-scatter.8.cloned.1.call-start
  108.8 32.8 %all-gather.7.cloned.1.call-done = bf16[8,64,1280]{2,1,0:T(8,128)(2,1)} async-done(((bf16[2,64,1280]{2,1,0:T(8,128)(2,1)}), bf16[8,64,1280]{2,1,0:T(8,128)(2,1)}) %all-gather.7.cloned.1.call-update) | async-done | bytes 1310736 | tf_op jit(solution)/shard_map/all_gather | solution.py:38
  141.6 1.3 conditional.9
  141.6 1.2 broadcast.327
  142.7 0.2 broadcast.326
  142.9 1.2 conditional.10
  142.9 1.1 broadcast.360
  144.1 0.0 reduce-scatter.8.cloned.1.call-update
  144.1 0.0 reduce-scatter.10.cloned.1.call-start
  144.2 0.3 multiply_reduce_fusion.4
  144.5 46.0 %reduce-scatter.8.cloned.1.call-done = bf16[128,1280]{1,0:T(8,128)(2,1)} async-done(((bf16[512,1280]{1,0:T(8,128)(2,1)}), bf16[128,1280]{1,0:T(8,128)(2,1)}) %reduce-scatter.8.cloned.1.call-update) | async-done | bytes 327696 | tf_op jit(solution)/shard_map/reduce_scatter | solution.py:42
  190.5 1.2 fusion.43
  191.7 0.2 multiply_reduce_fusion.3
  191.9 0.1 convert_bitcast_fusion
  191.9 13.1 %all-gather = bf16[4,2,1280]{2,1,0:T(2,128)(2,1)S(1)} all-gather(bf16[1,2,1280]{2,1,0:T(2,128)(2,1)S(1)} %get-tuple-element.101), channel_id=1, replica_groups=mesh['sec'=2,'dp'=4,'tp'=4] {'tp'}, dimensions={0}, use_global_device_ids=true | all-gather | bytes 25600 | tf_op jit(solution)/shard_map/all_gather | solution.py:38
  205.1 1.1 conditional.11
  205.1 1.1 broadcast.361
  206.2 0.1 conditional.12
  206.2 0.1 broadcast.367
  206.3 1.0 copy-done.3
  207.4 0.0 all-gather.9.cloned.1.call-start
  207.5 0.1 rsqrt.57
  207.6 37.5 %reduce-scatter.10.cloned.1.call-done = bf16[128,1280]{1,0:T(8,128)(2,1)} async-done(((bf16[512,1280]{1,0:T(8,128)(2,1)}), bf16[128,1280]{1,0:T(8,128)(2,1)}) %reduce-scatter.10.cloned.1.call-update) | async-done | bytes 327696 | tf_op jit(solution)/shard_map/reduce_scatter | solution.py:42
  245.0 1.2 fusion.46
  246.2 1.2 fusion.45
  247.5 1.3 collective-permute-start.1
  248.8 9.9 %collective-permute-done.1 = bf16[2,64,1280]{2,1,0:T(8,128)(2,1)S(1)} collective-permute-done((bf16[2,64,1280]{2,1,0:T(8,128)(2,1)S(1)}, bf16[2,64,1280]{2,1,0:T(8,128)(2,1)S(1)}, u32[]{:S(2)}, u32[]{:S(2)}) %collective-permute-start.1) | collective-permute-done | bytes 327712 | tf_op jit(solution)/shard_map/ppermute | solution.py:17
  258.6 0.8 multiply_convert_fusion
  259.5 0.0 all-gather.9.cloned.1.call-update
  259.5 0.0 reduce-scatter.14.cloned.1.call-start
  259.6 30.9 %all-gather.9.cloned.1.call-done = bf16[8,64,1280]{2,1,0:T(8,128)(2,1)} async-done(((bf16[2,64,1280]{2,1,0:T(8,128)(2,1)}), bf16[8,64,1280]{2,1,0:T(8,128)(2,1)}) %all-gather.9.cloned.1.call-update) | async-done | bytes 1310736 | tf_op jit(solution)/shard_map/all_gather | solution.py:38
  290.5 12.9 %conditional.13 = (bf16[1280,1280]{0,1:T(8,128)(2,1)}, bf16[1280,1280]{1,0:T(8,128)(2,1)S(1)}) conditional(s32[]{:T(128)} %convert_element_type.98, () %tuple.56, (bf16[8,64,1280]{2,1,0:T(8,128)(2,1)}, bf16[1280,1280]{1,0:T(8,128)(2,1)}, f32[512,1280]{1,0:T(8,128)}, bf16[512,1280]{1,0:T(8,128)(2,1)}, bf16[512,1280]{1,0:T(8,128)(2,1)}) %tuple.117), branch_computations={%region_23.0_spmd, %region_24.0_spmd} | conditional | flops 5039718400 | bytes 17694736 | solution.py:165
  290.5 9.3 %convolution_bitcast_fusion = bf16[1280,1280]{0,1:T(8,128)(2,1)} fusion(bf16[512,1280]{1,0:T(8,128)(2,1)} %get-tuple-element.74, bf16[512,1280]{1,0:T(8,128)(2,1)} %bitcast.63, bf16[1280,1280]{1,0:T(8,128)(2,1)} %get-tuple-element.72, f32[512,1280]{1,0:T(8,128)} %get-tuple-element.73), kind=kOutput, calls=%fused_computation.7 | convolution fusion | flops 3361996800 | bytes 11796480 | tf_op jit(solution)/shard_map/cond/branch_1_fun/dot_general | solution.py:135
  299.8 3.6 fusion.63
  303.4 1.7 copy-done.1
  305.1 0.0 reduce-scatter.14.cloned.1.call-update
  305.1 0.0 reduce-scatter.12.cloned.1.call-start
  305.2 5.7 %copy.12 = bf16[1280,1280]{1,0:T(8,128)(2,1)} copy(bf16[1280,1280]{0,1:T(8,128)(2,1)} %get-tuple-element.90) | data formatting | bytes 6553600 | tf_op jit(solution)/shard_map/cond | solution.py:165
  310.9 39.4 %reduce-scatter.14.cloned.1.call-done = bf16[160,1280]{1,0:T(8,128)(2,1)} async-done(((bf16[1280,1280]{1,0:T(8,128)(2,1)}), bf16[160,1280]{1,0:T(8,128)(2,1)}) %reduce-scatter.14.cloned.1.call-update) | async-done | bytes 409616 | tf_op jit(solution)/shard_map/reduce_scatter | solution.py:172
  350.2 1.9 convert_element_type.115
  352.2 48.4 %reduce-scatter.12.cloned.1.call-done = bf16[160,1280]{1,0:T(8,128)(2,1)} async-done(((bf16[1280,1280]{1,0:T(8,128)(2,1)}), bf16[160,1280]{1,0:T(8,128)(2,1)}) %reduce-scatter.12.cloned.1.call-update) | async-done | bytes 409616 | tf_op jit(solution)/shard_map/reduce_scatter | solution.py:169
  400.6 1.9 convert_element_type.113
  (28 shorter events, 0.2 us)
Async XLA Ops:
  7.2 137.0 %copy-start = (bf16[64,1280]{1,0:T(8,128)(2,1)S(1)}, bf16[64,1280]{1,0:T(8,128)(2,1)}, u32[]{:S(2)}) copy-start(bf16[64,1280]{1,0:T(8,128)(2,1)} %param.24) | copy-start | bytes 491524
  7.2 37.8 %all-gather.5.cloned.1.call-start = ((), (), s32[]{:S(2)}) async-start(), calls=%async_computation.5 | async-start | bytes 1638400 | tf_op jit(solution)/shard_map/all_gather | solution.py:38
  7.9 88.7 %reduce-scatter.6.cloned.1.call-start = ((), (), s32[]{:S(2)}) async-start(), calls=%async_computation.6 | async-start | bytes 1638400 | tf_op jit(solution)/shard_map/reduce_scatter | solution.py:42
  60.3 1.5 copy-start.6
  60.3 6.9 %copy-start.9 = (s32[2]{0:T(128)S(1)}, s32[2]{0:T(128)}, u32[]{:S(2)}) copy-start(s32[2]{0:T(128)} %param.22) | copy-start | bytes 28
  60.3 36.3 %copy-start.7 = (bf16[2,64,1280]{2,1,0:T(8,128)(2,1)S(1)}, bf16[2,64,1280]{2,1,0:T(8,128)(2,1)}, u32[]{:S(2)}) copy-start(bf16[2,64,1280]{2,1,0:T(8,128)(2,1)} %param.21) | copy-start | bytes 983044
  66.0 1.1 copy-start.2
  66.0 42.7 %copy-start.8 = (f32[2,1280]{1,0:T(2,128)S(1)}, f32[2,1280]{1,0:T(2,128)}, u32[]{:S(2)}) copy-start(f32[2,1280]{1,0:T(2,128)} %param.25) | copy-start | bytes 30724
  67.1 74.5 %all-gather.7.cloned.1.call-start = ((), (), s32[]{:S(2)}) async-start(), calls=%async_computation.7 | async-start | bytes 1638400 | tf_op jit(solution)/shard_map/all_gather | solution.py:38
  97.8 10.2 %collective-permute-start = (bf16[2,64,1280]{2,1,0:T(8,128)(2,1)S(1)}, bf16[2,64,1280]{2,1,0:T(8,128)(2,1)S(1)}, u32[]{:S(2)}, u32[]{:S(2)}) collective-permute-start(bf16[2,64,1280]{2,1,0:T(8,128)(2,1)S(1)} %fusion.47), channel_id=1, source_target_pairs={{0,16},{1,17},{2,18},{3,19},{4,20},{5,21},{6,22},{7,23},{8,24},{9,... | collective-permute-start | bytes 983048 | tf_op jit(solution)/shard_map/ppermute | solution.py:17
  107.9 0.7 copy-start.4
  108.7 81.8 %reduce-scatter.8.cloned.1.call-start = ((), (), s32[]{:S(2)}) async-start(), calls=%async_computation.8 | async-start | bytes 1638400 | tf_op jit(solution)/shard_map/reduce_scatter | solution.py:42
  142.9 1.3 copy-start.10
  142.9 47.5 %copy-start.5 = (bf16[2,64,1280]{2,1,0:T(8,128)(2,1)S(1)}, bf16[2,64,1280]{2,1,0:T(8,128)(2,1)}, u32[]{:S(2)}) copy-start(bf16[2,64,1280]{2,1,0:T(8,128)(2,1)} %copy-done.4) | copy-start | bytes 983044
  144.1 100.9 %reduce-scatter.10.cloned.1.call-start = ((), (), s32[]{:S(2)}) async-start(), calls=%async_computation.9 | async-start | bytes 1638400 | tf_op jit(solution)/shard_map/reduce_scatter | solution.py:42
  206.3 1.1 copy-start.3
  207.4 83.1 %all-gather.9.cloned.1.call-start = ((), (), s32[]{:S(2)}) async-start(), calls=%async_computation.10 | async-start | bytes 1638400 | tf_op jit(solution)/shard_map/all_gather | solution.py:38
  247.5 11.2 %collective-permute-start.1 = (bf16[2,64,1280]{2,1,0:T(8,128)(2,1)S(1)}, bf16[2,64,1280]{2,1,0:T(8,128)(2,1)S(1)}, u32[]{:S(2)}, u32[]{:S(2)}) collective-permute-start(bf16[2,64,1280]{2,1,0:T(8,128)(2,1)S(1)} %add_convert_fusion), channel_id=1, source_target_pairs={{16,0},{17,1},{18,2},{19,3},{20,4},{21,5},{22,6},{23,7},{24,8},{25... | collective-permute-start | bytes 983048 | tf_op jit(solution)/shard_map/ppermute | solution.py:17
  259.5 90.7 %reduce-scatter.14.cloned.1.call-start = ((), (), s32[]{:S(2)}) async-start(), calls=%async_computation.12 | async-start | bytes 3686400 | tf_op jit(solution)/shard_map/reduce_scatter | solution.py:172
  303.4 1.7 copy-start.1
  305.1 95.4 %reduce-scatter.12.cloned.1.call-start = ((), (), s32[]{:S(2)}) async-start(), calls=%async_computation.11 | async-start | bytes 3686400 | tf_op jit(solution)/shard_map/reduce_scatter | solution.py:169
Sparse Core Ops, SparseCore 0:
  9.6 35.3 all-gather.4
  67.2 29.2 reduce-scatter.5
  108.8 32.7 all-gather.6
  144.2 46.1 reduce-scatter.7
  207.5 37.4 reduce-scatter.9
  259.6 30.7 all-gather.8
  305.2 44.9 reduce-scatter.13
  353.7 46.8 reduce-scatter.11
where the time goes:
time: 410 us; the launch traced here: 409 us
  waiting for transfers between devices  319 us (78%)
  matrix products  27.5 us (7%)
  local copies, waits for them, and re-layouts  16.4 us (4%)
  other arithmetic  14.3 us (3%)
  between operations  14.3 us (3%)
  blocking collectives  13.1 us (3%)
  starting transfers between devices  5.01 us (1%)
    reduce_scatter x3, waiting for transfers between devices, reduce_rows(): lax.psum_scatter(term_fn(jnp.int32(0), local_rows * lax.axis_size('tp'))....  113 us
    all_gather x3, waiting for transfers between devices, collect(): return lax.all_gather(piece, 'tp', axis=0, tiled=True)  101 us
    reduce_scatter x1, waiting for transfers between devices, on_device(): lax.psum_scatter(grad_w_in.astype(jnp.bfloat16), ('sec', 'dp'), scatter_d...  48.4 us
    reduce_scatter x1, waiting for transfers between devices, on_device(): lax.psum_scatter(grad_w_out.astype(jnp.bfloat16), ('sec', 'dp'), scatter_...  39.4 us
    ppermute x2, waiting for transfers between devices, shifted(): lax.ppermute(value, axis, [(source, source + steps) for source in range(l...  16.7 us
    all_gather x1, blocking collectives, collect(): return lax.all_gather(piece, 'tp', axis=0, tiled=True)  13.1 us
    dot_general x1, matrix products, compute(): hp = jnp.dot(xn, weight_in, preferred_element_type=jnp.float32)  10.1 us
    dot_general x1, matrix products, weight_terms(): lax.dot_general(xn0, g_hp0, contract_first, preferred_element_type=jnp.fl...  9.3 us
  transfers between devices with their start and end apart: 10, of which 10 were waited for; matrix products, arithmetic and copies ran while one was open for 2% of the time, Pallas kernels for 0%

commit v1 on v0

v1 whole, which is shorter than its diff:
```python
import math

import jax
import jax.numpy as jnp
from jax import lax
from jax.sharding import PartitionSpec as P

STEPS = 50


EPS = 1e-06


def rotated(value, axis, steps):
    count = lax.axis_size(axis)
    return lax.ppermute(value, axis, [(i, (i + steps) % count) for i in range(count)])


def sibling(value):
    count = lax.axis_size("dp")
    return lax.ppermute(value, "dp", [(i, i ^ 1) for i in range(count)])


def gelu_slope(value):
    return 0.5 * (1.0 + lax.erf(value / math.sqrt(2.0))) + value * jnp.exp(
        -0.5 * value * value
    ) / math.sqrt(2.0 * math.pi)


def normed(rows, gain):
    scale = lax.rsqrt(jnp.mean(rows * rows, axis=-1, keepdims=True) + EPS)
    return ((rows * scale * gain).astype(jnp.bfloat16), scale)


def score_of(pooled, text):
    unit_img = pooled * lax.rsqrt(jnp.mean(pooled * pooled, axis=-1, keepdims=True) + EPS)
    unit_txt = text * lax.rsqrt(jnp.mean(text * text, axis=-1, keepdims=True) + EPS)
    return 100.0 * jnp.sum(unit_img * unit_txt, axis=-1) / pooled.shape[-1]


def dot_nn(a, b):
    return jnp.dot(a, b, preferred_element_type=jnp.float32)


def dot_nt(a, b):
    return lax.dot_general(a, b, (((1,), (1,)), ((), ())), preferred_element_type=jnp.float32)


def dot_tn(a, b):
    return lax.dot_general(a, b, (((0,), (0,)), ((), ())), preferred_element_type=jnp.float32)


def gather_parts(piece):
    return [piece] + [rotated(piece, "tp", k) for k in range(1, lax.axis_size("tp"))]


def reduce_parts(parts):
    total = parts[0].astype(jnp.float32)
    for k in range(1, len(parts)):
        total = total + rotated(parts[k].astype(jnp.bfloat16), "tp", -k).astype(jnp.float32)
    return total


def from_other_section(weight, core):
    half = weight.shape[0] // 2
    piece = lax.dynamic_slice_in_dim(weight, core * half, half, 0)
    got = lax.ppermute(piece, "sec", [(0, 1), (1, 0)])
    beside = sibling(got)
    return jnp.where(
        core == 0, jnp.concatenate([got, beside], 0), jnp.concatenate([beside, got], 0)
    )


def sum_over_dp(partial, core):
    groups = lax.axis_size("dp") // 2
    rows = partial.shape[0] // (2 * groups)
    place = lax.axis_index("dp") // 2
    cut = partial.astype(jnp.bfloat16).reshape(groups, 2, rows, -1)
    away = lax.dynamic_index_in_dim(cut, 1 - core, 1, keepdims=False)
    keep = lax.dynamic_index_in_dim(cut, core, 1, keepdims=False)
    chip = keep.astype(jnp.float32) + sibling(away).astype(jnp.float32)
    total = lax.dynamic_index_in_dim(chip, place, 0, keepdims=False)
    sent = chip.astype(jnp.bfloat16)
    count = 2 * groups
    for k in range(1, groups):
        part = lax.dynamic_index_in_dim(sent, (place + k) % groups, 0, keepdims=False)
        total = total + rotated(part, "dp", 2 * k).astype(jnp.float32)
    return total


def on_device(latents, timesteps, prompt_ids, prompt_table, gains, w_in, w_out):
    count, tokens, width = latents.shape
    half = count // 2
    segment = lax.axis_index("sec")
    first = segment == 0
    core = lax.axis_index("dp") % 2
    own_in = w_in[0]
    own_out = w_out[0]
    theta = math.pi / 2.0 * (timesteps.astype(jnp.float32) + 1.0) / (STEPS + 1.0)
    alpha = jnp.cos(theta)[:, None, None]
    sigma = jnp.sin(theta)[:, None, None]

    flat = latents.reshape(count * tokens, width)
    lat_parts = gather_parts(flat)
    other_in = from_other_section(own_in, core)
    other_out = from_other_section(own_out, core)

    onehot = (
        prompt_ids[:, None] == jnp.arange(prompt_table.shape[0], dtype=jnp.int32)[None, :]
    ).astype(jnp.bfloat16)
    text = dot_nn(onehot, prompt_table).astype(jnp.bfloat16)
    text_mine = jnp.where(first, text[half:], text[:half])
    text_all = jnp.concatenate(gather_parts(text_mine), 0).astype(jnp.float32)

    eps_parts = []
    for part in lat_parts:
        xn, unused = normed(part.astype(jnp.float32), gains[0])
        act = jax.nn.gelu(dot_nn(xn, own_in), approximate=False).astype(jnp.bfloat16)
        eps_parts.append(dot_nt(act, own_out))
    eps_mix = reduce_parts(eps_parts).reshape(count, tokens, width)
    base = latents.astype(jnp.float32)
    images = ((base - sigma * (base + eps_mix)) / alpha).astype(jnp.bfloat16)

    arrived = lax.ppermute(images[:half], "sec", [(0, 1)])
    mine = jnp.where(first, images[half:], arrived)
    ratio = jnp.where(first, (sigma / alpha)[half:], (sigma / alpha)[:half])
    w1_in = jnp.where(first, other_in, own_in)
    w1_out = jnp.where(first, other_out, own_out)
    mine_rows = mine.reshape(half * tokens, width)
    seen_all = jnp.concatenate(gather_parts(mine_rows), 0).astype(jnp.float32)
    n_img = seen_all.shape[0] // tokens
    xn1, unused = normed(seen_all, gains[1])
    hp1 = dot_nn(xn1, w1_in)
    hidden = hp1.shape[1]
    act1 = jax.nn.gelu(hp1, approximate=False)
    slope1 = gelu_slope(hp1)
    act_mean = jnp.mean(act1.reshape(n_img, tokens, hidden), axis=1).astype(jnp.bfloat16)
    pool_part = dot_nt(act_mean, w1_out)
    pool = pool_part
    n_tp = lax.axis_size("tp")
    by_owner = pool_part.reshape(n_tp, half, width)
    for k in range(1, n_tp):
        theirs = rotated(by_owner, "tp", k)
        pool = pool + jnp.roll(theirs, k, axis=0).reshape(n_img, width)
    pooled = pool + jnp.mean(seen_all.reshape(n_img, tokens, width), axis=1)
    g_pooled = jax.grad(lambda p: -jnp.sum(score_of(p, text_all)))(pooled)
    g_mean = g_pooled / tokens
    g_h = dot_nn(g_mean.astype(jnp.bfloat16), w1_out)
    g_hp1 = (
        (g_h[:, None, :] * slope1.reshape(n_img, tokens, hidden))
        .reshape(n_img * tokens, hidden)
        .astype(jnp.bfloat16)
    )
    g_parts = dot_nt(g_hp1, w1_in).reshape(n_tp, half * tokens, width)
    g_xn = reduce_parts([g_parts[k] for k in range(n_tp)])
    seen = mine_rows.astype(jnp.float32)
    scale1 = lax.rsqrt(jnp.mean(seen * seen, axis=-1, keepdims=True) + EPS)
    weighted = gains[1] * g_xn
    g_norm = scale1 * weighted - seen * scale1**3 * jnp.mean(
        seen * weighted, axis=-1, keepdims=True
    )
    g_images = (g_mean[:half, None, :] + g_norm.reshape(half, tokens, width)).astype(jnp.bfloat16)
    g_eps = (-ratio * g_images.astype(jnp.float32)).astype(jnp.bfloat16)

    g_mine = gather_parts(g_eps.reshape(half * tokens, width))
    g_theirs = [lax.ppermute(part, "sec", [(0, 1), (1, 0)]) for part in g_mine]
    g_rows = jnp.concatenate(g_mine + g_theirs, 0)

    w0_in = jnp.where(first, own_in, other_in)
    w0_out = jnp.where(first, own_out, other_out)
    late = half * tokens
    lat_b = jnp.concatenate([part[late:] for part in lat_parts], 0)
    lat_a = jnp.concatenate([part[:late] for part in lat_parts], 0)
    lat_rows = jnp.concatenate(
        [jnp.where(first, lat_b, lat_a), jnp.where(first, lat_a, lat_b)], 0
    )
    xn0, unused = normed(lat_rows.astype(jnp.float32), gains[0])
    hp0 = dot_nn(xn0, w0_in)
    act0 = jax.nn.gelu(hp0, approximate=False).astype(jnp.bfloat16)
    slope0 = gelu_slope(hp0)

    share = width // 2
    g_cols = lax.dynamic_slice_in_dim(g_rows, segment * share, share, 1)
    xn_cols = lax.dynamic_slice_in_dim(xn0, segment * share, share, 1)
    grad_out = sum_over_dp(dot_tn(g_cols, act0), core)
    g_hp0 = (dot_nn(g_rows, w0_out) * slope0).astype(jnp.bfloat16)
    grad_in = sum_over_dp(dot_tn(xn_cols, g_hp0), core)
    return (grad_in, grad_out)


def solution(mesh):
    in_specs = (
        P(("dp", "tp"), None, None),
        P(("dp", "tp")),
        P(("dp", "tp")),
        P(),
        P(),
        P("sec", None, "tp"),
        P("sec", None, "tp"),
    )
    out_specs = (P(("sec", "dp"), "tp"), P(("sec", "dp"), "tp"))
    return jax.shard_map(
        on_device, mesh=mesh, in_specs=in_specs, out_specs=out_specs, check_vma=False
    )
```

time: 410 us -> 230 us (0.56)
  waiting for transfers between devices: 319 us -> 88.9 us
  starting transfers between devices: 5.01 us -> 48.2 us
  matrix products: 27.5 us -> 66 us
  blocking collectives: 13.1 us -> 0 us
  between operations: 14.3 us -> 2.3 us
    reduce_scatter x5 -> x0, waiting for transfers between devices: 201 us -> none  [the longest x3 113 us: reduce_rows(): lax.psum_scatter(term_fn(jnp.int32(0), local_rows * lax.axis_size('tp'))....]
    all_gather x3 -> x0, waiting for transfers between devices: 101 us -> none  [collect(): return lax.all_gather(piece, 'tp', axis=0, tiled=True)]
    ppermute x2 -> x34, waiting for transfers between devices: 16.7 us -> 88.9 us  [the longest x23 56.6 us: rotated(): lax.ppermute(value, axis, [(i, (i + steps) % count) for i in range(count)])]
    ppermute x2 -> x34, starting transfers between devices: 4.68 us -> 48.2 us  [the longest x23 36.7 us: rotated(): lax.ppermute(value, axis, [(i, (i + steps) % count) for i in range(count)])]
    dot_general x5 -> x12, matrix products: 27.5 us -> 66 us  [the longest x6 33 us: dot_nt(): lax.dot_general(a, b, (((1,), (1,)), ((), ())), preferred_element_type=jn...]
    all_gather x1 -> x0, blocking collectives: 13.1 us -> none  [collect(): return lax.all_gather(piece, 'tp', axis=0, tiled=True)]
    add x0 -> x5, other arithmetic: none -> 5.75 us  [the longest x2 2.61 us: sum_over_dp(): chip = keep.astype(jnp.float32) + sibling(away).astype(jnp.float32)]
    cond x1 -> x0, local copies, waits for them, and re-layouts: 5.7 us -> none  [on_device(): lax.cond(diffusing, lambda: weight_terms(g_all, xn0, hp0, act0, weight_ou...]
  transfers between devices with their start and end apart: 10 -> 34, of which waited for: 10 -> 15; matrix products, arithmetic and copies ran while one was open for 2% -> 29% of each run, Pallas kernels for 0% -> 0%
where the time goes in v1:
time: 230 us
  waiting for transfers between devices  88.9 us (39%)
  matrix products  66 us (29%)
  starting transfers between devices  48.2 us (21%)
  local copies, waits for them, and re-layouts  13.3 us (6%)
  other arithmetic  11.2 us (5%)
    ppermute x23, waiting for transfers between devices, rotated(): lax.ppermute(value, axis, [(i, (i + steps) % count) for i in range(count)])  56.6 us
    ppermute x23, starting transfers between devices, rotated(): lax.ppermute(value, axis, [(i, (i + steps) % count) for i in range(count)])  36.7 us
    dot_general x6, matrix products, dot_nt(): lax.dot_general(a, b, (((1,), (1,)), ((), ())), preferred_element_type=jn...  33 us
    ppermute x1, waiting for transfers between devices, on_device(): arrived = lax.ppermute(images[:half], 'sec', [(0, 1)])  28.6 us
    dot_general x2, matrix products, dot_tn(): lax.dot_general(a, b, (((0,), (0,)), ((), ())), preferred_element_type=jn...  16.7 us
    dot_general x4, matrix products, dot_nn(): return jnp.dot(a, b, preferred_element_type=jnp.float32)  16.3 us
    ppermute x4, starting transfers between devices, on_device(): g_theirs = [lax.ppermute(part, 'sec', [(0, 1), (1, 0)]) for part in g_mine]  5.19 us
    unnamed x22, local copies, waits for them, and re-layouts  5.01 us
  transfers between devices with their start and end apart: 34, of which 15 were waited for; matrix products, arithmetic and copies ran while one was open for 29% of the time, Pallas kernels for 0%

profile of v1, /device:TPU:0, one launch (start us, length us, event | category | flops | bytes accessed | tf_op | source)
XLA Modules:
  0.0 229.9 jit_solution(3246198523845893135)
XLA Ops:
  0.6 5.1 %collective-permute-start.2 = (bf16[128,1280]{1,0:T(8,128)(2,1)}, bf16[128,1280]{1,0:T(8,128)(2,1)S(1)}, u32[]{:S(2)}, u32[]{:S(2)}) collective-permute-start(bf16[128,1280]{1,0:T(8,128)(2,1)} %bitcast.129), channel_id=1, source_target_pairs={{0,3},{1,0},{2,1},{3,2},{4,7},{5,4},{6,5},{7,6},{8,11},{9,8},{10,9... | collective-permute-start | bytes 983048 | tf_op jit(solution)/shard_map/ppermute | solution.py:16
  5.8 0.9 convolution_convert_fusion.2
  6.6 0.9 collective-permute-start.5
  7.5 2.2 collective-permute-start.4
  9.7 1.9 collective-permute-start.3
  11.6 1.1 fusion.87
  12.7 1.0 slice_bitcast_fusion.1
  13.8 0.8 slice_reduce_fusion.1
  14.6 2.9 %dynamic-slice_bitcast_fusion.1 = bf16[640,1280]{1,0:T(8,128)(2,1)} fusion(bf16[1,1280,1280]{2,1,0:T(8,128)(2,1)} %param.12, s32[]{:T(128)S(6)} %select_n.124), kind=kLoop, calls=%fused_computation.67 | loop fusion | bytes 3276804 | tf_op jit(solution)/shard_map/dynamic_slice | solution.py:66
  17.7 0.9 copy-done.1
  18.7 6.5 %fusion.6 = f32[128,1280]{1,0:T(8,128)} fusion(bf16[1,1280,1280]{2,1,0:T(8,128)(2,1)} %param.13, bf16[128,1280]{1,0:T(8,128)(2,1)S(1)} %bitcast.137, bf16[1,1280,1280]{2,1,0:T(8,128)(2,1)} %param.12), kind=kOutput, calls=%fused_computation.13 | convolution fusion | flops 849510400 | bytes 7536640 | tf_op jit(solution)/shard_map/dot_general | solution.py:46
  27.8 1.5 collective-permute-start.13
  30.2 6.4 %fusion.43 = bf16[128,1280]{1,0:T(8,128)(2,1)} fusion(bf16[1,1280,1280]{2,1,0:T(8,128)(2,1)} %param.13, bf16[1,1280,1280]{2,1,0:T(8,128)(2,1)} %param.12, bf16[128,1280]{1,0:T(8,128)(2,1)S(1)} %collective-permute-done.2, f32[128]{0:T(128)S(1)} %add_rsqrt_fusion.4, f32[1280]{0:T(1024)S(1)} %get-tuple-element.7), kind=kOutput, calls=%fused_computation.60 | convolution fusion | flops 850329600 | bytes 7214592 | tf_op jit(solution)/shard_map/dot_general | solution.py:46
  36.6 1.1 collective-permute-start.8
  37.9 6.4 %fusion.40 = bf16[128,1280]{1,0:T(8,128)(2,1)} fusion(bf16[1,1280,1280]{2,1,0:T(8,128)(2,1)} %param.13, bf16[1,1280,1280]{2,1,0:T(8,128)(2,1)} %param.12, bf16[128,1280]{1,0:T(8,128)(2,1)S(1)} %collective-permute-done.1, f32[128]{0:T(128)S(1)} %add_rsqrt_fusion.5, f32[1280]{0:T(1024)S(1)} %get-tuple-element.7), kind=kOutput, calls=%fused_computation.59 | convolution fusion | flops 850329600 | bytes 7214592 | tf_op jit(solution)/shard_map/dot_general | solution.py:46
  44.3 3.4 %collective-permute-start.7 = (bf16[128,1280]{1,0:T(8,128)(2,1)}, bf16[128,1280]{1,0:T(8,128)(2,1)}, u32[]{:S(2)}, u32[]{:S(2)}) collective-permute-start(bf16[128,1280]{1,0:T(8,128)(2,1)} %fusion.40), channel_id=1, source_target_pairs={{0,2},{1,3},{2,0},{3,1},{4,6},{5,7},{6,4},{7,5},{8,10},{9,11},{10,... | collective-permute-start | bytes 983048 | tf_op jit(solution)/shard_map/ppermute | solution.py:16
  47.9 6.5 %fusion.37 = bf16[128,1280]{1,0:T(8,128)(2,1)} fusion(bf16[1,1280,1280]{2,1,0:T(8,128)(2,1)} %param.13, bf16[1,1280,1280]{2,1,0:T(8,128)(2,1)} %param.12, bf16[128,1280]{1,0:T(8,128)(2,1)S(1)} %collective-permute-done, f32[1280]{0:T(1024)S(1)} %get-tuple-element.7, f32[128]{0:T(128)S(1)} %add_rsqrt_fusion.6), kind=kOutput, calls=%fused_computation.58 | convolution fusion | flops 850329600 | bytes 7214592 | tf_op jit(solution)/shard_map/dot_general | solution.py:46
  54.3 1.1 collective-permute-start.6
  55.5 5.9 %collective-permute-done.7 = bf16[128,1280]{1,0:T(8,128)(2,1)} collective-permute-done((bf16[128,1280]{1,0:T(8,128)(2,1)}, bf16[128,1280]{1,0:T(8,128)(2,1)}, u32[]{:S(2)}, u32[]{:S(2)}) %collective-permute-start.7) | collective-permute-done | bytes 327712 | tf_op jit(solution)/shard_map/ppermute | solution.py:16
  61.4 6.1 %collective-permute-done.6 = bf16[128,1280]{1,0:T(8,128)(2,1)S(1)} collective-permute-done((bf16[128,1280]{1,0:T(8,128)(2,1)}, bf16[128,1280]{1,0:T(8,128)(2,1)S(1)}, u32[]{:S(2)}, u32[]{:S(2)}) %collective-permute-start.6) | collective-permute-done | bytes 327712 | tf_op jit(solution)/shard_map/ppermute | solution.py:16
  67.5 1.2 convert_add_fusion.3
  69.2 3.5 %collective-permute-start.9 = (bf16[1,64,1280]{2,1,0:T(8,128)(2,1)S(1)}, bf16[1,64,1280]{2,1,0:T(8,128)(2,1)S(1)}, u32[]{:S(2)}, u32[]{:S(2)}) collective-permute-start(bf16[1,64,1280]{2,1,0:T(8,128)(2,1)S(1)} %slice.151), channel_id=1, source_target_pairs={{0,16},{1,17},{2,18},{3,19},{4,20},{5,21},{6,22},{7,23},{8,24},{9,... | collective-permute-start | bytes 491528 | tf_op jit(solution)/shard_map/ppermute | solution.py:124
  73.2 28.6 %collective-permute-done.9 = bf16[1,64,1280]{2,1,0:T(8,128)(2,1)S(1)} collective-permute-done((bf16[1,64,1280]{2,1,0:T(8,128)(2,1)S(1)}, bf16[1,64,1280]{2,1,0:T(8,128)(2,1)S(1)}, u32[]{:S(2)}, u32[]{:S(2)}) %collective-permute-start.9) | collective-permute-done | bytes 163872 | tf_op jit(solution)/shard_map/ppermute | solution.py:124
  101.9 3.9 %collective-permute-start.12 = (bf16[64,1280]{1,0:T(8,128)(2,1)S(1)}, bf16[64,1280]{1,0:T(8,128)(2,1)S(1)}, u32[]{:S(2)}, u32[]{:S(2)}) collective-permute-start(bf16[64,1280]{1,0:T(8,128)(2,1)S(1)} %fusion.291), channel_id=1, source_target_pairs={{0,3},{1,0},{2,1},{3,2},{4,7},{5,4},{6,5},{7,6},{8,11},{9,8},{10,9... | collective-permute-start | bytes 491528 | tf_op jit(solution)/shard_map/ppermute | solution.py:16
  106.4 4.0 %collective-permute-done.12 = bf16[64,1280]{1,0:T(8,128)(2,1)S(1)} collective-permute-done((bf16[64,1280]{1,0:T(8,128)(2,1)S(1)}, bf16[64,1280]{1,0:T(8,128)(2,1)S(1)}, u32[]{:S(2)}, u32[]{:S(2)}) %collective-permute-start.12) | collective-permute-done | bytes 163872 | tf_op jit(solution)/shard_map/ppermute | solution.py:16
  110.4 7.7 %collective-permute-done.11 = bf16[64,1280]{1,0:T(8,128)(2,1)S(1)} collective-permute-done((bf16[64,1280]{1,0:T(8,128)(2,1)S(1)}, bf16[64,1280]{1,0:T(8,128)(2,1)S(1)}, u32[]{:S(2)}, u32[]{:S(2)}) %collective-permute-start.11) | collective-permute-done | bytes 163872 | tf_op jit(solution)/shard_map/ppermute | solution.py:16
  118.5 6.7 %bitcast_reduce_fusion.1 = (f32[4,1280]{1,0:T(4,128)S(1)}, f32[256,1280]{1,0:T(8,128)S(1)}) fusion(bf16[1,1280,1280]{2,1,0:T(8,128)(2,1)S(1)} %copy-done.2, pred[]{:T(512)} %eq.24, bf16[640,1280]{1,0:T(8,128)(2,1)} %collective-permute-done.13, bf16[640,1280]{1,0:T(8,128)(2,1)S(1)} %collective-permute-done.14, pred[]{:T(512)S(6)} %eq.28, ...), kind=kOutput, calls=%fused_computation.78 | convolution fusion | flops 880143360 | bytes 8546306 | tf_op jit(solution)/shard_map/dot_general | solution.py:42
  125.1 3.5 %fusion.65 = f32[4,1280]{1,0:T(4,128)S(1)} fusion(bf16[1,1280,1280]{2,1,0:T(8,128)(2,1)S(1)} %copy-done.4, pred[]{:T(512)} %eq.24, f32[4,1280]{1,0:T(4,128)S(1)} %get-tuple-element.37, bf16[640,1280]{1,0:T(8,128)(2,1)S(1)} %collective-permute-done.16, bf16[640,1280]{1,0:T(8,128)(2,1)} %collective-permute-done.15, pred[]{:T(512)S(6)} %eq.28), kind=kOutput, calls=%fused_computation.99 | convolution fusion | flops 29501440 | bytes 6594562 | tf_op jit(solution)/shard_map/dot_general | solution.py:46
  128.7 1.9 collective-permute-start.18
  131.2 1.6 collective-permute-start.17
  133.5 1.1 collective-permute-done.19
  134.6 2.2 collective-permute-done.17
  137.1 3.3 %fusion.64 = f32[4,1280]{1,0:T(4,128)S(1)} fusion(bf16[1,1280,1280]{2,1,0:T(8,128)(2,1)S(1)} %copy-done.4, pred[]{:T(512)} %eq.24, f32[4,1280]{1,0:T(4,128)S(1)} %fusion.297, bf16[640,1280]{1,0:T(8,128)(2,1)S(1)} %collective-permute-done.16, bf16[640,1280]{1,0:T(8,128)(2,1)} %collective-permute-done.15, pred[]{:T(512)S(6)} %eq.28), kind=kOutput, calls=%fused_computation.98 | convolution fusion | flops 29496320 | bytes 6594562 | tf_op jit(solution)/shard_map/dot_general | solution.py:42
  141.0 3.7 %fusion.479 = (bf16[256,1280]{1,0:T(8,128)(2,1)S(1)}, f32[256,1280]{1,0:T(8,128)S(1)}) fusion(bf16[256,1280]{1,0:T(8,128)(2,1)S(1)} %fusion.53, bf16[1,1280,1280]{2,1,0:T(8,128)(2,1)S(1)} %copy-done.2, pred[]{:T(512)} %eq.24, bf16[640,1280]{1,0:T(8,128)(2,1)} %collective-permute-done.13, bf16[640,1280]{1,0:T(8,128)(2,1)S(1)} %collective-permute-done.14, ...), kind=kOutput, calls=%fused_computation.586 | convolution fusion | flops 855572480 | bytes 9175042 | tf_op jit(solution)/shard_map/dot_general | solution.py:46
  144.8 0.8 collective-permute-start.21
  145.6 3.0 %collective-permute-start.20 = (bf16[64,1280]{1,0:T(8,128)(2,1)S(1)}, bf16[64,1280]{1,0:T(8,128)(2,1)S(1)}, u32[]{:S(2)}, u32[]{:S(2)}) collective-permute-start(bf16[64,1280]{1,0:T(8,128)(2,1)S(1)} %get-tuple-element.15), channel_id=1, source_target_pairs={{0,3},{1,0},{2,1},{3,2},{4,7},{5,4},{6,5},{7,6},{8,11},{9,8},{10,9... | collective-permute-start | bytes 491528 | tf_op jit(solution)/shard_map/ppermute | solution.py:16
  149.0 4.8 %collective-permute-done.22 = bf16[64,1280]{1,0:T(8,128)(2,1)S(1)} collective-permute-done((bf16[64,1280]{1,0:T(8,128)(2,1)S(1)}, bf16[64,1280]{1,0:T(8,128)(2,1)S(1)}, u32[]{:S(2)}, u32[]{:S(2)}) %collective-permute-start.22) | collective-permute-done | bytes 163872 | tf_op jit(solution)/shard_map/ppermute | solution.py:16
  153.8 4.9 %collective-permute-done.21 = bf16[64,1280]{1,0:T(8,128)(2,1)S(1)} collective-permute-done((bf16[64,1280]{1,0:T(8,128)(2,1)S(1)}, bf16[64,1280]{1,0:T(8,128)(2,1)S(1)}, u32[]{:S(2)}, u32[]{:S(2)}) %collective-permute-start.21) | collective-permute-done | bytes 163872 | tf_op jit(solution)/shard_map/ppermute | solution.py:16
  158.9 0.9 constant_dynamic-update-slice_fusion.7
  159.7 3.1 %collective-permute-start.23 = (bf16[64,1280]{1,0:T(8,128)(2,1)S(1)}, bf16[64,1280]{1,0:T(8,128)(2,1)S(1)}, u32[]{:S(2)}, u32[]{:S(2)}) collective-permute-start(bf16[64,1280]{1,0:T(8,128)(2,1)S(1)} %get-tuple-element.9), channel_id=1, source_target_pairs={{0,1},{1,2},{2,3},{3,0},{4,5},{5,6},{6,7},{7,4},{8,9},{9,10},{10,1... | collective-permute-start | bytes 491528 | tf_op jit(solution)/shard_map/ppermute | solution.py:16
  162.8 5.5 %fusion.16 = f32[512,1280]{1,0:T(8,128)} fusion(bf16[512,1280]{1,0:T(8,128)(2,1)S(1)} %fusion.22, bf16[1,1280,1280]{2,1,0:T(8,128)(2,1)S(1)} %copy-done.2, pred[]{:T(512)} %eq.24, bf16[640,1280]{1,0:T(8,128)(2,1)S(1)} %collective-permute-done.14, bf16[640,1280]{1,0:T(8,128)(2,1)} %collective-permute-done.13, pred[]{:T(512)S(6)} %eq.28), kind=kOutput, calls=%fused_computation.25 | convolution fusion | flops 1694105600 | bytes 10485762 | tf_op jit(solution)/shard_map/dot_general | solution.py:42
  168.3 2.3 %collective-permute-start.25 = (bf16[64,1280]{1,0:T(8,128)(2,1)S(1)}, bf16[64,1280]{1,0:T(8,128)(2,1)S(1)}, u32[]{:S(2)}, u32[]{:S(2)}) collective-permute-start(bf16[64,1280]{1,0:T(8,128)(2,1)S(1)} %get-tuple-element.9), channel_id=1, source_target_pairs={{0,3},{1,0},{2,1},{3,2},{4,7},{5,4},{6,5},{7,6},{8,11},{9,8},{10,9... | collective-permute-start | bytes 491528 | tf_op jit(solution)/shard_map/ppermute | solution.py:16
  170.7 2.6 %collective-permute-start.26 = (bf16[64,1280]{1,0:T(8,128)(2,1)S(1)}, bf16[64,1280]{1,0:T(8,128)(2,1)S(1)}, u32[]{:S(2)}, u32[]{:S(2)}) collective-permute-start(bf16[64,1280]{1,0:T(8,128)(2,1)S(1)} %get-tuple-element.9), channel_id=1, source_target_pairs={{0,16},{16,0},{1,17},{17,1},{2,18},{18,2},{3,19},{19,3},{4,20},{20... | collective-permute-start | bytes 491528 | tf_op jit(solution)/shard_map/ppermute | solution.py:166
  173.3 0.7 constant_dynamic-update-slice_fusion.6
  174.0 3.9 %collective-permute-done.24 = bf16[64,1280]{1,0:T(8,128)(2,1)S(1)} collective-permute-done((bf16[64,1280]{1,0:T(8,128)(2,1)S(1)}, bf16[64,1280]{1,0:T(8,128)(2,1)S(1)}, u32[]{:S(2)}, u32[]{:S(2)}) %collective-permute-start.24) | collective-permute-done | bytes 163872 | tf_op jit(solution)/shard_map/ppermute | solution.py:16
  177.8 2.6 %collective-permute-start.28 = (bf16[64,1280]{1,0:T(8,128)(2,1)S(1)}, bf16[64,1280]{1,0:T(8,128)(2,1)S(1)}, u32[]{:S(2)}, u32[]{:S(2)}) collective-permute-start(bf16[64,1280]{1,0:T(8,128)(2,1)S(1)} %collective-permute-done.24), channel_id=1, source_target_pairs={{0,16},{16,0},{1,17},{17,1},{2,18},{18,2},{3,19},{19,3},{4,20},{20... | collective-permute-start | bytes 491528 | tf_op jit(solution)/shard_map/ppermute | solution.py:166
  181.1 0.7 constant_dynamic-update-slice_fusion.4
  181.8 0.7 constant_dynamic-update-slice_fusion.3
  182.5 0.7 constant_dynamic-update-slice_fusion.2
  183.2 2.2 collective-permute-done.28
  186.1 1.4 collective-permute-done.29
  187.5 0.7 constant_dynamic-update-slice_fusion
  188.2 8.5 %convolution_convert_fusion.1 = bf16[640,1280]{1,0:T(8,128)(2,1)S(1)} fusion(bf16[512,1280]{1,0:T(8,128)(2,1)} %constant_dynamic-update-slice_fusion, bf16[1,1280,1280]{2,1,0:T(8,128)(2,1)} %param.13, pred[]{:T(512)} %eq.24, f32[512,1280]{1,0:T(8,128)} %fusion.16, bf16[512,1280]{1,0:T(8,128)(2,1)S(1)} %fusion.22, s32[]{:T(128)S(6)} %select_n.114, ...), kind=kOutput, calls=%fused_computation.31 | convolution fusion | flops 2540339200 | bytes 12779526 | tf_op jit(solution)/shard_map/dot_general | solution.py:50
  196.7 1.0 dynamic-slice_bitcast_fusion.3
  197.6 8.2 %convolution_convert_fusion = bf16[640,1280]{1,0:T(8,128)(2,1)S(1)} fusion(f32[512,1280]{1,0:T(8,128)} %fusion.16, bf16[512,1280]{1,0:T(8,128)(2,1)} %constant_dynamic-update-slice_fusion, s32[]{:T(128)S(6)} %select_n.114), kind=kOutput, calls=%fused_computation.30 | convolution fusion | flops 882278400 | bytes 4915204 | tf_op jit(solution)/shard_map/dot_general | solution.py:50
  205.9 1.0 dynamic-slice_bitcast_fusion.2
  207.3 1.3 convert_add_fusion.1
  208.7 1.6 collective-permute-start.31
  210.3 1.3 convert_add_fusion
  211.6 0.9 collective-permute-start.33
  212.6 8.5 %collective-permute-done.31 = bf16[160,1280]{1,0:T(8,128)(2,1)S(1)} collective-permute-done((bf16[160,1280]{1,0:T(8,128)(2,1)S(1)}, bf16[160,1280]{1,0:T(8,128)(2,1)S(1)}, u32[]{:S(2)}, u32[]{:S(2)}) %collective-permute-start.31) | collective-permute-done | bytes 409632 | tf_op jit(solution)/shard_map/ppermute | solution.py:16
  221.1 1.0 bitcast_add_fusion.1
  222.1 6.9 %collective-permute-done.33 = bf16[160,1280]{1,0:T(8,128)(2,1)S(1)} collective-permute-done((bf16[160,1280]{1,0:T(8,128)(2,1)S(1)}, bf16[160,1280]{1,0:T(8,128)(2,1)S(1)}, u32[]{:S(2)}, u32[]{:S(2)}) %collective-permute-start.33) | collective-permute-done | bytes 409632 | tf_op jit(solution)/shard_map/ppermute | solution.py:16
  228.9 1.0 bitcast_add_fusion
  (92 shorter events, 9.7 us)
Async XLA Ops:
  0.6 5.1 %copy-start = (bf16[64,1280]{1,0:T(8,128)(2,1)S(1)}, bf16[64,1280]{1,0:T(8,128)(2,1)}, u32[]{:S(2)}) copy-start(bf16[64,1280]{1,0:T(8,128)(2,1)} %param.10) | copy-start | bytes 491524
  0.6 29.4 %collective-permute-start.2 = (bf16[128,1280]{1,0:T(8,128)(2,1)}, bf16[128,1280]{1,0:T(8,128)(2,1)S(1)}, u32[]{:S(2)}, u32[]{:S(2)}) collective-permute-start(bf16[128,1280]{1,0:T(8,128)(2,1)} %bitcast.129), channel_id=1, source_target_pairs={{0,3},{1,0},{2,1},{3,2},{4,7},{5,4},{6,5},{7,6},{8,11},{9,8},{10,9... | collective-permute-start | bytes 983048 | tf_op jit(solution)/shard_map/ppermute | solution.py:16
  5.7 32.0 %collective-permute-start.1 = (bf16[128,1280]{1,0:T(8,128)(2,1)}, bf16[128,1280]{1,0:T(8,128)(2,1)S(1)}, u32[]{:S(2)}, u32[]{:S(2)}) collective-permute-start(bf16[128,1280]{1,0:T(8,128)(2,1)} %bitcast.130), channel_id=1, source_target_pairs={{0,2},{1,3},{2,0},{3,1},{4,6},{5,7},{6,4},{7,5},{8,10},{9,11},{10,... | collective-permute-start | bytes 983048 | tf_op jit(solution)/shard_map/ppermute | solution.py:16
  6.6 20.5 %collective-permute-start.5 = (bf16[1,1280]{1,0:T(2,128)(2,1)S(1)}, bf16[1,1280]{1,0:T(2,128)(2,1)S(1)}, u32[]{:S(2)}, u32[]{:S(2)}) collective-permute-start(bf16[1,1280]{1,0:T(2,128)(2,1)S(1)} %broadcast_select_fusion.2), channel_id=1, source_target_pairs={{0,3},{1,0},{2,1},{3,2},{4,7},{5,4},{6,5},{7,6},{8,11},{9,8},{10,9... | collective-permute-start | bytes 7688 | tf_op jit(solution)/shard_map/ppermute | solution.py:16
  7.5 20.3 %collective-permute-start.4 = (bf16[1,1280]{1,0:T(2,128)(2,1)S(1)}, bf16[1,1280]{1,0:T(2,128)(2,1)S(1)}, u32[]{:S(2)}, u32[]{:S(2)}) collective-permute-start(bf16[1,1280]{1,0:T(2,128)(2,1)S(1)} %broadcast_select_fusion.2), channel_id=1, source_target_pairs={{0,2},{1,3},{2,0},{3,1},{4,6},{5,7},{6,4},{7,5},{8,10},{9,11},{10,... | collective-permute-start | bytes 7688 | tf_op jit(solution)/shard_map/ppermute | solution.py:16
  9.7 19.7 %collective-permute-start.3 = (bf16[1,1280]{1,0:T(2,128)(2,1)S(1)}, bf16[1,1280]{1,0:T(2,128)(2,1)S(1)}, u32[]{:S(2)}, u32[]{:S(2)}) collective-permute-start(bf16[1,1280]{1,0:T(2,128)(2,1)S(1)} %broadcast_select_fusion.2), channel_id=1, source_target_pairs={{0,1},{1,2},{2,3},{3,0},{4,5},{5,6},{6,7},{7,4},{8,9},{9,10},{10,1... | collective-permute-start | bytes 7688 | tf_op jit(solution)/shard_map/ppermute | solution.py:16
  14.6 2.9 %copy-start.3 = (bf16[1,1280,1280]{2,1,0:T(8,128)(2,1)S(1)}, bf16[1,1280,1280]{2,1,0:T(8,128)(2,1)}, u32[]{:S(2)}) copy-start(bf16[1,1280,1280]{2,1,0:T(8,128)(2,1)} %param.13) | copy-start | bytes 9830404
  17.5 1.0 copy-start.1
  18.7 6.5 %copy-start.6 = (s32[2]{0:T(128)S(1)}, s32[2]{0:T(128)}, u32[]{:S(2)}) copy-start(s32[2]{0:T(128)} %param.8) | copy-start | bytes 28
  27.1 20.6 %collective-permute-start = (bf16[128,1280]{1,0:T(8,128)(2,1)S(1)}, bf16[128,1280]{1,0:T(8,128)(2,1)S(1)}, u32[]{:S(2)}, u32[]{:S(2)}) collective-permute-start(bf16[128,1280]{1,0:T(8,128)(2,1)S(1)} %bitcast.131), channel_id=1, source_target_pairs={{0,1},{1,2},{2,3},{3,0},{4,5},{5,6},{6,7},{7,4},{8,9},{9,10},{10,1... | collective-permute-start | bytes 983048 | tf_op jit(solution)/shard_map/ppermute | solution.py:16
  27.8 40.9 %collective-permute-start.13 = (bf16[640,1280]{1,0:T(8,128)(2,1)}, bf16[640,1280]{1,0:T(8,128)(2,1)}, u32[]{:S(2)}, u32[]{:S(2)}) collective-permute-start(bf16[640,1280]{1,0:T(8,128)(2,1)} %dynamic-slice_bitcast_fusion.1), channel_id=1, source_target_pairs={{0,16},{16,0},{1,17},{17,1},{2,18},{18,2},{3,19},{19,3},{4,20},{20... | collective-permute-start | bytes 4915208 | tf_op jit(solution)/shard_map/ppermute | solution.py:67
  29.3 89.0 %collective-permute-start.15 = (bf16[640,1280]{1,0:T(8,128)(2,1)S(1)}, bf16[640,1280]{1,0:T(8,128)(2,1)}, u32[]{:S(2)}, u32[]{:S(2)}) collective-permute-start(bf16[640,1280]{1,0:T(8,128)(2,1)S(1)} %dynamic-slice_bitcast_fusion), channel_id=1, source_target_pairs={{0,16},{16,0},{1,17},{17,1},{2,18},{18,2},{3,19},{19,3},{4,20},{20... | collective-permute-start | bytes 4915208 | tf_op jit(solution)/shard_map/ppermute | solution.py:67
  36.6 18.9 %collective-permute-start.8 = (bf16[128,1280]{1,0:T(8,128)(2,1)}, bf16[128,1280]{1,0:T(8,128)(2,1)}, u32[]{:S(2)}, u32[]{:S(2)}) collective-permute-start(bf16[128,1280]{1,0:T(8,128)(2,1)} %fusion.43), channel_id=1, source_target_pairs={{0,1},{1,2},{2,3},{3,0},{4,5},{5,6},{6,7},{7,4},{8,9},{9,10},{10,1... | collective-permute-start | bytes 983048 | tf_op jit(solution)/shard_map/ppermute | solution.py:16
  44.3 17.1 %collective-permute-start.7 = (bf16[128,1280]{1,0:T(8,128)(2,1)}, bf16[128,1280]{1,0:T(8,128)(2,1)}, u32[]{:S(2)}, u32[]{:S(2)}) collective-permute-start(bf16[128,1280]{1,0:T(8,128)(2,1)} %fusion.40), channel_id=1, source_target_pairs={{0,2},{1,3},{2,0},{3,1},{4,6},{5,7},{6,4},{7,5},{8,10},{9,11},{10,... | collective-permute-start | bytes 983048 | tf_op jit(solution)/shard_map/ppermute | solution.py:16
  54.3 13.2 %copy-start.5 = (f32[128,1280]{1,0:T(8,128)S(1)}, f32[128,1280]{1,0:T(8,128)}, u32[]{:S(2)}) copy-start(f32[128,1280]{1,0:T(8,128)} %fusion.6) | copy-start | bytes 1966084
  54.3 13.2 %collective-permute-start.6 = (bf16[128,1280]{1,0:T(8,128)(2,1)}, bf16[128,1280]{1,0:T(8,128)(2,1)S(1)}, u32[]{:S(2)}, u32[]{:S(2)}) collective-permute-start(bf16[128,1280]{1,0:T(8,128)(2,1)} %fusion.37), channel_id=1, source_target_pairs={{0,3},{1,0},{2,1},{3,2},{4,7},{5,4},{6,5},{7,6},{8,11},{9,8},{10,9... | collective-permute-start | bytes 983048 | tf_op jit(solution)/shard_map/ppermute | solution.py:16
  68.7 49.7 %collective-permute-start.14 = (bf16[640,1280]{1,0:T(8,128)(2,1)}, bf16[640,1280]{1,0:T(8,128)(2,1)S(1)}, u32[]{:S(2)}, u32[]{:S(2)}) collective-permute-start(bf16[640,1280]{1,0:T(8,128)(2,1)} %collective-permute-done.13), channel_id=1, source_target_pairs={{0,4},{4,0},{8,12},{12,8},{1,5},{5,1},{9,13},{13,9},{2,6},{6,2},{1... | collective-permute-start | bytes 4915208 | tf_op jit(solution)/shard_map/ppermute | solution.py:21
  69.2 32.7 %collective-permute-start.9 = (bf16[1,64,1280]{2,1,0:T(8,128)(2,1)S(1)}, bf16[1,64,1280]{2,1,0:T(8,128)(2,1)S(1)}, u32[]{:S(2)}, u32[]{:S(2)}) collective-permute-start(bf16[1,64,1280]{2,1,0:T(8,128)(2,1)S(1)} %slice.151), channel_id=1, source_target_pairs={{0,16},{1,17},{2,18},{3,19},{4,20},{5,21},{6,22},{7,23},{8,24},{9,... | collective-permute-start | bytes 491528 | tf_op jit(solution)/shard_map/ppermute | solution.py:124
  72.6 45.8 %copy-start.2 = (bf16[1,1280,1280]{2,1,0:T(8,128)(2,1)S(1)}, bf16[1,1280,1280]{2,1,0:T(8,128)(2,1)}, u32[]{:S(2)}) copy-start(bf16[1,1280,1280]{2,1,0:T(8,128)(2,1)} %param.12) | copy-start | bytes 9830404
  101.9 8.6 %collective-permute-start.12 = (bf16[64,1280]{1,0:T(8,128)(2,1)S(1)}, bf16[64,1280]{1,0:T(8,128)(2,1)S(1)}, u32[]{:S(2)}, u32[]{:S(2)}) collective-permute-start(bf16[64,1280]{1,0:T(8,128)(2,1)S(1)} %fusion.291), channel_id=1, source_target_pairs={{0,3},{1,0},{2,1},{3,2},{4,7},{5,4},{6,5},{7,6},{8,11},{9,8},{10,9... | collective-permute-start | bytes 491528 | tf_op jit(solution)/shard_map/ppermute | solution.py:16
  105.8 12.3 %collective-permute-start.11 = (bf16[64,1280]{1,0:T(8,128)(2,1)S(1)}, bf16[64,1280]{1,0:T(8,128)(2,1)S(1)}, u32[]{:S(2)}, u32[]{:S(2)}) collective-permute-start(bf16[64,1280]{1,0:T(8,128)(2,1)S(1)} %fusion.291), channel_id=1, source_target_pairs={{0,2},{1,3},{2,0},{3,1},{4,6},{5,7},{6,4},{7,5},{8,10},{9,11},{10,... | collective-permute-start | bytes 491528 | tf_op jit(solution)/shard_map/ppermute | solution.py:16
  105.8 12.3 %collective-permute-start.10 = (bf16[64,1280]{1,0:T(8,128)(2,1)S(1)}, bf16[64,1280]{1,0:T(8,128)(2,1)S(1)}, u32[]{:S(2)}, u32[]{:S(2)}) collective-permute-start(bf16[64,1280]{1,0:T(8,128)(2,1)S(1)} %fusion.291), channel_id=1, source_target_pairs={{0,1},{1,2},{2,3},{3,0},{4,5},{5,6},{6,7},{7,4},{8,9},{9,10},{10,1... | collective-permute-start | bytes 491528 | tf_op jit(solution)/shard_map/ppermute | solution.py:16
  118.3 6.8 %collective-permute-start.16 = (bf16[640,1280]{1,0:T(8,128)(2,1)}, bf16[640,1280]{1,0:T(8,128)(2,1)S(1)}, u32[]{:S(2)}, u32[]{:S(2)}) collective-permute-start(bf16[640,1280]{1,0:T(8,128)(2,1)} %collective-permute-done.15), channel_id=1, source_target_pairs={{0,4},{4,0},{8,12},{12,8},{1,5},{5,1},{9,13},{13,9},{2,6},{6,2},{1... | collective-permute-start | bytes 4915208 | tf_op jit(solution)/shard_map/ppermute | solution.py:21
  118.4 6.7 %copy-start.4 = (bf16[1,1280,1280]{2,1,0:T(8,128)(2,1)S(1)}, bf16[1,1280,1280]{2,1,0:T(8,128)(2,1)}, u32[]{:S(2)}) copy-start(bf16[1,1280,1280]{2,1,0:T(8,128)(2,1)} %param.13) | copy-start | bytes 9830404
  125.1 12.0 %copy-start.7 = (bf16[640,1280]{1,0:T(8,128)(2,1)}, bf16[640,1280]{1,0:T(8,128)(2,1)S(1)}, u32[]{:S(2)}) copy-start(bf16[640,1280]{1,0:T(8,128)(2,1)S(1)} %collective-permute-done.16) | copy-start | bytes 4915204
  128.7 4.8 %collective-permute-start.18 = (f32[4,1,1280]{2,0,1:T(4,128)S(1)}, f32[4,1,1280]{2,0,1:T(4,128)S(1)}, u32[]{:S(2)}, u32[]{:S(2)}) collective-permute-start(f32[4,1,1280]{2,0,1:T(4,128)S(1)} %bitcast.139), channel_id=1, source_target_pairs={{0,2},{1,3},{2,0},{3,1},{4,6},{5,7},{6,4},{7,5},{8,10},{9,11},{10,... | collective-permute-start | bytes 61448 | tf_op jit(solution)/shard_map/ppermute | solution.py:16
  130.7 3.8 %collective-permute-start.19 = (f32[4,1,1280]{2,0,1:T(4,128)S(1)}, f32[4,1,1280]{2,0,1:T(4,128)S(1)}, u32[]{:S(2)}, u32[]{:S(2)}) collective-permute-start(f32[4,1,1280]{2,0,1:T(4,128)S(1)} %bitcast.140), channel_id=1, source_target_pairs={{0,3},{1,0},{2,1},{3,2},{4,7},{5,4},{6,5},{7,6},{8,11},{9,8},{10,9... | collective-permute-start | bytes 61448 | tf_op jit(solution)/shard_map/ppermute | solution.py:16
  131.2 5.6 %collective-permute-start.17 = (f32[4,1,1280]{2,0,1:T(4,128)S(1)}, f32[4,1,1280]{2,0,1:T(4,128)S(1)}, u32[]{:S(2)}, u32[]{:S(2)}) collective-permute-start(f32[4,1,1280]{2,0,1:T(4,128)S(1)} %bitcast.141), channel_id=1, source_target_pairs={{0,1},{1,2},{2,3},{3,0},{4,5},{5,6},{6,7},{7,4},{8,9},{9,10},{10,1... | collective-permute-start | bytes 61448 | tf_op jit(solution)/shard_map/ppermute | solution.py:16
  144.7 9.1 %collective-permute-start.22 = (bf16[64,1280]{1,0:T(8,128)(2,1)S(1)}, bf16[64,1280]{1,0:T(8,128)(2,1)S(1)}, u32[]{:S(2)}, u32[]{:S(2)}) collective-permute-start(bf16[64,1280]{1,0:T(8,128)(2,1)S(1)} %get-tuple-element.16), channel_id=1, source_target_pairs={{0,1},{1,2},{2,3},{3,0},{4,5},{5,6},{6,7},{7,4},{8,9},{9,10},{10,1... | collective-permute-start | bytes 491528 | tf_op jit(solution)/shard_map/ppermute | solution.py:16
  144.8 13.8 %collective-permute-start.21 = (bf16[64,1280]{1,0:T(8,128)(2,1)S(1)}, bf16[64,1280]{1,0:T(8,128)(2,1)S(1)}, u32[]{:S(2)}, u32[]{:S(2)}) collective-permute-start(bf16[64,1280]{1,0:T(8,128)(2,1)S(1)} %get-tuple-element.17), channel_id=1, source_target_pairs={{0,2},{1,3},{2,0},{3,1},{4,6},{5,7},{6,4},{7,5},{8,10},{9,11},{10,... | collective-permute-start | bytes 491528 | tf_op jit(solution)/shard_map/ppermute | solution.py:16
  145.6 13.0 %collective-permute-start.20 = (bf16[64,1280]{1,0:T(8,128)(2,1)S(1)}, bf16[64,1280]{1,0:T(8,128)(2,1)S(1)}, u32[]{:S(2)}, u32[]{:S(2)}) collective-permute-start(bf16[64,1280]{1,0:T(8,128)(2,1)S(1)} %get-tuple-element.15), channel_id=1, source_target_pairs={{0,3},{1,0},{2,1},{3,2},{4,7},{5,4},{6,5},{7,6},{8,11},{9,8},{10,9... | collective-permute-start | bytes 491528 | tf_op jit(solution)/shard_map/ppermute | solution.py:16
  159.7 13.5 %collective-permute-start.23 = (bf16[64,1280]{1,0:T(8,128)(2,1)S(1)}, bf16[64,1280]{1,0:T(8,128)(2,1)S(1)}, u32[]{:S(2)}, u32[]{:S(2)}) collective-permute-start(bf16[64,1280]{1,0:T(8,128)(2,1)S(1)} %get-tuple-element.9), channel_id=1, source_target_pairs={{0,1},{1,2},{2,3},{3,0},{4,5},{5,6},{6,7},{7,4},{8,9},{9,10},{10,1... | collective-permute-start | bytes 491528 | tf_op jit(solution)/shard_map/ppermute | solution.py:16
  168.3 9.5 %collective-permute-start.24 = (bf16[64,1280]{1,0:T(8,128)(2,1)S(1)}, bf16[64,1280]{1,0:T(8,128)(2,1)S(1)}, u32[]{:S(2)}, u32[]{:S(2)}) collective-permute-start(bf16[64,1280]{1,0:T(8,128)(2,1)S(1)} %get-tuple-element.9), channel_id=1, source_target_pairs={{0,2},{1,3},{2,0},{3,1},{4,6},{5,7},{6,4},{7,5},{8,10},{9,11},{10,... | collective-permute-start | bytes 491528 | tf_op jit(solution)/shard_map/ppermute | solution.py:16
  168.3 12.8 %collective-permute-start.25 = (bf16[64,1280]{1,0:T(8,128)(2,1)S(1)}, bf16[64,1280]{1,0:T(8,128)(2,1)S(1)}, u32[]{:S(2)}, u32[]{:S(2)}) collective-permute-start(bf16[64,1280]{1,0:T(8,128)(2,1)S(1)} %get-tuple-element.9), channel_id=1, source_target_pairs={{0,3},{1,0},{2,1},{3,2},{4,7},{5,4},{6,5},{7,6},{8,11},{9,8},{10,9... | collective-permute-start | bytes 491528 | tf_op jit(solution)/shard_map/ppermute | solution.py:16
  170.7 11.1 %collective-permute-start.26 = (bf16[64,1280]{1,0:T(8,128)(2,1)S(1)}, bf16[64,1280]{1,0:T(8,128)(2,1)S(1)}, u32[]{:S(2)}, u32[]{:S(2)}) collective-permute-start(bf16[64,1280]{1,0:T(8,128)(2,1)S(1)} %get-tuple-element.9), channel_id=1, source_target_pairs={{0,16},{16,0},{1,17},{17,1},{2,18},{18,2},{3,19},{19,3},{4,20},{20... | collective-permute-start | bytes 491528 | tf_op jit(solution)/shard_map/ppermute | solution.py:166
  173.3 9.3 %collective-permute-start.27 = (bf16[64,1280]{1,0:T(8,128)(2,1)S(1)}, bf16[64,1280]{1,0:T(8,128)(2,1)S(1)}, u32[]{:S(2)}, u32[]{:S(2)}) collective-permute-start(bf16[64,1280]{1,0:T(8,128)(2,1)S(1)} %collective-permute-done.23), channel_id=1, source_target_pairs={{0,16},{16,0},{1,17},{17,1},{2,18},{18,2},{3,19},{19,3},{4,20},{20... | collective-permute-start | bytes 491528 | tf_op jit(solution)/shard_map/ppermute | solution.py:166
  177.8 7.6 %collective-permute-start.28 = (bf16[64,1280]{1,0:T(8,128)(2,1)S(1)}, bf16[64,1280]{1,0:T(8,128)(2,1)S(1)}, u32[]{:S(2)}, u32[]{:S(2)}) collective-permute-start(bf16[64,1280]{1,0:T(8,128)(2,1)S(1)} %collective-permute-done.24), channel_id=1, source_target_pairs={{0,16},{16,0},{1,17},{17,1},{2,18},{18,2},{3,19},{19,3},{4,20},{20... | collective-permute-start | bytes 491528 | tf_op jit(solution)/shard_map/ppermute | solution.py:166
  181.1 6.4 %collective-permute-start.29 = (bf16[64,1280]{1,0:T(8,128)(2,1)S(1)}, bf16[64,1280]{1,0:T(8,128)(2,1)S(1)}, u32[]{:S(2)}, u32[]{:S(2)}) collective-permute-start(bf16[64,1280]{1,0:T(8,128)(2,1)S(1)} %collective-permute-done.25), channel_id=1, source_target_pairs={{0,16},{16,0},{1,17},{17,1},{2,18},{18,2},{3,19},{19,3},{4,20},{20... | collective-permute-start | bytes 491528 | tf_op jit(solution)/shard_map/ppermute | solution.py:166
  197.6 9.7 %collective-permute-start.30 = (bf16[2,160,1280]{2,1,0:T(8,128)(2,1)}, bf16[2,160,1280]{2,1,0:T(8,128)(2,1)}, u32[]{:S(2)}, u32[]{:S(2)}) collective-permute-start(bf16[2,160,1280]{2,1,0:T(8,128)(2,1)} %dynamic-slice_bitcast_fusion.3), channel_id=1, source_target_pairs={{0,4},{4,0},{8,12},{12,8},{1,5},{5,1},{9,13},{13,9},{2,6},{6,2},{1... | collective-permute-start | bytes 2457608 | tf_op jit(solution)/shard_map/ppermute | solution.py:21
  206.8 3.4 %collective-permute-start.32 = (bf16[2,160,1280]{2,1,0:T(8,128)(2,1)}, bf16[2,160,1280]{2,1,0:T(8,128)(2,1)}, u32[]{:S(2)}, u32[]{:S(2)}) collective-permute-start(bf16[2,160,1280]{2,1,0:T(8,128)(2,1)} %dynamic-slice_bitcast_fusion.2), channel_id=1, source_target_pairs={{0,4},{4,0},{8,12},{12,8},{1,5},{5,1},{9,13},{13,9},{2,6},{6,2},{1... | collective-permute-start | bytes 2457608 | tf_op jit(solution)/shard_map/ppermute | solution.py:21
  208.7 12.4 %collective-permute-start.31 = (bf16[160,1280]{1,0:T(8,128)(2,1)S(1)}, bf16[160,1280]{1,0:T(8,128)(2,1)S(1)}, u32[]{:S(2)}, u32[]{:S(2)}) collective-permute-start(bf16[160,1280]{1,0:T(8,128)(2,1)S(1)} %fusion.142), channel_id=1, source_target_pairs={{0,8},{4,12},{8,0},{12,4},{1,9},{5,13},{9,1},{13,5},{2,10},{6,14},... | collective-permute-start | bytes 1228808 | tf_op jit(solution)/shard_map/ppermute | solution.py:16
  211.6 17.3 %collective-permute-start.33 = (bf16[160,1280]{1,0:T(8,128)(2,1)S(1)}, bf16[160,1280]{1,0:T(8,128)(2,1)S(1)}, u32[]{:S(2)}, u32[]{:S(2)}) collective-permute-start(bf16[160,1280]{1,0:T(8,128)(2,1)S(1)} %fusion.143), channel_id=1, source_target_pairs={{0,8},{4,12},{8,0},{12,4},{1,9},{5,13},{9,1},{13,5},{2,10},{6,14},... | collective-permute-start | bytes 1228808 | tf_op jit(solution)/shard_map/ppermute | solution.py:16

commit v2 on v1

v2 whole, which is shorter than its diff:
```python
import functools
import math

import jax
import jax.numpy as jnp
from jax import lax
from jax.experimental import pallas as pl
from jax.experimental.pallas import tpu as pltpu
from jax.sharding import PartitionSpec as P

STEPS = 50


EPS = 1e-06
VMEM_BYTES = 48 * 1024 * 1024
POOL_ROWS = 8


def rotated(value, axis, steps):
    count = lax.axis_size(axis)
    return lax.ppermute(value, axis, [(i, (i + steps) % count) for i in range(count)])


def swapped(value, axis, bit):
    count = lax.axis_size(axis)
    return lax.ppermute(value, axis, [(i, i ^ bit) for i in range(count)])


def gather_parts(piece):
    return [piece] + [rotated(piece, "tp", k) for k in range(1, lax.axis_size("tp"))]


def reduce_parts(parts):
    total = parts[0].astype(jnp.float32)
    for k in range(1, len(parts)):
        total = total + rotated(parts[k], "tp", -k).astype(jnp.float32)
    return total


def assemble_body(place_ref, *refs):
    pieces, out, sems = refs[:4], refs[4], refs[5]
    rows = pieces[0].shape[0]
    copies = []
    for q, piece in enumerate(pieces):
        start = pl.multiple_of((place_ref[0] ^ q) * rows, rows)
        copies.append(pltpu.make_async_copy(piece, out.at[pl.ds(start, rows), :], sems.at[q]))
    for copy in copies:
        copy.start()
    for copy in copies:
        copy.wait()


def from_other_section(weight):
    place = lax.axis_index("dp") % 4
    rows = weight.shape[0] // 4
    piece = lax.dynamic_slice_in_dim(weight, place * rows, rows, 0)
    got = swapped(piece, "sec", 1)
    beside = swapped(got, "dp", 1)
    across = swapped(got, "dp", 2)
    diagonal = swapped(across, "dp", 1)
    return pl.pallas_call(
        assemble_body,
        grid_spec=pltpu.PrefetchScalarGridSpec(
            num_scalar_prefetch=1,
            grid=(1,),
            in_specs=[pl.BlockSpec(memory_space=pl.ANY)] * 4,
            out_specs=pl.BlockSpec(memory_space=pl.ANY),
            scratch_shapes=[pltpu.SemaphoreType.DMA((4,))],
        ),
        out_shape=jax.ShapeDtypeStruct(weight.shape, weight.dtype),
        name="assemble",
    )(place.astype(jnp.int32)[None], got, beside, across, diagonal)


def gelu_pair(value):
    cdf = 0.5 * (1.0 + lax.erf(value * (1.0 / math.sqrt(2.0))))
    density = jnp.exp(-0.5 * value * value) * (1.0 / math.sqrt(2.0 * math.pi))
    return (value * cdf, cdf + value * density)


def normed(rows, gain):
    scale = lax.rsqrt(jnp.mean(rows * rows, axis=-1, keepdims=True) + EPS)
    return (rows * scale * gain).astype(jnp.bfloat16)


def dot_nn(a, b):
    return jnp.dot(a, b, preferred_element_type=jnp.float32)


def dot_nt(a, b):
    return lax.dot_general(a, b, (((1,), (1,)), ((), ())), preferred_element_type=jnp.float32)


def tile_of(hidden):
    for tile in (256, 128):
        if hidden % tile == 0:
            return tile
    return hidden


def whole(shape):
    return pl.BlockSpec(shape, lambda h, sel: (0,) * len(shape))


def columns(rows, tile):
    return pl.BlockSpec((rows, tile), lambda h, sel: (0, h))


def chosen(rows, tile, section):
    return pl.BlockSpec((rows, tile), lambda h, sel: (0, jnp.where(sel[0] == section, h, 0)))


def run(body, name, steps, sel, operands, in_specs, outs, out_specs, scratch, flops, elements=0):
    read = sum(x.size * x.dtype.itemsize for x in operands)
    written = sum(math.prod(o.shape) * o.dtype.itemsize for o in outs)
    return pl.pallas_call(
        body,
        grid_spec=pltpu.PrefetchScalarGridSpec(
            num_scalar_prefetch=1,
            grid=(steps,),
            in_specs=in_specs,
            out_specs=out_specs,
            scratch_shapes=scratch,
        ),
        out_shape=outs,
        compiler_params=pltpu.CompilerParams(
            dimension_semantics=("arbitrary",), vmem_limit_bytes=VMEM_BYTES
        ),
        cost_estimate=pl.CostEstimate(
            flops=flops, bytes_accessed=read + written, transcendentals=elements
        ),
        name=name,
    )(sel, *operands)


def bf16(*shape):
    return jax.ShapeDtypeStruct(shape, jnp.bfloat16)


def partial_body(count, sel_ref, *refs):
    parts, (gain, w_in, w_out) = refs[:count], refs[count : count + 3]
    outs, (xn, acc) = refs[count + 3 : 2 * count + 3], refs[2 * count + 3 :]
    h = pl.program_id(0)
    rows = parts[0].shape[0]

    @pl.when(h == 0)
    def _():
        for i, part in enumerate(parts):
            xn[i * rows : (i + 1) * rows, :] = normed(part[...].astype(jnp.float32), gain[...])
        acc[...] = jnp.zeros_like(acc)

    act, unused = gelu_pair(dot_nn(xn[...], w_in[...]))
    acc[...] += dot_nt(act.astype(jnp.bfloat16), w_out[...])

    @pl.when(h == pl.num_programs(0) - 1)
    def _():
        for i, out in enumerate(outs):
            out[...] = acc[i * rows : (i + 1) * rows, :].astype(jnp.bfloat16)


def block0_partials(parts, gain, w_in, w_out, sel):
    rows, width = parts[0].shape
    hidden = w_in.shape[1]
    tile, n = tile_of(hidden), len(parts)
    return run(
        functools.partial(partial_body, n),
        "block0_partial",
        hidden // tile,
        sel,
        [*parts, gain, w_in, w_out],
        [whole((rows, width))] * n
        + [whole((1, width)), columns(width, tile), columns(width, tile)],
        [bf16(rows, width)] * n,
        [whole((rows, width))] * n,
        [
            pltpu.VMEM((n * rows, width), jnp.bfloat16),
            pltpu.VMEM((n * rows, width), jnp.float32),
        ],
        4 * n * rows * width * hidden,
        n * rows * hidden,
    )


def state_body(sel_ref, part, gain, own_in, other_in, act, slope, xn_cols, xn):
    h = pl.program_id(0)
    rows = part.shape[0]
    late = rows // 2
    share = xn_cols.shape[0]
    first = sel_ref[0] == 0

    @pl.when(h == 0)
    def _():
        mine = pl.multiple_of(jnp.where(first, late, 0), late)
        theirs = pl.multiple_of(jnp.where(first, 0, late), late)
        for i, start in enumerate((mine, theirs)):
            xn[i * late : (i + 1) * late, :] = normed(
                part[pl.ds(start, late), :].astype(jnp.float32), gain[...]
            )
        cols = xn[:, pl.ds(pl.multiple_of(sel_ref[0] * share, share), share)]
        xn_cols[...] = cols.T

    def work(weight):
        value, grad = gelu_pair(dot_nn(xn[...], weight[...]))
        act[...] = value.astype(jnp.bfloat16)
        slope[...] = grad.astype(jnp.bfloat16)

    @pl.when(first)
    def _():
        work(own_in)

    @pl.when(jnp.logical_not(first))
    def _():
        work(other_in)


def block0_state(part, gain, own_in, other_in, sel):
    rows, width = part.shape
    hidden = own_in.shape[1]
    tile = tile_of(hidden)
    return run(
        state_body,
        "block0_state",
        hidden // tile,
        sel,
        [part, gain, own_in, other_in],
        [whole((rows, width)), whole((1, width)), chosen(width, tile, 0), chosen(width, tile, 1)],
        [bf16(rows, hidden), bf16(rows, hidden), bf16(width // 2, rows)],
        [columns(rows, tile), columns(rows, tile), whole((width // 2, rows))],
        [pltpu.VMEM((rows, width), jnp.bfloat16)],
        2 * rows * width * hidden,
        2 * rows * hidden,
    )


def reward_body(count, tokens, sel_ref, *refs):
    parts = refs[:count]
    gain, own_in, own_out, other_in, other_out = refs[count : count + 5]
    slopes = refs[count + 5 : 2 * count + 5]
    pools = refs[2 * count + 5 : 3 * count + 5]
    xn = refs[3 * count + 5]
    h = pl.program_id(0)
    rows = parts[0].shape[0]

    @pl.when(h == 0)
    def _():
        for i, part in enumerate(parts):
            xn[i * rows : (i + 1) * rows, :] = normed(part[...].astype(jnp.float32), gain[...])
            pools[i][...] = jnp.zeros_like(pools[i])

    def work(w_in, w_out):
        act, grad = gelu_pair(dot_nn(xn[...], w_in[...]))
        for i in range(count):
            slopes[i][...] = grad[i * rows : (i + 1) * rows, :].astype(jnp.bfloat16)
            row = lax.broadcasted_iota(jnp.int32, (POOL_ROWS, act.shape[1]), 0)
            means = jnp.zeros((POOL_ROWS, act.shape[1]), jnp.float32)
            for image in range(rows // tokens):
                start = i * rows + image * tokens
                mean = jnp.mean(act[start : start + tokens, :], axis=0, keepdims=True)
                means = jnp.where(row == image, mean, means)
            pools[i][...] += dot_nt(means.astype(jnp.bfloat16), w_out[...])

    @pl.when(sel_ref[0] == 1)
    def _():
        work(own_in, own_out)

    @pl.when(sel_ref[0] == 0)
    def _():
        work(other_in, other_out)


def reward_forward(parts, tokens, gain, own, other, sel):
    rows, width = parts[0].shape
    hidden = own[0].shape[1]
    tile, n = tile_of(hidden), len(parts)
    outs = run(
        functools.partial(reward_body, n, tokens),
        "reward_forward",
        hidden // tile,
        sel,
        [*parts, gain, *own, *other],
        [whole((rows, width))] * n
        + [whole((1, width))]
        + [chosen(width, tile, 1)] * 2
        + [chosen(width, tile, 0)] * 2,
        [bf16(rows, hidden)] * n + [jax.ShapeDtypeStruct((POOL_ROWS, width), jnp.float32)] * n,
        [columns(rows, tile)] * n + [whole((POOL_ROWS, width))] * n,
        [pltpu.VMEM((n * rows, width), jnp.bfloat16)],
        2 * n * rows * width * hidden,
        2 * n * rows * hidden,
    )
    return outs[:n], outs[n:]


def back_body(count, tokens, sel_ref, *refs):
    g_tok = refs[0]
    slopes = refs[1 : count + 1]
    own_in, own_out, other_in, other_out = refs[count + 1 : count + 5]
    outs = refs[count + 5 : 2 * count + 5]
    acc = refs[2 * count + 5]
    h = pl.program_id(0)
    rows = slopes[0].shape[0]
    per = rows // tokens

    @pl.when(h == 0)
    def _():
        acc[...] = jnp.zeros_like(acc)

    def work(w_in, w_out):
        g_h = dot_nn(g_tok[...], w_out[...])
        terms = []
        for i in range(count):
            for image in range(per):
                at = i * per + image
                slope = slopes[i][image * tokens : (image + 1) * tokens, :].astype(jnp.float32)
                terms.append((slope * g_h[at : at + 1, :]).astype(jnp.bfloat16))
        acc[...] += dot_nt(jnp.concatenate(terms, axis=0), w_in[...])

    @pl.when(sel_ref[0] == 1)
    def _():
        work(own_in, own_out)

    @pl.when(sel_ref[0] == 0)
    def _():
        work(other_in, other_out)

    @pl.when(h == pl.num_programs(0) - 1)
    def _():
        for i, out in enumerate(outs):
            out[...] = acc[i * rows : (i + 1) * rows, :].astype(jnp.bfloat16)


def reward_back(g_tok, slopes, tokens, own, other, sel):
    rows, hidden = slopes[0].shape
    width = own[0].shape[0]
    tile, n = tile_of(hidden), len(slopes)
    return run(
        functools.partial(back_body, n, tokens),
        "reward_back",
        hidden // tile,
        sel,
        [g_tok, *slopes, *own, *other],
        [whole(g_tok.shape)]
        + [columns(rows, tile)] * n
        + [chosen(width, tile, 1)] * 2
        + [chosen(width, tile, 0)] * 2,
        [bf16(rows, width)] * n,
        [whole((rows, width))] * n,
        [pltpu.VMEM((n * rows, width), jnp.float32)],
        2 * n * rows * width * hidden,
    )


def put_rows(result, core, keep, away):
    groups, rows, unused = keep.shape
    for g in range(groups):
        even = result[2 * g * rows : (2 * g + 1) * rows, :]
        odd = result[(2 * g + 1) * rows : (2 * g + 2) * rows, :]
        keep[g] = jnp.where(core == 0, even, odd).astype(jnp.bfloat16)
        away[g] = jnp.where(core == 0, odd, even).astype(jnp.bfloat16)


def grad_out_body(count, sel_ref, *refs):
    pieces, acts = refs[: 2 * count], refs[2 * count : 3 * count]
    keep, away, turned = refs[3 * count :]
    share = turned.shape[0]

    @pl.when(pl.program_id(0) == 0)
    def _():
        start = pl.multiple_of(sel_ref[0] * share, share)
        cols = jnp.concatenate([piece[:, pl.ds(start, share)] for piece in pieces], axis=0)
        turned[...] = cols.T

    act = jnp.concatenate([part[...] for part in acts], axis=0)
    put_rows(dot_nn(turned[...], act), sel_ref[1], keep, away)


def grad_in_body(count, sel_ref, *refs):
    pieces, slopes = refs[: 2 * count], refs[2 * count : 3 * count]
    xn_cols = refs[3 * count : 4 * count]
    own_out, other_out, keep, away, g_all, turned, g_hidden = refs[4 * count :]
    rows = pieces[0].shape[0]
    wide = xn_cols[0].shape[1]

    @pl.when(pl.program_id(0) == 0)
    def _():
        for i, piece in enumerate(pieces):
            g_all[i * rows : (i + 1) * rows, :] = piece[...]
        for i, part in enumerate(xn_cols):
            turned[:, i * wide : (i + 1) * wide] = part[...]

    def work(weight):
        g_h = dot_nn(g_all[...], weight[...])
        slope = jnp.concatenate([part[...] for part in slopes], axis=0).astype(jnp.float32)
        g_hidden[...] = (g_h * slope).astype(jnp.bfloat16)

    @pl.when(sel_ref[0] == 0)
    def _():
        work(own_out)

    @pl.when(sel_ref[0] == 1)
    def _():
        work(other_out)

    put_rows(dot_nn(turned[...], g_hidden[...]), sel_ref[1], keep, away)


def gradient_call(body, name, pieces, states, extra, extra_specs, scratch, sel, flops):
    rows, width = pieces[0].shape
    hidden = states[0].shape[1]
    tile = tile_of(hidden)
    groups = lax.axis_size("dp") // 2
    cut = (groups, width // 2 // (2 * groups))
    return run(
        body,
        name,
        hidden // tile,
        sel,
        [*pieces, *states, *extra],
        [whole((rows, width))] * len(pieces)
        + [columns(states[0].shape[0], tile)] * len(states)
        + extra_specs,
        [bf16(*cut, hidden)] * 2,
        [pl.BlockSpec((*cut, tile), lambda h, sel: (0, 0, h))] * 2,
        scratch,
        flops,
    )


def grad_out_parts(pieces, acts, sel):
    rows, width = pieces[0].shape
    total = rows * len(pieces)
    return gradient_call(
        functools.partial(grad_out_body, len(acts)),
        "grad_out",
        pieces,
        acts,
        [],
        [],
        [pltpu.VMEM((width // 2, total), jnp.bfloat16)],
        sel,
        total * width * acts[0].shape[1],
    )


def grad_in_parts(pieces, slopes, xn_cols, own_out, other_out, sel):
    rows, width = pieces[0].shape
    total = rows * len(pieces)
    hidden = slopes[0].shape[1]
    tile = tile_of(hidden)
    return gradient_call(
        functools.partial(grad_in_body, len(slopes)),
        "grad_in",
        pieces,
        slopes,
        [*xn_cols, own_out, other_out],
        [whole(xn_cols[0].shape)] * len(xn_cols)
        + [chosen(width, tile, 0), chosen(width, tile, 1)],
        [
            pltpu.VMEM((total, width), jnp.bfloat16),
            pltpu.VMEM((width // 2, total), jnp.bfloat16),
            pltpu.VMEM((total, tile), jnp.bfloat16),
        ],
        sel,
        3 * total * width * hidden,
    )


def sum_over_dp(keep, away):
    groups = keep.shape[0]
    place = lax.axis_index("dp") // 2
    chip = keep.astype(jnp.float32) + swapped(away, "dp", 1).astype(jnp.float32)
    total = lax.dynamic_index_in_dim(chip, place, 0, keepdims=False)
    sent = chip.astype(jnp.bfloat16)
    for k in range(1, groups):
        part = lax.dynamic_index_in_dim(sent, (place + k) % groups, 0, keepdims=False)
        total = total + rotated(part, "dp", 2 * k).astype(jnp.float32)
    return total


def score_of(pooled, text):
    unit_img = pooled * lax.rsqrt(jnp.mean(pooled * pooled, axis=-1, keepdims=True) + EPS)
    unit_txt = text * lax.rsqrt(jnp.mean(text * text, axis=-1, keepdims=True) + EPS)
    return 100.0 * jnp.sum(unit_img * unit_txt, axis=-1) / pooled.shape[-1]


def on_device(latents, timesteps, prompt_ids, prompt_table, gains, w_in, w_out):
    count, tokens, width = latents.shape
    half = count // 2
    n_tp = lax.axis_size("tp")
    segment = lax.axis_index("sec")
    first = segment == 0
    core = lax.axis_index("dp") % 2
    sel = jnp.stack([segment, core]).astype(jnp.int32)
    own = (w_in[0], w_out[0])
    theta = math.pi / 2.0 * (timesteps.astype(jnp.float32) + 1.0) / (STEPS + 1.0)
    alpha = jnp.cos(theta)[:, None, None]
    sigma = jnp.sin(theta)[:, None, None]

    flat = latents.reshape(count * tokens, width)
    lat_parts = gather_parts(flat)
    other = (from_other_section(own[0]), from_other_section(own[1]))

    onehot = (
        prompt_ids[:, None] == jnp.arange(prompt_table.shape[0], dtype=jnp.int32)[None, :]
    ).astype(jnp.bfloat16)
    text = dot_nn(onehot, prompt_table).astype(jnp.bfloat16)
    text_mine = jnp.where(first, text[half:], text[:half])
    text_all = jnp.concatenate(gather_parts(text_mine), 0).astype(jnp.float32)

    near = [k for k in range(1, n_tp) if 2 * k != n_tp]
    far = [k for k in range(1, n_tp) if 2 * k == n_tp]
    eps_parts = [None] * n_tp
    for ks in ([0], near, far):
        if ks:
            results = block0_partials([lat_parts[k] for k in ks], gains[:1], *own, sel)
            for k, result in zip(ks, results):
                eps_parts[k] = result
    eps_mix = reduce_parts(eps_parts).reshape(count, tokens, width)
    base = latents.astype(jnp.float32)
    images = ((base - sigma * (base + eps_mix)) / alpha).astype(jnp.bfloat16)

    arrived = lax.ppermute(images[:half], "sec", [(0, 1)])
    mine = jnp.where(first, images[half:], arrived)
    ratio = jnp.where(first, (sigma / alpha)[half:], (sigma / alpha)[:half])
    mine_rows = mine.reshape(half * tokens, width)
    seen_parts = gather_parts(mine_rows)
    slopes1, pool_parts = [None] * n_tp, [None] * n_tp
    for ks in ([0] + near, far):
        if ks:
            some_slopes, some_pools = reward_forward(
                [seen_parts[k] for k in ks], tokens, gains[1:], own, other, sel
            )
            for k, slope, pool in zip(ks, some_slopes, some_pools):
                slopes1[k], pool_parts[k] = slope, pool[:half]
    pool_part = jnp.stack(pool_parts)
    pool = pool_part
    for k in range(1, n_tp):
        pool = pool + jnp.roll(rotated(pool_part, "tp", k), k, axis=0)
    seen_mean = jnp.stack(
        [
            jnp.mean(part.astype(jnp.float32).reshape(half, tokens, width), axis=1)
            for part in seen_parts
        ]
    )
    pooled = (pool + seen_mean).reshape(n_tp * half, width)
    g_pooled = jax.grad(lambda p: -jnp.sum(score_of(p, text_all)))(pooled)
    g_mean = g_pooled / tokens
    padded = -(-n_tp * half // 16) * 16
    g_tok = jnp.pad(g_mean.astype(jnp.bfloat16), ((0, padded - n_tp * half), (0, 0)))
    g_xn = reduce_parts(reward_back(g_tok, slopes1, tokens, own, other, sel))
    seen = mine_rows.astype(jnp.float32)
    scale1 = lax.rsqrt(jnp.mean(seen * seen, axis=-1, keepdims=True) + EPS)
    weighted = gains[1] * g_xn
    g_norm = scale1 * weighted - seen * scale1**3 * jnp.mean(
        seen * weighted, axis=-1, keepdims=True
    )
    g_images = (g_mean[:half, None, :] + g_norm.reshape(half, tokens, width)).astype(jnp.bfloat16)
    g_eps = (-ratio * g_images.astype(jnp.float32)).astype(jnp.bfloat16)

    acts, slopes0, xn_cols = [], [], []
    for part in lat_parts:
        act, slope, cols = block0_state(part, gains[:1], own[0], other[0], sel)
        acts.append(act)
        slopes0.append(slope)
        xn_cols.append(cols)

    pieces = []
    for part in gather_parts(g_eps.reshape(half * tokens, width)):
        pieces += [part, swapped(part, "sec", 1)]
    grad_out = sum_over_dp(*grad_out_parts(pieces, acts, sel))
    grad_in = sum_over_dp(*grad_in_parts(pieces, slopes0, xn_cols, own[1], other[1], sel))
    return (grad_in, grad_out)


def solution(mesh):
    in_specs = (
        P(("dp", "tp"), None, None),
        P(("dp", "tp")),
        P(("dp", "tp")),
        P(),
        P(),
        P("sec", None, "tp"),
        P("sec", None, "tp"),
    )
    out_specs = (P(("sec", "dp"), "tp"), P(("sec", "dp"), "tp"))
    return jax.shard_map(
        on_device, mesh=mesh, in_specs=in_specs, out_specs=out_specs, check_vma=False
    )
```

time: 230 us -> 454 us (1.97); the launches traced: 230 us -> 448 us
  Pallas kernels: 0 us -> 271 us
  matrix products: 66 us -> 0.2 us
  waiting for transfers between devices: 88.9 us -> 100 us
  local copies, waits for them, and re-layouts: 13.3 us -> 20.8 us
  other arithmetic: 11.2 us -> 6.28 us
    pallas_call x0 -> x14, Pallas kernels: none -> 271 us  [the longest x2 201 us: from_other_section(): pl.pallas_call(assemble_body, grid_spec=pltpu.PrefetchScalarGridSpec(num_...]
    dot_general x8 -> x0, matrix products: 49.8 us -> none  [the longest x6 33 us: dot_nt(): lax.dot_general(a, b, (((1,), (1,)), ((), ())), preferred_element_type=jn...]
    ppermute x1, waiting for transfers between devices: 28.6 us -> 0.01 us  [on_device(): arrived = lax.ppermute(images[:half], 'sec', [(0, 1)])]
    ppermute x10 -> x14, waiting for transfers between devices: 3.64 us -> 25.6 us  [swapped(): return lax.ppermute(value, axis, [(i, i ^ bit) for i in range(count)])]
    ppermute x23, waiting for transfers between devices: 56.6 us -> 74.6 us  [rotated(): lax.ppermute(value, axis, [(i, (i + steps) % count) for i in range(count)])]
    dot_general x4 -> x1, matrix products: 16.3 us -> 0.2 us  [dot_nn(): return jnp.dot(a, b, preferred_element_type=jnp.float32)]
    unnamed x22 -> x100, local copies, waits for them, and re-layouts: 5.01 us -> 15.6 us
  transfers between devices with their start and end apart: 34 -> 38, of which waited for: 15 -> 18; matrix products, arithmetic and copies ran while one was open for 29% -> 2% of each run, Pallas kernels for 0% -> 32%
where the time goes in v2:
time: 454 us; the launch traced here: 448 us
  Pallas kernels  271 us (60%)
  waiting for transfers between devices  100 us (22%)
  starting transfers between devices  46.8 us (10%)
  local copies, waits for them, and re-layouts  20.8 us (5%)
  other arithmetic  6.28 us (1%)
    pallas_call x2, Pallas kernels, from_other_section(): pl.pallas_call(assemble_body, grid_spec=pltpu.PrefetchScalarGridSpec(num_...  201 us
    ppermute x23, waiting for transfers between devices, rotated(): lax.ppermute(value, axis, [(i, (i + steps) % count) for i in range(count)])  74.6 us
    pallas_call x12, Pallas kernels, run(): pl.pallas_call(body, grid_spec=pltpu.PrefetchScalarGridSpec(num_scalar_pr...  70.5 us
    ppermute x23, starting transfers between devices, rotated(): lax.ppermute(value, axis, [(i, (i + steps) % count) for i in range(count)])  36.7 us
    ppermute x14, waiting for transfers between devices, swapped(): return lax.ppermute(value, axis, [(i, i ^ bit) for i in range(count)])  25.6 us
    unnamed x100, local copies, waits for them, and re-layouts  15.6 us
  transfers between devices with their start and end apart: 38, of which 18 were waited for; matrix products, arithmetic and copies ran while one was open for 2% of the time, Pallas kernels for 32%

profile of v2, /device:TPU:0, one launch (start us, length us, event | category | flops | bytes accessed | tf_op | source)
XLA Modules:
  0.0 448.3 jit_solution(4410279910655443610)
XLA Ops:
  0.6 3.1 collective-permute-start.3
  3.7 2.1 collective-permute-start.4
  5.8 0.9 collective-permute-start.6
  6.8 2.2 dynamic-slice_bitcast_fusion
  9.0 1.5 collective-permute-start.16
  10.5 2.1 dynamic-slice_bitcast_fusion.1
  13.2 1.4 collective-permute-done.3.refs_0_.part
  14.7 5.6 %collective-permute-done.4.refs_1_.part = bf16[128,1280]{1,0:T(8,128)(2,1)} collective-permute-done((bf16[128,1280]{1,0:T(8,128)(2,1)}, bf16[128,1280]{1,0:T(8,128)(2,1)}, u32[]{:S(2)}, u32[]{:S(2)}) %collective-permute-start.4) | collective-permute-done | bytes 327712 | tf_op jit(solution)/shard_map/ppermute | solution.py:21
  20.2 8.1 %block0_partial.4 = (bf16[128,1280]{1,0:T(8,128)(2,1)}, bf16[128,1280]{1,0:T(8,128)(2,1)}) custom-call(s32[2]{0:T(128)S(1)} %pad_add_fusion.sel_ref, bf16[128,1280]{1,0:T(8,128)(2,1)} %collective-permute-done.3.refs_0_.part, bf16[128,1280]{1,0:T(8,128)(2,1)} %collective-permute-done.4.refs_1_.part, f32[1,1280]{1,0:T(1,128)S(1)} %get-tuple-element.83.refs_1_.refs_2_.gain, ...), custom_call_target="tpu_custom_call" | custom-call | flops 1677721600 | bytes 7869440 | tf_op jit(solution)/shard_map/block0_partial/pallas_call | solution.py:116
  28.3 3.3 collective-permute-start.5
  31.6 4.3 collective-permute-start.8
  35.9 2.6 collective-permute-done.6.refs_0_.part
  38.5 7.0 %block0_partial.5 = bf16[128,1280]{1,0:T(8,128)(2,1)} custom-call(s32[2]{0:T(128)S(1)} %pad_add_fusion.sel_ref, bf16[128,1280]{1,0:T(8,128)(2,1)} %collective-permute-done.6.refs_0_.part, f32[1,1280]{1,0:T(1,128)S(1)} %get-tuple-element.83.refs_1_.refs_2_.gain, bf16[1280,1280]{1,0:T(8,128)(2,1)S(1)} %bitcast.47, bf16[1280,1280]{1,0:T(8,128)(2,1)} %bitcast.62), custom_call_target="tpu_custom_call" | custom-call | flops 838860800 | bytes 7214080 | tf_op jit(solution)/shard_map/block0_partial/pallas_call | solution.py:116
  45.5 1.3 collective-permute-start.7
  46.9 1.0 copy-done.2
  47.8 6.2 %block0_partial.3 = bf16[128,1280]{1,0:T(8,128)(2,1)S(1)} custom-call(s32[2]{0:T(128)S(1)} %pad_add_fusion.sel_ref, bf16[128,1280]{1,0:T(8,128)(2,1)S(1)} %bitcast.59, f32[1,1280]{1,0:T(1,128)S(1)} %get-tuple-element.83.refs_1_.refs_2_.gain, bf16[1280,1280]{1,0:T(8,128)(2,1)S(1)} %bitcast.48, bf16[1280,1280]{1,0:T(8,128)(2,1)} %bitcast.63), custom_call_target="tpu_custom_call" | custom-call | flops 838860800 | bytes 7214080 | tf_op jit(solution)/shard_map/block0_partial/pallas_call | solution.py:116
  54.3 8.7 %collective-permute-done.7 = bf16[128,1280]{1,0:T(8,128)(2,1)} collective-permute-done((bf16[128,1280]{1,0:T(8,128)(2,1)}, bf16[128,1280]{1,0:T(8,128)(2,1)}, u32[]{:S(2)}, u32[]{:S(2)}) %collective-permute-start.7) | collective-permute-done | bytes 327712 | tf_op jit(solution)/shard_map/ppermute | solution.py:21
  63.0 1.3 convert_add_fusion.3
  64.6 3.4 collective-permute-start.9
  68.1 2.2 collective-permute-start.1
  70.3 3.2 collective-permute-done
  73.5 3.6 collective-permute-done.2
  77.3 1.6 collective-permute-start.18
  79.5 2.3 collective-permute-start.20
  81.9 4.8 %collective-permute-done.10.refs_1_ = bf16[64,1280]{1,0:T(8,128)(2,1)S(1)} collective-permute-done((bf16[64,1280]{1,0:T(8,128)(2,1)S(1)}, bf16[64,1280]{1,0:T(8,128)(2,1)S(1)}, u32[]{:S(2)}, u32[]{:S(2)}) %collective-permute-start.10) | collective-permute-done | bytes 163872 | tf_op jit(solution)/shard_map/ppermute | solution.py:21
  86.7 12.0 %collective-permute-done.18.refs_2_ = bf16[320,1280]{1,0:T(8,128)(2,1)S(1)} collective-permute-done((bf16[320,1280]{1,0:T(8,128)(2,1)}, bf16[320,1280]{1,0:T(8,128)(2,1)S(1)}, u32[]{:S(2)}, u32[]{:S(2)}) %collective-permute-start.18) | collective-permute-done | bytes 819232 | tf_op jit(solution)/shard_map/ppermute | solution.py:26
  98.7 13.5 %collective-permute-done.14.refs_2_ = bf16[320,1280]{1,0:T(8,128)(2,1)} collective-permute-done((bf16[320,1280]{1,0:T(8,128)(2,1)}, bf16[320,1280]{1,0:T(8,128)(2,1)}, u32[]{:S(2)}, u32[]{:S(2)}) %collective-permute-start.14) | collective-permute-done | bytes 819232 | tf_op jit(solution)/shard_map/ppermute | solution.py:26
  112.3 2.1 collective-permute-start.11
  114.5 4.4 collective-permute-done.11.refs_2_
  120.5 0.9 copy-done.46
  121.4 100.4 %assemble.3.refs_7_.refs_5_.refs_8_.refs_17_ = bf16[1280,1280]{1,0:T(8,128)(2,1)} custom-call(s32[1]{0:T(128)} %bitcast.11.place_ref, bf16[320,1280]{1,0:T(8,128)(2,1)} %collective-permute-done.16.refs_0_, bf16[320,1280]{1,0:T(8,128)(2,1)} %copy-done.45, bf16[320,1280]{1,0:T(8,128)(2,1)} %copy-done.44, bf16[320,1280]{1,0:T(8,128)(2,1)} %copy-done.46), custom_call_target="tpu_custom_call" | custom-call | tf_op jit(solution)/shard_map/assemble/pallas_call | solution.py:61
  221.9 100.4 %assemble.2.refs_6_.refs_4_.refs_7_.other_in = bf16[1280,1280]{1,0:T(8,128)(2,1)} custom-call(s32[1]{0:T(128)} %bitcast.11.place_ref, bf16[320,1280]{1,0:T(8,128)(2,1)} %collective-permute-done.12.refs_0_, bf16[320,1280]{1,0:T(8,128)(2,1)} %collective-permute-done.13.refs_1_, bf16[320,1280]{1,0:T(8,128)(2,1)} %collective-permute-done.14.refs_2_, ...), custom_call_target="tpu_custom_call" | custom-call | tf_op jit(solution)/shard_map/assemble/pallas_call | solution.py:61
  323.2 6.8 %reward_forward.3 = (bf16[64,1280]{1,0:T(8,128)(2,1)S(1)}, f32[8,1280]{1,0:T(8,128)S(1)}) custom-call(s32[2]{0:T(128)S(1)} %pad_add_fusion.sel_ref, bf16[64,1280]{1,0:T(8,128)(2,1)S(1)} %copy-done.7, f32[1,1280]{1,0:T(1,128)S(1)} %get-tuple-element.82.refs_3_.refs_1_, bf16[1280,1280]{1,0:T(8,128)(2,1)S(1)} %bitcast.49, bf16[1280,1280]{1,0:T(8,128)(2,1)} %bitcast.64, ...), custom_call_target="tpu_custom_call" | custom-call | flops 209715200 | bytes 13480960 | tf_op jit(solution)/shard_map/reward_forward/pallas_call | solution.py:116
  330.1 8.3 %reward_forward.2 = (bf16[64,1280]{1,0:T(8,128)(2,1)S(1)}, bf16[64,1280]{1,0:T(8,128)(2,1)S(1)}, bf16[64,1280]{1,0:T(8,128)(2,1)S(1)}, f32[8,1280]{1,0:T(8,128)S...) custom-call(s32[2]{0:T(128)S(1)} %pad_add_fusion.sel_ref, bf16[64,1280]{1,0:T(8,128)(2,1)S(1)} %copy-done.5, ...), custom_call_target="tpu_custom_call" | custom-call | flops 629145600 | bytes 14218240 | tf_op jit(solution)/shard_map/reward_forward/pallas_call | solution.py:116
  338.5 3.9 collective-permute-start.23
  343.9 4.2 collective-permute-done.21
  348.5 7.1 %reward_back.1 = (bf16[64,1280]{1,0:T(8,128)(2,1)S(1)}, bf16[64,1280]{1,0:T(8,128)(2,1)S(1)}, bf16[64,1280]{1,0:T(8,128)(2,1)S(1)}, bf16[64,1280]{1,0:T(8,128)(2,1)S(1)}) custom-call(s32[2]{0:T(128)S(1)} %pad_add_fusion.sel_ref, bf16[16,1280]{1,0:T(8,128)(2,1)S(1)} %pad.4.refs_0_, bf16[64,1280]{1,0:T(8,128)(2,1)S(1)} %get-tuple-element.38.refs_1_, ...), custom_call_target="tpu_custom_call" | custom-call | flops 838860800 | bytes 14458880 | tf_op jit(solution)/shard_map/reward_back/pallas_call | solution.py:116
  356.9 1.9 collective-permute-start.26
  361.4 9.1 %collective-permute-done.25 = bf16[64,1280]{1,0:T(8,128)(2,1)S(1)} collective-permute-done((bf16[64,1280]{1,0:T(8,128)(2,1)S(1)}, bf16[64,1280]{1,0:T(8,128)(2,1)S(1)}, u32[]{:S(2)}, u32[]{:S(2)}) %collective-permute-start.25) | collective-permute-done | bytes 163872 | tf_op jit(solution)/shard_map/ppermute | solution.py:21
  371.2 2.0 collective-permute-start.30
  373.2 2.8 collective-permute-start.32
  376.1 4.0 collective-permute-done.28.refs_2_
  380.0 4.4 collective-permute-done.30.refs_4_
  384.5 2.0 collective-permute-start.33
  386.5 3.9 block0_state.4
  391.2 4.0 block0_state.5
  395.9 4.0 block0_state.6
  400.7 4.0 block0_state.7
  405.7 3.9 grad_out.1
  410.8 0.9 copy-done.23
  411.7 0.9 copy-done.25
  412.6 0.9 copy-done.27
  413.5 0.9 copy-done.29
  414.4 0.9 copy-done.31
  415.4 0.9 copy-done.33
  416.3 0.9 copy-done.35
  417.2 0.9 copy-done.43
  418.1 7.1 %grad_in.1 = (bf16[2,160,1280]{2,1,0:T(8,128)(2,1)S(1)}, bf16[2,160,1280]{2,1,0:T(8,128)(2,1)S(1)}) custom-call(s32[2]{0:T(128)S(1)} %pad_add_fusion.sel_ref, bf16[64,1280]{1,0:T(8,128)(2,1)S(1)} %copy-done.9, bf16[64,1280]{1,0:T(8,128)(2,1)S(1)} %copy-done.29, bf16[64,1280]{1,0:T(8,128)(2,1)S(1)} %copy-done.23, bf16[64,1280]{1,0:T(8,128)(2,1)S(1)} %copy-done.31, ...), custom_call_target="tpu_custom_call" | custom-call | flops 2516582400 | bytes 11468800 | tf_op jit(solution)/shard_map/grad_in/pallas_call | solution.py:116
  425.7 1.3 convert_add_fusion
  427.0 1.5 collective-permute-start.37
  429.4 10.0 %collective-permute-done.37 = bf16[160,1280]{1,0:T(8,128)(2,1)S(1)} collective-permute-done((bf16[160,1280]{1,0:T(8,128)(2,1)S(1)}, bf16[160,1280]{1,0:T(8,128)(2,1)S(1)}, u32[]{:S(2)}, u32[]{:S(2)}) %collective-permute-start.37) | collective-permute-done | bytes 409632 | tf_op jit(solution)/shard_map/ppermute | solution.py:21
  439.4 1.0 bitcast_add_fusion
  440.4 6.9 %collective-permute-done.35 = bf16[160,1280]{1,0:T(8,128)(2,1)S(1)} collective-permute-done((bf16[160,1280]{1,0:T(8,128)(2,1)S(1)}, bf16[160,1280]{1,0:T(8,128)(2,1)S(1)}, u32[]{:S(2)}, u32[]{:S(2)}) %collective-permute-start.35) | collective-permute-done | bytes 409632 | tf_op jit(solution)/shard_map/ppermute | solution.py:21
  447.3 1.0 bitcast_add_fusion.1
  (176 shorter events, 15.0 us)
Async XLA Ops:
  0.6 53.4 %copy-start = (bf16[64,1280]{1,0:T(8,128)(2,1)S(1)}, bf16[64,1280]{1,0:T(8,128)(2,1)}, u32[]{:S(2)}) copy-start(bf16[64,1280]{1,0:T(8,128)(2,1)} %param.10) | copy-start | bytes 491524
  0.6 14.0 %collective-permute-start.3 = (bf16[128,1280]{1,0:T(8,128)(2,1)}, bf16[128,1280]{1,0:T(8,128)(2,1)}, u32[]{:S(2)}, u32[]{:S(2)}) collective-permute-start(bf16[128,1280]{1,0:T(8,128)(2,1)} %bitcast.56), channel_id=1, source_target_pairs={{0,1},{1,2},{2,3},{3,0},{4,5},{5,6},{6,7},{7,4},{8,9},{9,10},{10,1... | collective-permute-start | bytes 983048 | tf_op jit(solution)/shard_map/ppermute | solution.py:21
  3.7 16.5 %collective-permute-start.4 = (bf16[128,1280]{1,0:T(8,128)(2,1)}, bf16[128,1280]{1,0:T(8,128)(2,1)}, u32[]{:S(2)}, u32[]{:S(2)}) collective-permute-start(bf16[128,1280]{1,0:T(8,128)(2,1)} %bitcast.57), channel_id=1, source_target_pairs={{0,3},{1,0},{2,1},{3,2},{4,7},{5,4},{6,5},{7,6},{8,11},{9,8},{10,9... | collective-permute-start | bytes 983048 | tf_op jit(solution)/shard_map/ppermute | solution.py:21
  5.8 32.7 %collective-permute-start.6 = (bf16[128,1280]{1,0:T(8,128)(2,1)}, bf16[128,1280]{1,0:T(8,128)(2,1)}, u32[]{:S(2)}, u32[]{:S(2)}) collective-permute-start(bf16[128,1280]{1,0:T(8,128)(2,1)} %bitcast.58), channel_id=1, source_target_pairs={{0,2},{1,3},{2,0},{3,1},{4,6},{5,7},{6,4},{7,5},{8,10},{9,11},{10,... | collective-permute-start | bytes 983048 | tf_op jit(solution)/shard_map/ppermute | solution.py:21
  6.8 6.4 %copy-start.47 = (f32[2,1280]{1,0:T(2,128)S(1)}, f32[2,1280]{1,0:T(2,128)}, u32[]{:S(2)}) copy-start(f32[2,1280]{1,0:T(2,128)} %param.11) | copy-start | bytes 30724
  6.8 13.5 %copy-start.1 = (bf16[1,1280,1280]{2,1,0:T(8,128)(2,1)S(1)}, bf16[1,1280,1280]{2,1,0:T(8,128)(2,1)}, u32[]{:S(2)}) copy-start(bf16[1,1280,1280]{2,1,0:T(8,128)(2,1)} %param.12) | copy-start | bytes 9830404
  9.0 68.3 %collective-permute-start.16 = (bf16[320,1280]{1,0:T(8,128)(2,1)}, bf16[320,1280]{1,0:T(8,128)(2,1)}, u32[]{:S(2)}, u32[]{:S(2)}) collective-permute-start(bf16[320,1280]{1,0:T(8,128)(2,1)} %dynamic-slice_bitcast_fusion), channel_id=1, source_target_pairs={{0,16},{16,0},{1,17},{17,1},{2,18},{18,2},{3,19},{19,3},{4,20},{20... | collective-permute-start | bytes 2457608 | tf_op jit(solution)/shard_map/ppermute | solution.py:26
  12.6 66.2 %collective-permute-start.12 = (bf16[320,1280]{1,0:T(8,128)(2,1)}, bf16[320,1280]{1,0:T(8,128)(2,1)}, u32[]{:S(2)}, u32[]{:S(2)}) collective-permute-start(bf16[320,1280]{1,0:T(8,128)(2,1)} %dynamic-slice_bitcast_fusion.1), channel_id=1, source_target_pairs={{0,16},{16,0},{1,17},{17,1},{2,18},{18,2},{3,19},{19,3},{4,20},{20... | collective-permute-start | bytes 2457608 | tf_op jit(solution)/shard_map/ppermute | solution.py:26
  28.3 26.0 %collective-permute-start.5 = (bf16[128,1280]{1,0:T(8,128)(2,1)}, bf16[128,1280]{1,0:T(8,128)(2,1)}, u32[]{:S(2)}, u32[]{:S(2)}) collective-permute-start(bf16[128,1280]{1,0:T(8,128)(2,1)} %get-tuple-element.32), channel_id=1, source_target_pairs={{0,3},{1,0},{2,1},{3,2},{4,7},{5,4},{6,5},{7,6},{8,11},{9,8},{10,9... | collective-permute-start | bytes 983048 | tf_op jit(solution)/shard_map/ppermute | solution.py:21
  31.6 15.2 %copy-start.48 = (s32[2]{0:T(128)S(1)}, s32[2]{0:T(128)}, u32[]{:S(2)}) copy-start(s32[2]{0:T(128)} %param.8) | copy-start | bytes 28
  31.6 22.7 %collective-permute-start.8 = (bf16[128,1280]{1,0:T(8,128)(2,1)}, bf16[128,1280]{1,0:T(8,128)(2,1)}, u32[]{:S(2)}, u32[]{:S(2)}) collective-permute-start(bf16[128,1280]{1,0:T(8,128)(2,1)} %get-tuple-element.33), channel_id=1, source_target_pairs={{0,1},{1,2},{2,3},{3,0},{4,5},{5,6},{6,7},{7,4},{8,9},{9,10},{10,1... | collective-permute-start | bytes 983048 | tf_op jit(solution)/shard_map/ppermute | solution.py:21
  45.5 17.5 %collective-permute-start.7 = (bf16[128,1280]{1,0:T(8,128)(2,1)}, bf16[128,1280]{1,0:T(8,128)(2,1)}, u32[]{:S(2)}, u32[]{:S(2)}) collective-permute-start(bf16[128,1280]{1,0:T(8,128)(2,1)} %block0_partial.5), channel_id=1, source_target_pairs={{0,2},{1,3},{2,0},{3,1},{4,6},{5,7},{6,4},{7,5},{8,10},{9,11},{10,... | collective-permute-start | bytes 983048 | tf_op jit(solution)/shard_map/ppermute | solution.py:21
  47.8 6.2 %copy-start.49 = (s32[2]{0:T(128)S(1)}, s32[2]{0:T(128)}, u32[]{:S(2)}) copy-start(s32[2]{0:T(128)} %param.9) | copy-start | bytes 28
  64.6 14.8 %collective-permute-start.9 = (bf16[1,64,1280]{2,1,0:T(8,128)(2,1)S(1)}, bf16[1,64,1280]{2,1,0:T(8,128)(2,1)S(1)}, u32[]{:S(2)}, u32[]{:S(2)}) collective-permute-start(bf16[1,64,1280]{2,1,0:T(8,128)(2,1)S(1)} %slice.101), channel_id=1, source_target_pairs={{0,16},{1,17},{2,18},{3,19},{4,20},{5,21},{6,22},{7,23},{8,24},{9,... | collective-permute-start | bytes 491528 | tf_op jit(solution)/shard_map/ppermute | solution.py:522
  68.0 5.5 %collective-permute-start = (bf16[1,1280]{1,0:T(2,128)(2,1)S(1)}, bf16[1,1280]{1,0:T(2,128)(2,1)S(1)}, u32[]{:S(2)}, u32[]{:S(2)}) collective-permute-start(bf16[1,1280]{1,0:T(2,128)(2,1)S(1)} %broadcast_select_fusion), channel_id=1, source_target_pairs={{0,1},{1,2},{2,3},{3,0},{4,5},{5,6},{6,7},{7,4},{8,9},{9,10},{10,1... | collective-permute-start | bytes 7688 | tf_op jit(solution)/shard_map/ppermute | solution.py:21
  68.1 5.4 %collective-permute-start.1 = (bf16[1,1280]{1,0:T(2,128)(2,1)S(1)}, bf16[1,1280]{1,0:T(2,128)(2,1)S(1)}, u32[]{:S(2)}, u32[]{:S(2)}) collective-permute-start(bf16[1,1280]{1,0:T(2,128)(2,1)S(1)} %broadcast_select_fusion), channel_id=1, source_target_pairs={{0,2},{1,3},{2,0},{3,1},{4,6},{5,7},{6,4},{7,5},{8,10},{9,11},{10,... | collective-permute-start | bytes 7688 | tf_op jit(solution)/shard_map/ppermute | solution.py:21
  73.5 3.6 collective-permute-start.2
  77.3 21.5 %collective-permute-start.18 = (bf16[320,1280]{1,0:T(8,128)(2,1)}, bf16[320,1280]{1,0:T(8,128)(2,1)S(1)}, u32[]{:S(2)}, u32[]{:S(2)}) collective-permute-start(bf16[320,1280]{1,0:T(8,128)(2,1)} %collective-permute-done.16.refs_0_), channel_id=1, source_target_pairs={{0,8},{4,12},{8,0},{12,4},{1,9},{5,13},{9,1},{13,5},{2,10},{6,14},... | collective-permute-start | bytes 2457608 | tf_op jit(solution)/shard_map/ppermute | solution.py:26
  78.8 33.4 %collective-permute-start.14 = (bf16[320,1280]{1,0:T(8,128)(2,1)}, bf16[320,1280]{1,0:T(8,128)(2,1)}, u32[]{:S(2)}, u32[]{:S(2)}) collective-permute-start(bf16[320,1280]{1,0:T(8,128)(2,1)} %collective-permute-done.12.refs_0_), channel_id=1, source_target_pairs={{0,8},{4,12},{8,0},{12,4},{1,9},{5,13},{9,1},{13,5},{2,10},{6,14},... | collective-permute-start | bytes 2457608 | tf_op jit(solution)/shard_map/ppermute | solution.py:26
  79.4 32.9 %copy-start.4 = (bf16[64,1280]{1,0:T(8,128)(2,1)}, bf16[64,1280]{1,0:T(8,128)(2,1)S(1)}, u32[]{:S(2)}) copy-start(bf16[64,1280]{1,0:T(8,128)(2,1)S(1)} %fusion.11.refs_0_) | copy-start | bytes 491524
  79.4 7.3 %collective-permute-start.10 = (bf16[64,1280]{1,0:T(8,128)(2,1)S(1)}, bf16[64,1280]{1,0:T(8,128)(2,1)S(1)}, u32[]{:S(2)}, u32[]{:S(2)}) collective-permute-start(bf16[64,1280]{1,0:T(8,128)(2,1)S(1)} %fusion.11.refs_0_), channel_id=1, source_target_pairs={{0,1},{1,2},{2,3},{3,0},{4,5},{5,6},{6,7},{7,4},{8,9},{9,10},{10,1... | collective-permute-start | bytes 491528 | tf_op jit(solution)/shard_map/ppermute | solution.py:21
  79.5 32.8 %collective-permute-start.20 = (bf16[64,1280]{1,0:T(8,128)(2,1)S(1)}, bf16[64,1280]{1,0:T(8,128)(2,1)S(1)}, u32[]{:S(2)}, u32[]{:S(2)}) collective-permute-start(bf16[64,1280]{1,0:T(8,128)(2,1)S(1)} %fusion.11.refs_0_), channel_id=1, source_target_pairs={{0,2},{1,3},{2,0},{3,1},{4,6},{5,7},{6,4},{7,5},{8,10},{9,11},{10,... | collective-permute-start | bytes 491528 | tf_op jit(solution)/shard_map/ppermute | solution.py:21
  81.8 37.8 %collective-permute-start.17 = (bf16[320,1280]{1,0:T(8,128)(2,1)}, bf16[320,1280]{1,0:T(8,128)(2,1)S(1)}, u32[]{:S(2)}, u32[]{:S(2)}) collective-permute-start(bf16[320,1280]{1,0:T(8,128)(2,1)} %collective-permute-done.16.refs_0_), channel_id=1, source_target_pairs={{0,4},{4,0},{8,12},{12,8},{1,5},{5,1},{9,13},{13,9},{2,6},{6,2},{1... | collective-permute-start | bytes 2457608 | tf_op jit(solution)/shard_map/ppermute | solution.py:26
  86.7 32.3 %copy-start.10 = (bf16[64,1280]{1,0:T(8,128)(2,1)}, bf16[64,1280]{1,0:T(8,128)(2,1)S(1)}, u32[]{:S(2)}) copy-start(bf16[64,1280]{1,0:T(8,128)(2,1)S(1)} %collective-permute-done.10.refs_1_) | copy-start | bytes 491524
  86.7 135.2 %collective-permute-start.13 = (bf16[320,1280]{1,0:T(8,128)(2,1)}, bf16[320,1280]{1,0:T(8,128)(2,1)}, u32[]{:S(2)}, u32[]{:S(2)}) collective-permute-start(bf16[320,1280]{1,0:T(8,128)(2,1)} %collective-permute-done.12.refs_0_), channel_id=1, source_target_pairs={{0,4},{4,0},{8,12},{12,8},{1,5},{5,1},{9,13},{13,9},{2,6},{6,2},{1... | collective-permute-start | bytes 2457608 | tf_op jit(solution)/shard_map/ppermute | solution.py:26
  98.7 20.9 %copy-start.44 = (bf16[320,1280]{1,0:T(8,128)(2,1)}, bf16[320,1280]{1,0:T(8,128)(2,1)S(1)}, u32[]{:S(2)}) copy-start(bf16[320,1280]{1,0:T(8,128)(2,1)S(1)} %collective-permute-done.18.refs_2_) | copy-start | bytes 2457604
  98.7 20.9 %collective-permute-start.19 = (bf16[320,1280]{1,0:T(8,128)(2,1)S(1)}, bf16[320,1280]{1,0:T(8,128)(2,1)S(1)}, u32[]{:S(2)}, u32[]{:S(2)}) collective-permute-start(bf16[320,1280]{1,0:T(8,128)(2,1)S(1)} %collective-permute-done.18.refs_2_), channel_id=1, source_target_pairs={{0,4},{4,0},{8,12},{12,8},{1,5},{5,1},{9,13},{13,9},{2,6},{6,2},{1... | collective-permute-start | bytes 2457608 | tf_op jit(solution)/shard_map/ppermute | solution.py:26
  112.2 109.6 %collective-permute-start.15 = (bf16[320,1280]{1,0:T(8,128)(2,1)}, bf16[320,1280]{1,0:T(8,128)(2,1)}, u32[]{:S(2)}, u32[]{:S(2)}) collective-permute-start(bf16[320,1280]{1,0:T(8,128)(2,1)} %collective-permute-done.14.refs_2_), channel_id=1, source_target_pairs={{0,4},{4,0},{8,12},{12,8},{1,5},{5,1},{9,13},{13,9},{2,6},{6,2},{1... | collective-permute-start | bytes 2457608 | tf_op jit(solution)/shard_map/ppermute | solution.py:26
  112.3 6.7 %copy-start.6 = (bf16[64,1280]{1,0:T(8,128)(2,1)}, bf16[64,1280]{1,0:T(8,128)(2,1)S(1)}, u32[]{:S(2)}) copy-start(bf16[64,1280]{1,0:T(8,128)(2,1)S(1)} %collective-permute-done.20.refs_0_) | copy-start | bytes 491524
  112.3 6.7 %collective-permute-start.11 = (bf16[64,1280]{1,0:T(8,128)(2,1)S(1)}, bf16[64,1280]{1,0:T(8,128)(2,1)S(1)}, u32[]{:S(2)}, u32[]{:S(2)}) collective-permute-start(bf16[64,1280]{1,0:T(8,128)(2,1)S(1)} %fusion.11.refs_0_), channel_id=1, source_target_pairs={{0,3},{1,0},{2,1},{3,2},{4,7},{5,4},{6,5},{7,6},{8,11},{9,8},{10,9... | collective-permute-start | bytes 491528 | tf_op jit(solution)/shard_map/ppermute | solution.py:21
  323.2 6.9 %copy-start.5 = (bf16[64,1280]{1,0:T(8,128)(2,1)S(1)}, bf16[64,1280]{1,0:T(8,128)(2,1)}, u32[]{:S(2)}) copy-start(bf16[64,1280]{1,0:T(8,128)(2,1)} %copy-done.4) | copy-start | bytes 491524
  323.2 6.9 %copy-start.11 = (bf16[64,1280]{1,0:T(8,128)(2,1)S(1)}, bf16[64,1280]{1,0:T(8,128)(2,1)}, u32[]{:S(2)}) copy-start(bf16[64,1280]{1,0:T(8,128)(2,1)} %copy-done.10) | copy-start | bytes 491524
  323.2 6.9 %copy-start.13 = (bf16[64,1280]{1,0:T(8,128)(2,1)S(1)}, bf16[64,1280]{1,0:T(8,128)(2,1)}, u32[]{:S(2)}) copy-start(bf16[64,1280]{1,0:T(8,128)(2,1)} %copy-done.12) | copy-start | bytes 491524
  338.5 5.4 %collective-permute-start.23 = (f32[4,1,1280]{2,0,1:T(4,128)S(1)}, f32[4,1,1280]{2,0,1:T(4,128)S(1)}, u32[]{:S(2)}, u32[]{:S(2)}) collective-permute-start(f32[4,1,1280]{2,0,1:T(4,128)S(1)} %pad_maximum_fusion), channel_id=1, source_target_pairs={{0,3},{1,0},{2,1},{3,2},{4,7},{5,4},{6,5},{7,6},{8,11},{9,8},{10,9... | collective-permute-start | bytes 61448 | tf_op jit(solution)/shard_map/ppermute | solution.py:21
  342.5 5.7 %collective-permute-start.22 = (f32[4,1,1280]{2,0,1:T(4,128)S(1)}, f32[4,1,1280]{2,0,1:T(4,128)S(1)}, u32[]{:S(2)}, u32[]{:S(2)}) collective-permute-start(f32[4,1,1280]{2,0,1:T(4,128)S(1)} %pad_maximum_fusion), channel_id=1, source_target_pairs={{0,2},{1,3},{2,0},{3,1},{4,6},{5,7},{6,4},{7,5},{8,10},{9,11},{10,... | collective-permute-start | bytes 61448 | tf_op jit(solution)/shard_map/ppermute | solution.py:21
  342.5 5.6 %collective-permute-start.21 = (f32[4,1,1280]{2,0,1:T(4,128)S(1)}, f32[4,1,1280]{2,0,1:T(4,128)S(1)}, u32[]{:S(2)}, u32[]{:S(2)}) collective-permute-start(f32[4,1,1280]{2,0,1:T(4,128)S(1)} %pad_maximum_fusion), channel_id=1, source_target_pairs={{0,1},{1,2},{2,3},{3,0},{4,5},{5,6},{6,7},{7,4},{8,9},{9,10},{10,1... | collective-permute-start | bytes 61448 | tf_op jit(solution)/shard_map/ppermute | solution.py:21
  355.7 30.8 %copy-start.3 = (bf16[2,64,1280]{2,1,0:T(8,128)(2,1)S(1)}, bf16[2,64,1280]{2,1,0:T(8,128)(2,1)}, u32[]{:S(2)}) copy-start(bf16[2,64,1280]{2,1,0:T(8,128)(2,1)} %param.7) | copy-start | bytes 983044
  355.7 5.7 %collective-permute-start.24 = (bf16[64,1280]{1,0:T(8,128)(2,1)S(1)}, bf16[64,1280]{1,0:T(8,128)(2,1)S(1)}, u32[]{:S(2)}, u32[]{:S(2)}) collective-permute-start(bf16[64,1280]{1,0:T(8,128)(2,1)S(1)} %get-tuple-element.43), channel_id=1, source_target_pairs={{0,3},{1,0},{2,1},{3,2},{4,7},{5,4},{6,5},{7,6},{8,11},{9,8},{10,9... | collective-permute-start | bytes 491528 | tf_op jit(solution)/shard_map/ppermute | solution.py:21
  356.2 14.3 %collective-permute-start.25 = (bf16[64,1280]{1,0:T(8,128)(2,1)S(1)}, bf16[64,1280]{1,0:T(8,128)(2,1)S(1)}, u32[]{:S(2)}, u32[]{:S(2)}) collective-permute-start(bf16[64,1280]{1,0:T(8,128)(2,1)S(1)} %get-tuple-element.44), channel_id=1, source_target_pairs={{0,2},{1,3},{2,0},{3,1},{4,6},{5,7},{6,4},{7,5},{8,10},{9,11},{10,... | collective-permute-start | bytes 491528 | tf_op jit(solution)/shard_map/ppermute | solution.py:21
  356.9 13.7 %collective-permute-start.26 = (bf16[64,1280]{1,0:T(8,128)(2,1)S(1)}, bf16[64,1280]{1,0:T(8,128)(2,1)S(1)}, u32[]{:S(2)}, u32[]{:S(2)}) collective-permute-start(bf16[64,1280]{1,0:T(8,128)(2,1)S(1)} %get-tuple-element.45), channel_id=1, source_target_pairs={{0,1},{1,2},{2,3},{3,0},{4,5},{5,6},{6,7},{7,4},{8,9},{9,10},{10,1... | collective-permute-start | bytes 491528 | tf_op jit(solution)/shard_map/ppermute | solution.py:21
  371.0 34.6 %copy-start.8 = (bf16[64,1280]{1,0:T(8,128)(2,1)}, bf16[64,1280]{1,0:T(8,128)(2,1)S(1)}, u32[]{:S(2)}) copy-start(bf16[64,1280]{1,0:T(8,128)(2,1)S(1)} %multiply_convert_fusion.refs_0_) | copy-start | bytes 491524
  371.0 9.0 %collective-permute-start.28 = (bf16[64,1280]{1,0:T(8,128)(2,1)S(1)}, bf16[64,1280]{1,0:T(8,128)(2,1)S(1)}, u32[]{:S(2)}, u32[]{:S(2)}) collective-permute-start(bf16[64,1280]{1,0:T(8,128)(2,1)S(1)} %multiply_convert_fusion.refs_0_), channel_id=1, source_target_pairs={{0,1},{1,2},{2,3},{3,0},{4,5},{5,6},{6,7},{7,4},{8,9},{9,10},{10,1... | collective-permute-start | bytes 491528 | tf_op jit(solution)/shard_map/ppermute | solution.py:21
  371.2 13.3 %collective-permute-start.30 = (bf16[64,1280]{1,0:T(8,128)(2,1)S(1)}, bf16[64,1280]{1,0:T(8,128)(2,1)S(1)}, u32[]{:S(2)}, u32[]{:S(2)}) collective-permute-start(bf16[64,1280]{1,0:T(8,128)(2,1)S(1)} %multiply_convert_fusion.refs_0_), channel_id=1, source_target_pairs={{0,2},{1,3},{2,0},{3,1},{4,6},{5,7},{6,4},{7,5},{8,10},{9,11},{10,... | collective-permute-start | bytes 491528 | tf_op jit(solution)/shard_map/ppermute | solution.py:21
  373.2 11.3 %collective-permute-start.32 = (bf16[64,1280]{1,0:T(8,128)(2,1)S(1)}, bf16[64,1280]{1,0:T(8,128)(2,1)S(1)}, u32[]{:S(2)}, u32[]{:S(2)}) collective-permute-start(bf16[64,1280]{1,0:T(8,128)(2,1)S(1)} %multiply_convert_fusion.refs_0_), channel_id=1, source_target_pairs={{0,3},{1,0},{2,1},{3,2},{4,7},{5,4},{6,5},{7,6},{8,11},{9,8},{10,9... | collective-permute-start | bytes 491528 | tf_op jit(solution)/shard_map/ppermute | solution.py:21
  376.0 29.5 %collective-permute-start.27 = (bf16[64,1280]{1,0:T(8,128)(2,1)S(1)}, bf16[64,1280]{1,0:T(8,128)(2,1)S(1)}, u32[]{:S(2)}, u32[]{:S(2)}) collective-permute-start(bf16[64,1280]{1,0:T(8,128)(2,1)S(1)} %multiply_convert_fusion.refs_0_), channel_id=1, source_target_pairs={{0,16},{16,0},{1,17},{17,1},{2,18},{18,2},{3,19},{19,3},{4,20},{20... | collective-permute-start | bytes 491528 | tf_op jit(solution)/shard_map/ppermute | solution.py:26
  380.0 25.6 %copy-start.22 = (bf16[64,1280]{1,0:T(8,128)(2,1)}, bf16[64,1280]{1,0:T(8,128)(2,1)S(1)}, u32[]{:S(2)}) copy-start(bf16[64,1280]{1,0:T(8,128)(2,1)S(1)} %collective-permute-done.28.refs_2_) | copy-start | bytes 491524
  380.0 25.6 %collective-permute-start.29 = (bf16[64,1280]{1,0:T(8,128)(2,1)S(1)}, bf16[64,1280]{1,0:T(8,128)(2,1)S(1)}, u32[]{:S(2)}, u32[]{:S(2)}) collective-permute-start(bf16[64,1280]{1,0:T(8,128)(2,1)S(1)} %collective-permute-done.28.refs_2_), channel_id=1, source_target_pairs={{0,16},{16,0},{1,17},{17,1},{2,18},{18,2},{3,19},{19,3},{4,20},{20... | collective-permute-start | bytes 491528 | tf_op jit(solution)/shard_map/ppermute | solution.py:26
  384.5 21.2 %copy-start.24 = (bf16[64,1280]{1,0:T(8,128)(2,1)}, bf16[64,1280]{1,0:T(8,128)(2,1)S(1)}, u32[]{:S(2)}) copy-start(bf16[64,1280]{1,0:T(8,128)(2,1)S(1)} %collective-permute-done.30.refs_4_) | copy-start | bytes 491524
  384.5 21.1 %collective-permute-start.31 = (bf16[64,1280]{1,0:T(8,128)(2,1)S(1)}, bf16[64,1280]{1,0:T(8,128)(2,1)S(1)}, u32[]{:S(2)}, u32[]{:S(2)}) collective-permute-start(bf16[64,1280]{1,0:T(8,128)(2,1)S(1)} %collective-permute-done.30.refs_4_), channel_id=1, source_target_pairs={{0,16},{16,0},{1,17},{17,1},{2,18},{18,2},{3,19},{19,3},{4,20},{20... | collective-permute-start | bytes 491528 | tf_op jit(solution)/shard_map/ppermute | solution.py:26
  384.5 21.2 %copy-start.26 = (bf16[64,1280]{1,0:T(8,128)(2,1)}, bf16[64,1280]{1,0:T(8,128)(2,1)S(1)}, u32[]{:S(2)}) copy-start(bf16[64,1280]{1,0:T(8,128)(2,1)S(1)} %collective-permute-done.32.refs_6_) | copy-start | bytes 491524
  384.5 21.1 %collective-permute-start.33 = (bf16[64,1280]{1,0:T(8,128)(2,1)S(1)}, bf16[64,1280]{1,0:T(8,128)(2,1)S(1)}, u32[]{:S(2)}, u32[]{:S(2)}) collective-permute-start(bf16[64,1280]{1,0:T(8,128)(2,1)S(1)} %collective-permute-done.32.refs_6_), channel_id=1, source_target_pairs={{0,16},{16,0},{1,17},{17,1},{2,18},{18,2},{3,19},{19,3},{4,20},{20... | collective-permute-start | bytes 491528 | tf_op jit(solution)/shard_map/ppermute | solution.py:26
  405.5 4.1 copy-start.42
  405.5 4.3 copy-start.15
  405.5 4.3 copy-start.17
  405.5 4.3 copy-start.19
  405.5 4.3 copy-start.37
  405.5 4.3 copy-start.39
  405.6 4.1 copy-start.28
  405.6 4.3 copy-start.21
  405.6 4.3 copy-start.41
  409.7 16.0 %collective-permute-start.36 = (bf16[2,160,1280]{2,1,0:T(8,128)(2,1)}, bf16[2,160,1280]{2,1,0:T(8,128)(2,1)}, u32[]{:S(2)}, u32[]{:S(2)}) collective-permute-start(bf16[2,160,1280]{2,1,0:T(8,128)(2,1)} %get-tuple-element.61), channel_id=1, source_target_pairs={{0,4},{4,0},{8,12},{12,8},{1,5},{5,1},{9,13},{13,9},{2,6},{6,2},{1... | collective-permute-start | bytes 2457608 | tf_op jit(solution)/shard_map/ppermute | solution.py:26
  425.2 3.4 collective-permute-start.34
  427.0 12.4 %collective-permute-start.37 = (bf16[160,1280]{1,0:T(8,128)(2,1)S(1)}, bf16[160,1280]{1,0:T(8,128)(2,1)S(1)}, u32[]{:S(2)}, u32[]{:S(2)}) collective-permute-start(bf16[160,1280]{1,0:T(8,128)(2,1)S(1)} %fusion.4), channel_id=1, source_target_pairs={{0,8},{4,12},{8,0},{12,4},{1,9},{5,13},{9,1},{13,5},{2,10},{6,14},... | collective-permute-start | bytes 1228808 | tf_op jit(solution)/shard_map/ppermute | solution.py:21
  428.8 18.5 %collective-permute-start.35 = (bf16[160,1280]{1,0:T(8,128)(2,1)S(1)}, bf16[160,1280]{1,0:T(8,128)(2,1)S(1)}, u32[]{:S(2)}, u32[]{:S(2)}) collective-permute-start(bf16[160,1280]{1,0:T(8,128)(2,1)S(1)} %fusion.3), channel_id=1, source_target_pairs={{0,8},{4,12},{8,0},{12,4},{1,9},{5,13},{9,1},{13,5},{2,10},{6,14},... | collective-permute-start | bytes 1228808 | tf_op jit(solution)/shard_map/ppermute | solution.py:21
  (24 other events, 39.8 us)

commit v3 on v2

v3 whole, which is shorter than its diff:
```python
import functools
import math

import jax
import jax.numpy as jnp
from jax import lax
from jax.experimental import pallas as pl
from jax.experimental.pallas import tpu as pltpu
from jax.sharding import PartitionSpec as P

STEPS = 50


EPS = 1e-06
VMEM_BYTES = 32 * 1024 * 1024
POOL_ROWS = 8


def rotated(value, axis, steps):
    count = lax.axis_size(axis)
    return lax.ppermute(value, axis, [(i, (i + steps) % count) for i in range(count)])


def swapped(value, axis, bit):
    count = lax.axis_size(axis)
    return lax.ppermute(value, axis, [(i, i ^ bit) for i in range(count)])


def gather_parts(piece):
    return [piece] + [rotated(piece, "tp", k) for k in range(1, lax.axis_size("tp"))]


def reduce_parts(parts):
    total = parts[0].astype(jnp.float32)
    for k in range(1, len(parts)):
        total = total + rotated(parts[k], "tp", -k).astype(jnp.float32)
    return total


def quarter(weight, place):
    rows = weight.shape[0] // 4
    return lax.dynamic_slice_in_dim(weight, place * rows, rows, 0)


def quarters(got, across):
    return (got, swapped(got, "dp", 1), across, swapped(across, "dp", 1))


def gelu_pair(value):
    cdf = 0.5 * (1.0 + lax.erf(value * (1.0 / math.sqrt(2.0))))
    density = jnp.exp(-0.5 * value * value) * (1.0 / math.sqrt(2.0 * math.pi))
    return (value * cdf, cdf + value * density)


def normed(rows, gain):
    scale = lax.rsqrt(jnp.mean(rows * rows, axis=-1, keepdims=True) + EPS)
    return (rows * scale * gain).astype(jnp.bfloat16)


def dot_nn(a, b):
    return jnp.dot(a, b, preferred_element_type=jnp.float32)


def dot_nt(a, b):
    return lax.dot_general(a, b, (((1,), (1,)), ((), ())), preferred_element_type=jnp.float32)


def tile_of(hidden):
    for tile in (256, 128):
        if hidden % tile == 0:
            return tile
    return hidden


def whole(shape):
    return pl.BlockSpec(shape, lambda h, sel: (0,) * len(shape))


def columns(rows, tile):
    return pl.BlockSpec((rows, tile), lambda h, sel: (0, h))


IN_HBM = pl.BlockSpec(memory_space=pltpu.HBM)


def weight_buffers(width, hidden, tile):
    steps = hidden // tile
    return [pltpu.VMEM((steps, width, tile), jnp.bfloat16), pltpu.SemaphoreType.DMA((steps,))]


def fetch_own(own, buffer, sems):
    steps, unused, tile = buffer.shape
    for t in range(steps):
        pltpu.make_async_copy(own.at[:, pl.ds(t * tile, tile)], buffer.at[t], sems.at[t]).start()


def fetch(sel_ref, section, own, pieces, buffer, sems):
    steps, unused, tile = buffer.shape

    @pl.when(sel_ref[0] == section)
    def _():
        fetch_own(own, buffer, sems)

    @pl.when(sel_ref[0] != section)
    def _():
        for t in range(steps):
            for q, piece in enumerate(pieces):
                rows = piece.shape[0]
                start = pl.multiple_of((sel_ref[2] ^ q) * rows, rows)
                pltpu.make_async_copy(
                    piece.at[:, pl.ds(t * tile, tile)],
                    buffer.at[t, pl.ds(start, rows), :],
                    sems.at[t],
                ).start()


def fetched(own, buffer, sems, h):
    tile = buffer.shape[2]
    pltpu.make_async_copy(own.at[:, pl.ds(0, tile)], buffer.at[h], sems.at[h]).wait()
    return buffer[h]


def run(body, name, steps, sel, operands, in_specs, outs, out_specs, scratch, flops, elements=0):
    read = sum(x.size * x.dtype.itemsize for x in operands)
    written = sum(math.prod(o.shape) * o.dtype.itemsize for o in outs)
    return pl.pallas_call(
        body,
        grid_spec=pltpu.PrefetchScalarGridSpec(
            num_scalar_prefetch=1,
            grid=(steps,),
            in_specs=in_specs,
            out_specs=out_specs,
            scratch_shapes=scratch,
        ),
        out_shape=outs,
        compiler_params=pltpu.CompilerParams(
            dimension_semantics=("arbitrary",), vmem_limit_bytes=VMEM_BYTES
        ),
        cost_estimate=pl.CostEstimate(
            flops=flops, bytes_accessed=read + written, transcendentals=elements
        ),
        name=name,
    )(sel, *operands)


def bf16(*shape):
    return jax.ShapeDtypeStruct(shape, jnp.bfloat16)


def partial_body(count, sel_ref, *refs):
    parts, (gain, w_in, w_out) = refs[:count], refs[count : count + 3]
    outs = refs[count + 3 : 2 * count + 3]
    xn, acc, in_buffer, in_sems, out_buffer, out_sems = refs[2 * count + 3 :]
    h = pl.program_id(0)
    rows = parts[0].shape[0]

    @pl.when(h == 0)
    def _():
        fetch_own(w_in, in_buffer, in_sems)
        fetch_own(w_out, out_buffer, out_sems)
        for i, part in enumerate(parts):
            xn[i * rows : (i + 1) * rows, :] = normed(part[...].astype(jnp.float32), gain[...])
        acc[...] = jnp.zeros_like(acc)

    act, unused = gelu_pair(dot_nn(xn[...], fetched(w_in, in_buffer, in_sems, h)))
    acc[...] += dot_nt(act.astype(jnp.bfloat16), fetched(w_out, out_buffer, out_sems, h))

    @pl.when(h == pl.num_programs(0) - 1)
    def _():
        for i, out in enumerate(outs):
            out[...] = acc[i * rows : (i + 1) * rows, :].astype(jnp.bfloat16)


def block0_partials(parts, gain, w_in, w_out, sel):
    rows, width = parts[0].shape
    hidden = w_in.shape[1]
    tile, n = tile_of(hidden), len(parts)
    return run(
        functools.partial(partial_body, n),
        "block0_partial",
        hidden // tile,
        sel,
        [*parts, gain, w_in, w_out],
        [whole((rows, width))] * n
        + [whole((1, width)), IN_HBM, IN_HBM],
        [bf16(rows, width)] * n,
        [whole((rows, width))] * n,
        [
            pltpu.VMEM((n * rows, width), jnp.bfloat16),
            pltpu.VMEM((n * rows, width), jnp.float32),
            *weight_buffers(width, hidden, tile),
            *weight_buffers(width, hidden, tile),
        ],
        4 * n * rows * width * hidden,
        n * rows * hidden,
    )


def state_body(sel_ref, part, gain, own, p0, p1, p2, p3, act, slope, xn_cols, xn, buffer, sems):
    h = pl.program_id(0)
    rows = part.shape[0]
    late = rows // 2
    share = xn_cols.shape[0]

    @pl.when(h == 0)
    def _():
        fetch(sel_ref, 0, own, (p0, p1, p2, p3), buffer, sems)
        mine = pl.multiple_of((1 - sel_ref[0]) * late, late)
        theirs = pl.multiple_of(sel_ref[0] * late, late)
        for i, start in enumerate((mine, theirs)):
            xn[i * late : (i + 1) * late, :] = normed(
                part[pl.ds(start, late), :].astype(jnp.float32), gain[...]
            )
        cols = xn[:, pl.ds(pl.multiple_of(sel_ref[0] * share, share), share)]
        xn_cols[...] = cols.T

    value, grad = gelu_pair(dot_nn(xn[...], fetched(own, buffer, sems, h)))
    act[...] = value.astype(jnp.bfloat16)
    slope[...] = grad.astype(jnp.bfloat16)


def block0_state(part, gain, own, pieces, sel):
    rows, width = part.shape
    hidden = own.shape[1]
    tile = tile_of(hidden)
    return run(
        state_body,
        "block0_state",
        hidden // tile,
        sel,
        [part, gain, own, *pieces],
        [whole((rows, width)), whole((1, width))] + [IN_HBM] * 5,
        [bf16(rows, hidden), bf16(rows, hidden), bf16(width // 2, rows)],
        [columns(rows, tile), columns(rows, tile), whole((width // 2, rows))],
        [pltpu.VMEM((rows, width), jnp.bfloat16), *weight_buffers(width, hidden, tile)],
        2 * rows * width * hidden,
        2 * rows * hidden,
    )


def reward_body(count, tokens, sel_ref, *refs):
    parts, gain = refs[:count], refs[count]
    own_in, own_out, *pieces = refs[count + 1 : count + 11]
    slopes = refs[count + 11 : 2 * count + 11]
    pools = refs[2 * count + 11 : 3 * count + 11]
    xn, in_buffer, in_sems, out_buffer, out_sems = refs[3 * count + 11 :]
    h = pl.program_id(0)
    rows = parts[0].shape[0]

    @pl.when(h == 0)
    def _():
        fetch(sel_ref, 1, own_in, pieces[:4], in_buffer, in_sems)
        fetch(sel_ref, 1, own_out, pieces[4:], out_buffer, out_sems)
        for i, part in enumerate(parts):
            xn[i * rows : (i + 1) * rows, :] = normed(part[...].astype(jnp.float32), gain[...])
            pools[i][...] = jnp.zeros_like(pools[i])

    act, grad = gelu_pair(dot_nn(xn[...], fetched(own_in, in_buffer, in_sems, h)))
    weight = fetched(own_out, out_buffer, out_sems, h)
    row = lax.broadcasted_iota(jnp.int32, (POOL_ROWS, act.shape[1]), 0)
    for i in range(count):
        slopes[i][...] = grad[i * rows : (i + 1) * rows, :].astype(jnp.bfloat16)
        means = jnp.zeros((POOL_ROWS, act.shape[1]), jnp.float32)
        for image in range(rows // tokens):
            start = i * rows + image * tokens
            mean = jnp.mean(act[start : start + tokens, :], axis=0, keepdims=True)
            means = jnp.where(row == image, mean, means)
        pools[i][...] += dot_nt(means.astype(jnp.bfloat16), weight)


def reward_forward(parts, tokens, gain, own, pieces, sel):
    rows, width = parts[0].shape
    hidden = own[0].shape[1]
    tile, n = tile_of(hidden), len(parts)
    outs = run(
        functools.partial(reward_body, n, tokens),
        "reward_forward",
        hidden // tile,
        sel,
        [*parts, gain, *own, *pieces[0], *pieces[1]],
        [whole((rows, width))] * n + [whole((1, width))] + [IN_HBM] * 10,
        [bf16(rows, hidden)] * n + [jax.ShapeDtypeStruct((POOL_ROWS, width), jnp.float32)] * n,
        [columns(rows, tile)] * n + [whole((POOL_ROWS, width))] * n,
        [
            pltpu.VMEM((n * rows, width), jnp.bfloat16),
            *weight_buffers(width, hidden, tile),
            *weight_buffers(width, hidden, tile),
        ],
        2 * n * rows * width * hidden,
        2 * n * rows * hidden,
    )
    return outs[:n], outs[n:]


def back_body(count, tokens, sel_ref, *refs):
    g_tok = refs[0]
    slopes = refs[1 : count + 1]
    own_in, own_out, *pieces = refs[count + 1 : count + 11]
    outs = refs[count + 11 : 2 * count + 11]
    acc, in_buffer, in_sems, out_buffer, out_sems = refs[2 * count + 11 :]
    h = pl.program_id(0)
    rows = slopes[0].shape[0]
    per = rows // tokens

    @pl.when(h == 0)
    def _():
        fetch(sel_ref, 1, own_out, pieces[4:], out_buffer, out_sems)
        fetch(sel_ref, 1, own_in, pieces[:4], in_buffer, in_sems)
        acc[...] = jnp.zeros_like(acc)

    g_h = dot_nn(g_tok[...], fetched(own_out, out_buffer, out_sems, h))
    terms = []
    for i in range(count):
        for image in range(per):
            at = i * per + image
            slope = slopes[i][image * tokens : (image + 1) * tokens, :].astype(jnp.float32)
            terms.append((slope * g_h[at : at + 1, :]).astype(jnp.bfloat16))
    weight = fetched(own_in, in_buffer, in_sems, h)
    acc[...] += dot_nt(jnp.concatenate(terms, axis=0), weight)

    @pl.when(h == pl.num_programs(0) - 1)
    def _():
        for i, out in enumerate(outs):
            out[...] = acc[i * rows : (i + 1) * rows, :].astype(jnp.bfloat16)


def reward_back(g_tok, slopes, tokens, own, pieces, sel):
    rows, hidden = slopes[0].shape
    width = own[0].shape[0]
    tile, n = tile_of(hidden), len(slopes)
    return run(
        functools.partial(back_body, n, tokens),
        "reward_back",
        hidden // tile,
        sel,
        [g_tok, *slopes, *own, *pieces[0], *pieces[1]],
        [whole(g_tok.shape)] + [columns(rows, tile)] * n + [IN_HBM] * 10,
        [bf16(rows, width)] * n,
        [whole((rows, width))] * n,
        [
            pltpu.VMEM((n * rows, width), jnp.float32),
            *weight_buffers(width, hidden, tile),
            *weight_buffers(width, hidden, tile),
        ],
        2 * n * rows * width * hidden,
    )


def put_rows(result, core, keep, away):
    groups, rows, unused = keep.shape
    for g in range(groups):
        even = result[2 * g * rows : (2 * g + 1) * rows, :]
        odd = result[(2 * g + 1) * rows : (2 * g + 2) * rows, :]
        keep[g] = jnp.where(core == 0, even, odd).astype(jnp.bfloat16)
        away[g] = jnp.where(core == 0, odd, even).astype(jnp.bfloat16)


def grad_out_body(count, sel_ref, *refs):
    pieces, acts = refs[: 2 * count], refs[2 * count : 3 * count]
    keep, away, turned = refs[3 * count :]
    share = turned.shape[0]

    @pl.when(pl.program_id(0) == 0)
    def _():
        start = pl.multiple_of(sel_ref[0] * share, share)
        cols = jnp.concatenate([piece[:, pl.ds(start, share)] for piece in pieces], axis=0)
        turned[...] = cols.T

    act = jnp.concatenate([part[...] for part in acts], axis=0)
    put_rows(dot_nn(turned[...], act), sel_ref[1], keep, away)


def grad_in_body(count, sel_ref, *refs):
    pieces, slopes = refs[: 2 * count], refs[2 * count : 3 * count]
    xn_cols = refs[3 * count : 4 * count]
    own, *quarters = refs[4 * count : 4 * count + 5]
    keep, away, g_all, turned, buffer, sems = refs[4 * count + 5 :]
    rows = pieces[0].shape[0]
    wide = xn_cols[0].shape[1]
    h = pl.program_id(0)

    @pl.when(h == 0)
    def _():
        fetch(sel_ref, 0, own, quarters, buffer, sems)
        for i, piece in enumerate(pieces):
            g_all[i * rows : (i + 1) * rows, :] = piece[...]
        for i, part in enumerate(xn_cols):
            turned[:, i * wide : (i + 1) * wide] = part[...]

    g_h = dot_nn(g_all[...], fetched(own, buffer, sems, h))
    slope = jnp.concatenate([part[...] for part in slopes], axis=0).astype(jnp.float32)
    g_hidden = (g_h * slope).astype(jnp.bfloat16)
    put_rows(dot_nn(turned[...], g_hidden), sel_ref[1], keep, away)


def gradient_call(body, name, pieces, states, extra, extra_specs, scratch, sel, flops):
    rows, width = pieces[0].shape
    hidden = states[0].shape[1]
    tile = tile_of(hidden)
    groups = lax.axis_size("dp") // 2
    cut = (groups, width // 2 // (2 * groups))
    return run(
        body,
        name,
        hidden // tile,
        sel,
        [*pieces, *states, *extra],
        [whole((rows, width))] * len(pieces)
        + [columns(states[0].shape[0], tile)] * len(states)
        + extra_specs,
        [bf16(*cut, hidden)] * 2,
        [pl.BlockSpec((*cut, tile), lambda h, sel: (0, 0, h))] * 2,
        scratch,
        flops,
    )


def grad_out_parts(pieces, acts, sel):
    rows, width = pieces[0].shape
    total = rows * len(pieces)
    return gradient_call(
        functools.partial(grad_out_body, len(acts)),
        "grad_out",
        pieces,
        acts,
        [],
        [],
        [pltpu.VMEM((width // 2, total), jnp.bfloat16)],
        sel,
        total * width * acts[0].shape[1],
    )


def grad_in_parts(pieces, slopes, xn_cols, own, quarters, sel):
    rows, width = pieces[0].shape
    total = rows * len(pieces)
    hidden = slopes[0].shape[1]
    return gradient_call(
        functools.partial(grad_in_body, len(slopes)),
        "grad_in",
        pieces,
        slopes,
        [*xn_cols, own, *quarters],
        [whole(xn_cols[0].shape)] * len(xn_cols) + [IN_HBM] * 5,
        [
            pltpu.VMEM((total, width), jnp.bfloat16),
            pltpu.VMEM((width // 2, total), jnp.bfloat16),
            *weight_buffers(width, hidden, tile_of(hidden)),
        ],
        sel,
        3 * total * width * hidden,
    )


def sum_over_dp(keep, away):
    groups = keep.shape[0]
    place = lax.axis_index("dp") // 2
    chip = keep.astype(jnp.float32) + swapped(away, "dp", 1).astype(jnp.float32)
    total = lax.dynamic_index_in_dim(chip, place, 0, keepdims=False)
    sent = chip.astype(jnp.bfloat16)
    for k in range(1, groups):
        part = lax.dynamic_index_in_dim(sent, (place + k) % groups, 0, keepdims=False)
        total = total + rotated(part, "dp", 2 * k).astype(jnp.float32)
    return total


def score_of(pooled, text):
    unit_img = pooled * lax.rsqrt(jnp.mean(pooled * pooled, axis=-1, keepdims=True) + EPS)
    unit_txt = text * lax.rsqrt(jnp.mean(text * text, axis=-1, keepdims=True) + EPS)
    return 100.0 * jnp.sum(unit_img * unit_txt, axis=-1) / pooled.shape[-1]


def on_device(latents, timesteps, prompt_ids, prompt_table, gains, w_in, w_out):
    count, tokens, width = latents.shape
    half = count // 2
    n_tp = lax.axis_size("tp")
    segment = lax.axis_index("sec")
    first = segment == 0
    core = lax.axis_index("dp") % 2
    place = lax.axis_index("dp") % 4
    sel = jnp.stack([segment, core, place]).astype(jnp.int32)
    own = (w_in[0], w_out[0])
    theta = math.pi / 2.0 * (timesteps.astype(jnp.float32) + 1.0) / (STEPS + 1.0)
    alpha = jnp.cos(theta)[:, None, None]
    sigma = jnp.sin(theta)[:, None, None]

    flat = latents.reshape(count * tokens, width)
    got_in = swapped(quarter(own[0], place), "sec", 1)
    lat_parts = gather_parts(flat)
    got_out = swapped(quarter(own[1], place), "sec", 1)
    across_in = swapped(got_in, "dp", 2)
    across_out = swapped(got_out, "dp", 2)

    onehot = (
        prompt_ids[:, None] == jnp.arange(prompt_table.shape[0], dtype=jnp.int32)[None, :]
    ).astype(jnp.bfloat16)
    text = dot_nn(onehot, prompt_table).astype(jnp.bfloat16)
    text_mine = jnp.where(first, text[half:], text[:half])
    text_all = jnp.concatenate(gather_parts(text_mine), 0).astype(jnp.float32)

    near = [k for k in range(1, n_tp) if 2 * k != n_tp]
    far = [k for k in range(1, n_tp) if 2 * k == n_tp]
    eps_parts = [None] * n_tp
    arrivals = ([], [got_in, text_all], [got_out, across_in])
    for ks, arrived in zip(([0], near, far), arrivals):
        if ks:
            operands, unused = lax.optimization_barrier(([lat_parts[k] for k in ks], arrived))
            results = block0_partials(operands, gains[:1], *own, sel)
            for k, result in zip(ks, results):
                eps_parts[k] = result
    eps_mix, across_out = lax.optimization_barrier((reduce_parts(eps_parts), across_out))
    eps_mix = eps_mix.reshape(count, tokens, width)
    other = (quarters(got_in, across_in), quarters(got_out, across_out))
    base = latents.astype(jnp.float32)
    images = ((base - sigma * (base + eps_mix)) / alpha).astype(jnp.bfloat16)

    arrived = lax.ppermute(images[:half], "sec", [(0, 1)])
    mine = jnp.where(first, images[half:], arrived)
    ratio = jnp.where(first, (sigma / alpha)[half:], (sigma / alpha)[:half])
    mine_rows = mine.reshape(half * tokens, width)
    seen_parts = gather_parts(mine_rows)

    states = [block0_state(part, gains[:1], own[0], other[0], sel) for part in lat_parts]
    slopes1, pool_parts = [None] * n_tp, [None] * n_tp
    early = n_tp // 2
    done = (states[: early // 2], states[early // 2 : early])
    for ks, before in zip(([0] + near, far), done):
        if ks:
            operands, unused = lax.optimization_barrier(([seen_parts[k] for k in ks], before))
            some_slopes, some_pools = reward_forward(
                operands, tokens, gains[1:], own, other, sel
            )
            for k, slope, pool in zip(ks, some_slopes, some_pools):
                slopes1[k], pool_parts[k] = slope, pool[:half]
    pool_part = jnp.stack(pool_parts)
    pool = pool_part
    for k in range(1, n_tp):
        pool = pool + jnp.roll(rotated(pool_part, "tp", k), k, axis=0)
    seen_mean = jnp.stack(
        [
            jnp.mean(part.astype(jnp.float32).reshape(half, tokens, width), axis=1)
            for part in seen_parts
        ]
    )
    pooled = (pool + seen_mean).reshape(n_tp * half, width)
    g_pooled = jax.grad(lambda p: -jnp.sum(score_of(p, text_all)))(pooled)
    g_mean = g_pooled / tokens
    padded = -(-n_tp * half // 16) * 16
    g_tok = jnp.pad(g_mean.astype(jnp.bfloat16), ((0, padded - n_tp * half), (0, 0)))
    g_parts = reward_back(g_tok, slopes1, tokens, own, other, sel)
    g_xn, unused = lax.optimization_barrier((reduce_parts(g_parts), states[early:]))
    seen = mine_rows.astype(jnp.float32)
    scale1 = lax.rsqrt(jnp.mean(seen * seen, axis=-1, keepdims=True) + EPS)
    weighted = gains[1] * g_xn
    g_norm = scale1 * weighted - seen * scale1**3 * jnp.mean(
        seen * weighted, axis=-1, keepdims=True
    )
    g_images = (g_mean[:half, None, :] + g_norm.reshape(half, tokens, width)).astype(jnp.bfloat16)
    g_eps = (-ratio * g_images.astype(jnp.float32)).astype(jnp.bfloat16)

    pieces = []
    for part in gather_parts(g_eps.reshape(half * tokens, width)):
        pieces += [part, swapped(part, "sec", 1)]
    grad_out = sum_over_dp(*grad_out_parts(pieces, [state[0] for state in states], sel))
    slopes0, xn_cols = [state[1] for state in states], [state[2] for state in states]
    grad_in = sum_over_dp(*grad_in_parts(pieces, slopes0, xn_cols, own[1], other[1], sel))
    return (grad_in, grad_out)


def solution(mesh):
    in_specs = (
        P(("dp", "tp"), None, None),
        P(("dp", "tp")),
        P(("dp", "tp")),
        P(),
        P(),
        P("sec", None, "tp"),
        P("sec", None, "tp"),
    )
    out_specs = (P(("sec", "dp"), "tp"), P(("sec", "dp"), "tp"))
    return jax.shard_map(
        on_device, mesh=mesh, in_specs=in_specs, out_specs=out_specs, check_vma=False
    )
```

time: 454 us -> 207 us (0.46); the launches traced: 448 us -> 207 us
  Pallas kernels: 271 us -> 63.5 us
  waiting for transfers between devices: 100 us -> 75.3 us
  local copies, waits for them, and re-layouts: 20.8 us -> 12.2 us
    pallas_call x2 -> x0, Pallas kernels: 201 us -> none  [from_other_section(): pl.pallas_call(assemble_body, grid_spec=pltpu.PrefetchScalarGridSpec(num_...]
    ppermute x23, waiting for transfers between devices: 74.6 us -> 53.5 us  [rotated(): lax.ppermute(value, axis, [(i, (i + steps) % count) for i in range(count)])]
    unnamed x100 -> x32, local copies, waits for them, and re-layouts: 15.6 us -> 7.04 us
    pallas_call x12, Pallas kernels: 70.5 us -> 63.5 us  [run(): pl.pallas_call(body, grid_spec=pltpu.PrefetchScalarGridSpec(num_scalar_pr...]
    ppermute x14, waiting for transfers between devices: 25.6 us -> 19.7 us  [swapped(): return lax.ppermute(value, axis, [(i, i ^ bit) for i in range(count)])]
    ppermute x14, starting transfers between devices: 6.71 us -> 11.9 us  [swapped(): return lax.ppermute(value, axis, [(i, i ^ bit) for i in range(count)])]
  transfers between devices with their start and end apart: 38 -> 38, of which waited for: 18 -> 17; matrix products, arithmetic and copies ran while one was open for 2% -> 3% of each run, Pallas kernels for 32% -> 18%
where the time goes in v3:
time: 207 us
  waiting for transfers between devices  75.3 us (36%)
  Pallas kernels  63.5 us (31%)
  starting transfers between devices  47.7 us (23%)
  local copies, waits for them, and re-layouts  12.2 us (6%)
  other arithmetic  5.06 us (2%)
  between operations  2.55 us (1%)
    pallas_call x12, Pallas kernels, run(): pl.pallas_call(body, grid_spec=pltpu.PrefetchScalarGridSpec(num_scalar_pr...  63.5 us
    ppermute x23, waiting for transfers between devices, rotated(): lax.ppermute(value, axis, [(i, (i + steps) % count) for i in range(count)])  53.5 us
    ppermute x23, starting transfers between devices, rotated(): lax.ppermute(value, axis, [(i, (i + steps) % count) for i in range(count)])  32.4 us
    ppermute x14, waiting for transfers between devices, swapped(): return lax.ppermute(value, axis, [(i, i ^ bit) for i in range(count)])  19.7 us
    ppermute x14, starting transfers between devices, swapped(): return lax.ppermute(value, axis, [(i, i ^ bit) for i in range(count)])  11.9 us
    unnamed x32, local copies, waits for them, and re-layouts  7.04 us
    dynamic_slice x2, local copies, waits for them, and re-layouts, quarter(): return lax.dynamic_slice_in_dim(weight, place * rows, rows, 0)  4.33 us
  transfers between devices with their start and end apart: 38, of which 17 were waited for; matrix products, arithmetic and copies ran while one was open for 3% of the time, Pallas kernels for 18%

profile of v3, /device:TPU:0, one launch (start us, length us, event | category | flops | bytes accessed | tf_op | source)
XLA Modules:
  0.0 206.6 jit_solution(14182846566353006317)
XLA Ops:
  0.7 2.2 %dynamic-slice_bitcast_fusion.1 = bf16[320,1280]{1,0:T(8,128)(2,1)} fusion(bf16[1,1280,1280]{2,1,0:T(8,128)(2,1)} %param.12, s32[]{:T(128)S(6)} %select_n.67), kind=kLoop, calls=%fused_computation.8 | loop fusion | bytes 1638404 | tf_op jit(solution)/shard_map/dynamic_slice | solution.py:42
  2.9 3.0 %collective-permute-start.5 = (bf16[320,1280]{1,0:T(8,128)(2,1)}, bf16[320,1280]{1,0:T(8,128)(2,1)}, u32[]{:S(2)}, u32[]{:S(2)}) collective-permute-start(bf16[320,1280]{1,0:T(8,128)(2,1)} %dynamic-slice_bitcast_fusion.1), channel_id=1, source_target_pairs={{0,16},{16,0},{1,17},{17,1},{2,18},{18,2},{3,19},{19,3},{4,20},{20... | collective-permute-start | bytes 2457608 | tf_op jit(solution)/shard_map/ppermute | solution.py:26
  5.9 1.6 collective-permute-start.3
  7.5 2.2 %collective-permute-start.4 = (bf16[128,1280]{1,0:T(8,128)(2,1)}, bf16[128,1280]{1,0:T(8,128)(2,1)}, u32[]{:S(2)}, u32[]{:S(2)}) collective-permute-start(bf16[128,1280]{1,0:T(8,128)(2,1)} %bitcast.64), channel_id=1, source_target_pairs={{0,3},{1,0},{2,1},{3,2},{4,7},{5,4},{6,5},{7,6},{8,11},{9,8},{10,9... | collective-permute-start | bytes 983048 | tf_op jit(solution)/shard_map/ppermute | solution.py:21
  9.7 0.8 collective-permute-start.7
  10.5 2.1 %dynamic-slice_bitcast_fusion = bf16[320,1280]{1,0:T(8,128)(2,1)} fusion(bf16[1,1280,1280]{2,1,0:T(8,128)(2,1)} %param.13, s32[]{:T(128)S(6)} %select_n.67), kind=kLoop, calls=%fused_computation.7 | loop fusion | bytes 1638404 | tf_op jit(solution)/shard_map/dynamic_slice | solution.py:42
  13.3 12.0 %collective-permute-done.5.p0.refs_6_.refs_4_.refs_7_ = bf16[320,1280]{1,0:T(8,128)(2,1)} collective-permute-done((bf16[320,1280]{1,0:T(8,128)(2,1)}, bf16[320,1280]{1,0:T(8,128)(2,1)}, u32[]{:S(2)}, u32[]{:S(2)}) %collective-permute-start.5) | collective-permute-done | bytes 819232 | tf_op jit(solution)/shard_map/ppermute | solution.py:26
  25.3 2.0 collective-permute-start.9
  27.5 3.7 %collective-permute-start.2 = (bf16[1,1280]{1,0:T(2,128)(2,1)S(1)}, bf16[1,1280]{1,0:T(2,128)(2,1)S(1)}, u32[]{:S(2)}, u32[]{:S(2)}) collective-permute-start(bf16[1,1280]{1,0:T(2,128)(2,1)S(1)} %broadcast_select_fusion), channel_id=1, source_target_pairs={{0,3},{1,0},{2,1},{3,2},{4,7},{5,4},{6,5},{7,6},{8,11},{9,8},{10,9... | collective-permute-start | bytes 7688 | tf_op jit(solution)/shard_map/ppermute | solution.py:21
  31.1 2.5 %collective-permute-start.1 = (bf16[1,1280]{1,0:T(2,128)(2,1)S(1)}, bf16[1,1280]{1,0:T(2,128)(2,1)S(1)}, u32[]{:S(2)}, u32[]{:S(2)}) collective-permute-start(bf16[1,1280]{1,0:T(2,128)(2,1)S(1)} %broadcast_select_fusion), channel_id=1, source_target_pairs={{0,2},{1,3},{2,0},{3,1},{4,6},{5,7},{6,4},{7,5},{8,10},{9,11},{10,... | collective-permute-start | bytes 7688 | tf_op jit(solution)/shard_map/ppermute | solution.py:21
  33.6 1.9 copy-done.2
  35.5 8.2 %block0_partial.4 = (bf16[128,1280]{1,0:T(8,128)(2,1)S(1)}, bf16[128,1280]{1,0:T(8,128)(2,1)S(1)}) custom-call(s32[3]{0:T(128)S(1)} %pad_add_fusion.sel_ref, bf16[128,1280]{1,0:T(8,128)(2,1)} %collective-permute-done.3.refs_0_.part, bf16[128,1280]{1,0:T(8,128)(2,1)} %collective-permute-done.4.refs_1_.part, ...), custom_call_target="tpu_custom_call" | custom-call | flops 1677721600 | bytes 7869440 | tf_op jit(solution)/shard_map/block0_partial/pallas_call | solution.py:126
  43.8 2.1 %collective-permute-start.11 = (bf16[128,1280]{1,0:T(8,128)(2,1)S(1)}, bf16[128,1280]{1,0:T(8,128)(2,1)S(1)}, u32[]{:S(2)}, u32[]{:S(2)}) collective-permute-start(bf16[128,1280]{1,0:T(8,128)(2,1)S(1)} %get-tuple-element.46), channel_id=1, source_target_pairs={{0,1},{1,2},{2,3},{3,0},{4,5},{5,6},{6,7},{7,4},{8,9},{9,10},{10,1... | collective-permute-start | bytes 983048 | tf_op jit(solution)/shard_map/ppermute | solution.py:21
  45.8 1.8 collective-permute-start.6
  47.7 6.4 %block0_partial.5 = bf16[128,1280]{1,0:T(8,128)(2,1)S(1)} custom-call(s32[3]{0:T(128)S(1)} %pad_add_fusion.sel_ref, bf16[128,1280]{1,0:T(8,128)(2,1)} %collective-permute-done.7.refs_0_.part, f32[1,1280]{1,0:T(1,128)S(1)} %get-tuple-element.103.refs_1_.refs_2_.gain, bf16[1280,1280]{1,0:T(8,128)(2,1)S(1)} %bitcast.47, bf16[1280,1280]{1,0:T(8,128)(2,1)S(1)} %bitcast.57), custom_call_target="tpu_custom_call" | custom-call | flops 838860800 | bytes 7214080 | tf_op jit(solution)/shard_map/block0_partial/pallas_call | solution.py:126
  54.2 1.6 collective-permute-start.12
  55.8 0.6 fusion.32
  56.4 0.6 collective-permute-start
  56.9 5.4 %block0_partial.3 = bf16[128,1280]{1,0:T(8,128)(2,1)S(1)} custom-call(s32[3]{0:T(128)S(1)} %pad_add_fusion.sel_ref, bf16[128,1280]{1,0:T(8,128)(2,1)S(1)} %bitcast.66, f32[1,1280]{1,0:T(1,128)S(1)} %get-tuple-element.103.refs_1_.refs_2_.gain, bf16[1280,1280]{1,0:T(8,128)(2,1)S(1)} %bitcast.48, bf16[1280,1280]{1,0:T(8,128)(2,1)S(1)} %bitcast.58), custom_call_target="tpu_custom_call" | custom-call | flops 838860800 | bytes 7214080 | tf_op jit(solution)/shard_map/block0_partial/pallas_call | solution.py:126
  63.6 0.7 collective-permute-done
  64.5 6.7 %collective-permute-done.10 = bf16[128,1280]{1,0:T(8,128)(2,1)S(1)} collective-permute-done((bf16[128,1280]{1,0:T(8,128)(2,1)S(1)}, bf16[128,1280]{1,0:T(8,128)(2,1)S(1)}, u32[]{:S(2)}, u32[]{:S(2)}) %collective-permute-start.10) | collective-permute-done | bytes 327712 | tf_op jit(solution)/shard_map/ppermute | solution.py:21
  71.8 3.4 %collective-permute-start.13 = (bf16[1,64,1280]{2,1,0:T(8,128)(2,1)S(1)}, bf16[1,64,1280]{2,1,0:T(8,128)(2,1)S(1)}, u32[]{:S(2)}, u32[]{:S(2)}) collective-permute-start(bf16[1,64,1280]{2,1,0:T(8,128)(2,1)S(1)} %slice.101), channel_id=1, source_target_pairs={{0,16},{1,17},{2,18},{3,19},{4,20},{5,21},{6,22},{7,23},{8,24},{9,... | collective-permute-start | bytes 491528 | tf_op jit(solution)/shard_map/ppermute | solution.py:517
  75.9 2.1 %collective-permute-done.13 = bf16[1,64,1280]{2,1,0:T(8,128)(2,1)S(1)} collective-permute-done((bf16[1,64,1280]{2,1,0:T(8,128)(2,1)S(1)}, bf16[1,64,1280]{2,1,0:T(8,128)(2,1)S(1)}, u32[]{:S(2)}, u32[]{:S(2)}) %collective-permute-start.13) | collective-permute-done | bytes 163872 | tf_op jit(solution)/shard_map/ppermute | solution.py:517
  78.1 2.3 %collective-permute-start.15 = (bf16[64,1280]{1,0:T(8,128)(2,1)S(1)}, bf16[64,1280]{1,0:T(8,128)(2,1)S(1)}, u32[]{:S(2)}, u32[]{:S(2)}) collective-permute-start(bf16[64,1280]{1,0:T(8,128)(2,1)S(1)} %fusion.11.refs_0_), channel_id=1, source_target_pairs={{0,3},{1,0},{2,1},{3,2},{4,7},{5,4},{6,5},{7,6},{8,11},{9,8},{10,9... | collective-permute-start | bytes 491528 | tf_op jit(solution)/shard_map/ppermute | solution.py:21
  80.9 3.2 %collective-permute-done.15.refs_2_ = bf16[64,1280]{1,0:T(8,128)(2,1)S(1)} collective-permute-done((bf16[64,1280]{1,0:T(8,128)(2,1)S(1)}, bf16[64,1280]{1,0:T(8,128)(2,1)S(1)}, u32[]{:S(2)}, u32[]{:S(2)}) %collective-permute-start.15) | collective-permute-done | bytes 163872 | tf_op jit(solution)/shard_map/ppermute | solution.py:21
  84.1 6.5 %collective-permute-done.20.refs_0_ = bf16[64,1280]{1,0:T(8,128)(2,1)S(1)} collective-permute-done((bf16[64,1280]{1,0:T(8,128)(2,1)S(1)}, bf16[64,1280]{1,0:T(8,128)(2,1)S(1)}, u32[]{:S(2)}, u32[]{:S(2)}) %collective-permute-start.20) | collective-permute-done | bytes 163872 | tf_op jit(solution)/shard_map/ppermute | solution.py:21
  90.9 7.1 %collective-permute-done.14.refs_1_ = bf16[64,1280]{1,0:T(8,128)(2,1)S(1)} collective-permute-done((bf16[64,1280]{1,0:T(8,128)(2,1)S(1)}, bf16[64,1280]{1,0:T(8,128)(2,1)S(1)}, u32[]{:S(2)}, u32[]{:S(2)}) %collective-permute-start.14) | collective-permute-done | bytes 163872 | tf_op jit(solution)/shard_map/ppermute | solution.py:21
  98.1 2.9 %block0_state.4 = (bf16[128,1280]{1,0:T(8,128)(2,1)S(1)}, bf16[128,1280]{1,0:T(8,128)(2,1)S(1)}, bf16[640,128]{1,0:T(8,128)(2,1)S(1)}) custom-call(s32[3]{0:T(128)S(1)} %pad_add_fusion.sel_ref, bf16[128,1280]{1,0:T(8,128)(2,1)S(1)} %bitcast.67, f32[1,1280]{1,0:T(1,128)S(1)} %get-tuple-element.103.refs_1_.refs_2_.gain, bf16[1280,1280]{1,0:T(8,128)(2,1)S(1)} %bitcast.49, ...), custom_call_target="tpu_custom_call" | custom-call | flops 419430400 | bytes 7705600 | tf_op jit(solution)/shard_map/block0_state/pallas_call | solution.py:126
  101.0 0.7 copy-done.5
  101.7 4.2 %block0_state.5 = (bf16[128,1280]{1,0:T(8,128)(2,1)S(1)}, bf16[128,1280]{1,0:T(8,128)(2,1)S(1)}, bf16[640,128]{1,0:T(8,128)(2,1)S(1)}) custom-call(s32[3]{0:T(128)S(1)} %pad_add_fusion.sel_ref, bf16[128,1280]{1,0:T(8,128)(2,1)} %collective-permute-done.3.refs_0_.part, f32[1,1280]{1,0:T(1,128)S(1)} %get-tuple-element.103.refs_1_.refs_2_.gain, ...), custom_call_target="tpu_custom_call" | custom-call | flops 419430400 | bytes 7705600 | tf_op jit(solution)/shard_map/block0_state/pallas_call | solution.py:126
  105.9 0.7 copy-done.7
  106.6 7.7 %reward_forward.2 = (bf16[64,1280]{1,0:T(8,128)(2,1)S(1)}, bf16[64,1280]{1,0:T(8,128)(2,1)S(1)}, bf16[64,1280]{1,0:T(8,128)(2,1)S(1)}, f32[8,1280]{1,0:T(8,128)S...) custom-call(s32[3]{0:T(128)S(1)} %pad_add_fusion.sel_ref, bf16[64,1280]{1,0:T(8,128)(2,1)S(1)} %fusion.11.refs_0_, ...), custom_call_target="tpu_custom_call" | custom-call | flops 629145600 | bytes 14218240 | tf_op jit(solution)/shard_map/reward_forward/pallas_call | solution.py:126
  114.3 5.3 %reward_forward.3 = (bf16[64,1280]{1,0:T(8,128)(2,1)S(1)}, f32[8,1280]{1,0:T(8,128)S(1)}) custom-call(s32[3]{0:T(128)S(1)} %pad_add_fusion.sel_ref, bf16[64,1280]{1,0:T(8,128)(2,1)S(1)} %collective-permute-done.20.refs_0_, f32[1,1280]{1,0:T(1,128)S(1)} %get-tuple-element.102.refs_3_.refs_1_, bf16[1280,1280]{1,0:T(8,128)(2,1)S(1)} %bitcast.52, ...), custom_call_target="tpu_custom_call" | custom-call | flops 209715200 | bytes 13480960 | tf_op jit(solution)/shard_map/reward_forward/pallas_call | solution.py:126
  119.7 1.8 collective-permute-start.23
  121.6 0.6 collective-permute-start.21
  122.2 1.3 collective-permute-done.23
  123.5 3.7 %collective-permute-done.21 = f32[4,1,1280]{2,0,1:T(4,128)S(1)} collective-permute-done((f32[4,1,1280]{2,0,1:T(4,128)S(1)}, f32[4,1,1280]{2,0,1:T(4,128)S(1)}, u32[]{:S(2)}, u32[]{:S(2)}) %collective-permute-start.21) | collective-permute-done | bytes 20512 | tf_op jit(solution)/shard_map/ppermute | solution.py:21
  127.6 5.8 %reward_back.1 = (bf16[64,1280]{1,0:T(8,128)(2,1)S(1)}, bf16[64,1280]{1,0:T(8,128)(2,1)S(1)}, bf16[64,1280]{1,0:T(8,128)(2,1)S(1)}, bf16[64,1280]{1,0:T(8,128)(2,1)S(1)}) custom-call(s32[3]{0:T(128)S(1)} %pad_add_fusion.sel_ref, bf16[16,1280]{1,0:T(8,128)(2,1)S(1)} %pad.4.refs_0_, bf16[64,1280]{1,0:T(8,128)(2,1)S(1)} %get-tuple-element.63.refs_1_, ...), custom_call_target="tpu_custom_call" | custom-call | flops 838860800 | bytes 14458880 | tf_op jit(solution)/shard_map/reward_back/pallas_call | solution.py:126
  133.4 1.3 collective-permute-start.25
  134.8 2.6 %collective-permute-start.24 = (bf16[64,1280]{1,0:T(8,128)(2,1)S(1)}, bf16[64,1280]{1,0:T(8,128)(2,1)S(1)}, u32[]{:S(2)}, u32[]{:S(2)}) collective-permute-start(bf16[64,1280]{1,0:T(8,128)(2,1)S(1)} %get-tuple-element.68), channel_id=1, source_target_pairs={{0,3},{1,0},{2,1},{3,2},{4,7},{5,4},{6,5},{7,6},{8,11},{9,8},{10,9... | collective-permute-start | bytes 491528 | tf_op jit(solution)/shard_map/ppermute | solution.py:21
  137.4 3.9 %block0_state.6 = (bf16[128,1280]{1,0:T(8,128)(2,1)S(1)}, bf16[128,1280]{1,0:T(8,128)(2,1)S(1)}, bf16[640,128]{1,0:T(8,128)(2,1)S(1)}) custom-call(s32[3]{0:T(128)S(1)} %pad_add_fusion.sel_ref, bf16[128,1280]{1,0:T(8,128)(2,1)} %collective-permute-done.7.refs_0_.part, f32[1,1280]{1,0:T(1,128)S(1)} %get-tuple-element.103.refs_1_.refs_2_.gain, ...), custom_call_target="tpu_custom_call" | custom-call | flops 419430400 | bytes 7705600 | tf_op jit(solution)/shard_map/block0_state/pallas_call | solution.py:126
  141.3 0.7 copy-done.9
  142.0 3.9 %block0_state.7 = (bf16[128,1280]{1,0:T(8,128)(2,1)S(1)}, bf16[128,1280]{1,0:T(8,128)(2,1)S(1)}, bf16[640,128]{1,0:T(8,128)(2,1)S(1)}) custom-call(s32[3]{0:T(128)S(1)} %pad_add_fusion.sel_ref, bf16[128,1280]{1,0:T(8,128)(2,1)} %collective-permute-done.4.refs_1_.part, f32[1,1280]{1,0:T(1,128)S(1)} %get-tuple-element.103.refs_1_.refs_2_.gain, ...), custom_call_target="tpu_custom_call" | custom-call | flops 419430400 | bytes 7705600 | tf_op jit(solution)/shard_map/block0_state/pallas_call | solution.py:126
  146.8 3.1 %collective-permute-start.28 = (bf16[64,1280]{1,0:T(8,128)(2,1)S(1)}, bf16[64,1280]{1,0:T(8,128)(2,1)S(1)}, u32[]{:S(2)}, u32[]{:S(2)}) collective-permute-start(bf16[64,1280]{1,0:T(8,128)(2,1)S(1)} %multiply_convert_fusion.refs_0_), channel_id=1, source_target_pairs={{0,1},{1,2},{2,3},{3,0},{4,5},{5,6},{6,7},{7,4},{8,9},{9,10},{10,1... | collective-permute-start | bytes 491528 | tf_op jit(solution)/shard_map/ppermute | solution.py:21
  149.9 1.1 collective-permute-start.30
  151.0 1.4 collective-permute-start.32
  152.8 3.0 %collective-permute-done.28.refs_2_ = bf16[64,1280]{1,0:T(8,128)(2,1)S(1)} collective-permute-done((bf16[64,1280]{1,0:T(8,128)(2,1)S(1)}, bf16[64,1280]{1,0:T(8,128)(2,1)S(1)}, u32[]{:S(2)}, u32[]{:S(2)}) %collective-permute-start.28) | collective-permute-done | bytes 163872 | tf_op jit(solution)/shard_map/ppermute | solution.py:21
  155.8 1.2 collective-permute-start.29
  156.9 4.0 %collective-permute-done.30.refs_4_ = bf16[64,1280]{1,0:T(8,128)(2,1)S(1)} collective-permute-done((bf16[64,1280]{1,0:T(8,128)(2,1)S(1)}, bf16[64,1280]{1,0:T(8,128)(2,1)S(1)}, u32[]{:S(2)}, u32[]{:S(2)}) %collective-permute-start.30) | collective-permute-done | bytes 163872 | tf_op jit(solution)/shard_map/ppermute | solution.py:21
  160.9 2.0 collective-permute-start.33
  163.0 5.0 %collective-permute-done.31.refs_5_ = bf16[64,1280]{1,0:T(8,128)(2,1)S(1)} collective-permute-done((bf16[64,1280]{1,0:T(8,128)(2,1)S(1)}, bf16[64,1280]{1,0:T(8,128)(2,1)S(1)}, u32[]{:S(2)}, u32[]{:S(2)}) %collective-permute-start.31) | collective-permute-done | bytes 163872 | tf_op jit(solution)/shard_map/ppermute | solution.py:26
  168.0 2.5 %collective-permute-done.33.refs_7_ = bf16[64,1280]{1,0:T(8,128)(2,1)S(1)} collective-permute-done((bf16[64,1280]{1,0:T(8,128)(2,1)S(1)}, bf16[64,1280]{1,0:T(8,128)(2,1)S(1)}, u32[]{:S(2)}, u32[]{:S(2)}) %collective-permute-start.33) | collective-permute-done | bytes 163872 | tf_op jit(solution)/shard_map/ppermute | solution.py:26
  170.5 7.1 %grad_in.1 = (bf16[2,160,1280]{2,1,0:T(8,128)(2,1)S(1)}, bf16[2,160,1280]{2,1,0:T(8,128)(2,1)S(1)}) custom-call(s32[3]{0:T(128)S(1)} %pad_add_fusion.sel_ref, bf16[64,1280]{1,0:T(8,128)(2,1)S(1)} %multiply_convert_fusion.refs_0_, bf16[64,1280]{1,0:T(8,128)(2,1)S(1)} %collective-permute-done.27.refs_1_, bf16[64,1280]{1,0:T(8,128)(2,1)S(1)} %collective-permute-done.28.refs_2_, ...), custom_call_target="tpu_custom_call" | custom-call | flops 2516582400 | bytes 11468800 | tf_op jit(solution)/shard_map/grad_in/pallas_call | solution.py:126
  177.7 1.0 copy-done.8
  178.7 1.0 copy-done.10
  179.7 1.0 copy-done.12
  180.6 2.8 %grad_out.1 = (bf16[2,160,1280]{2,1,0:T(8,128)(2,1)S(1)}, bf16[2,160,1280]{2,1,0:T(8,128)(2,1)S(1)}) custom-call(s32[3]{0:T(128)S(1)} %pad_add_fusion.sel_ref, bf16[64,1280]{1,0:T(8,128)(2,1)S(1)} %multiply_convert_fusion.refs_0_, bf16[64,1280]{1,0:T(8,128)(2,1)S(1)} %collective-permute-done.27.refs_1_, ...), custom_call_target="tpu_custom_call" | custom-call | flops 838860800 | bytes 4259840 | tf_op jit(solution)/shard_map/grad_out/pallas_call | solution.py:126
  184.0 1.3 convert_add_fusion.1
  185.4 1.6 collective-permute-start.35
  187.2 0.6 collective-permute-start.37
  187.8 10.0 %collective-permute-done.35 = bf16[160,1280]{1,0:T(8,128)(2,1)S(1)} collective-permute-done((bf16[160,1280]{1,0:T(8,128)(2,1)S(1)}, bf16[160,1280]{1,0:T(8,128)(2,1)S(1)}, u32[]{:S(2)}, u32[]{:S(2)}) %collective-permute-start.35) | collective-permute-done | bytes 409632 | tf_op jit(solution)/shard_map/ppermute | solution.py:21
  197.7 1.0 bitcast_add_fusion.1
  198.7 6.9 %collective-permute-done.37 = bf16[160,1280]{1,0:T(8,128)(2,1)S(1)} collective-permute-done((bf16[160,1280]{1,0:T(8,128)(2,1)S(1)}, bf16[160,1280]{1,0:T(8,128)(2,1)S(1)}, u32[]{:S(2)}, u32[]{:S(2)}) %collective-permute-start.37) | collective-permute-done | bytes 409632 | tf_op jit(solution)/shard_map/ppermute | solution.py:21
  205.6 1.0 bitcast_add_fusion
  (107 shorter events, 5.9 us)
Async XLA Ops:
  0.6 12.5 %copy-start = (bf16[64,1280]{1,0:T(8,128)(2,1)S(1)}, bf16[64,1280]{1,0:T(8,128)(2,1)}, u32[]{:S(2)}) copy-start(bf16[64,1280]{1,0:T(8,128)(2,1)} %param.10) | copy-start | bytes 491524
  0.7 12.5 %copy-start.15 = (s32[2]{0:T(128)S(1)}, s32[2]{0:T(128)}, u32[]{:S(2)}) copy-start(s32[2]{0:T(128)} %param.9) | copy-start | bytes 28
  0.7 26.7 %copy-start.13 = (f32[2,1280]{1,0:T(2,128)S(1)}, f32[2,1280]{1,0:T(2,128)}, u32[]{:S(2)}) copy-start(f32[2,1280]{1,0:T(2,128)} %param.11) | copy-start | bytes 30724
  0.7 32.9 %copy-start.1 = (bf16[1,1280,1280]{2,1,0:T(8,128)(2,1)S(1)}, bf16[1,1280,1280]{2,1,0:T(8,128)(2,1)}, u32[]{:S(2)}) copy-start(bf16[1,1280,1280]{2,1,0:T(8,128)(2,1)} %param.12) | copy-start | bytes 9830404
  2.9 22.4 %collective-permute-start.5 = (bf16[320,1280]{1,0:T(8,128)(2,1)}, bf16[320,1280]{1,0:T(8,128)(2,1)}, u32[]{:S(2)}, u32[]{:S(2)}) collective-permute-start(bf16[320,1280]{1,0:T(8,128)(2,1)} %dynamic-slice_bitcast_fusion.1), channel_id=1, source_target_pairs={{0,16},{16,0},{1,17},{17,1},{2,18},{18,2},{3,19},{19,3},{4,20},{20... | collective-permute-start | bytes 2457608 | tf_op jit(solution)/shard_map/ppermute | solution.py:26
  5.9 21.5 %collective-permute-start.3 = (bf16[128,1280]{1,0:T(8,128)(2,1)}, bf16[128,1280]{1,0:T(8,128)(2,1)}, u32[]{:S(2)}, u32[]{:S(2)}) collective-permute-start(bf16[128,1280]{1,0:T(8,128)(2,1)} %bitcast.63), channel_id=1, source_target_pairs={{0,1},{1,2},{2,3},{3,0},{4,5},{5,6},{6,7},{7,4},{8,9},{9,10},{10,1... | collective-permute-start | bytes 983048 | tf_op jit(solution)/shard_map/ppermute | solution.py:21
  7.5 23.6 %collective-permute-start.4 = (bf16[128,1280]{1,0:T(8,128)(2,1)}, bf16[128,1280]{1,0:T(8,128)(2,1)}, u32[]{:S(2)}, u32[]{:S(2)}) collective-permute-start(bf16[128,1280]{1,0:T(8,128)(2,1)} %bitcast.64), channel_id=1, source_target_pairs={{0,3},{1,0},{2,1},{3,2},{4,7},{5,4},{6,5},{7,6},{8,11},{9,8},{10,9... | collective-permute-start | bytes 983048 | tf_op jit(solution)/shard_map/ppermute | solution.py:21
  9.7 34.0 %collective-permute-start.7 = (bf16[128,1280]{1,0:T(8,128)(2,1)}, bf16[128,1280]{1,0:T(8,128)(2,1)}, u32[]{:S(2)}, u32[]{:S(2)}) collective-permute-start(bf16[128,1280]{1,0:T(8,128)(2,1)} %bitcast.65), channel_id=1, source_target_pairs={{0,2},{1,3},{2,0},{3,1},{4,6},{5,7},{6,4},{7,5},{8,10},{9,11},{10,... | collective-permute-start | bytes 983048 | tf_op jit(solution)/shard_map/ppermute | solution.py:21
  12.6 33.2 %collective-permute-start.8 = (bf16[320,1280]{1,0:T(8,128)(2,1)}, bf16[320,1280]{1,0:T(8,128)(2,1)}, u32[]{:S(2)}, u32[]{:S(2)}) collective-permute-start(bf16[320,1280]{1,0:T(8,128)(2,1)} %dynamic-slice_bitcast_fusion), channel_id=1, source_target_pairs={{0,16},{16,0},{1,17},{17,1},{2,18},{18,2},{3,19},{19,3},{4,20},{20... | collective-permute-start | bytes 2457608 | tf_op jit(solution)/shard_map/ppermute | solution.py:26
  25.3 22.4 %collective-permute-start.9 = (bf16[320,1280]{1,0:T(8,128)(2,1)}, bf16[320,1280]{1,0:T(8,128)(2,1)S(1)}, u32[]{:S(2)}, u32[]{:S(2)}) collective-permute-start(bf16[320,1280]{1,0:T(8,128)(2,1)} %collective-permute-done.5.p0.refs_6_.refs_4_.refs_7_), channel_id=1, source_target_pairs={{0,8},{4,12},{8,0},{12,4},{1,9},{5,13},{9,1},{13,5},{2,10},{6,14},... | collective-permute-start | bytes 2457608 | tf_op jit(solution)/shard_map/ppermute | solution.py:26
  27.5 26.7 %collective-permute-start.2 = (bf16[1,1280]{1,0:T(2,128)(2,1)S(1)}, bf16[1,1280]{1,0:T(2,128)(2,1)S(1)}, u32[]{:S(2)}, u32[]{:S(2)}) collective-permute-start(bf16[1,1280]{1,0:T(2,128)(2,1)S(1)} %broadcast_select_fusion), channel_id=1, source_target_pairs={{0,3},{1,0},{2,1},{3,2},{4,7},{5,4},{6,5},{7,6},{8,11},{9,8},{10,9... | collective-permute-start | bytes 7688 | tf_op jit(solution)/shard_map/ppermute | solution.py:21
  31.1 25.2 %collective-permute-start.1 = (bf16[1,1280]{1,0:T(2,128)(2,1)S(1)}, bf16[1,1280]{1,0:T(2,128)(2,1)S(1)}, u32[]{:S(2)}, u32[]{:S(2)}) collective-permute-start(bf16[1,1280]{1,0:T(2,128)(2,1)S(1)} %broadcast_select_fusion), channel_id=1, source_target_pairs={{0,2},{1,3},{2,0},{3,1},{4,6},{5,7},{6,4},{7,5},{8,10},{9,11},{10,... | collective-permute-start | bytes 7688 | tf_op jit(solution)/shard_map/ppermute | solution.py:21
  33.6 1.9 copy-start.2
  43.8 20.7 %collective-permute-start.11 = (bf16[128,1280]{1,0:T(8,128)(2,1)S(1)}, bf16[128,1280]{1,0:T(8,128)(2,1)S(1)}, u32[]{:S(2)}, u32[]{:S(2)}) collective-permute-start(bf16[128,1280]{1,0:T(8,128)(2,1)S(1)} %get-tuple-element.46), channel_id=1, source_target_pairs={{0,1},{1,2},{2,3},{3,0},{4,5},{5,6},{6,7},{7,4},{8,9},{9,10},{10,1... | collective-permute-start | bytes 983048 | tf_op jit(solution)/shard_map/ppermute | solution.py:21
  45.8 8.3 %copy-start.14 = (s32[2]{0:T(128)S(1)}, s32[2]{0:T(128)}, u32[]{:S(2)}) copy-start(s32[2]{0:T(128)} %param.8) | copy-start | bytes 28
  45.8 11.1 %copy-start.4 = (bf16[2,64,1280]{2,1,0:T(8,128)(2,1)S(1)}, bf16[2,64,1280]{2,1,0:T(8,128)(2,1)}, u32[]{:S(2)}) copy-start(bf16[2,64,1280]{2,1,0:T(8,128)(2,1)} %param.7) | copy-start | bytes 983044
  45.8 18.6 %collective-permute-start.6 = (bf16[128,1280]{1,0:T(8,128)(2,1)S(1)}, bf16[128,1280]{1,0:T(8,128)(2,1)S(1)}, u32[]{:S(2)}, u32[]{:S(2)}) collective-permute-start(bf16[128,1280]{1,0:T(8,128)(2,1)S(1)} %get-tuple-element.44), channel_id=1, source_target_pairs={{0,3},{1,0},{2,1},{3,2},{4,7},{5,4},{6,5},{7,6},{8,11},{9,8},{10,9... | collective-permute-start | bytes 983048 | tf_op jit(solution)/shard_map/ppermute | solution.py:21
  54.1 17.1 %collective-permute-start.10 = (bf16[128,1280]{1,0:T(8,128)(2,1)S(1)}, bf16[128,1280]{1,0:T(8,128)(2,1)S(1)}, u32[]{:S(2)}, u32[]{:S(2)}) collective-permute-start(bf16[128,1280]{1,0:T(8,128)(2,1)S(1)} %block0_partial.5), channel_id=1, source_target_pairs={{0,2},{1,3},{2,0},{3,1},{4,6},{5,7},{6,4},{7,5},{8,10},{9,11},{10,... | collective-permute-start | bytes 983048 | tf_op jit(solution)/shard_map/ppermute | solution.py:21
  54.2 17.3 %collective-permute-start.12 = (bf16[320,1280]{1,0:T(8,128)(2,1)}, bf16[320,1280]{1,0:T(8,128)(2,1)S(1)}, u32[]{:S(2)}, u32[]{:S(2)}) collective-permute-start(bf16[320,1280]{1,0:T(8,128)(2,1)} %collective-permute-done.8.refs_10_.refs_8_.refs_11_.refs_17_), channel_id=1, source_target_pairs={{0,8},{4,12},{8,0},{12,4},{1,9},{5,13},{9,1},{13,5},{2,10},{6,14},... | collective-permute-start | bytes 2457608 | tf_op jit(solution)/shard_map/ppermute | solution.py:26
  56.4 8.0 %collective-permute-start = (bf16[1,1280]{1,0:T(2,128)(2,1)S(1)}, bf16[1,1280]{1,0:T(2,128)(2,1)S(1)}, u32[]{:S(2)}, u32[]{:S(2)}) collective-permute-start(bf16[1,1280]{1,0:T(2,128)(2,1)S(1)} %broadcast_select_fusion), channel_id=1, source_target_pairs={{0,1},{1,2},{2,3},{3,0},{4,5},{5,6},{6,7},{7,4},{8,9},{9,10},{10,1... | collective-permute-start | bytes 7688 | tf_op jit(solution)/shard_map/ppermute | solution.py:21
  71.8 6.2 %collective-permute-start.13 = (bf16[1,64,1280]{2,1,0:T(8,128)(2,1)S(1)}, bf16[1,64,1280]{2,1,0:T(8,128)(2,1)S(1)}, u32[]{:S(2)}, u32[]{:S(2)}) collective-permute-start(bf16[1,64,1280]{2,1,0:T(8,128)(2,1)S(1)} %slice.101), channel_id=1, source_target_pairs={{0,16},{1,17},{2,18},{3,19},{4,20},{5,21},{6,22},{7,23},{8,24},{9,... | collective-permute-start | bytes 491528 | tf_op jit(solution)/shard_map/ppermute | solution.py:517
  75.2 22.8 %collective-permute-start.16 = (bf16[320,1280]{1,0:T(8,128)(2,1)}, bf16[320,1280]{1,0:T(8,128)(2,1)S(1)}, u32[]{:S(2)}, u32[]{:S(2)}) collective-permute-start(bf16[320,1280]{1,0:T(8,128)(2,1)} %collective-permute-done.5.p0.refs_6_.refs_4_.refs_7_), channel_id=1, source_target_pairs={{0,4},{4,0},{8,12},{12,8},{1,5},{5,1},{9,13},{13,9},{2,6},{6,2},{1... | collective-permute-start | bytes 2457608 | tf_op jit(solution)/shard_map/ppermute | solution.py:26
  75.3 31.3 %collective-permute-start.18 = (bf16[320,1280]{1,0:T(8,128)(2,1)}, bf16[320,1280]{1,0:T(8,128)(2,1)S(1)}, u32[]{:S(2)}, u32[]{:S(2)}) collective-permute-start(bf16[320,1280]{1,0:T(8,128)(2,1)} %collective-permute-done.8.refs_10_.refs_8_.refs_11_.refs_17_), channel_id=1, source_target_pairs={{0,4},{4,0},{8,12},{12,8},{1,5},{5,1},{9,13},{13,9},{2,6},{6,2},{1... | collective-permute-start | bytes 2457608 | tf_op jit(solution)/shard_map/ppermute | solution.py:26
  75.8 22.2 %collective-permute-start.17 = (bf16[320,1280]{1,0:T(8,128)(2,1)S(1)}, bf16[320,1280]{1,0:T(8,128)(2,1)S(1)}, u32[]{:S(2)}, u32[]{:S(2)}) collective-permute-start(bf16[320,1280]{1,0:T(8,128)(2,1)S(1)} %collective-permute-done.9.p2.refs_8_.refs_6_.refs_9_), channel_id=1, source_target_pairs={{0,4},{4,0},{8,12},{12,8},{1,5},{5,1},{9,13},{13,9},{2,6},{6,2},{1... | collective-permute-start | bytes 2457608 | tf_op jit(solution)/shard_map/ppermute | solution.py:26
  78.1 6.1 %collective-permute-start.15 = (bf16[64,1280]{1,0:T(8,128)(2,1)S(1)}, bf16[64,1280]{1,0:T(8,128)(2,1)S(1)}, u32[]{:S(2)}, u32[]{:S(2)}) collective-permute-start(bf16[64,1280]{1,0:T(8,128)(2,1)S(1)} %fusion.11.refs_0_), channel_id=1, source_target_pairs={{0,3},{1,0},{2,1},{3,2},{4,7},{5,4},{6,5},{7,6},{8,11},{9,8},{10,9... | collective-permute-start | bytes 491528 | tf_op jit(solution)/shard_map/ppermute | solution.py:21
  80.3 10.4 %collective-permute-start.20 = (bf16[64,1280]{1,0:T(8,128)(2,1)S(1)}, bf16[64,1280]{1,0:T(8,128)(2,1)S(1)}, u32[]{:S(2)}, u32[]{:S(2)}) collective-permute-start(bf16[64,1280]{1,0:T(8,128)(2,1)S(1)} %fusion.11.refs_0_), channel_id=1, source_target_pairs={{0,2},{1,3},{2,0},{3,1},{4,6},{5,7},{6,4},{7,5},{8,10},{9,11},{10,... | collective-permute-start | bytes 491528 | tf_op jit(solution)/shard_map/ppermute | solution.py:21
  84.1 22.5 %collective-permute-start.19 = (bf16[320,1280]{1,0:T(8,128)(2,1)S(1)}, bf16[320,1280]{1,0:T(8,128)(2,1)S(1)}, u32[]{:S(2)}, u32[]{:S(2)}) collective-permute-start(bf16[320,1280]{1,0:T(8,128)(2,1)S(1)} %collective-permute-done.12.refs_12_.refs_10_.refs_13_.refs_19_), channel_id=1, source_target_pairs={{0,4},{4,0},{8,12},{12,8},{1,5},{5,1},{9,13},{13,9},{2,6},{6,2},{1... | collective-permute-start | bytes 2457608 | tf_op jit(solution)/shard_map/ppermute | solution.py:26
  90.7 7.3 %collective-permute-start.14 = (bf16[64,1280]{1,0:T(8,128)(2,1)S(1)}, bf16[64,1280]{1,0:T(8,128)(2,1)S(1)}, u32[]{:S(2)}, u32[]{:S(2)}) collective-permute-start(bf16[64,1280]{1,0:T(8,128)(2,1)S(1)} %fusion.11.refs_0_), channel_id=1, source_target_pairs={{0,1},{1,2},{2,3},{3,0},{4,5},{5,6},{6,7},{7,4},{8,9},{9,10},{10,1... | collective-permute-start | bytes 491528 | tf_op jit(solution)/shard_map/ppermute | solution.py:21
  101.0 0.7 copy-start.5
  101.7 4.9 %copy-start.3 = (bf16[1,1280,1280]{2,1,0:T(8,128)(2,1)S(1)}, bf16[1,1280,1280]{2,1,0:T(8,128)(2,1)}, u32[]{:S(2)}) copy-start(bf16[1,1280,1280]{2,1,0:T(8,128)(2,1)} %param.13) | copy-start | bytes 9830404
  105.9 0.7 copy-start.7
  119.7 3.8 %collective-permute-start.23 = (f32[4,1,1280]{2,0,1:T(4,128)S(1)}, f32[4,1,1280]{2,0,1:T(4,128)S(1)}, u32[]{:S(2)}, u32[]{:S(2)}) collective-permute-start(f32[4,1,1280]{2,0,1:T(4,128)S(1)} %pad_maximum_fusion), channel_id=1, source_target_pairs={{0,3},{1,0},{2,1},{3,2},{4,7},{5,4},{6,5},{7,6},{8,11},{9,8},{10,9... | collective-permute-start | bytes 61448 | tf_op jit(solution)/shard_map/ppermute | solution.py:21
  121.5 5.7 %collective-permute-start.22 = (f32[4,1,1280]{2,0,1:T(4,128)S(1)}, f32[4,1,1280]{2,0,1:T(4,128)S(1)}, u32[]{:S(2)}, u32[]{:S(2)}) collective-permute-start(f32[4,1,1280]{2,0,1:T(4,128)S(1)} %pad_maximum_fusion), channel_id=1, source_target_pairs={{0,2},{1,3},{2,0},{3,1},{4,6},{5,7},{6,4},{7,5},{8,10},{9,11},{10,... | collective-permute-start | bytes 61448 | tf_op jit(solution)/shard_map/ppermute | solution.py:21
  121.6 5.6 %collective-permute-start.21 = (f32[4,1,1280]{2,0,1:T(4,128)S(1)}, f32[4,1,1280]{2,0,1:T(4,128)S(1)}, u32[]{:S(2)}, u32[]{:S(2)}) collective-permute-start(f32[4,1,1280]{2,0,1:T(4,128)S(1)} %pad_maximum_fusion), channel_id=1, source_target_pairs={{0,1},{1,2},{2,3},{3,0},{4,5},{5,6},{6,7},{7,4},{8,9},{9,10},{10,1... | collective-permute-start | bytes 61448 | tf_op jit(solution)/shard_map/ppermute | solution.py:21
  133.4 12.6 %collective-permute-start.26 = (bf16[64,1280]{1,0:T(8,128)(2,1)S(1)}, bf16[64,1280]{1,0:T(8,128)(2,1)S(1)}, u32[]{:S(2)}, u32[]{:S(2)}) collective-permute-start(bf16[64,1280]{1,0:T(8,128)(2,1)S(1)} %get-tuple-element.70), channel_id=1, source_target_pairs={{0,1},{1,2},{2,3},{3,0},{4,5},{5,6},{6,7},{7,4},{8,9},{9,10},{10,1... | collective-permute-start | bytes 491528 | tf_op jit(solution)/shard_map/ppermute | solution.py:21
  133.4 12.9 %collective-permute-start.25 = (bf16[64,1280]{1,0:T(8,128)(2,1)S(1)}, bf16[64,1280]{1,0:T(8,128)(2,1)S(1)}, u32[]{:S(2)}, u32[]{:S(2)}) collective-permute-start(bf16[64,1280]{1,0:T(8,128)(2,1)S(1)} %get-tuple-element.69), channel_id=1, source_target_pairs={{0,2},{1,3},{2,0},{3,1},{4,6},{5,7},{6,4},{7,5},{8,10},{9,11},{10,... | collective-permute-start | bytes 491528 | tf_op jit(solution)/shard_map/ppermute | solution.py:21
  134.8 11.5 %collective-permute-start.24 = (bf16[64,1280]{1,0:T(8,128)(2,1)S(1)}, bf16[64,1280]{1,0:T(8,128)(2,1)S(1)}, u32[]{:S(2)}, u32[]{:S(2)}) collective-permute-start(bf16[64,1280]{1,0:T(8,128)(2,1)S(1)} %get-tuple-element.68), channel_id=1, source_target_pairs={{0,3},{1,0},{2,1},{3,2},{4,7},{5,4},{6,5},{7,6},{8,11},{9,8},{10,9... | collective-permute-start | bytes 491528 | tf_op jit(solution)/shard_map/ppermute | solution.py:21
  141.3 0.7 copy-start.9
  145.9 31.7 %copy-start.11 = (bf16[128,1280]{1,0:T(8,128)(2,1)}, bf16[128,1280]{1,0:T(8,128)(2,1)S(1)}, u32[]{:S(2)}) copy-start(bf16[128,1280]{1,0:T(8,128)(2,1)S(1)} %get-tuple-element.74.refs_11_) | copy-start | bytes 983044
  146.8 31.0 %copy-start.6 = (bf16[128,1280]{1,0:T(8,128)(2,1)S(1)}, bf16[128,1280]{1,0:T(8,128)(2,1)}, u32[]{:S(2)}) copy-start(bf16[128,1280]{1,0:T(8,128)(2,1)} %copy-done.5) | copy-start | bytes 983044
  146.8 9.0 %collective-permute-start.28 = (bf16[64,1280]{1,0:T(8,128)(2,1)S(1)}, bf16[64,1280]{1,0:T(8,128)(2,1)S(1)}, u32[]{:S(2)}, u32[]{:S(2)}) collective-permute-start(bf16[64,1280]{1,0:T(8,128)(2,1)S(1)} %multiply_convert_fusion.refs_0_), channel_id=1, source_target_pairs={{0,1},{1,2},{2,3},{3,0},{4,5},{5,6},{6,7},{7,4},{8,9},{9,10},{10,1... | collective-permute-start | bytes 491528 | tf_op jit(solution)/shard_map/ppermute | solution.py:21
  149.9 11.0 %collective-permute-start.30 = (bf16[64,1280]{1,0:T(8,128)(2,1)S(1)}, bf16[64,1280]{1,0:T(8,128)(2,1)S(1)}, u32[]{:S(2)}, u32[]{:S(2)}) collective-permute-start(bf16[64,1280]{1,0:T(8,128)(2,1)S(1)} %multiply_convert_fusion.refs_0_), channel_id=1, source_target_pairs={{0,2},{1,3},{2,0},{3,1},{4,6},{5,7},{6,4},{7,5},{8,10},{9,11},{10,... | collective-permute-start | bytes 491528 | tf_op jit(solution)/shard_map/ppermute | solution.py:21
  151.0 10.0 %collective-permute-start.32 = (bf16[64,1280]{1,0:T(8,128)(2,1)S(1)}, bf16[64,1280]{1,0:T(8,128)(2,1)S(1)}, u32[]{:S(2)}, u32[]{:S(2)}) collective-permute-start(bf16[64,1280]{1,0:T(8,128)(2,1)S(1)} %multiply_convert_fusion.refs_0_), channel_id=1, source_target_pairs={{0,3},{1,0},{2,1},{3,2},{4,7},{5,4},{6,5},{7,6},{8,11},{9,8},{10,9... | collective-permute-start | bytes 491528 | tf_op jit(solution)/shard_map/ppermute | solution.py:21
  152.3 10.6 %collective-permute-start.27 = (bf16[64,1280]{1,0:T(8,128)(2,1)S(1)}, bf16[64,1280]{1,0:T(8,128)(2,1)S(1)}, u32[]{:S(2)}, u32[]{:S(2)}) collective-permute-start(bf16[64,1280]{1,0:T(8,128)(2,1)S(1)} %multiply_convert_fusion.refs_0_), channel_id=1, source_target_pairs={{0,16},{16,0},{1,17},{17,1},{2,18},{18,2},{3,19},{19,3},{4,20},{20... | collective-permute-start | bytes 491528 | tf_op jit(solution)/shard_map/ppermute | solution.py:26
  155.8 7.2 %collective-permute-start.29 = (bf16[64,1280]{1,0:T(8,128)(2,1)S(1)}, bf16[64,1280]{1,0:T(8,128)(2,1)S(1)}, u32[]{:S(2)}, u32[]{:S(2)}) collective-permute-start(bf16[64,1280]{1,0:T(8,128)(2,1)S(1)} %collective-permute-done.28.refs_2_), channel_id=1, source_target_pairs={{0,16},{16,0},{1,17},{17,1},{2,18},{18,2},{3,19},{19,3},{4,20},{20... | collective-permute-start | bytes 491528 | tf_op jit(solution)/shard_map/ppermute | solution.py:26
  160.9 7.1 %collective-permute-start.31 = (bf16[64,1280]{1,0:T(8,128)(2,1)S(1)}, bf16[64,1280]{1,0:T(8,128)(2,1)S(1)}, u32[]{:S(2)}, u32[]{:S(2)}) collective-permute-start(bf16[64,1280]{1,0:T(8,128)(2,1)S(1)} %collective-permute-done.30.refs_4_), channel_id=1, source_target_pairs={{0,16},{16,0},{1,17},{17,1},{2,18},{18,2},{3,19},{19,3},{4,20},{20... | collective-permute-start | bytes 491528 | tf_op jit(solution)/shard_map/ppermute | solution.py:26
  160.9 9.5 %collective-permute-start.33 = (bf16[64,1280]{1,0:T(8,128)(2,1)S(1)}, bf16[64,1280]{1,0:T(8,128)(2,1)S(1)}, u32[]{:S(2)}, u32[]{:S(2)}) collective-permute-start(bf16[64,1280]{1,0:T(8,128)(2,1)S(1)} %collective-permute-done.32.refs_6_), channel_id=1, source_target_pairs={{0,16},{16,0},{1,17},{17,1},{2,18},{18,2},{3,19},{19,3},{4,20},{20... | collective-permute-start | bytes 491528 | tf_op jit(solution)/shard_map/ppermute | solution.py:26
  177.6 6.4 %collective-permute-start.34 = (bf16[2,160,1280]{2,1,0:T(8,128)(2,1)S(1)}, bf16[2,160,1280]{2,1,0:T(8,128)(2,1)}, u32[]{:S(2)}, u32[]{:S(2)}) collective-permute-start(bf16[2,160,1280]{2,1,0:T(8,128)(2,1)S(1)} %get-tuple-element.79), channel_id=1, source_target_pairs={{0,4},{4,0},{8,12},{12,8},{1,5},{5,1},{9,13},{13,9},{2,6},{6,2},{1... | collective-permute-start | bytes 2457608 | tf_op jit(solution)/shard_map/ppermute | solution.py:26
  177.7 1.0 copy-start.8
  178.7 1.0 copy-start.10
  179.7 1.0 copy-start.12
  183.5 3.4 %collective-permute-start.36 = (bf16[2,160,1280]{2,1,0:T(8,128)(2,1)S(1)}, bf16[2,160,1280]{2,1,0:T(8,128)(2,1)S(1)}, u32[]{:S(2)}, u32[]{:S(2)}) collective-permute-start(bf16[2,160,1280]{2,1,0:T(8,128)(2,1)S(1)} %get-tuple-element.81), channel_id=1, source_target_pairs={{0,4},{4,0},{8,12},{12,8},{1,5},{5,1},{9,13},{13,9},{2,6},{6,2},{1... | collective-permute-start | bytes 2457608 | tf_op jit(solution)/shard_map/ppermute | solution.py:26
  185.4 12.4 %collective-permute-start.35 = (bf16[160,1280]{1,0:T(8,128)(2,1)S(1)}, bf16[160,1280]{1,0:T(8,128)(2,1)S(1)}, u32[]{:S(2)}, u32[]{:S(2)}) collective-permute-start(bf16[160,1280]{1,0:T(8,128)(2,1)S(1)} %fusion.3), channel_id=1, source_target_pairs={{0,8},{4,12},{8,0},{12,4},{1,9},{5,13},{9,1},{13,5},{2,10},{6,14},... | collective-permute-start | bytes 1228808 | tf_op jit(solution)/shard_map/ppermute | solution.py:21
  187.2 18.5 %collective-permute-start.37 = (bf16[160,1280]{1,0:T(8,128)(2,1)S(1)}, bf16[160,1280]{1,0:T(8,128)(2,1)S(1)}, u32[]{:S(2)}, u32[]{:S(2)}) collective-permute-start(bf16[160,1280]{1,0:T(8,128)(2,1)S(1)} %fusion.4), channel_id=1, source_target_pairs={{0,8},{4,12},{8,0},{12,4},{1,9},{5,13},{9,1},{13,5},{2,10},{6,14},... | collective-permute-start | bytes 1228808 | tf_op jit(solution)/shard_map/ppermute | solution.py:21

commit v4 on v3

v4 whole, which is shorter than its diff:
```python
import functools
import math

import jax
import jax.numpy as jnp
from jax import lax
from jax.experimental import pallas as pl
from jax.experimental.pallas import tpu as pltpu
from jax.sharding import PartitionSpec as P

STEPS = 50


EPS = 1e-06
VMEM_BYTES = 16 * 1024 * 1024


def rotated(value, axis, steps):
    count = lax.axis_size(axis)
    return lax.ppermute(value, axis, [(i, (i + steps) % count) for i in range(count)])


def swapped(value, axis, bit):
    count = lax.axis_size(axis)
    return lax.ppermute(value, axis, [(i, i ^ bit) for i in range(count)])


def gather_parts(piece):
    return [piece] + [rotated(piece, "tp", k) for k in range(1, lax.axis_size("tp"))]


def reduce_parts(parts):
    total = parts[0].astype(jnp.float32)
    for k in range(1, len(parts)):
        total = total + rotated(parts[k], "tp", -k).astype(jnp.float32)
    return total


def quarter(weight, place):
    rows = weight.shape[0] // 4
    return lax.dynamic_slice_in_dim(weight, place * rows, rows, 0)


def assembled(got, across, place):
    pieces = (got, swapped(got, "dp", 1), across, swapped(across, "dp", 1))
    rows, columns = got.shape
    full = jnp.zeros((4 * rows, columns), got.dtype)
    for q, piece in enumerate(pieces):
        full = lax.dynamic_update_slice_in_dim(full, piece, (place ^ q) * rows, 0)
    return full


def gelu_pair(value):
    cdf = 0.5 * (1.0 + lax.erf(value * (1.0 / math.sqrt(2.0))))
    density = jnp.exp(-0.5 * value * value) * (1.0 / math.sqrt(2.0 * math.pi))
    return (value * cdf, cdf + value * density)


def normed(rows, gain):
    scale = lax.rsqrt(jnp.mean(rows * rows, axis=-1, keepdims=True) + EPS)
    return (rows * scale * gain).astype(jnp.bfloat16)


def dot_nn(a, b):
    return jnp.dot(a, b, preferred_element_type=jnp.float32)


def dot_nt(a, b):
    return lax.dot_general(a, b, (((1,), (1,)), ((), ())), preferred_element_type=jnp.float32)


def tile_of(hidden):
    for tile in (256, 128):
        if hidden % tile == 0:
            return tile
    return hidden


IN_VMEM = pl.BlockSpec(memory_space=pltpu.VMEM)
IN_SMEM = pl.BlockSpec(memory_space=pltpu.SMEM)


def run(body, name, sel, operands, outs, scratch, flops, elements=0):
    read = sum(x.size * x.dtype.itemsize for x in operands)
    written = sum(math.prod(o.shape) * o.dtype.itemsize for o in outs)
    return pl.pallas_call(
        body,
        in_specs=[IN_SMEM] + [IN_VMEM] * len(operands),
        out_specs=[IN_VMEM] * len(outs),
        scratch_shapes=scratch,
        out_shape=outs,
        compiler_params=pltpu.CompilerParams(vmem_limit_bytes=VMEM_BYTES),
        cost_estimate=pl.CostEstimate(
            flops=flops, bytes_accessed=read + written, transcendentals=elements
        ),
        name=name,
    )(sel, *operands)


def bf16(*shape):
    return jax.ShapeDtypeStruct(shape, jnp.bfloat16)


def tiles(hidden):
    tile = tile_of(hidden)
    return [slice(t, t + tile) for t in range(0, hidden, tile)]


def by_section(sel_ref, section, work, own, other):
    @pl.when(sel_ref[0] == section)
    def _():
        work(*own)

    @pl.when(sel_ref[0] != section)
    def _():
        work(*other)


def partial_body(count, sel_ref, *refs):
    parts, (gain, w_in, w_out) = refs[:count], refs[count : count + 3]
    outs, (xn, acc) = refs[count + 3 : 2 * count + 3], refs[2 * count + 3 :]
    rows = parts[0].shape[0]
    for i, part in enumerate(parts):
        xn[i * rows : (i + 1) * rows, :] = normed(part[...].astype(jnp.float32), gain[...])
    for t, tile in enumerate(tiles(w_in.shape[1])):
        act, unused = gelu_pair(dot_nn(xn[...], w_in[:, tile]))
        term = dot_nt(act.astype(jnp.bfloat16), w_out[:, tile])
        acc[...] = term if t == 0 else acc[...] + term
    for i, out in enumerate(outs):
        out[...] = acc[i * rows : (i + 1) * rows, :].astype(jnp.bfloat16)


def block0_partials(parts, gain, w_in, w_out, sel):
    rows, width = parts[0].shape
    hidden, n = w_in.shape[1], len(parts)
    return run(
        functools.partial(partial_body, n),
        "block0_partial",
        sel,
        [*parts, gain, w_in, w_out],
        [bf16(rows, width)] * n,
        [
            pltpu.VMEM((n * rows, width), jnp.bfloat16),
            pltpu.VMEM((n * rows, width), jnp.float32),
        ],
        4 * n * rows * width * hidden,
        n * rows * hidden,
    )


def state_body(sel_ref, part, gain, own, other, act, slope, xn_cols, xn):
    rows = part.shape[0]
    late = rows // 2
    share = xn_cols.shape[0]
    mine = pl.multiple_of((1 - sel_ref[0]) * late, late)
    theirs = pl.multiple_of(sel_ref[0] * late, late)
    for i, start in enumerate((mine, theirs)):
        xn[i * late : (i + 1) * late, :] = normed(
            part[pl.ds(start, late), :].astype(jnp.float32), gain[...]
        )
    cols = xn[:, pl.ds(pl.multiple_of(sel_ref[0] * share, share), share)]
    xn_cols[...] = cols.T

    def work(weight):
        for tile in tiles(weight.shape[1]):
            value, grad = gelu_pair(dot_nn(xn[...], weight[:, tile]))
            act[:, tile] = value.astype(jnp.bfloat16)
            slope[:, tile] = grad.astype(jnp.bfloat16)

    by_section(sel_ref, 0, work, (own,), (other,))


def block0_state(part, gain, own, other, sel):
    rows, width = part.shape
    hidden = own.shape[1]
    return run(
        state_body,
        "block0_state",
        sel,
        [part, gain, own, other],
        [bf16(rows, hidden), bf16(rows, hidden), bf16(width // 2, rows)],
        [pltpu.VMEM((rows, width), jnp.bfloat16)],
        2 * rows * width * hidden,
        2 * rows * hidden,
    )


def reward_body(count, tokens, sel_ref, *refs):
    parts, gain = refs[:count], refs[count]
    own_in, own_out, other_in, other_out = refs[count + 1 : count + 5]
    slopes, (pool, xn) = refs[count + 5 : 2 * count + 5], refs[2 * count + 5 :]
    rows = parts[0].shape[0]
    for i, part in enumerate(parts):
        xn[i * rows : (i + 1) * rows, :] = normed(part[...].astype(jnp.float32), gain[...])

    def work(w_in, w_out):
        for t, tile in enumerate(tiles(w_in.shape[1])):
            act, grad = gelu_pair(dot_nn(xn[...], w_in[:, tile]))
            for i in range(count):
                slopes[i][:, tile] = grad[i * rows : (i + 1) * rows, :].astype(jnp.bfloat16)
            means = [
                jnp.mean(act[start : start + tokens, :], axis=0, keepdims=True)
                for start in range(0, count * rows, tokens)
            ]
            row = lax.broadcasted_iota(jnp.int32, (pool.shape[0], act.shape[1]), 0)
            stacked = jnp.zeros(row.shape, jnp.float32)
            for i, mean in enumerate(means):
                stacked = jnp.where(row == i, mean, stacked)
            term = dot_nt(stacked.astype(jnp.bfloat16), w_out[:, tile])
            pool[...] = term if t == 0 else pool[...] + term

    by_section(sel_ref, 1, work, (own_in, own_out), (other_in, other_out))


def reward_forward(parts, tokens, gain, own, other, sel):
    rows, width = parts[0].shape
    hidden, n = own[0].shape[1], len(parts)
    images = n * rows // tokens
    outs = run(
        functools.partial(reward_body, n, tokens),
        "reward_forward",
        sel,
        [*parts, gain, *own, *other],
        [bf16(rows, hidden)] * n
        + [jax.ShapeDtypeStruct((-(-images // 8) * 8, width), jnp.float32)],
        [pltpu.VMEM((n * rows, width), jnp.bfloat16)],
        2 * n * rows * width * hidden,
        2 * n * rows * hidden,
    )
    return outs[:n], outs[n][:images]


def back_body(count, tokens, sel_ref, *refs):
    g_tok = refs[0]
    slopes = refs[1 : count + 1]
    own_in, own_out, other_in, other_out = refs[count + 1 : count + 5]
    outs, acc = refs[count + 5 : 2 * count + 5], refs[2 * count + 5]
    rows = slopes[0].shape[0]
    per = rows // tokens

    def work(w_in, w_out):
        for t, tile in enumerate(tiles(w_in.shape[1])):
            g_h = dot_nn(g_tok[...], w_out[:, tile])
            terms = []
            for i in range(count):
                for image in range(per):
                    at = i * per + image
                    slope = slopes[i][image * tokens : (image + 1) * tokens, tile]
                    terms.append(
                        (slope.astype(jnp.float32) * g_h[at : at + 1, :]).astype(jnp.bfloat16)
                    )
            term = dot_nt(jnp.concatenate(terms, axis=0), w_in[:, tile])
            acc[...] = term if t == 0 else acc[...] + term

    by_section(sel_ref, 1, work, (own_in, own_out), (other_in, other_out))
    for i, out in enumerate(outs):
        out[...] = acc[i * rows : (i + 1) * rows, :].astype(jnp.bfloat16)


def reward_back(g_tok, slopes, tokens, own, other, sel):
    rows, hidden = slopes[0].shape
    width, n = own[0].shape[0], len(slopes)
    return run(
        functools.partial(back_body, n, tokens),
        "reward_back",
        sel,
        [g_tok, *slopes, *own, *other],
        [bf16(rows, width)] * n,
        [pltpu.VMEM((n * rows, width), jnp.float32)],
        2 * n * rows * width * hidden,
    )


def put_rows(result, core, keep, away, tile):
    groups, rows, unused = keep.shape
    for g in range(groups):
        even = result[2 * g * rows : (2 * g + 1) * rows, :]
        odd = result[(2 * g + 1) * rows : (2 * g + 2) * rows, :]
        keep[g, :, tile] = jnp.where(core == 0, even, odd).astype(jnp.bfloat16)
        away[g, :, tile] = jnp.where(core == 0, odd, even).astype(jnp.bfloat16)


def grad_out_body(count, sel_ref, *refs):
    pieces, acts = refs[: 2 * count], refs[2 * count : 3 * count]
    keep, away, turned, state = refs[3 * count :]
    share = turned.shape[0]
    rows = acts[0].shape[0]
    start = pl.multiple_of(sel_ref[0] * share, share)
    cols = jnp.concatenate([piece[:, pl.ds(start, share)] for piece in pieces], axis=0)
    turned[...] = cols.T
    for i, part in enumerate(acts):
        state[i * rows : (i + 1) * rows, :] = part[...]
    for tile in tiles(state.shape[1]):
        put_rows(dot_nn(turned[...], state[:, tile]), sel_ref[1], keep, away, tile)


def grad_in_body(count, sel_ref, *refs):
    pieces, slopes = refs[: 2 * count], refs[2 * count : 3 * count]
    xn_cols = refs[3 * count : 4 * count]
    own, other, keep, away, g_all, turned = refs[4 * count :]
    rows = pieces[0].shape[0]
    wide = xn_cols[0].shape[1]
    for i, piece in enumerate(pieces):
        g_all[i * rows : (i + 1) * rows, :] = piece[...]
    for i, part in enumerate(xn_cols):
        turned[:, i * wide : (i + 1) * wide] = part[...]

    def work(weight):
        for tile in tiles(weight.shape[1]):
            g_h = dot_nn(g_all[...], weight[:, tile])
            slope = jnp.concatenate([part[:, tile] for part in slopes], axis=0)
            g_hidden = (g_h * slope.astype(jnp.float32)).astype(jnp.bfloat16)
            put_rows(dot_nn(turned[...], g_hidden), sel_ref[1], keep, away, tile)

    by_section(sel_ref, 0, work, (own,), (other,))


def gradient_outs(width, hidden):
    groups = lax.axis_size("dp") // 2
    return [bf16(groups, width // 2 // (2 * groups), hidden)] * 2


def grad_out_parts(pieces, acts, sel):
    rows, width = pieces[0].shape
    total, hidden = rows * len(pieces), acts[0].shape[1]
    return run(
        functools.partial(grad_out_body, len(acts)),
        "grad_out",
        sel,
        [*pieces, *acts],
        gradient_outs(width, hidden),
        [
            pltpu.VMEM((width // 2, total), jnp.bfloat16),
            pltpu.VMEM((total, hidden), jnp.bfloat16),
        ],
        total * width * hidden,
    )


def grad_in_parts(pieces, slopes, xn_cols, own, other, sel):
    rows, width = pieces[0].shape
    total, hidden = rows * len(pieces), slopes[0].shape[1]
    return run(
        functools.partial(grad_in_body, len(slopes)),
        "grad_in",
        sel,
        [*pieces, *slopes, *xn_cols, own, other],
        gradient_outs(width, hidden),
        [
            pltpu.VMEM((total, width), jnp.bfloat16),
            pltpu.VMEM((width // 2, total), jnp.bfloat16),
        ],
        3 * total * width * hidden,
    )


def sum_over_dp(keep, away):
    groups = keep.shape[0]
    place = lax.axis_index("dp") // 2
    chip = keep.astype(jnp.float32) + swapped(away, "dp", 1).astype(jnp.float32)
    total = lax.dynamic_index_in_dim(chip, place, 0, keepdims=False)
    sent = chip.astype(jnp.bfloat16)
    for k in range(1, groups):
        part = lax.dynamic_index_in_dim(sent, (place + k) % groups, 0, keepdims=False)
        total = total + rotated(part, "dp", 2 * k).astype(jnp.float32)
    return total


def score_of(pooled, text):
    unit_img = pooled * lax.rsqrt(jnp.mean(pooled * pooled, axis=-1, keepdims=True) + EPS)
    unit_txt = text * lax.rsqrt(jnp.mean(text * text, axis=-1, keepdims=True) + EPS)
    return 100.0 * jnp.sum(unit_img * unit_txt, axis=-1) / pooled.shape[-1]


def on_device(latents, timesteps, prompt_ids, prompt_table, gains, w_in, w_out):
    count, tokens, width = latents.shape
    half = count // 2
    n_tp = lax.axis_size("tp")
    segment = lax.axis_index("sec")
    first = segment == 0
    core = lax.axis_index("dp") % 2
    place = lax.axis_index("dp") % 4
    sel = jnp.stack([segment, core, place]).astype(jnp.int32)
    own = (w_in[0], w_out[0])
    theta = math.pi / 2.0 * (timesteps.astype(jnp.float32) + 1.0) / (STEPS + 1.0)
    alpha = jnp.cos(theta)[:, None, None]
    sigma = jnp.sin(theta)[:, None, None]

    flat = latents.reshape(count * tokens, width)
    got_in = swapped(quarter(own[0], place), "sec", 1)
    lat_parts = gather_parts(flat)
    got_out = swapped(quarter(own[1], place), "sec", 1)
    across_in = swapped(got_in, "dp", 2)
    across_out = swapped(got_out, "dp", 2)

    onehot = (
        prompt_ids[:, None] == jnp.arange(prompt_table.shape[0], dtype=jnp.int32)[None, :]
    ).astype(jnp.bfloat16)
    text = dot_nn(onehot, prompt_table)
    text_mine = jnp.where(first, text[half:], text[:half])

    near = [k for k in range(1, n_tp) if 2 * k != n_tp]
    far = [k for k in range(1, n_tp) if 2 * k == n_tp]
    eps_parts = [None] * n_tp
    arrivals = ([], [got_in], [got_out, across_in])
    for ks, arrived in zip(([0], near, far), arrivals):
        if ks:
            operands, unused = lax.optimization_barrier(([lat_parts[k] for k in ks], arrived))
            results = block0_partials(operands, gains[:1], *own, sel)
            for k, result in zip(ks, results):
                eps_parts[k] = result
    eps_mix, across_out = lax.optimization_barrier((reduce_parts(eps_parts), across_out))
    eps_mix = eps_mix.reshape(count, tokens, width)
    other = (assembled(got_in, across_in, place), assembled(got_out, across_out, place))
    base = latents.astype(jnp.float32)
    images = ((base - sigma * (base + eps_mix)) / alpha).astype(jnp.bfloat16)

    arrived = lax.ppermute(images[:half], "sec", [(0, 1)])
    mine = jnp.where(first, images[half:], arrived)
    ratio = jnp.where(first, (sigma / alpha)[half:], (sigma / alpha)[:half])
    mine_rows = mine.reshape(half * tokens, width)
    seen_parts = gather_parts(mine_rows)

    states = [block0_state(part, gains[:1], own[0], other[0], sel) for part in lat_parts]
    slopes1, pool_parts = [None] * n_tp, [None] * n_tp
    for ks in ([0] + near, far):
        if ks:
            operands = [seen_parts[k] for k in ks]
            some_slopes, some_pools = reward_forward(
                operands, tokens, gains[1:], own, other, sel
            )
            for i, k in enumerate(ks):
                slopes1[k] = some_slopes[i]
                pool_parts[k] = some_pools[i * half : (i + 1) * half]
    pool_part = jnp.concatenate(pool_parts, 0)
    with_text = jnp.concatenate([pool_part, text_mine], 0)
    pool, texts = pool_part, [text_mine]
    for k in range(1, n_tp):
        theirs = rotated(with_text, "tp", k)
        pool = pool + jnp.roll(theirs[: n_tp * half], k * half, axis=0)
        texts.append(theirs[n_tp * half :])
    text_all = jnp.concatenate(texts, 0)
    seen_mean = [
        jnp.mean(part.astype(jnp.float32).reshape(half, tokens, width), axis=1)
        for part in seen_parts
    ]
    pooled = pool + jnp.concatenate(seen_mean, 0)
    g_pooled = jax.grad(lambda p: -jnp.sum(score_of(p, text_all)))(pooled)
    g_mean = g_pooled / tokens
    padded = -(-n_tp * half // 16) * 16
    g_tok = jnp.pad(g_mean.astype(jnp.bfloat16), ((0, padded - n_tp * half), (0, 0)))
    g_parts = reward_back(g_tok, slopes1, tokens, own, other, sel)
    g_xn, unused = lax.optimization_barrier((reduce_parts(g_parts), states))
    seen = mine_rows.astype(jnp.float32)
    scale1 = lax.rsqrt(jnp.mean(seen * seen, axis=-1, keepdims=True) + EPS)
    weighted = gains[1] * g_xn
    g_norm = scale1 * weighted - seen * scale1**3 * jnp.mean(
        seen * weighted, axis=-1, keepdims=True
    )
    g_images = (g_mean[:half, None, :] + g_norm.reshape(half, tokens, width)).astype(jnp.bfloat16)
    g_eps = (-ratio * g_images.astype(jnp.float32)).astype(jnp.bfloat16)

    pieces = []
    for part in gather_parts(g_eps.reshape(half * tokens, width)):
        pieces += [part, swapped(part, "sec", 1)]
    out_parts = grad_out_parts(pieces, [state[0] for state in states], sel)
    slopes0, xn_cols = [state[1] for state in states], [state[2] for state in states]
    out_parts, slopes0 = lax.optimization_barrier((out_parts, slopes0))
    in_parts = grad_in_parts(pieces, slopes0, xn_cols, own[1], other[1], sel)
    grad_out, grad_in = sum_over_dp(*out_parts), sum_over_dp(*in_parts)
    return (grad_in, grad_out)


def solution(mesh):
    in_specs = (
        P(("dp", "tp"), None, None),
        P(("dp", "tp")),
        P(("dp", "tp")),
        P(),
        P(),
        P("sec", None, "tp"),
        P("sec", None, "tp"),
    )
    out_specs = (P(("sec", "dp"), "tp"), P(("sec", "dp"), "tp"))
    return jax.shard_map(
        on_device, mesh=mesh, in_specs=in_specs, out_specs=out_specs, check_vma=False
    )
```

time: 207 us -> 226 us (1.092)
  waiting for transfers between devices: 75.3 us -> 105 us
  Pallas kernels: 63.5 us -> 34.3 us
  local copies, waits for them, and re-layouts: 12.2 us -> 32.5 us
  starting transfers between devices: 47.7 us -> 43.8 us
    pallas_call x12, Pallas kernels: 63.5 us -> 34.3 us  [run(): pl.pallas_call(body, in_specs=[IN_SMEM] + [IN_VMEM] * len(operands), out_...]
    ppermute x14, waiting for transfers between devices: 19.7 us -> 39.5 us  [swapped(): return lax.ppermute(value, axis, [(i, i ^ bit) for i in range(count)])]
    unnamed x32 -> x92, local copies, waits for them, and re-layouts: 7.04 us -> 24 us
    ppermute x23 -> x20, waiting for transfers between devices: 53.5 us -> 61.7 us  [rotated(): lax.ppermute(value, axis, [(i, (i + steps) % count) for i in range(count)])]
    ppermute x23 -> x20, starting transfers between devices: 32.4 us -> 27.1 us  [rotated(): lax.ppermute(value, axis, [(i, (i + steps) % count) for i in range(count)])]
    dynamic_update_slice x0 -> x8, local copies, waits for them, and re-layouts: none -> 2.98 us  [assembled(): full = lax.dynamic_update_slice_in_dim(full, piece, (place ^ q) * rows, 0)]
  transfers between devices with their start and end apart: 38 -> 35, of which waited for: 17 -> 17; matrix products, arithmetic and copies ran while one was open for 3% -> 5% of each run, Pallas kernels for 18% -> 10%
where the time goes in v4:
time: 226 us; the launch traced here: 224 us
  waiting for transfers between devices  105 us (46%)
  starting transfers between devices  43.8 us (19%)
  Pallas kernels  34.3 us (15%)
  local copies, waits for them, and re-layouts  32.5 us (14%)
  other arithmetic  5.08 us (2%)
  between operations  2.78 us (1%)
    ppermute x20, waiting for transfers between devices, rotated(): lax.ppermute(value, axis, [(i, (i + steps) % count) for i in range(count)])  61.7 us
    ppermute x14, waiting for transfers between devices, swapped(): return lax.ppermute(value, axis, [(i, i ^ bit) for i in range(count)])  39.5 us
    pallas_call x12, Pallas kernels, run(): pl.pallas_call(body, in_specs=[IN_SMEM] + [IN_VMEM] * len(operands), out_...  34.3 us
    ppermute x20, starting transfers between devices, rotated(): lax.ppermute(value, axis, [(i, (i + steps) % count) for i in range(count)])  27.1 us
    unnamed x92, local copies, waits for them, and re-layouts  24 us
    ppermute x14, starting transfers between devices, swapped(): return lax.ppermute(value, axis, [(i, i ^ bit) for i in range(count)])  13.3 us
  transfers between devices with their start and end apart: 35, of which 17 were waited for; matrix products, arithmetic and copies ran while one was open for 5% of the time, Pallas kernels for 10%

profile of v4, /device:TPU:0, one launch (start us, length us, event | category | flops | bytes accessed | tf_op | source)
XLA Modules:
  0.0 223.9 jit_solution(8550494661259530495)
XLA Ops:
  0.7 4.1 %collective-permute-start.4 = (bf16[128,1280]{1,0:T(8,128)(2,1)}, bf16[128,1280]{1,0:T(8,128)(2,1)}, u32[]{:S(2)}, u32[]{:S(2)}) collective-permute-start(bf16[128,1280]{1,0:T(8,128)(2,1)} %bitcast.43), channel_id=1, source_target_pairs={{0,2},{1,3},{2,0},{3,1},{4,6},{5,7},{6,4},{7,5},{8,10},{9,11},{10,... | collective-permute-start | bytes 983048 | tf_op jit(solution)/shard_map/ppermute | solution.py:20
  4.8 1.6 collective-permute-start
  6.4 2.2 %collective-permute-start.1 = (bf16[128,1280]{1,0:T(8,128)(2,1)}, bf16[128,1280]{1,0:T(8,128)(2,1)}, u32[]{:S(2)}, u32[]{:S(2)}) collective-permute-start(bf16[128,1280]{1,0:T(8,128)(2,1)} %bitcast.45), channel_id=1, source_target_pairs={{0,3},{1,0},{2,1},{3,2},{4,7},{5,4},{6,5},{7,6},{8,11},{9,8},{10,9... | collective-permute-start | bytes 983048 | tf_op jit(solution)/shard_map/ppermute | solution.py:20
  8.6 2.1 dynamic-slice_bitcast_fusion
  10.7 1.5 collective-permute-start.5
  12.2 2.1 dynamic-slice_bitcast_fusion.1
  17.1 30.6 %collective-permute-done.2 = bf16[320,1280]{1,0:T(8,128)(2,1)} collective-permute-done((bf16[320,1280]{1,0:T(8,128)(2,1)}, bf16[320,1280]{1,0:T(8,128)(2,1)}, u32[]{:S(2)}, u32[]{:S(2)}) %collective-permute-start.2) | collective-permute-done | bytes 819232 | tf_op jit(solution)/shard_map/ppermute | solution.py:25
  47.7 1.5 collective-permute-start.6
  49.3 1.9 copy-done.2
  51.3 1.0 copy-done.7
  52.2 2.7 %block0_partial.3 = bf16[128,1280]{1,0:T(8,128)(2,1)S(1)} custom-call(s32[3]{0:T(128)S(1)} %pad_add_fusion.sel_ref, bf16[128,1280]{1,0:T(8,128)(2,1)S(1)} %bitcast.46, f32[1,1280]{1,0:T(1,128)S(1)} %get-tuple-element.97.refs_1_.refs_2_.gain, bf16[1280,1280]{1,0:T(8,128)(2,1)S(1)} %bitcast.26, bf16[1280,1280]{1,0:T(8,128)(2,1)S(1)} %bitcast.36), custom_call_target="tpu_custom_call" | custom-call | flops 838860800 | bytes 7214080 | tf_op jit(solution)/shard_map/block0_partial/pallas_call | solution.py:86
  54.9 3.4 %block0_partial.4 = (bf16[128,1280]{1,0:T(8,128)(2,1)S(1)}, bf16[128,1280]{1,0:T(8,128)(2,1)S(1)}) custom-call(s32[3]{0:T(128)S(1)} %pad_add_fusion.sel_ref, bf16[128,1280]{1,0:T(8,128)(2,1)} %collective-permute-done.refs_0_.part, bf16[128,1280]{1,0:T(8,128)(2,1)} %collective-permute-done.1.refs_1_.part, ...), custom_call_target="tpu_custom_call" | custom-call | flops 1677721600 | bytes 7869440 | tf_op jit(solution)/shard_map/block0_partial/pallas_call | solution.py:86
  59.2 1.4 constant_dynamic-update-slice_fusion.3
  60.8 1.2 constant_dynamic-update-slice_fusion.7
  62.0 1.7 collective-permute-start.8
  63.7 2.4 %collective-permute-done.6 = bf16[320,1280]{1,0:T(8,128)(2,1)S(1)} collective-permute-done((bf16[320,1280]{1,0:T(8,128)(2,1)}, bf16[320,1280]{1,0:T(8,128)(2,1)S(1)}, u32[]{:S(2)}, u32[]{:S(2)}) %collective-permute-start.6) | collective-permute-done | bytes 819232 | tf_op jit(solution)/shard_map/ppermute | solution.py:25
  66.1 1.5 collective-permute-start.9
  67.6 3.1 %block0_partial.5 = bf16[128,1280]{1,0:T(8,128)(2,1)S(1)} custom-call(s32[3]{0:T(128)S(1)} %pad_add_fusion.sel_ref, bf16[128,1280]{1,0:T(8,128)(2,1)} %collective-permute-done.4.refs_0_.part, f32[1,1280]{1,0:T(1,128)S(1)} %get-tuple-element.97.refs_1_.refs_2_.gain, bf16[1280,1280]{1,0:T(8,128)(2,1)S(1)} %bitcast.28, bf16[1280,1280]{1,0:T(8,128)(2,1)S(1)} %bitcast.38), custom_call_target="tpu_custom_call" | custom-call | flops 838860800 | bytes 7214080 | tf_op jit(solution)/shard_map/block0_partial/pallas_call | solution.py:86
  71.2 4.4 %collective-permute-done.3 = bf16[128,1280]{1,0:T(8,128)(2,1)S(1)} collective-permute-done((bf16[128,1280]{1,0:T(8,128)(2,1)S(1)}, bf16[128,1280]{1,0:T(8,128)(2,1)S(1)}, u32[]{:S(2)}, u32[]{:S(2)}) %collective-permute-start.3) | collective-permute-done | bytes 327712 | tf_op jit(solution)/shard_map/ppermute | solution.py:20
  75.5 13.3 %collective-permute-done.7 = bf16[128,1280]{1,0:T(8,128)(2,1)S(1)} collective-permute-done((bf16[128,1280]{1,0:T(8,128)(2,1)S(1)}, bf16[128,1280]{1,0:T(8,128)(2,1)S(1)}, u32[]{:S(2)}, u32[]{:S(2)}) %collective-permute-start.7) | collective-permute-done | bytes 327712 | tf_op jit(solution)/shard_map/ppermute | solution.py:20
  89.3 3.4 %collective-permute-start.10 = (bf16[1,64,1280]{2,1,0:T(8,128)(2,1)S(1)}, bf16[1,64,1280]{2,1,0:T(8,128)(2,1)S(1)}, u32[]{:S(2)}, u32[]{:S(2)}) collective-permute-start(bf16[1,64,1280]{2,1,0:T(8,128)(2,1)S(1)} %slice.125), channel_id=1, source_target_pairs={{0,16},{1,17},{2,18},{3,19},{4,20},{5,21},{6,22},{7,23},{8,24},{9,... | collective-permute-start | bytes 491528 | tf_op jit(solution)/shard_map/ppermute | solution.py:418
  92.8 4.0 %collective-permute-done.10 = bf16[1,64,1280]{2,1,0:T(8,128)(2,1)S(1)} collective-permute-done((bf16[1,64,1280]{2,1,0:T(8,128)(2,1)S(1)}, bf16[1,64,1280]{2,1,0:T(8,128)(2,1)S(1)}, u32[]{:S(2)}, u32[]{:S(2)}) %collective-permute-start.10) | collective-permute-done | bytes 163872 | tf_op jit(solution)/shard_map/ppermute | solution.py:418
  96.9 3.5 %collective-permute-start.11 = (bf16[64,1280]{1,0:T(8,128)(2,1)S(1)}, bf16[64,1280]{1,0:T(8,128)(2,1)S(1)}, u32[]{:S(2)}, u32[]{:S(2)}) collective-permute-start(bf16[64,1280]{1,0:T(8,128)(2,1)S(1)} %fusion.11.refs_0_), channel_id=1, source_target_pairs={{0,1},{1,2},{2,3},{3,0},{4,5},{5,6},{6,7},{7,4},{8,9},{9,10},{10,1... | collective-permute-start | bytes 491528 | tf_op jit(solution)/shard_map/ppermute | solution.py:20
  100.9 7.6 %collective-permute-done.11.refs_1_ = bf16[64,1280]{1,0:T(8,128)(2,1)S(1)} collective-permute-done((bf16[64,1280]{1,0:T(8,128)(2,1)S(1)}, bf16[64,1280]{1,0:T(8,128)(2,1)S(1)}, u32[]{:S(2)}, u32[]{:S(2)}) %collective-permute-start.11) | collective-permute-done | bytes 163872 | tf_op jit(solution)/shard_map/ppermute | solution.py:20
  108.5 2.5 %collective-permute-done.17.refs_0_ = bf16[64,1280]{1,0:T(8,128)(2,1)S(1)} collective-permute-done((bf16[64,1280]{1,0:T(8,128)(2,1)S(1)}, bf16[64,1280]{1,0:T(8,128)(2,1)S(1)}, u32[]{:S(2)}, u32[]{:S(2)}) %collective-permute-start.17) | collective-permute-done | bytes 163872 | tf_op jit(solution)/shard_map/ppermute | solution.py:20
  111.1 1.2 collective-permute-done.12.refs_2_
  112.5 1.5 block0_state.4
  114.1 3.6 %reward_forward.2 = (bf16[64,1280]{1,0:T(8,128)(2,1)S(1)}, bf16[64,1280]{1,0:T(8,128)(2,1)S(1)}, bf16[64,1280]{1,0:T(8,128)(2,1)S(1)}, f32[8,1280]{1,0:T(8,128)S(1)}) custom-call(s32[3]{0:T(128)S(1)} %pad_add_fusion.sel_ref, bf16[64,1280]{1,0:T(8,128)(2,1)S(1)} %fusion.11.refs_0_, bf16[64,1280]{1,0:T(8,128)(2,1)S(1)} %collective-permute-done.11.refs_1_, ...), custom_call_target="tpu_custom_call" | custom-call | flops 629145600 | bytes 14136320 | tf_op jit(solution)/shard_map/reward_forward/pallas_call | solution.py:86
  117.7 2.7 %reward_forward.3 = (bf16[64,1280]{1,0:T(8,128)(2,1)S(1)}, f32[8,1280]{1,0:T(8,128)S(1)}) custom-call(s32[3]{0:T(128)S(1)} %pad_add_fusion.sel_ref, bf16[64,1280]{1,0:T(8,128)(2,1)S(1)} %collective-permute-done.17.refs_0_, f32[1,1280]{1,0:T(1,128)S(1)} %get-tuple-element.96.refs_3_.refs_1_, bf16[1280,1280]{1,0:T(8,128)(2,1)S(1)} %bitcast.31, ...), custom_call_target="tpu_custom_call" | custom-call | flops 209715200 | bytes 13480960 | tf_op jit(solution)/shard_map/reward_forward/pallas_call | solution.py:86
  120.5 2.5 %collective-permute-start.18 = (f32[5,1280]{1,0:T(8,128)S(1)}, f32[5,1280]{1,0:T(8,128)S(1)}, u32[]{:S(2)}, u32[]{:S(2)}) collective-permute-start(f32[5,1280]{1,0:T(8,128)S(1)} %pad_maximum_fusion), channel_id=1, source_target_pairs={{0,1},{1,2},{2,3},{3,0},{4,5},{5,6},{6,7},{7,4},{8,9},{9,10},{10,1... | collective-permute-start | bytes 76808 | tf_op jit(solution)/shard_map/ppermute | solution.py:20
  123.1 1.9 block0_state.5
  125.0 1.4 collective-permute-start.20
  127.0 2.2 collective-permute-done.20
  129.2 2.6 %collective-permute-done.19 = f32[5,1280]{1,0:T(8,128)S(1)} collective-permute-done((f32[5,1280]{1,0:T(8,128)S(1)}, f32[5,1280]{1,0:T(8,128)S(1)}, u32[]{:S(2)}, u32[]{:S(2)}) %collective-permute-start.19) | collective-permute-done | bytes 25632 | tf_op jit(solution)/shard_map/ppermute | solution.py:20
  132.3 2.7 %reward_back.1 = (bf16[64,1280]{1,0:T(8,128)(2,1)S(1)}, bf16[64,1280]{1,0:T(8,128)(2,1)S(1)}, bf16[64,1280]{1,0:T(8,128)(2,1)S(1)}, bf16[64,1280]{1,0:T(8,128)(2,1)S(1)}) custom-call(s32[3]{0:T(128)S(1)} %pad_add_fusion.sel_ref, bf16[16,1280]{1,0:T(8,128)(2,1)S(1)} %pad.4.refs_0_, bf16[64,1280]{1,0:T(8,128)(2,1)S(1)} %get-tuple-element.51.refs_1_, ...), custom_call_target="tpu_custom_call" | custom-call | flops 838860800 | bytes 14458880 | tf_op jit(solution)/shard_map/reward_back/pallas_call | solution.py:86
  135.6 1.3 collective-permute-start.22
  137.2 1.9 block0_state.6
  140.5 2.1 block0_state.7
  142.8 6.7 %collective-permute-done.22 = bf16[64,1280]{1,0:T(8,128)(2,1)S(1)} collective-permute-done((bf16[64,1280]{1,0:T(8,128)(2,1)S(1)}, bf16[64,1280]{1,0:T(8,128)(2,1)S(1)}, u32[]{:S(2)}, u32[]{:S(2)}) %collective-permute-start.22) | collective-permute-done | bytes 163872 | tf_op jit(solution)/shard_map/ppermute | solution.py:20
  150.0 1.4 collective-permute-start.27
  151.4 2.8 %collective-permute-start.29 = (bf16[64,1280]{1,0:T(8,128)(2,1)S(1)}, bf16[64,1280]{1,0:T(8,128)(2,1)S(1)}, u32[]{:S(2)}, u32[]{:S(2)}) collective-permute-start(bf16[64,1280]{1,0:T(8,128)(2,1)S(1)} %multiply_convert_fusion.refs_0_), channel_id=1, source_target_pairs={{0,3},{1,0},{2,1},{3,2},{4,7},{5,4},{6,5},{7,6},{8,11},{9,8},{10,9... | collective-permute-start | bytes 491528 | tf_op jit(solution)/shard_map/ppermute | solution.py:20
  154.2 2.4 %collective-permute-start.24 = (bf16[64,1280]{1,0:T(8,128)(2,1)S(1)}, bf16[64,1280]{1,0:T(8,128)(2,1)S(1)}, u32[]{:S(2)}, u32[]{:S(2)}) collective-permute-start(bf16[64,1280]{1,0:T(8,128)(2,1)S(1)} %multiply_convert_fusion.refs_0_), channel_id=1, source_target_pairs={{0,16},{16,0},{1,17},{17,1},{2,18},{18,2},{3,19},{19,3},{4,20},{20... | collective-permute-start | bytes 491528 | tf_op jit(solution)/shard_map/ppermute | solution.py:25
  156.6 2.3 %collective-permute-done.25.refs_2_ = bf16[64,1280]{1,0:T(8,128)(2,1)S(1)} collective-permute-done((bf16[64,1280]{1,0:T(8,128)(2,1)S(1)}, bf16[64,1280]{1,0:T(8,128)(2,1)S(1)}, u32[]{:S(2)}, u32[]{:S(2)}) %collective-permute-start.25) | collective-permute-done | bytes 163872 | tf_op jit(solution)/shard_map/ppermute | solution.py:20
  158.9 2.4 %collective-permute-start.26 = (bf16[64,1280]{1,0:T(8,128)(2,1)S(1)}, bf16[64,1280]{1,0:T(8,128)(2,1)S(1)}, u32[]{:S(2)}, u32[]{:S(2)}) collective-permute-start(bf16[64,1280]{1,0:T(8,128)(2,1)S(1)} %collective-permute-done.25.refs_2_), channel_id=1, source_target_pairs={{0,16},{16,0},{1,17},{17,1},{2,18},{18,2},{3,19},{19,3},{4,20},{20... | collective-permute-start | bytes 491528 | tf_op jit(solution)/shard_map/ppermute | solution.py:25
  161.3 2.1 collective-permute-done.27.refs_4_
  163.4 2.4 %collective-permute-start.28 = (bf16[64,1280]{1,0:T(8,128)(2,1)S(1)}, bf16[64,1280]{1,0:T(8,128)(2,1)S(1)}, u32[]{:S(2)}, u32[]{:S(2)}) collective-permute-start(bf16[64,1280]{1,0:T(8,128)(2,1)S(1)} %collective-permute-done.27.refs_4_), channel_id=1, source_target_pairs={{0,16},{16,0},{1,17},{17,1},{2,18},{18,2},{3,19},{19,3},{4,20},{20... | collective-permute-start | bytes 491528 | tf_op jit(solution)/shard_map/ppermute | solution.py:25
  165.8 4.8 %collective-permute-done.28.refs_5_ = bf16[64,1280]{1,0:T(8,128)(2,1)S(1)} collective-permute-done((bf16[64,1280]{1,0:T(8,128)(2,1)S(1)}, bf16[64,1280]{1,0:T(8,128)(2,1)S(1)}, u32[]{:S(2)}, u32[]{:S(2)}) %collective-permute-start.28) | collective-permute-done | bytes 163872 | tf_op jit(solution)/shard_map/ppermute | solution.py:25
  170.6 1.8 collective-permute-done.30.refs_7_
  172.4 2.5 %grad_out.1 = (bf16[2,160,1280]{2,1,0:T(8,128)(2,1)S(1)}, bf16[2,160,1280]{2,1,0:T(8,128)(2,1)}) custom-call(s32[3]{0:T(128)S(1)} %pad_add_fusion.sel_ref, bf16[64,1280]{1,0:T(8,128)(2,1)S(1)} %multiply_convert_fusion.refs_0_, bf16[64,1280]{1,0:T(8,128)(2,1)S(1)} %collective-permute-done.24.refs_1_, bf16[64,1280]{1,0:T(8,128)(2,1)S(1)} %collective-permute-done.25.refs_2_, ...), custom_call_target="tpu_custom_call" | custom-call | flops 838860800 | bytes 4259840 | tf_op jit(solution)/shard_map/grad_out/pallas_call | solution.py:86
  175.9 1.9 copy-done.4
  177.9 1.9 copy-done.6
  179.8 0.9 copy-done.12
  180.7 1.0 copy-done.14
  181.7 1.0 copy-done.16
  182.6 1.0 copy-done.18
  183.6 1.0 copy-done.20
  186.4 0.9 copy-done.26
  194.7 6.1 %grad_in.1 = (bf16[2,160,1280]{2,1,0:T(8,128)(2,1)S(1)}, bf16[2,160,1280]{2,1,0:T(8,128)(2,1)S(1)}) custom-call(s32[3]{0:T(128)S(1)} %pad_add_fusion.sel_ref, bf16[64,1280]{1,0:T(8,128)(2,1)S(1)} %copy-done.12, bf16[64,1280]{1,0:T(8,128)(2,1)S(1)} %copy-done.36, bf16[64,1280]{1,0:T(8,128)(2,1)S(1)} %copy-done.30, bf16[64,1280]{1,0:T(8,128)(2,1)S(1)} %copy-done.38, ...), custom_call_target="tpu_custom_call" | custom-call | flops 2516582400 | bytes 11468800 | tf_op jit(solution)/shard_map/grad_in/pallas_call | solution.py:86
  201.3 1.3 convert_add_fusion
  203.5 1.6 collective-permute-start.32
  205.1 10.0 %collective-permute-done.34 = bf16[160,1280]{1,0:T(8,128)(2,1)S(1)} collective-permute-done((bf16[160,1280]{1,0:T(8,128)(2,1)S(1)}, bf16[160,1280]{1,0:T(8,128)(2,1)S(1)}, u32[]{:S(2)}, u32[]{:S(2)}) %collective-permute-start.34) | collective-permute-done | bytes 409632 | tf_op jit(solution)/shard_map/ppermute | solution.py:20
  215.1 1.0 bitcast_add_fusion
  216.0 6.9 %collective-permute-done.32 = bf16[160,1280]{1,0:T(8,128)(2,1)S(1)} collective-permute-done((bf16[160,1280]{1,0:T(8,128)(2,1)S(1)}, bf16[160,1280]{1,0:T(8,128)(2,1)S(1)}, u32[]{:S(2)}, u32[]{:S(2)}) %collective-permute-start.32) | collective-permute-done | bytes 409632 | tf_op jit(solution)/shard_map/ppermute | solution.py:20
  223.0 1.0 bitcast_add_fusion.1
  (171 shorter events, 20.0 us)
Async XLA Ops:
  0.6 14.2 %copy-start = (bf16[64,1280]{1,0:T(8,128)(2,1)S(1)}, bf16[64,1280]{1,0:T(8,128)(2,1)}, u32[]{:S(2)}) copy-start(bf16[64,1280]{1,0:T(8,128)(2,1)} %param.10) | copy-start | bytes 491524
  0.6 48.7 %copy-start.1 = (bf16[1,1280,1280]{2,1,0:T(8,128)(2,1)S(1)}, bf16[1,1280,1280]{2,1,0:T(8,128)(2,1)}, u32[]{:S(2)}) copy-start(bf16[1,1280,1280]{2,1,0:T(8,128)(2,1)} %param.12) | copy-start | bytes 9830404
  0.7 14.2 %copy-start.45 = (s32[2]{0:T(128)S(1)}, s32[2]{0:T(128)}, u32[]{:S(2)}) copy-start(s32[2]{0:T(128)} %param.9) | copy-start | bytes 28
  0.7 14.4 %copy-start.44 = (s32[2]{0:T(128)S(1)}, s32[2]{0:T(128)}, u32[]{:S(2)}) copy-start(s32[2]{0:T(128)} %param.8) | copy-start | bytes 28
  0.7 16.4 %copy-start.43 = (f32[2,1280]{1,0:T(2,128)S(1)}, f32[2,1280]{1,0:T(2,128)}, u32[]{:S(2)}) copy-start(f32[2,1280]{1,0:T(2,128)} %param.11) | copy-start | bytes 30724
  0.7 61.3 %collective-permute-start.4 = (bf16[128,1280]{1,0:T(8,128)(2,1)}, bf16[128,1280]{1,0:T(8,128)(2,1)}, u32[]{:S(2)}, u32[]{:S(2)}) collective-permute-start(bf16[128,1280]{1,0:T(8,128)(2,1)} %bitcast.43), channel_id=1, source_target_pairs={{0,2},{1,3},{2,0},{3,1},{4,6},{5,7},{6,4},{7,5},{8,10},{9,11},{10,... | collective-permute-start | bytes 983048 | tf_op jit(solution)/shard_map/ppermute | solution.py:20
  4.8 50.1 %collective-permute-start = (bf16[128,1280]{1,0:T(8,128)(2,1)}, bf16[128,1280]{1,0:T(8,128)(2,1)}, u32[]{:S(2)}, u32[]{:S(2)}) collective-permute-start(bf16[128,1280]{1,0:T(8,128)(2,1)} %bitcast.44), channel_id=1, source_target_pairs={{0,1},{1,2},{2,3},{3,0},{4,5},{5,6},{6,7},{7,4},{8,9},{9,10},{10,1... | collective-permute-start | bytes 983048 | tf_op jit(solution)/shard_map/ppermute | solution.py:20
  6.4 48.5 %collective-permute-start.1 = (bf16[128,1280]{1,0:T(8,128)(2,1)}, bf16[128,1280]{1,0:T(8,128)(2,1)}, u32[]{:S(2)}, u32[]{:S(2)}) collective-permute-start(bf16[128,1280]{1,0:T(8,128)(2,1)} %bitcast.45), channel_id=1, source_target_pairs={{0,3},{1,0},{2,1},{3,2},{4,7},{5,4},{6,5},{7,6},{8,11},{9,8},{10,9... | collective-permute-start | bytes 983048 | tf_op jit(solution)/shard_map/ppermute | solution.py:20
  10.7 38.6 %collective-permute-start.5 = (bf16[320,1280]{1,0:T(8,128)(2,1)}, bf16[320,1280]{1,0:T(8,128)(2,1)}, u32[]{:S(2)}, u32[]{:S(2)}) collective-permute-start(bf16[320,1280]{1,0:T(8,128)(2,1)} %dynamic-slice_bitcast_fusion), channel_id=1, source_target_pairs={{0,16},{16,0},{1,17},{17,1},{2,18},{18,2},{3,19},{19,3},{4,20},{20... | collective-permute-start | bytes 2457608 | tf_op jit(solution)/shard_map/ppermute | solution.py:25
  14.3 33.4 %collective-permute-start.2 = (bf16[320,1280]{1,0:T(8,128)(2,1)}, bf16[320,1280]{1,0:T(8,128)(2,1)}, u32[]{:S(2)}, u32[]{:S(2)}) collective-permute-start(bf16[320,1280]{1,0:T(8,128)(2,1)} %dynamic-slice_bitcast_fusion.1), channel_id=1, source_target_pairs={{0,16},{16,0},{1,17},{17,1},{2,18},{18,2},{3,19},{19,3},{4,20},{20... | collective-permute-start | bytes 2457608 | tf_op jit(solution)/shard_map/ppermute | solution.py:25
  47.7 18.4 %collective-permute-start.6 = (bf16[320,1280]{1,0:T(8,128)(2,1)}, bf16[320,1280]{1,0:T(8,128)(2,1)S(1)}, u32[]{:S(2)}, u32[]{:S(2)}) collective-permute-start(bf16[320,1280]{1,0:T(8,128)(2,1)} %collective-permute-done.2), channel_id=1, source_target_pairs={{0,8},{4,12},{8,0},{12,4},{1,9},{5,13},{9,1},{13,5},{2,10},{6,14},... | collective-permute-start | bytes 2457608 | tf_op jit(solution)/shard_map/ppermute | solution.py:25
  49.3 21.5 %collective-permute-start.15 = (bf16[320,1280]{1,0:T(8,128)(2,1)}, bf16[320,1280]{1,0:T(8,128)(2,1)S(1)}, u32[]{:S(2)}, u32[]{:S(2)}) collective-permute-start(bf16[320,1280]{1,0:T(8,128)(2,1)} %collective-permute-done.5), channel_id=1, source_target_pairs={{0,4},{4,0},{8,12},{12,8},{1,5},{5,1},{9,13},{13,9},{2,6},{6,2},{1... | collective-permute-start | bytes 2457608 | tf_op jit(solution)/shard_map/ppermute | solution.py:25
  49.3 1.9 copy-start.2
  51.2 1.0 copy-start.7
  58.4 17.2 %collective-permute-start.3 = (bf16[128,1280]{1,0:T(8,128)(2,1)S(1)}, bf16[128,1280]{1,0:T(8,128)(2,1)S(1)}, u32[]{:S(2)}, u32[]{:S(2)}) collective-permute-start(bf16[128,1280]{1,0:T(8,128)(2,1)S(1)} %get-tuple-element.44), channel_id=1, source_target_pairs={{0,3},{1,0},{2,1},{3,2},{4,7},{5,4},{6,5},{7,6},{8,11},{9,8},{10,9... | collective-permute-start | bytes 983048 | tf_op jit(solution)/shard_map/ppermute | solution.py:20
  58.7 12.2 %collective-permute-start.13 = (bf16[320,1280]{1,0:T(8,128)(2,1)}, bf16[320,1280]{1,0:T(8,128)(2,1)S(1)}, u32[]{:S(2)}, u32[]{:S(2)}) collective-permute-start(bf16[320,1280]{1,0:T(8,128)(2,1)} %collective-permute-done.2), channel_id=1, source_target_pairs={{0,4},{4,0},{8,12},{12,8},{1,5},{5,1},{9,13},{13,9},{2,6},{6,2},{1... | collective-permute-start | bytes 2457608 | tf_op jit(solution)/shard_map/ppermute | solution.py:25
  59.2 8.4 %copy-start.3 = (bf16[1,1280,1280]{2,1,0:T(8,128)(2,1)S(1)}, bf16[1,1280,1280]{2,1,0:T(8,128)(2,1)}, u32[]{:S(2)}) copy-start(bf16[1,1280,1280]{2,1,0:T(8,128)(2,1)} %param.13) | copy-start | bytes 9830404
  62.0 13.5 %collective-permute-start.8 = (bf16[128,1280]{1,0:T(8,128)(2,1)S(1)}, bf16[128,1280]{1,0:T(8,128)(2,1)S(1)}, u32[]{:S(2)}, u32[]{:S(2)}) collective-permute-start(bf16[128,1280]{1,0:T(8,128)(2,1)S(1)} %get-tuple-element.46), channel_id=1, source_target_pairs={{0,1},{1,2},{2,3},{3,0},{4,5},{5,6},{6,7},{7,4},{8,9},{9,10},{10,1... | collective-permute-start | bytes 983048 | tf_op jit(solution)/shard_map/ppermute | solution.py:20
  66.1 22.8 %collective-permute-start.9 = (bf16[320,1280]{1,0:T(8,128)(2,1)}, bf16[320,1280]{1,0:T(8,128)(2,1)S(1)}, u32[]{:S(2)}, u32[]{:S(2)}) collective-permute-start(bf16[320,1280]{1,0:T(8,128)(2,1)} %collective-permute-done.5), channel_id=1, source_target_pairs={{0,8},{4,12},{8,0},{12,4},{1,9},{5,13},{9,1},{13,5},{2,10},{6,14},... | collective-permute-start | bytes 2457608 | tf_op jit(solution)/shard_map/ppermute | solution.py:25
  70.7 18.3 %copy-start.8 = (bf16[2,64,1280]{2,1,0:T(8,128)(2,1)S(1)}, bf16[2,64,1280]{2,1,0:T(8,128)(2,1)}, u32[]{:S(2)}) copy-start(bf16[2,64,1280]{2,1,0:T(8,128)(2,1)} %param.7) | copy-start | bytes 983044
  70.8 18.0 %collective-permute-start.7 = (bf16[128,1280]{1,0:T(8,128)(2,1)S(1)}, bf16[128,1280]{1,0:T(8,128)(2,1)S(1)}, u32[]{:S(2)}, u32[]{:S(2)}) collective-permute-start(bf16[128,1280]{1,0:T(8,128)(2,1)S(1)} %block0_partial.5), channel_id=1, source_target_pairs={{0,2},{1,3},{2,0},{3,1},{4,6},{5,7},{6,4},{7,5},{8,10},{9,11},{10,... | collective-permute-start | bytes 983048 | tf_op jit(solution)/shard_map/ppermute | solution.py:20
  70.9 41.4 %collective-permute-start.14 = (bf16[320,1280]{1,0:T(8,128)(2,1)S(1)}, bf16[320,1280]{1,0:T(8,128)(2,1)S(1)}, u32[]{:S(2)}, u32[]{:S(2)}) collective-permute-start(bf16[320,1280]{1,0:T(8,128)(2,1)S(1)} %collective-permute-done.6), channel_id=1, source_target_pairs={{0,4},{4,0},{8,12},{12,8},{1,5},{5,1},{9,13},{13,9},{2,6},{6,2},{1... | collective-permute-start | bytes 2457608 | tf_op jit(solution)/shard_map/ppermute | solution.py:25
  89.0 25.0 %collective-permute-start.16 = (bf16[320,1280]{1,0:T(8,128)(2,1)S(1)}, bf16[320,1280]{1,0:T(8,128)(2,1)S(1)}, u32[]{:S(2)}, u32[]{:S(2)}) collective-permute-start(bf16[320,1280]{1,0:T(8,128)(2,1)S(1)} %collective-permute-done.9), channel_id=1, source_target_pairs={{0,4},{4,0},{8,12},{12,8},{1,5},{5,1},{9,13},{13,9},{2,6},{6,2},{1... | collective-permute-start | bytes 2457608 | tf_op jit(solution)/shard_map/ppermute | solution.py:25
  89.3 7.5 %collective-permute-start.10 = (bf16[1,64,1280]{2,1,0:T(8,128)(2,1)S(1)}, bf16[1,64,1280]{2,1,0:T(8,128)(2,1)S(1)}, u32[]{:S(2)}, u32[]{:S(2)}) collective-permute-start(bf16[1,64,1280]{2,1,0:T(8,128)(2,1)S(1)} %slice.125), channel_id=1, source_target_pairs={{0,16},{1,17},{2,18},{3,19},{4,20},{5,21},{6,22},{7,23},{8,24},{9,... | collective-permute-start | bytes 491528 | tf_op jit(solution)/shard_map/ppermute | solution.py:418
  96.9 14.2 %collective-permute-start.17 = (bf16[64,1280]{1,0:T(8,128)(2,1)S(1)}, bf16[64,1280]{1,0:T(8,128)(2,1)S(1)}, u32[]{:S(2)}, u32[]{:S(2)}) collective-permute-start(bf16[64,1280]{1,0:T(8,128)(2,1)S(1)} %fusion.11.refs_0_), channel_id=1, source_target_pairs={{0,2},{1,3},{2,0},{3,1},{4,6},{5,7},{6,4},{7,5},{8,10},{9,11},{10,... | collective-permute-start | bytes 491528 | tf_op jit(solution)/shard_map/ppermute | solution.py:20
  96.9 11.5 %collective-permute-start.11 = (bf16[64,1280]{1,0:T(8,128)(2,1)S(1)}, bf16[64,1280]{1,0:T(8,128)(2,1)S(1)}, u32[]{:S(2)}, u32[]{:S(2)}) collective-permute-start(bf16[64,1280]{1,0:T(8,128)(2,1)S(1)} %fusion.11.refs_0_), channel_id=1, source_target_pairs={{0,1},{1,2},{2,3},{3,0},{4,5},{5,6},{6,7},{7,4},{8,9},{9,10},{10,1... | collective-permute-start | bytes 491528 | tf_op jit(solution)/shard_map/ppermute | solution.py:20
  100.4 11.9 %collective-permute-start.12 = (bf16[64,1280]{1,0:T(8,128)(2,1)S(1)}, bf16[64,1280]{1,0:T(8,128)(2,1)S(1)}, u32[]{:S(2)}, u32[]{:S(2)}) collective-permute-start(bf16[64,1280]{1,0:T(8,128)(2,1)S(1)} %fusion.11.refs_0_), channel_id=1, source_target_pairs={{0,3},{1,0},{2,1},{3,2},{4,7},{5,4},{6,5},{7,6},{8,11},{9,8},{10,9... | collective-permute-start | bytes 491528 | tf_op jit(solution)/shard_map/ppermute | solution.py:20
  114.0 3.7 %copy-start.13 = (bf16[128,1280]{1,0:T(8,128)(2,1)}, bf16[128,1280]{1,0:T(8,128)(2,1)S(1)}, u32[]{:S(2)}) copy-start(bf16[128,1280]{1,0:T(8,128)(2,1)S(1)} %get-tuple-element.74.refs_8_) | copy-start | bytes 983044
  114.0 3.7 %copy-start.21 = (bf16[640,128]{1,0:T(8,128)(2,1)}, bf16[640,128]{1,0:T(8,128)(2,1)S(1)}, u32[]{:S(2)}) copy-start(bf16[640,128]{1,0:T(8,128)(2,1)S(1)} %get-tuple-element.61.refs_12_) | copy-start | bytes 491524
  114.1 18.2 %copy-start.5 = (bf16[1280,1280]{1,0:T(8,128)(2,1)}, bf16[1280,1280]{1,0:T(8,128)(2,1)S(1)}, u32[]{:S(2)}) copy-start(bf16[1280,1280]{1,0:T(8,128)(2,1)S(1)} %constant_dynamic-update-slice_fusion.refs_7_.refs_5_.refs_8_.refs_17_) | copy-start | bytes 9830404
  120.5 6.4 %collective-permute-start.18 = (f32[5,1280]{1,0:T(8,128)S(1)}, f32[5,1280]{1,0:T(8,128)S(1)}, u32[]{:S(2)}, u32[]{:S(2)}) collective-permute-start(f32[5,1280]{1,0:T(8,128)S(1)} %pad_maximum_fusion), channel_id=1, source_target_pairs={{0,1},{1,2},{2,3},{3,0},{4,5},{5,6},{6,7},{7,4},{8,9},{9,10},{10,1... | collective-permute-start | bytes 76808 | tf_op jit(solution)/shard_map/ppermute | solution.py:20
  125.0 10.0 %copy-start.15 = (bf16[128,1280]{1,0:T(8,128)(2,1)}, bf16[128,1280]{1,0:T(8,128)(2,1)S(1)}, u32[]{:S(2)}) copy-start(bf16[128,1280]{1,0:T(8,128)(2,1)S(1)} %get-tuple-element.75.refs_9_) | copy-start | bytes 983044
  125.0 10.0 %copy-start.23 = (bf16[640,128]{1,0:T(8,128)(2,1)}, bf16[640,128]{1,0:T(8,128)(2,1)S(1)}, u32[]{:S(2)}) copy-start(bf16[640,128]{1,0:T(8,128)(2,1)S(1)} %get-tuple-element.64.refs_13_) | copy-start | bytes 491524
  125.0 4.1 %collective-permute-start.20 = (f32[5,1280]{1,0:T(8,128)S(1)}, f32[5,1280]{1,0:T(8,128)S(1)}, u32[]{:S(2)}, u32[]{:S(2)}) collective-permute-start(f32[5,1280]{1,0:T(8,128)S(1)} %pad_maximum_fusion), channel_id=1, source_target_pairs={{0,3},{1,0},{2,1},{3,2},{4,7},{5,4},{6,5},{7,6},{8,11},{9,8},{10,9... | collective-permute-start | bytes 76808 | tf_op jit(solution)/shard_map/ppermute | solution.py:20
  126.4 5.3 %collective-permute-start.19 = (f32[5,1280]{1,0:T(8,128)S(1)}, f32[5,1280]{1,0:T(8,128)S(1)}, u32[]{:S(2)}, u32[]{:S(2)}) collective-permute-start(f32[5,1280]{1,0:T(8,128)S(1)} %pad_maximum_fusion), channel_id=1, source_target_pairs={{0,2},{1,3},{2,0},{3,1},{4,6},{5,7},{6,4},{7,5},{8,10},{9,11},{10,... | collective-permute-start | bytes 76808 | tf_op jit(solution)/shard_map/ppermute | solution.py:20
  135.0 7.7 %collective-permute-start.21 = (bf16[64,1280]{1,0:T(8,128)(2,1)S(1)}, bf16[64,1280]{1,0:T(8,128)(2,1)S(1)}, u32[]{:S(2)}, u32[]{:S(2)}) collective-permute-start(bf16[64,1280]{1,0:T(8,128)(2,1)S(1)} %get-tuple-element.56), channel_id=1, source_target_pairs={{0,3},{1,0},{2,1},{3,2},{4,7},{5,4},{6,5},{7,6},{8,11},{9,8},{10,9... | collective-permute-start | bytes 491528 | tf_op jit(solution)/shard_map/ppermute | solution.py:20
  135.6 13.9 %collective-permute-start.22 = (bf16[64,1280]{1,0:T(8,128)(2,1)S(1)}, bf16[64,1280]{1,0:T(8,128)(2,1)S(1)}, u32[]{:S(2)}, u32[]{:S(2)}) collective-permute-start(bf16[64,1280]{1,0:T(8,128)(2,1)S(1)} %get-tuple-element.57), channel_id=1, source_target_pairs={{0,2},{1,3},{2,0},{3,1},{4,6},{5,7},{6,4},{7,5},{8,10},{9,11},{10,... | collective-permute-start | bytes 491528 | tf_op jit(solution)/shard_map/ppermute | solution.py:20
  136.9 12.6 %collective-permute-start.23 = (bf16[64,1280]{1,0:T(8,128)(2,1)S(1)}, bf16[64,1280]{1,0:T(8,128)(2,1)S(1)}, u32[]{:S(2)}, u32[]{:S(2)}) collective-permute-start(bf16[64,1280]{1,0:T(8,128)(2,1)S(1)} %get-tuple-element.58), channel_id=1, source_target_pairs={{0,1},{1,2},{2,3},{3,0},{4,5},{5,6},{6,7},{7,4},{8,9},{9,10},{10,1... | collective-permute-start | bytes 491528 | tf_op jit(solution)/shard_map/ppermute | solution.py:20
  142.7 7.0 %copy-start.27 = (bf16[640,128]{1,0:T(8,128)(2,1)}, bf16[640,128]{1,0:T(8,128)(2,1)S(1)}, u32[]{:S(2)}) copy-start(bf16[640,128]{1,0:T(8,128)(2,1)S(1)} %get-tuple-element.70.refs_15_) | copy-start | bytes 491524
  142.7 27.9 %copy-start.19 = (bf16[128,1280]{1,0:T(8,128)(2,1)}, bf16[128,1280]{1,0:T(8,128)(2,1)S(1)}, u32[]{:S(2)}) copy-start(bf16[128,1280]{1,0:T(8,128)(2,1)S(1)} %get-tuple-element.77.refs_11_) | copy-start | bytes 983044
  149.9 25.0 %copy-start.11 = (bf16[64,1280]{1,0:T(8,128)(2,1)}, bf16[64,1280]{1,0:T(8,128)(2,1)S(1)}, u32[]{:S(2)}) copy-start(bf16[64,1280]{1,0:T(8,128)(2,1)S(1)} %multiply_convert_fusion.refs_0_) | copy-start | bytes 491524
  149.9 9.0 %collective-permute-start.25 = (bf16[64,1280]{1,0:T(8,128)(2,1)S(1)}, bf16[64,1280]{1,0:T(8,128)(2,1)S(1)}, u32[]{:S(2)}, u32[]{:S(2)}) collective-permute-start(bf16[64,1280]{1,0:T(8,128)(2,1)S(1)} %multiply_convert_fusion.refs_0_), channel_id=1, source_target_pairs={{0,1},{1,2},{2,3},{3,0},{4,5},{5,6},{6,7},{7,4},{8,9},{9,10},{10,1... | collective-permute-start | bytes 491528 | tf_op jit(solution)/shard_map/ppermute | solution.py:20
  150.0 13.4 %collective-permute-start.27 = (bf16[64,1280]{1,0:T(8,128)(2,1)S(1)}, bf16[64,1280]{1,0:T(8,128)(2,1)S(1)}, u32[]{:S(2)}, u32[]{:S(2)}) collective-permute-start(bf16[64,1280]{1,0:T(8,128)(2,1)S(1)} %multiply_convert_fusion.refs_0_), channel_id=1, source_target_pairs={{0,2},{1,3},{2,0},{3,1},{4,6},{5,7},{6,4},{7,5},{8,10},{9,11},{10,... | collective-permute-start | bytes 491528 | tf_op jit(solution)/shard_map/ppermute | solution.py:20
  151.4 14.4 %collective-permute-start.29 = (bf16[64,1280]{1,0:T(8,128)(2,1)S(1)}, bf16[64,1280]{1,0:T(8,128)(2,1)S(1)}, u32[]{:S(2)}, u32[]{:S(2)}) collective-permute-start(bf16[64,1280]{1,0:T(8,128)(2,1)S(1)} %multiply_convert_fusion.refs_0_), channel_id=1, source_target_pairs={{0,3},{1,0},{2,1},{3,2},{4,7},{5,4},{6,5},{7,6},{8,11},{9,8},{10,9... | collective-permute-start | bytes 491528 | tf_op jit(solution)/shard_map/ppermute | solution.py:20
  154.2 11.6 %collective-permute-start.24 = (bf16[64,1280]{1,0:T(8,128)(2,1)S(1)}, bf16[64,1280]{1,0:T(8,128)(2,1)S(1)}, u32[]{:S(2)}, u32[]{:S(2)}) collective-permute-start(bf16[64,1280]{1,0:T(8,128)(2,1)S(1)} %multiply_convert_fusion.refs_0_), channel_id=1, source_target_pairs={{0,16},{16,0},{1,17},{17,1},{2,18},{18,2},{3,19},{19,3},{4,20},{20... | collective-permute-start | bytes 491528 | tf_op jit(solution)/shard_map/ppermute | solution.py:25
  158.9 17.0 %copy-start.29 = (bf16[64,1280]{1,0:T(8,128)(2,1)}, bf16[64,1280]{1,0:T(8,128)(2,1)S(1)}, u32[]{:S(2)}) copy-start(bf16[64,1280]{1,0:T(8,128)(2,1)S(1)} %collective-permute-done.25.refs_2_) | copy-start | bytes 491524
  158.9 6.9 %collective-permute-start.26 = (bf16[64,1280]{1,0:T(8,128)(2,1)S(1)}, bf16[64,1280]{1,0:T(8,128)(2,1)S(1)}, u32[]{:S(2)}, u32[]{:S(2)}) collective-permute-start(bf16[64,1280]{1,0:T(8,128)(2,1)S(1)} %collective-permute-done.25.refs_2_), channel_id=1, source_target_pairs={{0,16},{16,0},{1,17},{17,1},{2,18},{18,2},{3,19},{19,3},{4,20},{20... | collective-permute-start | bytes 491528 | tf_op jit(solution)/shard_map/ppermute | solution.py:25
  163.4 12.4 %copy-start.31 = (bf16[64,1280]{1,0:T(8,128)(2,1)}, bf16[64,1280]{1,0:T(8,128)(2,1)S(1)}, u32[]{:S(2)}) copy-start(bf16[64,1280]{1,0:T(8,128)(2,1)S(1)} %collective-permute-done.27.refs_4_) | copy-start | bytes 491524
  163.4 7.2 %collective-permute-start.28 = (bf16[64,1280]{1,0:T(8,128)(2,1)S(1)}, bf16[64,1280]{1,0:T(8,128)(2,1)S(1)}, u32[]{:S(2)}, u32[]{:S(2)}) collective-permute-start(bf16[64,1280]{1,0:T(8,128)(2,1)S(1)} %collective-permute-done.27.refs_4_), channel_id=1, source_target_pairs={{0,16},{16,0},{1,17},{17,1},{2,18},{18,2},{3,19},{19,3},{4,20},{20... | collective-permute-start | bytes 491528 | tf_op jit(solution)/shard_map/ppermute | solution.py:25
  165.7 10.0 %copy-start.33 = (bf16[64,1280]{1,0:T(8,128)(2,1)}, bf16[64,1280]{1,0:T(8,128)(2,1)S(1)}, u32[]{:S(2)}) copy-start(bf16[64,1280]{1,0:T(8,128)(2,1)S(1)} %collective-permute-done.29.refs_6_) | copy-start | bytes 491524
  165.8 6.6 %collective-permute-start.30 = (bf16[64,1280]{1,0:T(8,128)(2,1)S(1)}, bf16[64,1280]{1,0:T(8,128)(2,1)S(1)}, u32[]{:S(2)}, u32[]{:S(2)}) collective-permute-start(bf16[64,1280]{1,0:T(8,128)(2,1)S(1)} %collective-permute-done.29.refs_6_), channel_id=1, source_target_pairs={{0,16},{16,0},{1,17},{17,1},{2,18},{18,2},{3,19},{19,3},{4,20},{20... | collective-permute-start | bytes 491528 | tf_op jit(solution)/shard_map/ppermute | solution.py:25
  165.8 9.9 %copy-start.35 = (bf16[64,1280]{1,0:T(8,128)(2,1)}, bf16[64,1280]{1,0:T(8,128)(2,1)S(1)}, u32[]{:S(2)}) copy-start(bf16[64,1280]{1,0:T(8,128)(2,1)S(1)} %collective-permute-done.24.refs_1_) | copy-start | bytes 491524
  165.8 10.1 %copy-start.37 = (bf16[64,1280]{1,0:T(8,128)(2,1)}, bf16[64,1280]{1,0:T(8,128)(2,1)S(1)}, u32[]{:S(2)}) copy-start(bf16[64,1280]{1,0:T(8,128)(2,1)S(1)} %collective-permute-done.26.refs_3_) | copy-start | bytes 491524
  170.6 5.2 %copy-start.39 = (bf16[64,1280]{1,0:T(8,128)(2,1)}, bf16[64,1280]{1,0:T(8,128)(2,1)S(1)}, u32[]{:S(2)}) copy-start(bf16[64,1280]{1,0:T(8,128)(2,1)S(1)} %collective-permute-done.28.refs_5_) | copy-start | bytes 491524
  172.4 3.4 %copy-start.41 = (bf16[64,1280]{1,0:T(8,128)(2,1)}, bf16[64,1280]{1,0:T(8,128)(2,1)S(1)}, u32[]{:S(2)}) copy-start(bf16[64,1280]{1,0:T(8,128)(2,1)S(1)} %collective-permute-done.30.refs_7_) | copy-start | bytes 491524
  175.8 25.5 %collective-permute-start.33 = (bf16[2,160,1280]{2,1,0:T(8,128)(2,1)}, bf16[2,160,1280]{2,1,0:T(8,128)(2,1)}, u32[]{:S(2)}, u32[]{:S(2)}) collective-permute-start(bf16[2,160,1280]{2,1,0:T(8,128)(2,1)} %get-tuple-element.81), channel_id=1, source_target_pairs={{0,4},{4,0},{8,12},{12,8},{1,5},{5,1},{9,13},{13,9},{2,6},{6,2},{1... | collective-permute-start | bytes 2457608 | tf_op jit(solution)/shard_map/ppermute | solution.py:25
  175.9 1.9 copy-start.4
  177.9 1.9 copy-start.6
  180.7 1.0 copy-start.14
  181.7 1.0 copy-start.16
  194.7 6.6 %copy-start.10 = (bf16[2,160,1280]{2,1,0:T(8,128)(2,1)S(1)}, bf16[2,160,1280]{2,1,0:T(8,128)(2,1)}, u32[]{:S(2)}) copy-start(bf16[2,160,1280]{2,1,0:T(8,128)(2,1)} %copy-done.9) | copy-start | bytes 2457604
  200.8 2.5 %collective-permute-start.31 = (bf16[2,160,1280]{2,1,0:T(8,128)(2,1)S(1)}, bf16[2,160,1280]{2,1,0:T(8,128)(2,1)S(1)}, u32[]{:S(2)}, u32[]{:S(2)}) collective-permute-start(bf16[2,160,1280]{2,1,0:T(8,128)(2,1)S(1)} %get-tuple-element.79), channel_id=1, source_target_pairs={{0,4},{4,0},{8,12},{12,8},{1,5},{5,1},{9,13},{13,9},{2,6},{6,2},{1... | collective-permute-start | bytes 2457608 | tf_op jit(solution)/shard_map/ppermute | solution.py:25
  202.7 12.4 %collective-permute-start.34 = (bf16[160,1280]{1,0:T(8,128)(2,1)S(1)}, bf16[160,1280]{1,0:T(8,128)(2,1)S(1)}, u32[]{:S(2)}, u32[]{:S(2)}) collective-permute-start(bf16[160,1280]{1,0:T(8,128)(2,1)S(1)} %fusion.4), channel_id=1, source_target_pairs={{0,8},{4,12},{8,0},{12,4},{1,9},{5,13},{9,1},{13,5},{2,10},{6,14},... | collective-permute-start | bytes 1228808 | tf_op jit(solution)/shard_map/ppermute | solution.py:20
  203.5 19.4 %collective-permute-start.32 = (bf16[160,1280]{1,0:T(8,128)(2,1)S(1)}, bf16[160,1280]{1,0:T(8,128)(2,1)S(1)}, u32[]{:S(2)}, u32[]{:S(2)}) collective-permute-start(bf16[160,1280]{1,0:T(8,128)(2,1)S(1)} %fusion.3), channel_id=1, source_target_pairs={{0,8},{4,12},{8,0},{12,4},{1,9},{5,13},{9,1},{13,5},{2,10},{6,14},... | collective-permute-start | bytes 1228808 | tf_op jit(solution)/shard_map/ppermute | solution.py:20
  (17 other events, 15.2 us)

commit v5 on v4

--- a/solution.py
+++ b/solution.py
@@ -12,7 +12,7 @@
 
 
 EPS = 1e-06
-VMEM_BYTES = 16 * 1024 * 1024
+VMEM_BYTES = 6 * 1024 * 1024
 
 
 def rotated(value, axis, steps):
@@ -27,6 +27,18 @@
 
 def gather_parts(piece):
     return [piece] + [rotated(piece, "tp", k) for k in range(1, lax.axis_size("tp"))]
+
+
+def gather_chain(piece):
+    count, half = lax.axis_size("tp"), piece.shape[0] // 2
+    parts = [[piece]] + [None] * (count - 1)
+    right, left = piece, piece
+    for k in range(1, (count + 1) // 2):
+        right, left = rotated(right, "tp", 1), rotated(left, "tp", -1)
+        parts[k], parts[count - k] = [right], [left]
+    if count % 2 == 0:
+        parts[count // 2] = [rotated(right[:half], "tp", 1), rotated(left[half:], "tp", -1)]
+    return parts
 
 
 def reduce_parts(parts):
@@ -117,27 +129,31 @@
 
 
 def partial_body(count, sel_ref, *refs):
-    parts, (gain, w_in, w_out) = refs[:count], refs[count : count + 3]
-    outs, (xn, acc) = refs[count + 3 : 2 * count + 3], refs[2 * count + 3 :]
-    rows = parts[0].shape[0]
-    for i, part in enumerate(parts):
-        xn[i * rows : (i + 1) * rows, :] = normed(part[...].astype(jnp.float32), gain[...])
+    pieces, (gain, w_in, w_out) = refs[:count], refs[count : count + 3]
+    outs, (xn, acc) = refs[count + 3 : -2], refs[-2:]
+    start = 0
+    for piece in pieces:
+        stop = start + piece.shape[0]
+        xn[start:stop, :] = normed(piece[...].astype(jnp.float32), gain[...])
+        start = stop
     for t, tile in enumerate(tiles(w_in.shape[1])):
         act, unused = gelu_pair(dot_nn(xn[...], w_in[:, tile]))
         term = dot_nt(act.astype(jnp.bfloat16), w_out[:, tile])
         acc[...] = term if t == 0 else acc[...] + term
+    rows = outs[0].shape[0]
     for i, out in enumerate(outs):
         out[...] = acc[i * rows : (i + 1) * rows, :].astype(jnp.bfloat16)
 
 
 def block0_partials(parts, gain, w_in, w_out, sel):
-    rows, width = parts[0].shape
+    pieces = [piece for part in parts for piece in part]
+    rows, width = sum(piece.shape[0] for piece in parts[0]), w_in.shape[0]
     hidden, n = w_in.shape[1], len(parts)
     return run(
-        functools.partial(partial_body, n),
+        functools.partial(partial_body, len(pieces)),
         "block0_partial",
         sel,
-        [*parts, gain, w_in, w_out],
+        [*pieces, gain, w_in, w_out],
         [bf16(rows, width)] * n,
         [
             pltpu.VMEM((n * rows, width), jnp.bfloat16),
@@ -388,9 +404,10 @@
 
     flat = latents.reshape(count * tokens, width)
     got_in = swapped(quarter(own[0], place), "sec", 1)
-    lat_parts = gather_parts(flat)
-    got_out = swapped(quarter(own[1], place), "sec", 1)
+    lat_parts = gather_chain(flat)
+    out_quarter, got_in = lax.optimization_barrier((quarter(own[1], place), got_in))
     across_in = swapped(got_in, "dp", 2)
+    got_out = swapped(out_quarter, "sec", 1)
     across_out = swapped(got_out, "dp", 2)
 
     onehot = (
@@ -402,15 +419,16 @@
     near = [k for k in range(1, n_tp) if 2 * k != n_tp]
     far = [k for k in range(1, n_tp) if 2 * k == n_tp]
     eps_parts = [None] * n_tp
-    arrivals = ([], [got_in], [got_out, across_in])
-    for ks, arrived in zip(([0], near, far), arrivals):
+    results = []
+    for ks, hop in ((near, got_in), (far, None), ([0], got_out)):
         if ks:
-            operands, unused = lax.optimization_barrier(([lat_parts[k] for k in ks], arrived))
+            operands, unused = lax.optimization_barrier(
+                ([lat_parts[k] for k in ks], (hop, results))
+            )
             results = block0_partials(operands, gains[:1], *own, sel)
             for k, result in zip(ks, results):
                 eps_parts[k] = result
-    eps_mix, across_out = lax.optimization_barrier((reduce_parts(eps_parts), across_out))
-    eps_mix = eps_mix.reshape(count, tokens, width)
+    eps_mix = reduce_parts(eps_parts).reshape(count, tokens, width)
     other = (assembled(got_in, across_in, place), assembled(got_out, across_out, place))
     base = latents.astype(jnp.float32)
     images = ((base - sigma * (base + eps_mix)) / alpha).astype(jnp.bfloat16)
@@ -421,7 +439,10 @@
     mine_rows = mine.reshape(half * tokens, width)
     seen_parts = gather_parts(mine_rows)
 
-    states = [block0_state(part, gains[:1], own[0], other[0], sel) for part in lat_parts]
+    states = [
+        block0_state(jnp.concatenate(part, 0), gains[:1], own[0], other[0], sel)
+        for part in lat_parts
+    ]
     slopes1, pool_parts = [None] * n_tp, [None] * n_tp
     for ks in ([0] + near, far):
         if ks:

time: 226 us -> 211 us (0.934)
  waiting for transfers between devices: 105 us -> 80 us
  local copies, waits for them, and re-layouts: 32.5 us -> 37.8 us
  starting transfers between devices: 43.8 us -> 47.7 us
    ppermute x14, waiting for transfers between devices: 39.5 us -> 10.9 us  [swapped(): return lax.ppermute(value, axis, [(i, i ^ bit) for i in range(count)])]
    ppermute x20 -> x21, waiting for transfers between devices: 61.7 us -> 68 us  [rotated(): lax.ppermute(value, axis, [(i, (i + steps) % count) for i in range(count)])]
    ppermute x20 -> x21, starting transfers between devices: 27.1 us -> 32.9 us  [rotated(): lax.ppermute(value, axis, [(i, (i + steps) % count) for i in range(count)])]
    slice x0 -> x2, local copies, waits for them, and re-layouts: none -> 3.19 us  [the longest x1 1.61 us: gather_chain(): right[:half]]
    ppermute x1, waiting for transfers between devices: 4.01 us -> 1.05 us  [on_device(): arrived = lax.ppermute(images[:half], 'sec', [(0, 1)])]
    unnamed x92 -> x84, local copies, waits for them, and re-layouts: 24 us -> 26.5 us
  transfers between devices with their start and end apart: 35 -> 36, of which waited for: 17 -> 19; matrix products, arithmetic and copies ran while one was open for 5% -> 8% of each run, Pallas kernels for 10% -> 11%
where the time goes in v5:
time: 211 us; the launch traced here: 210 us
  waiting for transfers between devices  80 us (38%)
  starting transfers between devices  47.7 us (23%)
  local copies, waits for them, and re-layouts  37.8 us (18%)
  Pallas kernels  33.9 us (16%)
  other arithmetic  6.77 us (3%)
  between operations  2.59 us (1%)
    ppermute x21, waiting for transfers between devices, rotated(): lax.ppermute(value, axis, [(i, (i + steps) % count) for i in range(count)])  68 us
    pallas_call x12, Pallas kernels, run(): pl.pallas_call(body, in_specs=[IN_SMEM] + [IN_VMEM] * len(operands), out_...  33.9 us
    ppermute x21, starting transfers between devices, rotated(): lax.ppermute(value, axis, [(i, (i + steps) % count) for i in range(count)])  32.9 us
    unnamed x84, local copies, waits for them, and re-layouts  26.5 us
    ppermute x14, starting transfers between devices, swapped(): return lax.ppermute(value, axis, [(i, i ^ bit) for i in range(count)])  11.3 us
    ppermute x14, waiting for transfers between devices, swapped(): return lax.ppermute(value, axis, [(i, i ^ bit) for i in range(count)])  10.9 us
  transfers between devices with their start and end apart: 36, of which 19 were waited for; matrix products, arithmetic and copies ran while one was open for 8% of the time, Pallas kernels for 11%

profile of v5, /device:TPU:0, one launch (start us, length us, event | category | flops | bytes accessed | tf_op | source)
XLA Modules:
  0.0 209.6 jit_solution(11302276075632784676)
XLA Ops:
  0.7 3.1 %collective-permute-start.2 = (bf16[128,1280]{1,0:T(8,128)(2,1)}, bf16[128,1280]{1,0:T(8,128)(2,1)}, u32[]{:S(2)}, u32[]{:S(2)}) collective-permute-start(bf16[128,1280]{1,0:T(8,128)(2,1)} %bitcast.43), channel_id=1, source_target_pairs={{0,1},{1,2},{2,3},{3,0},{4,5},{5,6},{6,7},{7,4},{8,9},{9,10},{10,1... | collective-permute-start | bytes 983048 | tf_op jit(solution)/shard_map/ppermute | solution.py:20
  3.7 2.1 collective-permute-start.4
  5.8 2.1 dynamic-slice_bitcast_fusion
  7.9 1.7 collective-permute-start
  12.0 2.1 dynamic-slice_bitcast_fusion.1
  14.7 1.6 slice.132
  16.3 4.2 %collective-permute-done.4.refs_1_.part = bf16[128,1280]{1,0:T(8,128)(2,1)} collective-permute-done((bf16[128,1280]{1,0:T(8,128)(2,1)}, bf16[128,1280]{1,0:T(8,128)(2,1)}, u32[]{:S(2)}, u32[]{:S(2)}) %collective-permute-start.4) | collective-permute-done | bytes 327712 | tf_op jit(solution)/shard_map/ppermute | solution.py:20
  20.5 1.6 slice.133
  22.0 3.1 %collective-permute-start.5 = (bf16[64,1280]{1,0:T(8,128)(2,1)}, bf16[64,1280]{1,0:T(8,128)(2,1)}, u32[]{:S(2)}, u32[]{:S(2)}) collective-permute-start(bf16[64,1280]{1,0:T(8,128)(2,1)} %slice.133), channel_id=1, source_target_pairs={{0,3},{1,0},{2,1},{3,2},{4,7},{5,4},{6,5},{7,6},{8,11},{9,8},{10,9... | collective-permute-start | bytes 491528 | tf_op jit(solution)/shard_map/ppermute | solution.py:20
  27.9 1.5 collective-permute-start.1
  30.1 1.0 pad_maximum_fusion.part
  31.2 1.9 copy-done.2
  33.1 3.4 %block0_partial.3 = (bf16[128,1280]{1,0:T(8,128)(2,1)S(1)}, bf16[128,1280]{1,0:T(8,128)(2,1)S(1)}) custom-call(s32[3]{0:T(128)S(1)} %pad_add_fusion.sel_ref, bf16[128,1280]{1,0:T(8,128)(2,1)} %collective-permute-done.2.refs_0_.part, bf16[128,1280]{1,0:T(8,128)(2,1)} %collective-permute-done.4.refs_1_.part, ...), custom_call_target="tpu_custom_call" | custom-call | flops 1677721600 | bytes 7869440 | tf_op jit(solution)/shard_map/block0_partial/pallas_call | solution.py:98
  36.6 2.5 %collective-permute-start.6 = (bf16[128,1280]{1,0:T(8,128)(2,1)S(1)}, bf16[128,1280]{1,0:T(8,128)(2,1)S(1)}, u32[]{:S(2)}, u32[]{:S(2)}) collective-permute-start(bf16[128,1280]{1,0:T(8,128)(2,1)S(1)} %get-tuple-element.48), channel_id=1, source_target_pairs={{0,3},{1,0},{2,1},{3,2},{4,7},{5,4},{6,5},{7,6},{8,11},{9,8},{10,9... | collective-permute-start | bytes 983048 | tf_op jit(solution)/shard_map/ppermute | solution.py:20
  39.1 3.1 %block0_partial.4 = bf16[128,1280]{1,0:T(8,128)(2,1)S(1)} custom-call(s32[3]{0:T(128)S(1)} %pad_add_fusion.sel_ref, bf16[64,1280]{1,0:T(8,128)(2,1)} %collective-permute-done.3.refs_0_, bf16[64,1280]{1,0:T(8,128)(2,1)} %collective-permute-done.5.refs_1_, f32[1,1280]{1,0:T(1,128)S(1)} %get-tuple-element.101.refs_2_.refs_1_.gain, ...), custom_call_target="tpu_custom_call" | custom-call | flops 838860800 | bytes 7214080 | tf_op jit(solution)/shard_map/block0_partial/pallas_call | solution.py:98
  43.1 1.4 constant_dynamic-update-slice_fusion.7
  44.5 2.4 %collective-permute-done.1 = bf16[320,1280]{1,0:T(8,128)(2,1)S(1)} collective-permute-done((bf16[320,1280]{1,0:T(8,128)(2,1)}, bf16[320,1280]{1,0:T(8,128)(2,1)S(1)}, u32[]{:S(2)}, u32[]{:S(2)}) %collective-permute-start.1) | collective-permute-done | bytes 819232 | tf_op jit(solution)/shard_map/ppermute | solution.py:25
  46.9 1.3 collective-permute-start.13
  48.3 2.7 %block0_partial.5 = bf16[128,1280]{1,0:T(8,128)(2,1)S(1)} custom-call(s32[3]{0:T(128)S(1)} %pad_add_fusion.sel_ref, bf16[128,1280]{1,0:T(8,128)(2,1)S(1)} %bitcast.45, f32[1,1280]{1,0:T(1,128)S(1)} %get-tuple-element.101.refs_2_.refs_1_.gain, bf16[1280,1280]{1,0:T(8,128)(2,1)S(1)} %bitcast.28, bf16[1280,1280]{1,0:T(8,128)(2,1)S(1)} %bitcast.38), custom_call_target="tpu_custom_call" | custom-call | flops 838860800 | bytes 7214080 | tf_op jit(solution)/shard_map/block0_partial/pallas_call | solution.py:98
  50.9 17.5 %collective-permute-done.7 = bf16[128,1280]{1,0:T(8,128)(2,1)S(1)} collective-permute-done((bf16[128,1280]{1,0:T(8,128)(2,1)S(1)}, bf16[128,1280]{1,0:T(8,128)(2,1)S(1)}, u32[]{:S(2)}, u32[]{:S(2)}) %collective-permute-start.7) | collective-permute-done | bytes 327712 | tf_op jit(solution)/shard_map/ppermute | solution.py:20
  68.9 3.6 %collective-permute-start.9 = (bf16[1,64,1280]{2,1,0:T(8,128)(2,1)S(1)}, bf16[1,64,1280]{2,1,0:T(8,128)(2,1)S(1)}, u32[]{:S(2)}, u32[]{:S(2)}) collective-permute-start(bf16[1,64,1280]{2,1,0:T(8,128)(2,1)S(1)} %slice.135), channel_id=1, source_target_pairs={{0,16},{1,17},{2,18},{3,19},{4,20},{5,21},{6,22},{7,23},{8,24},{9,... | collective-permute-start | bytes 491528 | tf_op jit(solution)/shard_map/ppermute | solution.py:436
  72.6 1.6 collective-permute-start.16
  74.8 1.0 collective-permute-done.9
  75.9 2.9 %collective-permute-start.10 = (bf16[64,1280]{1,0:T(8,128)(2,1)S(1)}, bf16[64,1280]{1,0:T(8,128)(2,1)S(1)}, u32[]{:S(2)}, u32[]{:S(2)}) collective-permute-start(bf16[64,1280]{1,0:T(8,128)(2,1)S(1)} %fusion.11.refs_0_), channel_id=1, source_target_pairs={{0,1},{1,2},{2,3},{3,0},{4,5},{5,6},{6,7},{7,4},{8,9},{9,10},{10,1... | collective-permute-start | bytes 491528 | tf_op jit(solution)/shard_map/ppermute | solution.py:20
  78.9 7.0 %collective-permute-done.10.refs_1_ = bf16[64,1280]{1,0:T(8,128)(2,1)S(1)} collective-permute-done((bf16[64,1280]{1,0:T(8,128)(2,1)S(1)}, bf16[64,1280]{1,0:T(8,128)(2,1)S(1)}, u32[]{:S(2)}, u32[]{:S(2)}) %collective-permute-start.10) | collective-permute-done | bytes 163872 | tf_op jit(solution)/shard_map/ppermute | solution.py:20
  85.8 1.7 collective-permute-start.11
  87.6 1.6 collective-permute-done.18.refs_0_
  89.3 4.4 %collective-permute-done.11.refs_2_ = bf16[64,1280]{1,0:T(8,128)(2,1)S(1)} collective-permute-done((bf16[64,1280]{1,0:T(8,128)(2,1)S(1)}, bf16[64,1280]{1,0:T(8,128)(2,1)S(1)}, u32[]{:S(2)}, u32[]{:S(2)}) %collective-permute-start.11) | collective-permute-done | bytes 163872 | tf_op jit(solution)/shard_map/ppermute | solution.py:20
  93.9 1.5 block0_state.4
  97.0 3.6 %reward_forward.2 = (bf16[64,1280]{1,0:T(8,128)(2,1)S(1)}, bf16[64,1280]{1,0:T(8,128)(2,1)S(1)}, bf16[64,1280]{1,0:T(8,128)(2,1)S(1)}, f32[8,1280]{1,0:T(8,128)S(1)}) custom-call(s32[3]{0:T(128)S(1)} %pad_add_fusion.sel_ref, bf16[64,1280]{1,0:T(8,128)(2,1)S(1)} %fusion.11.refs_0_, bf16[64,1280]{1,0:T(8,128)(2,1)S(1)} %collective-permute-done.10.refs_1_, ...), custom_call_target="tpu_custom_call" | custom-call | flops 629145600 | bytes 14136320 | tf_op jit(solution)/shard_map/reward_forward/pallas_call | solution.py:98
  100.7 2.7 %reward_forward.3 = (bf16[64,1280]{1,0:T(8,128)(2,1)S(1)}, f32[8,1280]{1,0:T(8,128)S(1)}) custom-call(s32[3]{0:T(128)S(1)} %pad_add_fusion.sel_ref, bf16[64,1280]{1,0:T(8,128)(2,1)S(1)} %collective-permute-done.18.refs_0_, f32[1,1280]{1,0:T(1,128)S(1)} %get-tuple-element.100.refs_3_.refs_1_, bf16[1280,1280]{1,0:T(8,128)(2,1)S(1)} %bitcast.31, ...), custom_call_target="tpu_custom_call" | custom-call | flops 209715200 | bytes 13480960 | tf_op jit(solution)/shard_map/reward_forward/pallas_call | solution.py:98
  103.5 2.7 %collective-permute-start.19 = (f32[5,1280]{1,0:T(8,128)S(1)}, f32[5,1280]{1,0:T(8,128)S(1)}, u32[]{:S(2)}, u32[]{:S(2)}) collective-permute-start(f32[5,1280]{1,0:T(8,128)S(1)} %pad_maximum_fusion.1), channel_id=1, source_target_pairs={{0,1},{1,2},{2,3},{3,0},{4,5},{5,6},{6,7},{7,4},{8,9},{9,10},{10,1... | collective-permute-start | bytes 76808 | tf_op jit(solution)/shard_map/ppermute | solution.py:20
  106.2 1.5 block0_state.6
  108.4 1.2 collective-permute-start.21
  109.6 2.0 collective-permute-start.20
  112.4 2.8 %collective-permute-done.20 = f32[5,1280]{1,0:T(8,128)S(1)} collective-permute-done((f32[5,1280]{1,0:T(8,128)S(1)}, f32[5,1280]{1,0:T(8,128)S(1)}, u32[]{:S(2)}, u32[]{:S(2)}) %collective-permute-start.20) | collective-permute-done | bytes 25632 | tf_op jit(solution)/shard_map/ppermute | solution.py:20
  115.8 2.7 %reward_back.1 = (bf16[64,1280]{1,0:T(8,128)(2,1)S(1)}, bf16[64,1280]{1,0:T(8,128)(2,1)S(1)}, bf16[64,1280]{1,0:T(8,128)(2,1)S(1)}, bf16[64,1280]{1,0:T(8,128)(2,1)S(1)}) custom-call(s32[3]{0:T(128)S(1)} %pad_add_fusion.sel_ref, bf16[16,1280]{1,0:T(8,128)(2,1)S(1)} %pad.4.refs_0_, bf16[64,1280]{1,0:T(8,128)(2,1)S(1)} %get-tuple-element.55.refs_1_, ...), custom_call_target="tpu_custom_call" | custom-call | flops 838860800 | bytes 14458880 | tf_op jit(solution)/shard_map/reward_back/pallas_call | solution.py:98
  118.4 1.4 collective-permute-start.22
  120.2 1.6 collective-permute-start.24
  121.8 1.9 block0_state.5
  125.2 2.1 %block0_state.7 = (bf16[128,1280]{1,0:T(8,128)(2,1)S(1)}, bf16[128,1280]{1,0:T(8,128)(2,1)S(1)}, bf16[640,128]{1,0:T(8,128)(2,1)S(1)}) custom-call(s32[3]{0:T(128)S(1)} %pad_add_fusion.sel_ref, bf16[128,1280]{1,0:T(8,128)(2,1)} %collective-permute-done.4.refs_1_.part, f32[1,1280]{1,0:T(1,128)S(1)} %get-tuple-element.101.refs_2_.refs_1_.gain, ...), custom_call_target="tpu_custom_call" | custom-call | flops 419430400 | bytes 7705600 | tf_op jit(solution)/shard_map/block0_state/pallas_call | solution.py:98
  128.7 5.3 %collective-permute-done.23 = bf16[64,1280]{1,0:T(8,128)(2,1)S(1)} collective-permute-done((bf16[64,1280]{1,0:T(8,128)(2,1)S(1)}, bf16[64,1280]{1,0:T(8,128)(2,1)S(1)}, u32[]{:S(2)}, u32[]{:S(2)}) %collective-permute-start.23) | collective-permute-done | bytes 163872 | tf_op jit(solution)/shard_map/ppermute | solution.py:20
  135.0 2.0 collective-permute-start.28
  137.0 2.8 %collective-permute-start.30 = (bf16[64,1280]{1,0:T(8,128)(2,1)S(1)}, bf16[64,1280]{1,0:T(8,128)(2,1)S(1)}, u32[]{:S(2)}, u32[]{:S(2)}) collective-permute-start(bf16[64,1280]{1,0:T(8,128)(2,1)S(1)} %multiply_convert_fusion.refs_0_), channel_id=1, source_target_pairs={{0,3},{1,0},{2,1},{3,2},{4,7},{5,4},{6,5},{7,6},{8,11},{9,8},{10,9... | collective-permute-start | bytes 491528 | tf_op jit(solution)/shard_map/ppermute | solution.py:20
  139.8 1.1 collective-permute-start.25
  140.9 2.5 %collective-permute-done.26.refs_2_ = bf16[64,1280]{1,0:T(8,128)(2,1)S(1)} collective-permute-done((bf16[64,1280]{1,0:T(8,128)(2,1)S(1)}, bf16[64,1280]{1,0:T(8,128)(2,1)S(1)}, u32[]{:S(2)}, u32[]{:S(2)}) %collective-permute-start.26) | collective-permute-done | bytes 163872 | tf_op jit(solution)/shard_map/ppermute | solution.py:20
  143.4 1.1 collective-permute-start.27
  144.5 3.9 %collective-permute-done.28.refs_4_ = bf16[64,1280]{1,0:T(8,128)(2,1)S(1)} collective-permute-done((bf16[64,1280]{1,0:T(8,128)(2,1)S(1)}, bf16[64,1280]{1,0:T(8,128)(2,1)S(1)}, u32[]{:S(2)}, u32[]{:S(2)}) %collective-permute-start.28) | collective-permute-done | bytes 163872 | tf_op jit(solution)/shard_map/ppermute | solution.py:20
  148.5 1.1 collective-permute-start.29
  150.5 5.0 %collective-permute-done.29.refs_5_ = bf16[64,1280]{1,0:T(8,128)(2,1)S(1)} collective-permute-done((bf16[64,1280]{1,0:T(8,128)(2,1)S(1)}, bf16[64,1280]{1,0:T(8,128)(2,1)S(1)}, u32[]{:S(2)}, u32[]{:S(2)}) %collective-permute-start.29) | collective-permute-done | bytes 163872 | tf_op jit(solution)/shard_map/ppermute | solution.py:25
  155.5 2.5 %collective-permute-done.31.refs_7_ = bf16[64,1280]{1,0:T(8,128)(2,1)S(1)} collective-permute-done((bf16[64,1280]{1,0:T(8,128)(2,1)S(1)}, bf16[64,1280]{1,0:T(8,128)(2,1)S(1)}, u32[]{:S(2)}, u32[]{:S(2)}) %collective-permute-start.31) | collective-permute-done | bytes 163872 | tf_op jit(solution)/shard_map/ppermute | solution.py:25
  158.0 2.5 %grad_out.1 = (bf16[2,160,1280]{2,1,0:T(8,128)(2,1)S(1)}, bf16[2,160,1280]{2,1,0:T(8,128)(2,1)}) custom-call(s32[3]{0:T(128)S(1)} %pad_add_fusion.sel_ref, bf16[64,1280]{1,0:T(8,128)(2,1)S(1)} %multiply_convert_fusion.refs_0_, bf16[64,1280]{1,0:T(8,128)(2,1)S(1)} %collective-permute-done.25.refs_1_, bf16[64,1280]{1,0:T(8,128)(2,1)S(1)} %collective-permute-done.26.refs_2_, ...), custom_call_target="tpu_custom_call" | custom-call | flops 838860800 | bytes 4259840 | tf_op jit(solution)/shard_map/grad_out/pallas_call | solution.py:98
  161.6 1.9 copy-done.4
  163.5 1.9 copy-done.6
  166.3 1.0 copy-done.13
  167.3 1.0 copy-done.15
  168.3 1.0 copy-done.17
  169.3 1.0 copy-done.19
  180.3 6.1 %grad_in.1 = (bf16[2,160,1280]{2,1,0:T(8,128)(2,1)S(1)}, bf16[2,160,1280]{2,1,0:T(8,128)(2,1)S(1)}) custom-call(s32[3]{0:T(128)S(1)} %pad_add_fusion.sel_ref, bf16[64,1280]{1,0:T(8,128)(2,1)S(1)} %copy-done.11, bf16[64,1280]{1,0:T(8,128)(2,1)S(1)} %copy-done.35, bf16[64,1280]{1,0:T(8,128)(2,1)S(1)} %copy-done.29, bf16[64,1280]{1,0:T(8,128)(2,1)S(1)} %copy-done.37, ...), custom_call_target="tpu_custom_call" | custom-call | flops 2516582400 | bytes 11468800 | tf_op jit(solution)/shard_map/grad_in/pallas_call | solution.py:98
  187.0 1.3 convert_add_fusion
  189.5 1.3 collective-permute-start.33
  190.8 10.0 %collective-permute-done.35 = bf16[160,1280]{1,0:T(8,128)(2,1)S(1)} collective-permute-done((bf16[160,1280]{1,0:T(8,128)(2,1)S(1)}, bf16[160,1280]{1,0:T(8,128)(2,1)S(1)}, u32[]{:S(2)}, u32[]{:S(2)}) %collective-permute-start.35) | collective-permute-done | bytes 409632 | tf_op jit(solution)/shard_map/ppermute | solution.py:20
  200.8 1.0 bitcast_add_fusion
  201.7 6.9 %collective-permute-done.33 = bf16[160,1280]{1,0:T(8,128)(2,1)S(1)} collective-permute-done((bf16[160,1280]{1,0:T(8,128)(2,1)S(1)}, bf16[160,1280]{1,0:T(8,128)(2,1)S(1)}, u32[]{:S(2)}, u32[]{:S(2)}) %collective-permute-start.33) | collective-permute-done | bytes 409632 | tf_op jit(solution)/shard_map/ppermute | solution.py:20
  (168 shorter events, 31.1 us)
Async XLA Ops:
  0.6 9.0 %copy-start = (bf16[64,1280]{1,0:T(8,128)(2,1)S(1)}, bf16[64,1280]{1,0:T(8,128)(2,1)}, u32[]{:S(2)}) copy-start(bf16[64,1280]{1,0:T(8,128)(2,1)} %param.10) | copy-start | bytes 491524
  0.6 30.5 %copy-start.1 = (bf16[1,1280,1280]{2,1,0:T(8,128)(2,1)S(1)}, bf16[1,1280,1280]{2,1,0:T(8,128)(2,1)}, u32[]{:S(2)}) copy-start(bf16[1,1280,1280]{2,1,0:T(8,128)(2,1)} %param.12) | copy-start | bytes 9830404
  0.7 14.0 %collective-permute-start.2 = (bf16[128,1280]{1,0:T(8,128)(2,1)}, bf16[128,1280]{1,0:T(8,128)(2,1)}, u32[]{:S(2)}, u32[]{:S(2)}) collective-permute-start(bf16[128,1280]{1,0:T(8,128)(2,1)} %bitcast.43), channel_id=1, source_target_pairs={{0,1},{1,2},{2,3},{3,0},{4,5},{5,6},{6,7},{7,4},{8,9},{9,10},{10,1... | collective-permute-start | bytes 983048 | tf_op jit(solution)/shard_map/ppermute | solution.py:20
  3.7 16.7 %collective-permute-start.4 = (bf16[128,1280]{1,0:T(8,128)(2,1)}, bf16[128,1280]{1,0:T(8,128)(2,1)}, u32[]{:S(2)}, u32[]{:S(2)}) collective-permute-start(bf16[128,1280]{1,0:T(8,128)(2,1)} %bitcast.44), channel_id=1, source_target_pairs={{0,3},{1,0},{2,1},{3,2},{4,7},{5,4},{6,5},{7,6},{8,11},{9,8},{10,9... | collective-permute-start | bytes 983048 | tf_op jit(solution)/shard_map/ppermute | solution.py:20
  7.9 20.0 %collective-permute-start = (bf16[320,1280]{1,0:T(8,128)(2,1)}, bf16[320,1280]{1,0:T(8,128)(2,1)}, u32[]{:S(2)}, u32[]{:S(2)}) collective-permute-start(bf16[320,1280]{1,0:T(8,128)(2,1)} %dynamic-slice_bitcast_fusion), channel_id=1, source_target_pairs={{0,16},{16,0},{1,17},{17,1},{2,18},{18,2},{3,19},{19,3},{4,20},{20... | collective-permute-start | bytes 2457608 | tf_op jit(solution)/shard_map/ppermute | solution.py:25
  16.3 13.3 %collective-permute-start.3 = (bf16[64,1280]{1,0:T(8,128)(2,1)}, bf16[64,1280]{1,0:T(8,128)(2,1)}, u32[]{:S(2)}, u32[]{:S(2)}) collective-permute-start(bf16[64,1280]{1,0:T(8,128)(2,1)} %slice.132), channel_id=1, source_target_pairs={{0,1},{1,2},{2,3},{3,0},{4,5},{5,6},{6,7},{7,4},{8,9},{9,10},{10,1... | collective-permute-start | bytes 491528 | tf_op jit(solution)/shard_map/ppermute | solution.py:20
  22.0 8.1 %collective-permute-start.5 = (bf16[64,1280]{1,0:T(8,128)(2,1)}, bf16[64,1280]{1,0:T(8,128)(2,1)}, u32[]{:S(2)}, u32[]{:S(2)}) collective-permute-start(bf16[64,1280]{1,0:T(8,128)(2,1)} %slice.133), channel_id=1, source_target_pairs={{0,3},{1,0},{2,1},{3,2},{4,7},{5,4},{6,5},{7,6},{8,11},{9,8},{10,9... | collective-permute-start | bytes 491528 | tf_op jit(solution)/shard_map/ppermute | solution.py:20
  27.9 19.0 %collective-permute-start.1 = (bf16[320,1280]{1,0:T(8,128)(2,1)}, bf16[320,1280]{1,0:T(8,128)(2,1)S(1)}, u32[]{:S(2)}, u32[]{:S(2)}) collective-permute-start(bf16[320,1280]{1,0:T(8,128)(2,1)} %dynamic-slice_bitcast_fusion.1), channel_id=1, source_target_pairs={{0,16},{16,0},{1,17},{17,1},{2,18},{18,2},{3,19},{19,3},{4,20},{20... | collective-permute-start | bytes 2457608 | tf_op jit(solution)/shard_map/ppermute | solution.py:25
  31.1 43.5 %collective-permute-start.12 = (bf16[320,1280]{1,0:T(8,128)(2,1)}, bf16[320,1280]{1,0:T(8,128)(2,1)S(1)}, u32[]{:S(2)}, u32[]{:S(2)}) collective-permute-start(bf16[320,1280]{1,0:T(8,128)(2,1)} %collective-permute-done), channel_id=1, source_target_pairs={{0,4},{4,0},{8,12},{12,8},{1,5},{5,1},{9,13},{13,9},{2,6},{6,2},{1... | collective-permute-start | bytes 2457608 | tf_op jit(solution)/shard_map/ppermute | solution.py:25
  31.2 1.9 copy-start.2
  36.6 31.9 %collective-permute-start.6 = (bf16[128,1280]{1,0:T(8,128)(2,1)S(1)}, bf16[128,1280]{1,0:T(8,128)(2,1)S(1)}, u32[]{:S(2)}, u32[]{:S(2)}) collective-permute-start(bf16[128,1280]{1,0:T(8,128)(2,1)S(1)} %get-tuple-element.48), channel_id=1, source_target_pairs={{0,3},{1,0},{2,1},{3,2},{4,7},{5,4},{6,5},{7,6},{8,11},{9,8},{10,9... | collective-permute-start | bytes 983048 | tf_op jit(solution)/shard_map/ppermute | solution.py:20
  39.1 29.4 %collective-permute-start.8 = (bf16[128,1280]{1,0:T(8,128)(2,1)S(1)}, bf16[128,1280]{1,0:T(8,128)(2,1)S(1)}, u32[]{:S(2)}, u32[]{:S(2)}) collective-permute-start(bf16[128,1280]{1,0:T(8,128)(2,1)S(1)} %get-tuple-element.49), channel_id=1, source_target_pairs={{0,1},{1,2},{2,3},{3,0},{4,5},{5,6},{6,7},{7,4},{8,9},{9,10},{10,1... | collective-permute-start | bytes 983048 | tf_op jit(solution)/shard_map/ppermute | solution.py:20
  42.2 6.1 %copy-start.3 = (bf16[1,1280,1280]{2,1,0:T(8,128)(2,1)S(1)}, bf16[1,1280,1280]{2,1,0:T(8,128)(2,1)}, u32[]{:S(2)}) copy-start(bf16[1,1280,1280]{2,1,0:T(8,128)(2,1)} %param.13) | copy-start | bytes 9830404
  42.2 6.0 %copy-start.7 = (bf16[2,64,1280]{2,1,0:T(8,128)(2,1)S(1)}, bf16[2,64,1280]{2,1,0:T(8,128)(2,1)}, u32[]{:S(2)}) copy-start(bf16[2,64,1280]{2,1,0:T(8,128)(2,1)} %param.7) | copy-start | bytes 983044
  42.2 26.2 %collective-permute-start.7 = (bf16[128,1280]{1,0:T(8,128)(2,1)S(1)}, bf16[128,1280]{1,0:T(8,128)(2,1)S(1)}, u32[]{:S(2)}, u32[]{:S(2)}) collective-permute-start(bf16[128,1280]{1,0:T(8,128)(2,1)S(1)} %block0_partial.4), channel_id=1, source_target_pairs={{0,2},{1,3},{2,0},{3,1},{4,6},{5,7},{6,4},{7,5},{8,10},{9,11},{10,... | collective-permute-start | bytes 983048 | tf_op jit(solution)/shard_map/ppermute | solution.py:20
  46.9 27.2 %collective-permute-start.13 = (bf16[320,1280]{1,0:T(8,128)(2,1)}, bf16[320,1280]{1,0:T(8,128)(2,1)S(1)}, u32[]{:S(2)}, u32[]{:S(2)}) collective-permute-start(bf16[320,1280]{1,0:T(8,128)(2,1)} %collective-permute-done), channel_id=1, source_target_pairs={{0,8},{4,12},{8,0},{12,4},{1,9},{5,13},{9,1},{13,5},{2,10},{6,14},... | collective-permute-start | bytes 2457608 | tf_op jit(solution)/shard_map/ppermute | solution.py:25
  68.9 6.9 %collective-permute-start.9 = (bf16[1,64,1280]{2,1,0:T(8,128)(2,1)S(1)}, bf16[1,64,1280]{2,1,0:T(8,128)(2,1)S(1)}, u32[]{:S(2)}, u32[]{:S(2)}) collective-permute-start(bf16[1,64,1280]{2,1,0:T(8,128)(2,1)S(1)} %slice.135), channel_id=1, source_target_pairs={{0,16},{1,17},{2,18},{3,19},{4,20},{5,21},{6,22},{7,23},{8,24},{9,... | collective-permute-start | bytes 491528 | tf_op jit(solution)/shard_map/ppermute | solution.py:436
  72.5 24.3 %collective-permute-start.15 = (bf16[320,1280]{1,0:T(8,128)(2,1)S(1)}, bf16[320,1280]{1,0:T(8,128)(2,1)S(1)}, u32[]{:S(2)}, u32[]{:S(2)}) collective-permute-start(bf16[320,1280]{1,0:T(8,128)(2,1)S(1)} %collective-permute-done.1), channel_id=1, source_target_pairs={{0,4},{4,0},{8,12},{12,8},{1,5},{5,1},{9,13},{13,9},{2,6},{6,2},{1... | collective-permute-start | bytes 2457608 | tf_op jit(solution)/shard_map/ppermute | solution.py:25
  72.6 21.1 %collective-permute-start.16 = (bf16[320,1280]{1,0:T(8,128)(2,1)S(1)}, bf16[320,1280]{1,0:T(8,128)(2,1)S(1)}, u32[]{:S(2)}, u32[]{:S(2)}) collective-permute-start(bf16[320,1280]{1,0:T(8,128)(2,1)S(1)} %collective-permute-done.1), channel_id=1, source_target_pairs={{0,8},{4,12},{8,0},{12,4},{1,9},{5,13},{9,1},{13,5},{2,10},{6,14},... | collective-permute-start | bytes 2457608 | tf_op jit(solution)/shard_map/ppermute | solution.py:25
  74.1 19.7 %collective-permute-start.14 = (bf16[320,1280]{1,0:T(8,128)(2,1)S(1)}, bf16[320,1280]{1,0:T(8,128)(2,1)S(1)}, u32[]{:S(2)}, u32[]{:S(2)}) collective-permute-start(bf16[320,1280]{1,0:T(8,128)(2,1)S(1)} %collective-permute-done.13), channel_id=1, source_target_pairs={{0,4},{4,0},{8,12},{12,8},{1,5},{5,1},{9,13},{13,9},{2,6},{6,2},{1... | collective-permute-start | bytes 2457608 | tf_op jit(solution)/shard_map/ppermute | solution.py:25
  75.8 13.4 %collective-permute-start.18 = (bf16[64,1280]{1,0:T(8,128)(2,1)S(1)}, bf16[64,1280]{1,0:T(8,128)(2,1)S(1)}, u32[]{:S(2)}, u32[]{:S(2)}) collective-permute-start(bf16[64,1280]{1,0:T(8,128)(2,1)S(1)} %fusion.11.refs_0_), channel_id=1, source_target_pairs={{0,2},{1,3},{2,0},{3,1},{4,6},{5,7},{6,4},{7,5},{8,10},{9,11},{10,... | collective-permute-start | bytes 491528 | tf_op jit(solution)/shard_map/ppermute | solution.py:20
  75.9 9.9 %collective-permute-start.10 = (bf16[64,1280]{1,0:T(8,128)(2,1)S(1)}, bf16[64,1280]{1,0:T(8,128)(2,1)S(1)}, u32[]{:S(2)}, u32[]{:S(2)}) collective-permute-start(bf16[64,1280]{1,0:T(8,128)(2,1)S(1)} %fusion.11.refs_0_), channel_id=1, source_target_pairs={{0,1},{1,2},{2,3},{3,0},{4,5},{5,6},{6,7},{7,4},{8,9},{9,10},{10,1... | collective-permute-start | bytes 491528 | tf_op jit(solution)/shard_map/ppermute | solution.py:20
  85.8 7.8 %collective-permute-start.11 = (bf16[64,1280]{1,0:T(8,128)(2,1)S(1)}, bf16[64,1280]{1,0:T(8,128)(2,1)S(1)}, u32[]{:S(2)}, u32[]{:S(2)}) collective-permute-start(bf16[64,1280]{1,0:T(8,128)(2,1)S(1)} %fusion.11.refs_0_), channel_id=1, source_target_pairs={{0,3},{1,0},{2,1},{3,2},{4,7},{5,4},{6,5},{7,6},{8,11},{9,8},{10,9... | collective-permute-start | bytes 491528 | tf_op jit(solution)/shard_map/ppermute | solution.py:20
  93.7 3.3 %collective-permute-start.17 = (bf16[320,1280]{1,0:T(8,128)(2,1)S(1)}, bf16[320,1280]{1,0:T(8,128)(2,1)S(1)}, u32[]{:S(2)}, u32[]{:S(2)}) collective-permute-start(bf16[320,1280]{1,0:T(8,128)(2,1)S(1)} %collective-permute-done.16), channel_id=1, source_target_pairs={{0,4},{4,0},{8,12},{12,8},{1,5},{5,1},{9,13},{13,9},{2,6},{6,2},{1... | collective-permute-start | bytes 2457608 | tf_op jit(solution)/shard_map/ppermute | solution.py:25
  97.0 18.7 %copy-start.5 = (bf16[1280,1280]{1,0:T(8,128)(2,1)}, bf16[1280,1280]{1,0:T(8,128)(2,1)S(1)}, u32[]{:S(2)}) copy-start(bf16[1280,1280]{1,0:T(8,128)(2,1)S(1)} %constant_dynamic-update-slice_fusion.refs_7_.refs_5_.refs_8_.refs_17_) | copy-start | bytes 9830404
  103.5 8.1 %collective-permute-start.19 = (f32[5,1280]{1,0:T(8,128)S(1)}, f32[5,1280]{1,0:T(8,128)S(1)}, u32[]{:S(2)}, u32[]{:S(2)}) collective-permute-start(f32[5,1280]{1,0:T(8,128)S(1)} %pad_maximum_fusion.1), channel_id=1, source_target_pairs={{0,1},{1,2},{2,3},{3,0},{4,5},{5,6},{6,7},{7,4},{8,9},{9,10},{10,1... | collective-permute-start | bytes 76808 | tf_op jit(solution)/shard_map/ppermute | solution.py:20
  108.4 10.0 %copy-start.22 = (bf16[640,128]{1,0:T(8,128)(2,1)}, bf16[640,128]{1,0:T(8,128)(2,1)S(1)}, u32[]{:S(2)}) copy-start(bf16[640,128]{1,0:T(8,128)(2,1)S(1)} %get-tuple-element.71.refs_14_) | copy-start | bytes 491524
  108.4 4.0 %collective-permute-start.21 = (f32[5,1280]{1,0:T(8,128)S(1)}, f32[5,1280]{1,0:T(8,128)S(1)}, u32[]{:S(2)}, u32[]{:S(2)}) collective-permute-start(f32[5,1280]{1,0:T(8,128)S(1)} %pad_maximum_fusion.1), channel_id=1, source_target_pairs={{0,3},{1,0},{2,1},{3,2},{4,7},{5,4},{6,5},{7,6},{8,11},{9,8},{10,9... | collective-permute-start | bytes 76808 | tf_op jit(solution)/shard_map/ppermute | solution.py:20
  109.6 5.6 %collective-permute-start.20 = (f32[5,1280]{1,0:T(8,128)S(1)}, f32[5,1280]{1,0:T(8,128)S(1)}, u32[]{:S(2)}, u32[]{:S(2)}) collective-permute-start(f32[5,1280]{1,0:T(8,128)S(1)} %pad_maximum_fusion.1), channel_id=1, source_target_pairs={{0,2},{1,3},{2,0},{3,1},{4,6},{5,7},{6,4},{7,5},{8,10},{9,11},{10,... | collective-permute-start | bytes 76808 | tf_op jit(solution)/shard_map/ppermute | solution.py:20
  118.4 10.3 %collective-permute-start.22 = (bf16[64,1280]{1,0:T(8,128)(2,1)S(1)}, bf16[64,1280]{1,0:T(8,128)(2,1)S(1)}, u32[]{:S(2)}, u32[]{:S(2)}) collective-permute-start(bf16[64,1280]{1,0:T(8,128)(2,1)S(1)} %get-tuple-element.60), channel_id=1, source_target_pairs={{0,3},{1,0},{2,1},{3,2},{4,7},{5,4},{6,5},{7,6},{8,11},{9,8},{10,9... | collective-permute-start | bytes 491528 | tf_op jit(solution)/shard_map/ppermute | solution.py:20
  119.8 14.2 %collective-permute-start.23 = (bf16[64,1280]{1,0:T(8,128)(2,1)S(1)}, bf16[64,1280]{1,0:T(8,128)(2,1)S(1)}, u32[]{:S(2)}, u32[]{:S(2)}) collective-permute-start(bf16[64,1280]{1,0:T(8,128)(2,1)S(1)} %get-tuple-element.61), channel_id=1, source_target_pairs={{0,2},{1,3},{2,0},{3,1},{4,6},{5,7},{6,4},{7,5},{8,10},{9,11},{10,... | collective-permute-start | bytes 491528 | tf_op jit(solution)/shard_map/ppermute | solution.py:20
  120.2 13.8 %collective-permute-start.24 = (bf16[64,1280]{1,0:T(8,128)(2,1)S(1)}, bf16[64,1280]{1,0:T(8,128)(2,1)S(1)}, u32[]{:S(2)}, u32[]{:S(2)}) collective-permute-start(bf16[64,1280]{1,0:T(8,128)(2,1)S(1)} %get-tuple-element.62), channel_id=1, source_target_pairs={{0,1},{1,2},{2,3},{3,0},{4,5},{5,6},{6,7},{7,4},{8,9},{9,10},{10,1... | collective-permute-start | bytes 491528 | tf_op jit(solution)/shard_map/ppermute | solution.py:20
  134.5 26.1 %copy-start.10 = (bf16[64,1280]{1,0:T(8,128)(2,1)}, bf16[64,1280]{1,0:T(8,128)(2,1)S(1)}, u32[]{:S(2)}) copy-start(bf16[64,1280]{1,0:T(8,128)(2,1)S(1)} %multiply_convert_fusion.refs_0_) | copy-start | bytes 491524
  134.5 8.9 %collective-permute-start.26 = (bf16[64,1280]{1,0:T(8,128)(2,1)S(1)}, bf16[64,1280]{1,0:T(8,128)(2,1)S(1)}, u32[]{:S(2)}, u32[]{:S(2)}) collective-permute-start(bf16[64,1280]{1,0:T(8,128)(2,1)S(1)} %multiply_convert_fusion.refs_0_), channel_id=1, source_target_pairs={{0,1},{1,2},{2,3},{3,0},{4,5},{5,6},{6,7},{7,4},{8,9},{9,10},{10,1... | collective-permute-start | bytes 491528 | tf_op jit(solution)/shard_map/ppermute | solution.py:20
  135.0 13.5 %collective-permute-start.28 = (bf16[64,1280]{1,0:T(8,128)(2,1)S(1)}, bf16[64,1280]{1,0:T(8,128)(2,1)S(1)}, u32[]{:S(2)}, u32[]{:S(2)}) collective-permute-start(bf16[64,1280]{1,0:T(8,128)(2,1)S(1)} %multiply_convert_fusion.refs_0_), channel_id=1, source_target_pairs={{0,2},{1,3},{2,0},{3,1},{4,6},{5,7},{6,4},{7,5},{8,10},{9,11},{10,... | collective-permute-start | bytes 491528 | tf_op jit(solution)/shard_map/ppermute | solution.py:20
  137.0 12.6 %collective-permute-start.30 = (bf16[64,1280]{1,0:T(8,128)(2,1)S(1)}, bf16[64,1280]{1,0:T(8,128)(2,1)S(1)}, u32[]{:S(2)}, u32[]{:S(2)}) collective-permute-start(bf16[64,1280]{1,0:T(8,128)(2,1)S(1)} %multiply_convert_fusion.refs_0_), channel_id=1, source_target_pairs={{0,3},{1,0},{2,1},{3,2},{4,7},{5,4},{6,5},{7,6},{8,11},{9,8},{10,9... | collective-permute-start | bytes 491528 | tf_op jit(solution)/shard_map/ppermute | solution.py:20
  139.8 10.7 %collective-permute-start.25 = (bf16[64,1280]{1,0:T(8,128)(2,1)S(1)}, bf16[64,1280]{1,0:T(8,128)(2,1)S(1)}, u32[]{:S(2)}, u32[]{:S(2)}) collective-permute-start(bf16[64,1280]{1,0:T(8,128)(2,1)S(1)} %multiply_convert_fusion.refs_0_), channel_id=1, source_target_pairs={{0,16},{16,0},{1,17},{17,1},{2,18},{18,2},{3,19},{19,3},{4,20},{20... | collective-permute-start | bytes 491528 | tf_op jit(solution)/shard_map/ppermute | solution.py:25
  143.4 18.1 %copy-start.28 = (bf16[64,1280]{1,0:T(8,128)(2,1)}, bf16[64,1280]{1,0:T(8,128)(2,1)S(1)}, u32[]{:S(2)}) copy-start(bf16[64,1280]{1,0:T(8,128)(2,1)S(1)} %collective-permute-done.26.refs_2_) | copy-start | bytes 491524
  143.4 7.1 %collective-permute-start.27 = (bf16[64,1280]{1,0:T(8,128)(2,1)S(1)}, bf16[64,1280]{1,0:T(8,128)(2,1)S(1)}, u32[]{:S(2)}, u32[]{:S(2)}) collective-permute-start(bf16[64,1280]{1,0:T(8,128)(2,1)S(1)} %collective-permute-done.26.refs_2_), channel_id=1, source_target_pairs={{0,16},{16,0},{1,17},{17,1},{2,18},{18,2},{3,19},{19,3},{4,20},{20... | collective-permute-start | bytes 491528 | tf_op jit(solution)/shard_map/ppermute | solution.py:25
  148.5 12.9 %copy-start.30 = (bf16[64,1280]{1,0:T(8,128)(2,1)}, bf16[64,1280]{1,0:T(8,128)(2,1)S(1)}, u32[]{:S(2)}) copy-start(bf16[64,1280]{1,0:T(8,128)(2,1)S(1)} %collective-permute-done.28.refs_4_) | copy-start | bytes 491524
  148.5 7.1 %collective-permute-start.29 = (bf16[64,1280]{1,0:T(8,128)(2,1)S(1)}, bf16[64,1280]{1,0:T(8,128)(2,1)S(1)}, u32[]{:S(2)}, u32[]{:S(2)}) collective-permute-start(bf16[64,1280]{1,0:T(8,128)(2,1)S(1)} %collective-permute-done.28.refs_4_), channel_id=1, source_target_pairs={{0,16},{16,0},{1,17},{17,1},{2,18},{18,2},{3,19},{19,3},{4,20},{20... | collective-permute-start | bytes 491528 | tf_op jit(solution)/shard_map/ppermute | solution.py:25
  149.6 11.8 %copy-start.32 = (bf16[64,1280]{1,0:T(8,128)(2,1)}, bf16[64,1280]{1,0:T(8,128)(2,1)S(1)}, u32[]{:S(2)}) copy-start(bf16[64,1280]{1,0:T(8,128)(2,1)S(1)} %collective-permute-done.30.refs_6_) | copy-start | bytes 491524
  149.6 8.4 %collective-permute-start.31 = (bf16[64,1280]{1,0:T(8,128)(2,1)S(1)}, bf16[64,1280]{1,0:T(8,128)(2,1)S(1)}, u32[]{:S(2)}, u32[]{:S(2)}) collective-permute-start(bf16[64,1280]{1,0:T(8,128)(2,1)S(1)} %collective-permute-done.30.refs_6_), channel_id=1, source_target_pairs={{0,16},{16,0},{1,17},{17,1},{2,18},{18,2},{3,19},{19,3},{4,20},{20... | collective-permute-start | bytes 491528 | tf_op jit(solution)/shard_map/ppermute | solution.py:25
  150.5 10.9 %copy-start.34 = (bf16[64,1280]{1,0:T(8,128)(2,1)}, bf16[64,1280]{1,0:T(8,128)(2,1)S(1)}, u32[]{:S(2)}) copy-start(bf16[64,1280]{1,0:T(8,128)(2,1)S(1)} %collective-permute-done.25.refs_1_) | copy-start | bytes 491524
  150.5 11.1 %copy-start.36 = (bf16[64,1280]{1,0:T(8,128)(2,1)}, bf16[64,1280]{1,0:T(8,128)(2,1)S(1)}, u32[]{:S(2)}) copy-start(bf16[64,1280]{1,0:T(8,128)(2,1)S(1)} %collective-permute-done.27.refs_3_) | copy-start | bytes 491524
  155.5 5.9 %copy-start.38 = (bf16[64,1280]{1,0:T(8,128)(2,1)}, bf16[64,1280]{1,0:T(8,128)(2,1)S(1)}, u32[]{:S(2)}) copy-start(bf16[64,1280]{1,0:T(8,128)(2,1)S(1)} %collective-permute-done.29.refs_5_) | copy-start | bytes 491524
  158.0 3.4 %copy-start.40 = (bf16[64,1280]{1,0:T(8,128)(2,1)}, bf16[64,1280]{1,0:T(8,128)(2,1)S(1)}, u32[]{:S(2)}) copy-start(bf16[64,1280]{1,0:T(8,128)(2,1)S(1)} %collective-permute-done.31.refs_7_) | copy-start | bytes 491524
  161.4 25.5 %collective-permute-start.34 = (bf16[2,160,1280]{2,1,0:T(8,128)(2,1)}, bf16[2,160,1280]{2,1,0:T(8,128)(2,1)}, u32[]{:S(2)}, u32[]{:S(2)}) collective-permute-start(bf16[2,160,1280]{2,1,0:T(8,128)(2,1)} %get-tuple-element.85), channel_id=1, source_target_pairs={{0,4},{4,0},{8,12},{12,8},{1,5},{5,1},{9,13},{13,9},{2,6},{6,2},{1... | collective-permute-start | bytes 2457608 | tf_op jit(solution)/shard_map/ppermute | solution.py:25
  161.6 1.9 copy-start.4
  163.5 1.9 copy-start.6
  165.4 0.9 copy-start.11
  166.3 1.0 copy-start.13
  167.3 1.0 copy-start.15
  168.3 1.0 copy-start.17
  169.3 1.0 copy-start.19
  171.2 0.9 copy-start.23
  172.1 0.9 copy-start.25
  173.0 0.9 copy-start.27
  175.7 0.9 copy-start.33
  176.6 0.9 copy-start.35
  180.3 6.6 %copy-start.9 = (bf16[2,160,1280]{2,1,0:T(8,128)(2,1)S(1)}, bf16[2,160,1280]{2,1,0:T(8,128)(2,1)}, u32[]{:S(2)}) copy-start(bf16[2,160,1280]{2,1,0:T(8,128)(2,1)} %copy-done.8) | copy-start | bytes 2457604
  186.4 2.8 %collective-permute-start.32 = (bf16[2,160,1280]{2,1,0:T(8,128)(2,1)S(1)}, bf16[2,160,1280]{2,1,0:T(8,128)(2,1)S(1)}, u32[]{:S(2)}, u32[]{:S(2)}) collective-permute-start(bf16[2,160,1280]{2,1,0:T(8,128)(2,1)S(1)} %get-tuple-element.83), channel_id=1, source_target_pairs={{0,4},{4,0},{8,12},{12,8},{1,5},{5,1},{9,13},{13,9},{2,6},{6,2},{1... | collective-permute-start | bytes 2457608 | tf_op jit(solution)/shard_map/ppermute | solution.py:25
  188.4 12.4 %collective-permute-start.35 = (bf16[160,1280]{1,0:T(8,128)(2,1)S(1)}, bf16[160,1280]{1,0:T(8,128)(2,1)S(1)}, u32[]{:S(2)}, u32[]{:S(2)}) collective-permute-start(bf16[160,1280]{1,0:T(8,128)(2,1)S(1)} %fusion.4), channel_id=1, source_target_pairs={{0,8},{4,12},{8,0},{12,4},{1,9},{5,13},{9,1},{13,5},{2,10},{6,14},... | collective-permute-start | bytes 1228808 | tf_op jit(solution)/shard_map/ppermute | solution.py:20
  189.5 19.2 %collective-permute-start.33 = (bf16[160,1280]{1,0:T(8,128)(2,1)S(1)}, bf16[160,1280]{1,0:T(8,128)(2,1)S(1)}, u32[]{:S(2)}, u32[]{:S(2)}) collective-permute-start(bf16[160,1280]{1,0:T(8,128)(2,1)S(1)} %fusion.3), channel_id=1, source_target_pairs={{0,8},{4,12},{8,0},{12,4},{1,9},{5,13},{9,1},{13,5},{2,10},{6,14},... | collective-permute-start | bytes 1228808 | tf_op jit(solution)/shard_map/ppermute | solution.py:20
  (14 other events, 11.3 us)

commit v6 on v4

--- a/solution.py
+++ b/solution.py
@@ -12,7 +12,7 @@
 
 
 EPS = 1e-06
-VMEM_BYTES = 16 * 1024 * 1024
+VMEM_BYTES = 8 * 1024 * 1024
 
 
 def rotated(value, axis, steps):
@@ -27,6 +27,13 @@
 
 def gather_parts(piece):
     return [piece] + [rotated(piece, "tp", k) for k in range(1, lax.axis_size("tp"))]
+
+
+def to_second(value, steps):
+    count = lax.axis_size("tp")
+    return lax.ppermute(
+        value, ("sec", "tp"), [(i, count + (i + steps) % count) for i in range(count)]
+    )
 
 
 def reduce_parts(parts):
@@ -39,15 +46,6 @@
 def quarter(weight, place):
     rows = weight.shape[0] // 4
     return lax.dynamic_slice_in_dim(weight, place * rows, rows, 0)
-
-
-def assembled(got, across, place):
-    pieces = (got, swapped(got, "dp", 1), across, swapped(across, "dp", 1))
-    rows, columns = got.shape
-    full = jnp.zeros((4 * rows, columns), got.dtype)
-    for q, piece in enumerate(pieces):
-        full = lax.dynamic_update_slice_in_dim(full, piece, (place ^ q) * rows, 0)
-    return full
 
 
 def gelu_pair(value):
@@ -116,9 +114,21 @@
         work(*other)
 
 
+def assemble_body(sel_ref, p0, p1, p2, p3, out):
+    rows = p0.shape[0]
+    for q, piece in enumerate((p0, p1, p2, p3)):
+        out[pl.ds(pl.multiple_of((sel_ref[2] ^ q) * rows, rows), rows), :] = piece[...]
+
+
+def assembled(got, across, sel):
+    pieces = [got, swapped(got, "dp", 1), across, swapped(across, "dp", 1)]
+    out = bf16(4 * got.shape[0], got.shape[1])
+    return run(assemble_body, "assemble", sel, pieces, [out], [], 0)[0]
+
+
 def partial_body(count, sel_ref, *refs):
     parts, (gain, w_in, w_out) = refs[:count], refs[count : count + 3]
-    outs, (xn, acc) = refs[count + 3 : 2 * count + 3], refs[2 * count + 3 :]
+    outs, (xn, acc) = refs[count + 3 : -2], refs[-2:]
     rows = parts[0].shape[0]
     for i, part in enumerate(parts):
         xn[i * rows : (i + 1) * rows, :] = normed(part[...].astype(jnp.float32), gain[...])
@@ -126,19 +136,20 @@
         act, unused = gelu_pair(dot_nn(xn[...], w_in[:, tile]))
         term = dot_nt(act.astype(jnp.bfloat16), w_out[:, tile])
         acc[...] = term if t == 0 else acc[...] + term
+    late = rows // 2
     for i, out in enumerate(outs):
-        out[...] = acc[i * rows : (i + 1) * rows, :].astype(jnp.bfloat16)
+        out[...] = acc[i * late : (i + 1) * late, :].astype(jnp.bfloat16)
 
 
 def block0_partials(parts, gain, w_in, w_out, sel):
     rows, width = parts[0].shape
     hidden, n = w_in.shape[1], len(parts)
-    return run(
+    outs = run(
         functools.partial(partial_body, n),
         "block0_partial",
         sel,
         [*parts, gain, w_in, w_out],
-        [bf16(rows, width)] * n,
+        [bf16(rows // 2, width)] * (2 * n),
         [
             pltpu.VMEM((n * rows, width), jnp.bfloat16),
             pltpu.VMEM((n * rows, width), jnp.float32),
@@ -146,18 +157,23 @@
         4 * n * rows * width * hidden,
         n * rows * hidden,
     )
-
-
-def state_body(sel_ref, part, gain, own, other, act, slope, xn_cols, xn):
-    rows = part.shape[0]
+    return [(outs[2 * i], outs[2 * i + 1]) for i in range(n)]
+
+
+def state_body(count, sel_ref, *refs):
+    parts = refs[:count]
+    gain, own, other, act, slope, xn_cols, xn = refs[count:]
+    rows = parts[0].shape[0]
     late = rows // 2
     share = xn_cols.shape[0]
     mine = pl.multiple_of((1 - sel_ref[0]) * late, late)
     theirs = pl.multiple_of(sel_ref[0] * late, late)
-    for i, start in enumerate((mine, theirs)):
-        xn[i * late : (i + 1) * late, :] = normed(
-            part[pl.ds(start, late), :].astype(jnp.float32), gain[...]
-        )
+    for i, part in enumerate(parts):
+        for j, start in enumerate((mine, theirs)):
+            at = i * rows + j * late
+            xn[at : at + late, :] = normed(
+                part[pl.ds(start, late), :].astype(jnp.float32), gain[...]
+            )
     cols = xn[:, pl.ds(pl.multiple_of(sel_ref[0] * share, share), share)]
     xn_cols[...] = cols.T
 
@@ -170,18 +186,18 @@
     by_section(sel_ref, 0, work, (own,), (other,))
 
 
-def block0_state(part, gain, own, other, sel):
-    rows, width = part.shape
+def block0_state(parts, gain, own, other, sel):
+    total, width = sum(part.shape[0] for part in parts), parts[0].shape[1]
     hidden = own.shape[1]
     return run(
-        state_body,
+        functools.partial(state_body, len(parts)),
         "block0_state",
         sel,
-        [part, gain, own, other],
-        [bf16(rows, hidden), bf16(rows, hidden), bf16(width // 2, rows)],
-        [pltpu.VMEM((rows, width), jnp.bfloat16)],
-        2 * rows * width * hidden,
-        2 * rows * hidden,
+        [*parts, gain, own, other],
+        [bf16(total, hidden), bf16(total, hidden), bf16(width // 2, total)],
+        [pltpu.VMEM((total, width), jnp.bfloat16)],
+        2 * total * width * hidden,
+        2 * total * hidden,
     )
 
 
@@ -280,78 +296,45 @@
         away[g, :, tile] = jnp.where(core == 0, odd, even).astype(jnp.bfloat16)
 
 
-def grad_out_body(count, sel_ref, *refs):
-    pieces, acts = refs[: 2 * count], refs[2 * count : 3 * count]
-    keep, away, turned, state = refs[3 * count :]
+def gradient_body(count, sel_ref, *refs):
+    pieces = refs[:count]
+    act, slope, xn_cols, own, other = refs[count : count + 5]
+    out_keep, out_away, in_keep, in_away, g_all, turned = refs[count + 5 :]
+    rows = pieces[0].shape[0]
     share = turned.shape[0]
-    rows = acts[0].shape[0]
-    start = pl.multiple_of(sel_ref[0] * share, share)
-    cols = jnp.concatenate([piece[:, pl.ds(start, share)] for piece in pieces], axis=0)
-    turned[...] = cols.T
-    for i, part in enumerate(acts):
-        state[i * rows : (i + 1) * rows, :] = part[...]
-    for tile in tiles(state.shape[1]):
-        put_rows(dot_nn(turned[...], state[:, tile]), sel_ref[1], keep, away, tile)
-
-
-def grad_in_body(count, sel_ref, *refs):
-    pieces, slopes = refs[: 2 * count], refs[2 * count : 3 * count]
-    xn_cols = refs[3 * count : 4 * count]
-    own, other, keep, away, g_all, turned = refs[4 * count :]
-    rows = pieces[0].shape[0]
-    wide = xn_cols[0].shape[1]
+    core = sel_ref[1]
     for i, piece in enumerate(pieces):
         g_all[i * rows : (i + 1) * rows, :] = piece[...]
-    for i, part in enumerate(xn_cols):
-        turned[:, i * wide : (i + 1) * wide] = part[...]
+    cols = g_all[:, pl.ds(pl.multiple_of(sel_ref[0] * share, share), share)]
+    turned[...] = cols.T
 
     def work(weight):
         for tile in tiles(weight.shape[1]):
+            put_rows(dot_nn(turned[...], act[:, tile]), core, out_keep, out_away, tile)
             g_h = dot_nn(g_all[...], weight[:, tile])
-            slope = jnp.concatenate([part[:, tile] for part in slopes], axis=0)
-            g_hidden = (g_h * slope.astype(jnp.float32)).astype(jnp.bfloat16)
-            put_rows(dot_nn(turned[...], g_hidden), sel_ref[1], keep, away, tile)
+            g_hidden = (g_h * slope[:, tile].astype(jnp.float32)).astype(jnp.bfloat16)
+            put_rows(dot_nn(xn_cols[...], g_hidden), core, in_keep, in_away, tile)
 
     by_section(sel_ref, 0, work, (own,), (other,))
 
 
-def gradient_outs(width, hidden):
+def gradients(pieces, states, own, other, sel):
+    rows, width = pieces[0].shape
+    total, hidden = rows * len(pieces), own.shape[1]
     groups = lax.axis_size("dp") // 2
-    return [bf16(groups, width // 2 // (2 * groups), hidden)] * 2
-
-
-def grad_out_parts(pieces, acts, sel):
-    rows, width = pieces[0].shape
-    total, hidden = rows * len(pieces), acts[0].shape[1]
-    return run(
-        functools.partial(grad_out_body, len(acts)),
-        "grad_out",
+    outs = run(
+        functools.partial(gradient_body, len(pieces)),
+        "gradients",
         sel,
-        [*pieces, *acts],
-        gradient_outs(width, hidden),
-        [
-            pltpu.VMEM((width // 2, total), jnp.bfloat16),
-            pltpu.VMEM((total, hidden), jnp.bfloat16),
-        ],
-        total * width * hidden,
-    )
-
-
-def grad_in_parts(pieces, slopes, xn_cols, own, other, sel):
-    rows, width = pieces[0].shape
-    total, hidden = rows * len(pieces), slopes[0].shape[1]
-    return run(
-        functools.partial(grad_in_body, len(slopes)),
-        "grad_in",
-        sel,
-        [*pieces, *slopes, *xn_cols, own, other],
-        gradient_outs(width, hidden),
+        [*pieces, *states, own, other],
+        [bf16(groups, width // 2 // (2 * groups), hidden)] * 4,
         [
             pltpu.VMEM((total, width), jnp.bfloat16),
             pltpu.VMEM((width // 2, total), jnp.bfloat16),
         ],
-        3 * total * width * hidden,
-    )
+        4 * total * width * hidden,
+    )
+    return outs[:2], outs[2:]
 
 
 def sum_over_dp(keep, away):
@@ -382,46 +365,50 @@
     place = lax.axis_index("dp") % 4
     sel = jnp.stack([segment, core, place]).astype(jnp.int32)
     own = (w_in[0], w_out[0])
-    theta = math.pi / 2.0 * (timesteps.astype(jnp.float32) + 1.0) / (STEPS + 1.0)
+
+    def my_half(value):
+        return jnp.where(first, value[half:], value[:half])
+
+    theta = math.pi / 2.0 * (my_half(timesteps).astype(jnp.float32) + 1.0) / (STEPS + 1.0)
     alpha = jnp.cos(theta)[:, None, None]
     sigma = jnp.sin(theta)[:, None, None]
 
     flat = latents.reshape(count * tokens, width)
+    lat_parts = gather_parts(flat)
     got_in = swapped(quarter(own[0], place), "sec", 1)
-    lat_parts = gather_parts(flat)
-    got_out = swapped(quarter(own[1], place), "sec", 1)
+    out_quarter, lat_parts[1], lat_parts[-1] = lax.optimization_barrier(
+        (quarter(own[1], place), lat_parts[1], lat_parts[-1])
+    )
     across_in = swapped(got_in, "dp", 2)
+    got_out = lax.ppermute(out_quarter, "sec", [(1, 0)])
     across_out = swapped(got_out, "dp", 2)
 
     onehot = (
-        prompt_ids[:, None] == jnp.arange(prompt_table.shape[0], dtype=jnp.int32)[None, :]
+        my_half(prompt_ids)[:, None] == jnp.arange(prompt_table.shape[0], dtype=jnp.int32)[None, :]
     ).astype(jnp.bfloat16)
-    text = dot_nn(onehot, prompt_table)
-    text_mine = jnp.where(first, text[half:], text[:half])
+    text_mine = dot_nn(onehot, prompt_table)
 
     near = [k for k in range(1, n_tp) if 2 * k != n_tp]
     far = [k for k in range(1, n_tp) if 2 * k == n_tp]
     eps_parts = [None] * n_tp
-    arrivals = ([], [got_in], [got_out, across_in])
-    for ks, arrived in zip(([0], near, far), arrivals):
+    results = []
+    for ks, hop in ((near, got_in), ([0], None), (far, None)):
         if ks:
-            operands, unused = lax.optimization_barrier(([lat_parts[k] for k in ks], arrived))
+            operands, unused = lax.optimization_barrier(
+                ([lat_parts[k] for k in ks], (hop, results))
+            )
             results = block0_partials(operands, gains[:1], *own, sel)
             for k, result in zip(ks, results):
                 eps_parts[k] = result
-    eps_mix, across_out = lax.optimization_barrier((reduce_parts(eps_parts), across_out))
-    eps_mix = eps_mix.reshape(count, tokens, width)
-    other = (assembled(got_in, across_in, place), assembled(got_out, across_out, place))
-    base = latents.astype(jnp.float32)
-    images = ((base - sigma * (base + eps_mix)) / alpha).astype(jnp.bfloat16)
-
-    arrived = lax.ppermute(images[:half], "sec", [(0, 1)])
-    mine = jnp.where(first, images[half:], arrived)
-    ratio = jnp.where(first, (sigma / alpha)[half:], (sigma / alpha)[:half])
+    stay = reduce_parts([part[1] for part in eps_parts])
+    leave = [to_second(part[0], -k).astype(jnp.float32) for k, part in enumerate(eps_parts)]
+    eps_mix = jnp.where(first, stay, sum(leave)).reshape(half, tokens, width)
+    base = my_half(latents).astype(jnp.float32)
+    mine = ((base - sigma * (base + eps_mix)) / alpha).astype(jnp.bfloat16)
     mine_rows = mine.reshape(half * tokens, width)
+
+    other = (assembled(got_in, across_in, sel), assembled(got_out, across_out, sel))
     seen_parts = gather_parts(mine_rows)
-
-    states = [block0_state(part, gains[:1], own[0], other[0], sel) for part in lat_parts]
     slopes1, pool_parts = [None] * n_tp, [None] * n_tp
     for ks in ([0] + near, far):
         if ks:
@@ -450,7 +437,15 @@
     padded = -(-n_tp * half // 16) * 16
     g_tok = jnp.pad(g_mean.astype(jnp.bfloat16), ((0, padded - n_tp * half), (0, 0)))
     g_parts = reward_back(g_tok, slopes1, tokens, own, other, sel)
-    g_xn, unused = lax.optimization_barrier((reduce_parts(g_parts), states))
+
+    states = block0_state(lat_parts, gains[:1], own[0], other[0], sel)
+    late_quarter, unused = lax.optimization_barrier((out_quarter, mine_rows))
+    got_late = lax.ppermute(late_quarter, "sec", [(0, 1)])
+
+    g_xn, states, got_late = lax.optimization_barrier(
+        (reduce_parts(g_parts), states, got_late)
+    )
+    across_late = swapped(got_late, "dp", 2)
     seen = mine_rows.astype(jnp.float32)
     scale1 = lax.rsqrt(jnp.mean(seen * seen, axis=-1, keepdims=True) + EPS)
     weighted = gains[1] * g_xn
@@ -458,15 +453,13 @@
         seen * weighted, axis=-1, keepdims=True
     )
     g_images = (g_mean[:half, None, :] + g_norm.reshape(half, tokens, width)).astype(jnp.bfloat16)
-    g_eps = (-ratio * g_images.astype(jnp.float32)).astype(jnp.bfloat16)
+    g_eps = (-(sigma / alpha) * g_images.astype(jnp.float32)).astype(jnp.bfloat16)
 
     pieces = []
     for part in gather_parts(g_eps.reshape(half * tokens, width)):
         pieces += [part, swapped(part, "sec", 1)]
-    out_parts = grad_out_parts(pieces, [state[0] for state in states], sel)
-    slopes0, xn_cols = [state[1] for state in states], [state[2] for state in states]
-    out_parts, slopes0 = lax.optimization_barrier((out_parts, slopes0))
-    in_parts = grad_in_parts(pieces, slopes0, xn_cols, own[1], other[1], sel)
+    other_out = assembled(got_late, across_late, sel)
+    out_parts, in_parts = gradients(pieces, states, own[1], other_out, sel)
     grad_out, grad_in = sum_over_dp(*out_parts), sum_over_dp(*in_parts)
     return (grad_in, grad_out)
 

time: 226 us -> 223 us (0.987)
  local copies, waits for them, and re-layouts: 32.5 us -> 15.1 us
  starting transfers between devices: 43.8 us -> 57.1 us
  Pallas kernels: 34.3 us -> 31.7 us
    ppermute x1 -> x6, starting transfers between devices: 3.43 us -> 23.2 us  [the longest x4 16.8 us: to_second(): lax.ppermute(value, ('sec', 'tp'), [(i, count + (i + steps) % count) for...]
    ppermute x20, waiting for transfers between devices: 61.7 us -> 78.3 us  [rotated(): lax.ppermute(value, axis, [(i, (i + steps) % count) for i in range(count)])]
    unnamed x92 -> x46, local copies, waits for them, and re-layouts: 24 us -> 9.15 us
    ppermute x14 -> x16, waiting for transfers between devices: 39.5 us -> 28.2 us  [swapped(): return lax.ppermute(value, axis, [(i, i ^ bit) for i in range(count)])]
    ppermute x1 -> x6, waiting for transfers between devices: 4.01 us -> 0.02 us  [the longest x4 0.01 us: to_second(): lax.ppermute(value, ('sec', 'tp'), [(i, count + (i + steps) % count) for...]
    ppermute x14 -> x16, starting transfers between devices: 13.3 us -> 9.75 us  [swapped(): return lax.ppermute(value, axis, [(i, i ^ bit) for i in range(count)])]
    dynamic_update_slice x8 -> x0, local copies, waits for them, and re-layouts: 2.98 us -> none  [assembled(): full = lax.dynamic_update_slice_in_dim(full, piece, (place ^ q) * rows, 0)]
    ppermute x20, starting transfers between devices: 27.1 us -> 24.2 us  [rotated(): lax.ppermute(value, axis, [(i, (i + steps) % count) for i in range(count)])]
  transfers between devices with their start and end apart: 35 -> 42, of which waited for: 17 -> 20; matrix products, arithmetic and copies ran while one was open for 5% -> 4% of each run, Pallas kernels for 10% -> 12%
where the time goes in v6:
time: 223 us; the launch traced here: 221 us
  waiting for transfers between devices  107 us (48%)
  starting transfers between devices  57.1 us (26%)
  Pallas kernels  31.7 us (14%)
  local copies, waits for them, and re-layouts  15.1 us (7%)
  other arithmetic  6.47 us (3%)
  between operations  3.93 us (2%)
    ppermute x20, waiting for transfers between devices, rotated(): lax.ppermute(value, axis, [(i, (i + steps) % count) for i in range(count)])  78.3 us
    pallas_call x11, Pallas kernels, run(): pl.pallas_call(body, in_specs=[IN_SMEM] + [IN_VMEM] * len(operands), out_...  31.7 us
    ppermute x16, waiting for transfers between devices, swapped(): return lax.ppermute(value, axis, [(i, i ^ bit) for i in range(count)])  28.2 us
    ppermute x20, starting transfers between devices, rotated(): lax.ppermute(value, axis, [(i, (i + steps) % count) for i in range(count)])  24.2 us
    ppermute x4, starting transfers between devices, to_second(): lax.ppermute(value, ('sec', 'tp'), [(i, count + (i + steps) % count) for...  16.8 us
    ppermute x16, starting transfers between devices, swapped(): return lax.ppermute(value, axis, [(i, i ^ bit) for i in range(count)])  9.75 us
    unnamed x46, local copies, waits for them, and re-layouts  9.15 us
    ppermute x1, starting transfers between devices, on_device(): got_late = lax.ppermute(late_quarter, 'sec', [(0, 1)])  5.1 us
  transfers between devices with their start and end apart: 42, of which 20 were waited for; matrix products, arithmetic and copies ran while one was open for 4% of the time, Pallas kernels for 12%

profile of v6, /device:TPU:0, one launch (start us, length us, event | category | flops | bytes accessed | tf_op | source)
XLA Modules:
  0.0 220.9 jit_solution(7935769975063948912)
XLA Ops:
  0.7 2.2 %dynamic-slice_bitcast_fusion = bf16[320,1280]{1,0:T(8,128)(2,1)} fusion(bf16[1,1280,1280]{2,1,0:T(8,128)(2,1)} %param.12, s32[]{:T(128)S(6)} %select_n.72), kind=kLoop, calls=%fused_computation.6 | loop fusion | bytes 1638404 | tf_op jit(solution)/shard_map/dynamic_slice | solution.py:48
  2.9 3.0 %collective-permute-start.2 = (bf16[320,1280]{1,0:T(8,128)(2,1)}, bf16[320,1280]{1,0:T(8,128)(2,1)}, u32[]{:S(2)}, u32[]{:S(2)}) collective-permute-start(bf16[320,1280]{1,0:T(8,128)(2,1)} %dynamic-slice_bitcast_fusion), channel_id=1, source_target_pairs={{0,16},{16,0},{1,17},{17,1},{2,18},{18,2},{3,19},{19,3},{4,20},{20... | collective-permute-start | bytes 2457608 | tf_op jit(solution)/shard_map/ppermute | solution.py:25
  5.9 1.6 collective-permute-start
  7.5 2.2 %collective-permute-start.1 = (bf16[128,1280]{1,0:T(8,128)(2,1)}, bf16[128,1280]{1,0:T(8,128)(2,1)S(1)}, u32[]{:S(2)}, u32[]{:S(2)}) collective-permute-start(bf16[128,1280]{1,0:T(8,128)(2,1)} %bitcast.51), channel_id=1, source_target_pairs={{0,3},{1,0},{2,1},{3,2},{4,7},{5,4},{6,5},{7,6},{8,11},{9,8},{10,9... | collective-permute-start | bytes 983048 | tf_op jit(solution)/shard_map/ppermute | solution.py:20
  9.7 2.1 dynamic-slice_bitcast_fusion.1
  11.8 6.8 %collective-permute-done.refs_0_.refs_1_ = bf16[128,1280]{1,0:T(8,128)(2,1)S(1)} collective-permute-done((bf16[128,1280]{1,0:T(8,128)(2,1)}, bf16[128,1280]{1,0:T(8,128)(2,1)S(1)}, u32[]{:S(2)}, u32[]{:S(2)}) %collective-permute-start) | collective-permute-done | bytes 327712 | tf_op jit(solution)/shard_map/ppermute | solution.py:20
  18.6 0.7 copy-done.6
  19.3 4.3 %collective-permute-done.1.refs_1_.refs_3_ = bf16[128,1280]{1,0:T(8,128)(2,1)S(1)} collective-permute-done((bf16[128,1280]{1,0:T(8,128)(2,1)}, bf16[128,1280]{1,0:T(8,128)(2,1)S(1)}, u32[]{:S(2)}, u32[]{:S(2)}) %collective-permute-start.1) | collective-permute-done | bytes 327712 | tf_op jit(solution)/shard_map/ppermute | solution.py:20
  23.6 0.7 copy-done.9
  24.3 1.3 collective-permute-start.16
  25.6 2.1 collective-permute-start.4
  27.8 1.9 copy-done.2
  29.8 1.0 copy-done.7
  30.7 1.0 copy-done.10
  31.7 3.6 %block0_partial.3 = (bf16[64,1280]{1,0:T(8,128)(2,1)}, bf16[64,1280]{1,0:T(8,128)(2,1)}, bf16[64,1280]{1,0:T(8,128)(2,1)S(1)}, bf16[64,1280]{1,0:T(8,128)(2,1)}) custom-call(s32[3]{0:T(128)S(1)} %pad_add_fusion.sel_ref, bf16[128,1280]{1,0:T(8,128)(2,1)S(1)} %copy-done.7, bf16[128,1280]{1,0:T(8,128)(2,1)S(1)} %copy-done.10, ...), custom_call_target="tpu_custom_call" | custom-call | flops 1677721600 | bytes 7869440 | tf_op jit(solution)/shard_map/block0_partial/pallas_call | solution.py:84
  35.3 2.7 %block0_partial.4 = (bf16[64,1280]{1,0:T(8,128)(2,1)S(1)}, bf16[64,1280]{1,0:T(8,128)(2,1)S(1)}) custom-call(s32[3]{0:T(128)S(1)} %pad_add_fusion.sel_ref, bf16[128,1280]{1,0:T(8,128)(2,1)S(1)} %bitcast.53, f32[1,1280]{1,0:T(1,128)S(1)} %get-tuple-element.95.refs_2_.refs_1_.refs_4_, bf16[1280,1280]{1,0:T(8,128)(2,1)S(1)} %bitcast.37, ...), custom_call_target="tpu_custom_call" | custom-call | flops 838860800 | bytes 7214080 | tf_op jit(solution)/shard_map/block0_partial/pallas_call | solution.py:84
  38.7 4.4 %collective-permute-done.4.refs_0_.refs_2_ = bf16[128,1280]{1,0:T(8,128)(2,1)} collective-permute-done((bf16[128,1280]{1,0:T(8,128)(2,1)}, bf16[128,1280]{1,0:T(8,128)(2,1)}, u32[]{:S(2)}, u32[]{:S(2)}) %collective-permute-start.4) | collective-permute-done | bytes 327712 | tf_op jit(solution)/shard_map/ppermute | solution.py:20
  43.0 3.1 %block0_partial.5 = (bf16[64,1280]{1,0:T(8,128)(2,1)S(1)}, bf16[64,1280]{1,0:T(8,128)(2,1)S(1)}) custom-call(s32[3]{0:T(128)S(1)} %pad_add_fusion.sel_ref, bf16[128,1280]{1,0:T(8,128)(2,1)} %collective-permute-done.4.refs_0_.refs_2_, f32[1,1280]{1,0:T(1,128)S(1)} %get-tuple-element.95.refs_2_.refs_1_.refs_4_, bf16[1280,1280]{1,0:T(8,128)(2,1)S(1)} %bitcast.38, ...), custom_call_target="tpu_custom_call" | custom-call | flops 838860800 | bytes 7214080 | tf_op jit(solution)/shard_map/block0_partial/pallas_call | solution.py:84
  46.3 7.4 %collective-permute-start.9 = (bf16[64,1280]{1,0:T(8,128)(2,1)S(1)}, bf16[64,1280]{1,0:T(8,128)(2,1)S(1)}, u32[]{:S(2)}, u32[]{:S(2)}) collective-permute-start(bf16[64,1280]{1,0:T(8,128)(2,1)S(1)} %get-tuple-element.53), channel_id=1, source_target_pairs={{0,18},{1,19},{2,16},{3,17},{4,22},{5,23},{6,20},{7,21},{8,26},{9,... | collective-permute-start | bytes 491528 | tf_op jit(solution)/shard_map/ppermute | solution.py:34
  53.7 1.3 collective-permute-start.7
  55.0 1.3 collective-permute-start.10
  56.3 6.3 %collective-permute-done.5 = bf16[64,1280]{1,0:T(8,128)(2,1)S(1)} collective-permute-done((bf16[64,1280]{1,0:T(8,128)(2,1)S(1)}, bf16[64,1280]{1,0:T(8,128)(2,1)S(1)}, u32[]{:S(2)}, u32[]{:S(2)}) %collective-permute-start.5) | collective-permute-done | bytes 163872 | tf_op jit(solution)/shard_map/ppermute | solution.py:20
  62.7 1.5 collective-permute-start.14
  64.7 2.0 collective-permute-start.6
  66.8 0.7 copy-done.19
  67.4 6.7 %collective-permute-start.8 = (bf16[64,1280]{1,0:T(8,128)(2,1)}, bf16[64,1280]{1,0:T(8,128)(2,1)}, u32[]{:S(2)}, u32[]{:S(2)}) collective-permute-start(bf16[64,1280]{1,0:T(8,128)(2,1)} %get-tuple-element.44), channel_id=1, source_target_pairs={{0,19},{1,16},{2,17},{3,18},{4,23},{5,20},{6,21},{7,22},{8,27},{9,... | collective-permute-start | bytes 491528 | tf_op jit(solution)/shard_map/ppermute | solution.py:34
  78.2 1.8 convert_reduce_fusion.3
  80.6 12.1 %collective-permute-done.20.refs_0_ = bf16[64,1280]{1,0:T(8,128)(2,1)S(1)} collective-permute-done((bf16[64,1280]{1,0:T(8,128)(2,1)S(1)}, bf16[64,1280]{1,0:T(8,128)(2,1)S(1)}, u32[]{:S(2)}, u32[]{:S(2)}) %collective-permute-start.20) | collective-permute-done | bytes 163872 | tf_op jit(solution)/shard_map/ppermute | solution.py:20
  93.5 1.7 collective-permute-start.12
  95.4 4.8 %collective-permute-done.12.refs_2_ = bf16[64,1280]{1,0:T(8,128)(2,1)S(1)} collective-permute-done((bf16[64,1280]{1,0:T(8,128)(2,1)S(1)}, bf16[64,1280]{1,0:T(8,128)(2,1)S(1)}, u32[]{:S(2)}, u32[]{:S(2)}) %collective-permute-start.12) | collective-permute-done | bytes 163872 | tf_op jit(solution)/shard_map/ppermute | solution.py:20
  100.2 5.1 %collective-permute-start.27 = (bf16[320,1280]{1,0:T(8,128)(2,1)}, bf16[320,1280]{1,0:T(8,128)(2,1)S(1)}, u32[]{:S(2)}, u32[]{:S(2)}) collective-permute-start(bf16[320,1280]{1,0:T(8,128)(2,1)} %dynamic-slice_bitcast_fusion.1), channel_id=1, source_target_pairs={{0,16},{1,17},{2,18},{3,19},{4,20},{5,21},{6,22},{7,23},{8,24},{9,... | collective-permute-start | bytes 2457608 | tf_op jit(solution)/shard_map/ppermute | solution.py:443
  105.4 1.6 assemble.3.refs_6_.refs_4_.refs_7_
  107.1 1.8 assemble.4.refs_7_.refs_5_.refs_8_
  109.5 3.4 %reward_forward.2 = (bf16[64,1280]{1,0:T(8,128)(2,1)S(1)}, bf16[64,1280]{1,0:T(8,128)(2,1)S(1)}, bf16[64,1280]{1,0:T(8,128)(2,1)S(1)}, f32[8,1280]{1,0:T(8,128)S(1)}) custom-call(s32[3]{0:T(128)S(1)} %pad_add_fusion.sel_ref, bf16[64,1280]{1,0:T(8,128)(2,1)S(1)} %bitcast.58, bf16[64,1280]{1,0:T(8,128)(2,1)S(1)} %collective-permute-done.11.refs_1_, ...), custom_call_target="tpu_custom_call" | custom-call | flops 629145600 | bytes 14136320 | tf_op jit(solution)/shard_map/reward_forward/pallas_call | solution.py:84
  112.9 2.9 %reward_forward.3 = (bf16[64,1280]{1,0:T(8,128)(2,1)S(1)}, f32[8,1280]{1,0:T(8,128)S(1)}) custom-call(s32[3]{0:T(128)S(1)} %pad_add_fusion.sel_ref, bf16[64,1280]{1,0:T(8,128)(2,1)S(1)} %collective-permute-done.20.refs_0_, f32[1,1280]{1,0:T(1,128)S(1)} %get-tuple-element.94.refs_3_.refs_1_, bf16[1280,1280]{1,0:T(8,128)(2,1)S(1)} %bitcast.40, ...), custom_call_target="tpu_custom_call" | custom-call | flops 209715200 | bytes 13480960 | tf_op jit(solution)/shard_map/reward_forward/pallas_call | solution.py:84
  116.0 3.8 %collective-permute-start.23 = (f32[5,1280]{1,0:T(8,128)S(1)}, f32[5,1280]{1,0:T(8,128)S(1)}, u32[]{:S(2)}, u32[]{:S(2)}) collective-permute-start(f32[5,1280]{1,0:T(8,128)S(1)} %pad_maximum_fusion), channel_id=1, source_target_pairs={{0,3},{1,0},{2,1},{3,2},{4,7},{5,4},{6,5},{7,6},{8,11},{9,8},{10,9... | collective-permute-start | bytes 76808 | tf_op jit(solution)/shard_map/ppermute | solution.py:20
  119.9 2.3 %collective-permute-done.21 = f32[5,1280]{1,0:T(8,128)S(1)} collective-permute-done((f32[5,1280]{1,0:T(8,128)S(1)}, f32[5,1280]{1,0:T(8,128)S(1)}, u32[]{:S(2)}, u32[]{:S(2)}) %collective-permute-start.21) | collective-permute-done | bytes 25632 | tf_op jit(solution)/shard_map/ppermute | solution.py:20
  122.2 2.6 %collective-permute-done.22 = f32[5,1280]{1,0:T(8,128)S(1)} collective-permute-done((f32[5,1280]{1,0:T(8,128)S(1)}, f32[5,1280]{1,0:T(8,128)S(1)}, u32[]{:S(2)}, u32[]{:S(2)}) %collective-permute-start.22) | collective-permute-done | bytes 25632 | tf_op jit(solution)/shard_map/ppermute | solution.py:20
  125.3 2.7 %reward_back.1 = (bf16[64,1280]{1,0:T(8,128)(2,1)S(1)}, bf16[64,1280]{1,0:T(8,128)(2,1)S(1)}, bf16[64,1280]{1,0:T(8,128)(2,1)S(1)}, bf16[64,1280]{1,0:T(8,128)(2,1)S(1)}) custom-call(s32[3]{0:T(128)S(1)} %pad_add_fusion.sel_ref, bf16[16,1280]{1,0:T(8,128)(2,1)S(1)} %pad.4.refs_0_, bf16[64,1280]{1,0:T(8,128)(2,1)S(1)} %get-tuple-element.57.refs_1_, ...), custom_call_target="tpu_custom_call" | custom-call | flops 838860800 | bytes 14458880 | tf_op jit(solution)/shard_map/reward_back/pallas_call | solution.py:84
  128.0 1.8 collective-permute-start.24
  129.8 0.7 collective-permute-start.26
  130.6 4.3 %block0_state.1 = (bf16[512,1280]{1,0:T(8,128)(2,1)S(1)}, bf16[512,1280]{1,0:T(8,128)(2,1)S(1)}, bf16[640,512]{1,0:T(8,128)(2,1)S(1)}) custom-call(s32[3]{0:T(128)S(1)} %pad_add_fusion.sel_ref, bf16[128,1280]{1,0:T(8,128)(2,1)S(1)} %bitcast.54, bf16[128,1280]{1,0:T(8,128)(2,1)S(1)} %copy-done.8, bf16[128,1280]{1,0:T(8,128)(2,1)} %collective-permute-done.4.refs_0_.refs_2_, ...), custom_call_target="tpu_custom_call" | custom-call | flops 1677721600 | bytes 11146240 | tf_op jit(solution)/shard_map/block0_state/pallas_call | solution.py:84
  135.2 7.3 %collective-permute-done.25 = bf16[64,1280]{1,0:T(8,128)(2,1)S(1)} collective-permute-done((bf16[64,1280]{1,0:T(8,128)(2,1)S(1)}, bf16[64,1280]{1,0:T(8,128)(2,1)S(1)}, u32[]{:S(2)}, u32[]{:S(2)}) %collective-permute-start.25) | collective-permute-done | bytes 163872 | tf_op jit(solution)/shard_map/ppermute | solution.py:20
  142.7 1.6 collective-permute-start.36
  144.6 17.1 %collective-permute-done.36.p2 = bf16[320,1280]{1,0:T(8,128)(2,1)S(1)} collective-permute-done((bf16[320,1280]{1,0:T(8,128)(2,1)S(1)}, bf16[320,1280]{1,0:T(8,128)(2,1)S(1)}, u32[]{:S(2)}, u32[]{:S(2)}) %collective-permute-start.36) | collective-permute-done | bytes 819232 | tf_op jit(solution)/shard_map/ppermute | solution.py:25
  162.3 2.0 collective-permute-start.31
  164.3 2.8 %collective-permute-start.33 = (bf16[64,1280]{1,0:T(8,128)(2,1)S(1)}, bf16[64,1280]{1,0:T(8,128)(2,1)S(1)}, u32[]{:S(2)}, u32[]{:S(2)}) collective-permute-start(bf16[64,1280]{1,0:T(8,128)(2,1)S(1)} %multiply_convert_fusion.refs_0_), channel_id=1, source_target_pairs={{0,3},{1,0},{2,1},{3,2},{4,7},{5,4},{6,5},{7,6},{8,11},{9,8},{10,9... | collective-permute-start | bytes 491528 | tf_op jit(solution)/shard_map/ppermute | solution.py:20
  167.2 3.6 %collective-permute-done.29.refs_2_ = bf16[64,1280]{1,0:T(8,128)(2,1)S(1)} collective-permute-done((bf16[64,1280]{1,0:T(8,128)(2,1)S(1)}, bf16[64,1280]{1,0:T(8,128)(2,1)S(1)}, u32[]{:S(2)}, u32[]{:S(2)}) %collective-permute-start.29) | collective-permute-done | bytes 163872 | tf_op jit(solution)/shard_map/ppermute | solution.py:20
  170.8 6.5 %collective-permute-done.31.refs_4_ = bf16[64,1280]{1,0:T(8,128)(2,1)S(1)} collective-permute-done((bf16[64,1280]{1,0:T(8,128)(2,1)S(1)}, bf16[64,1280]{1,0:T(8,128)(2,1)S(1)}, u32[]{:S(2)}, u32[]{:S(2)}) %collective-permute-start.31) | collective-permute-done | bytes 163872 | tf_op jit(solution)/shard_map/ppermute | solution.py:20
  177.3 2.0 collective-permute-start.32
  179.4 0.8 assemble.5.refs_12_
  180.2 4.3 %collective-permute-done.30.refs_3_ = bf16[64,1280]{1,0:T(8,128)(2,1)S(1)} collective-permute-done((bf16[64,1280]{1,0:T(8,128)(2,1)S(1)}, bf16[64,1280]{1,0:T(8,128)(2,1)S(1)}, u32[]{:S(2)}, u32[]{:S(2)}) %collective-permute-start.30) | collective-permute-done | bytes 163872 | tf_op jit(solution)/shard_map/ppermute | solution.py:25
  184.5 3.0 %collective-permute-done.32.refs_5_ = bf16[64,1280]{1,0:T(8,128)(2,1)S(1)} collective-permute-done((bf16[64,1280]{1,0:T(8,128)(2,1)S(1)}, bf16[64,1280]{1,0:T(8,128)(2,1)S(1)}, u32[]{:S(2)}, u32[]{:S(2)}) %collective-permute-start.32) | collective-permute-done | bytes 163872 | tf_op jit(solution)/shard_map/ppermute | solution.py:25
  187.4 1.8 collective-permute-done.34.refs_7_
  189.2 4.8 %gradients.1 = (bf16[2,160,1280]{2,1,0:T(8,128)(2,1)S(1)}, bf16[2,160,1280]{2,1,0:T(8,128)(2,1)S(1)}, bf16[2,160,1280]{2,1,0:T(8,128)(2,1)S(1)}, bf16[2,160,1280]{2,1,0:T(8,128)(2,1)S(1)}) custom-call(s32[3]{0:T(128)S(1)} %pad_add_fusion.sel_ref, bf16[64,1280]{1,0:T(8,128)(2,1)S(1)} %multiply_convert_fusion.refs_0_, ...), custom_call_target="tpu_custom_call" | custom-call | flops 3355443200 | bytes 14417920 | tf_op jit(solution)/shard_map/gradients/pallas_call | solution.py:84
  194.0 0.9 copy-done.12
  194.9 0.9 copy-done.14
  196.3 1.8 collective-permute-done.40
  198.1 1.4 convert_add_fusion
  199.6 1.6 collective-permute-start.41
  202.0 9.9 %collective-permute-done.41 = bf16[160,1280]{1,0:T(8,128)(2,1)S(1)} collective-permute-done((bf16[160,1280]{1,0:T(8,128)(2,1)S(1)}, bf16[160,1280]{1,0:T(8,128)(2,1)S(1)}, u32[]{:S(2)}, u32[]{:S(2)}) %collective-permute-start.41) | collective-permute-done | bytes 409632 | tf_op jit(solution)/shard_map/ppermute | solution.py:20
  212.0 1.0 bitcast_add_fusion
  213.0 7.0 %collective-permute-done.39 = bf16[160,1280]{1,0:T(8,128)(2,1)S(1)} collective-permute-done((bf16[160,1280]{1,0:T(8,128)(2,1)S(1)}, bf16[160,1280]{1,0:T(8,128)(2,1)S(1)}, u32[]{:S(2)}, u32[]{:S(2)}) %collective-permute-start.39) | collective-permute-done | bytes 409632 | tf_op jit(solution)/shard_map/ppermute | solution.py:20
  220.0 1.0 bitcast_add_fusion.1
  (124 shorter events, 8.5 us)
Async XLA Ops:
  0.6 79.6 %copy-start = (bf16[64,1280]{1,0:T(8,128)(2,1)S(1)}, bf16[64,1280]{1,0:T(8,128)(2,1)}, u32[]{:S(2)}) copy-start(bf16[64,1280]{1,0:T(8,128)(2,1)} %param.10) | copy-start | bytes 491524
  0.7 27.1 %copy-start.20 = (f32[2,1280]{1,0:T(2,128)S(1)}, f32[2,1280]{1,0:T(2,128)}, u32[]{:S(2)}) copy-start(f32[2,1280]{1,0:T(2,128)} %param.11) | copy-start | bytes 30724
  0.7 27.2 %copy-start.1 = (bf16[1,1280,1280]{2,1,0:T(8,128)(2,1)S(1)}, bf16[1,1280,1280]{2,1,0:T(8,128)(2,1)}, u32[]{:S(2)}) copy-start(bf16[1,1280,1280]{2,1,0:T(8,128)(2,1)} %param.12) | copy-start | bytes 9830404
  2.9 24.9 %collective-permute-start.2 = (bf16[320,1280]{1,0:T(8,128)(2,1)}, bf16[320,1280]{1,0:T(8,128)(2,1)}, u32[]{:S(2)}, u32[]{:S(2)}) collective-permute-start(bf16[320,1280]{1,0:T(8,128)(2,1)} %dynamic-slice_bitcast_fusion), channel_id=1, source_target_pairs={{0,16},{16,0},{1,17},{17,1},{2,18},{18,2},{3,19},{19,3},{4,20},{20... | collective-permute-start | bytes 2457608 | tf_op jit(solution)/shard_map/ppermute | solution.py:25
  5.9 12.7 %collective-permute-start = (bf16[128,1280]{1,0:T(8,128)(2,1)}, bf16[128,1280]{1,0:T(8,128)(2,1)S(1)}, u32[]{:S(2)}, u32[]{:S(2)}) collective-permute-start(bf16[128,1280]{1,0:T(8,128)(2,1)} %bitcast.50), channel_id=1, source_target_pairs={{0,1},{1,2},{2,3},{3,0},{4,5},{5,6},{6,7},{7,4},{8,9},{9,10},{10,1... | collective-permute-start | bytes 983048 | tf_op jit(solution)/shard_map/ppermute | solution.py:20
  7.5 16.1 %collective-permute-start.1 = (bf16[128,1280]{1,0:T(8,128)(2,1)}, bf16[128,1280]{1,0:T(8,128)(2,1)S(1)}, u32[]{:S(2)}, u32[]{:S(2)}) collective-permute-start(bf16[128,1280]{1,0:T(8,128)(2,1)} %bitcast.51), channel_id=1, source_target_pairs={{0,3},{1,0},{2,1},{3,2},{4,7},{5,4},{6,5},{7,6},{8,11},{9,8},{10,9... | collective-permute-start | bytes 983048 | tf_op jit(solution)/shard_map/ppermute | solution.py:20
  18.6 0.7 copy-start.6
  23.6 0.7 copy-start.9
  24.3 39.8 %collective-permute-start.16 = (bf16[320,1280]{1,0:T(8,128)(2,1)}, bf16[320,1280]{1,0:T(8,128)(2,1)}, u32[]{:S(2)}, u32[]{:S(2)}) collective-permute-start(bf16[320,1280]{1,0:T(8,128)(2,1)} %dynamic-slice_bitcast_fusion.1), channel_id=1, source_target_pairs={{16,0},{17,1},{18,2},{19,3},{20,4},{21,5},{22,6},{23,7},{24,8},{25... | collective-permute-start | bytes 2457608 | tf_op jit(solution)/shard_map/ppermute | solution.py:383
  25.6 17.4 %collective-permute-start.4 = (bf16[128,1280]{1,0:T(8,128)(2,1)}, bf16[128,1280]{1,0:T(8,128)(2,1)}, u32[]{:S(2)}, u32[]{:S(2)}) collective-permute-start(bf16[128,1280]{1,0:T(8,128)(2,1)} %bitcast.52), channel_id=1, source_target_pairs={{0,2},{1,3},{2,0},{3,1},{4,6},{5,7},{6,4},{7,5},{8,10},{9,11},{10,... | collective-permute-start | bytes 983048 | tf_op jit(solution)/shard_map/ppermute | solution.py:20
  27.8 1.9 copy-start.2
  29.8 1.0 copy-start.7
  30.7 1.0 copy-start.10
  31.7 3.6 %copy-start.4 = (bf16[2,64,1280]{2,1,0:T(8,128)(2,1)S(1)}, bf16[2,64,1280]{2,1,0:T(8,128)(2,1)}, u32[]{:S(2)}) copy-start(bf16[2,64,1280]{2,1,0:T(8,128)(2,1)} %param.7) | copy-start | bytes 983044
  43.0 31.1 %copy-start.21 = (s32[2]{0:T(128)S(1)}, s32[2]{0:T(128)}, u32[]{:S(2)}) copy-start(s32[2]{0:T(128)} %param.8) | copy-start | bytes 28
  43.0 33.3 %copy-start.22 = (s32[2]{0:T(128)S(1)}, s32[2]{0:T(128)}, u32[]{:S(2)}) copy-start(s32[2]{0:T(128)} %param.9) | copy-start | bytes 28
  46.2 16.5 %collective-permute-start.5 = (bf16[64,1280]{1,0:T(8,128)(2,1)S(1)}, bf16[64,1280]{1,0:T(8,128)(2,1)S(1)}, u32[]{:S(2)}, u32[]{:S(2)}) collective-permute-start(bf16[64,1280]{1,0:T(8,128)(2,1)S(1)} %get-tuple-element.52), channel_id=1, source_target_pairs={{0,2},{1,3},{2,0},{3,1},{4,6},{5,7},{6,4},{7,5},{8,10},{9,11},{10,... | collective-permute-start | bytes 491528 | tf_op jit(solution)/shard_map/ppermute | solution.py:20
  46.3 18.4 %collective-permute-start.9 = (bf16[64,1280]{1,0:T(8,128)(2,1)S(1)}, bf16[64,1280]{1,0:T(8,128)(2,1)S(1)}, u32[]{:S(2)}, u32[]{:S(2)}) collective-permute-start(bf16[64,1280]{1,0:T(8,128)(2,1)S(1)} %get-tuple-element.53), channel_id=1, source_target_pairs={{0,18},{1,19},{2,16},{3,17},{4,22},{5,23},{6,20},{7,21},{8,26},{9,... | collective-permute-start | bytes 491528 | tf_op jit(solution)/shard_map/ppermute | solution.py:34
  53.7 11.0 %collective-permute-start.7 = (bf16[64,1280]{1,0:T(8,128)(2,1)S(1)}, bf16[64,1280]{1,0:T(8,128)(2,1)S(1)}, u32[]{:S(2)}, u32[]{:S(2)}) collective-permute-start(bf16[64,1280]{1,0:T(8,128)(2,1)S(1)} %get-tuple-element.50), channel_id=1, source_target_pairs={{0,16},{1,17},{2,18},{3,19},{4,20},{5,21},{6,22},{7,23},{8,24},{9,... | collective-permute-start | bytes 491528 | tf_op jit(solution)/shard_map/ppermute | solution.py:34
  55.0 11.7 %collective-permute-start.10 = (bf16[64,1280]{1,0:T(8,128)(2,1)S(1)}, bf16[64,1280]{1,0:T(8,128)(2,1)S(1)}, u32[]{:S(2)}, u32[]{:S(2)}) collective-permute-start(bf16[64,1280]{1,0:T(8,128)(2,1)S(1)} %get-tuple-element.46), channel_id=1, source_target_pairs={{0,17},{1,18},{2,19},{3,16},{4,21},{5,22},{6,23},{7,20},{8,25},{9,... | collective-permute-start | bytes 491528 | tf_op jit(solution)/shard_map/ppermute | solution.py:34
  62.7 4.1 %copy-start.16 = (bf16[64,1280]{1,0:T(8,128)(2,1)}, bf16[64,1280]{1,0:T(8,128)(2,1)S(1)}, u32[]{:S(2)}) copy-start(bf16[64,1280]{1,0:T(8,128)(2,1)S(1)} %collective-permute-done.5) | copy-start | bytes 491524
  62.7 30.1 %collective-permute-start.14 = (bf16[320,1280]{1,0:T(8,128)(2,1)}, bf16[320,1280]{1,0:T(8,128)(2,1)}, u32[]{:S(2)}, u32[]{:S(2)}) collective-permute-start(bf16[320,1280]{1,0:T(8,128)(2,1)} %collective-permute-done.2.p0), channel_id=1, source_target_pairs={{0,8},{4,12},{8,0},{12,4},{1,9},{5,13},{9,1},{13,5},{2,10},{6,14},... | collective-permute-start | bytes 2457608 | tf_op jit(solution)/shard_map/ppermute | solution.py:25
  64.2 29.4 %collective-permute-start.18 = (bf16[320,1280]{1,0:T(8,128)(2,1)}, bf16[320,1280]{1,0:T(8,128)(2,1)}, u32[]{:S(2)}, u32[]{:S(2)}) collective-permute-start(bf16[320,1280]{1,0:T(8,128)(2,1)} %collective-permute-done.16.p0), channel_id=1, source_target_pairs={{0,8},{4,12},{8,0},{12,4},{1,9},{5,13},{9,1},{13,5},{2,10},{6,14},... | collective-permute-start | bytes 2457608 | tf_op jit(solution)/shard_map/ppermute | solution.py:25
  64.7 2.0 copy-start.17
  64.7 13.5 %collective-permute-start.3 = (bf16[64,1280]{1,0:T(8,128)(2,1)}, bf16[64,1280]{1,0:T(8,128)(2,1)}, u32[]{:S(2)}, u32[]{:S(2)}) collective-permute-start(bf16[64,1280]{1,0:T(8,128)(2,1)} %get-tuple-element.45), channel_id=1, source_target_pairs={{0,3},{1,0},{2,1},{3,2},{4,7},{5,4},{6,5},{7,6},{8,11},{9,8},{10,9... | collective-permute-start | bytes 491528 | tf_op jit(solution)/shard_map/ppermute | solution.py:20
  64.7 2.0 copy-start.18
  64.7 13.4 %collective-permute-start.6 = (bf16[64,1280]{1,0:T(8,128)(2,1)}, bf16[64,1280]{1,0:T(8,128)(2,1)}, u32[]{:S(2)}, u32[]{:S(2)}) collective-permute-start(bf16[64,1280]{1,0:T(8,128)(2,1)} %get-tuple-element.47), channel_id=1, source_target_pairs={{0,1},{1,2},{2,3},{3,0},{4,5},{5,6},{6,7},{7,4},{8,9},{9,10},{10,1... | collective-permute-start | bytes 491528 | tf_op jit(solution)/shard_map/ppermute | solution.py:20
  66.8 0.7 copy-start.19
  67.4 10.8 %collective-permute-start.8 = (bf16[64,1280]{1,0:T(8,128)(2,1)}, bf16[64,1280]{1,0:T(8,128)(2,1)}, u32[]{:S(2)}, u32[]{:S(2)}) collective-permute-start(bf16[64,1280]{1,0:T(8,128)(2,1)} %get-tuple-element.44), channel_id=1, source_target_pairs={{0,19},{1,16},{2,17},{3,18},{4,23},{5,20},{6,21},{7,22},{8,27},{9,... | collective-permute-start | bytes 491528 | tf_op jit(solution)/shard_map/ppermute | solution.py:34
  80.0 12.8 %collective-permute-start.20 = (bf16[64,1280]{1,0:T(8,128)(2,1)S(1)}, bf16[64,1280]{1,0:T(8,128)(2,1)S(1)}, u32[]{:S(2)}, u32[]{:S(2)}) collective-permute-start(bf16[64,1280]{1,0:T(8,128)(2,1)S(1)} %bitcast.55), channel_id=1, source_target_pairs={{0,2},{1,3},{2,0},{3,1},{4,6},{5,7},{6,4},{7,5},{8,10},{9,11},{10,... | collective-permute-start | bytes 491528 | tf_op jit(solution)/shard_map/ppermute | solution.py:20
  80.4 25.0 %collective-permute-start.13 = (bf16[320,1280]{1,0:T(8,128)(2,1)}, bf16[320,1280]{1,0:T(8,128)(2,1)S(1)}, u32[]{:S(2)}, u32[]{:S(2)}) collective-permute-start(bf16[320,1280]{1,0:T(8,128)(2,1)} %collective-permute-done.2.p0), channel_id=1, source_target_pairs={{0,4},{4,0},{8,12},{12,8},{1,5},{5,1},{9,13},{13,9},{2,6},{6,2},{1... | collective-permute-start | bytes 2457608 | tf_op jit(solution)/shard_map/ppermute | solution.py:25
  80.4 13.1 %collective-permute-start.11 = (bf16[64,1280]{1,0:T(8,128)(2,1)S(1)}, bf16[64,1280]{1,0:T(8,128)(2,1)S(1)}, u32[]{:S(2)}, u32[]{:S(2)}) collective-permute-start(bf16[64,1280]{1,0:T(8,128)(2,1)S(1)} %bitcast.56), channel_id=1, source_target_pairs={{0,1},{1,2},{2,3},{3,0},{4,5},{5,6},{6,7},{7,4},{8,9},{9,10},{10,1... | collective-permute-start | bytes 491528 | tf_op jit(solution)/shard_map/ppermute | solution.py:20
  92.8 14.3 %collective-permute-start.17 = (bf16[320,1280]{1,0:T(8,128)(2,1)}, bf16[320,1280]{1,0:T(8,128)(2,1)S(1)}, u32[]{:S(2)}, u32[]{:S(2)}) collective-permute-start(bf16[320,1280]{1,0:T(8,128)(2,1)} %collective-permute-done.16.p0), channel_id=1, source_target_pairs={{0,4},{4,0},{8,12},{12,8},{1,5},{5,1},{9,13},{13,9},{2,6},{6,2},{1... | collective-permute-start | bytes 2457608 | tf_op jit(solution)/shard_map/ppermute | solution.py:25
  92.8 12.6 %collective-permute-start.15 = (bf16[320,1280]{1,0:T(8,128)(2,1)}, bf16[320,1280]{1,0:T(8,128)(2,1)S(1)}, u32[]{:S(2)}, u32[]{:S(2)}) collective-permute-start(bf16[320,1280]{1,0:T(8,128)(2,1)} %collective-permute-done.14.p2), channel_id=1, source_target_pairs={{0,4},{4,0},{8,12},{12,8},{1,5},{5,1},{9,13},{13,9},{2,6},{6,2},{1... | collective-permute-start | bytes 2457608 | tf_op jit(solution)/shard_map/ppermute | solution.py:25
  93.5 13.5 %collective-permute-start.19 = (bf16[320,1280]{1,0:T(8,128)(2,1)}, bf16[320,1280]{1,0:T(8,128)(2,1)S(1)}, u32[]{:S(2)}, u32[]{:S(2)}) collective-permute-start(bf16[320,1280]{1,0:T(8,128)(2,1)} %collective-permute-done.18.p2), channel_id=1, source_target_pairs={{0,4},{4,0},{8,12},{12,8},{1,5},{5,1},{9,13},{13,9},{2,6},{6,2},{1... | collective-permute-start | bytes 2457608 | tf_op jit(solution)/shard_map/ppermute | solution.py:25
  93.5 6.7 %collective-permute-start.12 = (bf16[64,1280]{1,0:T(8,128)(2,1)S(1)}, bf16[64,1280]{1,0:T(8,128)(2,1)S(1)}, u32[]{:S(2)}, u32[]{:S(2)}) collective-permute-start(bf16[64,1280]{1,0:T(8,128)(2,1)S(1)} %bitcast.57), channel_id=1, source_target_pairs={{0,3},{1,0},{2,1},{3,2},{4,7},{5,4},{6,5},{7,6},{8,11},{9,8},{10,9... | collective-permute-start | bytes 491528 | tf_op jit(solution)/shard_map/ppermute | solution.py:20
  100.2 42.5 %collective-permute-start.27 = (bf16[320,1280]{1,0:T(8,128)(2,1)}, bf16[320,1280]{1,0:T(8,128)(2,1)S(1)}, u32[]{:S(2)}, u32[]{:S(2)}) collective-permute-start(bf16[320,1280]{1,0:T(8,128)(2,1)} %dynamic-slice_bitcast_fusion.1), channel_id=1, source_target_pairs={{0,16},{1,17},{2,18},{3,19},{4,20},{5,21},{6,22},{7,23},{8,24},{9,... | collective-permute-start | bytes 2457608 | tf_op jit(solution)/shard_map/ppermute | solution.py:443
  107.1 2.4 %copy-start.3 = (bf16[1,1280,1280]{2,1,0:T(8,128)(2,1)S(1)}, bf16[1,1280,1280]{2,1,0:T(8,128)(2,1)}, u32[]{:S(2)}) copy-start(bf16[1,1280,1280]{2,1,0:T(8,128)(2,1)} %param.13) | copy-start | bytes 9830404
  115.9 6.3 %collective-permute-start.21 = (f32[5,1280]{1,0:T(8,128)S(1)}, f32[5,1280]{1,0:T(8,128)S(1)}, u32[]{:S(2)}, u32[]{:S(2)}) collective-permute-start(f32[5,1280]{1,0:T(8,128)S(1)} %pad_maximum_fusion), channel_id=1, source_target_pairs={{0,1},{1,2},{2,3},{3,0},{4,5},{5,6},{6,7},{7,4},{8,9},{9,10},{10,1... | collective-permute-start | bytes 76808 | tf_op jit(solution)/shard_map/ppermute | solution.py:20
  116.0 6.2 %collective-permute-start.23 = (f32[5,1280]{1,0:T(8,128)S(1)}, f32[5,1280]{1,0:T(8,128)S(1)}, u32[]{:S(2)}, u32[]{:S(2)}) collective-permute-start(f32[5,1280]{1,0:T(8,128)S(1)} %pad_maximum_fusion), channel_id=1, source_target_pairs={{0,3},{1,0},{2,1},{3,2},{4,7},{5,4},{6,5},{7,6},{8,11},{9,8},{10,9... | collective-permute-start | bytes 76808 | tf_op jit(solution)/shard_map/ppermute | solution.py:20
  119.9 4.9 %collective-permute-start.22 = (f32[5,1280]{1,0:T(8,128)S(1)}, f32[5,1280]{1,0:T(8,128)S(1)}, u32[]{:S(2)}, u32[]{:S(2)}) collective-permute-start(f32[5,1280]{1,0:T(8,128)S(1)} %pad_maximum_fusion), channel_id=1, source_target_pairs={{0,2},{1,3},{2,0},{3,1},{4,6},{5,7},{6,4},{7,5},{8,10},{9,11},{10,... | collective-permute-start | bytes 76808 | tf_op jit(solution)/shard_map/ppermute | solution.py:20
  125.3 5.3 %copy-start.5 = (bf16[2,64,1280]{2,1,0:T(8,128)(2,1)S(1)}, bf16[2,64,1280]{2,1,0:T(8,128)(2,1)}, u32[]{:S(2)}) copy-start(bf16[2,64,1280]{2,1,0:T(8,128)(2,1)} %param.7) | copy-start | bytes 983044
  125.3 5.3 %copy-start.8 = (bf16[128,1280]{1,0:T(8,128)(2,1)S(1)}, bf16[128,1280]{1,0:T(8,128)(2,1)}, u32[]{:S(2)}) copy-start(bf16[128,1280]{1,0:T(8,128)(2,1)} %copy-done.6) | copy-start | bytes 983044
  125.3 5.3 %copy-start.11 = (bf16[128,1280]{1,0:T(8,128)(2,1)S(1)}, bf16[128,1280]{1,0:T(8,128)(2,1)}, u32[]{:S(2)}) copy-start(bf16[128,1280]{1,0:T(8,128)(2,1)} %copy-done.9) | copy-start | bytes 983044
  128.0 7.2 %collective-permute-start.24 = (bf16[64,1280]{1,0:T(8,128)(2,1)S(1)}, bf16[64,1280]{1,0:T(8,128)(2,1)S(1)}, u32[]{:S(2)}, u32[]{:S(2)}) collective-permute-start(bf16[64,1280]{1,0:T(8,128)(2,1)S(1)} %get-tuple-element.62), channel_id=1, source_target_pairs={{0,3},{1,0},{2,1},{3,2},{4,7},{5,4},{6,5},{7,6},{8,11},{9,8},{10,9... | collective-permute-start | bytes 491528 | tf_op jit(solution)/shard_map/ppermute | solution.py:20
  129.8 12.7 %collective-permute-start.25 = (bf16[64,1280]{1,0:T(8,128)(2,1)S(1)}, bf16[64,1280]{1,0:T(8,128)(2,1)S(1)}, u32[]{:S(2)}, u32[]{:S(2)}) collective-permute-start(bf16[64,1280]{1,0:T(8,128)(2,1)S(1)} %get-tuple-element.63), channel_id=1, source_target_pairs={{0,2},{1,3},{2,0},{3,1},{4,6},{5,7},{6,4},{7,5},{8,10},{9,11},{10,... | collective-permute-start | bytes 491528 | tf_op jit(solution)/shard_map/ppermute | solution.py:20
  129.8 12.7 %collective-permute-start.26 = (bf16[64,1280]{1,0:T(8,128)(2,1)S(1)}, bf16[64,1280]{1,0:T(8,128)(2,1)S(1)}, u32[]{:S(2)}, u32[]{:S(2)}) collective-permute-start(bf16[64,1280]{1,0:T(8,128)(2,1)S(1)} %get-tuple-element.64), channel_id=1, source_target_pairs={{0,1},{1,2},{2,3},{3,0},{4,5},{5,6},{6,7},{7,4},{8,9},{9,10},{10,1... | collective-permute-start | bytes 491528 | tf_op jit(solution)/shard_map/ppermute | solution.py:20
  142.7 19.0 %collective-permute-start.36 = (bf16[320,1280]{1,0:T(8,128)(2,1)S(1)}, bf16[320,1280]{1,0:T(8,128)(2,1)S(1)}, u32[]{:S(2)}, u32[]{:S(2)}) collective-permute-start(bf16[320,1280]{1,0:T(8,128)(2,1)S(1)} %collective-permute-done.27.p0), channel_id=1, source_target_pairs={{0,8},{4,12},{8,0},{12,4},{1,9},{5,13},{9,1},{13,5},{2,10},{6,14},... | collective-permute-start | bytes 2457608 | tf_op jit(solution)/shard_map/ppermute | solution.py:25
  144.3 35.0 %collective-permute-start.35 = (bf16[320,1280]{1,0:T(8,128)(2,1)S(1)}, bf16[320,1280]{1,0:T(8,128)(2,1)S(1)}, u32[]{:S(2)}, u32[]{:S(2)}) collective-permute-start(bf16[320,1280]{1,0:T(8,128)(2,1)S(1)} %collective-permute-done.27.p0), channel_id=1, source_target_pairs={{0,4},{4,0},{8,12},{12,8},{1,5},{5,1},{9,13},{13,9},{2,6},{6,2},{1... | collective-permute-start | bytes 2457608 | tf_op jit(solution)/shard_map/ppermute | solution.py:25
  161.7 17.8 %collective-permute-start.37 = (bf16[320,1280]{1,0:T(8,128)(2,1)S(1)}, bf16[320,1280]{1,0:T(8,128)(2,1)S(1)}, u32[]{:S(2)}, u32[]{:S(2)}) collective-permute-start(bf16[320,1280]{1,0:T(8,128)(2,1)S(1)} %collective-permute-done.36.p2), channel_id=1, source_target_pairs={{0,4},{4,0},{8,12},{12,8},{1,5},{5,1},{9,13},{13,9},{2,6},{6,2},{1... | collective-permute-start | bytes 2457608 | tf_op jit(solution)/shard_map/ppermute | solution.py:25
  161.8 9.0 %collective-permute-start.29 = (bf16[64,1280]{1,0:T(8,128)(2,1)S(1)}, bf16[64,1280]{1,0:T(8,128)(2,1)S(1)}, u32[]{:S(2)}, u32[]{:S(2)}) collective-permute-start(bf16[64,1280]{1,0:T(8,128)(2,1)S(1)} %multiply_convert_fusion.refs_0_), channel_id=1, source_target_pairs={{0,1},{1,2},{2,3},{3,0},{4,5},{5,6},{6,7},{7,4},{8,9},{9,10},{10,1... | collective-permute-start | bytes 491528 | tf_op jit(solution)/shard_map/ppermute | solution.py:20
  162.3 15.0 %collective-permute-start.31 = (bf16[64,1280]{1,0:T(8,128)(2,1)S(1)}, bf16[64,1280]{1,0:T(8,128)(2,1)S(1)}, u32[]{:S(2)}, u32[]{:S(2)}) collective-permute-start(bf16[64,1280]{1,0:T(8,128)(2,1)S(1)} %multiply_convert_fusion.refs_0_), channel_id=1, source_target_pairs={{0,2},{1,3},{2,0},{3,1},{4,6},{5,7},{6,4},{7,5},{8,10},{9,11},{10,... | collective-permute-start | bytes 491528 | tf_op jit(solution)/shard_map/ppermute | solution.py:20
  164.3 13.0 %collective-permute-start.33 = (bf16[64,1280]{1,0:T(8,128)(2,1)S(1)}, bf16[64,1280]{1,0:T(8,128)(2,1)S(1)}, u32[]{:S(2)}, u32[]{:S(2)}) collective-permute-start(bf16[64,1280]{1,0:T(8,128)(2,1)S(1)} %multiply_convert_fusion.refs_0_), channel_id=1, source_target_pairs={{0,3},{1,0},{2,1},{3,2},{4,7},{5,4},{6,5},{7,6},{8,11},{9,8},{10,9... | collective-permute-start | bytes 491528 | tf_op jit(solution)/shard_map/ppermute | solution.py:20
  170.8 9.4 %collective-permute-start.28 = (bf16[64,1280]{1,0:T(8,128)(2,1)S(1)}, bf16[64,1280]{1,0:T(8,128)(2,1)S(1)}, u32[]{:S(2)}, u32[]{:S(2)}) collective-permute-start(bf16[64,1280]{1,0:T(8,128)(2,1)S(1)} %multiply_convert_fusion.refs_0_), channel_id=1, source_target_pairs={{0,16},{16,0},{1,17},{17,1},{2,18},{18,2},{3,19},{19,3},{4,20},{20... | collective-permute-start | bytes 491528 | tf_op jit(solution)/shard_map/ppermute | solution.py:25
  177.3 7.1 %collective-permute-start.30 = (bf16[64,1280]{1,0:T(8,128)(2,1)S(1)}, bf16[64,1280]{1,0:T(8,128)(2,1)S(1)}, u32[]{:S(2)}, u32[]{:S(2)}) collective-permute-start(bf16[64,1280]{1,0:T(8,128)(2,1)S(1)} %collective-permute-done.29.refs_2_), channel_id=1, source_target_pairs={{0,16},{16,0},{1,17},{17,1},{2,18},{18,2},{3,19},{19,3},{4,20},{20... | collective-permute-start | bytes 491528 | tf_op jit(solution)/shard_map/ppermute | solution.py:25
  177.3 10.1 %collective-permute-start.32 = (bf16[64,1280]{1,0:T(8,128)(2,1)S(1)}, bf16[64,1280]{1,0:T(8,128)(2,1)S(1)}, u32[]{:S(2)}, u32[]{:S(2)}) collective-permute-start(bf16[64,1280]{1,0:T(8,128)(2,1)S(1)} %collective-permute-done.31.refs_4_), channel_id=1, source_target_pairs={{0,16},{16,0},{1,17},{17,1},{2,18},{18,2},{3,19},{19,3},{4,20},{20... | collective-permute-start | bytes 491528 | tf_op jit(solution)/shard_map/ppermute | solution.py:25
  179.3 9.8 %collective-permute-start.34 = (bf16[64,1280]{1,0:T(8,128)(2,1)S(1)}, bf16[64,1280]{1,0:T(8,128)(2,1)S(1)}, u32[]{:S(2)}, u32[]{:S(2)}) collective-permute-start(bf16[64,1280]{1,0:T(8,128)(2,1)S(1)} %collective-permute-done.33.refs_6_), channel_id=1, source_target_pairs={{0,16},{16,0},{1,17},{17,1},{2,18},{18,2},{3,19},{19,3},{4,20},{20... | collective-permute-start | bytes 491528 | tf_op jit(solution)/shard_map/ppermute | solution.py:25
  194.0 0.9 copy-start.12
  194.9 0.9 copy-start.14
  195.8 2.3 %collective-permute-start.40 = (bf16[2,160,1280]{2,1,0:T(8,128)(2,1)S(1)}, bf16[2,160,1280]{2,1,0:T(8,128)(2,1)S(1)}, u32[]{:S(2)}, u32[]{:S(2)}) collective-permute-start(bf16[2,160,1280]{2,1,0:T(8,128)(2,1)S(1)} %get-tuple-element.77), channel_id=1, source_target_pairs={{0,4},{4,0},{8,12},{12,8},{1,5},{5,1},{9,13},{13,9},{2,6},{6,2},{1... | collective-permute-start | bytes 2457608 | tf_op jit(solution)/shard_map/ppermute | solution.py:25
  195.8 5.4 %collective-permute-start.38 = (bf16[2,160,1280]{2,1,0:T(8,128)(2,1)S(1)}, bf16[2,160,1280]{2,1,0:T(8,128)(2,1)S(1)}, u32[]{:S(2)}, u32[]{:S(2)}) collective-permute-start(bf16[2,160,1280]{2,1,0:T(8,128)(2,1)S(1)} %get-tuple-element.75), channel_id=1, source_target_pairs={{0,4},{4,0},{8,12},{12,8},{1,5},{5,1},{9,13},{13,9},{2,6},{6,2},{1... | collective-permute-start | bytes 2457608 | tf_op jit(solution)/shard_map/ppermute | solution.py:25
  198.1 3.1 %copy-start.13 = (bf16[2,160,1280]{2,1,0:T(8,128)(2,1)S(1)}, bf16[2,160,1280]{2,1,0:T(8,128)(2,1)}, u32[]{:S(2)}) copy-start(bf16[2,160,1280]{2,1,0:T(8,128)(2,1)} %copy-done.12) | copy-start | bytes 2457604
  199.6 12.4 %collective-permute-start.41 = (bf16[160,1280]{1,0:T(8,128)(2,1)S(1)}, bf16[160,1280]{1,0:T(8,128)(2,1)S(1)}, u32[]{:S(2)}, u32[]{:S(2)}) collective-permute-start(bf16[160,1280]{1,0:T(8,128)(2,1)S(1)} %fusion.1), channel_id=1, source_target_pairs={{0,8},{4,12},{8,0},{12,4},{1,9},{5,13},{9,1},{13,5},{2,10},{6,14},... | collective-permute-start | bytes 1228808 | tf_op jit(solution)/shard_map/ppermute | solution.py:20
  201.5 18.5 %collective-permute-start.39 = (bf16[160,1280]{1,0:T(8,128)(2,1)S(1)}, bf16[160,1280]{1,0:T(8,128)(2,1)S(1)}, u32[]{:S(2)}, u32[]{:S(2)}) collective-permute-start(bf16[160,1280]{1,0:T(8,128)(2,1)S(1)} %fusion), channel_id=1, source_target_pairs={{0,8},{4,12},{8,0},{12,4},{1,9},{5,13},{9,1},{13,5},{2,10},{6,14},... | collective-permute-start | bytes 1228808 | tf_op jit(solution)/shard_map/ppermute | solution.py:20
  (1 other events, 0.7 us)

commit v7 on v6

v7 whole, which is shorter than its diff:
```python
import functools
import math

import jax
import jax.numpy as jnp
from jax import lax
from jax.experimental import pallas as pl
from jax.experimental.pallas import tpu as pltpu
from jax.sharding import PartitionSpec as P

STEPS = 50


EPS = 1e-06
VMEM_BYTES = 8 * 1024 * 1024


def rotated(value, axis, steps):
    count = lax.axis_size(axis)
    return lax.ppermute(value, axis, [(i, (i + steps) % count) for i in range(count)])


def swapped(value, axis, bit):
    count = lax.axis_size(axis)
    return lax.ppermute(value, axis, [(i, i ^ bit) for i in range(count)])


def gather_parts(piece):
    return [piece] + [rotated(piece, "tp", k) for k in range(1, lax.axis_size("tp"))]


def own_share(weight):
    rows = weight.shape[0] // lax.axis_size("dp")
    return lax.dynamic_slice_in_dim(weight, lax.axis_index("dp") * rows, rows, 0)


def joined(share):
    return lax.all_gather(share, "dp", axis=0, tiled=True)


def gelu_pair(value):
    cdf = 0.5 * (1.0 + lax.erf(value * (1.0 / math.sqrt(2.0))))
    density = jnp.exp(-0.5 * value * value) * (1.0 / math.sqrt(2.0 * math.pi))
    return (value * cdf, cdf + value * density)


def normed(rows, gain):
    scale = lax.rsqrt(jnp.mean(rows * rows, axis=-1, keepdims=True) + EPS)
    return (rows * scale * gain).astype(jnp.bfloat16)


def dot_nn(a, b):
    return jnp.dot(a, b, preferred_element_type=jnp.float32)


def dot_nt(a, b):
    return lax.dot_general(a, b, (((1,), (1,)), ((), ())), preferred_element_type=jnp.float32)


def tile_of(hidden):
    for tile in (256, 128):
        if hidden % tile == 0:
            return tile
    return hidden


IN_VMEM = pl.BlockSpec(memory_space=pltpu.VMEM)
IN_SMEM = pl.BlockSpec(memory_space=pltpu.SMEM)


def run(body, name, sel, operands, outs, scratch):
    return pl.pallas_call(
        body,
        in_specs=[IN_SMEM] + [IN_VMEM] * len(operands),
        out_specs=[IN_VMEM] * len(outs),
        scratch_shapes=scratch,
        out_shape=outs,
        compiler_params=pltpu.CompilerParams(vmem_limit_bytes=VMEM_BYTES),
        name=name,
    )(sel, *operands)


def bf16(*shape):
    return jax.ShapeDtypeStruct(shape, jnp.bfloat16)


def tiles(hidden):
    tile = tile_of(hidden)
    return [slice(t, t + tile) for t in range(0, hidden, tile)]


def by_section(sel_ref, section, work, own, other):
    @pl.when(sel_ref[0] == section)
    def _():
        work(*own)

    @pl.when(sel_ref[0] != section)
    def _():
        work(*other)


def partial_body(count, sel_ref, *refs):
    parts, (gain, w_in, w_out) = refs[:count], refs[count : count + 3]
    stay, leave, xn, acc = refs[count + 3 :]
    rows = parts[0].shape[0]
    late = rows // 2
    for i, part in enumerate(parts):
        xn[i * rows : (i + 1) * rows, :] = normed(part[...].astype(jnp.float32), gain[...])
    for t, tile in enumerate(tiles(w_in.shape[1])):
        act, unused = gelu_pair(dot_nn(xn[...], w_in[:, tile]))
        term = dot_nt(act.astype(jnp.bfloat16), w_out[:, tile])
        acc[...] = term if t == 0 else acc[...] + term
    for i in range(count):
        start = i * rows
        leave[i] = acc[start : start + late, :].astype(jnp.bfloat16)
        stay[i] = acc[start + late : start + rows, :].astype(jnp.bfloat16)


def block0_partials(parts, gain, w_in, w_out, sel):
    rows, width = parts[0].shape
    hidden, n = w_in.shape[1], len(parts)
    return run(
        functools.partial(partial_body, n),
        "block0_partial",
        sel,
        [*parts, gain, w_in, w_out],
        [bf16(n, rows // 2, width)] * 2,
        [
            pltpu.VMEM((n * rows, width), jnp.bfloat16),
            pltpu.VMEM((n * rows, width), jnp.float32),
        ],
    )


def denoise_body(tokens, count, sel_ref, *refs):
    latents, sigma, alpha = refs[:3]
    sums, out = refs[3 : 3 + count], refs[3 + count]
    late = out.shape[0]
    base = latents[pl.ds(pl.multiple_of((1 - sel_ref[0]) * late, late), late), :]
    base = base.astype(jnp.float32)
    eps = base
    for part in sums:
        eps = eps + part[...].astype(jnp.float32)
    out[...] = ((base - sigma[...] * eps) / alpha[...]).astype(jnp.bfloat16)


def denoised(latents, sigma, alpha, sums, tokens, sel):
    return run(
        functools.partial(denoise_body, tokens, len(sums)),
        "denoise",
        sel,
        [latents, sigma, alpha, *sums],
        [bf16(latents.shape[0] // 2, latents.shape[1])],
        [],
    )[0]


def crossing(count):
    near = [k for k in range(1, count) if 2 * k != count]
    return [0] + near + [k for k in range(1, count) if 2 * k == count]


def state_body(count, sel_ref, *refs):
    parts = refs[:count]
    gain, own, other, act, slope, xn_cols, xn = refs[count:]
    rows = parts[0].shape[0]
    late = rows // 2
    share = xn_cols.shape[0]
    mine = pl.multiple_of((1 - sel_ref[0]) * late, late)
    theirs = pl.multiple_of(sel_ref[0] * late, late)
    at = 0
    for start, order in ((mine, range(len(parts))), (theirs, crossing(len(parts)))):
        for k in order:
            rows_k = parts[k][pl.ds(start, late), :].astype(jnp.float32)
            xn[at : at + late, :] = normed(rows_k, gain[...])
            at += late
    cols = xn[:, pl.ds(pl.multiple_of(sel_ref[0] * share, share), share)]
    xn_cols[...] = cols.T

    def work(weight):
        for tile in tiles(weight.shape[1]):
            value, grad = gelu_pair(dot_nn(xn[...], weight[:, tile]))
            act[:, tile] = value.astype(jnp.bfloat16)
            slope[:, tile] = grad.astype(jnp.bfloat16)

    by_section(sel_ref, 0, work, (own,), (other,))


def block0_state(parts, gain, own, other, sel):
    total, width = sum(part.shape[0] for part in parts), parts[0].shape[1]
    hidden = own.shape[1]
    return run(
        functools.partial(state_body, len(parts)),
        "block0_state",
        sel,
        [*parts, gain, own, other],
        [bf16(total, hidden), bf16(total, hidden), bf16(width // 2, total)],
        [pltpu.VMEM((total, width), jnp.bfloat16)],
    )


def reward_body(count, tokens, sel_ref, *refs):
    parts, (gain, text) = refs[:count], refs[count : count + 2]
    own_in, own_out, other_in, other_out = refs[count + 2 : count + 6]
    slopes, (pool, xn) = refs[count + 6 : 2 * count + 6], refs[2 * count + 6 :]
    rows = parts[0].shape[0]
    half = rows // tokens
    row = lax.broadcasted_iota(jnp.int32, pool.shape, 0)
    start = jnp.zeros(pool.shape, jnp.float32)
    for image in range(half):
        own_rows = parts[0][image * tokens : (image + 1) * tokens, :].astype(jnp.float32)
        start = jnp.where(row == image, jnp.mean(own_rows, axis=0, keepdims=True), start)
        start = jnp.where(row == count * half + image, text[image : image + 1, :], start)
    pool[...] = start
    for i, part in enumerate(parts):
        xn[i * rows : (i + 1) * rows, :] = normed(part[...].astype(jnp.float32), gain[...])

    def work(w_in, w_out):
        for tile in tiles(w_in.shape[1]):
            act, grad = gelu_pair(dot_nn(xn[...], w_in[:, tile]))
            for i in range(count):
                slopes[i][:, tile] = grad[i * rows : (i + 1) * rows, :].astype(jnp.bfloat16)
            means = [
                jnp.mean(act[at : at + tokens, :], axis=0, keepdims=True)
                for at in range(0, count * rows, tokens)
            ]
            place = lax.broadcasted_iota(jnp.int32, (pool.shape[0], act.shape[1]), 0)
            stacked = jnp.zeros(place.shape, jnp.float32)
            for i, mean in enumerate(means):
                stacked = jnp.where(place == i, mean, stacked)
            pool[...] += dot_nt(stacked.astype(jnp.bfloat16), w_out[:, tile])

    by_section(sel_ref, 1, work, (own_in, own_out), (other_in, other_out))


def reward_forward(parts, tokens, gain, text, own, other, sel):
    rows, width = parts[0].shape
    hidden, n = own[0].shape[1], len(parts)
    images = (n + 1) * rows // tokens
    outs = run(
        functools.partial(reward_body, n, tokens),
        "reward_forward",
        sel,
        [*parts, gain, text, *own, *other],
        [bf16(rows, hidden)] * n
        + [jax.ShapeDtypeStruct((-(-images // 8) * 8, width), jnp.float32)],
        [pltpu.VMEM((n * rows, width), jnp.bfloat16)],
    )
    return outs[:n], outs[n]


def score_gradient(pooled, text):
    unit = text * lax.rsqrt(jnp.mean(text * text, axis=-1, keepdims=True) + EPS)
    scale = lax.rsqrt(jnp.mean(pooled * pooled, axis=-1, keepdims=True) + EPS)
    along = jnp.mean(pooled * unit, axis=-1, keepdims=True)
    return (-100.0 / pooled.shape[-1]) * (scale * unit - pooled * scale**3 * along)


def back_body(count, tokens, sel_ref, *refs):
    pools, slopes = refs[:count], refs[count : 2 * count]
    own_in, own_out, other_in, other_out = refs[2 * count : 2 * count + 4]
    outs = refs[2 * count + 4 : 3 * count + 4]
    g_mean, acc = refs[3 * count + 4 :]
    rows = slopes[0].shape[0]
    half = rows // tokens
    images = count * half
    pooled, texts = [], []
    for j in range(images):
        at = [(j - k * half) % images for k in range(count)]
        pooled.append(sum(pools[k][at[k] : at[k] + 1, :] for k in range(count)))
        text = images + j % half
        texts.append(pools[j // half][text : text + 1, :])
    padded = -(-images // 16) * 16
    row = lax.broadcasted_iota(jnp.int32, (padded, acc.shape[1]), 0)
    stacked, spoken = jnp.zeros(row.shape, jnp.float32), jnp.zeros(row.shape, jnp.float32)
    for j in range(images):
        stacked = jnp.where(row == j, pooled[j], stacked)
        spoken = jnp.where(row == j, texts[j], spoken)
    g_all = score_gradient(stacked, spoken) * (1.0 / tokens)
    g_mean[...] = g_all[: g_mean.shape[0], :]
    g_tok = g_all.astype(jnp.bfloat16)

    def work(w_in, w_out):
        for t, tile in enumerate(tiles(w_in.shape[1])):
            g_h = dot_nn(g_tok, w_out[:, tile])
            terms = []
            for i in range(count):
                for image in range(half):
                    at = i * half + image
                    slope = slopes[i][image * tokens : (image + 1) * tokens, tile]
                    terms.append(
                        (slope.astype(jnp.float32) * g_h[at : at + 1, :]).astype(jnp.bfloat16)
                    )
            term = dot_nt(jnp.concatenate(terms, axis=0), w_in[:, tile])
            acc[...] = term if t == 0 else acc[...] + term

    by_section(sel_ref, 1, work, (own_in, own_out), (other_in, other_out))
    for i, out in enumerate(outs):
        out[...] = acc[i * rows : (i + 1) * rows, :].astype(jnp.bfloat16)


def reward_back(pools, slopes, tokens, own, other, sel):
    rows, hidden = slopes[0].shape
    width, n = own[0].shape[0], len(slopes)
    outs = run(
        functools.partial(back_body, n, tokens),
        "reward_back",
        sel,
        [*pools, *slopes, *own, *other],
        [bf16(rows, width)] * n + [jax.ShapeDtypeStruct((8, width), jnp.float32)],
        [pltpu.VMEM((n * rows, width), jnp.float32)],
    )
    return outs[:n], outs[n]


def eps_gradient_body(tokens, count, sel_ref, *refs):
    seen_ref, g_mean, gain, ratio = refs[:4]
    sums, out = refs[4 : 4 + count], refs[4 + count]
    g_xn = sums[0][...].astype(jnp.float32)
    for part in sums[1:]:
        g_xn = g_xn + part[...].astype(jnp.float32)
    seen = seen_ref[...].astype(jnp.float32)
    scale = lax.rsqrt(jnp.mean(seen * seen, axis=-1, keepdims=True) + EPS)
    weighted = gain[...] * g_xn
    along = jnp.mean(seen * weighted, axis=-1, keepdims=True)
    g_norm = scale * weighted - seen * scale**3 * along
    for image in range(out.shape[0] // tokens):
        at = slice(image * tokens, (image + 1) * tokens)
        g_images = (g_mean[image : image + 1, :] + g_norm[at, :]).astype(jnp.bfloat16)
        out[at, :] = (ratio[at, :] * g_images.astype(jnp.float32)).astype(jnp.bfloat16)


def eps_gradient(seen, g_mean, gain, ratio, sums, tokens, sel):
    return run(
        functools.partial(eps_gradient_body, tokens, len(sums)),
        "eps_gradient",
        sel,
        [seen, g_mean, gain, ratio, *sums],
        [bf16(*seen.shape)],
        [],
    )[0]


def put_rows(result, core, keep, away, tile):
    groups, rows, unused = keep.shape
    for g in range(groups):
        even = result[2 * g * rows : (2 * g + 1) * rows, :]
        odd = result[(2 * g + 1) * rows : (2 * g + 2) * rows, :]
        keep[g, :, tile] = jnp.where(core == 0, even, odd).astype(jnp.bfloat16)
        away[g, :, tile] = jnp.where(core == 0, odd, even).astype(jnp.bfloat16)


def gradient_body(count, sel_ref, *refs):
    pieces = refs[:count]
    act, slope, xn_cols, own, other = refs[count : count + 5]
    out_keep, out_away, in_keep, in_away, g_all, turned = refs[count + 5 :]
    share = turned.shape[0]
    core = sel_ref[1]
    at = 0
    for piece in pieces:
        g_all[at : at + piece.shape[0], :] = piece[...]
        at += piece.shape[0]
    cols = g_all[:, pl.ds(pl.multiple_of(sel_ref[0] * share, share), share)]
    turned[...] = cols.T

    def work(weight):
        for tile in tiles(weight.shape[1]):
            put_rows(dot_nn(turned[...], act[:, tile]), core, out_keep, out_away, tile)
            g_h = dot_nn(g_all[...], weight[:, tile])
            g_hidden = (g_h * slope[:, tile].astype(jnp.float32)).astype(jnp.bfloat16)
            put_rows(dot_nn(xn_cols[...], g_hidden), core, in_keep, in_away, tile)

    by_section(sel_ref, 0, work, (own,), (other,))


def gradients(pieces, states, own, other, sel):
    total, width = sum(piece.shape[0] for piece in pieces), pieces[0].shape[1]
    hidden = own.shape[1]
    groups = lax.axis_size("dp") // 2
    outs = run(
        functools.partial(gradient_body, len(pieces)),
        "gradients",
        sel,
        [*pieces, *states, own, other],
        [bf16(groups, width // 2 // (2 * groups), hidden)] * 4,
        [
            pltpu.VMEM((total, width), jnp.bfloat16),
            pltpu.VMEM((width // 2, total), jnp.bfloat16),
        ],
    )
    return outs[:2], outs[2:]


def chip_body(sel_ref, keep, arrived, mine, others):
    groups = keep.shape[0]
    for k in range(groups):
        at = (sel_ref[2] + k) % groups
        total = keep[at].astype(jnp.float32) + arrived[at].astype(jnp.float32)
        if k == 0:
            mine[...] = total
        else:
            others[k - 1] = total.astype(jnp.bfloat16)


def sum_over_dp(keep, away, sel):
    groups, rows, hidden = keep.shape
    total, others = run(
        chip_body,
        "chip_sum",
        sel,
        [keep, swapped(away, "dp", 1)],
        [jax.ShapeDtypeStruct((rows, hidden), jnp.float32), bf16(groups - 1, rows, hidden)],
        [],
    )
    for k in range(1, groups):
        total = total + rotated(others[k - 1], "dp", 2 * k).astype(jnp.float32)
    return total


def on_device(latents, timesteps, prompt_ids, prompt_table, gains, w_in, w_out):
    count, tokens, width = latents.shape
    half = count // 2
    n_tp = lax.axis_size("tp")
    segment = lax.axis_index("sec")
    first = segment == 0
    dp = lax.axis_index("dp")
    sel = jnp.stack([segment, dp % 2, dp // 2]).astype(jnp.int32)
    own = (w_in[0], w_out[0])

    def my_half(value):
        return jnp.where(first, value[half:], value[:half])

    theta = math.pi / 2.0 * (my_half(timesteps).astype(jnp.float32) + 1.0) / (STEPS + 1.0)
    theta = jnp.repeat(theta, tokens)[:, None]
    alpha, sigma = jnp.cos(theta), jnp.sin(theta)

    flat = latents.reshape(count * tokens, width)
    lat_parts = gather_parts(flat)
    got_in = swapped(own_share(own[0]), "sec", 1)
    out_share, got_in, lat_parts[1], lat_parts[-1] = lax.optimization_barrier(
        (own_share(own[1]), got_in, lat_parts[1], lat_parts[-1])
    )
    got_out = lax.ppermute(out_share, "sec", [(1, 0)])

    onehot = (
        my_half(prompt_ids)[:, None] == jnp.arange(prompt_table.shape[0], dtype=jnp.int32)[None, :]
    ).astype(jnp.bfloat16)
    text_mine = dot_nn(onehot, prompt_table)

    near = [k for k in range(1, n_tp) if 2 * k != n_tp]
    rest = [0] + [k for k in range(1, n_tp) if 2 * k == n_tp]
    sums = [None] * n_tp
    hop = got_in
    for ks in (near, rest):
        if ks:
            operands, unused = lax.optimization_barrier(([lat_parts[k] for k in ks], hop))
            stay, leave = block0_partials(operands, gains[:1], *own, sel)
            crossed = lax.ppermute(leave, "sec", [(0, 1)])
            if ks is rest:
                crossed, got_out, sums = lax.optimization_barrier((crossed, got_out, sums))
            chosen = jnp.where(first, stay, crossed)
            for i, k in enumerate(ks):
                sums[k] = rotated(chosen[i], "tp", -k) if k else chosen[i]
            hop = crossed
    mine_rows = denoised(flat, sigma, alpha, sums, tokens, sel)

    other = (joined(got_in), joined(got_out))
    seen_parts = gather_parts(mine_rows)
    slopes1, pool = reward_forward(seen_parts, tokens, gains[1:], text_mine, own, other, sel)
    pools = gather_parts(pool)
    g_parts, g_mean = reward_back(pools, slopes1, tokens, own, other, sel)

    states = block0_state(lat_parts, gains[:1], own[0], other[0], sel)
    late_share, unused = lax.optimization_barrier((out_share, mine_rows))
    got_late = lax.ppermute(late_share, "sec", [(0, 1)])

    g_sums = [g_parts[0]] + [rotated(g_parts[k], "tp", -k) for k in range(1, n_tp)]
    g_sums, states, got_late = lax.optimization_barrier((g_sums, states, got_late))
    g_eps = eps_gradient(mine_rows, g_mean, gains[1:], -(sigma / alpha), g_sums, tokens, sel)

    g_mine = gather_parts(g_eps)
    pieces = list(g_mine)
    for ks in ([0], near, rest[1:]):
        if ks:
            pieces.append(swapped(jnp.concatenate([g_mine[k] for k in ks], 0), "sec", 1))
    out_parts, in_parts = gradients(pieces, states, own[1], joined(got_late), sel)
    grad_out, grad_in = sum_over_dp(*out_parts, sel), sum_over_dp(*in_parts, sel)
    return (grad_in, grad_out)


def solution(mesh):
    in_specs = (
        P(("dp", "tp"), None, None),
        P(("dp", "tp")),
        P(("dp", "tp")),
        P(),
        P(),
        P("sec", None, "tp"),
        P("sec", None, "tp"),
    )
    out_specs = (P(("sec", "dp"), "tp"), P(("sec", "dp"), "tp"))
    return jax.shard_map(
        on_device, mesh=mesh, in_specs=in_specs, out_specs=out_specs, check_vma=False
    )
```

time: 223 us -> 225 us (level)
  local copies, waits for them, and re-layouts: 15.1 us -> 53 us
  waiting for transfers between devices: 107 us -> 77.5 us
  between operations: 3.93 us -> 16.8 us
  starting transfers between devices: 57.1 us -> 46.6 us
  Pallas kernels: 31.7 us -> 26.8 us
  other arithmetic: 6.47 us -> 3.1 us
    unnamed x46 -> x120, local copies, waits for them, and re-layouts: 9.15 us -> 48.3 us
    ppermute x16 -> x6, waiting for transfers between devices: 28.2 us -> 8.86 us  [swapped(): return lax.ppermute(value, axis, [(i, i ^ bit) for i in range(count)])]
    ppermute x20, waiting for transfers between devices: 78.3 us -> 65.3 us  [rotated(): lax.ppermute(value, axis, [(i, (i + steps) % count) for i in range(count)])]
    ppermute x6 -> x4, starting transfers between devices: 23.2 us -> 13.4 us  [the longest x2 8.65 us: on_device(): crossed = lax.ppermute(leave, 'sec', [(0, 1)])]
    pallas_call x11 -> x10, Pallas kernels: 31.7 us -> 26.8 us  [run(): pl.pallas_call(body, in_specs=[IN_SMEM] + [IN_VMEM] * len(operands), out_...]
    ppermute x6 -> x4, waiting for transfers between devices: 0.02 us -> 3.37 us  [the longest x2 3.36 us: on_device(): crossed = lax.ppermute(leave, 'sec', [(0, 1)])]
    reduce_sum x7 -> x0, other arithmetic: 2.38 us -> none  [the longest x4 1.86 us: on_device(): jnp.mean(part.astype(jnp.float32).reshape(half, tokens, width), axis=1)]
    ppermute x16 -> x6, starting transfers between devices: 9.75 us -> 7.79 us  [swapped(): return lax.ppermute(value, axis, [(i, i ^ bit) for i in range(count)])]
  transfers between devices with their start and end apart: 42 -> 33, of which waited for: 20 -> 21; matrix products, arithmetic and copies ran while one was open for 4% -> 3% of each run, Pallas kernels for 12% -> 10%
where the time goes in v7:
time: 225 us; the launch traced here: 224 us
  waiting for transfers between devices  77.5 us (34%)
  local copies, waits for them, and re-layouts  53 us (24%)
  starting transfers between devices  46.6 us (21%)
  Pallas kernels  26.8 us (12%)
  between operations  16.8 us (7%)
  other arithmetic  3.1 us (1%)
    ppermute x20, waiting for transfers between devices, rotated(): lax.ppermute(value, axis, [(i, (i + steps) % count) for i in range(count)])  65.3 us
    unnamed x120, local copies, waits for them, and re-layouts  48.3 us
    pallas_call x10, Pallas kernels, run(): pl.pallas_call(body, in_specs=[IN_SMEM] + [IN_VMEM] * len(operands), out_...  26.8 us
    ppermute x20, starting transfers between devices, rotated(): lax.ppermute(value, axis, [(i, (i + steps) % count) for i in range(count)])  25.3 us
    ppermute x6, waiting for transfers between devices, swapped(): return lax.ppermute(value, axis, [(i, i ^ bit) for i in range(count)])  8.86 us
    ppermute x2, starting transfers between devices, on_device(): crossed = lax.ppermute(leave, 'sec', [(0, 1)])  8.65 us
    ppermute x6, starting transfers between devices, swapped(): return lax.ppermute(value, axis, [(i, i ^ bit) for i in range(count)])  7.79 us
  transfers between devices with their start and end apart: 33, of which 21 were waited for; matrix products, arithmetic and copies ran while one was open for 3% of the time, Pallas kernels for 10%

profile of v7, /device:TPU:0, one launch (start us, length us, event | category | flops | bytes accessed | tf_op | source)
XLA Modules:
  0.0 224.1 jit_solution(531273437689537082)
XLA Ops:
  7.3 1.4 dynamic-slice_bitcast_fusion
  8.6 3.0 %collective-permute-start.1 = (bf16[320,1280]{1,0:T(8,128)(2,1)S(1)}, bf16[320,1280]{1,0:T(8,128)(2,1)}, u32[]{:S(2)}, u32[]{:S(2)}) collective-permute-start(bf16[320,1280]{1,0:T(8,128)(2,1)S(1)} %dynamic-slice_bitcast_fusion), channel_id=1, source_target_pairs={{0,16},{16,0},{1,17},{17,1},{2,18},{18,2},{3,19},{19,3},{4,20},{20... | collective-permute-start | bytes 2457608 | tf_op jit(solution)/shard_map/ppermute | solution.py:25
  11.6 3.6 %collective-permute-start.3 = (bf16[128,1280]{1,0:T(8,128)(2,1)}, bf16[128,1280]{1,0:T(8,128)(2,1)S(1)}, u32[]{:S(2)}, u32[]{:S(2)}) collective-permute-start(bf16[128,1280]{1,0:T(8,128)(2,1)} %bitcast.38), channel_id=1, source_target_pairs={{0,3},{1,0},{2,1},{3,2},{4,7},{5,4},{6,5},{7,6},{8,11},{9,8},{10,9... | collective-permute-start | bytes 983048 | tf_op jit(solution)/shard_map/ppermute | solution.py:20
  15.2 2.1 dynamic-slice_bitcast_fusion.1
  17.3 6.4 %collective-permute-done.3.refs_1_.refs_3_ = bf16[128,1280]{1,0:T(8,128)(2,1)S(1)} collective-permute-done((bf16[128,1280]{1,0:T(8,128)(2,1)}, bf16[128,1280]{1,0:T(8,128)(2,1)S(1)}, u32[]{:S(2)}, u32[]{:S(2)}) %collective-permute-start.3) | collective-permute-done | bytes 327712 | tf_op jit(solution)/shard_map/ppermute | solution.py:20
  24.5 5.6 %collective-permute-done.2.refs_0_.refs_1_ = bf16[128,1280]{1,0:T(8,128)(2,1)S(1)} collective-permute-done((bf16[128,1280]{1,0:T(8,128)(2,1)}, bf16[128,1280]{1,0:T(8,128)(2,1)S(1)}, u32[]{:S(2)}, u32[]{:S(2)}) %collective-permute-start.2) | collective-permute-done | bytes 327712 | tf_op jit(solution)/shard_map/ppermute | solution.py:20
  30.9 2.1 collective-permute-start
  33.1 1.9 copy-done.2
  35.0 1.0 copy-done.16
  35.9 1.0 copy-done.19
  36.9 3.6 %block0_partial.2 = (bf16[2,64,1280]{2,1,0:T(8,128)(2,1)S(1)}, bf16[2,64,1280]{2,1,0:T(8,128)(2,1)}) custom-call(s32[3]{0:T(128)S(1)} %pad_add_fusion.sel_ref, bf16[128,1280]{1,0:T(8,128)(2,1)S(1)} %copy-done.19, bf16[128,1280]{1,0:T(8,128)(2,1)S(1)} %copy-done.16, f32[1,1280]{1,0:T(1,128)S(1)} %get-tuple-element.99.refs_2_.refs_4_, ...), custom_call_target="tpu_custom_call" | custom-call | tf_op jit(solution)/shard_map/block0_partial/pallas_call | solution.py:72
  41.3 4.2 %collective-permute-start.4 = (bf16[2,64,1280]{2,1,0:T(8,128)(2,1)}, bf16[2,64,1280]{2,1,0:T(8,128)(2,1)}, u32[]{:S(2)}, u32[]{:S(2)}) collective-permute-start(bf16[2,64,1280]{2,1,0:T(8,128)(2,1)} %get-tuple-element.53), channel_id=1, source_target_pairs={{0,16},{1,17},{2,18},{3,19},{4,20},{5,21},{6,22},{7,23},{8,24},{9,... | collective-permute-start | bytes 983048 | tf_op jit(solution)/shard_map/ppermute | solution.py:458
  45.4 1.3 collective-permute-start.6
  47.4 3.4 %collective-permute-done.4 = bf16[2,64,1280]{2,1,0:T(8,128)(2,1)} collective-permute-done((bf16[2,64,1280]{2,1,0:T(8,128)(2,1)}, bf16[2,64,1280]{2,1,0:T(8,128)(2,1)}, u32[]{:S(2)}, u32[]{:S(2)}) %collective-permute-start.4) | collective-permute-done | bytes 327712 | tf_op jit(solution)/shard_map/ppermute | solution.py:458
  50.8 2.0 copy-done.3
  52.8 1.0 copy-done.9
  53.7 3.4 %block0_partial.3 = (bf16[2,64,1280]{2,1,0:T(8,128)(2,1)S(1)}, bf16[2,64,1280]{2,1,0:T(8,128)(2,1)S(1)}) custom-call(s32[3]{0:T(128)S(1)} %pad_add_fusion.sel_ref, bf16[128,1280]{1,0:T(8,128)(2,1)S(1)} %bitcast.41, bf16[128,1280]{1,0:T(8,128)(2,1)} %collective-permute-done.refs_1_.refs_2_, f32[1,1280]{1,0:T(1,128)S(1)} %get-tuple-element.99.refs_2_.refs_4_, ...), custom_call_target="tpu_custom_call" | custom-call | tf_op jit(solution)/shard_map/block0_partial/pallas_call | solution.py:72
  57.9 4.5 %collective-permute-start.5 = (bf16[2,64,1280]{2,1,0:T(8,128)(2,1)S(1)}, bf16[2,64,1280]{2,1,0:T(8,128)(2,1)S(1)}, u32[]{:S(2)}, u32[]{:S(2)}) collective-permute-start(bf16[2,64,1280]{2,1,0:T(8,128)(2,1)S(1)} %get-tuple-element.57), channel_id=1, source_target_pairs={{0,16},{1,17},{2,18},{3,19},{4,20},{5,21},{6,22},{7,23},{8,24},{9,... | collective-permute-start | bytes 983048 | tf_op jit(solution)/shard_map/ppermute | solution.py:458
  62.5 1.6 collective-permute-start.8
  64.1 2.2 %collective-permute-start.7 = (bf16[64,1280]{1,0:T(8,128)(2,1)S(1)}, bf16[64,1280]{1,0:T(8,128)(2,1)S(1)}, u32[]{:S(2)}, u32[]{:S(2)}) collective-permute-start(bf16[64,1280]{1,0:T(8,128)(2,1)S(1)} %get-tuple-element.97), channel_id=1, source_target_pairs={{0,3},{1,0},{2,1},{3,2},{4,7},{5,4},{6,5},{7,6},{8,11},{9,8},{10,9... | collective-permute-start | bytes 491528 | tf_op jit(solution)/shard_map/ppermute | solution.py:20
  66.3 3.5 %collective-permute-done.8.refs_6_ = bf16[64,1280]{1,0:T(8,128)(2,1)S(1)} collective-permute-done((bf16[64,1280]{1,0:T(8,128)(2,1)S(1)}, bf16[64,1280]{1,0:T(8,128)(2,1)S(1)}, u32[]{:S(2)}, u32[]{:S(2)}) %collective-permute-start.8) | collective-permute-done | bytes 163872 | tf_op jit(solution)/shard_map/ppermute | solution.py:20
  72.7 1.0 broadcast_select_fusion
  76.8 4.4 %collective-permute-done.9.refs_5_ = bf16[64,1280]{1,0:T(8,128)(2,1)S(1)} collective-permute-done((bf16[64,1280]{1,0:T(8,128)(2,1)S(1)}, bf16[64,1280]{1,0:T(8,128)(2,1)S(1)}, u32[]{:S(2)}, u32[]{:S(2)}) %collective-permute-start.9) | collective-permute-done | bytes 163872 | tf_op jit(solution)/shard_map/ppermute | solution.py:20
  84.8 3.5 %collective-permute-start.19 = (bf16[320,1280]{1,0:T(8,128)(2,1)}, bf16[320,1280]{1,0:T(8,128)(2,1)}, u32[]{:S(2)}, u32[]{:S(2)}) collective-permute-start(bf16[320,1280]{1,0:T(8,128)(2,1)} %dynamic-slice_bitcast_fusion.1), channel_id=1, source_target_pairs={{0,16},{1,17},{2,18},{3,19},{4,20},{5,21},{6,22},{7,23},{8,24},{9,... | collective-permute-start | bytes 2457608 | tf_op jit(solution)/shard_map/ppermute | solution.py:475
  90.1 2.3 %collective-permute-start.12 = (bf16[64,1280]{1,0:T(8,128)(2,1)S(1)}, bf16[64,1280]{1,0:T(8,128)(2,1)S(1)}, u32[]{:S(2)}, u32[]{:S(2)}) collective-permute-start(bf16[64,1280]{1,0:T(8,128)(2,1)S(1)} %denoise.1.refs_0_), channel_id=1, source_target_pairs={{0,3},{1,0},{2,1},{3,2},{4,7},{5,4},{6,5},{7,6},{8,11},{9,8},{10,9... | collective-permute-start | bytes 491528 | tf_op jit(solution)/shard_map/ppermute | solution.py:20
  93.9 3.0 %collective-permute-done.12.refs_3_ = bf16[64,1280]{1,0:T(8,128)(2,1)S(1)} collective-permute-done((bf16[64,1280]{1,0:T(8,128)(2,1)S(1)}, bf16[64,1280]{1,0:T(8,128)(2,1)S(1)}, u32[]{:S(2)}, u32[]{:S(2)}) %collective-permute-start.12) | collective-permute-done | bytes 163872 | tf_op jit(solution)/shard_map/ppermute | solution.py:20
  97.5 5.2 %collective-permute-done.11.refs_2_ = bf16[64,1280]{1,0:T(8,128)(2,1)S(1)} collective-permute-done((bf16[64,1280]{1,0:T(8,128)(2,1)S(1)}, bf16[64,1280]{1,0:T(8,128)(2,1)S(1)}, u32[]{:S(2)}, u32[]{:S(2)}) %collective-permute-start.11) | collective-permute-done | bytes 163872 | tf_op jit(solution)/shard_map/ppermute | solution.py:20
  104.0 1.9 copy-done.4
  106.0 1.9 copy-done.6
  107.9 1.9 copy-done.7
  113.5 3.1 %reward_forward.1 = (bf16[64,1280]{1,0:T(8,128)(2,1)S(1)}, bf16[64,1280]{1,0:T(8,128)(2,1)S(1)}, bf16[64,1280]{1,0:T(8,128)(2,1)S(1)}, bf16[64,1280]{1,0:T(8,128)(2,1)S(1)}, f32[8,1280]{1,0:T(8,128)S(1)}) custom-call(s32[3]{0:T(128)S(1)} %pad_add_fusion.sel_ref, bf16[64,1280]{1,0:T(8,128)(2,1)S(1)} %copy-done.13, bf16[64,1280]{1,0:T(8,128)(2,1)S(1)} %copy-done.55, ...), custom_call_target="tpu_custom_call" | custom-call | tf_op jit(solution)/shard_map/reward_forward/pallas_call | solution.py:72
  116.6 1.0 collective-permute-start.15
  117.8 2.0 collective-permute-start.13
  119.8 1.2 collective-permute-done.15.refs_3_
  121.1 1.4 collective-permute-done.14.refs_2_
  122.5 1.1 collective-permute-done.13.refs_1_
  123.6 3.8 %reward_back.1 = (bf16[64,1280]{1,0:T(8,128)(2,1)S(1)}, bf16[64,1280]{1,0:T(8,128)(2,1)}, bf16[64,1280]{1,0:T(8,128)(2,1)}, bf16[64,1280]{1,0:T(8,128)(2,1)}, f32[8,1280]{1,0:T(8,128)S(1)}) custom-call(s32[3]{0:T(128)S(1)} %pad_add_fusion.sel_ref, f32[8,1280]{1,0:T(8,128)S(1)} %get-tuple-element.64.refs_0_, f32[8,1280]{1,0:T(8,128)S(1)} %collective-permute-done.13.refs_1_, ...), custom_call_target="tpu_custom_call" | custom-call | tf_op jit(solution)/shard_map/reward_back/pallas_call | solution.py:72
  127.5 1.5 collective-permute-start.16
  129.1 1.3 collective-permute-start.18
  130.4 4.3 %block0_state.1 = (bf16[512,1280]{1,0:T(8,128)(2,1)S(1)}, bf16[512,1280]{1,0:T(8,128)(2,1)S(1)}, bf16[640,512]{1,0:T(8,128)(2,1)S(1)}) custom-call(s32[3]{0:T(128)S(1)} %pad_add_fusion.sel_ref, bf16[128,1280]{1,0:T(8,128)(2,1)S(1)} %bitcast.43, bf16[128,1280]{1,0:T(8,128)(2,1)S(1)} %copy-done.20, bf16[128,1280]{1,0:T(8,128)(2,1)} %collective-permute-done.refs_1_.refs_2_, ...), custom_call_target="tpu_custom_call" | custom-call | tf_op jit(solution)/shard_map/block0_state/pallas_call | solution.py:72
  134.8 1.1 copy-done.21
  135.8 1.1 copy-done.23
  137.8 4.9 %collective-permute-done.17.refs_6_ = bf16[64,1280]{1,0:T(8,128)(2,1)} collective-permute-done((bf16[64,1280]{1,0:T(8,128)(2,1)}, bf16[64,1280]{1,0:T(8,128)(2,1)}, u32[]{:S(2)}, u32[]{:S(2)}) %collective-permute-start.17) | collective-permute-done | bytes 163872 | tf_op jit(solution)/shard_map/ppermute | solution.py:20
  144.6 1.3 eps_gradient.1.refs_0_
  146.0 2.0 collective-permute-start.20
  148.0 1.4 collective-permute-start.21
  149.4 2.3 %collective-permute-done.22.refs_3_ = bf16[64,1280]{1,0:T(8,128)(2,1)S(1)} collective-permute-done((bf16[64,1280]{1,0:T(8,128)(2,1)S(1)}, bf16[64,1280]{1,0:T(8,128)(2,1)S(1)}, u32[]{:S(2)}, u32[]{:S(2)}) %collective-permute-start.22) | collective-permute-done | bytes 163872 | tf_op jit(solution)/shard_map/ppermute | solution.py:20
  151.7 5.8 %collective-permute-done.20.refs_1_ = bf16[64,1280]{1,0:T(8,128)(2,1)S(1)} collective-permute-done((bf16[64,1280]{1,0:T(8,128)(2,1)S(1)}, bf16[64,1280]{1,0:T(8,128)(2,1)S(1)}, u32[]{:S(2)}, u32[]{:S(2)}) %collective-permute-start.20) | collective-permute-done | bytes 163872 | tf_op jit(solution)/shard_map/ppermute | solution.py:20
  157.5 2.0 collective-permute-start.24
  159.6 2.5 %collective-permute-done.21.refs_2_ = bf16[64,1280]{1,0:T(8,128)(2,1)S(1)} collective-permute-done((bf16[64,1280]{1,0:T(8,128)(2,1)S(1)}, bf16[64,1280]{1,0:T(8,128)(2,1)S(1)}, u32[]{:S(2)}, u32[]{:S(2)}) %collective-permute-start.21) | collective-permute-done | bytes 163872 | tf_op jit(solution)/shard_map/ppermute | solution.py:20
  162.2 2.1 collective-permute-start.25
  164.9 5.9 %collective-permute-done.23.refs_4_ = bf16[64,1280]{1,0:T(8,128)(2,1)S(1)} collective-permute-done((bf16[64,1280]{1,0:T(8,128)(2,1)S(1)}, bf16[64,1280]{1,0:T(8,128)(2,1)S(1)}, u32[]{:S(2)}, u32[]{:S(2)}) %collective-permute-start.23) | collective-permute-done | bytes 163872 | tf_op jit(solution)/shard_map/ppermute | solution.py:25
  171.5 1.1 collective-permute-done.25.refs_6_
  174.0 1.9 copy-done.5
  176.0 1.9 copy-done.8
  177.9 1.3 copy-done.22
  179.2 1.3 copy-done.24
  180.5 1.1 copy-done.26
  188.1 5.0 %gradients.1 = (bf16[2,160,1280]{2,1,0:T(8,128)(2,1)S(1)}, bf16[2,160,1280]{2,1,0:T(8,128)(2,1)S(1)}, bf16[2,160,1280]{2,1,0:T(8,128)(2,1)S(1)}, bf16[2,160,1280]{2,1,0:T(8,128)(2,1)S(1)}) custom-call(s32[3]{0:T(128)S(1)} %pad_add_fusion.sel_ref, bf16[64,1280]{1,0:T(8,128)(2,1)S(1)} %copy-done.28, bf16[64,1280]{1,0:T(8,128)(2,1)S(1)} %copy-done.32, ...), custom_call_target="tpu_custom_call" | custom-call | tf_op jit(solution)/shard_map/gradients/pallas_call | solution.py:72
  193.7 1.8 collective-permute-done.26.arrived
  197.6 1.5 collective-permute-start.29
  199.1 9.5 %collective-permute-done.27 = bf16[160,1280]{1,0:T(8,128)(2,1)S(1)} collective-permute-done((bf16[160,1280]{1,0:T(8,128)(2,1)S(1)}, bf16[160,1280]{1,0:T(8,128)(2,1)S(1)}, u32[]{:S(2)}, u32[]{:S(2)}) %collective-permute-start.27) | collective-permute-done | bytes 409632 | tf_op jit(solution)/shard_map/ppermute | solution.py:20
  208.6 1.0 convert_add_fusion.1
  209.6 7.0 %collective-permute-done.29 = bf16[160,1280]{1,0:T(8,128)(2,1)S(1)} collective-permute-done((bf16[160,1280]{1,0:T(8,128)(2,1)S(1)}, bf16[160,1280]{1,0:T(8,128)(2,1)S(1)}, u32[]{:S(2)}, u32[]{:S(2)}) %collective-permute-start.29) | collective-permute-done | bytes 409632 | tf_op jit(solution)/shard_map/ppermute | solution.py:20
  (152 shorter events, 35.6 us)
Async XLA Ops:
  7.2 86.6 %copy-start = (bf16[64,1280]{1,0:T(8,128)(2,1)S(1)}, bf16[64,1280]{1,0:T(8,128)(2,1)}, u32[]{:S(2)}) copy-start(bf16[64,1280]{1,0:T(8,128)(2,1)} %param.10) | copy-start | bytes 491524
  7.2 25.9 %copy-start.1 = (bf16[1,1280,1280]{2,1,0:T(8,128)(2,1)S(1)}, bf16[1,1280,1280]{2,1,0:T(8,128)(2,1)}, u32[]{:S(2)}) copy-start(bf16[1,1280,1280]{2,1,0:T(8,128)(2,1)} %param.12) | copy-start | bytes 9830404
  7.2 25.8 %copy-start.57 = (f32[2,1280]{1,0:T(2,128)S(1)}, f32[2,1280]{1,0:T(2,128)}, u32[]{:S(2)}) copy-start(f32[2,1280]{1,0:T(2,128)} %param.11) | copy-start | bytes 30724
  7.2 96.8 %all-gather.4.cloned.1.call-start = ((), (), s32[]{:S(2)}) async-start(), calls=%async_computation | async-start | bytes 4096000 | tf_op jit(solution)/shard_map/all_gather | solution.py:38
  8.6 22.2 %collective-permute-start.1 = (bf16[320,1280]{1,0:T(8,128)(2,1)S(1)}, bf16[320,1280]{1,0:T(8,128)(2,1)}, u32[]{:S(2)}, u32[]{:S(2)}) collective-permute-start(bf16[320,1280]{1,0:T(8,128)(2,1)S(1)} %dynamic-slice_bitcast_fusion), channel_id=1, source_target_pairs={{0,16},{16,0},{1,17},{17,1},{2,18},{18,2},{3,19},{19,3},{4,20},{20... | collective-permute-start | bytes 2457608 | tf_op jit(solution)/shard_map/ppermute | solution.py:25
  11.6 12.1 %collective-permute-start.3 = (bf16[128,1280]{1,0:T(8,128)(2,1)}, bf16[128,1280]{1,0:T(8,128)(2,1)S(1)}, u32[]{:S(2)}, u32[]{:S(2)}) collective-permute-start(bf16[128,1280]{1,0:T(8,128)(2,1)} %bitcast.38), channel_id=1, source_target_pairs={{0,3},{1,0},{2,1},{3,2},{4,7},{5,4},{6,5},{7,6},{8,11},{9,8},{10,9... | collective-permute-start | bytes 983048 | tf_op jit(solution)/shard_map/ppermute | solution.py:20
  15.2 14.8 %collective-permute-start.2 = (bf16[128,1280]{1,0:T(8,128)(2,1)}, bf16[128,1280]{1,0:T(8,128)(2,1)S(1)}, u32[]{:S(2)}, u32[]{:S(2)}) collective-permute-start(bf16[128,1280]{1,0:T(8,128)(2,1)} %bitcast.39), channel_id=1, source_target_pairs={{0,1},{1,2},{2,3},{3,0},{4,5},{5,6},{6,7},{7,4},{8,9},{9,10},{10,1... | collective-permute-start | bytes 983048 | tf_op jit(solution)/shard_map/ppermute | solution.py:20
  30.8 73.2 %all-gather.6.cloned.1.call-start = ((), (), s32[]{:S(2)}) async-start(), calls=%async_computation.1 | async-start | bytes 4096000 | tf_op jit(solution)/shard_map/all_gather | solution.py:38
  30.9 16.6 %collective-permute-start = (bf16[128,1280]{1,0:T(8,128)(2,1)}, bf16[128,1280]{1,0:T(8,128)(2,1)}, u32[]{:S(2)}, u32[]{:S(2)}) collective-permute-start(bf16[128,1280]{1,0:T(8,128)(2,1)} %bitcast.40), channel_id=1, source_target_pairs={{0,2},{1,3},{2,0},{3,1},{4,6},{5,7},{6,4},{7,5},{8,10},{9,11},{10,... | collective-permute-start | bytes 983048 | tf_op jit(solution)/shard_map/ppermute | solution.py:20
  33.0 1.9 copy-start.2
  35.0 1.0 copy-start.16
  35.9 1.0 copy-start.19
  41.3 9.5 %collective-permute-start.4 = (bf16[2,64,1280]{2,1,0:T(8,128)(2,1)}, bf16[2,64,1280]{2,1,0:T(8,128)(2,1)}, u32[]{:S(2)}, u32[]{:S(2)}) collective-permute-start(bf16[2,64,1280]{2,1,0:T(8,128)(2,1)} %get-tuple-element.53), channel_id=1, source_target_pairs={{0,16},{1,17},{2,18},{3,19},{4,20},{5,21},{6,22},{7,23},{8,24},{9,... | collective-permute-start | bytes 983048 | tf_op jit(solution)/shard_map/ppermute | solution.py:458
  45.4 27.2 %collective-permute-start.6 = (bf16[320,1280]{1,0:T(8,128)(2,1)}, bf16[320,1280]{1,0:T(8,128)(2,1)}, u32[]{:S(2)}, u32[]{:S(2)}) collective-permute-start(bf16[320,1280]{1,0:T(8,128)(2,1)} %dynamic-slice_bitcast_fusion.1), channel_id=1, source_target_pairs={{16,0},{17,1},{18,2},{19,3},{20,4},{21,5},{22,6},{23,7},{24,8},{25... | collective-permute-start | bytes 2457608 | tf_op jit(solution)/shard_map/ppermute | solution.py:443
  50.8 2.0 copy-start.3
  52.8 1.0 copy-start.9
  53.7 8.6 %copy-start.37 = (bf16[2,64,1280]{2,1,0:T(8,128)(2,1)S(1)}, bf16[2,64,1280]{2,1,0:T(8,128)(2,1)}, u32[]{:S(2)}) copy-start(bf16[2,64,1280]{2,1,0:T(8,128)(2,1)} %copy-done.36) | copy-start | bytes 983044
  57.9 16.8 %copy-start.58 = (s32[2]{0:T(128)S(1)}, s32[2]{0:T(128)}, u32[]{:S(2)}) copy-start(s32[2]{0:T(128)} %param.8) | copy-start | bytes 28
  57.9 30.4 %copy-start.59 = (s32[2]{0:T(128)S(1)}, s32[2]{0:T(128)}, u32[]{:S(2)}) copy-start(s32[2]{0:T(128)} %param.9) | copy-start | bytes 28
  57.9 14.0 %collective-permute-start.5 = (bf16[2,64,1280]{2,1,0:T(8,128)(2,1)S(1)}, bf16[2,64,1280]{2,1,0:T(8,128)(2,1)S(1)}, u32[]{:S(2)}, u32[]{:S(2)}) collective-permute-start(bf16[2,64,1280]{2,1,0:T(8,128)(2,1)S(1)} %get-tuple-element.57), channel_id=1, source_target_pairs={{0,16},{1,17},{2,18},{3,19},{4,20},{5,21},{6,22},{7,23},{8,24},{9,... | collective-permute-start | bytes 983048 | tf_op jit(solution)/shard_map/ppermute | solution.py:458
  62.5 7.4 %collective-permute-start.8 = (bf16[64,1280]{1,0:T(8,128)(2,1)S(1)}, bf16[64,1280]{1,0:T(8,128)(2,1)S(1)}, u32[]{:S(2)}, u32[]{:S(2)}) collective-permute-start(bf16[64,1280]{1,0:T(8,128)(2,1)S(1)} %get-tuple-element.96), channel_id=1, source_target_pairs={{0,1},{1,2},{2,3},{3,0},{4,5},{5,6},{6,7},{7,4},{8,9},{9,10},{10,1... | collective-permute-start | bytes 491528 | tf_op jit(solution)/shard_map/ppermute | solution.py:20
  64.1 7.1 %collective-permute-start.7 = (bf16[64,1280]{1,0:T(8,128)(2,1)S(1)}, bf16[64,1280]{1,0:T(8,128)(2,1)S(1)}, u32[]{:S(2)}, u32[]{:S(2)}) collective-permute-start(bf16[64,1280]{1,0:T(8,128)(2,1)S(1)} %get-tuple-element.97), channel_id=1, source_target_pairs={{0,3},{1,0},{2,1},{3,2},{4,7},{5,4},{6,5},{7,6},{8,11},{9,8},{10,9... | collective-permute-start | bytes 491528 | tf_op jit(solution)/shard_map/ppermute | solution.py:20
  72.6 101.4 %all-gather.8.cloned.1.call-start = ((), (), s32[]{:S(2)}) async-start(), calls=%async_computation.2 | async-start | bytes 4096000 | tf_op jit(solution)/shard_map/all_gather | solution.py:38
  73.7 7.6 %collective-permute-start.9 = (bf16[64,1280]{1,0:T(8,128)(2,1)S(1)}, bf16[64,1280]{1,0:T(8,128)(2,1)S(1)}, u32[]{:S(2)}, u32[]{:S(2)}) collective-permute-start(bf16[64,1280]{1,0:T(8,128)(2,1)S(1)} %get-tuple-element.94), channel_id=1, source_target_pairs={{0,2},{1,3},{2,0},{3,1},{4,6},{5,7},{6,4},{7,5},{8,10},{9,11},{10,... | collective-permute-start | bytes 491528 | tf_op jit(solution)/shard_map/ppermute | solution.py:20
  81.3 1.0 copy-start.10
  84.8 53.0 %collective-permute-start.19 = (bf16[320,1280]{1,0:T(8,128)(2,1)}, bf16[320,1280]{1,0:T(8,128)(2,1)}, u32[]{:S(2)}, u32[]{:S(2)}) collective-permute-start(bf16[320,1280]{1,0:T(8,128)(2,1)} %dynamic-slice_bitcast_fusion.1), channel_id=1, source_target_pairs={{0,16},{1,17},{2,18},{3,19},{4,20},{5,21},{6,22},{7,23},{8,24},{9,... | collective-permute-start | bytes 2457608 | tf_op jit(solution)/shard_map/ppermute | solution.py:475
  90.1 6.8 %collective-permute-start.12 = (bf16[64,1280]{1,0:T(8,128)(2,1)S(1)}, bf16[64,1280]{1,0:T(8,128)(2,1)S(1)}, u32[]{:S(2)}, u32[]{:S(2)}) collective-permute-start(bf16[64,1280]{1,0:T(8,128)(2,1)S(1)} %denoise.1.refs_0_), channel_id=1, source_target_pairs={{0,3},{1,0},{2,1},{3,2},{4,7},{5,4},{6,5},{7,6},{8,11},{9,8},{10,9... | collective-permute-start | bytes 491528 | tf_op jit(solution)/shard_map/ppermute | solution.py:20
  92.4 10.3 %collective-permute-start.11 = (bf16[64,1280]{1,0:T(8,128)(2,1)S(1)}, bf16[64,1280]{1,0:T(8,128)(2,1)S(1)}, u32[]{:S(2)}, u32[]{:S(2)}) collective-permute-start(bf16[64,1280]{1,0:T(8,128)(2,1)S(1)} %denoise.1.refs_0_), channel_id=1, source_target_pairs={{0,2},{1,3},{2,0},{3,1},{4,6},{5,7},{6,4},{7,5},{8,10},{9,11},{10,... | collective-permute-start | bytes 491528 | tf_op jit(solution)/shard_map/ppermute | solution.py:20
  92.4 10.9 %collective-permute-start.10 = (bf16[64,1280]{1,0:T(8,128)(2,1)S(1)}, bf16[64,1280]{1,0:T(8,128)(2,1)S(1)}, u32[]{:S(2)}, u32[]{:S(2)}) collective-permute-start(bf16[64,1280]{1,0:T(8,128)(2,1)S(1)} %denoise.1.refs_0_), channel_id=1, source_target_pairs={{0,1},{1,2},{2,3},{3,0},{4,5},{5,6},{6,7},{7,4},{8,9},{9,10},{10,1... | collective-permute-start | bytes 491528 | tf_op jit(solution)/shard_map/ppermute | solution.py:20
  104.0 1.9 copy-start.4
  106.0 1.9 copy-start.6
  107.9 1.9 copy-start.7
  116.6 4.5 %collective-permute-start.15 = (f32[8,1280]{1,0:T(8,128)S(1)}, f32[8,1280]{1,0:T(8,128)S(1)}, u32[]{:S(2)}, u32[]{:S(2)}) collective-permute-start(f32[8,1280]{1,0:T(8,128)S(1)} %get-tuple-element.64.refs_0_), channel_id=1, source_target_pairs={{0,3},{1,0},{2,1},{3,2},{4,7},{5,4},{6,5},{7,6},{8,11},{9,8},{10,9... | collective-permute-start | bytes 122888 | tf_op jit(solution)/shard_map/ppermute | solution.py:20
  117.6 4.9 %collective-permute-start.14 = (f32[8,1280]{1,0:T(8,128)S(1)}, f32[8,1280]{1,0:T(8,128)S(1)}, u32[]{:S(2)}, u32[]{:S(2)}) collective-permute-start(f32[8,1280]{1,0:T(8,128)S(1)} %get-tuple-element.64.refs_0_), channel_id=1, source_target_pairs={{0,2},{1,3},{2,0},{3,1},{4,6},{5,7},{6,4},{7,5},{8,10},{9,11},{10,... | collective-permute-start | bytes 122888 | tf_op jit(solution)/shard_map/ppermute | solution.py:20
  117.8 5.8 %collective-permute-start.13 = (f32[8,1280]{1,0:T(8,128)S(1)}, f32[8,1280]{1,0:T(8,128)S(1)}, u32[]{:S(2)}, u32[]{:S(2)}) collective-permute-start(f32[8,1280]{1,0:T(8,128)S(1)} %get-tuple-element.64.refs_0_), channel_id=1, source_target_pairs={{0,1},{1,2},{2,3},{3,0},{4,5},{5,6},{6,7},{7,4},{8,9},{9,10},{10,1... | collective-permute-start | bytes 122888 | tf_op jit(solution)/shard_map/ppermute | solution.py:20
  123.6 6.8 %copy-start.11 = (bf16[2,64,1280]{2,1,0:T(8,128)(2,1)S(1)}, bf16[2,64,1280]{2,1,0:T(8,128)(2,1)}, u32[]{:S(2)}) copy-start(bf16[2,64,1280]{2,1,0:T(8,128)(2,1)} %param.7) | copy-start | bytes 983044
  123.6 6.8 %copy-start.17 = (bf16[128,1280]{1,0:T(8,128)(2,1)S(1)}, bf16[128,1280]{1,0:T(8,128)(2,1)}, u32[]{:S(2)}) copy-start(bf16[128,1280]{1,0:T(8,128)(2,1)} %copy-done.15) | copy-start | bytes 983044
  123.6 6.8 %copy-start.20 = (bf16[128,1280]{1,0:T(8,128)(2,1)S(1)}, bf16[128,1280]{1,0:T(8,128)(2,1)}, u32[]{:S(2)}) copy-start(bf16[128,1280]{1,0:T(8,128)(2,1)} %copy-done.18) | copy-start | bytes 983044
  127.5 7.3 %copy-start.40 = (bf16[64,1280]{1,0:T(8,128)(2,1)}, bf16[64,1280]{1,0:T(8,128)(2,1)S(1)}, u32[]{:S(2)}) copy-start(bf16[64,1280]{1,0:T(8,128)(2,1)S(1)} %get-tuple-element.78.refs_4_) | copy-start | bytes 491524
  127.5 10.3 %collective-permute-start.16 = (bf16[64,1280]{1,0:T(8,128)(2,1)}, bf16[64,1280]{1,0:T(8,128)(2,1)}, u32[]{:S(2)}, u32[]{:S(2)}) collective-permute-start(bf16[64,1280]{1,0:T(8,128)(2,1)} %get-tuple-element.71), channel_id=1, source_target_pairs={{0,3},{1,0},{2,1},{3,2},{4,7},{5,4},{6,5},{7,6},{8,11},{9,8},{10,9... | collective-permute-start | bytes 491528 | tf_op jit(solution)/shard_map/ppermute | solution.py:20
  129.0 13.7 %collective-permute-start.17 = (bf16[64,1280]{1,0:T(8,128)(2,1)}, bf16[64,1280]{1,0:T(8,128)(2,1)}, u32[]{:S(2)}, u32[]{:S(2)}) collective-permute-start(bf16[64,1280]{1,0:T(8,128)(2,1)} %get-tuple-element.72), channel_id=1, source_target_pairs={{0,2},{1,3},{2,0},{3,1},{4,6},{5,7},{6,4},{7,5},{8,10},{9,11},{10,... | collective-permute-start | bytes 491528 | tf_op jit(solution)/shard_map/ppermute | solution.py:20
  129.1 13.5 %collective-permute-start.18 = (bf16[64,1280]{1,0:T(8,128)(2,1)}, bf16[64,1280]{1,0:T(8,128)(2,1)}, u32[]{:S(2)}, u32[]{:S(2)}) collective-permute-start(bf16[64,1280]{1,0:T(8,128)(2,1)} %get-tuple-element.73), channel_id=1, source_target_pairs={{0,1},{1,2},{2,3},{3,0},{4,5},{5,6},{6,7},{7,4},{8,9},{9,10},{10,1... | collective-permute-start | bytes 491528 | tf_op jit(solution)/shard_map/ppermute | solution.py:20
  134.8 1.1 copy-start.21
  135.8 1.1 copy-start.23
  142.7 0.9 copy-start.14
  145.9 27.4 %copy-start.27 = (bf16[64,1280]{1,0:T(8,128)(2,1)}, bf16[64,1280]{1,0:T(8,128)(2,1)S(1)}, u32[]{:S(2)}) copy-start(bf16[64,1280]{1,0:T(8,128)(2,1)S(1)} %eps_gradient.1.refs_0_) | copy-start | bytes 491524
  145.9 5.8 %collective-permute-start.22 = (bf16[64,1280]{1,0:T(8,128)(2,1)S(1)}, bf16[64,1280]{1,0:T(8,128)(2,1)S(1)}, u32[]{:S(2)}, u32[]{:S(2)}) collective-permute-start(bf16[64,1280]{1,0:T(8,128)(2,1)S(1)} %eps_gradient.1.refs_0_), channel_id=1, source_target_pairs={{0,3},{1,0},{2,1},{3,2},{4,7},{5,4},{6,5},{7,6},{8,11},{9,8},{10,9... | collective-permute-start | bytes 491528 | tf_op jit(solution)/shard_map/ppermute | solution.py:20
  146.0 11.5 %collective-permute-start.20 = (bf16[64,1280]{1,0:T(8,128)(2,1)S(1)}, bf16[64,1280]{1,0:T(8,128)(2,1)S(1)}, u32[]{:S(2)}, u32[]{:S(2)}) collective-permute-start(bf16[64,1280]{1,0:T(8,128)(2,1)S(1)} %eps_gradient.1.refs_0_), channel_id=1, source_target_pairs={{0,1},{1,2},{2,3},{3,0},{4,5},{5,6},{6,7},{7,4},{8,9},{9,10},{10,1... | collective-permute-start | bytes 491528 | tf_op jit(solution)/shard_map/ppermute | solution.py:20
  148.0 14.2 %collective-permute-start.21 = (bf16[64,1280]{1,0:T(8,128)(2,1)S(1)}, bf16[64,1280]{1,0:T(8,128)(2,1)S(1)}, u32[]{:S(2)}, u32[]{:S(2)}) collective-permute-start(bf16[64,1280]{1,0:T(8,128)(2,1)S(1)} %eps_gradient.1.refs_0_), channel_id=1, source_target_pairs={{0,2},{1,3},{2,0},{3,1},{4,6},{5,7},{6,4},{7,5},{8,10},{9,11},{10,... | collective-permute-start | bytes 491528 | tf_op jit(solution)/shard_map/ppermute | solution.py:20
  151.7 21.6 %copy-start.29 = (bf16[64,1280]{1,0:T(8,128)(2,1)}, bf16[64,1280]{1,0:T(8,128)(2,1)S(1)}, u32[]{:S(2)}) copy-start(bf16[64,1280]{1,0:T(8,128)(2,1)S(1)} %collective-permute-done.22.refs_3_) | copy-start | bytes 491524
  157.5 15.8 %copy-start.31 = (bf16[64,1280]{1,0:T(8,128)(2,1)}, bf16[64,1280]{1,0:T(8,128)(2,1)S(1)}, u32[]{:S(2)}) copy-start(bf16[64,1280]{1,0:T(8,128)(2,1)S(1)} %collective-permute-done.20.refs_1_) | copy-start | bytes 491524
  157.5 15.7 %collective-permute-start.24 = (bf16[128,1280]{1,0:T(8,128)(2,1)S(1)}, bf16[128,1280]{1,0:T(8,128)(2,1)S(1)}, u32[]{:S(2)}, u32[]{:S(2)}) collective-permute-start(bf16[128,1280]{1,0:T(8,128)(2,1)S(1)} %pad_maximum_fusion), channel_id=1, source_target_pairs={{0,16},{16,0},{1,17},{17,1},{2,18},{18,2},{3,19},{19,3},{4,20},{20... | collective-permute-start | bytes 983048 | tf_op jit(solution)/shard_map/ppermute | solution.py:25
  159.5 11.3 %collective-permute-start.23 = (bf16[64,1280]{1,0:T(8,128)(2,1)S(1)}, bf16[64,1280]{1,0:T(8,128)(2,1)S(1)}, u32[]{:S(2)}, u32[]{:S(2)}) collective-permute-start(bf16[64,1280]{1,0:T(8,128)(2,1)S(1)} %eps_gradient.1.refs_0_), channel_id=1, source_target_pairs={{0,16},{16,0},{1,17},{17,1},{2,18},{18,2},{3,19},{19,3},{4,20},{20... | collective-permute-start | bytes 491528 | tf_op jit(solution)/shard_map/ppermute | solution.py:25
  162.2 10.5 %collective-permute-start.25 = (bf16[64,1280]{1,0:T(8,128)(2,1)S(1)}, bf16[64,1280]{1,0:T(8,128)(2,1)S(1)}, u32[]{:S(2)}, u32[]{:S(2)}) collective-permute-start(bf16[64,1280]{1,0:T(8,128)(2,1)S(1)} %collective-permute-done.21.refs_2_), channel_id=1, source_target_pairs={{0,16},{16,0},{1,17},{17,1},{2,18},{18,2},{3,19},{19,3},{4,20},{20... | collective-permute-start | bytes 491528 | tf_op jit(solution)/shard_map/ppermute | solution.py:25
  174.0 1.9 copy-start.5
  176.0 1.9 copy-start.8
  177.9 1.3 copy-start.22
  179.2 1.3 copy-start.24
  180.5 1.1 copy-start.26
  184.4 1.0 copy-start.34
  193.1 2.4 %collective-permute-start.26 = (bf16[2,160,1280]{2,1,0:T(8,128)(2,1)S(1)}, bf16[2,160,1280]{2,1,0:T(8,128)(2,1)S(1)}, u32[]{:S(2)}, u32[]{:S(2)}) collective-permute-start(bf16[2,160,1280]{2,1,0:T(8,128)(2,1)S(1)} %get-tuple-element.87), channel_id=1, source_target_pairs={{0,4},{4,0},{8,12},{12,8},{1,5},{5,1},{9,13},{13,9},{2,6},{6,2},{1... | collective-permute-start | bytes 2457608 | tf_op jit(solution)/shard_map/ppermute | solution.py:25
  193.2 3.7 %collective-permute-start.28 = (bf16[2,160,1280]{2,1,0:T(8,128)(2,1)S(1)}, bf16[2,160,1280]{2,1,0:T(8,128)(2,1)S(1)}, u32[]{:S(2)}, u32[]{:S(2)}) collective-permute-start(bf16[2,160,1280]{2,1,0:T(8,128)(2,1)S(1)} %get-tuple-element.91), channel_id=1, source_target_pairs={{0,4},{4,0},{8,12},{12,8},{1,5},{5,1},{9,13},{13,9},{2,6},{6,2},{1... | collective-permute-start | bytes 2457608 | tf_op jit(solution)/shard_map/ppermute | solution.py:25
  196.2 12.4 %collective-permute-start.27 = (bf16[160,1280]{1,0:T(8,128)(2,1)S(1)}, bf16[160,1280]{1,0:T(8,128)(2,1)S(1)}, u32[]{:S(2)}, u32[]{:S(2)}) collective-permute-start(bf16[160,1280]{1,0:T(8,128)(2,1)S(1)} %bitcast.44), channel_id=1, source_target_pairs={{0,8},{4,12},{8,0},{12,4},{1,9},{5,13},{9,1},{13,5},{2,10},{6,14},... | collective-permute-start | bytes 1228808 | tf_op jit(solution)/shard_map/ppermute | solution.py:20
  197.6 19.0 %collective-permute-start.29 = (bf16[160,1280]{1,0:T(8,128)(2,1)S(1)}, bf16[160,1280]{1,0:T(8,128)(2,1)S(1)}, u32[]{:S(2)}, u32[]{:S(2)}) collective-permute-start(bf16[160,1280]{1,0:T(8,128)(2,1)S(1)} %bitcast.45), channel_id=1, source_target_pairs={{0,8},{4,12},{8,0},{12,4},{1,9},{5,13},{9,1},{13,5},{2,10},{6,14},... | collective-permute-start | bytes 1228808 | tf_op jit(solution)/shard_map/ppermute | solution.py:20
  (29 other events, 23.1 us)
Sparse Core Ops, SparseCore 0:
  30.9 29.9 all-gather.3
  72.7 28.2 all-gather.5
  142.8 27.8 all-gather.7

commit v8 on v7

--- a/solution.py
+++ b/solution.py
@@ -29,15 +29,6 @@
     return [piece] + [rotated(piece, "tp", k) for k in range(1, lax.axis_size("tp"))]
 
 
-def own_share(weight):
-    rows = weight.shape[0] // lax.axis_size("dp")
-    return lax.dynamic_slice_in_dim(weight, lax.axis_index("dp") * rows, rows, 0)
-
-
-def joined(share):
-    return lax.all_gather(share, "dp", axis=0, tiled=True)
-
-
 def gelu_pair(value):
     cdf = 0.5 * (1.0 + lax.erf(value * (1.0 / math.sqrt(2.0))))
     density = jnp.exp(-0.5 * value * value) * (1.0 / math.sqrt(2.0 * math.pi))
@@ -68,16 +59,24 @@
 IN_SMEM = pl.BlockSpec(memory_space=pltpu.SMEM)
 
 
-def run(body, name, sel, operands, outs, scratch):
+IN_ANY = pl.BlockSpec(memory_space=pl.ANY)
+
+
+def run(body, name, sel, operands, outs, scratch, after=()):
+    used = 1 + len(operands)
+
+    def without_after(*refs):
+        body(*refs[:used], *refs[used + len(after) :])
+
     return pl.pallas_call(
-        body,
-        in_specs=[IN_SMEM] + [IN_VMEM] * len(operands),
+        without_after,
+        in_specs=[IN_SMEM] + [IN_VMEM] * len(operands) + [IN_ANY] * len(after),
         out_specs=[IN_VMEM] * len(outs),
         scratch_shapes=scratch,
         out_shape=outs,
         compiler_params=pltpu.CompilerParams(vmem_limit_bytes=VMEM_BYTES),
         name=name,
-    )(sel, *operands)
+    )(sel, *operands, *after)
 
 
 def bf16(*shape):
@@ -97,6 +96,42 @@
     @pl.when(sel_ref[0] != section)
     def _():
         work(*other)
+
+
+def share_body(group, sel_ref, weight, out):
+    rows = out.shape[0]
+    start = pl.multiple_of((sel_ref[3] % group) * rows, rows)
+    out[...] = weight[pl.ds(start, rows), :]
+
+
+def share(weight, group, sel, after):
+    rows, hidden = weight.shape
+    body = functools.partial(share_body, group)
+    return run(body, "share", sel, [weight], [bf16(rows // group, hidden)], [], after)[0]
+
+
+def stack_body(sel_ref, *refs):
+    for i, piece in enumerate(refs[:-1]):
+        refs[-1][i] = piece[...]
+
+
+def assemble_body(count, sel_ref, *refs):
+    pieces, beside, out = refs[:count], refs[count], refs[count + 1]
+    rows = pieces[0].shape[0]
+    for i, piece in enumerate(pieces):
+        for q, value in ((2 * i, piece[...]), (2 * i + 1, beside[i])):
+            place = (sel_ref[3] % (2 * count)) ^ q
+            out[pl.ds(pl.multiple_of(place * rows, rows), rows), :] = value
+
+
+def assembled(pieces, sel, after):
+    rows, hidden = pieces[0].shape
+    count = len(pieces)
+    stacked = run(stack_body, "stack", sel, pieces, [bf16(count, rows, hidden)], [], after)[0]
+    beside = swapped(stacked, "dp", 1)
+    body = functools.partial(assemble_body, count)
+    out = bf16(2 * count * rows, hidden)
+    return run(body, "assemble", sel, [*pieces, beside], [out], [])[0]
 
 
 def partial_body(count, sel_ref, *refs):
@@ -116,7 +151,7 @@
         stay[i] = acc[start + late : start + rows, :].astype(jnp.bfloat16)
 
 
-def block0_partials(parts, gain, w_in, w_out, sel):
+def block0_partials(parts, gain, w_in, w_out, sel, after):
     rows, width = parts[0].shape
     hidden, n = w_in.shape[1], len(parts)
     return run(
@@ -129,7 +164,19 @@
             pltpu.VMEM((n * rows, width), jnp.bfloat16),
             pltpu.VMEM((n * rows, width), jnp.float32),
         ],
-    )
+        after,
+    )
+
+
+def pick_body(sel_ref, stay, crossed, *outs):
+    for i, out in enumerate(outs):
+        out[...] = jnp.where(sel_ref[0] == 0, stay[i], crossed[i])
+
+
+def picked(stay, crossed, sel, after):
+    count, rows, width = stay.shape
+    outs = [bf16(rows, width)] * count
+    return run(pick_body, "pick", sel, [stay, crossed], outs, [], after)
 
 
 def denoise_body(tokens, count, sel_ref, *refs):
@@ -330,7 +377,7 @@
         out[at, :] = (ratio[at, :] * g_images.astype(jnp.float32)).astype(jnp.bfloat16)
 
 
-def eps_gradient(seen, g_mean, gain, ratio, sums, tokens, sel):
+def eps_gradient(seen, g_mean, gain, ratio, sums, tokens, sel, after):
     return run(
         functools.partial(eps_gradient_body, tokens, len(sums)),
         "eps_gradient",
@@ -338,6 +385,7 @@
         [seen, g_mean, gain, ratio, *sums],
         [bf16(*seen.shape)],
         [],
+        after,
     )[0]
 
 
@@ -424,7 +472,7 @@
     segment = lax.axis_index("sec")
     first = segment == 0
     dp = lax.axis_index("dp")
-    sel = jnp.stack([segment, dp % 2, dp // 2]).astype(jnp.int32)
+    sel = jnp.stack([segment, dp % 2, dp // 2, dp % 4]).astype(jnp.int32)
     own = (w_in[0], w_out[0])
 
     def my_half(value):
@@ -436,10 +484,9 @@
 
     flat = latents.reshape(count * tokens, width)
     lat_parts = gather_parts(flat)
-    got_in = swapped(own_share(own[0]), "sec", 1)
-    out_share, got_in, lat_parts[1], lat_parts[-1] = lax.optimization_barrier(
-        (own_share(own[1]), got_in, lat_parts[1], lat_parts[-1])
-    )
+    got_in = swapped(share(own[0], 4, sel, ()), "sec", 1)
+    across_in = swapped(got_in, "dp", 2)
+    out_share = share(own[1], 2, sel, (lat_parts[1], lat_parts[-1]))
     got_out = lax.ppermute(out_share, "sec", [(1, 0)])
 
     onehot = (
@@ -450,40 +497,44 @@
     near = [k for k in range(1, n_tp) if 2 * k != n_tp]
     rest = [0] + [k for k in range(1, n_tp) if 2 * k == n_tp]
     sums = [None] * n_tp
-    hop = got_in
+    before_kernel, before_pick = [got_in], []
     for ks in (near, rest):
         if ks:
-            operands, unused = lax.optimization_barrier(([lat_parts[k] for k in ks], hop))
-            stay, leave = block0_partials(operands, gains[:1], *own, sel)
+            stay, leave = block0_partials(
+                [lat_parts[k] for k in ks], gains[:1], *own, sel, before_kernel
+            )
             crossed = lax.ppermute(leave, "sec", [(0, 1)])
-            if ks is rest:
-                crossed, got_out, sums = lax.optimization_barrier((crossed, got_out, sums))
-            chosen = jnp.where(first, stay, crossed)
-            for i, k in enumerate(ks):
-                sums[k] = rotated(chosen[i], "tp", -k) if k else chosen[i]
-            hop = crossed
+            chosen = picked(stay, crossed, sel, before_pick)
+            for k, part in zip(ks, chosen):
+                sums[k] = rotated(part, "tp", -k) if k else part
+            before_kernel, before_pick = [crossed], [sums[k] for k in ks]
     mine_rows = denoised(flat, sigma, alpha, sums, tokens, sel)
 
-    other = (joined(got_in), joined(got_out))
     seen_parts = gather_parts(mine_rows)
+    other = (
+        assembled([got_in, across_in], sel, [sums[0]]),
+        assembled([got_out], sel, [sums[0]]),
+    )
     slopes1, pool = reward_forward(seen_parts, tokens, gains[1:], text_mine, own, other, sel)
     pools = gather_parts(pool)
     g_parts, g_mean = reward_back(pools, slopes1, tokens, own, other, sel)
 
     states = block0_state(lat_parts, gains[:1], own[0], other[0], sel)
-    late_share, unused = lax.optimization_barrier((out_share, mine_rows))
-    got_late = lax.ppermute(late_share, "sec", [(0, 1)])
+    got_late = lax.ppermute(share(own[1], 2, sel, [pool]), "sec", [(0, 1)])
 
     g_sums = [g_parts[0]] + [rotated(g_parts[k], "tp", -k) for k in range(1, n_tp)]
-    g_sums, states, got_late = lax.optimization_barrier((g_sums, states, got_late))
-    g_eps = eps_gradient(mine_rows, g_mean, gains[1:], -(sigma / alpha), g_sums, tokens, sel)
+    ratio = -(sigma / alpha)
+    g_eps = eps_gradient(
+        mine_rows, g_mean, gains[1:], ratio, g_sums, tokens, sel, [states[0]]
+    )
 
     g_mine = gather_parts(g_eps)
     pieces = list(g_mine)
     for ks in ([0], near, rest[1:]):
         if ks:
             pieces.append(swapped(jnp.concatenate([g_mine[k] for k in ks], 0), "sec", 1))
-    out_parts, in_parts = gradients(pieces, states, own[1], joined(got_late), sel)
+    late_out = assembled([got_late], sel, [g_mine[1], g_mine[-1]])
+    out_parts, in_parts = gradients(pieces, states, own[1], late_out, sel)
     grad_out, grad_in = sum_over_dp(*out_parts, sel), sum_over_dp(*in_parts, sel)
     return (grad_in, grad_out)
 

time: 225 us -> 193 us (0.86)
  local copies, waits for them, and re-layouts: 53 us -> 14.6 us
  Pallas kernels: 26.8 us -> 43.1 us
  between operations: 16.8 us -> 3.83 us
  waiting for transfers between devices: 77.5 us -> 82 us
    unnamed x120 -> x64, local copies, waits for them, and re-layouts: 48.3 us -> 13.4 us
    pallas_call x10 -> x21, Pallas kernels: 26.8 us -> 43.1 us  [run(): pl.pallas_call(without_after, in_specs=[IN_SMEM] + [IN_VMEM] * len(operan...]
    ppermute x20, starting transfers between devices: 25.3 us -> 30.7 us  [rotated(): lax.ppermute(value, axis, [(i, (i + steps) % count) for i in range(count)])]
    ppermute x6 -> x10, waiting for transfers between devices: 8.86 us -> 13.7 us  [swapped(): return lax.ppermute(value, axis, [(i, i ^ bit) for i in range(count)])]
    dynamic_slice x2 -> x0, local copies, waits for them, and re-layouts: 3.44 us -> none  [own_share(): lax.dynamic_slice_in_dim(weight, lax.axis_index('dp') * rows, rows, 0)]
    ppermute x2, starting transfers between devices: 8.65 us -> 6.22 us  [on_device(): crossed = lax.ppermute(leave, 'sec', [(0, 1)])]
    ppermute x6 -> x10, starting transfers between devices: 7.79 us -> 6.19 us  [swapped(): return lax.ppermute(value, axis, [(i, i ^ bit) for i in range(count)])]
  transfers between devices with their start and end apart: 33 -> 34, of which waited for: 21 -> 21; matrix products, arithmetic and copies ran while one was open for 3% -> 1% of each run, Pallas kernels for 10% -> 16%
where the time goes in v8:
time: 193 us
  waiting for transfers between devices  82 us (42%)
  starting transfers between devices  47.1 us (24%)
  Pallas kernels  43.1 us (22%)
  local copies, waits for them, and re-layouts  14.6 us (8%)
  between operations  3.83 us (2%)
  other arithmetic  2.02 us (1%)
    ppermute x20, waiting for transfers between devices, rotated(): lax.ppermute(value, axis, [(i, (i + steps) % count) for i in range(count)])  64.2 us
    pallas_call x21, Pallas kernels, run(): pl.pallas_call(without_after, in_specs=[IN_SMEM] + [IN_VMEM] * len(operan...  43.1 us
    ppermute x20, starting transfers between devices, rotated(): lax.ppermute(value, axis, [(i, (i + steps) % count) for i in range(count)])  30.7 us
    ppermute x10, waiting for transfers between devices, swapped(): return lax.ppermute(value, axis, [(i, i ^ bit) for i in range(count)])  13.7 us
    unnamed x64, local copies, waits for them, and re-layouts  13.4 us
    ppermute x2, starting transfers between devices, on_device(): crossed = lax.ppermute(leave, 'sec', [(0, 1)])  6.22 us
    ppermute x10, starting transfers between devices, swapped(): return lax.ppermute(value, axis, [(i, i ^ bit) for i in range(count)])  6.19 us
  transfers between devices with their start and end apart: 34, of which 21 were waited for; matrix products, arithmetic and copies ran while one was open for 1% of the time, Pallas kernels for 16%

profile of v8, /device:TPU:0, one launch (start us, length us, event | category | flops | bytes accessed | tf_op | source)
XLA Modules:
  0.0 192.8 jit_solution(8715052441241732155)
XLA Ops:
  0.6 3.1 %collective-permute-start.1 = (bf16[128,1280]{1,0:T(8,128)(2,1)}, bf16[128,1280]{1,0:T(8,128)(2,1)}, u32[]{:S(2)}, u32[]{:S(2)}) collective-permute-start(bf16[128,1280]{1,0:T(8,128)(2,1)} %bitcast.30), channel_id=1, source_target_pairs={{0,1},{1,2},{2,3},{3,0},{4,5},{5,6},{6,7},{7,4},{8,9},{9,10},{10,1... | collective-permute-start | bytes 983048 | tf_op jit(solution)/shard_map/ppermute | solution.py:20
  3.7 2.1 %collective-permute-start.2 = (bf16[128,1280]{1,0:T(8,128)(2,1)}, bf16[128,1280]{1,0:T(8,128)(2,1)}, u32[]{:S(2)}, u32[]{:S(2)}) collective-permute-start(bf16[128,1280]{1,0:T(8,128)(2,1)} %bitcast.31), channel_id=1, source_target_pairs={{0,3},{1,0},{2,1},{3,2},{4,7},{5,4},{6,5},{7,6},{8,11},{9,8},{10,9... | collective-permute-start | bytes 983048 | tf_op jit(solution)/shard_map/ppermute | solution.py:20
  5.9 1.9 copy-done.2
  8.4 1.7 collective-permute-start.3
  10.2 4.5 %collective-permute-done.1.refs_1_.refs_2_ = bf16[128,1280]{1,0:T(8,128)(2,1)} collective-permute-done((bf16[128,1280]{1,0:T(8,128)(2,1)}, bf16[128,1280]{1,0:T(8,128)(2,1)}, u32[]{:S(2)}, u32[]{:S(2)}) %collective-permute-start.1) | collective-permute-done | bytes 327712 | tf_op jit(solution)/shard_map/ppermute | solution.py:20
  14.7 5.6 %collective-permute-done.2.refs_2_.refs_3_.refs_4_ = bf16[128,1280]{1,0:T(8,128)(2,1)} collective-permute-done((bf16[128,1280]{1,0:T(8,128)(2,1)}, bf16[128,1280]{1,0:T(8,128)(2,1)}, u32[]{:S(2)}, u32[]{:S(2)}) %collective-permute-start.2) | collective-permute-done | bytes 327712 | tf_op jit(solution)/shard_map/ppermute | solution.py:20
  20.9 1.4 collective-permute-start.14
  22.4 1.4 collective-permute-start
  23.7 5.9 %collective-permute-done.3.refs_6_.refs_1_ = bf16[320,1280]{1,0:T(8,128)(2,1)S(1)} collective-permute-done((bf16[320,1280]{1,0:T(8,128)(2,1)S(1)}, bf16[320,1280]{1,0:T(8,128)(2,1)S(1)}, u32[]{:S(2)}, u32[]{:S(2)}) %collective-permute-start.3) | collective-permute-done | bytes 819232 | tf_op jit(solution)/shard_map/ppermute | solution.py:25
  29.7 1.7 collective-permute-start.12
  31.4 3.5 %block0_partial.2 = (bf16[2,64,1280]{2,1,0:T(8,128)(2,1)S(1)}, bf16[2,64,1280]{2,1,0:T(8,128)(2,1)S(1)}) custom-call(s32[4]{0:T(128)S(1)} %pad_add_fusion.refs_0_, bf16[128,1280]{1,0:T(8,128)(2,1)} %collective-permute-done.1.refs_1_.refs_2_, bf16[128,1280]{1,0:T(8,128)(2,1)} %collective-permute-done.2.refs_2_.refs_3_.refs_4_, ...), custom_call_target="tpu_custom_call" | custom-call | tf_op jit(solution)/shard_map/block0_partial/pallas_call | solution.py:71
  34.8 1.8 collective-permute-start.4
  36.6 2.7 %collective-permute-done.refs_2_.refs_3_ = bf16[128,1280]{1,0:T(8,128)(2,1)S(1)} collective-permute-done((bf16[128,1280]{1,0:T(8,128)(2,1)S(1)}, bf16[128,1280]{1,0:T(8,128)(2,1)S(1)}, u32[]{:S(2)}, u32[]{:S(2)}) %collective-permute-start) | collective-permute-done | bytes 327712 | tf_op jit(solution)/shard_map/ppermute | solution.py:20
  39.3 2.6 %collective-permute-done.4.refs_6_.refs_2_ = bf16[2,64,1280]{2,1,0:T(8,128)(2,1)S(1)} collective-permute-done((bf16[2,64,1280]{2,1,0:T(8,128)(2,1)S(1)}, bf16[2,64,1280]{2,1,0:T(8,128)(2,1)S(1)}, u32[]{:S(2)}, u32[]{:S(2)}) %collective-permute-start.4) | collective-permute-done | bytes 327712 | tf_op jit(solution)/shard_map/ppermute | solution.py:506
  41.9 2.9 %block0_partial.3 = (bf16[2,64,1280]{2,1,0:T(8,128)(2,1)S(1)}, bf16[2,64,1280]{2,1,0:T(8,128)(2,1)S(1)}) custom-call(s32[4]{0:T(128)S(1)} %pad_add_fusion.refs_0_, bf16[128,1280]{1,0:T(8,128)(2,1)S(1)} %bitcast.33, bf16[128,1280]{1,0:T(8,128)(2,1)S(1)} %collective-permute-done.refs_2_.refs_3_, f32[1,1280]{1,0:T(1,128)S(1)} %get-tuple-element.61.refs_3_.refs_5_, ...), custom_call_target="tpu_custom_call" | custom-call | tf_op jit(solution)/shard_map/block0_partial/pallas_call | solution.py:71
  44.9 4.4 %collective-permute-start.5 = (bf16[2,64,1280]{2,1,0:T(8,128)(2,1)S(1)}, bf16[2,64,1280]{2,1,0:T(8,128)(2,1)S(1)}, u32[]{:S(2)}, u32[]{:S(2)}) collective-permute-start(bf16[2,64,1280]{2,1,0:T(8,128)(2,1)S(1)} %get-tuple-element.33), channel_id=1, source_target_pairs={{0,16},{1,17},{2,18},{3,19},{4,20},{5,21},{6,22},{7,23},{8,24},{9,... | collective-permute-start | bytes 983048 | tf_op jit(solution)/shard_map/ppermute | solution.py:506
  49.9 1.6 collective-permute-start.6
  52.0 4.2 %collective-permute-done.6.refs_3_.refs_5_ = bf16[64,1280]{1,0:T(8,128)(2,1)S(1)} collective-permute-done((bf16[64,1280]{1,0:T(8,128)(2,1)S(1)}, bf16[64,1280]{1,0:T(8,128)(2,1)S(1)}, u32[]{:S(2)}, u32[]{:S(2)}) %collective-permute-start.6) | collective-permute-done | bytes 163872 | tf_op jit(solution)/shard_map/ppermute | solution.py:20
  56.1 2.4 %collective-permute-done.7.refs_4_.refs_7_ = bf16[64,1280]{1,0:T(8,128)(2,1)S(1)} collective-permute-done((bf16[64,1280]{1,0:T(8,128)(2,1)S(1)}, bf16[64,1280]{1,0:T(8,128)(2,1)S(1)}, u32[]{:S(2)}, u32[]{:S(2)}) %collective-permute-start.7) | collective-permute-done | bytes 163872 | tf_op jit(solution)/shard_map/ppermute | solution.py:20
  58.6 1.3 pick.3
  59.9 1.8 stack.23
  61.8 1.5 collective-permute-done.14.refs_1_
  63.3 1.9 stack.24
  69.8 5.8 %collective-permute-done.8.refs_6_ = bf16[64,1280]{1,0:T(8,128)(2,1)} collective-permute-done((bf16[64,1280]{1,0:T(8,128)(2,1)}, bf16[64,1280]{1,0:T(8,128)(2,1)}, u32[]{:S(2)}, u32[]{:S(2)}) %collective-permute-start.8) | collective-permute-done | bytes 163872 | tf_op jit(solution)/shard_map/ppermute | solution.py:20
  75.7 1.0 copy-done.15
  76.6 0.9 copy-done.18
  79.4 1.1 denoise.1.refs_1_
  80.5 2.5 %collective-permute-start.11 = (bf16[64,1280]{1,0:T(8,128)(2,1)S(1)}, bf16[64,1280]{1,0:T(8,128)(2,1)S(1)}, u32[]{:S(2)}, u32[]{:S(2)}) collective-permute-start(bf16[64,1280]{1,0:T(8,128)(2,1)S(1)} %denoise.1.refs_1_), channel_id=1, source_target_pairs={{0,3},{1,0},{2,1},{3,2},{4,7},{5,4},{6,5},{7,6},{8,11},{9,8},{10,9... | collective-permute-start | bytes 491528 | tf_op jit(solution)/shard_map/ppermute | solution.py:20
  83.7 1.3 copy-done.13
  85.0 1.7 assemble.3.refs_9_.refs_11_.refs_7_
  86.7 2.9 %assemble.4.refs_10_.refs_12_ = bf16[1280,1280]{1,0:T(8,128)(2,1)S(1)} custom-call(s32[4]{0:T(128)S(1)} %pad_add_fusion.refs_0_, bf16[640,1280]{1,0:T(8,128)(2,1)S(1)} %copy-done.11, bf16[1,640,1280]{2,1,0:T(8,128)(2,1)} %collective-permute-done.15.refs_2_), custom_call_target="tpu_custom_call" | custom-call | tf_op jit(solution)/shard_map/assemble/pallas_call | solution.py:71
  89.6 2.1 %collective-permute-done.10.refs_3_ = bf16[64,1280]{1,0:T(8,128)(2,1)S(1)} collective-permute-done((bf16[64,1280]{1,0:T(8,128)(2,1)S(1)}, bf16[64,1280]{1,0:T(8,128)(2,1)S(1)}, u32[]{:S(2)}, u32[]{:S(2)}) %collective-permute-start.10) | collective-permute-done | bytes 163872 | tf_op jit(solution)/shard_map/ppermute | solution.py:20
  91.7 3.1 %collective-permute-done.11.refs_4_ = bf16[64,1280]{1,0:T(8,128)(2,1)S(1)} collective-permute-done((bf16[64,1280]{1,0:T(8,128)(2,1)S(1)}, bf16[64,1280]{1,0:T(8,128)(2,1)S(1)}, u32[]{:S(2)}, u32[]{:S(2)}) %collective-permute-start.11) | collective-permute-done | bytes 163872 | tf_op jit(solution)/shard_map/ppermute | solution.py:20
  94.7 3.1 %reward_forward.1 = (bf16[64,1280]{1,0:T(8,128)(2,1)S(1)}, bf16[64,1280]{1,0:T(8,128)(2,1)S(1)}, bf16[64,1280]{1,0:T(8,128)(2,1)S(1)}, bf16[64,1280]{1,0:T(8,128)(2,1)S(1)}, f32[8,1280]{1,0:T(8,128)S(1)}) custom-call(s32[4]{0:T(128)S(1)} %pad_add_fusion.refs_0_, bf16[64,1280]{1,0:T(8,128)(2,1)S(1)} %denoise.1.refs_1_, ...), custom_call_target="tpu_custom_call" | custom-call | tf_op jit(solution)/shard_map/reward_forward/pallas_call | solution.py:71
  97.9 1.9 share.5
  99.8 2.6 %collective-permute-start.28 = (bf16[640,1280]{1,0:T(8,128)(2,1)}, bf16[640,1280]{1,0:T(8,128)(2,1)}, u32[]{:S(2)}, u32[]{:S(2)}) collective-permute-start(bf16[640,1280]{1,0:T(8,128)(2,1)} %share.5), channel_id=1, source_target_pairs={{0,16},{1,17},{2,18},{3,19},{4,20},{5,21},{6,22},{7,23},{8,24},{9,... | collective-permute-start | bytes 4915208 | tf_op jit(solution)/shard_map/ppermute | solution.py:523
  102.4 3.8 %collective-permute-start.16 = (f32[8,1280]{1,0:T(8,128)S(1)}, f32[8,1280]{1,0:T(8,128)S(1)}, u32[]{:S(2)}, u32[]{:S(2)}) collective-permute-start(f32[8,1280]{1,0:T(8,128)S(1)} %get-tuple-element.39.refs_1_.refs_2_), channel_id=1, source_target_pairs={{0,1},{1,2},{2,3},{3,0},{4,5},{5,6},{6,7},{7,4},{8,9},{9,10},{10,1... | collective-permute-start | bytes 122888 | tf_op jit(solution)/shard_map/ppermute | solution.py:20
  106.2 2.8 %collective-permute-start.18 = (f32[8,1280]{1,0:T(8,128)S(1)}, f32[8,1280]{1,0:T(8,128)S(1)}, u32[]{:S(2)}, u32[]{:S(2)}) collective-permute-start(f32[8,1280]{1,0:T(8,128)S(1)} %get-tuple-element.39.refs_1_.refs_2_), channel_id=1, source_target_pairs={{0,3},{1,0},{2,1},{3,2},{4,7},{5,4},{6,5},{7,6},{8,11},{9,8},{10,9... | collective-permute-start | bytes 122888 | tf_op jit(solution)/shard_map/ppermute | solution.py:20
  109.0 2.5 %collective-permute-done.17.refs_3_ = f32[8,1280]{1,0:T(8,128)S(1)} collective-permute-done((f32[8,1280]{1,0:T(8,128)S(1)}, f32[8,1280]{1,0:T(8,128)S(1)}, u32[]{:S(2)}, u32[]{:S(2)}) %collective-permute-start.17) | collective-permute-done | bytes 40992 | tf_op jit(solution)/shard_map/ppermute | solution.py:20
  111.5 3.8 %reward_back.1 = (bf16[64,1280]{1,0:T(8,128)(2,1)S(1)}, bf16[64,1280]{1,0:T(8,128)(2,1)}, bf16[64,1280]{1,0:T(8,128)(2,1)}, bf16[64,1280]{1,0:T(8,128)(2,1)}, f32[8,1280]{1,0:T(8,128)S(1)}) custom-call(s32[4]{0:T(128)S(1)} %pad_add_fusion.refs_0_, f32[8,1280]{1,0:T(8,128)S(1)} %get-tuple-element.39.refs_1_.refs_2_, ...), custom_call_target="tpu_custom_call" | custom-call | tf_op jit(solution)/shard_map/reward_back/pallas_call | solution.py:71
  115.9 3.3 %collective-permute-start.19 = (bf16[64,1280]{1,0:T(8,128)(2,1)}, bf16[64,1280]{1,0:T(8,128)(2,1)}, u32[]{:S(2)}, u32[]{:S(2)}) collective-permute-start(bf16[64,1280]{1,0:T(8,128)(2,1)} %get-tuple-element.46), channel_id=1, source_target_pairs={{0,3},{1,0},{2,1},{3,2},{4,7},{5,4},{6,5},{7,6},{8,11},{9,8},{10,9... | collective-permute-start | bytes 491528 | tf_op jit(solution)/shard_map/ppermute | solution.py:20
  119.9 1.9 copy-done.5
  121.8 1.9 copy-done.7
  123.7 1.0 copy-done.16
  124.7 1.0 copy-done.22
  125.7 4.5 %block0_state.1 = (bf16[512,1280]{1,0:T(8,128)(2,1)S(1)}, bf16[512,1280]{1,0:T(8,128)(2,1)S(1)}, bf16[640,512]{1,0:T(8,128)(2,1)S(1)}) custom-call(s32[4]{0:T(128)S(1)} %pad_add_fusion.refs_0_, bf16[128,1280]{1,0:T(8,128)(2,1)S(1)} %bitcast.35, bf16[128,1280]{1,0:T(8,128)(2,1)} %collective-permute-done.1.refs_1_.refs_2_, bf16[128,1280]{1,0:T(8,128)(2,1)S(1)} %copy-done.22, ...), custom_call_target="tpu_custom_call" | custom-call | tf_op jit(solution)/shard_map/block0_state/pallas_call | solution.py:71
  130.2 2.4 %collective-permute-done.20.refs_7_ = bf16[64,1280]{1,0:T(8,128)(2,1)} collective-permute-done((bf16[64,1280]{1,0:T(8,128)(2,1)}, bf16[64,1280]{1,0:T(8,128)(2,1)}, u32[]{:S(2)}, u32[]{:S(2)}) %collective-permute-start.20) | collective-permute-done | bytes 163872 | tf_op jit(solution)/shard_map/ppermute | solution.py:20
  132.6 1.3 eps_gradient.1.refs_1_
  134.6 3.2 %collective-permute-start.24 = (bf16[64,1280]{1,0:T(8,128)(2,1)S(1)}, bf16[64,1280]{1,0:T(8,128)(2,1)S(1)}, u32[]{:S(2)}, u32[]{:S(2)}) collective-permute-start(bf16[64,1280]{1,0:T(8,128)(2,1)S(1)} %eps_gradient.1.refs_1_), channel_id=1, source_target_pairs={{0,3},{1,0},{2,1},{3,2},{4,7},{5,4},{6,5},{7,6},{8,11},{9,8},{10,9... | collective-permute-start | bytes 491528 | tf_op jit(solution)/shard_map/ppermute | solution.py:20
  137.8 4.5 %collective-permute-done.22.refs_2_ = bf16[64,1280]{1,0:T(8,128)(2,1)S(1)} collective-permute-done((bf16[64,1280]{1,0:T(8,128)(2,1)S(1)}, bf16[64,1280]{1,0:T(8,128)(2,1)S(1)}, u32[]{:S(2)}, u32[]{:S(2)}) %collective-permute-start.22) | collective-permute-done | bytes 163872 | tf_op jit(solution)/shard_map/ppermute | solution.py:20
  143.1 1.5 stack.25
  144.7 1.7 collective-permute-start.23
  146.5 2.0 %collective-permute-start.25 = (bf16[64,1280]{1,0:T(8,128)(2,1)S(1)}, bf16[64,1280]{1,0:T(8,128)(2,1)S(1)}, u32[]{:S(2)}, u32[]{:S(2)}) collective-permute-start(bf16[64,1280]{1,0:T(8,128)(2,1)S(1)} %eps_gradient.1.refs_1_), channel_id=1, source_target_pairs={{0,16},{16,0},{1,17},{17,1},{2,18},{18,2},{3,19},{19,3},{4,20},{20... | collective-permute-start | bytes 491528 | tf_op jit(solution)/shard_map/ppermute | solution.py:25
  148.5 7.2 %collective-permute-done.23.refs_3_ = bf16[64,1280]{1,0:T(8,128)(2,1)S(1)} collective-permute-done((bf16[64,1280]{1,0:T(8,128)(2,1)S(1)}, bf16[64,1280]{1,0:T(8,128)(2,1)S(1)}, u32[]{:S(2)}, u32[]{:S(2)}) %collective-permute-start.23) | collective-permute-done | bytes 163872 | tf_op jit(solution)/shard_map/ppermute | solution.py:20
  155.7 1.7 assemble.5.refs_12_
  157.4 3.1 %collective-permute-done.25.refs_5_ = bf16[64,1280]{1,0:T(8,128)(2,1)S(1)} collective-permute-done((bf16[64,1280]{1,0:T(8,128)(2,1)S(1)}, bf16[64,1280]{1,0:T(8,128)(2,1)S(1)}, u32[]{:S(2)}, u32[]{:S(2)}) %collective-permute-start.25) | collective-permute-done | bytes 163872 | tf_op jit(solution)/shard_map/ppermute | solution.py:25
  160.6 2.7 %collective-permute-done.27.refs_7_ = bf16[64,1280]{1,0:T(8,128)(2,1)S(1)} collective-permute-done((bf16[64,1280]{1,0:T(8,128)(2,1)S(1)}, bf16[64,1280]{1,0:T(8,128)(2,1)S(1)}, u32[]{:S(2)}, u32[]{:S(2)}) %collective-permute-start.27) | collective-permute-done | bytes 163872 | tf_op jit(solution)/shard_map/ppermute | solution.py:25
  163.3 5.0 %gradients.1 = (bf16[2,160,1280]{2,1,0:T(8,128)(2,1)S(1)}, bf16[2,160,1280]{2,1,0:T(8,128)(2,1)S(1)}, bf16[2,160,1280]{2,1,0:T(8,128)(2,1)S(1)}, bf16[2,160,1280]{2,1,0:T(8,128)(2,1)S(1)}) custom-call(s32[4]{0:T(128)S(1)} %pad_add_fusion.refs_0_, bf16[64,1280]{1,0:T(8,128)(2,1)S(1)} %eps_gradient.1.refs_1_, ...), custom_call_target="tpu_custom_call" | custom-call | tf_op jit(solution)/shard_map/gradients/pallas_call | solution.py:71
  168.9 1.8 collective-permute-done.32.refs_2_
  171.4 1.6 collective-permute-start.33
  174.3 9.5 %collective-permute-done.33 = bf16[160,1280]{1,0:T(8,128)(2,1)S(1)} collective-permute-done((bf16[160,1280]{1,0:T(8,128)(2,1)S(1)}, bf16[160,1280]{1,0:T(8,128)(2,1)S(1)}, u32[]{:S(2)}, u32[]{:S(2)}) %collective-permute-start.33) | collective-permute-done | bytes 409632 | tf_op jit(solution)/shard_map/ppermute | solution.py:20
  183.8 1.0 convert_add_fusion
  184.8 7.0 %collective-permute-done.31 = bf16[160,1280]{1,0:T(8,128)(2,1)S(1)} collective-permute-done((bf16[160,1280]{1,0:T(8,128)(2,1)S(1)}, bf16[160,1280]{1,0:T(8,128)(2,1)S(1)}, u32[]{:S(2)}, u32[]{:S(2)}) %collective-permute-start.31) | collective-permute-done | bytes 409632 | tf_op jit(solution)/shard_map/ppermute | solution.py:20
  191.8 1.0 convert_add_fusion.1
  (100 shorter events, 12.4 us)
Async XLA Ops:
  0.6 82.9 %copy-start = (bf16[64,1280]{1,0:T(8,128)(2,1)S(1)}, bf16[64,1280]{1,0:T(8,128)(2,1)}, u32[]{:S(2)}) copy-start(bf16[64,1280]{1,0:T(8,128)(2,1)} %param.10) | copy-start | bytes 491524
  0.6 14.0 %collective-permute-start.1 = (bf16[128,1280]{1,0:T(8,128)(2,1)}, bf16[128,1280]{1,0:T(8,128)(2,1)}, u32[]{:S(2)}, u32[]{:S(2)}) collective-permute-start(bf16[128,1280]{1,0:T(8,128)(2,1)} %bitcast.30), channel_id=1, source_target_pairs={{0,1},{1,2},{2,3},{3,0},{4,5},{5,6},{6,7},{7,4},{8,9},{9,10},{10,1... | collective-permute-start | bytes 983048 | tf_op jit(solution)/shard_map/ppermute | solution.py:20
  3.7 16.5 %collective-permute-start.2 = (bf16[128,1280]{1,0:T(8,128)(2,1)}, bf16[128,1280]{1,0:T(8,128)(2,1)}, u32[]{:S(2)}, u32[]{:S(2)}) collective-permute-start(bf16[128,1280]{1,0:T(8,128)(2,1)} %bitcast.31), channel_id=1, source_target_pairs={{0,3},{1,0},{2,1},{3,2},{4,7},{5,4},{6,5},{7,6},{8,11},{9,8},{10,9... | collective-permute-start | bytes 983048 | tf_op jit(solution)/shard_map/ppermute | solution.py:20
  5.9 1.9 %copy-start.2 = (bf16[1,1280,1280]{2,1,0:T(8,128)(2,1)S(1)}, bf16[1,1280,1280]{2,1,0:T(8,128)(2,1)}, u32[]{:S(2)}) copy-start(bf16[1,1280,1280]{2,1,0:T(8,128)(2,1)} %param.12) | copy-start | bytes 9830404
  7.8 12.4 %copy-start.1 = (bf16[1,1280,1280]{2,1,0:T(8,128)(2,1)S(1)}, bf16[1,1280,1280]{2,1,0:T(8,128)(2,1)}, u32[]{:S(2)}) copy-start(bf16[1,1280,1280]{2,1,0:T(8,128)(2,1)} %param.13) | copy-start | bytes 9830404
  8.4 21.2 %collective-permute-start.3 = (bf16[320,1280]{1,0:T(8,128)(2,1)S(1)}, bf16[320,1280]{1,0:T(8,128)(2,1)S(1)}, u32[]{:S(2)}, u32[]{:S(2)}) collective-permute-start(bf16[320,1280]{1,0:T(8,128)(2,1)S(1)} %share.3), channel_id=1, source_target_pairs={{0,16},{16,0},{1,17},{17,1},{2,18},{18,2},{3,19},{19,3},{4,20},{20... | collective-permute-start | bytes 2457608 | tf_op jit(solution)/shard_map/ppermute | solution.py:25
  20.2 2.1 %copy-start.14 = (bf16[2,64,1280]{2,1,0:T(8,128)(2,1)S(1)}, bf16[2,64,1280]{2,1,0:T(8,128)(2,1)}, u32[]{:S(2)}) copy-start(bf16[2,64,1280]{2,1,0:T(8,128)(2,1)} %param.7) | copy-start | bytes 983044
  20.2 11.1 %copy-start.29 = (f32[2,1280]{1,0:T(2,128)S(1)}, f32[2,1280]{1,0:T(2,128)}, u32[]{:S(2)}) copy-start(f32[2,1280]{1,0:T(2,128)} %param.11) | copy-start | bytes 30724
  20.2 11.1 %copy-start.3 = (bf16[1,1280,1280]{2,1,0:T(8,128)(2,1)S(1)}, bf16[1,1280,1280]{2,1,0:T(8,128)(2,1)}, u32[]{:S(2)}) copy-start(bf16[1,1280,1280]{2,1,0:T(8,128)(2,1)} %param.12) | copy-start | bytes 9830404
  20.9 42.4 %collective-permute-start.14 = (bf16[640,1280]{1,0:T(8,128)(2,1)S(1)}, bf16[640,1280]{1,0:T(8,128)(2,1)S(1)}, u32[]{:S(2)}, u32[]{:S(2)}) collective-permute-start(bf16[640,1280]{1,0:T(8,128)(2,1)S(1)} %share.4), channel_id=1, source_target_pairs={{16,0},{17,1},{18,2},{19,3},{20,4},{21,5},{22,6},{23,7},{24,8},{25... | collective-permute-start | bytes 4915208 | tf_op jit(solution)/shard_map/ppermute | solution.py:490
  22.4 17.0 %collective-permute-start = (bf16[128,1280]{1,0:T(8,128)(2,1)S(1)}, bf16[128,1280]{1,0:T(8,128)(2,1)S(1)}, u32[]{:S(2)}, u32[]{:S(2)}) collective-permute-start(bf16[128,1280]{1,0:T(8,128)(2,1)S(1)} %bitcast.32), channel_id=1, source_target_pairs={{0,2},{1,3},{2,0},{3,1},{4,6},{5,7},{6,4},{7,5},{8,10},{9,11},{10,... | collective-permute-start | bytes 983048 | tf_op jit(solution)/shard_map/ppermute | solution.py:20
  29.7 30.2 %copy-start.8 = (bf16[320,1280]{1,0:T(8,128)(2,1)}, bf16[320,1280]{1,0:T(8,128)(2,1)S(1)}, u32[]{:S(2)}) copy-start(bf16[320,1280]{1,0:T(8,128)(2,1)S(1)} %collective-permute-done.3.refs_6_.refs_1_) | copy-start | bytes 2457604
  29.7 30.2 %collective-permute-start.12 = (bf16[320,1280]{1,0:T(8,128)(2,1)S(1)}, bf16[320,1280]{1,0:T(8,128)(2,1)S(1)}, u32[]{:S(2)}, u32[]{:S(2)}) collective-permute-start(bf16[320,1280]{1,0:T(8,128)(2,1)S(1)} %collective-permute-done.3.refs_6_.refs_1_), channel_id=1, source_target_pairs={{0,8},{4,12},{8,0},{12,4},{1,9},{5,13},{9,1},{13,5},{2,10},{6,14},... | collective-permute-start | bytes 2457608 | tf_op jit(solution)/shard_map/ppermute | solution.py:25
  34.8 7.1 %collective-permute-start.4 = (bf16[2,64,1280]{2,1,0:T(8,128)(2,1)S(1)}, bf16[2,64,1280]{2,1,0:T(8,128)(2,1)S(1)}, u32[]{:S(2)}, u32[]{:S(2)}) collective-permute-start(bf16[2,64,1280]{2,1,0:T(8,128)(2,1)S(1)} %get-tuple-element.31), channel_id=1, source_target_pairs={{0,16},{1,17},{2,18},{3,19},{4,20},{5,21},{6,22},{7,23},{8,24},{9,... | collective-permute-start | bytes 983048 | tf_op jit(solution)/shard_map/ppermute | solution.py:506
  39.3 5.5 %copy-start.21 = (bf16[128,1280]{1,0:T(8,128)(2,1)}, bf16[128,1280]{1,0:T(8,128)(2,1)S(1)}, u32[]{:S(2)}) copy-start(bf16[128,1280]{1,0:T(8,128)(2,1)S(1)} %collective-permute-done.refs_2_.refs_3_) | copy-start | bytes 983044
  44.9 13.7 %collective-permute-start.5 = (bf16[2,64,1280]{2,1,0:T(8,128)(2,1)S(1)}, bf16[2,64,1280]{2,1,0:T(8,128)(2,1)S(1)}, u32[]{:S(2)}, u32[]{:S(2)}) collective-permute-start(bf16[2,64,1280]{2,1,0:T(8,128)(2,1)S(1)} %get-tuple-element.33), channel_id=1, source_target_pairs={{0,16},{1,17},{2,18},{3,19},{4,20},{5,21},{6,22},{7,23},{8,24},{9,... | collective-permute-start | bytes 983048 | tf_op jit(solution)/shard_map/ppermute | solution.py:506
  49.9 6.3 %collective-permute-start.6 = (bf16[64,1280]{1,0:T(8,128)(2,1)S(1)}, bf16[64,1280]{1,0:T(8,128)(2,1)S(1)}, u32[]{:S(2)}, u32[]{:S(2)}) collective-permute-start(bf16[64,1280]{1,0:T(8,128)(2,1)S(1)} %get-tuple-element.35), channel_id=1, source_target_pairs={{0,3},{1,0},{2,1},{3,2},{4,7},{5,4},{6,5},{7,6},{8,11},{9,8},{10,9... | collective-permute-start | bytes 491528 | tf_op jit(solution)/shard_map/ppermute | solution.py:20
  51.5 7.1 %collective-permute-start.7 = (bf16[64,1280]{1,0:T(8,128)(2,1)S(1)}, bf16[64,1280]{1,0:T(8,128)(2,1)S(1)}, u32[]{:S(2)}, u32[]{:S(2)}) collective-permute-start(bf16[64,1280]{1,0:T(8,128)(2,1)S(1)} %get-tuple-element.36), channel_id=1, source_target_pairs={{0,1},{1,2},{2,3},{3,0},{4,5},{5,6},{6,7},{7,4},{8,9},{9,10},{10,1... | collective-permute-start | bytes 491528 | tf_op jit(solution)/shard_map/ppermute | solution.py:20
  56.1 5.5 %copy-start.23 = (bf16[64,1280]{1,0:T(8,128)(2,1)}, bf16[64,1280]{1,0:T(8,128)(2,1)S(1)}, u32[]{:S(2)}) copy-start(bf16[64,1280]{1,0:T(8,128)(2,1)S(1)} %collective-permute-done.6.refs_3_.refs_5_) | copy-start | bytes 491524
  58.6 3.1 %copy-start.25 = (bf16[64,1280]{1,0:T(8,128)(2,1)}, bf16[64,1280]{1,0:T(8,128)(2,1)S(1)}, u32[]{:S(2)}) copy-start(bf16[64,1280]{1,0:T(8,128)(2,1)S(1)} %collective-permute-done.7.refs_4_.refs_7_) | copy-start | bytes 491524
  59.8 3.5 %copy-start.17 = (bf16[64,1280]{1,0:T(8,128)(2,1)}, bf16[64,1280]{1,0:T(8,128)(2,1)S(1)}, u32[]{:S(2)}) copy-start(bf16[64,1280]{1,0:T(8,128)(2,1)S(1)} %get-tuple-element.37.refs_4_.refs_3_.refs_2_) | copy-start | bytes 491524
  59.9 1.8 copy-start.12
  61.7 4.2 %copy-start.30 = (s32[2]{0:T(128)S(1)}, s32[2]{0:T(128)}, u32[]{:S(2)}) copy-start(s32[2]{0:T(128)} %param.8) | copy-start | bytes 28
  61.7 6.2 %copy-start.31 = (s32[2]{0:T(128)S(1)}, s32[2]{0:T(128)}, u32[]{:S(2)}) copy-start(s32[2]{0:T(128)} %param.9) | copy-start | bytes 28
  61.7 22.0 %collective-permute-start.13 = (bf16[2,320,1280]{2,1,0:T(8,128)(2,1)}, bf16[2,320,1280]{2,1,0:T(8,128)(2,1)}, u32[]{:S(2)}, u32[]{:S(2)}) collective-permute-start(bf16[2,320,1280]{2,1,0:T(8,128)(2,1)} %stack.23), channel_id=1, source_target_pairs={{0,4},{4,0},{8,12},{12,8},{1,5},{5,1},{9,13},{13,9},{2,6},{6,2},{1... | collective-permute-start | bytes 4915208 | tf_op jit(solution)/shard_map/ppermute | solution.py:25
  63.3 1.9 copy-start.10
  65.2 21.5 %collective-permute-start.15 = (bf16[1,640,1280]{2,1,0:T(8,128)(2,1)}, bf16[1,640,1280]{2,1,0:T(8,128)(2,1)}, u32[]{:S(2)}, u32[]{:S(2)}) collective-permute-start(bf16[1,640,1280]{2,1,0:T(8,128)(2,1)} %stack.24), channel_id=1, source_target_pairs={{0,4},{4,0},{8,12},{12,8},{1,5},{5,1},{9,13},{13,9},{2,6},{6,2},{1... | collective-permute-start | bytes 4915208 | tf_op jit(solution)/shard_map/ppermute | solution.py:25
  65.2 10.4 %collective-permute-start.8 = (bf16[64,1280]{1,0:T(8,128)(2,1)}, bf16[64,1280]{1,0:T(8,128)(2,1)}, u32[]{:S(2)}, u32[]{:S(2)}) collective-permute-start(bf16[64,1280]{1,0:T(8,128)(2,1)} %get-tuple-element.38), channel_id=1, source_target_pairs={{0,2},{1,3},{2,0},{3,1},{4,6},{5,7},{6,4},{7,5},{8,10},{9,11},{10,... | collective-permute-start | bytes 491528 | tf_op jit(solution)/shard_map/ppermute | solution.py:20
  66.5 17.3 %copy-start.9 = (bf16[320,1280]{1,0:T(8,128)(2,1)S(1)}, bf16[320,1280]{1,0:T(8,128)(2,1)}, u32[]{:S(2)}) copy-start(bf16[320,1280]{1,0:T(8,128)(2,1)} %copy-done.8) | copy-start | bytes 2457604
  75.7 1.0 copy-start.15
  76.6 0.9 copy-start.18
  77.5 0.9 copy-start.24
  80.5 14.3 %copy-start.19 = (bf16[64,1280]{1,0:T(8,128)(2,1)}, bf16[64,1280]{1,0:T(8,128)(2,1)S(1)}, u32[]{:S(2)}) copy-start(bf16[64,1280]{1,0:T(8,128)(2,1)S(1)} %denoise.1.refs_1_) | copy-start | bytes 491524
  80.5 11.2 %collective-permute-start.10 = (bf16[64,1280]{1,0:T(8,128)(2,1)S(1)}, bf16[64,1280]{1,0:T(8,128)(2,1)S(1)}, u32[]{:S(2)}, u32[]{:S(2)}) collective-permute-start(bf16[64,1280]{1,0:T(8,128)(2,1)S(1)} %denoise.1.refs_1_), channel_id=1, source_target_pairs={{0,2},{1,3},{2,0},{3,1},{4,6},{5,7},{6,4},{7,5},{8,10},{9,11},{10,... | collective-permute-start | bytes 491528 | tf_op jit(solution)/shard_map/ppermute | solution.py:20
  80.5 14.2 %collective-permute-start.11 = (bf16[64,1280]{1,0:T(8,128)(2,1)S(1)}, bf16[64,1280]{1,0:T(8,128)(2,1)S(1)}, u32[]{:S(2)}, u32[]{:S(2)}) collective-permute-start(bf16[64,1280]{1,0:T(8,128)(2,1)S(1)} %denoise.1.refs_1_), channel_id=1, source_target_pairs={{0,3},{1,0},{2,1},{3,2},{4,7},{5,4},{6,5},{7,6},{8,11},{9,8},{10,9... | collective-permute-start | bytes 491528 | tf_op jit(solution)/shard_map/ppermute | solution.py:20
  83.1 11.7 %collective-permute-start.9 = (bf16[64,1280]{1,0:T(8,128)(2,1)S(1)}, bf16[64,1280]{1,0:T(8,128)(2,1)S(1)}, u32[]{:S(2)}, u32[]{:S(2)}) collective-permute-start(bf16[64,1280]{1,0:T(8,128)(2,1)S(1)} %denoise.1.refs_1_), channel_id=1, source_target_pairs={{0,1},{1,2},{2,3},{3,0},{4,5},{5,6},{6,7},{7,4},{8,9},{9,10},{10,1... | collective-permute-start | bytes 491528 | tf_op jit(solution)/shard_map/ppermute | solution.py:20
  83.7 3.0 %copy-start.11 = (bf16[640,1280]{1,0:T(8,128)(2,1)S(1)}, bf16[640,1280]{1,0:T(8,128)(2,1)}, u32[]{:S(2)}) copy-start(bf16[640,1280]{1,0:T(8,128)(2,1)} %copy-done.10) | copy-start | bytes 4915204
  83.7 1.3 copy-start.13
  86.7 24.9 %copy-start.6 = (bf16[1280,1280]{1,0:T(8,128)(2,1)}, bf16[1280,1280]{1,0:T(8,128)(2,1)S(1)}, u32[]{:S(2)}) copy-start(bf16[1280,1280]{1,0:T(8,128)(2,1)S(1)} %assemble.3.refs_9_.refs_11_.refs_7_) | copy-start | bytes 9830404
  86.7 8.0 %copy-start.4 = (bf16[1,1280,1280]{2,1,0:T(8,128)(2,1)S(1)}, bf16[1,1280,1280]{2,1,0:T(8,128)(2,1)}, u32[]{:S(2)}) copy-start(bf16[1,1280,1280]{2,1,0:T(8,128)(2,1)} %param.12) | copy-start | bytes 9830404
  99.8 43.3 %collective-permute-start.28 = (bf16[640,1280]{1,0:T(8,128)(2,1)}, bf16[640,1280]{1,0:T(8,128)(2,1)}, u32[]{:S(2)}, u32[]{:S(2)}) collective-permute-start(bf16[640,1280]{1,0:T(8,128)(2,1)} %share.5), channel_id=1, source_target_pairs={{0,16},{1,17},{2,18},{3,19},{4,20},{5,21},{6,22},{7,23},{8,24},{9,... | collective-permute-start | bytes 4915208 | tf_op jit(solution)/shard_map/ppermute | solution.py:523
  102.4 6.7 %collective-permute-start.16 = (f32[8,1280]{1,0:T(8,128)S(1)}, f32[8,1280]{1,0:T(8,128)S(1)}, u32[]{:S(2)}, u32[]{:S(2)}) collective-permute-start(f32[8,1280]{1,0:T(8,128)S(1)} %get-tuple-element.39.refs_1_.refs_2_), channel_id=1, source_target_pairs={{0,1},{1,2},{2,3},{3,0},{4,5},{5,6},{6,7},{7,4},{8,9},{9,10},{10,1... | collective-permute-start | bytes 122888 | tf_op jit(solution)/shard_map/ppermute | solution.py:20
  106.2 5.3 %collective-permute-start.17 = (f32[8,1280]{1,0:T(8,128)S(1)}, f32[8,1280]{1,0:T(8,128)S(1)}, u32[]{:S(2)}, u32[]{:S(2)}) collective-permute-start(f32[8,1280]{1,0:T(8,128)S(1)} %get-tuple-element.39.refs_1_.refs_2_), channel_id=1, source_target_pairs={{0,2},{1,3},{2,0},{3,1},{4,6},{5,7},{6,4},{7,5},{8,10},{9,11},{10,... | collective-permute-start | bytes 122888 | tf_op jit(solution)/shard_map/ppermute | solution.py:20
  106.2 5.3 %collective-permute-start.18 = (f32[8,1280]{1,0:T(8,128)S(1)}, f32[8,1280]{1,0:T(8,128)S(1)}, u32[]{:S(2)}, u32[]{:S(2)}) collective-permute-start(f32[8,1280]{1,0:T(8,128)S(1)} %get-tuple-element.39.refs_1_.refs_2_), channel_id=1, source_target_pairs={{0,3},{1,0},{2,1},{3,2},{4,7},{5,4},{6,5},{7,6},{8,11},{9,8},{10,9... | collective-permute-start | bytes 122888 | tf_op jit(solution)/shard_map/ppermute | solution.py:20
  115.9 14.2 %collective-permute-start.19 = (bf16[64,1280]{1,0:T(8,128)(2,1)}, bf16[64,1280]{1,0:T(8,128)(2,1)}, u32[]{:S(2)}, u32[]{:S(2)}) collective-permute-start(bf16[64,1280]{1,0:T(8,128)(2,1)} %get-tuple-element.46), channel_id=1, source_target_pairs={{0,3},{1,0},{2,1},{3,2},{4,7},{5,4},{6,5},{7,6},{8,11},{9,8},{10,9... | collective-permute-start | bytes 491528 | tf_op jit(solution)/shard_map/ppermute | solution.py:20
  119.3 13.3 %collective-permute-start.20 = (bf16[64,1280]{1,0:T(8,128)(2,1)}, bf16[64,1280]{1,0:T(8,128)(2,1)}, u32[]{:S(2)}, u32[]{:S(2)}) collective-permute-start(bf16[64,1280]{1,0:T(8,128)(2,1)} %get-tuple-element.47), channel_id=1, source_target_pairs={{0,2},{1,3},{2,0},{3,1},{4,6},{5,7},{6,4},{7,5},{8,10},{9,11},{10,... | collective-permute-start | bytes 491528 | tf_op jit(solution)/shard_map/ppermute | solution.py:20
  119.3 13.3 %collective-permute-start.21 = (bf16[64,1280]{1,0:T(8,128)(2,1)}, bf16[64,1280]{1,0:T(8,128)(2,1)}, u32[]{:S(2)}, u32[]{:S(2)}) collective-permute-start(bf16[64,1280]{1,0:T(8,128)(2,1)} %get-tuple-element.48), channel_id=1, source_target_pairs={{0,1},{1,2},{2,3},{3,0},{4,5},{5,6},{6,7},{7,4},{8,9},{9,10},{10,1... | collective-permute-start | bytes 491528 | tf_op jit(solution)/shard_map/ppermute | solution.py:20
  119.9 1.9 %copy-start.5 = (bf16[1,1280,1280]{2,1,0:T(8,128)(2,1)S(1)}, bf16[1,1280,1280]{2,1,0:T(8,128)(2,1)}, u32[]{:S(2)}) copy-start(bf16[1,1280,1280]{2,1,0:T(8,128)(2,1)} %param.12) | copy-start | bytes 9830404
  121.8 1.9 copy-start.7
  123.7 1.0 copy-start.16
  124.7 1.0 copy-start.22
  125.7 6.9 %copy-start.20 = (bf16[64,1280]{1,0:T(8,128)(2,1)S(1)}, bf16[64,1280]{1,0:T(8,128)(2,1)}, u32[]{:S(2)}) copy-start(bf16[64,1280]{1,0:T(8,128)(2,1)} %copy-done.19) | copy-start | bytes 491524
  125.7 6.9 %copy-start.28 = (bf16[64,1280]{1,0:T(8,128)(2,1)S(1)}, bf16[64,1280]{1,0:T(8,128)(2,1)}, u32[]{:S(2)}) copy-start(bf16[64,1280]{1,0:T(8,128)(2,1)} %copy-done.27) | copy-start | bytes 491524
  133.9 8.4 %collective-permute-start.22 = (bf16[64,1280]{1,0:T(8,128)(2,1)S(1)}, bf16[64,1280]{1,0:T(8,128)(2,1)S(1)}, u32[]{:S(2)}, u32[]{:S(2)}) collective-permute-start(bf16[64,1280]{1,0:T(8,128)(2,1)S(1)} %eps_gradient.1.refs_1_), channel_id=1, source_target_pairs={{0,1},{1,2},{2,3},{3,0},{4,5},{5,6},{6,7},{7,4},{8,9},{9,10},{10,1... | collective-permute-start | bytes 491528 | tf_op jit(solution)/shard_map/ppermute | solution.py:20
  134.6 8.5 %collective-permute-start.24 = (bf16[64,1280]{1,0:T(8,128)(2,1)S(1)}, bf16[64,1280]{1,0:T(8,128)(2,1)S(1)}, u32[]{:S(2)}, u32[]{:S(2)}) collective-permute-start(bf16[64,1280]{1,0:T(8,128)(2,1)S(1)} %eps_gradient.1.refs_1_), channel_id=1, source_target_pairs={{0,3},{1,0},{2,1},{3,2},{4,7},{5,4},{6,5},{7,6},{8,11},{9,8},{10,9... | collective-permute-start | bytes 491528 | tf_op jit(solution)/shard_map/ppermute | solution.py:20
  144.6 11.1 %collective-permute-start.29 = (bf16[1,640,1280]{2,1,0:T(8,128)(2,1)S(1)}, bf16[1,640,1280]{2,1,0:T(8,128)(2,1)S(1)}, u32[]{:S(2)}, u32[]{:S(2)}) collective-permute-start(bf16[1,640,1280]{2,1,0:T(8,128)(2,1)S(1)} %stack.25), channel_id=1, source_target_pairs={{0,4},{4,0},{8,12},{12,8},{1,5},{5,1},{9,13},{13,9},{2,6},{6,2},{1... | collective-permute-start | bytes 4915208 | tf_op jit(solution)/shard_map/ppermute | solution.py:25
  144.7 11.0 %collective-permute-start.23 = (bf16[64,1280]{1,0:T(8,128)(2,1)S(1)}, bf16[64,1280]{1,0:T(8,128)(2,1)S(1)}, u32[]{:S(2)}, u32[]{:S(2)}) collective-permute-start(bf16[64,1280]{1,0:T(8,128)(2,1)S(1)} %eps_gradient.1.refs_1_), channel_id=1, source_target_pairs={{0,2},{1,3},{2,0},{3,1},{4,6},{5,7},{6,4},{7,5},{8,10},{9,11},{10,... | collective-permute-start | bytes 491528 | tf_op jit(solution)/shard_map/ppermute | solution.py:20
  146.4 16.9 %collective-permute-start.26 = (bf16[128,1280]{1,0:T(8,128)(2,1)S(1)}, bf16[128,1280]{1,0:T(8,128)(2,1)S(1)}, u32[]{:S(2)}, u32[]{:S(2)}) collective-permute-start(bf16[128,1280]{1,0:T(8,128)(2,1)S(1)} %pad_maximum_fusion), channel_id=1, source_target_pairs={{0,16},{16,0},{1,17},{17,1},{2,18},{18,2},{3,19},{19,3},{4,20},{20... | collective-permute-start | bytes 983048 | tf_op jit(solution)/shard_map/ppermute | solution.py:25
  146.5 14.1 %collective-permute-start.25 = (bf16[64,1280]{1,0:T(8,128)(2,1)S(1)}, bf16[64,1280]{1,0:T(8,128)(2,1)S(1)}, u32[]{:S(2)}, u32[]{:S(2)}) collective-permute-start(bf16[64,1280]{1,0:T(8,128)(2,1)S(1)} %eps_gradient.1.refs_1_), channel_id=1, source_target_pairs={{0,16},{16,0},{1,17},{17,1},{2,18},{18,2},{3,19},{19,3},{4,20},{20... | collective-permute-start | bytes 491528 | tf_op jit(solution)/shard_map/ppermute | solution.py:25
  155.7 7.6 %collective-permute-start.27 = (bf16[64,1280]{1,0:T(8,128)(2,1)S(1)}, bf16[64,1280]{1,0:T(8,128)(2,1)S(1)}, u32[]{:S(2)}, u32[]{:S(2)}) collective-permute-start(bf16[64,1280]{1,0:T(8,128)(2,1)S(1)} %collective-permute-done.23.refs_3_), channel_id=1, source_target_pairs={{0,16},{16,0},{1,17},{17,1},{2,18},{18,2},{3,19},{19,3},{4,20},{20... | collective-permute-start | bytes 491528 | tf_op jit(solution)/shard_map/ppermute | solution.py:25
  168.3 2.4 %collective-permute-start.32 = (bf16[2,160,1280]{2,1,0:T(8,128)(2,1)S(1)}, bf16[2,160,1280]{2,1,0:T(8,128)(2,1)S(1)}, u32[]{:S(2)}, u32[]{:S(2)}) collective-permute-start(bf16[2,160,1280]{2,1,0:T(8,128)(2,1)S(1)} %get-tuple-element.57), channel_id=1, source_target_pairs={{0,4},{4,0},{8,12},{12,8},{1,5},{5,1},{9,13},{13,9},{2,6},{6,2},{1... | collective-permute-start | bytes 2457608 | tf_op jit(solution)/shard_map/ppermute | solution.py:25
  168.4 4.6 %collective-permute-start.30 = (bf16[2,160,1280]{2,1,0:T(8,128)(2,1)S(1)}, bf16[2,160,1280]{2,1,0:T(8,128)(2,1)S(1)}, u32[]{:S(2)}, u32[]{:S(2)}) collective-permute-start(bf16[2,160,1280]{2,1,0:T(8,128)(2,1)S(1)} %get-tuple-element.53), channel_id=1, source_target_pairs={{0,4},{4,0},{8,12},{12,8},{1,5},{5,1},{9,13},{13,9},{2,6},{6,2},{1... | collective-permute-start | bytes 2457608 | tf_op jit(solution)/shard_map/ppermute | solution.py:25
  171.4 12.4 %collective-permute-start.33 = (bf16[160,1280]{1,0:T(8,128)(2,1)S(1)}, bf16[160,1280]{1,0:T(8,128)(2,1)S(1)}, u32[]{:S(2)}, u32[]{:S(2)}) collective-permute-start(bf16[160,1280]{1,0:T(8,128)(2,1)S(1)} %bitcast.36), channel_id=1, source_target_pairs={{0,8},{4,12},{8,0},{12,4},{1,9},{5,13},{9,1},{13,5},{2,10},{6,14},... | collective-permute-start | bytes 1228808 | tf_op jit(solution)/shard_map/ppermute | solution.py:20
  173.7 18.1 %collective-permute-start.31 = (bf16[160,1280]{1,0:T(8,128)(2,1)S(1)}, bf16[160,1280]{1,0:T(8,128)(2,1)S(1)}, u32[]{:S(2)}, u32[]{:S(2)}) collective-permute-start(bf16[160,1280]{1,0:T(8,128)(2,1)S(1)} %bitcast.37), channel_id=1, source_target_pairs={{0,8},{4,12},{8,0},{12,4},{1,9},{5,13},{9,1},{13,5},{2,10},{6,14},... | collective-permute-start | bytes 1228808 | tf_op jit(solution)/shard_map/ppermute | solution.py:20
  (2 other events, 1.6 us)

commit v9 on v8

--- a/solution.py
+++ b/solution.py
@@ -13,6 +13,7 @@
 
 EPS = 1e-06
 VMEM_BYTES = 8 * 1024 * 1024
+COST = 10**11
 
 
 def rotated(value, axis, steps):
@@ -59,22 +60,27 @@
 IN_SMEM = pl.BlockSpec(memory_space=pltpu.SMEM)
 
 
-IN_ANY = pl.BlockSpec(memory_space=pl.ANY)
+TOKEN = jax.ShapeDtypeStruct((8, 128), jnp.float32)
 
 
 def run(body, name, sel, operands, outs, scratch, after=()):
-    used = 1 + len(operands)
-
-    def without_after(*refs):
-        body(*refs[:used], *refs[used + len(after) :])
-
+    used, last = 1 + len(operands), 1 + len(operands) + len(after) + len(outs)
+
+    def with_token(*refs):
+        refs[last][...] = jnp.zeros(TOKEN.shape, TOKEN.dtype)
+        body(*refs[:used], *refs[used + len(after) : last], *refs[last + 1 :])
+
+    held = [math.prod(x.shape) * jnp.dtype(x.dtype).itemsize for x in scratch]
     return pl.pallas_call(
-        without_after,
-        in_specs=[IN_SMEM] + [IN_VMEM] * len(operands) + [IN_ANY] * len(after),
-        out_specs=[IN_VMEM] * len(outs),
+        with_token,
+        in_specs=[IN_SMEM] + [IN_VMEM] * (len(operands) + len(after)),
+        out_specs=[IN_VMEM] * (len(outs) + 1),
         scratch_shapes=scratch,
-        out_shape=outs,
-        compiler_params=pltpu.CompilerParams(vmem_limit_bytes=VMEM_BYTES),
+        out_shape=[*outs, TOKEN],
+        compiler_params=pltpu.CompilerParams(vmem_limit_bytes=max(VMEM_BYTES, 4 * sum(held))),
+        cost_estimate=pl.CostEstimate(
+            flops=COST, bytes_accessed=COST // 200, transcendentals=0
+        ),
         name=name,
     )(sel, *operands, *after)
 
@@ -107,7 +113,7 @@
 def share(weight, group, sel, after):
     rows, hidden = weight.shape
     body = functools.partial(share_body, group)
-    return run(body, "share", sel, [weight], [bf16(rows // group, hidden)], [], after)[0]
+    return run(body, "share", sel, [weight], [bf16(rows // group, hidden)], [], after)
 
 
 def stack_body(sel_ref, *refs):
@@ -127,11 +133,12 @@
 def assembled(pieces, sel, after):
     rows, hidden = pieces[0].shape
     count = len(pieces)
-    stacked = run(stack_body, "stack", sel, pieces, [bf16(count, rows, hidden)], [], after)[0]
+    out = bf16(count, rows, hidden)
+    stacked = run(stack_body, "stack", sel, pieces, [out], [], after)[0]
     beside = swapped(stacked, "dp", 1)
     body = functools.partial(assemble_body, count)
     out = bf16(2 * count * rows, hidden)
-    return run(body, "assemble", sel, [*pieces, beside], [out], [])[0]
+    return run(body, "assemble", sel, [*pieces, beside], [out], [])
 
 
 def partial_body(count, sel_ref, *refs):
@@ -168,15 +175,26 @@
     )
 
 
-def pick_body(sel_ref, stay, crossed, *outs):
+def pick_body(count, sel_ref, *refs):
+    stay, crossed = refs[:2]
+    arrived, outs = refs[2 : 2 + count], refs[2 + count :]
     for i, out in enumerate(outs):
-        out[...] = jnp.where(sel_ref[0] == 0, stay[i], crossed[i])
-
-
-def picked(stay, crossed, sel, after):
+        value = jnp.where(sel_ref[0] == 0, stay[i], crossed[i])
+        if count and i == 0:
+            value = value.astype(jnp.float32)
+            for part in arrived:
+                value = value + part[...].astype(jnp.float32)
+        out[...] = value
+
+
+def picked(stay, crossed, arrived, sel):
     count, rows, width = stay.shape
     outs = [bf16(rows, width)] * count
-    return run(pick_body, "pick", sel, [stay, crossed], outs, [], after)
+    if arrived:
+        outs[0] = jax.ShapeDtypeStruct((rows, width), jnp.float32)
+    body = functools.partial(pick_body, len(arrived))
+    *chosen, token = run(body, "pick", sel, [stay, crossed, *arrived], outs, [])
+    return chosen, token
 
 
 def denoise_body(tokens, count, sel_ref, *refs):
@@ -191,7 +209,7 @@
     out[...] = ((base - sigma[...] * eps) / alpha[...]).astype(jnp.bfloat16)
 
 
-def denoised(latents, sigma, alpha, sums, tokens, sel):
+def denoised(latents, sigma, alpha, sums, tokens, sel, after):
     return run(
         functools.partial(denoise_body, tokens, len(sums)),
         "denoise",
@@ -199,7 +217,8 @@
         [latents, sigma, alpha, *sums],
         [bf16(latents.shape[0] // 2, latents.shape[1])],
         [],
-    )[0]
+        after,
+    )[:2]
 
 
 def crossing(count):
@@ -233,7 +252,7 @@
     by_section(sel_ref, 0, work, (own,), (other,))
 
 
-def block0_state(parts, gain, own, other, sel):
+def block0_state(parts, gain, own, other, sel, after):
     total, width = sum(part.shape[0] for part in parts), parts[0].shape[1]
     hidden = own.shape[1]
     return run(
@@ -243,6 +262,7 @@
         [*parts, gain, own, other],
         [bf16(total, hidden), bf16(total, hidden), bf16(width // 2, total)],
         [pltpu.VMEM((total, width), jnp.bfloat16)],
+        after,
     )
 
 
@@ -280,7 +300,7 @@
     by_section(sel_ref, 1, work, (own_in, own_out), (other_in, other_out))
 
 
-def reward_forward(parts, tokens, gain, text, own, other, sel):
+def reward_forward(parts, tokens, gain, text, own, other, sel, after):
     rows, width = parts[0].shape
     hidden, n = own[0].shape[1], len(parts)
     images = (n + 1) * rows // tokens
@@ -292,6 +312,7 @@
         [bf16(rows, hidden)] * n
         + [jax.ShapeDtypeStruct((-(-images // 8) * 8, width), jnp.float32)],
         [pltpu.VMEM((n * rows, width), jnp.bfloat16)],
+        after,
     )
     return outs[:n], outs[n]
 
@@ -386,7 +407,7 @@
         [bf16(*seen.shape)],
         [],
         after,
-    )[0]
+    )
 
 
 def put_rows(result, core, keep, away, tile):
@@ -436,7 +457,7 @@
             pltpu.VMEM((width // 2, total), jnp.bfloat16),
         ],
     )
-    return outs[:2], outs[2:]
+    return outs[:2], outs[2:4]
 
 
 def chip_body(sel_ref, keep, arrived, mine, others):
@@ -452,7 +473,7 @@
 
 def sum_over_dp(keep, away, sel):
     groups, rows, hidden = keep.shape
-    total, others = run(
+    total, others, unused = run(
         chip_body,
         "chip_sum",
         sel,
@@ -484,9 +505,9 @@
 
     flat = latents.reshape(count * tokens, width)
     lat_parts = gather_parts(flat)
-    got_in = swapped(share(own[0], 4, sel, ()), "sec", 1)
+    got_in = swapped(share(own[0], 4, sel, ())[0], "sec", 1)
     across_in = swapped(got_in, "dp", 2)
-    out_share = share(own[1], 2, sel, (lat_parts[1], lat_parts[-1]))
+    out_share, out_token = share(own[1], 2, sel, [lat_parts[1], lat_parts[-1]])
     got_out = lax.ppermute(out_share, "sec", [(1, 0)])
 
     onehot = (
@@ -496,44 +517,51 @@
 
     near = [k for k in range(1, n_tp) if 2 * k != n_tp]
     rest = [0] + [k for k in range(1, n_tp) if 2 * k == n_tp]
-    sums = [None] * n_tp
-    before_kernel, before_pick = [got_in], []
+    sums, before = [], [got_in]
     for ks in (near, rest):
         if ks:
-            stay, leave = block0_partials(
-                [lat_parts[k] for k in ks], gains[:1], *own, sel, before_kernel
+            stay, leave, partial_token = block0_partials(
+                [lat_parts[k] for k in ks], gains[:1], *own, sel, before
             )
             crossed = lax.ppermute(leave, "sec", [(0, 1)])
-            chosen = picked(stay, crossed, sel, before_pick)
-            for k, part in zip(ks, chosen):
-                sums[k] = rotated(part, "tp", -k) if k else part
-            before_kernel, before_pick = [crossed], [sums[k] for k in ks]
-    mine_rows = denoised(flat, sigma, alpha, sums, tokens, sel)
+            chosen, picked_token = picked(stay, crossed, sums if ks is rest else [], sel)
+            if ks is rest:
+                sums = [chosen[0]] + [rotated(part, "tp", -k) for k, part in zip(ks[1:], chosen[1:])]
+            else:
+                sums = [rotated(part, "tp", -k) for k, part in zip(ks, chosen)]
+                before = [picked_token, out_token]
+    other_in, in_token = assembled([got_in, across_in], sel, [partial_token])
+    mine_rows, unused = denoised(flat, sigma, alpha, sums, tokens, sel, [in_token])
 
     seen_parts = gather_parts(mine_rows)
-    other = (
-        assembled([got_in, across_in], sel, [sums[0]]),
-        assembled([got_out], sel, [sums[0]]),
-    )
-    slopes1, pool = reward_forward(seen_parts, tokens, gains[1:], text_mine, own, other, sel)
+    near_seen = [seen_parts[k] for k in near]
+    other_out, out_token = assembled([got_out], sel, near_seen)
+    other = (other_in, other_out)
+    late_share, late_token = share(own[1], 2, sel, [out_token])
+    got_late = lax.ppermute(late_share, "sec", [(0, 1)])
+    slopes1, pool = reward_forward(
+        seen_parts, tokens, gains[1:], text_mine, own, other, sel, ()
+    )
     pools = gather_parts(pool)
     g_parts, g_mean = reward_back(pools, slopes1, tokens, own, other, sel)
 
-    states = block0_state(lat_parts, gains[:1], own[0], other[0], sel)
-    got_late = lax.ppermute(share(own[1], 2, sel, [pool]), "sec", [(0, 1)])
+    *states, state_token = block0_state(
+        lat_parts, gains[:1], own[0], other[0], sel, ()
+    )
 
     g_sums = [g_parts[0]] + [rotated(g_parts[k], "tp", -k) for k in range(1, n_tp)]
     ratio = -(sigma / alpha)
-    g_eps = eps_gradient(
-        mine_rows, g_mean, gains[1:], ratio, g_sums, tokens, sel, [states[0]]
-    )
+    g_eps, eps_token = eps_gradient(
+        mine_rows, g_mean, gains[1:], ratio, g_sums, tokens, sel, [state_token]
+    )
+
+    late_out = assembled([got_late], sel, [state_token])[0]
 
     g_mine = gather_parts(g_eps)
     pieces = list(g_mine)
     for ks in ([0], near, rest[1:]):
         if ks:
             pieces.append(swapped(jnp.concatenate([g_mine[k] for k in ks], 0), "sec", 1))
-    late_out = assembled([got_late], sel, [g_mine[1], g_mine[-1]])
     out_parts, in_parts = gradients(pieces, states, own[1], late_out, sel)
     grad_out, grad_in = sum_over_dp(*out_parts, sel), sum_over_dp(*in_parts, sel)
     return (grad_in, grad_out)

time: 193 us -> 217 us (1.12)
  waiting for transfers between devices: 82 us -> 96.2 us
  starting transfers between devices: 47.1 us -> 60.8 us
  local copies, waits for them, and re-layouts: 14.6 us -> 5.83 us
  Pallas kernels: 43.1 us -> 48.1 us
    ppermute x1, waiting for transfers between devices: 0.01 us -> 27.5 us  [on_device(): got_late = lax.ppermute(late_share, 'sec', [(0, 1)])]
    unnamed x64 -> x32, local copies, waits for them, and re-layouts: 13.4 us -> 4.55 us
    ppermute x10, waiting for transfers between devices: 13.7 us -> 4.78 us  [swapped(): return lax.ppermute(value, axis, [(i, i ^ bit) for i in range(count)])]
    ppermute x10, starting transfers between devices: 6.19 us -> 12.6 us  [swapped(): return lax.ppermute(value, axis, [(i, i ^ bit) for i in range(count)])]
    pallas_call x21, Pallas kernels: 43.1 us -> 48.1 us  [run(): pl.pallas_call(with_token, in_specs=[IN_SMEM] + [IN_VMEM] * (len(operands...]
    ppermute x1, starting transfers between devices: 2.6 us -> 5.47 us  [on_device(): got_late = lax.ppermute(late_share, 'sec', [(0, 1)])]
    ppermute x20, starting transfers between devices: 30.7 us -> 33.3 us  [rotated(): lax.ppermute(value, axis, [(i, (i + steps) % count) for i in range(count)])]
    ppermute x2, waiting for transfers between devices: 2.59 us -> 0.01 us  [on_device(): crossed = lax.ppermute(leave, 'sec', [(0, 1)])]
  transfers between devices with their start and end apart: 34 -> 34, of which waited for: 21 -> 15; matrix products, arithmetic and copies ran while one was open for 1% -> 1% of each run, Pallas kernels for 16% -> 17%
where the time goes in v9:
time: 217 us
  waiting for transfers between devices  96.2 us (44%)
  starting transfers between devices  60.8 us (28%)
  Pallas kernels  48.1 us (22%)
  local copies, waits for them, and re-layouts  5.83 us (3%)
  between operations  3.64 us (2%)
    ppermute x20, waiting for transfers between devices, rotated(): lax.ppermute(value, axis, [(i, (i + steps) % count) for i in range(count)])  63.9 us
    pallas_call x21, Pallas kernels, run(): pl.pallas_call(with_token, in_specs=[IN_SMEM] + [IN_VMEM] * (len(operands...  48.1 us
    ppermute x20, starting transfers between devices, rotated(): lax.ppermute(value, axis, [(i, (i + steps) % count) for i in range(count)])  33.3 us
    ppermute x1, waiting for transfers between devices, on_device(): got_late = lax.ppermute(late_share, 'sec', [(0, 1)])  27.5 us
    ppermute x10, starting transfers between devices, swapped(): return lax.ppermute(value, axis, [(i, i ^ bit) for i in range(count)])  12.6 us
    ppermute x2, starting transfers between devices, on_device(): crossed = lax.ppermute(leave, 'sec', [(0, 1)])  8.06 us
    ppermute x1, starting transfers between devices, on_device(): got_late = lax.ppermute(late_share, 'sec', [(0, 1)])  5.47 us
    ppermute x10, waiting for transfers between devices, swapped(): return lax.ppermute(value, axis, [(i, i ^ bit) for i in range(count)])  4.78 us
  transfers between devices with their start and end apart: 34, of which 15 were waited for; matrix products, arithmetic and copies ran while one was open for 1% of the time, Pallas kernels for 17%

profile of v9, /device:TPU:0, one launch (start us, length us, event | category | flops | bytes accessed | tf_op | source)
XLA Modules:
  0.0 216.7 jit_solution(12442551840775360852)
XLA Ops:
  0.8 1.9 copy-done.6
  2.7 1.5 share.3
  4.2 3.0 %collective-permute-start.3 = (bf16[320,1280]{1,0:T(8,128)(2,1)}, bf16[320,1280]{1,0:T(8,128)(2,1)}, u32[]{:S(2)}, u32[]{:S(2)}) collective-permute-start(bf16[320,1280]{1,0:T(8,128)(2,1)} %get-tuple-element.48), channel_id=1, source_target_pairs={{0,16},{16,0},{1,17},{17,1},{2,18},{18,2},{3,19},{19,3},{4,20},{20... | collective-permute-start | bytes 2457608 | tf_op jit(solution)/shard_map/ppermute | solution.py:26
  7.2 2.6 %collective-permute-start = (bf16[128,1280]{1,0:T(8,128)(2,1)}, bf16[128,1280]{1,0:T(8,128)(2,1)}, u32[]{:S(2)}, u32[]{:S(2)}) collective-permute-start(bf16[128,1280]{1,0:T(8,128)(2,1)} %bitcast.4.refs_1_), channel_id=1, source_target_pairs={{0,2},{1,3},{2,0},{3,1},{4,6},{5,7},{6,4},{7,5},{8,10},{9,11},{10,... | collective-permute-start | bytes 983048 | tf_op jit(solution)/shard_map/ppermute | solution.py:21
  9.7 1.6 collective-permute-start.1
  11.3 2.2 %collective-permute-start.2 = (bf16[128,1280]{1,0:T(8,128)(2,1)}, bf16[128,1280]{1,0:T(8,128)(2,1)}, u32[]{:S(2)}, u32[]{:S(2)}) collective-permute-start(bf16[128,1280]{1,0:T(8,128)(2,1)} %bitcast.4.refs_1_), channel_id=1, source_target_pairs={{0,3},{1,0},{2,1},{3,2},{4,7},{5,4},{6,5},{7,6},{8,11},{9,8},{10,9... | collective-permute-start | bytes 983048 | tf_op jit(solution)/shard_map/ppermute | solution.py:21
  13.6 0.6 fusion.7
  15.6 0.7 fusion.6
  17.6 9.6 %collective-permute-done.1.refs_1_.refs_2_ = bf16[128,1280]{1,0:T(8,128)(2,1)} collective-permute-done((bf16[128,1280]{1,0:T(8,128)(2,1)}, bf16[128,1280]{1,0:T(8,128)(2,1)}, u32[]{:S(2)}, u32[]{:S(2)}) %collective-permute-start.1) | collective-permute-done | bytes 327712 | tf_op jit(solution)/shard_map/ppermute | solution.py:21
  27.1 6.0 %collective-permute-done.2.refs_2_.refs_3_.refs_4_ = bf16[128,1280]{1,0:T(8,128)(2,1)} collective-permute-done((bf16[128,1280]{1,0:T(8,128)(2,1)}, bf16[128,1280]{1,0:T(8,128)(2,1)}, u32[]{:S(2)}, u32[]{:S(2)}) %collective-permute-start.2) | collective-permute-done | bytes 327712 | tf_op jit(solution)/shard_map/ppermute | solution.py:21
  33.2 1.9 copy-done.8
  35.1 4.4 %block0_partial.2 = (bf16[2,64,1280]{2,1,0:T(8,128)(2,1)S(1)}, bf16[2,64,1280]{2,1,0:T(8,128)(2,1)S(1)}, f32[8,128]{1,0:T(8,128)}) custom-call(s32[4]{0:T(128)S(1)} %pad_add_fusion.refs_0_, bf16[128,1280]{1,0:T(8,128)(2,1)} %collective-permute-done.1.refs_1_.refs_2_, bf16[128,1280]{1,0:T(8,128)(2,1)} %collective-permute-done.2.refs_2_.refs_3_.refs_4_, ...), custom_call_target="tpu_custom_call" | custom-call | flops 99999997952 | bytes 500000000 | tf_op jit(solution)/shard_map/block0_partial/pallas_call | solution.py:74
  39.5 2.4 %collective-permute-start.4 = (bf16[2,64,1280]{2,1,0:T(8,128)(2,1)S(1)}, bf16[2,64,1280]{2,1,0:T(8,128)(2,1)S(1)}, u32[]{:S(2)}, u32[]{:S(2)}) collective-permute-start(bf16[2,64,1280]{2,1,0:T(8,128)(2,1)S(1)} %get-tuple-element.50), channel_id=1, source_target_pairs={{0,16},{1,17},{2,18},{3,19},{4,20},{5,21},{6,22},{7,23},{8,24},{9,... | collective-permute-start | bytes 983048 | tf_op jit(solution)/shard_map/ppermute | solution.py:526
  41.9 2.4 %share.4 = (bf16[640,1280]{1,0:T(8,128)(2,1)}, f32[8,128]{1,0:T(8,128)S(1)}) custom-call(s32[4]{0:T(128)S(1)} %pad_add_fusion.refs_0_, bf16[1280,1280]{1,0:T(8,128)(2,1)S(1)} %bitcast.24, bf16[128,1280]{1,0:T(8,128)(2,1)} %collective-permute-done.1.refs_1_.refs_2_, bf16[128,1280]{1,0:T(8,128)(2,1)} %collective-permute-done.2.refs_2_.refs_3_.refs_4_), custom_call_target="tpu_custom_call" | custom-call | flops 99999997952 | bytes 500000000 | tf_op jit(solution)/shard_map/share/pallas_call | solution.py:74
  44.3 1.3 collective-permute-start.14
  45.6 1.6 collective-permute-start.9
  47.2 0.6 pick.2
  47.9 3.5 %block0_partial.3 = (bf16[2,64,1280]{2,1,0:T(8,128)(2,1)S(1)}, bf16[2,64,1280]{2,1,0:T(8,128)(2,1)S(1)}, f32[8,128]{1,0:T(8,128)S(1)}) custom-call(s32[4]{0:T(128)S(1)} %pad_add_fusion.refs_0_, bf16[128,1280]{1,0:T(8,128)(2,1)} %bitcast.4.refs_1_, bf16[128,1280]{1,0:T(8,128)(2,1)} %collective-permute-done.refs_2_.refs_3_, f32[1,1280]{1,0:T(1,128)S(1)} %copy-done.4, ...), custom_call_target="tpu_custom_call" | custom-call | flops 99999997952 | bytes 500000000 | tf_op jit(solution)/shard_map/block0_partial/pallas_call | solution.py:74
  51.3 5.7 %collective-permute-start.5 = (bf16[2,64,1280]{2,1,0:T(8,128)(2,1)S(1)}, bf16[2,64,1280]{2,1,0:T(8,128)(2,1)S(1)}, u32[]{:S(2)}, u32[]{:S(2)}) collective-permute-start(bf16[2,64,1280]{2,1,0:T(8,128)(2,1)S(1)} %get-tuple-element.54), channel_id=1, source_target_pairs={{0,16},{1,17},{2,18},{3,19},{4,20},{5,21},{6,22},{7,23},{8,24},{9,... | collective-permute-start | bytes 983048 | tf_op jit(solution)/shard_map/ppermute | solution.py:526
  57.0 2.1 collective-permute-start.6
  59.1 4.7 %collective-permute-start.7 = (bf16[64,1280]{1,0:T(8,128)(2,1)S(1)}, bf16[64,1280]{1,0:T(8,128)(2,1)S(1)}, u32[]{:S(2)}, u32[]{:S(2)}) collective-permute-start(bf16[64,1280]{1,0:T(8,128)(2,1)S(1)} %get-tuple-element.56), channel_id=1, source_target_pairs={{0,1},{1,2},{2,3},{3,0},{4,5},{5,6},{6,7},{7,4},{8,9},{9,10},{10,1... | collective-permute-start | bytes 491528 | tf_op jit(solution)/shard_map/ppermute | solution.py:21
  63.8 2.0 stack.23
  65.8 1.2 collective-permute-done.6.refs_3_
  67.1 6.6 %collective-permute-done.7.refs_4_ = bf16[64,1280]{1,0:T(8,128)(2,1)S(1)} collective-permute-done((bf16[64,1280]{1,0:T(8,128)(2,1)S(1)}, bf16[64,1280]{1,0:T(8,128)(2,1)S(1)}, u32[]{:S(2)}, u32[]{:S(2)}) %collective-permute-start.7) | collective-permute-done | bytes 163872 | tf_op jit(solution)/shard_map/ppermute | solution.py:21
  73.6 1.1 pick.3
  74.8 2.3 %collective-permute-start.8 = (bf16[64,1280]{1,0:T(8,128)(2,1)S(1)}, bf16[64,1280]{1,0:T(8,128)(2,1)S(1)}, u32[]{:S(2)}, u32[]{:S(2)}) collective-permute-start(bf16[64,1280]{1,0:T(8,128)(2,1)S(1)} %get-tuple-element.58), channel_id=1, source_target_pairs={{0,2},{1,3},{2,0},{3,1},{4,6},{5,7},{6,4},{7,5},{8,10},{9,11},{10,... | collective-permute-start | bytes 491528 | tf_op jit(solution)/shard_map/ppermute | solution.py:21
  77.1 1.6 assemble.3
  78.7 6.7 %collective-permute-done.8.refs_5_ = bf16[64,1280]{1,0:T(8,128)(2,1)S(1)} collective-permute-done((bf16[64,1280]{1,0:T(8,128)(2,1)S(1)}, bf16[64,1280]{1,0:T(8,128)(2,1)S(1)}, u32[]{:S(2)}, u32[]{:S(2)}) %collective-permute-start.8) | collective-permute-done | bytes 163872 | tf_op jit(solution)/shard_map/ppermute | solution.py:21
  85.4 1.8 denoise.1
  87.2 3.8 %collective-permute-start.13 = (bf16[64,1280]{1,0:T(8,128)(2,1)}, bf16[64,1280]{1,0:T(8,128)(2,1)S(1)}, u32[]{:S(2)}, u32[]{:S(2)}) collective-permute-start(bf16[64,1280]{1,0:T(8,128)(2,1)} %get-tuple-element.62.refs_1_), channel_id=1, source_target_pairs={{0,3},{1,0},{2,1},{3,2},{4,7},{5,4},{6,5},{7,6},{8,11},{9,8},{10,9... | collective-permute-start | bytes 491528 | tf_op jit(solution)/shard_map/ppermute | solution.py:21
  91.3 5.0 %collective-permute-done.11.refs_2_ = bf16[64,1280]{1,0:T(8,128)(2,1)S(1)} collective-permute-done((bf16[64,1280]{1,0:T(8,128)(2,1)}, bf16[64,1280]{1,0:T(8,128)(2,1)S(1)}, u32[]{:S(2)}, u32[]{:S(2)}) %collective-permute-start.11) | collective-permute-done | bytes 163872 | tf_op jit(solution)/shard_map/ppermute | solution.py:21
  96.3 2.8 %collective-permute-done.13.refs_3_.refs_4_ = bf16[64,1280]{1,0:T(8,128)(2,1)S(1)} collective-permute-done((bf16[64,1280]{1,0:T(8,128)(2,1)}, bf16[64,1280]{1,0:T(8,128)(2,1)S(1)}, u32[]{:S(2)}, u32[]{:S(2)}) %collective-permute-start.13) | collective-permute-done | bytes 163872 | tf_op jit(solution)/shard_map/ppermute | solution.py:21
  99.1 2.0 stack.24
  101.2 4.8 %block0_state.1 = (bf16[512,1280]{1,0:T(8,128)(2,1)S(1)}, bf16[512,1280]{1,0:T(8,128)(2,1)S(1)}, bf16[640,512]{1,0:T(8,128)(2,1)S(1)}, f32[8,128]{1,0:T(8,128)S(1)}) custom-call(s32[4]{0:T(128)S(1)} %pad_add_fusion.refs_0_, bf16[128,1280]{1,0:T(8,128)(2,1)} %bitcast.4.refs_1_, bf16[128,1280]{1,0:T(8,128)(2,1)} %collective-permute-done.1.refs_1_.refs_2_, ...), custom_call_target="tpu_custom_call" | custom-call | flops 99999997952 | bytes 500000000 | tf_op jit(solution)/shard_map/block0_state/pallas_call | solution.py:74
  106.0 1.8 assemble.4
  108.4 4.2 %reward_forward.1 = (bf16[64,1280]{1,0:T(8,128)(2,1)S(1)}, bf16[64,1280]{1,0:T(8,128)(2,1)S(1)}, bf16[64,1280]{1,0:T(8,128)(2,1)S(1)}, bf16[64,1280]{1,0:T(8,128...) custom-call(s32[4]{0:T(128)S(1)} %pad_add_fusion.refs_0_, bf16[64,1280]{1,0:T(8,128)(2,1)} %get-tuple-element.62.refs_1_, ...), custom_call_target="tpu_custom_call" | custom-call | flops 99999997952 | bytes 500000000 | tf_op jit(solution)/shard_map/reward_forward/pallas_call | solution.py:74
  112.6 1.7 collective-permute-start.17
  114.3 2.5 %collective-permute-start.18 = (f32[8,1280]{1,0:T(8,128)S(1)}, f32[8,1280]{1,0:T(8,128)S(1)}, u32[]{:S(2)}, u32[]{:S(2)}) collective-permute-start(f32[8,1280]{1,0:T(8,128)S(1)} %get-tuple-element.67.refs_1_), channel_id=1, source_target_pairs={{0,3},{1,0},{2,1},{3,2},{4,7},{5,4},{6,5},{7,6},{8,11},{9,8},{10,9... | collective-permute-start | bytes 122888 | tf_op jit(solution)/shard_map/ppermute | solution.py:21
  116.8 1.1 share.5
  118.0 5.5 %collective-permute-start.28 = (bf16[640,1280]{1,0:T(8,128)(2,1)S(1)}, bf16[640,1280]{1,0:T(8,128)(2,1)S(1)}, u32[]{:S(2)}, u32[]{:S(2)}) collective-permute-start(bf16[640,1280]{1,0:T(8,128)(2,1)S(1)} %get-tuple-element.83), channel_id=1, source_target_pairs={{0,16},{1,17},{2,18},{3,19},{4,20},{5,21},{6,22},{7,23},{8,24},{9,... | collective-permute-start | bytes 4915208 | tf_op jit(solution)/shard_map/ppermute | solution.py:541
  123.5 3.4 %reward_back.1 = (bf16[64,1280]{1,0:T(8,128)(2,1)S(1)}, bf16[64,1280]{1,0:T(8,128)(2,1)S(1)}, bf16[64,1280]{1,0:T(8,128)(2,1)S(1)}, bf16[64,1280]{1,0:T(8,128)(2...) custom-call(s32[4]{0:T(128)S(1)} %pad_add_fusion.refs_0_, f32[8,1280]{1,0:T(8,128)S(1)} %get-tuple-element.67.refs_1_, ...), custom_call_target="tpu_custom_call" | custom-call | flops 99999997952 | bytes 500000000 | tf_op jit(solution)/shard_map/reward_back/pallas_call | solution.py:74
  127.3 1.5 collective-permute-start.20
  128.7 2.0 collective-permute-start.21
  130.8 27.5 %collective-permute-done.28.refs_1_ = bf16[640,1280]{1,0:T(8,128)(2,1)S(1)} collective-permute-done((bf16[640,1280]{1,0:T(8,128)(2,1)S(1)}, bf16[640,1280]{1,0:T(8,128)(2,1)S(1)}, u32[]{:S(2)}, u32[]{:S(2)}) %collective-permute-start.28) | collective-permute-done | bytes 1638432 | tf_op jit(solution)/shard_map/ppermute | solution.py:541
  158.3 1.1 stack.25
  159.5 1.7 eps_gradient.1
  161.8 3.3 %collective-permute-start.24 = (bf16[64,1280]{1,0:T(8,128)(2,1)S(1)}, bf16[64,1280]{1,0:T(8,128)(2,1)S(1)}, u32[]{:S(2)}, u32[]{:S(2)}) collective-permute-start(bf16[64,1280]{1,0:T(8,128)(2,1)S(1)} %get-tuple-element.78.refs_1_), channel_id=1, source_target_pairs={{0,3},{1,0},{2,1},{3,2},{4,7},{5,4},{6,5},{7,6},{8,11},{9,8},{10,9... | collective-permute-start | bytes 491528 | tf_op jit(solution)/shard_map/ppermute | solution.py:21
  165.1 2.5 %collective-permute-start.25 = (bf16[64,1280]{1,0:T(8,128)(2,1)S(1)}, bf16[64,1280]{1,0:T(8,128)(2,1)S(1)}, u32[]{:S(2)}, u32[]{:S(2)}) collective-permute-start(bf16[64,1280]{1,0:T(8,128)(2,1)S(1)} %get-tuple-element.78.refs_1_), channel_id=1, source_target_pairs={{0,16},{16,0},{1,17},{17,1},{2,18},{18,2},{3,19},{19,3},{4,20},{20... | collective-permute-start | bytes 491528 | tf_op jit(solution)/shard_map/ppermute | solution.py:26
  167.5 2.5 %collective-permute-done.22.refs_2_ = bf16[64,1280]{1,0:T(8,128)(2,1)S(1)} collective-permute-done((bf16[64,1280]{1,0:T(8,128)(2,1)S(1)}, bf16[64,1280]{1,0:T(8,128)(2,1)S(1)}, u32[]{:S(2)}, u32[]{:S(2)}) %collective-permute-start.22) | collective-permute-done | bytes 163872 | tf_op jit(solution)/shard_map/ppermute | solution.py:21
  170.1 1.6 collective-permute-done.24.refs_4_
  171.7 2.5 %collective-permute-start.26 = (bf16[128,1280]{1,0:T(8,128)(2,1)S(1)}, bf16[128,1280]{1,0:T(8,128)(2,1)S(1)}, u32[]{:S(2)}, u32[]{:S(2)}) collective-permute-start(bf16[128,1280]{1,0:T(8,128)(2,1)S(1)} %pad_maximum_fusion), channel_id=1, source_target_pairs={{0,16},{16,0},{1,17},{17,1},{2,18},{18,2},{3,19},{19,3},{4,20},{20... | collective-permute-start | bytes 983048 | tf_op jit(solution)/shard_map/ppermute | solution.py:26
  174.2 5.6 %collective-permute-done.23.refs_3_ = bf16[64,1280]{1,0:T(8,128)(2,1)S(1)} collective-permute-done((bf16[64,1280]{1,0:T(8,128)(2,1)S(1)}, bf16[64,1280]{1,0:T(8,128)(2,1)S(1)}, u32[]{:S(2)}, u32[]{:S(2)}) %collective-permute-start.23) | collective-permute-done | bytes 163872 | tf_op jit(solution)/shard_map/ppermute | solution.py:21
  179.8 2.5 %collective-permute-start.27 = (bf16[64,1280]{1,0:T(8,128)(2,1)S(1)}, bf16[64,1280]{1,0:T(8,128)(2,1)S(1)}, u32[]{:S(2)}, u32[]{:S(2)}) collective-permute-start(bf16[64,1280]{1,0:T(8,128)(2,1)S(1)} %collective-permute-done.23.refs_3_), channel_id=1, source_target_pairs={{0,16},{16,0},{1,17},{17,1},{2,18},{18,2},{3,19},{19,3},{4,20},{20... | collective-permute-start | bytes 491528 | tf_op jit(solution)/shard_map/ppermute | solution.py:26
  182.3 1.1 assemble.5
  183.5 2.9 %collective-permute-done.27.refs_7_ = bf16[64,1280]{1,0:T(8,128)(2,1)S(1)} collective-permute-done((bf16[64,1280]{1,0:T(8,128)(2,1)S(1)}, bf16[64,1280]{1,0:T(8,128)(2,1)S(1)}, u32[]{:S(2)}, u32[]{:S(2)}) %collective-permute-start.27) | collective-permute-done | bytes 163872 | tf_op jit(solution)/shard_map/ppermute | solution.py:26
  186.4 5.6 %gradients.1 = (bf16[2,160,1280]{2,1,0:T(8,128)(2,1)S(1)}, bf16[2,160,1280]{2,1,0:T(8,128)(2,1)S(1)}, bf16[2,160,1280]{2,1,0:T(8,128)(2,1)S(1)}, bf16[2,160,1280]{2,1,0:T(8,128)(2,1)S(1)}, f32[8,128]{1,0:T(8,128)}) custom-call(s32[4]{0:T(128)S(1)} %pad_add_fusion.refs_0_, bf16[64,1280]{1,0:T(8,128)(2,1)S(1)} %get-tuple-element.78.refs_1_, ...), custom_call_target="tpu_custom_call" | custom-call | flops 99999997952 | bytes 500000000 | tf_op jit(solution)/shard_map/gradients/pallas_call | solution.py:74
  192.5 1.8 collective-permute-done.30.refs_2_
  194.3 1.1 chip_sum.2
  195.5 1.5 collective-permute-start.31
  197.0 1.1 chip_sum.3
  198.6 9.1 %collective-permute-done.31 = bf16[160,1280]{1,0:T(8,128)(2,1)S(1)} collective-permute-done((bf16[160,1280]{1,0:T(8,128)(2,1)S(1)}, bf16[160,1280]{1,0:T(8,128)(2,1)S(1)}, u32[]{:S(2)}, u32[]{:S(2)}) %collective-permute-start.31) | collective-permute-done | bytes 409632 | tf_op jit(solution)/shard_map/ppermute | solution.py:21
  207.8 1.0 convert_add_fusion.1
  208.7 7.0 %collective-permute-done.33 = bf16[160,1280]{1,0:T(8,128)(2,1)S(1)} collective-permute-done((bf16[160,1280]{1,0:T(8,128)(2,1)S(1)}, bf16[160,1280]{1,0:T(8,128)(2,1)S(1)}, u32[]{:S(2)}, u32[]{:S(2)}) %collective-permute-start.33) | collective-permute-done | bytes 409632 | tf_op jit(solution)/shard_map/ppermute | solution.py:21
  215.8 1.0 convert_add_fusion
  (68 shorter events, 3.1 us)
Async XLA Ops:
  0.6 90.4 %copy-start = (bf16[64,1280]{1,0:T(8,128)(2,1)S(1)}, bf16[64,1280]{1,0:T(8,128)(2,1)}, u32[]{:S(2)}) copy-start(bf16[64,1280]{1,0:T(8,128)(2,1)} %param.10) | copy-start | bytes 491524
  0.8 1.9 copy-start.6
  2.7 10.9 %copy-start.14 = (s32[2]{0:T(128)S(1)}, s32[2]{0:T(128)}, u32[]{:S(2)}) copy-start(s32[2]{0:T(128)} %param.8) | copy-start | bytes 28
  2.7 12.9 %copy-start.15 = (s32[2]{0:T(128)S(1)}, s32[2]{0:T(128)}, u32[]{:S(2)}) copy-start(s32[2]{0:T(128)} %param.9) | copy-start | bytes 28
  2.7 14.8 %copy-start.13 = (f32[2,1280]{1,0:T(2,128)S(1)}, f32[2,1280]{1,0:T(2,128)}, u32[]{:S(2)}) copy-start(f32[2,1280]{1,0:T(2,128)} %param.11) | copy-start | bytes 30724
  2.7 30.5 %copy-start.7 = (bf16[1,1280,1280]{2,1,0:T(8,128)(2,1)S(1)}, bf16[1,1280,1280]{2,1,0:T(8,128)(2,1)}, u32[]{:S(2)}) copy-start(bf16[1,1280,1280]{2,1,0:T(8,128)(2,1)} %param.12) | copy-start | bytes 9830404
  4.2 29.0 %collective-permute-start.3 = (bf16[320,1280]{1,0:T(8,128)(2,1)}, bf16[320,1280]{1,0:T(8,128)(2,1)}, u32[]{:S(2)}, u32[]{:S(2)}) collective-permute-start(bf16[320,1280]{1,0:T(8,128)(2,1)} %get-tuple-element.48), channel_id=1, source_target_pairs={{0,16},{16,0},{1,17},{17,1},{2,18},{18,2},{3,19},{19,3},{4,20},{20... | collective-permute-start | bytes 2457608 | tf_op jit(solution)/shard_map/ppermute | solution.py:26
  7.2 40.6 %collective-permute-start = (bf16[128,1280]{1,0:T(8,128)(2,1)}, bf16[128,1280]{1,0:T(8,128)(2,1)}, u32[]{:S(2)}, u32[]{:S(2)}) collective-permute-start(bf16[128,1280]{1,0:T(8,128)(2,1)} %bitcast.4.refs_1_), channel_id=1, source_target_pairs={{0,2},{1,3},{2,0},{3,1},{4,6},{5,7},{6,4},{7,5},{8,10},{9,11},{10,... | collective-permute-start | bytes 983048 | tf_op jit(solution)/shard_map/ppermute | solution.py:21
  9.7 17.4 %collective-permute-start.1 = (bf16[128,1280]{1,0:T(8,128)(2,1)}, bf16[128,1280]{1,0:T(8,128)(2,1)}, u32[]{:S(2)}, u32[]{:S(2)}) collective-permute-start(bf16[128,1280]{1,0:T(8,128)(2,1)} %bitcast.4.refs_1_), channel_id=1, source_target_pairs={{0,1},{1,2},{2,3},{3,0},{4,5},{5,6},{6,7},{7,4},{8,9},{9,10},{10,1... | collective-permute-start | bytes 983048 | tf_op jit(solution)/shard_map/ppermute | solution.py:21
  11.3 21.9 %collective-permute-start.2 = (bf16[128,1280]{1,0:T(8,128)(2,1)}, bf16[128,1280]{1,0:T(8,128)(2,1)}, u32[]{:S(2)}, u32[]{:S(2)}) collective-permute-start(bf16[128,1280]{1,0:T(8,128)(2,1)} %bitcast.4.refs_1_), channel_id=1, source_target_pairs={{0,3},{1,0},{2,1},{3,2},{4,7},{5,4},{6,5},{7,6},{8,11},{9,8},{10,9... | collective-permute-start | bytes 983048 | tf_op jit(solution)/shard_map/ppermute | solution.py:21
  17.6 21.9 %copy-start.3 = (f32[1,1280]{1,0:T(1,128)}, f32[1,1280]{1,0:T(1,128)S(1)}, u32[]{:S(2)}) copy-start(f32[1,1280]{1,0:T(1,128)S(1)} %get-tuple-element.95.refs_3_.refs_5_) | copy-start | bytes 15364
  17.6 90.3 %copy-start.1 = (f32[1,1280]{1,0:T(1,128)}, f32[1,1280]{1,0:T(1,128)S(1)}, u32[]{:S(2)}) copy-start(f32[1,1280]{1,0:T(1,128)S(1)} %get-tuple-element.94.refs_5_.refs_3_) | copy-start | bytes 15364
  33.2 1.9 copy-start.8
  35.1 6.8 %copy-start.9 = (bf16[1,1280,1280]{2,1,0:T(8,128)(2,1)S(1)}, bf16[1,1280,1280]{2,1,0:T(8,128)(2,1)}, u32[]{:S(2)}) copy-start(bf16[1,1280,1280]{2,1,0:T(8,128)(2,1)} %param.13) | copy-start | bytes 9830404
  39.5 7.7 %collective-permute-start.4 = (bf16[2,64,1280]{2,1,0:T(8,128)(2,1)S(1)}, bf16[2,64,1280]{2,1,0:T(8,128)(2,1)S(1)}, u32[]{:S(2)}, u32[]{:S(2)}) collective-permute-start(bf16[2,64,1280]{2,1,0:T(8,128)(2,1)S(1)} %get-tuple-element.50), channel_id=1, source_target_pairs={{0,16},{1,17},{2,18},{3,19},{4,20},{5,21},{6,22},{7,23},{8,24},{9,... | collective-permute-start | bytes 983048 | tf_op jit(solution)/shard_map/ppermute | solution.py:526
  44.3 47.0 %collective-permute-start.14 = (bf16[640,1280]{1,0:T(8,128)(2,1)}, bf16[640,1280]{1,0:T(8,128)(2,1)}, u32[]{:S(2)}, u32[]{:S(2)}) collective-permute-start(bf16[640,1280]{1,0:T(8,128)(2,1)} %get-tuple-element.64), channel_id=1, source_target_pairs={{16,0},{17,1},{18,2},{19,3},{20,4},{21,5},{22,6},{23,7},{24,8},{25... | collective-permute-start | bytes 4915208 | tf_op jit(solution)/shard_map/ppermute | solution.py:511
  45.6 18.3 %collective-permute-start.9 = (bf16[320,1280]{1,0:T(8,128)(2,1)}, bf16[320,1280]{1,0:T(8,128)(2,1)}, u32[]{:S(2)}, u32[]{:S(2)}) collective-permute-start(bf16[320,1280]{1,0:T(8,128)(2,1)} %collective-permute-done.3.refs_6_.refs_1_), channel_id=1, source_target_pairs={{0,8},{4,12},{8,0},{12,4},{1,9},{5,13},{9,1},{13,5},{2,10},{6,14},... | collective-permute-start | bytes 2457608 | tf_op jit(solution)/shard_map/ppermute | solution.py:26
  47.2 0.7 copy-start.4
  51.3 22.3 %collective-permute-start.5 = (bf16[2,64,1280]{2,1,0:T(8,128)(2,1)S(1)}, bf16[2,64,1280]{2,1,0:T(8,128)(2,1)S(1)}, u32[]{:S(2)}, u32[]{:S(2)}) collective-permute-start(bf16[2,64,1280]{2,1,0:T(8,128)(2,1)S(1)} %get-tuple-element.54), channel_id=1, source_target_pairs={{0,16},{1,17},{2,18},{3,19},{4,20},{5,21},{6,22},{7,23},{8,24},{9,... | collective-permute-start | bytes 983048 | tf_op jit(solution)/shard_map/ppermute | solution.py:526
  57.0 10.0 %collective-permute-start.6 = (bf16[64,1280]{1,0:T(8,128)(2,1)S(1)}, bf16[64,1280]{1,0:T(8,128)(2,1)S(1)}, u32[]{:S(2)}, u32[]{:S(2)}) collective-permute-start(bf16[64,1280]{1,0:T(8,128)(2,1)S(1)} %get-tuple-element.55), channel_id=1, source_target_pairs={{0,3},{1,0},{2,1},{3,2},{4,7},{5,4},{6,5},{7,6},{8,11},{9,8},{10,9... | collective-permute-start | bytes 491528 | tf_op jit(solution)/shard_map/ppermute | solution.py:21
  59.1 14.5 %collective-permute-start.7 = (bf16[64,1280]{1,0:T(8,128)(2,1)S(1)}, bf16[64,1280]{1,0:T(8,128)(2,1)S(1)}, u32[]{:S(2)}, u32[]{:S(2)}) collective-permute-start(bf16[64,1280]{1,0:T(8,128)(2,1)S(1)} %get-tuple-element.56), channel_id=1, source_target_pairs={{0,1},{1,2},{2,3},{3,0},{4,5},{5,6},{6,7},{7,4},{8,9},{9,10},{10,1... | collective-permute-start | bytes 491528 | tf_op jit(solution)/shard_map/ppermute | solution.py:21
  65.8 11.2 %collective-permute-start.10 = (bf16[2,320,1280]{2,1,0:T(8,128)(2,1)S(1)}, bf16[2,320,1280]{2,1,0:T(8,128)(2,1)S(1)}, u32[]{:S(2)}, u32[]{:S(2)}) collective-permute-start(bf16[2,320,1280]{2,1,0:T(8,128)(2,1)S(1)} %get-tuple-element.60), channel_id=1, source_target_pairs={{0,4},{4,0},{8,12},{12,8},{1,5},{5,1},{9,13},{13,9},{2,6},{6,2},{1... | collective-permute-start | bytes 4915208 | tf_op jit(solution)/shard_map/ppermute | solution.py:26
  74.8 10.7 %collective-permute-start.8 = (bf16[64,1280]{1,0:T(8,128)(2,1)S(1)}, bf16[64,1280]{1,0:T(8,128)(2,1)S(1)}, u32[]{:S(2)}, u32[]{:S(2)}) collective-permute-start(bf16[64,1280]{1,0:T(8,128)(2,1)S(1)} %get-tuple-element.58), channel_id=1, source_target_pairs={{0,2},{1,3},{2,0},{3,1},{4,6},{5,7},{6,4},{7,5},{8,10},{9,11},{10,... | collective-permute-start | bytes 491528 | tf_op jit(solution)/shard_map/ppermute | solution.py:21
  87.2 9.1 %collective-permute-start.11 = (bf16[64,1280]{1,0:T(8,128)(2,1)}, bf16[64,1280]{1,0:T(8,128)(2,1)S(1)}, u32[]{:S(2)}, u32[]{:S(2)}) collective-permute-start(bf16[64,1280]{1,0:T(8,128)(2,1)} %get-tuple-element.62.refs_1_), channel_id=1, source_target_pairs={{0,1},{1,2},{2,3},{3,0},{4,5},{5,6},{6,7},{7,4},{8,9},{9,10},{10,1... | collective-permute-start | bytes 491528 | tf_op jit(solution)/shard_map/ppermute | solution.py:21
  87.2 11.9 %collective-permute-start.13 = (bf16[64,1280]{1,0:T(8,128)(2,1)}, bf16[64,1280]{1,0:T(8,128)(2,1)S(1)}, u32[]{:S(2)}, u32[]{:S(2)}) collective-permute-start(bf16[64,1280]{1,0:T(8,128)(2,1)} %get-tuple-element.62.refs_1_), channel_id=1, source_target_pairs={{0,3},{1,0},{2,1},{3,2},{4,7},{5,4},{6,5},{7,6},{8,11},{9,8},{10,9... | collective-permute-start | bytes 491528 | tf_op jit(solution)/shard_map/ppermute | solution.py:21
  91.2 10.0 %copy-start.5 = (f32[1,1280]{1,0:T(1,128)S(1)}, f32[1,1280]{1,0:T(1,128)}, u32[]{:S(2)}) copy-start(f32[1,1280]{1,0:T(1,128)} %copy-done.3) | copy-start | bytes 15364
  91.2 16.7 %collective-permute-start.12 = (bf16[64,1280]{1,0:T(8,128)(2,1)}, bf16[64,1280]{1,0:T(8,128)(2,1)}, u32[]{:S(2)}, u32[]{:S(2)}) collective-permute-start(bf16[64,1280]{1,0:T(8,128)(2,1)} %get-tuple-element.62.refs_1_), channel_id=1, source_target_pairs={{0,2},{1,3},{2,0},{3,1},{4,6},{5,7},{6,4},{7,5},{8,10},{9,11},{10,... | collective-permute-start | bytes 491528 | tf_op jit(solution)/shard_map/ppermute | solution.py:21
  96.3 4.8 %copy-start.11 = (bf16[64,1280]{1,0:T(8,128)(2,1)}, bf16[64,1280]{1,0:T(8,128)(2,1)S(1)}, u32[]{:S(2)}) copy-start(bf16[64,1280]{1,0:T(8,128)(2,1)S(1)} %collective-permute-done.11.refs_2_) | copy-start | bytes 491524
  101.2 4.9 %collective-permute-start.15 = (bf16[1,640,1280]{2,1,0:T(8,128)(2,1)S(1)}, bf16[1,640,1280]{2,1,0:T(8,128)(2,1)S(1)}, u32[]{:S(2)}, u32[]{:S(2)}) collective-permute-start(bf16[1,640,1280]{2,1,0:T(8,128)(2,1)S(1)} %get-tuple-element.65), channel_id=1, source_target_pairs={{0,4},{4,0},{8,12},{12,8},{1,5},{5,1},{9,13},{13,9},{2,6},{6,2},{1... | collective-permute-start | bytes 4915208 | tf_op jit(solution)/shard_map/ppermute | solution.py:26
  106.0 2.4 %copy-start.10 = (bf16[1,1280,1280]{2,1,0:T(8,128)(2,1)S(1)}, bf16[1,1280,1280]{2,1,0:T(8,128)(2,1)}, u32[]{:S(2)}) copy-start(bf16[1,1280,1280]{2,1,0:T(8,128)(2,1)} %param.13) | copy-start | bytes 9830404
  106.0 2.4 %copy-start.12 = (bf16[64,1280]{1,0:T(8,128)(2,1)S(1)}, bf16[64,1280]{1,0:T(8,128)(2,1)}, u32[]{:S(2)}) copy-start(bf16[64,1280]{1,0:T(8,128)(2,1)} %copy-done.11) | copy-start | bytes 491524
  112.6 10.8 %collective-permute-start.16 = (f32[8,1280]{1,0:T(8,128)S(1)}, f32[8,1280]{1,0:T(8,128)S(1)}, u32[]{:S(2)}, u32[]{:S(2)}) collective-permute-start(f32[8,1280]{1,0:T(8,128)S(1)} %get-tuple-element.67.refs_1_), channel_id=1, source_target_pairs={{0,1},{1,2},{2,3},{3,0},{4,5},{5,6},{6,7},{7,4},{8,9},{9,10},{10,1... | collective-permute-start | bytes 122888 | tf_op jit(solution)/shard_map/ppermute | solution.py:21
  112.6 10.8 %collective-permute-start.17 = (f32[8,1280]{1,0:T(8,128)S(1)}, f32[8,1280]{1,0:T(8,128)S(1)}, u32[]{:S(2)}, u32[]{:S(2)}) collective-permute-start(f32[8,1280]{1,0:T(8,128)S(1)} %get-tuple-element.67.refs_1_), channel_id=1, source_target_pairs={{0,2},{1,3},{2,0},{3,1},{4,6},{5,7},{6,4},{7,5},{8,10},{9,11},{10,... | collective-permute-start | bytes 122888 | tf_op jit(solution)/shard_map/ppermute | solution.py:21
  114.3 9.1 %collective-permute-start.18 = (f32[8,1280]{1,0:T(8,128)S(1)}, f32[8,1280]{1,0:T(8,128)S(1)}, u32[]{:S(2)}, u32[]{:S(2)}) collective-permute-start(f32[8,1280]{1,0:T(8,128)S(1)} %get-tuple-element.67.refs_1_), channel_id=1, source_target_pairs={{0,3},{1,0},{2,1},{3,2},{4,7},{5,4},{6,5},{7,6},{8,11},{9,8},{10,9... | collective-permute-start | bytes 122888 | tf_op jit(solution)/shard_map/ppermute | solution.py:21
  118.0 40.4 %collective-permute-start.28 = (bf16[640,1280]{1,0:T(8,128)(2,1)S(1)}, bf16[640,1280]{1,0:T(8,128)(2,1)S(1)}, u32[]{:S(2)}, u32[]{:S(2)}) collective-permute-start(bf16[640,1280]{1,0:T(8,128)(2,1)S(1)} %get-tuple-element.83), channel_id=1, source_target_pairs={{0,16},{1,17},{2,18},{3,19},{4,20},{5,21},{6,22},{7,23},{8,24},{9,... | collective-permute-start | bytes 4915208 | tf_op jit(solution)/shard_map/ppermute | solution.py:541
  126.9 32.6 %collective-permute-start.19 = (bf16[64,1280]{1,0:T(8,128)(2,1)S(1)}, bf16[64,1280]{1,0:T(8,128)(2,1)S(1)}, u32[]{:S(2)}, u32[]{:S(2)}) collective-permute-start(bf16[64,1280]{1,0:T(8,128)(2,1)S(1)} %get-tuple-element.74), channel_id=1, source_target_pairs={{0,3},{1,0},{2,1},{3,2},{4,7},{5,4},{6,5},{7,6},{8,11},{9,8},{10,9... | collective-permute-start | bytes 491528 | tf_op jit(solution)/shard_map/ppermute | solution.py:21
  127.3 32.2 %collective-permute-start.20 = (bf16[64,1280]{1,0:T(8,128)(2,1)S(1)}, bf16[64,1280]{1,0:T(8,128)(2,1)S(1)}, u32[]{:S(2)}, u32[]{:S(2)}) collective-permute-start(bf16[64,1280]{1,0:T(8,128)(2,1)S(1)} %get-tuple-element.75), channel_id=1, source_target_pairs={{0,2},{1,3},{2,0},{3,1},{4,6},{5,7},{6,4},{7,5},{8,10},{9,11},{10,... | collective-permute-start | bytes 491528 | tf_op jit(solution)/shard_map/ppermute | solution.py:21
  128.7 30.7 %collective-permute-start.21 = (bf16[64,1280]{1,0:T(8,128)(2,1)S(1)}, bf16[64,1280]{1,0:T(8,128)(2,1)S(1)}, u32[]{:S(2)}, u32[]{:S(2)}) collective-permute-start(bf16[64,1280]{1,0:T(8,128)(2,1)S(1)} %get-tuple-element.76), channel_id=1, source_target_pairs={{0,1},{1,2},{2,3},{3,0},{4,5},{5,6},{6,7},{7,4},{8,9},{9,10},{10,1... | collective-permute-start | bytes 491528 | tf_op jit(solution)/shard_map/ppermute | solution.py:21
  158.3 1.2 copy-start.2
  159.4 22.9 %collective-permute-start.29 = (bf16[1,640,1280]{2,1,0:T(8,128)(2,1)S(1)}, bf16[1,640,1280]{2,1,0:T(8,128)(2,1)S(1)}, u32[]{:S(2)}, u32[]{:S(2)}) collective-permute-start(bf16[1,640,1280]{2,1,0:T(8,128)(2,1)S(1)} %get-tuple-element.84), channel_id=1, source_target_pairs={{0,4},{4,0},{8,12},{12,8},{1,5},{5,1},{9,13},{13,9},{2,6},{6,2},{1... | collective-permute-start | bytes 4915208 | tf_op jit(solution)/shard_map/ppermute | solution.py:26
  161.2 8.8 %collective-permute-start.22 = (bf16[64,1280]{1,0:T(8,128)(2,1)S(1)}, bf16[64,1280]{1,0:T(8,128)(2,1)S(1)}, u32[]{:S(2)}, u32[]{:S(2)}) collective-permute-start(bf16[64,1280]{1,0:T(8,128)(2,1)S(1)} %get-tuple-element.78.refs_1_), channel_id=1, source_target_pairs={{0,1},{1,2},{2,3},{3,0},{4,5},{5,6},{6,7},{7,4},{8,9},{9,10},{10,1... | collective-permute-start | bytes 491528 | tf_op jit(solution)/shard_map/ppermute | solution.py:21
  161.8 9.8 %collective-permute-start.24 = (bf16[64,1280]{1,0:T(8,128)(2,1)S(1)}, bf16[64,1280]{1,0:T(8,128)(2,1)S(1)}, u32[]{:S(2)}, u32[]{:S(2)}) collective-permute-start(bf16[64,1280]{1,0:T(8,128)(2,1)S(1)} %get-tuple-element.78.refs_1_), channel_id=1, source_target_pairs={{0,3},{1,0},{2,1},{3,2},{4,7},{5,4},{6,5},{7,6},{8,11},{9,8},{10,9... | collective-permute-start | bytes 491528 | tf_op jit(solution)/shard_map/ppermute | solution.py:21
  165.1 14.8 %collective-permute-start.23 = (bf16[64,1280]{1,0:T(8,128)(2,1)S(1)}, bf16[64,1280]{1,0:T(8,128)(2,1)S(1)}, u32[]{:S(2)}, u32[]{:S(2)}) collective-permute-start(bf16[64,1280]{1,0:T(8,128)(2,1)S(1)} %get-tuple-element.78.refs_1_), channel_id=1, source_target_pairs={{0,2},{1,3},{2,0},{3,1},{4,6},{5,7},{6,4},{7,5},{8,10},{9,11},{10,... | collective-permute-start | bytes 491528 | tf_op jit(solution)/shard_map/ppermute | solution.py:21
  165.1 18.4 %collective-permute-start.25 = (bf16[64,1280]{1,0:T(8,128)(2,1)S(1)}, bf16[64,1280]{1,0:T(8,128)(2,1)S(1)}, u32[]{:S(2)}, u32[]{:S(2)}) collective-permute-start(bf16[64,1280]{1,0:T(8,128)(2,1)S(1)} %get-tuple-element.78.refs_1_), channel_id=1, source_target_pairs={{0,16},{16,0},{1,17},{17,1},{2,18},{18,2},{3,19},{19,3},{4,20},{20... | collective-permute-start | bytes 491528 | tf_op jit(solution)/shard_map/ppermute | solution.py:26
  171.7 14.7 %collective-permute-start.26 = (bf16[128,1280]{1,0:T(8,128)(2,1)S(1)}, bf16[128,1280]{1,0:T(8,128)(2,1)S(1)}, u32[]{:S(2)}, u32[]{:S(2)}) collective-permute-start(bf16[128,1280]{1,0:T(8,128)(2,1)S(1)} %pad_maximum_fusion), channel_id=1, source_target_pairs={{0,16},{16,0},{1,17},{17,1},{2,18},{18,2},{3,19},{19,3},{4,20},{20... | collective-permute-start | bytes 983048 | tf_op jit(solution)/shard_map/ppermute | solution.py:26
  179.8 6.6 %collective-permute-start.27 = (bf16[64,1280]{1,0:T(8,128)(2,1)S(1)}, bf16[64,1280]{1,0:T(8,128)(2,1)S(1)}, u32[]{:S(2)}, u32[]{:S(2)}) collective-permute-start(bf16[64,1280]{1,0:T(8,128)(2,1)S(1)} %collective-permute-done.23.refs_3_), channel_id=1, source_target_pairs={{0,16},{16,0},{1,17},{17,1},{2,18},{18,2},{3,19},{19,3},{4,20},{20... | collective-permute-start | bytes 491528 | tf_op jit(solution)/shard_map/ppermute | solution.py:26
  192.0 2.3 %collective-permute-start.30 = (bf16[2,160,1280]{2,1,0:T(8,128)(2,1)S(1)}, bf16[2,160,1280]{2,1,0:T(8,128)(2,1)S(1)}, u32[]{:S(2)}, u32[]{:S(2)}) collective-permute-start(bf16[2,160,1280]{2,1,0:T(8,128)(2,1)S(1)} %get-tuple-element.87), channel_id=1, source_target_pairs={{0,4},{4,0},{8,12},{12,8},{1,5},{5,1},{9,13},{13,9},{2,6},{6,2},{1... | collective-permute-start | bytes 2457608 | tf_op jit(solution)/shard_map/ppermute | solution.py:26
  192.0 5.0 %collective-permute-start.32 = (bf16[2,160,1280]{2,1,0:T(8,128)(2,1)S(1)}, bf16[2,160,1280]{2,1,0:T(8,128)(2,1)S(1)}, u32[]{:S(2)}, u32[]{:S(2)}) collective-permute-start(bf16[2,160,1280]{2,1,0:T(8,128)(2,1)S(1)} %get-tuple-element.91), channel_id=1, source_target_pairs={{0,4},{4,0},{8,12},{12,8},{1,5},{5,1},{9,13},{13,9},{2,6},{6,2},{1... | collective-permute-start | bytes 2457608 | tf_op jit(solution)/shard_map/ppermute | solution.py:26
  195.5 12.3 %collective-permute-start.31 = (bf16[160,1280]{1,0:T(8,128)(2,1)S(1)}, bf16[160,1280]{1,0:T(8,128)(2,1)S(1)}, u32[]{:S(2)}, u32[]{:S(2)}) collective-permute-start(bf16[160,1280]{1,0:T(8,128)(2,1)S(1)} %bitcast.30), channel_id=1, source_target_pairs={{0,8},{4,12},{8,0},{12,4},{1,9},{5,13},{9,1},{13,5},{2,10},{6,14},... | collective-permute-start | bytes 1228808 | tf_op jit(solution)/shard_map/ppermute | solution.py:21
  198.1 17.7 %collective-permute-start.33 = (bf16[160,1280]{1,0:T(8,128)(2,1)S(1)}, bf16[160,1280]{1,0:T(8,128)(2,1)S(1)}, u32[]{:S(2)}, u32[]{:S(2)}) collective-permute-start(bf16[160,1280]{1,0:T(8,128)(2,1)S(1)} %bitcast.31), channel_id=1, source_target_pairs={{0,8},{4,12},{8,0},{12,4},{1,9},{5,13},{9,1},{13,5},{2,10},{6,14},... | collective-permute-start | bytes 1228808 | tf_op jit(solution)/shard_map/ppermute | solution.py:21

commit v10 on v9

--- a/solution.py
+++ b/solution.py
@@ -30,6 +30,22 @@
     return [piece] + [rotated(piece, "tp", k) for k in range(1, lax.axis_size("tp"))]
 
 
+def near_and_far(count):
+    near = [k for k in range(1, count) if 2 * k != count]
+    return near, [k for k in range(1, count) if 2 * k == count]
+
+
+def gather_in_turn(piece, sel):
+    near, far = near_and_far(lax.axis_size("tp"))
+    parts = [piece] + [None] * (len(near) + len(far))
+    for k in near:
+        parts[k] = rotated(piece, "tp", k)
+    again, token = relayed(piece, sel, [parts[k] for k in near])
+    for k in far:
+        parts[k] = rotated(again, "tp", k)
+    return parts, token
+
+
 def gelu_pair(value):
     cdf = 0.5 * (1.0 + lax.erf(value * (1.0 / math.sqrt(2.0))))
     density = jnp.exp(-0.5 * value * value) * (1.0 / math.sqrt(2.0 * math.pi))
@@ -63,7 +79,7 @@
 TOKEN = jax.ShapeDtypeStruct((8, 128), jnp.float32)
 
 
-def run(body, name, sel, operands, outs, scratch, after=()):
+def run(body, name, sel, operands, outs, scratch, after=(), cost=COST):
     used, last = 1 + len(operands), 1 + len(operands) + len(after) + len(outs)
 
     def with_token(*refs):
@@ -79,7 +95,7 @@
         out_shape=[*outs, TOKEN],
         compiler_params=pltpu.CompilerParams(vmem_limit_bytes=max(VMEM_BYTES, 4 * sum(held))),
         cost_estimate=pl.CostEstimate(
-            flops=COST, bytes_accessed=COST // 200, transcendentals=0
+            flops=cost, bytes_accessed=cost // 200, transcendentals=0
         ),
         name=name,
     )(sel, *operands, *after)
@@ -114,6 +130,14 @@
     rows, hidden = weight.shape
     body = functools.partial(share_body, group)
     return run(body, "share", sel, [weight], [bf16(rows // group, hidden)], [], after)
+
+
+def relay_body(sel_ref, value, out):
+    out[...] = value[...]
+
+
+def relayed(value, sel, after):
+    return run(relay_body, "relay", sel, [value], [bf16(*value.shape)], [], after)
 
 
 def stack_body(sel_ref, *refs):
@@ -134,11 +158,12 @@
     rows, hidden = pieces[0].shape
     count = len(pieces)
     out = bf16(count, rows, hidden)
-    stacked = run(stack_body, "stack", sel, pieces, [out], [], after)[0]
+    stacked, token = run(stack_body, "stack", sel, pieces, [out], [], after)
     beside = swapped(stacked, "dp", 1)
     body = functools.partial(assemble_body, count)
     out = bf16(2 * count * rows, hidden)
-    return run(body, "assemble", sel, [*pieces, beside], [out], [])
+    whole, done = run(body, "assemble", sel, [*pieces, beside], [out], [])
+    return whole, token, done
 
 
 def partial_body(count, sel_ref, *refs):
@@ -222,8 +247,8 @@
 
 
 def crossing(count):
-    near = [k for k in range(1, count) if 2 * k != count]
-    return [0] + near + [k for k in range(1, count) if 2 * k == count]
+    near, far = near_and_far(count)
+    return [0] + near + far
 
 
 def state_body(count, sel_ref, *refs):
@@ -263,6 +288,7 @@
         [bf16(total, hidden), bf16(total, hidden), bf16(width // 2, total)],
         [pltpu.VMEM((total, width), jnp.bfloat16)],
         after,
+        cost=COST // 100,
     )
 
 
@@ -313,6 +339,7 @@
         + [jax.ShapeDtypeStruct((-(-images // 8) * 8, width), jnp.float32)],
         [pltpu.VMEM((n * rows, width), jnp.bfloat16)],
         after,
+        cost=COST // 100,
     )
     return outs[:n], outs[n]
 
@@ -377,6 +404,7 @@
         [*pools, *slopes, *own, *other],
         [bf16(rows, width)] * n + [jax.ShapeDtypeStruct((8, width), jnp.float32)],
         [pltpu.VMEM((n * rows, width), jnp.float32)],
+        cost=COST // 100,
     )
     return outs[:n], outs[n]
 
@@ -504,10 +532,13 @@
     alpha, sigma = jnp.cos(theta), jnp.sin(theta)
 
     flat = latents.reshape(count * tokens, width)
-    lat_parts = gather_parts(flat)
-    got_in = swapped(share(own[0], 4, sel, ())[0], "sec", 1)
+    near, far = near_and_far(n_tp)
+    rest = [0] + far
+    lat_parts, near_token = gather_in_turn(flat, sel)
+    in_share, in_token = share(own[0], 4, sel, ())
+    got_in = swapped(in_share, "sec", 1)
     across_in = swapped(got_in, "dp", 2)
-    out_share, out_token = share(own[1], 2, sel, [lat_parts[1], lat_parts[-1]])
+    out_share, out_token = share(own[1], 2, sel, [in_token])
     got_out = lax.ppermute(out_share, "sec", [(1, 0)])
 
     onehot = (
@@ -515,9 +546,7 @@
     ).astype(jnp.bfloat16)
     text_mine = dot_nn(onehot, prompt_table)
 
-    near = [k for k in range(1, n_tp) if 2 * k != n_tp]
-    rest = [0] + [k for k in range(1, n_tp) if 2 * k == n_tp]
-    sums, before = [], [got_in]
+    sums, before = [], [got_in, near_token]
     for ks in (near, rest):
         if ks:
             stay, leave, partial_token = block0_partials(
@@ -530,15 +559,16 @@
             else:
                 sums = [rotated(part, "tp", -k) for k, part in zip(ks, chosen)]
                 before = [picked_token, out_token]
-    other_in, in_token = assembled([got_in, across_in], sel, [partial_token])
-    mine_rows, unused = denoised(flat, sigma, alpha, sums, tokens, sel, [in_token])
+    other_in, unused, in_token = assembled([got_in, across_in], sel, [partial_token])
+    other_out, out_token, unused = assembled([got_out], sel, [picked_token])
+    other = (other_in, other_out)
+    late_share, late_token = share(own[1], 2, sel, [picked_token])
+    got_late = lax.ppermute(late_share, "sec", [(0, 1)])
+    mine_rows, unused = denoised(
+        flat, sigma, alpha, sums, tokens, sel, [in_token, out_token, late_token]
+    )
 
     seen_parts = gather_parts(mine_rows)
-    near_seen = [seen_parts[k] for k in near]
-    other_out, out_token = assembled([got_out], sel, near_seen)
-    other = (other_in, other_out)
-    late_share, late_token = share(own[1], 2, sel, [out_token])
-    got_late = lax.ppermute(late_share, "sec", [(0, 1)])
     slopes1, pool = reward_forward(
         seen_parts, tokens, gains[1:], text_mine, own, other, sel, ()
     )
@@ -546,7 +576,7 @@
     g_parts, g_mean = reward_back(pools, slopes1, tokens, own, other, sel)
 
     *states, state_token = block0_state(
-        lat_parts, gains[:1], own[0], other[0], sel, ()
+        lat_parts, gains[:1], own[0], other[0], sel, g_parts[:1]
     )
 
     g_sums = [g_parts[0]] + [rotated(g_parts[k], "tp", -k) for k in range(1, n_tp)]
@@ -555,13 +585,13 @@
         mine_rows, g_mean, gains[1:], ratio, g_sums, tokens, sel, [state_token]
     )
 
-    late_out = assembled([got_late], sel, [state_token])[0]
 
     g_mine = gather_parts(g_eps)
     pieces = list(g_mine)
-    for ks in ([0], near, rest[1:]):
+    for ks in ([0], near, far):
         if ks:
             pieces.append(swapped(jnp.concatenate([g_mine[k] for k in ks], 0), "sec", 1))
+    late_out = assembled([got_late], sel, [state_token])[0]
     out_parts, in_parts = gradients(pieces, states, own[1], late_out, sel)
     grad_out, grad_in = sum_over_dp(*out_parts, sel), sum_over_dp(*in_parts, sel)
     return (grad_in, grad_out)

time: 217 us -> 214 us (0.986)
  starting transfers between devices: 60.8 us -> 47.4 us
  local copies, waits for them, and re-layouts: 5.83 us -> 17.1 us
  waiting for transfers between devices: 96.2 us -> 91.9 us
  Pallas kernels: 48.1 us -> 51.5 us
    ppermute x1, waiting for transfers between devices: 27.5 us -> 0.01 us  [on_device(): got_late = lax.ppermute(late_share, 'sec', [(0, 1)])]
    ppermute x10, waiting for transfers between devices: 4.78 us -> 17.6 us  [swapped(): return lax.ppermute(value, axis, [(i, i ^ bit) for i in range(count)])]
    unnamed x32 -> x76, local copies, waits for them, and re-layouts: 4.55 us -> 15.8 us
    ppermute x20, waiting for transfers between devices: 63.9 us -> 74.3 us  [rotated(): lax.ppermute(value, axis, [(i, (i + steps) % count) for i in range(count)])]
    ppermute x10, starting transfers between devices: 12.6 us -> 4.33 us  [swapped(): return lax.ppermute(value, axis, [(i, i ^ bit) for i in range(count)])]
    ppermute x20, starting transfers between devices: 33.3 us -> 29.5 us  [rotated(): lax.ppermute(value, axis, [(i, (i + steps) % count) for i in range(count)])]
    pallas_call x21 -> x22, Pallas kernels: 48.1 us -> 51.5 us  [run(): pl.pallas_call(with_token, in_specs=[IN_SMEM] + [IN_VMEM] * (len(operands...]
    ppermute x1, starting transfers between devices: 5.47 us -> 2.72 us  [on_device(): got_late = lax.ppermute(late_share, 'sec', [(0, 1)])]
  transfers between devices with their start and end apart: 34 -> 34, of which waited for: 15 -> 19; matrix products, arithmetic and copies ran while one was open for 1% -> 1% of each run, Pallas kernels for 17% -> 19%
where the time goes in v10:
time: 214 us
  waiting for transfers between devices  91.9 us (43%)
  Pallas kernels  51.5 us (24%)
  starting transfers between devices  47.4 us (22%)
  local copies, waits for them, and re-layouts  17.1 us (8%)
  between operations  3.64 us (2%)
    ppermute x20, waiting for transfers between devices, rotated(): lax.ppermute(value, axis, [(i, (i + steps) % count) for i in range(count)])  74.3 us
    pallas_call x22, Pallas kernels, run(): pl.pallas_call(with_token, in_specs=[IN_SMEM] + [IN_VMEM] * (len(operands...  51.5 us
    ppermute x20, starting transfers between devices, rotated(): lax.ppermute(value, axis, [(i, (i + steps) % count) for i in range(count)])  29.5 us
    ppermute x10, waiting for transfers between devices, swapped(): return lax.ppermute(value, axis, [(i, i ^ bit) for i in range(count)])  17.6 us
    unnamed x76, local copies, waits for them, and re-layouts  15.8 us
    ppermute x2, starting transfers between devices, on_device(): crossed = lax.ppermute(leave, 'sec', [(0, 1)])  9.6 us
    ppermute x10, starting transfers between devices, swapped(): return lax.ppermute(value, axis, [(i, i ^ bit) for i in range(count)])  4.33 us
  transfers between devices with their start and end apart: 34, of which 19 were waited for; matrix products, arithmetic and copies ran while one was open for 1% of the time, Pallas kernels for 19%

profile of v10, /device:TPU:0, one launch (start us, length us, event | category | flops | bytes accessed | tf_op | source)
XLA Modules:
  0.0 213.7 jit_solution(10442173097552754462)
XLA Ops:
  0.6 3.1 %collective-permute-start = (bf16[128,1280]{1,0:T(8,128)(2,1)}, bf16[128,1280]{1,0:T(8,128)(2,1)}, u32[]{:S(2)}, u32[]{:S(2)}) collective-permute-start(bf16[128,1280]{1,0:T(8,128)(2,1)} %bitcast.30), channel_id=1, source_target_pairs={{0,1},{1,2},{2,3},{3,0},{4,5},{5,6},{6,7},{7,4},{8,9},{9,10},{10,1... | collective-permute-start | bytes 983048 | tf_op jit(solution)/shard_map/ppermute | solution.py:21
  3.7 2.1 collective-permute-start.1
  5.9 1.9 copy-done.1
  8.4 1.7 collective-permute-start.3
  10.2 4.4 %collective-permute-done.refs_2_.refs_1_ = bf16[128,1280]{1,0:T(8,128)(2,1)} collective-permute-done((bf16[128,1280]{1,0:T(8,128)(2,1)}, bf16[128,1280]{1,0:T(8,128)(2,1)}, u32[]{:S(2)}, u32[]{:S(2)}) %collective-permute-start) | collective-permute-done | bytes 327712 | tf_op jit(solution)/shard_map/ppermute | solution.py:21
  14.7 5.6 %collective-permute-done.1.refs_3_.refs_2_.refs_4_ = bf16[128,1280]{1,0:T(8,128)(2,1)} collective-permute-done((bf16[128,1280]{1,0:T(8,128)(2,1)}, bf16[128,1280]{1,0:T(8,128)(2,1)}, u32[]{:S(2)}, u32[]{:S(2)}) %collective-permute-start.1) | collective-permute-done | bytes 327712 | tf_op jit(solution)/shard_map/ppermute | solution.py:21
  20.2 1.1 relay.1
  22.1 6.2 %collective-permute-done.3.refs_6_.refs_1_ = bf16[320,1280]{1,0:T(8,128)(2,1)} collective-permute-done((bf16[320,1280]{1,0:T(8,128)(2,1)S(1)}, bf16[320,1280]{1,0:T(8,128)(2,1)}, u32[]{:S(2)}, u32[]{:S(2)}) %collective-permute-start.3) | collective-permute-done | bytes 819232 | tf_op jit(solution)/shard_map/ppermute | solution.py:26
  28.3 4.5 %block0_partial.2 = (bf16[2,64,1280]{2,1,0:T(8,128)(2,1)S(1)}, bf16[2,64,1280]{2,1,0:T(8,128)(2,1)}, f32[8,128]{1,0:T(8,128)}) custom-call(s32[4]{0:T(128)S(1)} %pad_add_fusion.refs_0_, bf16[128,1280]{1,0:T(8,128)(2,1)} %collective-permute-done.refs_2_.refs_1_, bf16[128,1280]{1,0:T(8,128)(2,1)} %collective-permute-done.1.refs_3_.refs_2_.refs_4_, ...), custom_call_target="tpu_custom_call" | custom-call | flops 99999997952 | bytes 500000000 | tf_op jit(solution)/shard_map/block0_partial/pallas_call | solution.py:90
  32.8 4.2 %collective-permute-start.4 = (bf16[2,64,1280]{2,1,0:T(8,128)(2,1)}, bf16[2,64,1280]{2,1,0:T(8,128)(2,1)}, u32[]{:S(2)}, u32[]{:S(2)}) collective-permute-start(bf16[2,64,1280]{2,1,0:T(8,128)(2,1)} %get-tuple-element.57), channel_id=1, source_target_pairs={{0,16},{1,17},{2,18},{3,19},{4,20},{5,21},{6,22},{7,23},{8,24},{9,... | collective-permute-start | bytes 983048 | tf_op jit(solution)/shard_map/ppermute | solution.py:555
  36.9 1.8 share.4
  38.8 1.3 collective-permute-start.11
  42.7 1.0 copy-done.34
  43.7 1.2 pick.2
  44.9 12.1 %collective-permute-done.2.refs_2_.refs_3_ = bf16[128,1280]{1,0:T(8,128)(2,1)S(1)} collective-permute-done((bf16[128,1280]{1,0:T(8,128)(2,1)}, bf16[128,1280]{1,0:T(8,128)(2,1)S(1)}, u32[]{:S(2)}, u32[]{:S(2)}) %collective-permute-start.2) | collective-permute-done | bytes 327712 | tf_op jit(solution)/shard_map/ppermute | solution.py:21
  57.0 2.9 %block0_partial.3 = (bf16[2,64,1280]{2,1,0:T(8,128)(2,1)S(1)}, bf16[2,64,1280]{2,1,0:T(8,128)(2,1)S(1)}, f32[8,128]{1,0:T(8,128)S(1)}) custom-call(s32[4]{0:T(128)S(1)} %pad_add_fusion.refs_0_, bf16[128,1280]{1,0:T(8,128)(2,1)S(1)} %bitcast.33, bf16[128,1280]{1,0:T(8,128)(2,1)S(1)} %collective-permute-done.2.refs_2_.refs_3_, ...), custom_call_target="tpu_custom_call" | custom-call | flops 99999997952 | bytes 500000000 | tf_op jit(solution)/shard_map/block0_partial/pallas_call | solution.py:90
  59.9 5.5 %collective-permute-start.5 = (bf16[2,64,1280]{2,1,0:T(8,128)(2,1)S(1)}, bf16[2,64,1280]{2,1,0:T(8,128)(2,1)S(1)}, u32[]{:S(2)}, u32[]{:S(2)}) collective-permute-start(bf16[2,64,1280]{2,1,0:T(8,128)(2,1)S(1)} %get-tuple-element.62), channel_id=1, source_target_pairs={{0,16},{1,17},{2,18},{3,19},{4,20},{5,21},{6,22},{7,23},{8,24},{9,... | collective-permute-start | bytes 983048 | tf_op jit(solution)/shard_map/ppermute | solution.py:555
  67.3 2.5 %collective-permute-start.6 = (bf16[64,1280]{1,0:T(8,128)(2,1)S(1)}, bf16[64,1280]{1,0:T(8,128)(2,1)S(1)}, u32[]{:S(2)}, u32[]{:S(2)}) collective-permute-start(bf16[64,1280]{1,0:T(8,128)(2,1)S(1)} %get-tuple-element.63), channel_id=1, source_target_pairs={{0,3},{1,0},{2,1},{3,2},{4,7},{5,4},{6,5},{7,6},{8,11},{9,8},{10,9... | collective-permute-start | bytes 491528 | tf_op jit(solution)/shard_map/ppermute | solution.py:21
  70.0 1.5 collective-permute-start.9
  71.5 3.0 %collective-permute-done.6.refs_3_ = bf16[64,1280]{1,0:T(8,128)(2,1)S(1)} collective-permute-done((bf16[64,1280]{1,0:T(8,128)(2,1)S(1)}, bf16[64,1280]{1,0:T(8,128)(2,1)S(1)}, u32[]{:S(2)}, u32[]{:S(2)}) %collective-permute-start.6) | collective-permute-done | bytes 163872 | tf_op jit(solution)/shard_map/ppermute | solution.py:21
  74.5 3.0 %collective-permute-done.7.refs_4_ = bf16[64,1280]{1,0:T(8,128)(2,1)S(1)} collective-permute-done((bf16[64,1280]{1,0:T(8,128)(2,1)S(1)}, bf16[64,1280]{1,0:T(8,128)(2,1)S(1)}, u32[]{:S(2)}, u32[]{:S(2)}) %collective-permute-start.7) | collective-permute-done | bytes 163872 | tf_op jit(solution)/shard_map/ppermute | solution.py:21
  77.5 1.2 pick.3
  78.7 1.9 share.5
  81.4 2.7 %collective-permute-start.28 = (bf16[640,1280]{1,0:T(8,128)(2,1)}, bf16[640,1280]{1,0:T(8,128)(2,1)}, u32[]{:S(2)}, u32[]{:S(2)}) collective-permute-start(bf16[640,1280]{1,0:T(8,128)(2,1)} %get-tuple-element.93), channel_id=1, source_target_pairs={{0,16},{1,17},{2,18},{3,19},{4,20},{5,21},{6,22},{7,23},{8,24},{9,... | collective-permute-start | bytes 4915208 | tf_op jit(solution)/shard_map/ppermute | solution.py:566
  84.1 5.8 %collective-permute-done.9.refs_2_ = bf16[320,1280]{1,0:T(8,128)(2,1)} collective-permute-done((bf16[320,1280]{1,0:T(8,128)(2,1)}, bf16[320,1280]{1,0:T(8,128)(2,1)}, u32[]{:S(2)}, u32[]{:S(2)}) %collective-permute-start.9) | collective-permute-done | bytes 819232 | tf_op jit(solution)/shard_map/ppermute | solution.py:26
  89.9 2.0 stack.23
  91.9 2.7 %stack.24 = (bf16[1,640,1280]{2,1,0:T(8,128)(2,1)}, f32[8,128]{1,0:T(8,128)S(1)}) custom-call(s32[4]{0:T(128)S(1)} %pad_add_fusion.refs_0_, bf16[640,1280]{1,0:T(8,128)(2,1)} %collective-permute-done.11.refs_1_, f32[8,128]{1,0:T(8,128)S(1)} %get-tuple-element.71.refs_2_), custom_call_target="tpu_custom_call" | custom-call | flops 99999997952 | bytes 500000000 | tf_op jit(solution)/shard_map/stack/pallas_call | solution.py:90
  95.4 1.6 assemble.3
  97.1 1.7 denoise.1
  98.8 4.1 %collective-permute-start.13 = (bf16[64,1280]{1,0:T(8,128)(2,1)S(1)}, bf16[64,1280]{1,0:T(8,128)(2,1)S(1)}, u32[]{:S(2)}, u32[]{:S(2)}) collective-permute-start(bf16[64,1280]{1,0:T(8,128)(2,1)S(1)} %get-tuple-element.74.refs_1_), channel_id=1, source_target_pairs={{0,2},{1,3},{2,0},{3,1},{4,6},{5,7},{6,4},{7,5},{8,10},{9,11},{10,... | collective-permute-start | bytes 491528 | tf_op jit(solution)/shard_map/ppermute | solution.py:21
  103.0 2.7 %assemble.4 = (bf16[1280,1280]{1,0:T(8,128)(2,1)S(1)}, f32[8,128]{1,0:T(8,128)}) custom-call(s32[4]{0:T(128)S(1)} %pad_add_fusion.refs_0_, bf16[640,1280]{1,0:T(8,128)(2,1)} %collective-permute-done.11.refs_1_, bf16[1,640,1280]{2,1,0:T(8,128)(2,1)} %collective-permute-done.15.refs_2_), custom_call_target="tpu_custom_call" | custom-call | flops 99999997952 | bytes 500000000 | tf_op jit(solution)/shard_map/assemble/pallas_call | solution.py:90
  105.7 2.1 collective-permute-done.12.refs_2_
  107.8 6.2 %collective-permute-done.13.refs_3_ = bf16[64,1280]{1,0:T(8,128)(2,1)S(1)} collective-permute-done((bf16[64,1280]{1,0:T(8,128)(2,1)S(1)}, bf16[64,1280]{1,0:T(8,128)(2,1)S(1)}, u32[]{:S(2)}, u32[]{:S(2)}) %collective-permute-start.13) | collective-permute-done | bytes 163872 | tf_op jit(solution)/shard_map/ppermute | solution.py:21
  114.0 3.8 %reward_forward.1 = (bf16[64,1280]{1,0:T(8,128)(2,1)S(1)}, bf16[64,1280]{1,0:T(8,128)(2,1)S(1)}, bf16[64,1280]{1,0:T(8,128)(2,1)S(1)}, bf16[64,1280]{1,0:T(8,128...) custom-call(s32[4]{0:T(128)S(1)} %pad_add_fusion.refs_0_, bf16[64,1280]{1,0:T(8,128)(2,1)S(1)} %get-tuple-element.74.refs_1_, ...), custom_call_target="tpu_custom_call" | custom-call | flops 1000000000 | bytes 5000000 | tf_op jit(solution)/shard_map/reward_forward/pallas_call | solution.py:90
  120.4 4.0 %collective-permute-start.16 = (f32[8,1280]{1,0:T(8,128)S(1)}, f32[8,1280]{1,0:T(8,128)S(1)}, u32[]{:S(2)}, u32[]{:S(2)}) collective-permute-start(f32[8,1280]{1,0:T(8,128)S(1)} %get-tuple-element.78.refs_1_), channel_id=1, source_target_pairs={{0,1},{1,2},{2,3},{3,0},{4,5},{5,6},{6,7},{7,4},{8,9},{9,10},{10,1... | collective-permute-start | bytes 122888 | tf_op jit(solution)/shard_map/ppermute | solution.py:21
  124.4 2.4 %collective-permute-start.18 = (f32[8,1280]{1,0:T(8,128)S(1)}, f32[8,1280]{1,0:T(8,128)}, u32[]{:S(2)}, u32[]{:S(2)}) collective-permute-start(f32[8,1280]{1,0:T(8,128)S(1)} %get-tuple-element.78.refs_1_), channel_id=1, source_target_pairs={{0,3},{1,0},{2,1},{3,2},{4,7},{5,4},{6,5},{7,6},{8,11},{9,8},{10,9... | collective-permute-start | bytes 122888 | tf_op jit(solution)/shard_map/ppermute | solution.py:21
  126.9 2.8 %collective-permute-done.17.refs_3_ = f32[8,1280]{1,0:T(8,128)} collective-permute-done((f32[8,1280]{1,0:T(8,128)S(1)}, f32[8,1280]{1,0:T(8,128)}, u32[]{:S(2)}, u32[]{:S(2)}) %collective-permute-start.17) | collective-permute-done | bytes 40992 | tf_op jit(solution)/shard_map/ppermute | solution.py:21
  129.7 1.9 copy-done.6
  131.6 1.9 copy-done.10
  133.6 1.9 copy-done.13
  135.5 0.9 copy-done.21
  136.4 0.9 copy-done.23
  137.3 0.9 copy-done.25
  138.2 0.9 copy-done.27
  139.2 4.0 %reward_back.1 = (bf16[64,1280]{1,0:T(8,128)(2,1)S(1)}, bf16[64,1280]{1,0:T(8,128)(2,1)S(1)}, bf16[64,1280]{1,0:T(8,128)(2,1)S(1)}, bf16[64,1280]{1,0:T(8,128)(2...) custom-call(s32[4]{0:T(128)S(1)} %pad_add_fusion.refs_0_, f32[8,1280]{1,0:T(8,128)S(1)} %get-tuple-element.78.refs_1_, ...), custom_call_target="tpu_custom_call" | custom-call | flops 1000000000 | bytes 5000000 | tf_op jit(solution)/shard_map/reward_back/pallas_call | solution.py:90
  143.1 3.0 %collective-permute-start.19 = (bf16[64,1280]{1,0:T(8,128)(2,1)S(1)}, bf16[64,1280]{1,0:T(8,128)(2,1)S(1)}, u32[]{:S(2)}, u32[]{:S(2)}) collective-permute-start(bf16[64,1280]{1,0:T(8,128)(2,1)S(1)} %get-tuple-element.85), channel_id=1, source_target_pairs={{0,3},{1,0},{2,1},{3,2},{4,7},{5,4},{6,5},{7,6},{8,11},{9,8},{10,9... | collective-permute-start | bytes 491528 | tf_op jit(solution)/shard_map/ppermute | solution.py:21
  146.9 4.4 %block0_state.1 = (bf16[512,1280]{1,0:T(8,128)(2,1)S(1)}, bf16[512,1280]{1,0:T(8,128)(2,1)S(1)}, bf16[640,512]{1,0:T(8,128)(2,1)S(1)}, f32[8,128]{1,0:T(8,128)S(1)}) custom-call(s32[4]{0:T(128)S(1)} %pad_add_fusion.refs_0_, bf16[128,1280]{1,0:T(8,128)(2,1)S(1)} %bitcast.35, bf16[128,1280]{1,0:T(8,128)(2,1)} %collective-permute-done.refs_2_.refs_1_, ...), custom_call_target="tpu_custom_call" | custom-call | flops 1000000000 | bytes 5000000 | tf_op jit(solution)/shard_map/block0_state/pallas_call | solution.py:90
  151.4 2.1 stack.25
  153.5 5.9 %collective-permute-done.20.refs_7_ = bf16[64,1280]{1,0:T(8,128)(2,1)S(1)} collective-permute-done((bf16[64,1280]{1,0:T(8,128)(2,1)S(1)}, bf16[64,1280]{1,0:T(8,128)(2,1)S(1)}, u32[]{:S(2)}, u32[]{:S(2)}) %collective-permute-start.20) | collective-permute-done | bytes 163872 | tf_op jit(solution)/shard_map/ppermute | solution.py:21
  159.4 1.4 eps_gradient.1
  160.9 3.7 %collective-permute-start.24 = (bf16[64,1280]{1,0:T(8,128)(2,1)S(1)}, bf16[64,1280]{1,0:T(8,128)(2,1)S(1)}, u32[]{:S(2)}, u32[]{:S(2)}) collective-permute-start(bf16[64,1280]{1,0:T(8,128)(2,1)S(1)} %get-tuple-element.89.refs_1_), channel_id=1, source_target_pairs={{0,3},{1,0},{2,1},{3,2},{4,7},{5,4},{6,5},{7,6},{8,11},{9,8},{10,9... | collective-permute-start | bytes 491528 | tf_op jit(solution)/shard_map/ppermute | solution.py:21
  164.8 5.0 %collective-permute-done.22.refs_2_ = bf16[64,1280]{1,0:T(8,128)(2,1)S(1)} collective-permute-done((bf16[64,1280]{1,0:T(8,128)(2,1)S(1)}, bf16[64,1280]{1,0:T(8,128)(2,1)S(1)}, u32[]{:S(2)}, u32[]{:S(2)}) %collective-permute-start.22) | collective-permute-done | bytes 163872 | tf_op jit(solution)/shard_map/ppermute | solution.py:21
  170.1 7.8 %collective-permute-done.23.refs_3_ = bf16[64,1280]{1,0:T(8,128)(2,1)S(1)} collective-permute-done((bf16[64,1280]{1,0:T(8,128)(2,1)S(1)}, bf16[64,1280]{1,0:T(8,128)(2,1)S(1)}, u32[]{:S(2)}, u32[]{:S(2)}) %collective-permute-start.23) | collective-permute-done | bytes 163872 | tf_op jit(solution)/shard_map/ppermute | solution.py:21
  177.9 2.0 assemble.5
  179.9 3.4 %collective-permute-done.27.refs_7_ = bf16[64,1280]{1,0:T(8,128)(2,1)S(1)} collective-permute-done((bf16[64,1280]{1,0:T(8,128)(2,1)S(1)}, bf16[64,1280]{1,0:T(8,128)(2,1)S(1)}, u32[]{:S(2)}, u32[]{:S(2)}) %collective-permute-start.27) | collective-permute-done | bytes 163872 | tf_op jit(solution)/shard_map/ppermute | solution.py:26
  183.3 5.6 %gradients.1 = (bf16[2,160,1280]{2,1,0:T(8,128)(2,1)S(1)}, bf16[2,160,1280]{2,1,0:T(8,128)(2,1)S(1)}, bf16[2,160,1280]{2,1,0:T(8,128)(2,1)S(1)}, bf16[2,160,1280]{2,1,0:T(8,128)(2,1)S(1)}, f32[8,128]{1,0:T(8,128)}) custom-call(s32[4]{0:T(128)S(1)} %pad_add_fusion.refs_0_, bf16[64,1280]{1,0:T(8,128)(2,1)S(1)} %get-tuple-element.89.refs_1_, ...), custom_call_target="tpu_custom_call" | custom-call | flops 99999997952 | bytes 500000000 | tf_op jit(solution)/shard_map/gradients/pallas_call | solution.py:90
  189.5 1.8 collective-permute-done.32.refs_2_
  191.3 1.1 chip_sum.3
  192.4 1.5 collective-permute-start.33
  193.9 1.1 chip_sum.2
  195.6 9.1 %collective-permute-done.33 = bf16[160,1280]{1,0:T(8,128)(2,1)S(1)} collective-permute-done((bf16[160,1280]{1,0:T(8,128)(2,1)S(1)}, bf16[160,1280]{1,0:T(8,128)(2,1)S(1)}, u32[]{:S(2)}, u32[]{:S(2)}) %collective-permute-start.33) | collective-permute-done | bytes 409632 | tf_op jit(solution)/shard_map/ppermute | solution.py:21
  204.7 1.0 convert_add_fusion
  205.7 7.0 %collective-permute-done.31 = bf16[160,1280]{1,0:T(8,128)(2,1)S(1)} collective-permute-done((bf16[160,1280]{1,0:T(8,128)(2,1)S(1)}, bf16[160,1280]{1,0:T(8,128)(2,1)S(1)}, u32[]{:S(2)}, u32[]{:S(2)}) %collective-permute-start.31) | collective-permute-done | bytes 409632 | tf_op jit(solution)/shard_map/ppermute | solution.py:21
  212.7 1.0 convert_add_fusion.1
  (113 shorter events, 10.2 us)
Async XLA Ops:
  0.6 69.2 %copy-start = (bf16[64,1280]{1,0:T(8,128)(2,1)S(1)}, bf16[64,1280]{1,0:T(8,128)(2,1)}, u32[]{:S(2)}) copy-start(bf16[64,1280]{1,0:T(8,128)(2,1)} %param.10) | copy-start | bytes 491524
  0.6 14.0 %collective-permute-start = (bf16[128,1280]{1,0:T(8,128)(2,1)}, bf16[128,1280]{1,0:T(8,128)(2,1)}, u32[]{:S(2)}, u32[]{:S(2)}) collective-permute-start(bf16[128,1280]{1,0:T(8,128)(2,1)} %bitcast.30), channel_id=1, source_target_pairs={{0,1},{1,2},{2,3},{3,0},{4,5},{5,6},{6,7},{7,4},{8,9},{9,10},{10,1... | collective-permute-start | bytes 983048 | tf_op jit(solution)/shard_map/ppermute | solution.py:21
  3.7 16.5 %collective-permute-start.1 = (bf16[128,1280]{1,0:T(8,128)(2,1)}, bf16[128,1280]{1,0:T(8,128)(2,1)}, u32[]{:S(2)}, u32[]{:S(2)}) collective-permute-start(bf16[128,1280]{1,0:T(8,128)(2,1)} %bitcast.31), channel_id=1, source_target_pairs={{0,3},{1,0},{2,1},{3,2},{4,7},{5,4},{6,5},{7,6},{8,11},{9,8},{10,9... | collective-permute-start | bytes 983048 | tf_op jit(solution)/shard_map/ppermute | solution.py:21
  5.9 1.9 copy-start.1
  7.8 2.4 %copy-start.35 = (f32[2,1280]{1,0:T(2,128)S(1)}, f32[2,1280]{1,0:T(2,128)}, u32[]{:S(2)}) copy-start(f32[2,1280]{1,0:T(2,128)} %param.11) | copy-start | bytes 30724
  7.8 12.4 %copy-start.14 = (bf16[2,64,1280]{2,1,0:T(8,128)(2,1)S(1)}, bf16[2,64,1280]{2,1,0:T(8,128)(2,1)}, u32[]{:S(2)}) copy-start(bf16[2,64,1280]{2,1,0:T(8,128)(2,1)} %param.7) | copy-start | bytes 983044
  8.4 19.9 %collective-permute-start.3 = (bf16[320,1280]{1,0:T(8,128)(2,1)S(1)}, bf16[320,1280]{1,0:T(8,128)(2,1)}, u32[]{:S(2)}, u32[]{:S(2)}) collective-permute-start(bf16[320,1280]{1,0:T(8,128)(2,1)S(1)} %get-tuple-element.54), channel_id=1, source_target_pairs={{0,16},{16,0},{1,17},{17,1},{2,18},{18,2},{3,19},{19,3},{4,20},{20... | collective-permute-start | bytes 2457608 | tf_op jit(solution)/shard_map/ppermute | solution.py:26
  10.2 46.8 %copy-start.30 = (f32[1,1280]{1,0:T(1,128)}, f32[1,1280]{1,0:T(1,128)S(1)}, u32[]{:S(2)}) copy-start(f32[1,1280]{1,0:T(1,128)S(1)} %get-tuple-element.105.refs_3_.refs_5_) | copy-start | bytes 15364
  10.2 18.1 %copy-start.2 = (bf16[1,1280,1280]{2,1,0:T(8,128)(2,1)S(1)}, bf16[1,1280,1280]{2,1,0:T(8,128)(2,1)}, u32[]{:S(2)}) copy-start(bf16[1,1280,1280]{2,1,0:T(8,128)(2,1)} %param.12) | copy-start | bytes 9830404
  10.2 18.1 %copy-start.8 = (bf16[1,1280,1280]{2,1,0:T(8,128)(2,1)S(1)}, bf16[1,1280,1280]{2,1,0:T(8,128)(2,1)}, u32[]{:S(2)}) copy-start(bf16[1,1280,1280]{2,1,0:T(8,128)(2,1)} %param.13) | copy-start | bytes 9830404
  32.8 6.0 %copy-start.33 = (bf16[2,64,1280]{2,1,0:T(8,128)(2,1)}, bf16[2,64,1280]{2,1,0:T(8,128)(2,1)S(1)}, u32[]{:S(2)}) copy-start(bf16[2,64,1280]{2,1,0:T(8,128)(2,1)S(1)} %get-tuple-element.56.refs_1_) | copy-start | bytes 983044
  32.8 9.9 %collective-permute-start.4 = (bf16[2,64,1280]{2,1,0:T(8,128)(2,1)}, bf16[2,64,1280]{2,1,0:T(8,128)(2,1)}, u32[]{:S(2)}, u32[]{:S(2)}) collective-permute-start(bf16[2,64,1280]{2,1,0:T(8,128)(2,1)} %get-tuple-element.57), channel_id=1, source_target_pairs={{0,16},{1,17},{2,18},{3,19},{4,20},{5,21},{6,22},{7,23},{8,24},{9,... | collective-permute-start | bytes 983048 | tf_op jit(solution)/shard_map/ppermute | solution.py:555
  36.9 3.1 %copy-start.36 = (s32[2]{0:T(128)S(1)}, s32[2]{0:T(128)}, u32[]{:S(2)}) copy-start(s32[2]{0:T(128)} %param.8) | copy-start | bytes 28
  38.8 53.1 %collective-permute-start.11 = (bf16[640,1280]{1,0:T(8,128)(2,1)}, bf16[640,1280]{1,0:T(8,128)(2,1)}, u32[]{:S(2)}, u32[]{:S(2)}) collective-permute-start(bf16[640,1280]{1,0:T(8,128)(2,1)} %get-tuple-element.70), channel_id=1, source_target_pairs={{16,0},{17,1},{18,2},{19,3},{20,4},{21,5},{22,6},{23,7},{24,8},{25... | collective-permute-start | bytes 4915208 | tf_op jit(solution)/shard_map/ppermute | solution.py:542
  42.0 15.0 %collective-permute-start.2 = (bf16[128,1280]{1,0:T(8,128)(2,1)}, bf16[128,1280]{1,0:T(8,128)(2,1)S(1)}, u32[]{:S(2)}, u32[]{:S(2)}) collective-permute-start(bf16[128,1280]{1,0:T(8,128)(2,1)} %copy-done.32), channel_id=1, source_target_pairs={{0,2},{1,3},{2,0},{3,1},{4,6},{5,7},{6,4},{7,5},{8,10},{9,11},{10,... | collective-permute-start | bytes 983048 | tf_op jit(solution)/shard_map/ppermute | solution.py:21
  42.7 1.0 copy-start.34
  43.7 13.3 %copy-start.3 = (bf16[1,1280,1280]{2,1,0:T(8,128)(2,1)S(1)}, bf16[1,1280,1280]{2,1,0:T(8,128)(2,1)}, u32[]{:S(2)}) copy-start(bf16[1,1280,1280]{2,1,0:T(8,128)(2,1)} %param.12) | copy-start | bytes 9830404
  43.7 13.3 %copy-start.15 = (bf16[2,64,1280]{2,1,0:T(8,128)(2,1)S(1)}, bf16[2,64,1280]{2,1,0:T(8,128)(2,1)}, u32[]{:S(2)}) copy-start(bf16[2,64,1280]{2,1,0:T(8,128)(2,1)} %param.7) | copy-start | bytes 983044
  57.0 3.0 %copy-start.18 = (bf16[128,1280]{1,0:T(8,128)(2,1)}, bf16[128,1280]{1,0:T(8,128)(2,1)S(1)}, u32[]{:S(2)}) copy-start(bf16[128,1280]{1,0:T(8,128)(2,1)S(1)} %collective-permute-done.2.refs_2_.refs_3_) | copy-start | bytes 983044
  57.0 8.4 %copy-start.37 = (s32[2]{0:T(128)S(1)}, s32[2]{0:T(128)}, u32[]{:S(2)}) copy-start(s32[2]{0:T(128)} %param.9) | copy-start | bytes 28
  59.9 17.6 %collective-permute-start.5 = (bf16[2,64,1280]{2,1,0:T(8,128)(2,1)S(1)}, bf16[2,64,1280]{2,1,0:T(8,128)(2,1)S(1)}, u32[]{:S(2)}, u32[]{:S(2)}) collective-permute-start(bf16[2,64,1280]{2,1,0:T(8,128)(2,1)S(1)} %get-tuple-element.62), channel_id=1, source_target_pairs={{0,16},{1,17},{2,18},{3,19},{4,20},{5,21},{6,22},{7,23},{8,24},{9,... | collective-permute-start | bytes 983048 | tf_op jit(solution)/shard_map/ppermute | solution.py:555
  67.3 7.2 %collective-permute-start.6 = (bf16[64,1280]{1,0:T(8,128)(2,1)S(1)}, bf16[64,1280]{1,0:T(8,128)(2,1)S(1)}, u32[]{:S(2)}, u32[]{:S(2)}) collective-permute-start(bf16[64,1280]{1,0:T(8,128)(2,1)S(1)} %get-tuple-element.63), channel_id=1, source_target_pairs={{0,3},{1,0},{2,1},{3,2},{4,7},{5,4},{6,5},{7,6},{8,11},{9,8},{10,9... | collective-permute-start | bytes 491528 | tf_op jit(solution)/shard_map/ppermute | solution.py:21
  69.9 7.6 %collective-permute-start.7 = (bf16[64,1280]{1,0:T(8,128)(2,1)S(1)}, bf16[64,1280]{1,0:T(8,128)(2,1)S(1)}, u32[]{:S(2)}, u32[]{:S(2)}) collective-permute-start(bf16[64,1280]{1,0:T(8,128)(2,1)S(1)} %get-tuple-element.64), channel_id=1, source_target_pairs={{0,1},{1,2},{2,3},{3,0},{4,5},{5,6},{6,7},{7,4},{8,9},{9,10},{10,1... | collective-permute-start | bytes 491528 | tf_op jit(solution)/shard_map/ppermute | solution.py:21
  70.0 19.9 %collective-permute-start.9 = (bf16[320,1280]{1,0:T(8,128)(2,1)}, bf16[320,1280]{1,0:T(8,128)(2,1)}, u32[]{:S(2)}, u32[]{:S(2)}) collective-permute-start(bf16[320,1280]{1,0:T(8,128)(2,1)} %collective-permute-done.3.refs_6_.refs_1_), channel_id=1, source_target_pairs={{0,8},{4,12},{8,0},{12,4},{1,9},{5,13},{9,1},{13,5},{2,10},{6,14},... | collective-permute-start | bytes 2457608 | tf_op jit(solution)/shard_map/ppermute | solution.py:26
  80.7 16.4 %collective-permute-start.8 = (bf16[64,1280]{1,0:T(8,128)(2,1)}, bf16[64,1280]{1,0:T(8,128)(2,1)}, u32[]{:S(2)}, u32[]{:S(2)}) collective-permute-start(bf16[64,1280]{1,0:T(8,128)(2,1)} %get-tuple-element.66), channel_id=1, source_target_pairs={{0,2},{1,3},{2,0},{3,1},{4,6},{5,7},{6,4},{7,5},{8,10},{9,11},{10,... | collective-permute-start | bytes 491528 | tf_op jit(solution)/shard_map/ppermute | solution.py:21
  81.4 70.0 %collective-permute-start.28 = (bf16[640,1280]{1,0:T(8,128)(2,1)}, bf16[640,1280]{1,0:T(8,128)(2,1)}, u32[]{:S(2)}, u32[]{:S(2)}) collective-permute-start(bf16[640,1280]{1,0:T(8,128)(2,1)} %get-tuple-element.93), channel_id=1, source_target_pairs={{0,16},{1,17},{2,18},{3,19},{4,20},{5,21},{6,22},{7,23},{8,24},{9,... | collective-permute-start | bytes 4915208 | tf_op jit(solution)/shard_map/ppermute | solution.py:566
  91.9 3.5 %collective-permute-start.10 = (bf16[2,320,1280]{2,1,0:T(8,128)(2,1)S(1)}, bf16[2,320,1280]{2,1,0:T(8,128)(2,1)S(1)}, u32[]{:S(2)}, u32[]{:S(2)}) collective-permute-start(bf16[2,320,1280]{2,1,0:T(8,128)(2,1)S(1)} %get-tuple-element.68), channel_id=1, source_target_pairs={{0,4},{4,0},{8,12},{12,8},{1,5},{5,1},{9,13},{13,9},{2,6},{6,2},{1... | collective-permute-start | bytes 4915208 | tf_op jit(solution)/shard_map/ppermute | solution.py:26
  94.7 2.4 %copy-start.16 = (bf16[2,64,1280]{2,1,0:T(8,128)(2,1)S(1)}, bf16[2,64,1280]{2,1,0:T(8,128)(2,1)}, u32[]{:S(2)}) copy-start(bf16[2,64,1280]{2,1,0:T(8,128)(2,1)} %param.7) | copy-start | bytes 983044
  94.7 8.3 %collective-permute-start.15 = (bf16[1,640,1280]{2,1,0:T(8,128)(2,1)}, bf16[1,640,1280]{2,1,0:T(8,128)(2,1)}, u32[]{:S(2)}, u32[]{:S(2)}) collective-permute-start(bf16[1,640,1280]{2,1,0:T(8,128)(2,1)} %get-tuple-element.76), channel_id=1, source_target_pairs={{0,4},{4,0},{8,12},{12,8},{1,5},{5,1},{9,13},{13,9},{2,6},{6,2},{1... | collective-permute-start | bytes 4915208 | tf_op jit(solution)/shard_map/ppermute | solution.py:26
  97.0 16.9 %copy-start.5 = (bf16[1280,1280]{1,0:T(8,128)(2,1)}, bf16[1280,1280]{1,0:T(8,128)(2,1)S(1)}, u32[]{:S(2)}) copy-start(bf16[1280,1280]{1,0:T(8,128)(2,1)S(1)} %get-tuple-element.75.refs_9_.refs_11_.refs_7_) | copy-start | bytes 9830404
  98.8 15.1 %copy-start.28 = (bf16[64,1280]{1,0:T(8,128)(2,1)}, bf16[64,1280]{1,0:T(8,128)(2,1)S(1)}, u32[]{:S(2)}) copy-start(bf16[64,1280]{1,0:T(8,128)(2,1)S(1)} %get-tuple-element.74.refs_1_) | copy-start | bytes 491524
  98.8 8.9 %collective-permute-start.12 = (bf16[64,1280]{1,0:T(8,128)(2,1)S(1)}, bf16[64,1280]{1,0:T(8,128)(2,1)S(1)}, u32[]{:S(2)}, u32[]{:S(2)}) collective-permute-start(bf16[64,1280]{1,0:T(8,128)(2,1)S(1)} %get-tuple-element.74.refs_1_), channel_id=1, source_target_pairs={{0,1},{1,2},{2,3},{3,0},{4,5},{5,6},{6,7},{7,4},{8,9},{9,10},{10,1... | collective-permute-start | bytes 491528 | tf_op jit(solution)/shard_map/ppermute | solution.py:21
  98.8 15.1 %collective-permute-start.13 = (bf16[64,1280]{1,0:T(8,128)(2,1)S(1)}, bf16[64,1280]{1,0:T(8,128)(2,1)S(1)}, u32[]{:S(2)}, u32[]{:S(2)}) collective-permute-start(bf16[64,1280]{1,0:T(8,128)(2,1)S(1)} %get-tuple-element.74.refs_1_), channel_id=1, source_target_pairs={{0,2},{1,3},{2,0},{3,1},{4,6},{5,7},{6,4},{7,5},{8,10},{9,11},{10,... | collective-permute-start | bytes 491528 | tf_op jit(solution)/shard_map/ppermute | solution.py:21
  102.9 11.0 %collective-permute-start.14 = (bf16[64,1280]{1,0:T(8,128)(2,1)S(1)}, bf16[64,1280]{1,0:T(8,128)(2,1)S(1)}, u32[]{:S(2)}, u32[]{:S(2)}) collective-permute-start(bf16[64,1280]{1,0:T(8,128)(2,1)S(1)} %get-tuple-element.74.refs_1_), channel_id=1, source_target_pairs={{0,3},{1,0},{2,1},{3,2},{4,7},{5,4},{6,5},{7,6},{8,11},{9,8},{10,9... | collective-permute-start | bytes 491528 | tf_op jit(solution)/shard_map/ppermute | solution.py:21
  103.0 11.0 %copy-start.4 = (bf16[1,1280,1280]{2,1,0:T(8,128)(2,1)S(1)}, bf16[1,1280,1280]{2,1,0:T(8,128)(2,1)}, u32[]{:S(2)}) copy-start(bf16[1,1280,1280]{2,1,0:T(8,128)(2,1)} %param.12) | copy-start | bytes 9830404
  103.0 11.0 %copy-start.9 = (bf16[1,1280,1280]{2,1,0:T(8,128)(2,1)S(1)}, bf16[1,1280,1280]{2,1,0:T(8,128)(2,1)}, u32[]{:S(2)}) copy-start(bf16[1,1280,1280]{2,1,0:T(8,128)(2,1)} %param.13) | copy-start | bytes 9830404
  105.7 12.1 %copy-start.12 = (bf16[1280,1280]{1,0:T(8,128)(2,1)}, bf16[1280,1280]{1,0:T(8,128)(2,1)S(1)}, u32[]{:S(2)}) copy-start(bf16[1280,1280]{1,0:T(8,128)(2,1)S(1)} %get-tuple-element.77.refs_10_.refs_12_) | copy-start | bytes 9830404
  120.4 6.4 %collective-permute-start.16 = (f32[8,1280]{1,0:T(8,128)S(1)}, f32[8,1280]{1,0:T(8,128)S(1)}, u32[]{:S(2)}, u32[]{:S(2)}) collective-permute-start(f32[8,1280]{1,0:T(8,128)S(1)} %get-tuple-element.78.refs_1_), channel_id=1, source_target_pairs={{0,1},{1,2},{2,3},{3,0},{4,5},{5,6},{6,7},{7,4},{8,9},{9,10},{10,1... | collective-permute-start | bytes 122888 | tf_op jit(solution)/shard_map/ppermute | solution.py:21
  124.4 5.3 %collective-permute-start.17 = (f32[8,1280]{1,0:T(8,128)S(1)}, f32[8,1280]{1,0:T(8,128)}, u32[]{:S(2)}, u32[]{:S(2)}) collective-permute-start(f32[8,1280]{1,0:T(8,128)S(1)} %get-tuple-element.78.refs_1_), channel_id=1, source_target_pairs={{0,2},{1,3},{2,0},{3,1},{4,6},{5,7},{6,4},{7,5},{8,10},{9,11},{10,... | collective-permute-start | bytes 122888 | tf_op jit(solution)/shard_map/ppermute | solution.py:21
  124.4 5.3 %collective-permute-start.18 = (f32[8,1280]{1,0:T(8,128)S(1)}, f32[8,1280]{1,0:T(8,128)}, u32[]{:S(2)}, u32[]{:S(2)}) collective-permute-start(f32[8,1280]{1,0:T(8,128)S(1)} %get-tuple-element.78.refs_1_), channel_id=1, source_target_pairs={{0,3},{1,0},{2,1},{3,2},{4,7},{5,4},{6,5},{7,6},{8,11},{9,8},{10,9... | collective-permute-start | bytes 122888 | tf_op jit(solution)/shard_map/ppermute | solution.py:21
  129.7 1.9 copy-start.6
  131.6 1.9 copy-start.10
  133.6 1.9 copy-start.13
  137.3 0.9 copy-start.25
  139.1 7.8 %copy-start.7 = (bf16[1280,1280]{1,0:T(8,128)(2,1)S(1)}, bf16[1280,1280]{1,0:T(8,128)(2,1)}, u32[]{:S(2)}) copy-start(bf16[1280,1280]{1,0:T(8,128)(2,1)} %copy-done.5) | copy-start | bytes 9830404
  139.1 7.8 %copy-start.17 = (bf16[2,64,1280]{2,1,0:T(8,128)(2,1)S(1)}, bf16[2,64,1280]{2,1,0:T(8,128)(2,1)}, u32[]{:S(2)}) copy-start(bf16[2,64,1280]{2,1,0:T(8,128)(2,1)} %param.7) | copy-start | bytes 983044
  139.1 7.8 %copy-start.19 = (bf16[128,1280]{1,0:T(8,128)(2,1)S(1)}, bf16[128,1280]{1,0:T(8,128)(2,1)}, u32[]{:S(2)}) copy-start(bf16[128,1280]{1,0:T(8,128)(2,1)} %copy-done.18) | copy-start | bytes 983044
  139.2 7.8 %copy-start.31 = (f32[1,1280]{1,0:T(1,128)S(1)}, f32[1,1280]{1,0:T(1,128)}, u32[]{:S(2)}) copy-start(f32[1,1280]{1,0:T(1,128)} %copy-done.30) | copy-start | bytes 15364
  143.1 10.3 %collective-permute-start.19 = (bf16[64,1280]{1,0:T(8,128)(2,1)S(1)}, bf16[64,1280]{1,0:T(8,128)(2,1)S(1)}, u32[]{:S(2)}, u32[]{:S(2)}) collective-permute-start(bf16[64,1280]{1,0:T(8,128)(2,1)S(1)} %get-tuple-element.85), channel_id=1, source_target_pairs={{0,3},{1,0},{2,1},{3,2},{4,7},{5,4},{6,5},{7,6},{8,11},{9,8},{10,9... | collective-permute-start | bytes 491528 | tf_op jit(solution)/shard_map/ppermute | solution.py:21
  146.1 13.3 %collective-permute-start.20 = (bf16[64,1280]{1,0:T(8,128)(2,1)S(1)}, bf16[64,1280]{1,0:T(8,128)(2,1)S(1)}, u32[]{:S(2)}, u32[]{:S(2)}) collective-permute-start(bf16[64,1280]{1,0:T(8,128)(2,1)S(1)} %get-tuple-element.86), channel_id=1, source_target_pairs={{0,2},{1,3},{2,0},{3,1},{4,6},{5,7},{6,4},{7,5},{8,10},{9,11},{10,... | collective-permute-start | bytes 491528 | tf_op jit(solution)/shard_map/ppermute | solution.py:21
  146.1 13.3 %collective-permute-start.21 = (bf16[64,1280]{1,0:T(8,128)(2,1)S(1)}, bf16[64,1280]{1,0:T(8,128)(2,1)S(1)}, u32[]{:S(2)}, u32[]{:S(2)}) collective-permute-start(bf16[64,1280]{1,0:T(8,128)(2,1)S(1)} %get-tuple-element.87), channel_id=1, source_target_pairs={{0,1},{1,2},{2,3},{3,0},{4,5},{5,6},{6,7},{7,4},{8,9},{9,10},{10,1... | collective-permute-start | bytes 491528 | tf_op jit(solution)/shard_map/ppermute | solution.py:21
  151.4 8.0 %copy-start.29 = (bf16[64,1280]{1,0:T(8,128)(2,1)S(1)}, bf16[64,1280]{1,0:T(8,128)(2,1)}, u32[]{:S(2)}) copy-start(bf16[64,1280]{1,0:T(8,128)(2,1)} %copy-done.28) | copy-start | bytes 491524
  153.5 24.4 %collective-permute-start.29 = (bf16[1,640,1280]{2,1,0:T(8,128)(2,1)S(1)}, bf16[1,640,1280]{2,1,0:T(8,128)(2,1)S(1)}, u32[]{:S(2)}, u32[]{:S(2)}) collective-permute-start(bf16[1,640,1280]{2,1,0:T(8,128)(2,1)S(1)} %get-tuple-element.94), channel_id=1, source_target_pairs={{0,4},{4,0},{8,12},{12,8},{1,5},{5,1},{9,13},{13,9},{2,6},{6,2},{1... | collective-permute-start | bytes 4915208 | tf_op jit(solution)/shard_map/ppermute | solution.py:26
  160.8 9.0 %collective-permute-start.22 = (bf16[64,1280]{1,0:T(8,128)(2,1)S(1)}, bf16[64,1280]{1,0:T(8,128)(2,1)S(1)}, u32[]{:S(2)}, u32[]{:S(2)}) collective-permute-start(bf16[64,1280]{1,0:T(8,128)(2,1)S(1)} %get-tuple-element.89.refs_1_), channel_id=1, source_target_pairs={{0,1},{1,2},{2,3},{3,0},{4,5},{5,6},{6,7},{7,4},{8,9},{9,10},{10,1... | collective-permute-start | bytes 491528 | tf_op jit(solution)/shard_map/ppermute | solution.py:21
  160.9 9.1 %collective-permute-start.24 = (bf16[64,1280]{1,0:T(8,128)(2,1)S(1)}, bf16[64,1280]{1,0:T(8,128)(2,1)S(1)}, u32[]{:S(2)}, u32[]{:S(2)}) collective-permute-start(bf16[64,1280]{1,0:T(8,128)(2,1)S(1)} %get-tuple-element.89.refs_1_), channel_id=1, source_target_pairs={{0,3},{1,0},{2,1},{3,2},{4,7},{5,4},{6,5},{7,6},{8,11},{9,8},{10,9... | collective-permute-start | bytes 491528 | tf_op jit(solution)/shard_map/ppermute | solution.py:21
  164.6 13.3 %collective-permute-start.23 = (bf16[64,1280]{1,0:T(8,128)(2,1)S(1)}, bf16[64,1280]{1,0:T(8,128)(2,1)S(1)}, u32[]{:S(2)}, u32[]{:S(2)}) collective-permute-start(bf16[64,1280]{1,0:T(8,128)(2,1)S(1)} %get-tuple-element.89.refs_1_), channel_id=1, source_target_pairs={{0,2},{1,3},{2,0},{3,1},{4,6},{5,7},{6,4},{7,5},{8,10},{9,11},{10,... | collective-permute-start | bytes 491528 | tf_op jit(solution)/shard_map/ppermute | solution.py:21
  164.8 15.1 %collective-permute-start.25 = (bf16[64,1280]{1,0:T(8,128)(2,1)S(1)}, bf16[64,1280]{1,0:T(8,128)(2,1)S(1)}, u32[]{:S(2)}, u32[]{:S(2)}) collective-permute-start(bf16[64,1280]{1,0:T(8,128)(2,1)S(1)} %get-tuple-element.89.refs_1_), channel_id=1, source_target_pairs={{0,16},{16,0},{1,17},{17,1},{2,18},{18,2},{3,19},{19,3},{4,20},{20... | collective-permute-start | bytes 491528 | tf_op jit(solution)/shard_map/ppermute | solution.py:26
  170.0 13.3 %copy-start.11 = (bf16[1,1280,1280]{2,1,0:T(8,128)(2,1)S(1)}, bf16[1,1280,1280]{2,1,0:T(8,128)(2,1)}, u32[]{:S(2)}) copy-start(bf16[1,1280,1280]{2,1,0:T(8,128)(2,1)} %param.13) | copy-start | bytes 9830404
  170.0 13.3 %collective-permute-start.26 = (bf16[128,1280]{1,0:T(8,128)(2,1)S(1)}, bf16[128,1280]{1,0:T(8,128)(2,1)S(1)}, u32[]{:S(2)}, u32[]{:S(2)}) collective-permute-start(bf16[128,1280]{1,0:T(8,128)(2,1)S(1)} %pad_maximum_fusion), channel_id=1, source_target_pairs={{0,16},{16,0},{1,17},{17,1},{2,18},{18,2},{3,19},{19,3},{4,20},{20... | collective-permute-start | bytes 983048 | tf_op jit(solution)/shard_map/ppermute | solution.py:26
  177.9 5.5 %collective-permute-start.27 = (bf16[64,1280]{1,0:T(8,128)(2,1)S(1)}, bf16[64,1280]{1,0:T(8,128)(2,1)S(1)}, u32[]{:S(2)}, u32[]{:S(2)}) collective-permute-start(bf16[64,1280]{1,0:T(8,128)(2,1)S(1)} %collective-permute-done.23.refs_3_), channel_id=1, source_target_pairs={{0,16},{16,0},{1,17},{17,1},{2,18},{18,2},{3,19},{19,3},{4,20},{20... | collective-permute-start | bytes 491528 | tf_op jit(solution)/shard_map/ppermute | solution.py:26
  189.0 2.3 %collective-permute-start.32 = (bf16[2,160,1280]{2,1,0:T(8,128)(2,1)S(1)}, bf16[2,160,1280]{2,1,0:T(8,128)(2,1)S(1)}, u32[]{:S(2)}, u32[]{:S(2)}) collective-permute-start(bf16[2,160,1280]{2,1,0:T(8,128)(2,1)S(1)} %get-tuple-element.101), channel_id=1, source_target_pairs={{0,4},{4,0},{8,12},{12,8},{1,5},{5,1},{9,13},{13,9},{2,6},{6,2},{1... | collective-permute-start | bytes 2457608 | tf_op jit(solution)/shard_map/ppermute | solution.py:26
  189.0 5.0 %collective-permute-start.30 = (bf16[2,160,1280]{2,1,0:T(8,128)(2,1)S(1)}, bf16[2,160,1280]{2,1,0:T(8,128)(2,1)S(1)}, u32[]{:S(2)}, u32[]{:S(2)}) collective-permute-start(bf16[2,160,1280]{2,1,0:T(8,128)(2,1)S(1)} %get-tuple-element.97), channel_id=1, source_target_pairs={{0,4},{4,0},{8,12},{12,8},{1,5},{5,1},{9,13},{13,9},{2,6},{6,2},{1... | collective-permute-start | bytes 2457608 | tf_op jit(solution)/shard_map/ppermute | solution.py:26
  192.4 12.3 %collective-permute-start.33 = (bf16[160,1280]{1,0:T(8,128)(2,1)S(1)}, bf16[160,1280]{1,0:T(8,128)(2,1)S(1)}, u32[]{:S(2)}, u32[]{:S(2)}) collective-permute-start(bf16[160,1280]{1,0:T(8,128)(2,1)S(1)} %bitcast.36), channel_id=1, source_target_pairs={{0,8},{4,12},{8,0},{12,4},{1,9},{5,13},{9,1},{13,5},{2,10},{6,14},... | collective-permute-start | bytes 1228808 | tf_op jit(solution)/shard_map/ppermute | solution.py:21
  195.1 17.7 %collective-permute-start.31 = (bf16[160,1280]{1,0:T(8,128)(2,1)S(1)}, bf16[160,1280]{1,0:T(8,128)(2,1)S(1)}, u32[]{:S(2)}, u32[]{:S(2)}) collective-permute-start(bf16[160,1280]{1,0:T(8,128)(2,1)S(1)} %bitcast.37), channel_id=1, source_target_pairs={{0,8},{4,12},{8,0},{12,4},{1,9},{5,13},{9,1},{13,5},{2,10},{6,14},... | collective-permute-start | bytes 1228808 | tf_op jit(solution)/shard_map/ppermute | solution.py:21
  (8 other events, 6.1 us)

commit v11 on v9

--- a/solution.py
+++ b/solution.py
@@ -63,7 +63,7 @@
 TOKEN = jax.ShapeDtypeStruct((8, 128), jnp.float32)
 
 
-def run(body, name, sel, operands, outs, scratch, after=()):
+def run(body, name, sel, operands, outs, scratch, after=(), cost=COST):
     used, last = 1 + len(operands), 1 + len(operands) + len(after) + len(outs)
 
     def with_token(*refs):
@@ -79,7 +79,7 @@
         out_shape=[*outs, TOKEN],
         compiler_params=pltpu.CompilerParams(vmem_limit_bytes=max(VMEM_BYTES, 4 * sum(held))),
         cost_estimate=pl.CostEstimate(
-            flops=COST, bytes_accessed=COST // 200, transcendentals=0
+            flops=cost, bytes_accessed=cost // 200, transcendentals=0
         ),
         name=name,
     )(sel, *operands, *after)
@@ -114,6 +114,14 @@
     rows, hidden = weight.shape
     body = functools.partial(share_body, group)
     return run(body, "share", sel, [weight], [bf16(rows // group, hidden)], [], after)
+
+
+def relay_body(sel_ref, value, out):
+    out[...] = value[...]
+
+
+def relayed(value, sel, after):
+    return run(relay_body, "relay", sel, [value], [bf16(*value.shape)], [], after)
 
 
 def stack_body(sel_ref, *refs):
@@ -504,10 +512,18 @@
     alpha, sigma = jnp.cos(theta), jnp.sin(theta)
 
     flat = latents.reshape(count * tokens, width)
-    lat_parts = gather_parts(flat)
+    near = [k for k in range(1, n_tp) if 2 * k != n_tp]
+    rest = [0] + [k for k in range(1, n_tp) if 2 * k == n_tp]
+    lat_parts = [flat] + [None] * (n_tp - 1)
+    for k in near:
+        lat_parts[k] = rotated(flat, "tp", k)
+    again, near_token = relayed(flat, sel, [lat_parts[k] for k in near])
+    for k in rest[1:]:
+        lat_parts[k] = rotated(again, "tp", k)
     got_in = swapped(share(own[0], 4, sel, ())[0], "sec", 1)
-    across_in = swapped(got_in, "dp", 2)
-    out_share, out_token = share(own[1], 2, sel, [lat_parts[1], lat_parts[-1]])
+    got_again, in_token = relayed(got_in, sel, [near_token])
+    across_in = swapped(got_again, "dp", 2)
+    out_share, out_token = share(own[1], 2, sel, [near_token])
     got_out = lax.ppermute(out_share, "sec", [(1, 0)])
 
     onehot = (
@@ -515,9 +531,7 @@
     ).astype(jnp.bfloat16)
     text_mine = dot_nn(onehot, prompt_table)
 
-    near = [k for k in range(1, n_tp) if 2 * k != n_tp]
-    rest = [0] + [k for k in range(1, n_tp) if 2 * k == n_tp]
-    sums, before = [], [got_in]
+    sums, before = [], [in_token]
     for ks in (near, rest):
         if ks:
             stay, leave, partial_token = block0_partials(
@@ -529,15 +543,15 @@
                 sums = [chosen[0]] + [rotated(part, "tp", -k) for k, part in zip(ks[1:], chosen[1:])]
             else:
                 sums = [rotated(part, "tp", -k) for k, part in zip(ks, chosen)]
-                before = [picked_token, out_token]
+                before = [partial_token, out_token]
     other_in, in_token = assembled([got_in, across_in], sel, [partial_token])
     mine_rows, unused = denoised(flat, sigma, alpha, sums, tokens, sel, [in_token])
 
     seen_parts = gather_parts(mine_rows)
     near_seen = [seen_parts[k] for k in near]
-    other_out, out_token = assembled([got_out], sel, near_seen)
+    other_out, joined_token = assembled([got_out], sel, near_seen)
     other = (other_in, other_out)
-    late_share, late_token = share(own[1], 2, sel, [out_token])
+    late_share, late_token = share(own[1], 2, sel, [joined_token])
     got_late = lax.ppermute(late_share, "sec", [(0, 1)])
     slopes1, pool = reward_forward(
         seen_parts, tokens, gains[1:], text_mine, own, other, sel, ()
@@ -546,7 +560,7 @@
     g_parts, g_mean = reward_back(pools, slopes1, tokens, own, other, sel)
 
     *states, state_token = block0_state(
-        lat_parts, gains[:1], own[0], other[0], sel, ()
+        lat_parts, gains[:1], own[0], other[0], sel, g_parts[:1]
     )
 
     g_sums = [g_parts[0]] + [rotated(g_parts[k], "tp", -k) for k in range(1, n_tp)]
@@ -555,13 +569,13 @@
         mine_rows, g_mean, gains[1:], ratio, g_sums, tokens, sel, [state_token]
     )
 
-    late_out = assembled([got_late], sel, [state_token])[0]
 
     g_mine = gather_parts(g_eps)
     pieces = list(g_mine)
     for ks in ([0], near, rest[1:]):
         if ks:
             pieces.append(swapped(jnp.concatenate([g_mine[k] for k in ks], 0), "sec", 1))
+    late_out = assembled([got_late], sel, [g_mine[k] for k in near])[0]
     out_parts, in_parts = gradients(pieces, states, own[1], late_out, sel)
     grad_out, grad_in = sum_over_dp(*out_parts, sel), sum_over_dp(*in_parts, sel)
     return (grad_in, grad_out)

time: 217 us -> 191 us (0.88)
  waiting for transfers between devices: 96.2 us -> 79 us
  starting transfers between devices: 60.8 us -> 50 us
  Pallas kernels: 48.1 us -> 52.5 us
  local copies, waits for them, and re-layouts: 5.83 us -> 3.36 us
    ppermute x1, waiting for transfers between devices: 27.5 us -> 3.74 us  [on_device(): got_late = lax.ppermute(late_share, 'sec', [(0, 1)])]
    ppermute x10, waiting for transfers between devices: 4.78 us -> 9.95 us  [swapped(): return lax.ppermute(value, axis, [(i, i ^ bit) for i in range(count)])]
    pallas_call x21 -> x23, Pallas kernels: 48.1 us -> 52.5 us  [run(): pl.pallas_call(with_token, in_specs=[IN_SMEM] + [IN_VMEM] * (len(operands...]
    ppermute x10, starting transfers between devices: 12.6 us -> 8.96 us  [swapped(): return lax.ppermute(value, axis, [(i, i ^ bit) for i in range(count)])]
    ppermute x1, starting transfers between devices: 5.47 us -> 2.45 us  [on_device(): got_late = lax.ppermute(late_share, 'sec', [(0, 1)])]
    unnamed x32 -> x52, local copies, waits for them, and re-layouts: 4.55 us -> 2.04 us
    ppermute x20, starting transfers between devices: 33.3 us -> 31 us  [rotated(): lax.ppermute(value, axis, [(i, (i + steps) % count) for i in range(count)])]
  transfers between devices with their start and end apart: 34 -> 34, of which waited for: 15 -> 18; matrix products, arithmetic and copies ran while one was open for 1% -> 1% of each run, Pallas kernels for 17% -> 20%
where the time goes in v11:
time: 191 us
  waiting for transfers between devices  79 us (41%)
  Pallas kernels  52.5 us (27%)
  starting transfers between devices  50 us (26%)
  between operations  3.77 us (2%)
  local copies, waits for them, and re-layouts  3.36 us (2%)
  other arithmetic  2.02 us (1%)
    ppermute x20, waiting for transfers between devices, rotated(): lax.ppermute(value, axis, [(i, (i + steps) % count) for i in range(count)])  65.3 us
    pallas_call x23, Pallas kernels, run(): pl.pallas_call(with_token, in_specs=[IN_SMEM] + [IN_VMEM] * (len(operands...  52.5 us
    ppermute x20, starting transfers between devices, rotated(): lax.ppermute(value, axis, [(i, (i + steps) % count) for i in range(count)])  31 us
    ppermute x10, waiting for transfers between devices, swapped(): return lax.ppermute(value, axis, [(i, i ^ bit) for i in range(count)])  9.95 us
    ppermute x10, starting transfers between devices, swapped(): return lax.ppermute(value, axis, [(i, i ^ bit) for i in range(count)])  8.96 us
    ppermute x2, starting transfers between devices, on_device(): crossed = lax.ppermute(leave, 'sec', [(0, 1)])  6.1 us
  transfers between devices with their start and end apart: 34, of which 18 were waited for; matrix products, arithmetic and copies ran while one was open for 1% of the time, Pallas kernels for 20%

profile of v11, /device:TPU:0, one launch (start us, length us, event | category | flops | bytes accessed | tf_op | source)
XLA Modules:
  0.0 190.8 jit_solution(12239048820162076521)
XLA Ops:
  0.6 3.1 %collective-permute-start = (bf16[128,1280]{1,0:T(8,128)(2,1)}, bf16[128,1280]{1,0:T(8,128)(2,1)S(1)}, u32[]{:S(2)}, u32[]{:S(2)}) collective-permute-start(bf16[128,1280]{1,0:T(8,128)(2,1)} %bitcast.32), channel_id=1, source_target_pairs={{0,1},{1,2},{2,3},{3,0},{4,5},{5,6},{6,7},{7,4},{8,9},{9,10},{10,1... | collective-permute-start | bytes 983048 | tf_op jit(solution)/shard_map/ppermute | solution.py:21
  3.7 2.1 %collective-permute-start.1 = (bf16[128,1280]{1,0:T(8,128)(2,1)}, bf16[128,1280]{1,0:T(8,128)(2,1)S(1)}, u32[]{:S(2)}, u32[]{:S(2)}) collective-permute-start(bf16[128,1280]{1,0:T(8,128)(2,1)} %bitcast.33), channel_id=1, source_target_pairs={{0,3},{1,0},{2,1},{3,2},{4,7},{5,4},{6,5},{7,6},{8,11},{9,8},{10,9... | collective-permute-start | bytes 983048 | tf_op jit(solution)/shard_map/ppermute | solution.py:21
  5.9 1.9 %copy-done.3 = bf16[1,1280,1280]{2,1,0:T(8,128)(2,1)S(1)} copy-done((bf16[1,1280,1280]{2,1,0:T(8,128)(2,1)S(1)}, bf16[1,1280,1280]{2,1,0:T(8,128)(2,1)}, u32[]{:S(2)}) %copy-start.3) | copy-done | bytes 3276824
  7.8 1.5 share.3
  9.3 1.7 collective-permute-start.3
  13.2 1.4 collective-permute-done.refs_2_.refs_1_
  14.5 5.6 %collective-permute-done.1.refs_3_.refs_2_.refs_4_ = bf16[128,1280]{1,0:T(8,128)(2,1)S(1)} collective-permute-done((bf16[128,1280]{1,0:T(8,128)(2,1)}, bf16[128,1280]{1,0:T(8,128)(2,1)S(1)}, u32[]{:S(2)}, u32[]{:S(2)}) %collective-permute-start.1) | collective-permute-done | bytes 327712 | tf_op jit(solution)/shard_map/ppermute | solution.py:21
  20.1 1.3 relay.2
  21.4 1.3 collective-permute-start.2
  22.7 1.8 share.4
  24.6 1.5 collective-permute-start.14
  26.1 3.9 %collective-permute-done.3.refs_1_ = bf16[320,1280]{1,0:T(8,128)(2,1)} collective-permute-done((bf16[320,1280]{1,0:T(8,128)(2,1)}, bf16[320,1280]{1,0:T(8,128)(2,1)}, u32[]{:S(2)}, u32[]{:S(2)}) %collective-permute-start.3) | collective-permute-done | bytes 819232 | tf_op jit(solution)/shard_map/ppermute | solution.py:26
  30.0 2.1 %relay.3 = (bf16[320,1280]{1,0:T(8,128)(2,1)}, f32[8,128]{1,0:T(8,128)S(1)}) custom-call(s32[4]{0:T(128)S(1)} %pad_add_fusion.refs_0_, bf16[320,1280]{1,0:T(8,128)(2,1)} %collective-permute-done.3.refs_1_, f32[8,128]{1,0:T(8,128)S(1)} %get-tuple-element.54.refs_2_), custom_call_target="tpu_custom_call" | custom-call | flops 99999997952 | bytes 500000000 | tf_op jit(solution)/shard_map/relay/pallas_call | solution.py:74
  32.1 1.7 collective-permute-start.9
  33.9 2.9 %block0_partial.2 = (bf16[2,64,1280]{2,1,0:T(8,128)(2,1)S(1)}, bf16[2,64,1280]{2,1,0:T(8,128)(2,1)S(1)}, f32[8,128]{1,0:T(8,128)S(1)}) custom-call(s32[4]{0:T(128)S(1)} %pad_add_fusion.refs_0_, bf16[128,1280]{1,0:T(8,128)(2,1)S(1)} %collective-permute-done.refs_2_.refs_1_, bf16[128,1280]{1,0:T(8,128)(2,1)S(1)} %collective-permute-done.1.refs_3_.refs_2_.refs_4_, ...), custom_call_target="tpu_custom_call" | custom-call | flops 99999997952 | bytes 500000000 | tf_op jit(solution)/shard_map/block0_partial/pallas_call | solution.py:74
  36.8 2.5 %collective-permute-start.5 = (bf16[2,64,1280]{2,1,0:T(8,128)(2,1)S(1)}, bf16[2,64,1280]{2,1,0:T(8,128)(2,1)S(1)}, u32[]{:S(2)}, u32[]{:S(2)}) collective-permute-start(bf16[2,64,1280]{2,1,0:T(8,128)(2,1)S(1)} %get-tuple-element.61), channel_id=1, source_target_pairs={{0,16},{1,17},{2,18},{3,19},{4,20},{5,21},{6,22},{7,23},{8,24},{9,... | collective-permute-start | bytes 983048 | tf_op jit(solution)/shard_map/ppermute | solution.py:540
  39.3 4.1 %block0_partial.3 = (bf16[2,64,1280]{2,1,0:T(8,128)(2,1)S(1)}, bf16[2,64,1280]{2,1,0:T(8,128)(2,1)}, f32[8,128]{1,0:T(8,128)S(1)}) custom-call(s32[4]{0:T(128)S(1)} %pad_add_fusion.refs_0_, bf16[128,1280]{1,0:T(8,128)(2,1)S(1)} %bitcast.35, bf16[128,1280]{1,0:T(8,128)(2,1)} %collective-permute-done.2.refs_2_.refs_3_, ...), custom_call_target="tpu_custom_call" | custom-call | flops 99999997952 | bytes 500000000 | tf_op jit(solution)/shard_map/block0_partial/pallas_call | solution.py:74
  43.4 3.6 %collective-permute-start.4 = (bf16[2,64,1280]{2,1,0:T(8,128)(2,1)}, bf16[2,64,1280]{2,1,0:T(8,128)(2,1)}, u32[]{:S(2)}, u32[]{:S(2)}) collective-permute-start(bf16[2,64,1280]{2,1,0:T(8,128)(2,1)} %get-tuple-element.59), channel_id=1, source_target_pairs={{0,16},{1,17},{2,18},{3,19},{4,20},{5,21},{6,22},{7,23},{8,24},{9,... | collective-permute-start | bytes 983048 | tf_op jit(solution)/shard_map/ppermute | solution.py:540
  47.0 1.1 pick.2
  48.1 1.6 collective-permute-start.6
  50.5 2.0 %stack.23 = (bf16[2,320,1280]{2,1,0:T(8,128)(2,1)S(1)}, f32[8,128]{1,0:T(8,128)}) custom-call(s32[4]{0:T(128)S(1)} %pad_add_fusion.refs_0_, bf16[320,1280]{1,0:T(8,128)(2,1)} %collective-permute-done.3.refs_1_, bf16[320,1280]{1,0:T(8,128)(2,1)} %collective-permute-done.9.refs_2_, f32[8,128]{1,0:T(8,128)S(1)} %get-tuple-element.67.refs_3_), custom_call_target="tpu_custom_call" | custom-call | flops 99999997952 | bytes 500000000 | tf_op jit(solution)/shard_map/stack/pallas_call | solution.py:74
  52.5 1.9 collective-permute-done.6.refs_3_
  54.4 2.8 %collective-permute-done.7.refs_4_ = bf16[64,1280]{1,0:T(8,128)(2,1)S(1)} collective-permute-done((bf16[64,1280]{1,0:T(8,128)(2,1)S(1)}, bf16[64,1280]{1,0:T(8,128)(2,1)S(1)}, u32[]{:S(2)}, u32[]{:S(2)}) %collective-permute-start.7) | collective-permute-done | bytes 163872 | tf_op jit(solution)/shard_map/ppermute | solution.py:21
  57.2 1.6 pick.3
  59.7 1.6 assemble.3
  61.3 6.6 %collective-permute-done.8.refs_5_ = bf16[64,1280]{1,0:T(8,128)(2,1)S(1)} collective-permute-done((bf16[64,1280]{1,0:T(8,128)(2,1)S(1)}, bf16[64,1280]{1,0:T(8,128)(2,1)S(1)}, u32[]{:S(2)}, u32[]{:S(2)}) %collective-permute-start.8) | collective-permute-done | bytes 163872 | tf_op jit(solution)/shard_map/ppermute | solution.py:21
  68.0 1.2 denoise.1
  69.1 3.8 %collective-permute-start.13 = (bf16[64,1280]{1,0:T(8,128)(2,1)S(1)}, bf16[64,1280]{1,0:T(8,128)(2,1)S(1)}, u32[]{:S(2)}, u32[]{:S(2)}) collective-permute-start(bf16[64,1280]{1,0:T(8,128)(2,1)S(1)} %get-tuple-element.70.refs_1_), channel_id=1, source_target_pairs={{0,3},{1,0},{2,1},{3,2},{4,7},{5,4},{6,5},{7,6},{8,11},{9,8},{10,9... | collective-permute-start | bytes 491528 | tf_op jit(solution)/shard_map/ppermute | solution.py:21
  73.0 4.5 %collective-permute-done.11.refs_2_ = bf16[64,1280]{1,0:T(8,128)(2,1)S(1)} collective-permute-done((bf16[64,1280]{1,0:T(8,128)(2,1)S(1)}, bf16[64,1280]{1,0:T(8,128)(2,1)S(1)}, u32[]{:S(2)}, u32[]{:S(2)}) %collective-permute-start.11) | collective-permute-done | bytes 163872 | tf_op jit(solution)/shard_map/ppermute | solution.py:21
  77.4 2.2 %stack.24 = (bf16[1,640,1280]{2,1,0:T(8,128)(2,1)S(1)}, f32[8,128]{1,0:T(8,128)}) custom-call(s32[4]{0:T(128)S(1)} %pad_add_fusion.refs_0_, bf16[640,1280]{1,0:T(8,128)(2,1)} %collective-permute-done.14.refs_1_, bf16[64,1280]{1,0:T(8,128)(2,1)S(1)} %collective-permute-done.11.refs_2_, bf16[64,1280]{1,0:T(8,128)(2,1)S(1)} %collective-permute-done.13.refs_3_.refs_4_), custom_call_target="tpu_custom_call" | custom-call | flops 99999997952 | bytes 500000000 | tf_op jit(solution)/shard_map/stack/pallas_call | solution.py:74
  81.8 2.3 %collective-permute-start.12 = (bf16[64,1280]{1,0:T(8,128)(2,1)}, bf16[64,1280]{1,0:T(8,128)(2,1)S(1)}, u32[]{:S(2)}, u32[]{:S(2)}) collective-permute-start(bf16[64,1280]{1,0:T(8,128)(2,1)} %copy-done.14), channel_id=1, source_target_pairs={{0,2},{1,3},{2,0},{3,1},{4,6},{5,7},{6,4},{7,5},{8,10},{9,11},{10,... | collective-permute-start | bytes 491528 | tf_op jit(solution)/shard_map/ppermute | solution.py:21
  84.1 2.3 %assemble.4 = (bf16[1280,1280]{1,0:T(8,128)(2,1)S(1)}, f32[8,128]{1,0:T(8,128)S(1)}) custom-call(s32[4]{0:T(128)S(1)} %pad_add_fusion.refs_0_, bf16[640,1280]{1,0:T(8,128)(2,1)} %collective-permute-done.14.refs_1_, bf16[1,640,1280]{2,1,0:T(8,128)(2,1)S(1)} %collective-permute-done.15.refs_2_), custom_call_target="tpu_custom_call" | custom-call | flops 99999997952 | bytes 500000000 | tf_op jit(solution)/shard_map/assemble/pallas_call | solution.py:74
  86.4 6.6 %collective-permute-done.12.refs_3_ = bf16[64,1280]{1,0:T(8,128)(2,1)S(1)} collective-permute-done((bf16[64,1280]{1,0:T(8,128)(2,1)}, bf16[64,1280]{1,0:T(8,128)(2,1)S(1)}, u32[]{:S(2)}, u32[]{:S(2)}) %collective-permute-start.12) | collective-permute-done | bytes 163872 | tf_op jit(solution)/shard_map/ppermute | solution.py:21
  93.1 3.8 %reward_forward.1 = (bf16[64,1280]{1,0:T(8,128)(2,1)S(1)}, bf16[64,1280]{1,0:T(8,128)(2,1)S(1)}, bf16[64,1280]{1,0:T(8,128)(2,1)S(1)}, bf16[64,1280]{1,0:T(8,128...) custom-call(s32[4]{0:T(128)S(1)} %pad_add_fusion.refs_0_, bf16[64,1280]{1,0:T(8,128)(2,1)S(1)} %copy-done.15, ...), custom_call_target="tpu_custom_call" | custom-call | flops 99999997952 | bytes 500000000 | tf_op jit(solution)/shard_map/reward_forward/pallas_call | solution.py:74
  96.8 3.2 %collective-permute-start.17 = (f32[8,1280]{1,0:T(8,128)S(1)}, f32[8,1280]{1,0:T(8,128)S(1)}, u32[]{:S(2)}, u32[]{:S(2)}) collective-permute-start(f32[8,1280]{1,0:T(8,128)S(1)} %get-tuple-element.75.refs_1_), channel_id=1, source_target_pairs={{0,2},{1,3},{2,0},{3,1},{4,6},{5,7},{6,4},{7,5},{8,10},{9,11},{10,... | collective-permute-start | bytes 122888 | tf_op jit(solution)/shard_map/ppermute | solution.py:21
  100.7 1.8 share.5
  102.5 2.5 %collective-permute-start.28 = (bf16[640,1280]{1,0:T(8,128)(2,1)}, bf16[640,1280]{1,0:T(8,128)(2,1)}, u32[]{:S(2)}, u32[]{:S(2)}) collective-permute-start(bf16[640,1280]{1,0:T(8,128)(2,1)} %get-tuple-element.91), channel_id=1, source_target_pairs={{0,16},{1,17},{2,18},{3,19},{4,20},{5,21},{6,22},{7,23},{8,24},{9,... | collective-permute-start | bytes 4915208 | tf_op jit(solution)/shard_map/ppermute | solution.py:555
  105.0 3.5 %reward_back.1 = (bf16[64,1280]{1,0:T(8,128)(2,1)S(1)}, bf16[64,1280]{1,0:T(8,128)(2,1)S(1)}, bf16[64,1280]{1,0:T(8,128)(2,1)S(1)}, bf16[64,1280]{1,0:T(8,128)(2...) custom-call(s32[4]{0:T(128)S(1)} %pad_add_fusion.refs_0_, f32[8,1280]{1,0:T(8,128)S(1)} %get-tuple-element.75.refs_1_, ...), custom_call_target="tpu_custom_call" | custom-call | flops 99999997952 | bytes 500000000 | tf_op jit(solution)/shard_map/reward_back/pallas_call | solution.py:74
  108.5 1.6 collective-permute-start.19
  110.2 1.2 collective-permute-start.20
  111.4 1.2 collective-permute-start.21
  112.6 4.4 %block0_state.1 = (bf16[512,1280]{1,0:T(8,128)(2,1)S(1)}, bf16[512,1280]{1,0:T(8,128)(2,1)S(1)}, bf16[640,512]{1,0:T(8,128)(2,1)S(1)}, f32[8,128]{1,0:T(8,128)S(1)}) custom-call(s32[4]{0:T(128)S(1)} %pad_add_fusion.refs_0_, bf16[128,1280]{1,0:T(8,128)(2,1)S(1)} %bitcast.37, bf16[128,1280]{1,0:T(8,128)(2,1)S(1)} %copy-done.11, ...), custom_call_target="tpu_custom_call" | custom-call | flops 99999997952 | bytes 500000000 | tf_op jit(solution)/shard_map/block0_state/pallas_call | solution.py:74
  117.0 7.9 %collective-permute-done.20.refs_7_ = bf16[64,1280]{1,0:T(8,128)(2,1)S(1)} collective-permute-done((bf16[64,1280]{1,0:T(8,128)(2,1)S(1)}, bf16[64,1280]{1,0:T(8,128)(2,1)S(1)}, u32[]{:S(2)}, u32[]{:S(2)}) %collective-permute-start.20) | collective-permute-done | bytes 163872 | tf_op jit(solution)/shard_map/ppermute | solution.py:21
  124.9 1.4 eps_gradient.1
  126.3 3.8 %collective-permute-start.24 = (bf16[64,1280]{1,0:T(8,128)(2,1)S(1)}, bf16[64,1280]{1,0:T(8,128)(2,1)S(1)}, u32[]{:S(2)}, u32[]{:S(2)}) collective-permute-start(bf16[64,1280]{1,0:T(8,128)(2,1)S(1)} %get-tuple-element.86.refs_1_), channel_id=1, source_target_pairs={{0,3},{1,0},{2,1},{3,2},{4,7},{5,4},{6,5},{7,6},{8,11},{9,8},{10,9... | collective-permute-start | bytes 491528 | tf_op jit(solution)/shard_map/ppermute | solution.py:21
  130.1 3.7 %collective-permute-done.22.refs_2_ = bf16[64,1280]{1,0:T(8,128)(2,1)S(1)} collective-permute-done((bf16[64,1280]{1,0:T(8,128)(2,1)S(1)}, bf16[64,1280]{1,0:T(8,128)(2,1)S(1)}, u32[]{:S(2)}, u32[]{:S(2)}) %collective-permute-start.22) | collective-permute-done | bytes 163872 | tf_op jit(solution)/shard_map/ppermute | solution.py:21
  133.7 1.6 collective-permute-done.24.refs_3_.refs_4_
  135.3 3.7 %collective-permute-done.28.refs_1_ = bf16[640,1280]{1,0:T(8,128)(2,1)} collective-permute-done((bf16[640,1280]{1,0:T(8,128)(2,1)}, bf16[640,1280]{1,0:T(8,128)(2,1)}, u32[]{:S(2)}, u32[]{:S(2)}) %collective-permute-start.28) | collective-permute-done | bytes 1638432 | tf_op jit(solution)/shard_map/ppermute | solution.py:555
  139.1 2.0 %stack.25 = (bf16[1,640,1280]{2,1,0:T(8,128)(2,1)S(1)}, f32[8,128]{1,0:T(8,128)}) custom-call(s32[4]{0:T(128)S(1)} %pad_add_fusion.refs_0_, bf16[640,1280]{1,0:T(8,128)(2,1)} %collective-permute-done.28.refs_1_, bf16[64,1280]{1,0:T(8,128)(2,1)S(1)} %collective-permute-done.22.refs_2_, bf16[64,1280]{1,0:T(8,128)(2,1)S(1)} %collective-permute-done.24.refs_3_.refs_4_), custom_call_target="tpu_custom_call" | custom-call | flops 99999997952 | bytes 500000000 | tf_op jit(solution)/shard_map/stack/pallas_call | solution.py:74
  141.1 1.7 collective-permute-start.23
  142.9 2.5 %collective-permute-start.25 = (bf16[64,1280]{1,0:T(8,128)(2,1)S(1)}, bf16[64,1280]{1,0:T(8,128)(2,1)S(1)}, u32[]{:S(2)}, u32[]{:S(2)}) collective-permute-start(bf16[64,1280]{1,0:T(8,128)(2,1)S(1)} %get-tuple-element.86.refs_1_), channel_id=1, source_target_pairs={{0,16},{16,0},{1,17},{17,1},{2,18},{18,2},{3,19},{19,3},{4,20},{20... | collective-permute-start | bytes 491528 | tf_op jit(solution)/shard_map/ppermute | solution.py:26
  145.4 6.7 %collective-permute-done.23.refs_3_ = bf16[64,1280]{1,0:T(8,128)(2,1)S(1)} collective-permute-done((bf16[64,1280]{1,0:T(8,128)(2,1)S(1)}, bf16[64,1280]{1,0:T(8,128)(2,1)S(1)}, u32[]{:S(2)}, u32[]{:S(2)}) %collective-permute-start.23) | collective-permute-done | bytes 163872 | tf_op jit(solution)/shard_map/ppermute | solution.py:21
  152.1 2.5 %collective-permute-start.27 = (bf16[64,1280]{1,0:T(8,128)(2,1)S(1)}, bf16[64,1280]{1,0:T(8,128)(2,1)S(1)}, u32[]{:S(2)}, u32[]{:S(2)}) collective-permute-start(bf16[64,1280]{1,0:T(8,128)(2,1)S(1)} %collective-permute-done.23.refs_3_), channel_id=1, source_target_pairs={{0,16},{16,0},{1,17},{17,1},{2,18},{18,2},{3,19},{19,3},{4,20},{20... | collective-permute-start | bytes 491528 | tf_op jit(solution)/shard_map/ppermute | solution.py:26
  154.6 2.0 %assemble.5 = (bf16[1280,1280]{1,0:T(8,128)(2,1)S(1)}, f32[8,128]{1,0:T(8,128)}) custom-call(s32[4]{0:T(128)S(1)} %pad_add_fusion.refs_0_, bf16[640,1280]{1,0:T(8,128)(2,1)} %collective-permute-done.28.refs_1_, bf16[1,640,1280]{2,1,0:T(8,128)(2,1)S(1)} %collective-permute-done.29.refs_2_), custom_call_target="tpu_custom_call" | custom-call | flops 99999997952 | bytes 500000000 | tf_op jit(solution)/shard_map/assemble/pallas_call | solution.py:74
  156.7 3.8 %collective-permute-done.27.refs_7_ = bf16[64,1280]{1,0:T(8,128)(2,1)S(1)} collective-permute-done((bf16[64,1280]{1,0:T(8,128)(2,1)S(1)}, bf16[64,1280]{1,0:T(8,128)(2,1)S(1)}, u32[]{:S(2)}, u32[]{:S(2)}) %collective-permute-start.27) | collective-permute-done | bytes 163872 | tf_op jit(solution)/shard_map/ppermute | solution.py:26
  160.5 5.6 %gradients.1 = (bf16[2,160,1280]{2,1,0:T(8,128)(2,1)S(1)}, bf16[2,160,1280]{2,1,0:T(8,128)(2,1)S(1)}, bf16[2,160,1280]{2,1,0:T(8,128)(2,1)S(1)}, bf16[2,160,1280]{2,1,0:T(8,128)(2,1)S(1)}, f32[8,128]{1,0:T(8,128)}) custom-call(s32[4]{0:T(128)S(1)} %pad_add_fusion.refs_0_, bf16[64,1280]{1,0:T(8,128)(2,1)S(1)} %get-tuple-element.86.refs_1_, ...), custom_call_target="tpu_custom_call" | custom-call | flops 99999997952 | bytes 500000000 | tf_op jit(solution)/shard_map/gradients/pallas_call | solution.py:74
  166.6 1.8 collective-permute-done.32.refs_2_
  168.4 1.1 chip_sum.3
  169.5 1.5 collective-permute-start.33
  171.0 1.1 chip_sum.2
  172.7 9.1 %collective-permute-done.33 = bf16[160,1280]{1,0:T(8,128)(2,1)S(1)} collective-permute-done((bf16[160,1280]{1,0:T(8,128)(2,1)S(1)}, bf16[160,1280]{1,0:T(8,128)(2,1)S(1)}, u32[]{:S(2)}, u32[]{:S(2)}) %collective-permute-start.33) | collective-permute-done | bytes 409632 | tf_op jit(solution)/shard_map/ppermute | solution.py:21
  181.8 1.0 convert_add_fusion
  182.8 7.0 %collective-permute-done.31 = bf16[160,1280]{1,0:T(8,128)(2,1)S(1)} collective-permute-done((bf16[160,1280]{1,0:T(8,128)(2,1)S(1)}, bf16[160,1280]{1,0:T(8,128)(2,1)S(1)}, u32[]{:S(2)}, u32[]{:S(2)}) %collective-permute-start.31) | collective-permute-done | bytes 409632 | tf_op jit(solution)/shard_map/ppermute | solution.py:21
  189.8 1.0 convert_add_fusion.1
  (90 shorter events, 5.2 us)
Async XLA Ops:
  0.6 81.0 %copy-start = (bf16[64,1280]{1,0:T(8,128)(2,1)S(1)}, bf16[64,1280]{1,0:T(8,128)(2,1)}, u32[]{:S(2)}) copy-start(bf16[64,1280]{1,0:T(8,128)(2,1)} %param.10) | copy-start | bytes 491524
  0.6 13.9 %collective-permute-start = (bf16[128,1280]{1,0:T(8,128)(2,1)}, bf16[128,1280]{1,0:T(8,128)(2,1)S(1)}, u32[]{:S(2)}, u32[]{:S(2)}) collective-permute-start(bf16[128,1280]{1,0:T(8,128)(2,1)} %bitcast.32), channel_id=1, source_target_pairs={{0,1},{1,2},{2,3},{3,0},{4,5},{5,6},{6,7},{7,4},{8,9},{9,10},{10,1... | collective-permute-start | bytes 983048 | tf_op jit(solution)/shard_map/ppermute | solution.py:21
  3.7 16.4 %collective-permute-start.1 = (bf16[128,1280]{1,0:T(8,128)(2,1)}, bf16[128,1280]{1,0:T(8,128)(2,1)S(1)}, u32[]{:S(2)}, u32[]{:S(2)}) collective-permute-start(bf16[128,1280]{1,0:T(8,128)(2,1)} %bitcast.33), channel_id=1, source_target_pairs={{0,3},{1,0},{2,1},{3,2},{4,7},{5,4},{6,5},{7,6},{8,11},{9,8},{10,9... | collective-permute-start | bytes 983048 | tf_op jit(solution)/shard_map/ppermute | solution.py:21
  5.9 1.9 %copy-start.3 = (bf16[1,1280,1280]{2,1,0:T(8,128)(2,1)S(1)}, bf16[1,1280,1280]{2,1,0:T(8,128)(2,1)}, u32[]{:S(2)}) copy-start(bf16[1,1280,1280]{2,1,0:T(8,128)(2,1)} %param.12) | copy-start | bytes 9830404
  7.8 3.2 %copy-start.24 = (s32[2]{0:T(128)S(1)}, s32[2]{0:T(128)}, u32[]{:S(2)}) copy-start(s32[2]{0:T(128)} %param.8) | copy-start | bytes 28
  7.8 5.3 %copy-start.23 = (f32[2,1280]{1,0:T(2,128)S(1)}, f32[2,1280]{1,0:T(2,128)}, u32[]{:S(2)}) copy-start(f32[2,1280]{1,0:T(2,128)} %param.11) | copy-start | bytes 30724
  7.8 12.3 %copy-start.8 = (bf16[2,64,1280]{2,1,0:T(8,128)(2,1)S(1)}, bf16[2,64,1280]{2,1,0:T(8,128)(2,1)}, u32[]{:S(2)}) copy-start(bf16[2,64,1280]{2,1,0:T(8,128)(2,1)} %param.7) | copy-start | bytes 983044
  9.3 20.7 %collective-permute-start.3 = (bf16[320,1280]{1,0:T(8,128)(2,1)}, bf16[320,1280]{1,0:T(8,128)(2,1)}, u32[]{:S(2)}, u32[]{:S(2)}) collective-permute-start(bf16[320,1280]{1,0:T(8,128)(2,1)} %get-tuple-element.53), channel_id=1, source_target_pairs={{0,16},{16,0},{1,17},{17,1},{2,18},{18,2},{3,19},{19,3},{4,20},{20... | collective-permute-start | bytes 2457608 | tf_op jit(solution)/shard_map/ppermute | solution.py:26
  13.2 26.2 %copy-start.1 = (f32[1,1280]{1,0:T(1,128)}, f32[1,1280]{1,0:T(1,128)S(1)}, u32[]{:S(2)}) copy-start(f32[1,1280]{1,0:T(1,128)S(1)} %get-tuple-element.103.refs_3_.refs_5_) | copy-start | bytes 15364
  13.2 9.6 %copy-start.6 = (bf16[1,1280,1280]{2,1,0:T(8,128)(2,1)S(1)}, bf16[1,1280,1280]{2,1,0:T(8,128)(2,1)}, u32[]{:S(2)}) copy-start(bf16[1,1280,1280]{2,1,0:T(8,128)(2,1)} %param.13) | copy-start | bytes 9830404
  14.5 19.3 %copy-start.10 = (bf16[128,1280]{1,0:T(8,128)(2,1)}, bf16[128,1280]{1,0:T(8,128)(2,1)S(1)}, u32[]{:S(2)}) copy-start(bf16[128,1280]{1,0:T(8,128)(2,1)S(1)} %collective-permute-done.refs_2_.refs_1_) | copy-start | bytes 983044
  20.1 13.7 %copy-start.12 = (bf16[128,1280]{1,0:T(8,128)(2,1)}, bf16[128,1280]{1,0:T(8,128)(2,1)S(1)}, u32[]{:S(2)}) copy-start(bf16[128,1280]{1,0:T(8,128)(2,1)S(1)} %collective-permute-done.1.refs_3_.refs_2_.refs_4_) | copy-start | bytes 983044
  21.4 17.9 %collective-permute-start.2 = (bf16[128,1280]{1,0:T(8,128)(2,1)}, bf16[128,1280]{1,0:T(8,128)(2,1)}, u32[]{:S(2)}, u32[]{:S(2)}) collective-permute-start(bf16[128,1280]{1,0:T(8,128)(2,1)} %get-tuple-element.52), channel_id=1, source_target_pairs={{0,2},{1,3},{2,0},{3,1},{4,6},{5,7},{6,4},{7,5},{8,10},{9,11},{10,... | collective-permute-start | bytes 983048 | tf_op jit(solution)/shard_map/ppermute | solution.py:21
  24.6 9.3 %copy-start.4 = (bf16[1,1280,1280]{2,1,0:T(8,128)(2,1)S(1)}, bf16[1,1280,1280]{2,1,0:T(8,128)(2,1)}, u32[]{:S(2)}) copy-start(bf16[1,1280,1280]{2,1,0:T(8,128)(2,1)} %param.12) | copy-start | bytes 9830404
  24.6 48.4 %collective-permute-start.14 = (bf16[640,1280]{1,0:T(8,128)(2,1)}, bf16[640,1280]{1,0:T(8,128)(2,1)}, u32[]{:S(2)}, u32[]{:S(2)}) collective-permute-start(bf16[640,1280]{1,0:T(8,128)(2,1)} %get-tuple-element.72), channel_id=1, source_target_pairs={{16,0},{17,1},{18,2},{19,3},{20,4},{21,5},{22,6},{23,7},{24,8},{25... | collective-permute-start | bytes 4915208 | tf_op jit(solution)/shard_map/ppermute | solution.py:527
  32.1 18.4 %collective-permute-start.9 = (bf16[320,1280]{1,0:T(8,128)(2,1)}, bf16[320,1280]{1,0:T(8,128)(2,1)}, u32[]{:S(2)}, u32[]{:S(2)}) collective-permute-start(bf16[320,1280]{1,0:T(8,128)(2,1)} %get-tuple-element.66), channel_id=1, source_target_pairs={{0,8},{4,12},{8,0},{12,4},{1,9},{5,13},{9,1},{13,5},{2,10},{6,14},... | collective-permute-start | bytes 2457608 | tf_op jit(solution)/shard_map/ppermute | solution.py:26
  36.8 10.2 %collective-permute-start.5 = (bf16[2,64,1280]{2,1,0:T(8,128)(2,1)S(1)}, bf16[2,64,1280]{2,1,0:T(8,128)(2,1)S(1)}, u32[]{:S(2)}, u32[]{:S(2)}) collective-permute-start(bf16[2,64,1280]{2,1,0:T(8,128)(2,1)S(1)} %get-tuple-element.61), channel_id=1, source_target_pairs={{0,16},{1,17},{2,18},{3,19},{4,20},{5,21},{6,22},{7,23},{8,24},{9,... | collective-permute-start | bytes 983048 | tf_op jit(solution)/shard_map/ppermute | solution.py:540
  43.4 9.1 %collective-permute-start.4 = (bf16[2,64,1280]{2,1,0:T(8,128)(2,1)}, bf16[2,64,1280]{2,1,0:T(8,128)(2,1)}, u32[]{:S(2)}, u32[]{:S(2)}) collective-permute-start(bf16[2,64,1280]{2,1,0:T(8,128)(2,1)} %get-tuple-element.59), channel_id=1, source_target_pairs={{0,16},{1,17},{2,18},{3,19},{4,20},{5,21},{6,22},{7,23},{8,24},{9,... | collective-permute-start | bytes 983048 | tf_op jit(solution)/shard_map/ppermute | solution.py:540
  48.1 6.3 %collective-permute-start.6 = (bf16[64,1280]{1,0:T(8,128)(2,1)S(1)}, bf16[64,1280]{1,0:T(8,128)(2,1)S(1)}, u32[]{:S(2)}, u32[]{:S(2)}) collective-permute-start(bf16[64,1280]{1,0:T(8,128)(2,1)S(1)} %get-tuple-element.62), channel_id=1, source_target_pairs={{0,3},{1,0},{2,1},{3,2},{4,7},{5,4},{6,5},{7,6},{8,11},{9,8},{10,9... | collective-permute-start | bytes 491528 | tf_op jit(solution)/shard_map/ppermute | solution.py:21
  49.7 7.5 %collective-permute-start.7 = (bf16[64,1280]{1,0:T(8,128)(2,1)S(1)}, bf16[64,1280]{1,0:T(8,128)(2,1)S(1)}, u32[]{:S(2)}, u32[]{:S(2)}) collective-permute-start(bf16[64,1280]{1,0:T(8,128)(2,1)S(1)} %get-tuple-element.63), channel_id=1, source_target_pairs={{0,1},{1,2},{2,3},{3,0},{4,5},{5,6},{6,7},{7,4},{8,9},{9,10},{10,1... | collective-permute-start | bytes 491528 | tf_op jit(solution)/shard_map/ppermute | solution.py:21
  52.5 7.1 %collective-permute-start.10 = (bf16[2,320,1280]{2,1,0:T(8,128)(2,1)S(1)}, bf16[2,320,1280]{2,1,0:T(8,128)(2,1)S(1)}, u32[]{:S(2)}, u32[]{:S(2)}) collective-permute-start(bf16[2,320,1280]{2,1,0:T(8,128)(2,1)S(1)} %get-tuple-element.68), channel_id=1, source_target_pairs={{0,4},{4,0},{8,12},{12,8},{1,5},{5,1},{9,13},{13,9},{2,6},{6,2},{1... | collective-permute-start | bytes 4915208 | tf_op jit(solution)/shard_map/ppermute | solution.py:26
  58.8 9.2 %collective-permute-start.8 = (bf16[64,1280]{1,0:T(8,128)(2,1)S(1)}, bf16[64,1280]{1,0:T(8,128)(2,1)S(1)}, u32[]{:S(2)}, u32[]{:S(2)}) collective-permute-start(bf16[64,1280]{1,0:T(8,128)(2,1)S(1)} %get-tuple-element.65), channel_id=1, source_target_pairs={{0,2},{1,3},{2,0},{3,1},{4,6},{5,7},{6,4},{7,5},{8,10},{9,11},{10,... | collective-permute-start | bytes 491528 | tf_op jit(solution)/shard_map/ppermute | solution.py:21
  61.3 7.8 %copy-start.21 = (bf16[1280,1280]{1,0:T(8,128)(2,1)}, bf16[1280,1280]{1,0:T(8,128)(2,1)S(1)}, u32[]{:S(2)}) copy-start(bf16[1280,1280]{1,0:T(8,128)(2,1)S(1)} %get-tuple-element.71.refs_9_.refs_11_.refs_7_) | copy-start | bytes 9830404
  69.1 8.3 %copy-start.14 = (bf16[64,1280]{1,0:T(8,128)(2,1)}, bf16[64,1280]{1,0:T(8,128)(2,1)S(1)}, u32[]{:S(2)}) copy-start(bf16[64,1280]{1,0:T(8,128)(2,1)S(1)} %get-tuple-element.70.refs_1_) | copy-start | bytes 491524
  69.1 10.5 %copy-start.25 = (s32[2]{0:T(128)S(1)}, s32[2]{0:T(128)}, u32[]{:S(2)}) copy-start(s32[2]{0:T(128)} %param.9) | copy-start | bytes 28
  69.1 8.3 %collective-permute-start.11 = (bf16[64,1280]{1,0:T(8,128)(2,1)S(1)}, bf16[64,1280]{1,0:T(8,128)(2,1)S(1)}, u32[]{:S(2)}, u32[]{:S(2)}) collective-permute-start(bf16[64,1280]{1,0:T(8,128)(2,1)S(1)} %get-tuple-element.70.refs_1_), channel_id=1, source_target_pairs={{0,1},{1,2},{2,3},{3,0},{4,5},{5,6},{6,7},{7,4},{8,9},{9,10},{10,1... | collective-permute-start | bytes 491528 | tf_op jit(solution)/shard_map/ppermute | solution.py:21
  69.1 8.3 %collective-permute-start.13 = (bf16[64,1280]{1,0:T(8,128)(2,1)S(1)}, bf16[64,1280]{1,0:T(8,128)(2,1)S(1)}, u32[]{:S(2)}, u32[]{:S(2)}) collective-permute-start(bf16[64,1280]{1,0:T(8,128)(2,1)S(1)} %get-tuple-element.70.refs_1_), channel_id=1, source_target_pairs={{0,3},{1,0},{2,1},{3,2},{4,7},{5,4},{6,5},{7,6},{8,11},{9,8},{10,9... | collective-permute-start | bytes 491528 | tf_op jit(solution)/shard_map/ppermute | solution.py:21
  77.4 2.2 %copy-start.17 = (bf16[64,1280]{1,0:T(8,128)(2,1)}, bf16[64,1280]{1,0:T(8,128)(2,1)S(1)}, u32[]{:S(2)}) copy-start(bf16[64,1280]{1,0:T(8,128)(2,1)S(1)} %collective-permute-done.11.refs_2_) | copy-start | bytes 491524
  77.4 2.2 %copy-start.19 = (bf16[64,1280]{1,0:T(8,128)(2,1)}, bf16[64,1280]{1,0:T(8,128)(2,1)S(1)}, u32[]{:S(2)}) copy-start(bf16[64,1280]{1,0:T(8,128)(2,1)S(1)} %collective-permute-done.13.refs_3_.refs_4_) | copy-start | bytes 491524
  79.6 4.5 %collective-permute-start.15 = (bf16[1,640,1280]{2,1,0:T(8,128)(2,1)S(1)}, bf16[1,640,1280]{2,1,0:T(8,128)(2,1)S(1)}, u32[]{:S(2)}, u32[]{:S(2)}) collective-permute-start(bf16[1,640,1280]{2,1,0:T(8,128)(2,1)S(1)} %get-tuple-element.73), channel_id=1, source_target_pairs={{0,4},{4,0},{8,12},{12,8},{1,5},{5,1},{9,13},{13,9},{2,6},{6,2},{1... | collective-permute-start | bytes 4915208 | tf_op jit(solution)/shard_map/ppermute | solution.py:26
  81.7 11.3 %copy-start.5 = (bf16[1,1280,1280]{2,1,0:T(8,128)(2,1)S(1)}, bf16[1,1280,1280]{2,1,0:T(8,128)(2,1)}, u32[]{:S(2)}) copy-start(bf16[1,1280,1280]{2,1,0:T(8,128)(2,1)} %param.12) | copy-start | bytes 9830404
  81.7 11.3 %copy-start.7 = (bf16[1,1280,1280]{2,1,0:T(8,128)(2,1)S(1)}, bf16[1,1280,1280]{2,1,0:T(8,128)(2,1)}, u32[]{:S(2)}) copy-start(bf16[1,1280,1280]{2,1,0:T(8,128)(2,1)} %param.13) | copy-start | bytes 9830404
  81.7 11.3 %copy-start.15 = (bf16[64,1280]{1,0:T(8,128)(2,1)S(1)}, bf16[64,1280]{1,0:T(8,128)(2,1)}, u32[]{:S(2)}) copy-start(bf16[64,1280]{1,0:T(8,128)(2,1)} %copy-done.14) | copy-start | bytes 491524
  81.8 11.3 %copy-start.18 = (bf16[64,1280]{1,0:T(8,128)(2,1)S(1)}, bf16[64,1280]{1,0:T(8,128)(2,1)}, u32[]{:S(2)}) copy-start(bf16[64,1280]{1,0:T(8,128)(2,1)} %copy-done.17) | copy-start | bytes 491524
  81.8 11.3 %copy-start.20 = (bf16[64,1280]{1,0:T(8,128)(2,1)S(1)}, bf16[64,1280]{1,0:T(8,128)(2,1)}, u32[]{:S(2)}) copy-start(bf16[64,1280]{1,0:T(8,128)(2,1)} %copy-done.19) | copy-start | bytes 491524
  81.8 11.3 %copy-start.22 = (bf16[1280,1280]{1,0:T(8,128)(2,1)S(1)}, bf16[1280,1280]{1,0:T(8,128)(2,1)}, u32[]{:S(2)}) copy-start(bf16[1280,1280]{1,0:T(8,128)(2,1)} %copy-done.21) | copy-start | bytes 9830404
  81.8 11.2 %collective-permute-start.12 = (bf16[64,1280]{1,0:T(8,128)(2,1)}, bf16[64,1280]{1,0:T(8,128)(2,1)S(1)}, u32[]{:S(2)}, u32[]{:S(2)}) collective-permute-start(bf16[64,1280]{1,0:T(8,128)(2,1)} %copy-done.14), channel_id=1, source_target_pairs={{0,2},{1,3},{2,0},{3,1},{4,6},{5,7},{6,4},{7,5},{8,10},{9,11},{10,... | collective-permute-start | bytes 491528 | tf_op jit(solution)/shard_map/ppermute | solution.py:21
  96.8 8.1 %collective-permute-start.16 = (f32[8,1280]{1,0:T(8,128)S(1)}, f32[8,1280]{1,0:T(8,128)S(1)}, u32[]{:S(2)}, u32[]{:S(2)}) collective-permute-start(f32[8,1280]{1,0:T(8,128)S(1)} %get-tuple-element.75.refs_1_), channel_id=1, source_target_pairs={{0,1},{1,2},{2,3},{3,0},{4,5},{5,6},{6,7},{7,4},{8,9},{9,10},{10,1... | collective-permute-start | bytes 122888 | tf_op jit(solution)/shard_map/ppermute | solution.py:21
  96.8 8.1 %collective-permute-start.17 = (f32[8,1280]{1,0:T(8,128)S(1)}, f32[8,1280]{1,0:T(8,128)S(1)}, u32[]{:S(2)}, u32[]{:S(2)}) collective-permute-start(f32[8,1280]{1,0:T(8,128)S(1)} %get-tuple-element.75.refs_1_), channel_id=1, source_target_pairs={{0,2},{1,3},{2,0},{3,1},{4,6},{5,7},{6,4},{7,5},{8,10},{9,11},{10,... | collective-permute-start | bytes 122888 | tf_op jit(solution)/shard_map/ppermute | solution.py:21
  100.0 4.9 %collective-permute-start.18 = (f32[8,1280]{1,0:T(8,128)S(1)}, f32[8,1280]{1,0:T(8,128)S(1)}, u32[]{:S(2)}, u32[]{:S(2)}) collective-permute-start(f32[8,1280]{1,0:T(8,128)S(1)} %get-tuple-element.75.refs_1_), channel_id=1, source_target_pairs={{0,3},{1,0},{2,1},{3,2},{4,7},{5,4},{6,5},{7,6},{8,11},{9,8},{10,9... | collective-permute-start | bytes 122888 | tf_op jit(solution)/shard_map/ppermute | solution.py:21
  102.5 36.6 %collective-permute-start.28 = (bf16[640,1280]{1,0:T(8,128)(2,1)}, bf16[640,1280]{1,0:T(8,128)(2,1)}, u32[]{:S(2)}, u32[]{:S(2)}) collective-permute-start(bf16[640,1280]{1,0:T(8,128)(2,1)} %get-tuple-element.91), channel_id=1, source_target_pairs={{0,16},{1,17},{2,18},{3,19},{4,20},{5,21},{6,22},{7,23},{8,24},{9,... | collective-permute-start | bytes 4915208 | tf_op jit(solution)/shard_map/ppermute | solution.py:555
  104.9 7.6 %copy-start.2 = (f32[1,1280]{1,0:T(1,128)S(1)}, f32[1,1280]{1,0:T(1,128)}, u32[]{:S(2)}) copy-start(f32[1,1280]{1,0:T(1,128)} %copy-done.1) | copy-start | bytes 15364
  105.0 7.6 %copy-start.9 = (bf16[2,64,1280]{2,1,0:T(8,128)(2,1)S(1)}, bf16[2,64,1280]{2,1,0:T(8,128)(2,1)}, u32[]{:S(2)}) copy-start(bf16[2,64,1280]{2,1,0:T(8,128)(2,1)} %param.7) | copy-start | bytes 983044
  105.0 7.6 %copy-start.11 = (bf16[128,1280]{1,0:T(8,128)(2,1)S(1)}, bf16[128,1280]{1,0:T(8,128)(2,1)}, u32[]{:S(2)}) copy-start(bf16[128,1280]{1,0:T(8,128)(2,1)} %copy-done.10) | copy-start | bytes 983044
  105.0 7.6 %copy-start.13 = (bf16[128,1280]{1,0:T(8,128)(2,1)S(1)}, bf16[128,1280]{1,0:T(8,128)(2,1)}, u32[]{:S(2)}) copy-start(bf16[128,1280]{1,0:T(8,128)(2,1)} %copy-done.12) | copy-start | bytes 983044
  108.5 8.4 %collective-permute-start.19 = (bf16[64,1280]{1,0:T(8,128)(2,1)S(1)}, bf16[64,1280]{1,0:T(8,128)(2,1)S(1)}, u32[]{:S(2)}, u32[]{:S(2)}) collective-permute-start(bf16[64,1280]{1,0:T(8,128)(2,1)S(1)} %get-tuple-element.82), channel_id=1, source_target_pairs={{0,3},{1,0},{2,1},{3,2},{4,7},{5,4},{6,5},{7,6},{8,11},{9,8},{10,9... | collective-permute-start | bytes 491528 | tf_op jit(solution)/shard_map/ppermute | solution.py:21
  110.2 14.7 %collective-permute-start.20 = (bf16[64,1280]{1,0:T(8,128)(2,1)S(1)}, bf16[64,1280]{1,0:T(8,128)(2,1)S(1)}, u32[]{:S(2)}, u32[]{:S(2)}) collective-permute-start(bf16[64,1280]{1,0:T(8,128)(2,1)S(1)} %get-tuple-element.83), channel_id=1, source_target_pairs={{0,2},{1,3},{2,0},{3,1},{4,6},{5,7},{6,4},{7,5},{8,10},{9,11},{10,... | collective-permute-start | bytes 491528 | tf_op jit(solution)/shard_map/ppermute | solution.py:21
  111.4 13.5 %collective-permute-start.21 = (bf16[64,1280]{1,0:T(8,128)(2,1)S(1)}, bf16[64,1280]{1,0:T(8,128)(2,1)S(1)}, u32[]{:S(2)}, u32[]{:S(2)}) collective-permute-start(bf16[64,1280]{1,0:T(8,128)(2,1)S(1)} %get-tuple-element.84), channel_id=1, source_target_pairs={{0,1},{1,2},{2,3},{3,0},{4,5},{5,6},{6,7},{7,4},{8,9},{9,10},{10,1... | collective-permute-start | bytes 491528 | tf_op jit(solution)/shard_map/ppermute | solution.py:21
  112.6 12.3 %copy-start.16 = (bf16[64,1280]{1,0:T(8,128)(2,1)S(1)}, bf16[64,1280]{1,0:T(8,128)(2,1)}, u32[]{:S(2)}) copy-start(bf16[64,1280]{1,0:T(8,128)(2,1)} %copy-done.14) | copy-start | bytes 491524
  126.3 7.5 %collective-permute-start.22 = (bf16[64,1280]{1,0:T(8,128)(2,1)S(1)}, bf16[64,1280]{1,0:T(8,128)(2,1)S(1)}, u32[]{:S(2)}, u32[]{:S(2)}) collective-permute-start(bf16[64,1280]{1,0:T(8,128)(2,1)S(1)} %get-tuple-element.86.refs_1_), channel_id=1, source_target_pairs={{0,1},{1,2},{2,3},{3,0},{4,5},{5,6},{6,7},{7,4},{8,9},{9,10},{10,1... | collective-permute-start | bytes 491528 | tf_op jit(solution)/shard_map/ppermute | solution.py:21
  126.3 9.1 %collective-permute-start.24 = (bf16[64,1280]{1,0:T(8,128)(2,1)S(1)}, bf16[64,1280]{1,0:T(8,128)(2,1)S(1)}, u32[]{:S(2)}, u32[]{:S(2)}) collective-permute-start(bf16[64,1280]{1,0:T(8,128)(2,1)S(1)} %get-tuple-element.86.refs_1_), channel_id=1, source_target_pairs={{0,3},{1,0},{2,1},{3,2},{4,7},{5,4},{6,5},{7,6},{8,11},{9,8},{10,9... | collective-permute-start | bytes 491528 | tf_op jit(solution)/shard_map/ppermute | solution.py:21
  141.1 13.5 %collective-permute-start.29 = (bf16[1,640,1280]{2,1,0:T(8,128)(2,1)S(1)}, bf16[1,640,1280]{2,1,0:T(8,128)(2,1)S(1)}, u32[]{:S(2)}, u32[]{:S(2)}) collective-permute-start(bf16[1,640,1280]{2,1,0:T(8,128)(2,1)S(1)} %get-tuple-element.92), channel_id=1, source_target_pairs={{0,4},{4,0},{8,12},{12,8},{1,5},{5,1},{9,13},{13,9},{2,6},{6,2},{1... | collective-permute-start | bytes 4915208 | tf_op jit(solution)/shard_map/ppermute | solution.py:26
  141.1 11.0 %collective-permute-start.23 = (bf16[64,1280]{1,0:T(8,128)(2,1)S(1)}, bf16[64,1280]{1,0:T(8,128)(2,1)S(1)}, u32[]{:S(2)}, u32[]{:S(2)}) collective-permute-start(bf16[64,1280]{1,0:T(8,128)(2,1)S(1)} %get-tuple-element.86.refs_1_), channel_id=1, source_target_pairs={{0,2},{1,3},{2,0},{3,1},{4,6},{5,7},{6,4},{7,5},{8,10},{9,11},{10,... | collective-permute-start | bytes 491528 | tf_op jit(solution)/shard_map/ppermute | solution.py:21
  142.9 13.8 %collective-permute-start.25 = (bf16[64,1280]{1,0:T(8,128)(2,1)S(1)}, bf16[64,1280]{1,0:T(8,128)(2,1)S(1)}, u32[]{:S(2)}, u32[]{:S(2)}) collective-permute-start(bf16[64,1280]{1,0:T(8,128)(2,1)S(1)} %get-tuple-element.86.refs_1_), channel_id=1, source_target_pairs={{0,16},{16,0},{1,17},{17,1},{2,18},{18,2},{3,19},{19,3},{4,20},{20... | collective-permute-start | bytes 491528 | tf_op jit(solution)/shard_map/ppermute | solution.py:26
  145.4 15.1 %collective-permute-start.26 = (bf16[128,1280]{1,0:T(8,128)(2,1)S(1)}, bf16[128,1280]{1,0:T(8,128)(2,1)S(1)}, u32[]{:S(2)}, u32[]{:S(2)}) collective-permute-start(bf16[128,1280]{1,0:T(8,128)(2,1)S(1)} %pad_maximum_fusion), channel_id=1, source_target_pairs={{0,16},{16,0},{1,17},{17,1},{2,18},{18,2},{3,19},{19,3},{4,20},{20... | collective-permute-start | bytes 983048 | tf_op jit(solution)/shard_map/ppermute | solution.py:26
  152.1 8.3 %collective-permute-start.27 = (bf16[64,1280]{1,0:T(8,128)(2,1)S(1)}, bf16[64,1280]{1,0:T(8,128)(2,1)S(1)}, u32[]{:S(2)}, u32[]{:S(2)}) collective-permute-start(bf16[64,1280]{1,0:T(8,128)(2,1)S(1)} %collective-permute-done.23.refs_3_), channel_id=1, source_target_pairs={{0,16},{16,0},{1,17},{17,1},{2,18},{18,2},{3,19},{19,3},{4,20},{20... | collective-permute-start | bytes 491528 | tf_op jit(solution)/shard_map/ppermute | solution.py:26
  166.1 2.3 %collective-permute-start.32 = (bf16[2,160,1280]{2,1,0:T(8,128)(2,1)S(1)}, bf16[2,160,1280]{2,1,0:T(8,128)(2,1)S(1)}, u32[]{:S(2)}, u32[]{:S(2)}) collective-permute-start(bf16[2,160,1280]{2,1,0:T(8,128)(2,1)S(1)} %get-tuple-element.99), channel_id=1, source_target_pairs={{0,4},{4,0},{8,12},{12,8},{1,5},{5,1},{9,13},{13,9},{2,6},{6,2},{1... | collective-permute-start | bytes 2457608 | tf_op jit(solution)/shard_map/ppermute | solution.py:26
  166.1 5.0 %collective-permute-start.30 = (bf16[2,160,1280]{2,1,0:T(8,128)(2,1)S(1)}, bf16[2,160,1280]{2,1,0:T(8,128)(2,1)S(1)}, u32[]{:S(2)}, u32[]{:S(2)}) collective-permute-start(bf16[2,160,1280]{2,1,0:T(8,128)(2,1)S(1)} %get-tuple-element.95), channel_id=1, source_target_pairs={{0,4},{4,0},{8,12},{12,8},{1,5},{5,1},{9,13},{13,9},{2,6},{6,2},{1... | collective-permute-start | bytes 2457608 | tf_op jit(solution)/shard_map/ppermute | solution.py:26
  169.5 12.3 %collective-permute-start.33 = (bf16[160,1280]{1,0:T(8,128)(2,1)S(1)}, bf16[160,1280]{1,0:T(8,128)(2,1)S(1)}, u32[]{:S(2)}, u32[]{:S(2)}) collective-permute-start(bf16[160,1280]{1,0:T(8,128)(2,1)S(1)} %bitcast.30), channel_id=1, source_target_pairs={{0,8},{4,12},{8,0},{12,4},{1,9},{5,13},{9,1},{13,5},{2,10},{6,14},... | collective-permute-start | bytes 1228808 | tf_op jit(solution)/shard_map/ppermute | solution.py:21
  172.2 17.7 %collective-permute-start.31 = (bf16[160,1280]{1,0:T(8,128)(2,1)S(1)}, bf16[160,1280]{1,0:T(8,128)(2,1)S(1)}, u32[]{:S(2)}, u32[]{:S(2)}) collective-permute-start(bf16[160,1280]{1,0:T(8,128)(2,1)S(1)} %bitcast.31), channel_id=1, source_target_pairs={{0,8},{4,12},{8,0},{12,4},{1,9},{5,13},{9,1},{13,5},{2,10},{6,14},... | collective-permute-start | bytes 1228808 | tf_op jit(solution)/shard_map/ppermute | solution.py:21

commit v12 on v11

--- a/solution.py
+++ b/solution.py
@@ -124,6 +124,17 @@
     return run(relay_body, "relay", sel, [value], [bf16(*value.shape)], [], after)
 
 
+def join_body(sel_ref, *refs):
+    rows = refs[0].shape[0]
+    for i, piece in enumerate(refs[:-1]):
+        refs[-1][i * rows : (i + 1) * rows, :] = piece[...]
+
+
+def joined_rows(pieces, sel):
+    out = bf16(sum(piece.shape[0] for piece in pieces), pieces[0].shape[1])
+    return run(join_body, "join", sel, pieces, [out], [], (), 1)
+
+
 def stack_body(sel_ref, *refs):
     for i, piece in enumerate(refs[:-1]):
         refs[-1][i] = piece[...]
@@ -138,15 +149,15 @@
             out[pl.ds(pl.multiple_of(place * rows, rows), rows), :] = value
 
 
-def assembled(pieces, sel, after):
+def assembled(pieces, sel, after, cost=COST):
     rows, hidden = pieces[0].shape
     count = len(pieces)
     out = bf16(count, rows, hidden)
-    stacked = run(stack_body, "stack", sel, pieces, [out], [], after)[0]
+    stacked = run(stack_body, "stack", sel, pieces, [out], [], after, cost)[0]
     beside = swapped(stacked, "dp", 1)
     body = functools.partial(assemble_body, count)
     out = bf16(2 * count * rows, hidden)
-    return run(body, "assemble", sel, [*pieces, beside], [out], [])
+    return run(body, "assemble", sel, [*pieces, beside], [out], [], (), cost)
 
 
 def partial_body(count, sel_ref, *refs):
@@ -571,11 +582,14 @@
 
 
     g_mine = gather_parts(g_eps)
-    pieces = list(g_mine)
-    for ks in ([0], near, rest[1:]):
+    pieces = g_mine + [swapped(g_eps, "sec", 1)]
+    arrived = [pieces[-1]]
+    for ks in (near, rest[1:]):
         if ks:
-            pieces.append(swapped(jnp.concatenate([g_mine[k] for k in ks], 0), "sec", 1))
-    late_out = assembled([got_late], sel, [g_mine[k] for k in near])[0]
+            joined, token = joined_rows([g_mine[k] for k in ks], sel)
+            pieces.append(swapped(joined, "sec", 1))
+            arrived += [pieces[-1]] if ks is near else [token]
+    late_out = assembled([got_late], sel, arrived, 1)[0]
     out_parts, in_parts = gradients(pieces, states, own[1], late_out, sel)
     grad_out, grad_in = sum_over_dp(*out_parts, sel), sum_over_dp(*in_parts, sel)
     return (grad_in, grad_out)

time: 191 us -> 191 us (level)
  waiting for transfers between devices: 79 us -> 75 us
  Pallas kernels: 52.5 us -> 55 us
    ppermute x1, waiting for transfers between devices: 3.74 us -> 0.01 us  [on_device(): got_late = lax.ppermute(late_share, 'sec', [(0, 1)])]
    pallas_call x23 -> x25, Pallas kernels: 52.5 us -> 55 us  [run(): pl.pallas_call(with_token, in_specs=[IN_SMEM] + [IN_VMEM] * (len(operands...]
    ppermute x20, waiting for transfers between devices: 65.3 us -> 62.9 us  [rotated(): lax.ppermute(value, axis, [(i, (i + steps) % count) for i in range(count)])]
    ppermute x10, waiting for transfers between devices: 9.95 us -> 12 us  [swapped(): return lax.ppermute(value, axis, [(i, i ^ bit) for i in range(count)])]
  transfers between devices with their start and end apart: 34 -> 34, of which waited for: 18 -> 19; matrix products, arithmetic and copies ran while one was open for 1% -> 1% of each run, Pallas kernels for 20% -> 22%
where the time goes in v12:
time: 191 us; the launch traced here: 190 us
  waiting for transfers between devices  75 us (39%)
  Pallas kernels  55 us (29%)
  starting transfers between devices  49.1 us (26%)
  local copies, waits for them, and re-layouts  5 us (3%)
  between operations  3.72 us (2%)
  other arithmetic  1.99 us (1%)
    ppermute x20, waiting for transfers between devices, rotated(): lax.ppermute(value, axis, [(i, (i + steps) % count) for i in range(count)])  62.9 us
    pallas_call x25, Pallas kernels, run(): pl.pallas_call(with_token, in_specs=[IN_SMEM] + [IN_VMEM] * (len(operands...  55 us
    ppermute x20, starting transfers between devices, rotated(): lax.ppermute(value, axis, [(i, (i + steps) % count) for i in range(count)])  31.1 us
    ppermute x10, waiting for transfers between devices, swapped(): return lax.ppermute(value, axis, [(i, i ^ bit) for i in range(count)])  12 us
    ppermute x10, starting transfers between devices, swapped(): return lax.ppermute(value, axis, [(i, i ^ bit) for i in range(count)])  7.93 us
    ppermute x2, starting transfers between devices, on_device(): crossed = lax.ppermute(leave, 'sec', [(0, 1)])  6.12 us
  transfers between devices with their start and end apart: 34, of which 19 were waited for; matrix products, arithmetic and copies ran while one was open for 1% of the time, Pallas kernels for 22%

profile of v12, /device:TPU:0, one launch (start us, length us, event | category | flops | bytes accessed | tf_op | source)
XLA Modules:
  0.0 190.0 jit_solution(1317574461520405521)
XLA Ops:
  0.6 3.1 %collective-permute-start = (bf16[128,1280]{1,0:T(8,128)(2,1)}, bf16[128,1280]{1,0:T(8,128)(2,1)S(1)}, u32[]{:S(2)}, u32[]{:S(2)}) collective-permute-start(bf16[128,1280]{1,0:T(8,128)(2,1)} %bitcast.32), channel_id=1, source_target_pairs={{0,1},{1,2},{2,3},{3,0},{4,5},{5,6},{6,7},{7,4},{8,9},{9,10},{10,1... | collective-permute-start | bytes 983048 | tf_op jit(solution)/shard_map/ppermute | solution.py:21
  3.7 2.1 %collective-permute-start.1 = (bf16[128,1280]{1,0:T(8,128)(2,1)}, bf16[128,1280]{1,0:T(8,128)(2,1)S(1)}, u32[]{:S(2)}, u32[]{:S(2)}) collective-permute-start(bf16[128,1280]{1,0:T(8,128)(2,1)} %bitcast.33), channel_id=1, source_target_pairs={{0,3},{1,0},{2,1},{3,2},{4,7},{5,4},{6,5},{7,6},{8,11},{9,8},{10,9... | collective-permute-start | bytes 983048 | tf_op jit(solution)/shard_map/ppermute | solution.py:21
  5.9 1.9 %copy-done.3 = bf16[1,1280,1280]{2,1,0:T(8,128)(2,1)S(1)} copy-done((bf16[1,1280,1280]{2,1,0:T(8,128)(2,1)S(1)}, bf16[1,1280,1280]{2,1,0:T(8,128)(2,1)}, u32[]{:S(2)}) %copy-start.3) | copy-done | bytes 3276824
  7.8 1.5 share.3
  9.3 1.7 collective-permute-start.3
  13.2 1.4 collective-permute-done.refs_2_.refs_1_
  14.5 5.6 %collective-permute-done.1.refs_3_.refs_2_.refs_4_ = bf16[128,1280]{1,0:T(8,128)(2,1)S(1)} collective-permute-done((bf16[128,1280]{1,0:T(8,128)(2,1)}, bf16[128,1280]{1,0:T(8,128)(2,1)S(1)}, u32[]{:S(2)}, u32[]{:S(2)}) %collective-permute-start.1) | collective-permute-done | bytes 327712 | tf_op jit(solution)/shard_map/ppermute | solution.py:21
  20.1 1.3 relay.2
  21.4 1.3 collective-permute-start.2
  22.7 1.8 share.4
  24.5 1.5 collective-permute-start.14
  26.1 3.9 %collective-permute-done.3.refs_1_ = bf16[320,1280]{1,0:T(8,128)(2,1)} collective-permute-done((bf16[320,1280]{1,0:T(8,128)(2,1)}, bf16[320,1280]{1,0:T(8,128)(2,1)}, u32[]{:S(2)}, u32[]{:S(2)}) %collective-permute-start.3) | collective-permute-done | bytes 819232 | tf_op jit(solution)/shard_map/ppermute | solution.py:26
  30.0 2.1 %relay.3 = (bf16[320,1280]{1,0:T(8,128)(2,1)}, f32[8,128]{1,0:T(8,128)S(1)}) custom-call(s32[4]{0:T(128)S(1)} %pad_add_fusion.refs_0_, bf16[320,1280]{1,0:T(8,128)(2,1)} %collective-permute-done.3.refs_1_, f32[8,128]{1,0:T(8,128)S(1)} %get-tuple-element.57.refs_2_), custom_call_target="tpu_custom_call" | custom-call | flops 99999997952 | bytes 500000000 | tf_op jit(solution)/shard_map/relay/pallas_call | solution.py:74
  32.1 1.7 collective-permute-start.9
  33.9 2.9 %block0_partial.2 = (bf16[2,64,1280]{2,1,0:T(8,128)(2,1)S(1)}, bf16[2,64,1280]{2,1,0:T(8,128)(2,1)S(1)}, f32[8,128]{1,0:T(8,128)S(1)}) custom-call(s32[4]{0:T(128)S(1)} %pad_add_fusion.refs_0_, bf16[128,1280]{1,0:T(8,128)(2,1)S(1)} %collective-permute-done.refs_2_.refs_1_, bf16[128,1280]{1,0:T(8,128)(2,1)S(1)} %collective-permute-done.1.refs_3_.refs_2_.refs_4_, ...), custom_call_target="tpu_custom_call" | custom-call | flops 99999997952 | bytes 500000000 | tf_op jit(solution)/shard_map/block0_partial/pallas_call | solution.py:74
  36.8 2.5 %collective-permute-start.5 = (bf16[2,64,1280]{2,1,0:T(8,128)(2,1)S(1)}, bf16[2,64,1280]{2,1,0:T(8,128)(2,1)S(1)}, u32[]{:S(2)}, u32[]{:S(2)}) collective-permute-start(bf16[2,64,1280]{2,1,0:T(8,128)(2,1)S(1)} %get-tuple-element.64), channel_id=1, source_target_pairs={{0,16},{1,17},{2,18},{3,19},{4,20},{5,21},{6,22},{7,23},{8,24},{9,... | collective-permute-start | bytes 983048 | tf_op jit(solution)/shard_map/ppermute | solution.py:551
  39.3 4.1 %block0_partial.3 = (bf16[2,64,1280]{2,1,0:T(8,128)(2,1)S(1)}, bf16[2,64,1280]{2,1,0:T(8,128)(2,1)}, f32[8,128]{1,0:T(8,128)S(1)}) custom-call(s32[4]{0:T(128)S(1)} %pad_add_fusion.refs_0_, bf16[128,1280]{1,0:T(8,128)(2,1)S(1)} %bitcast.35, bf16[128,1280]{1,0:T(8,128)(2,1)} %collective-permute-done.2.refs_2_.refs_3_, ...), custom_call_target="tpu_custom_call" | custom-call | flops 99999997952 | bytes 500000000 | tf_op jit(solution)/shard_map/block0_partial/pallas_call | solution.py:74
  43.4 3.6 %collective-permute-start.4 = (bf16[2,64,1280]{2,1,0:T(8,128)(2,1)}, bf16[2,64,1280]{2,1,0:T(8,128)(2,1)}, u32[]{:S(2)}, u32[]{:S(2)}) collective-permute-start(bf16[2,64,1280]{2,1,0:T(8,128)(2,1)} %get-tuple-element.62), channel_id=1, source_target_pairs={{0,16},{1,17},{2,18},{3,19},{4,20},{5,21},{6,22},{7,23},{8,24},{9,... | collective-permute-start | bytes 983048 | tf_op jit(solution)/shard_map/ppermute | solution.py:551
  47.0 1.1 pick.2
  48.1 1.6 collective-permute-start.6
  50.5 2.0 %stack.23 = (bf16[2,320,1280]{2,1,0:T(8,128)(2,1)S(1)}, f32[8,128]{1,0:T(8,128)}) custom-call(s32[4]{0:T(128)S(1)} %pad_add_fusion.refs_0_, bf16[320,1280]{1,0:T(8,128)(2,1)} %collective-permute-done.3.refs_1_, bf16[320,1280]{1,0:T(8,128)(2,1)} %collective-permute-done.9.refs_2_, f32[8,128]{1,0:T(8,128)S(1)} %get-tuple-element.70.refs_3_), custom_call_target="tpu_custom_call" | custom-call | flops 99999997952 | bytes 500000000 | tf_op jit(solution)/shard_map/stack/pallas_call | solution.py:74
  52.5 1.8 collective-permute-done.6.refs_3_
  54.4 2.8 %collective-permute-done.7.refs_4_ = bf16[64,1280]{1,0:T(8,128)(2,1)S(1)} collective-permute-done((bf16[64,1280]{1,0:T(8,128)(2,1)S(1)}, bf16[64,1280]{1,0:T(8,128)(2,1)S(1)}, u32[]{:S(2)}, u32[]{:S(2)}) %collective-permute-start.7) | collective-permute-done | bytes 163872 | tf_op jit(solution)/shard_map/ppermute | solution.py:21
  57.2 1.6 pick.3
  59.7 1.6 assemble.3
  61.3 1.7 copy-done.18
  63.0 5.0 %collective-permute-done.8.refs_5_ = bf16[64,1280]{1,0:T(8,128)(2,1)S(1)} collective-permute-done((bf16[64,1280]{1,0:T(8,128)(2,1)S(1)}, bf16[64,1280]{1,0:T(8,128)(2,1)S(1)}, u32[]{:S(2)}, u32[]{:S(2)}) %collective-permute-start.8) | collective-permute-done | bytes 163872 | tf_op jit(solution)/shard_map/ppermute | solution.py:21
  68.0 1.3 denoise.1
  69.3 3.8 %collective-permute-start.13 = (bf16[64,1280]{1,0:T(8,128)(2,1)}, bf16[64,1280]{1,0:T(8,128)(2,1)S(1)}, u32[]{:S(2)}, u32[]{:S(2)}) collective-permute-start(bf16[64,1280]{1,0:T(8,128)(2,1)} %get-tuple-element.73.refs_1_), channel_id=1, source_target_pairs={{0,3},{1,0},{2,1},{3,2},{4,7},{5,4},{6,5},{7,6},{8,11},{9,8},{10,9... | collective-permute-start | bytes 491528 | tf_op jit(solution)/shard_map/ppermute | solution.py:21
  73.1 4.7 %collective-permute-done.11.refs_2_ = bf16[64,1280]{1,0:T(8,128)(2,1)S(1)} collective-permute-done((bf16[64,1280]{1,0:T(8,128)(2,1)}, bf16[64,1280]{1,0:T(8,128)(2,1)S(1)}, u32[]{:S(2)}, u32[]{:S(2)}) %collective-permute-start.11) | collective-permute-done | bytes 163872 | tf_op jit(solution)/shard_map/ppermute | solution.py:21
  77.8 2.2 %stack.24 = (bf16[1,640,1280]{2,1,0:T(8,128)(2,1)S(1)}, f32[8,128]{1,0:T(8,128)}) custom-call(s32[4]{0:T(128)S(1)} %pad_add_fusion.refs_0_, bf16[640,1280]{1,0:T(8,128)(2,1)} %collective-permute-done.14.refs_1_, bf16[64,1280]{1,0:T(8,128)(2,1)S(1)} %collective-permute-done.11.refs_2_, bf16[64,1280]{1,0:T(8,128)(2,1)S(1)} %collective-permute-done.13.refs_3_.refs_4_), custom_call_target="tpu_custom_call" | custom-call | flops 99999997952 | bytes 500000000 | tf_op jit(solution)/shard_map/stack/pallas_call | solution.py:74
  82.1 2.3 %collective-permute-start.12 = (bf16[64,1280]{1,0:T(8,128)(2,1)}, bf16[64,1280]{1,0:T(8,128)(2,1)S(1)}, u32[]{:S(2)}, u32[]{:S(2)}) collective-permute-start(bf16[64,1280]{1,0:T(8,128)(2,1)} %get-tuple-element.73.refs_1_), channel_id=1, source_target_pairs={{0,2},{1,3},{2,0},{3,1},{4,6},{5,7},{6,4},{7,5},{8,10},{9,11},{10,... | collective-permute-start | bytes 491528 | tf_op jit(solution)/shard_map/ppermute | solution.py:21
  84.4 2.3 %assemble.4 = (bf16[1280,1280]{1,0:T(8,128)(2,1)S(1)}, f32[8,128]{1,0:T(8,128)S(1)}) custom-call(s32[4]{0:T(128)S(1)} %pad_add_fusion.refs_0_, bf16[640,1280]{1,0:T(8,128)(2,1)} %collective-permute-done.14.refs_1_, bf16[1,640,1280]{2,1,0:T(8,128)(2,1)S(1)} %collective-permute-done.15.refs_2_), custom_call_target="tpu_custom_call" | custom-call | flops 99999997952 | bytes 500000000 | tf_op jit(solution)/shard_map/assemble/pallas_call | solution.py:74
  86.7 6.6 %collective-permute-done.12.refs_3_ = bf16[64,1280]{1,0:T(8,128)(2,1)S(1)} collective-permute-done((bf16[64,1280]{1,0:T(8,128)(2,1)}, bf16[64,1280]{1,0:T(8,128)(2,1)S(1)}, u32[]{:S(2)}, u32[]{:S(2)}) %collective-permute-start.12) | collective-permute-done | bytes 163872 | tf_op jit(solution)/shard_map/ppermute | solution.py:21
  93.4 4.2 %reward_forward.1 = (bf16[64,1280]{1,0:T(8,128)(2,1)S(1)}, bf16[64,1280]{1,0:T(8,128)(2,1)S(1)}, bf16[64,1280]{1,0:T(8,128)(2,1)S(1)}, bf16[64,1280]{1,0:T(8,128...) custom-call(s32[4]{0:T(128)S(1)} %pad_add_fusion.refs_0_, bf16[64,1280]{1,0:T(8,128)(2,1)} %get-tuple-element.73.refs_1_, ...), custom_call_target="tpu_custom_call" | custom-call | flops 99999997952 | bytes 500000000 | tf_op jit(solution)/shard_map/reward_forward/pallas_call | solution.py:74
  97.6 3.2 %collective-permute-start.17 = (f32[8,1280]{1,0:T(8,128)S(1)}, f32[8,1280]{1,0:T(8,128)S(1)}, u32[]{:S(2)}, u32[]{:S(2)}) collective-permute-start(f32[8,1280]{1,0:T(8,128)S(1)} %get-tuple-element.78.refs_1_), channel_id=1, source_target_pairs={{0,2},{1,3},{2,0},{3,1},{4,6},{5,7},{6,4},{7,5},{8,10},{9,11},{10,... | collective-permute-start | bytes 122888 | tf_op jit(solution)/shard_map/ppermute | solution.py:21
  101.4 1.8 share.5
  103.2 2.5 %collective-permute-start.28 = (bf16[640,1280]{1,0:T(8,128)(2,1)}, bf16[640,1280]{1,0:T(8,128)(2,1)}, u32[]{:S(2)}, u32[]{:S(2)}) collective-permute-start(bf16[640,1280]{1,0:T(8,128)(2,1)} %get-tuple-element.96), channel_id=1, source_target_pairs={{0,16},{1,17},{2,18},{3,19},{4,20},{5,21},{6,22},{7,23},{8,24},{9,... | collective-permute-start | bytes 4915208 | tf_op jit(solution)/shard_map/ppermute | solution.py:566
  105.7 3.5 %reward_back.1 = (bf16[64,1280]{1,0:T(8,128)(2,1)S(1)}, bf16[64,1280]{1,0:T(8,128)(2,1)S(1)}, bf16[64,1280]{1,0:T(8,128)(2,1)S(1)}, bf16[64,1280]{1,0:T(8,128)(2...) custom-call(s32[4]{0:T(128)S(1)} %pad_add_fusion.refs_0_, f32[8,1280]{1,0:T(8,128)S(1)} %get-tuple-element.78.refs_1_, ...), custom_call_target="tpu_custom_call" | custom-call | flops 99999997952 | bytes 500000000 | tf_op jit(solution)/shard_map/reward_back/pallas_call | solution.py:74
  109.3 1.6 collective-permute-start.19
  110.9 1.2 collective-permute-start.20
  112.1 1.2 collective-permute-start.21
  113.3 4.3 %block0_state.1 = (bf16[512,1280]{1,0:T(8,128)(2,1)S(1)}, bf16[512,1280]{1,0:T(8,128)(2,1)S(1)}, bf16[640,512]{1,0:T(8,128)(2,1)S(1)}, f32[8,128]{1,0:T(8,128)S(1)}) custom-call(s32[4]{0:T(128)S(1)} %pad_add_fusion.refs_0_, bf16[128,1280]{1,0:T(8,128)(2,1)S(1)} %bitcast.37, bf16[128,1280]{1,0:T(8,128)(2,1)S(1)} %copy-done.11, ...), custom_call_target="tpu_custom_call" | custom-call | flops 99999997952 | bytes 500000000 | tf_op jit(solution)/shard_map/block0_state/pallas_call | solution.py:74
  117.7 7.9 %collective-permute-done.20.refs_7_ = bf16[64,1280]{1,0:T(8,128)(2,1)S(1)} collective-permute-done((bf16[64,1280]{1,0:T(8,128)(2,1)S(1)}, bf16[64,1280]{1,0:T(8,128)(2,1)S(1)}, u32[]{:S(2)}, u32[]{:S(2)}) %collective-permute-start.20) | collective-permute-done | bytes 163872 | tf_op jit(solution)/shard_map/ppermute | solution.py:21
  125.6 1.7 eps_gradient.1
  127.4 3.8 %collective-permute-start.24 = (bf16[64,1280]{1,0:T(8,128)(2,1)S(1)}, bf16[64,1280]{1,0:T(8,128)(2,1)S(1)}, u32[]{:S(2)}, u32[]{:S(2)}) collective-permute-start(bf16[64,1280]{1,0:T(8,128)(2,1)S(1)} %get-tuple-element.89.refs_1_), channel_id=1, source_target_pairs={{0,3},{1,0},{2,1},{3,2},{4,7},{5,4},{6,5},{7,6},{8,11},{9,8},{10,9... | collective-permute-start | bytes 491528 | tf_op jit(solution)/shard_map/ppermute | solution.py:21
  131.2 3.7 %collective-permute-done.22.refs_1_.refs_2_ = bf16[64,1280]{1,0:T(8,128)(2,1)S(1)} collective-permute-done((bf16[64,1280]{1,0:T(8,128)(2,1)S(1)}, bf16[64,1280]{1,0:T(8,128)(2,1)S(1)}, u32[]{:S(2)}, u32[]{:S(2)}) %collective-permute-start.22) | collective-permute-done | bytes 163872 | tf_op jit(solution)/shard_map/ppermute | solution.py:21
  134.9 1.6 collective-permute-done.24.refs_2_.refs_4_
  136.5 1.1 join.2
  137.6 1.9 collective-permute-start.23
  139.5 2.0 %collective-permute-start.25 = (bf16[64,1280]{1,0:T(8,128)(2,1)S(1)}, bf16[64,1280]{1,0:T(8,128)(2,1)S(1)}, u32[]{:S(2)}, u32[]{:S(2)}) collective-permute-start(bf16[64,1280]{1,0:T(8,128)(2,1)S(1)} %get-tuple-element.89.refs_1_), channel_id=1, source_target_pairs={{0,16},{16,0},{1,17},{17,1},{2,18},{18,2},{3,19},{19,3},{4,20},{20... | collective-permute-start | bytes 491528 | tf_op jit(solution)/shard_map/ppermute | solution.py:26
  141.5 5.7 %collective-permute-done.23.refs_1_.refs_3_ = bf16[64,1280]{1,0:T(8,128)(2,1)S(1)} collective-permute-done((bf16[64,1280]{1,0:T(8,128)(2,1)S(1)}, bf16[64,1280]{1,0:T(8,128)(2,1)S(1)}, u32[]{:S(2)}, u32[]{:S(2)}) %collective-permute-start.23) | collective-permute-done | bytes 163872 | tf_op jit(solution)/shard_map/ppermute | solution.py:21
  147.7 3.0 %collective-permute-done.25.refs_2_.refs_5_ = bf16[64,1280]{1,0:T(8,128)(2,1)S(1)} collective-permute-done((bf16[64,1280]{1,0:T(8,128)(2,1)S(1)}, bf16[64,1280]{1,0:T(8,128)(2,1)S(1)}, u32[]{:S(2)}, u32[]{:S(2)}) %collective-permute-start.25) | collective-permute-done | bytes 163872 | tf_op jit(solution)/shard_map/ppermute | solution.py:26
  150.7 2.0 %stack.25 = (bf16[1,640,1280]{2,1,0:T(8,128)(2,1)S(1)}, f32[8,128]{1,0:T(8,128)}) custom-call(s32[4]{0:T(128)S(1)} %pad_add_fusion.refs_0_, bf16[640,1280]{1,0:T(8,128)(2,1)} %collective-permute-done.28.refs_1_, bf16[64,1280]{1,0:T(8,128)(2,1)S(1)} %collective-permute-done.25.refs_2_.refs_5_, bf16[128,1280]{1,0:T(8,128)(2,1)S(1)} %collective-permute-done.26.refs_3_.refs_6_, ...), custom_call_target="tpu_custom_call" | custom-call | flops 1 | tf_op jit(solution)/shard_map/stack/pallas_call | solution.py:74
  152.8 2.0 %collective-permute-start.27 = (bf16[64,1280]{1,0:T(8,128)(2,1)S(1)}, bf16[64,1280]{1,0:T(8,128)(2,1)S(1)}, u32[]{:S(2)}, u32[]{:S(2)}) collective-permute-start(bf16[64,1280]{1,0:T(8,128)(2,1)S(1)} %get-tuple-element.91), channel_id=1, source_target_pairs={{0,16},{16,0},{1,17},{17,1},{2,18},{18,2},{3,19},{19,3},{4,20},{20... | collective-permute-start | bytes 491528 | tf_op jit(solution)/shard_map/ppermute | solution.py:26
  154.8 1.5 collective-permute-done.29.refs_2_
  156.3 2.0 %assemble.5 = (bf16[1280,1280]{1,0:T(8,128)(2,1)S(1)}, f32[8,128]{1,0:T(8,128)}) custom-call(s32[4]{0:T(128)S(1)} %pad_add_fusion.refs_0_, bf16[640,1280]{1,0:T(8,128)(2,1)} %collective-permute-done.28.refs_1_, bf16[1,640,1280]{2,1,0:T(8,128)(2,1)S(1)} %collective-permute-done.29.refs_2_), custom_call_target="tpu_custom_call" | custom-call | flops 1 | tf_op jit(solution)/shard_map/assemble/pallas_call | solution.py:74
  158.3 1.3 collective-permute-done.27.refs_7_
  159.6 5.6 %gradients.1 = (bf16[2,160,1280]{2,1,0:T(8,128)(2,1)S(1)}, bf16[2,160,1280]{2,1,0:T(8,128)(2,1)S(1)}, bf16[2,160,1280]{2,1,0:T(8,128)(2,1)S(1)}, bf16[2,160,1280]{2,1,0:T(8,128)(2,1)S(1)}, f32[8,128]{1,0:T(8,128)}) custom-call(s32[4]{0:T(128)S(1)} %pad_add_fusion.refs_0_, bf16[64,1280]{1,0:T(8,128)(2,1)S(1)} %get-tuple-element.89.refs_1_, ...), custom_call_target="tpu_custom_call" | custom-call | flops 99999997952 | bytes 500000000 | tf_op jit(solution)/shard_map/gradients/pallas_call | solution.py:74
  165.8 1.8 collective-permute-done.32.refs_2_
  168.7 1.5 collective-permute-start.33
  170.2 1.1 chip_sum.2
  171.9 9.1 %collective-permute-done.33 = bf16[160,1280]{1,0:T(8,128)(2,1)S(1)} collective-permute-done((bf16[160,1280]{1,0:T(8,128)(2,1)S(1)}, bf16[160,1280]{1,0:T(8,128)(2,1)S(1)}, u32[]{:S(2)}, u32[]{:S(2)}) %collective-permute-start.33) | collective-permute-done | bytes 409632 | tf_op jit(solution)/shard_map/ppermute | solution.py:21
  182.0 7.0 %collective-permute-done.31 = bf16[160,1280]{1,0:T(8,128)(2,1)S(1)} collective-permute-done((bf16[160,1280]{1,0:T(8,128)(2,1)S(1)}, bf16[160,1280]{1,0:T(8,128)(2,1)S(1)}, u32[]{:S(2)}, u32[]{:S(2)}) %collective-permute-start.31) | collective-permute-done | bytes 409632 | tf_op jit(solution)/shard_map/ppermute | solution.py:21
  (85 shorter events, 8.7 us)
Async XLA Ops:
  0.6 81.3 %copy-start = (bf16[64,1280]{1,0:T(8,128)(2,1)S(1)}, bf16[64,1280]{1,0:T(8,128)(2,1)}, u32[]{:S(2)}) copy-start(bf16[64,1280]{1,0:T(8,128)(2,1)} %param.10) | copy-start | bytes 491524
  0.6 13.9 %collective-permute-start = (bf16[128,1280]{1,0:T(8,128)(2,1)}, bf16[128,1280]{1,0:T(8,128)(2,1)S(1)}, u32[]{:S(2)}, u32[]{:S(2)}) collective-permute-start(bf16[128,1280]{1,0:T(8,128)(2,1)} %bitcast.32), channel_id=1, source_target_pairs={{0,1},{1,2},{2,3},{3,0},{4,5},{5,6},{6,7},{7,4},{8,9},{9,10},{10,1... | collective-permute-start | bytes 983048 | tf_op jit(solution)/shard_map/ppermute | solution.py:21
  3.7 16.4 %collective-permute-start.1 = (bf16[128,1280]{1,0:T(8,128)(2,1)}, bf16[128,1280]{1,0:T(8,128)(2,1)S(1)}, u32[]{:S(2)}, u32[]{:S(2)}) collective-permute-start(bf16[128,1280]{1,0:T(8,128)(2,1)} %bitcast.33), channel_id=1, source_target_pairs={{0,3},{1,0},{2,1},{3,2},{4,7},{5,4},{6,5},{7,6},{8,11},{9,8},{10,9... | collective-permute-start | bytes 983048 | tf_op jit(solution)/shard_map/ppermute | solution.py:21
  5.9 1.9 %copy-start.3 = (bf16[1,1280,1280]{2,1,0:T(8,128)(2,1)S(1)}, bf16[1,1280,1280]{2,1,0:T(8,128)(2,1)}, u32[]{:S(2)}) copy-start(bf16[1,1280,1280]{2,1,0:T(8,128)(2,1)} %param.12) | copy-start | bytes 9830404
  7.8 3.2 %copy-start.21 = (s32[2]{0:T(128)S(1)}, s32[2]{0:T(128)}, u32[]{:S(2)}) copy-start(s32[2]{0:T(128)} %param.8) | copy-start | bytes 28
  7.8 5.3 %copy-start.20 = (f32[2,1280]{1,0:T(2,128)S(1)}, f32[2,1280]{1,0:T(2,128)}, u32[]{:S(2)}) copy-start(f32[2,1280]{1,0:T(2,128)} %param.11) | copy-start | bytes 30724
  7.8 12.3 %copy-start.8 = (bf16[2,64,1280]{2,1,0:T(8,128)(2,1)S(1)}, bf16[2,64,1280]{2,1,0:T(8,128)(2,1)}, u32[]{:S(2)}) copy-start(bf16[2,64,1280]{2,1,0:T(8,128)(2,1)} %param.7) | copy-start | bytes 983044
  9.3 20.7 %collective-permute-start.3 = (bf16[320,1280]{1,0:T(8,128)(2,1)}, bf16[320,1280]{1,0:T(8,128)(2,1)}, u32[]{:S(2)}, u32[]{:S(2)}) collective-permute-start(bf16[320,1280]{1,0:T(8,128)(2,1)} %get-tuple-element.56), channel_id=1, source_target_pairs={{0,16},{16,0},{1,17},{17,1},{2,18},{18,2},{3,19},{19,3},{4,20},{20... | collective-permute-start | bytes 2457608 | tf_op jit(solution)/shard_map/ppermute | solution.py:26
  13.2 26.1 %copy-start.1 = (f32[1,1280]{1,0:T(1,128)}, f32[1,1280]{1,0:T(1,128)S(1)}, u32[]{:S(2)}) copy-start(f32[1,1280]{1,0:T(1,128)S(1)} %get-tuple-element.109.refs_3_.refs_5_) | copy-start | bytes 15364
  13.2 9.6 %copy-start.6 = (bf16[1,1280,1280]{2,1,0:T(8,128)(2,1)S(1)}, bf16[1,1280,1280]{2,1,0:T(8,128)(2,1)}, u32[]{:S(2)}) copy-start(bf16[1,1280,1280]{2,1,0:T(8,128)(2,1)} %param.13) | copy-start | bytes 9830404
  14.5 19.3 %copy-start.10 = (bf16[128,1280]{1,0:T(8,128)(2,1)}, bf16[128,1280]{1,0:T(8,128)(2,1)S(1)}, u32[]{:S(2)}) copy-start(bf16[128,1280]{1,0:T(8,128)(2,1)S(1)} %collective-permute-done.refs_2_.refs_1_) | copy-start | bytes 983044
  20.1 13.8 %copy-start.12 = (bf16[128,1280]{1,0:T(8,128)(2,1)}, bf16[128,1280]{1,0:T(8,128)(2,1)S(1)}, u32[]{:S(2)}) copy-start(bf16[128,1280]{1,0:T(8,128)(2,1)S(1)} %collective-permute-done.1.refs_3_.refs_2_.refs_4_) | copy-start | bytes 983044
  21.4 17.9 %collective-permute-start.2 = (bf16[128,1280]{1,0:T(8,128)(2,1)}, bf16[128,1280]{1,0:T(8,128)(2,1)}, u32[]{:S(2)}, u32[]{:S(2)}) collective-permute-start(bf16[128,1280]{1,0:T(8,128)(2,1)} %get-tuple-element.55), channel_id=1, source_target_pairs={{0,2},{1,3},{2,0},{3,1},{4,6},{5,7},{6,4},{7,5},{8,10},{9,11},{10,... | collective-permute-start | bytes 983048 | tf_op jit(solution)/shard_map/ppermute | solution.py:21
  24.5 9.3 %copy-start.4 = (bf16[1,1280,1280]{2,1,0:T(8,128)(2,1)S(1)}, bf16[1,1280,1280]{2,1,0:T(8,128)(2,1)}, u32[]{:S(2)}) copy-start(bf16[1,1280,1280]{2,1,0:T(8,128)(2,1)} %param.12) | copy-start | bytes 9830404
  24.5 48.6 %collective-permute-start.14 = (bf16[640,1280]{1,0:T(8,128)(2,1)}, bf16[640,1280]{1,0:T(8,128)(2,1)}, u32[]{:S(2)}, u32[]{:S(2)}) collective-permute-start(bf16[640,1280]{1,0:T(8,128)(2,1)} %get-tuple-element.75), channel_id=1, source_target_pairs={{16,0},{17,1},{18,2},{19,3},{20,4},{21,5},{22,6},{23,7},{24,8},{25... | collective-permute-start | bytes 4915208 | tf_op jit(solution)/shard_map/ppermute | solution.py:538
  32.1 18.4 %collective-permute-start.9 = (bf16[320,1280]{1,0:T(8,128)(2,1)}, bf16[320,1280]{1,0:T(8,128)(2,1)}, u32[]{:S(2)}, u32[]{:S(2)}) collective-permute-start(bf16[320,1280]{1,0:T(8,128)(2,1)} %get-tuple-element.69), channel_id=1, source_target_pairs={{0,8},{4,12},{8,0},{12,4},{1,9},{5,13},{9,1},{13,5},{2,10},{6,14},... | collective-permute-start | bytes 2457608 | tf_op jit(solution)/shard_map/ppermute | solution.py:26
  36.8 10.2 %collective-permute-start.5 = (bf16[2,64,1280]{2,1,0:T(8,128)(2,1)S(1)}, bf16[2,64,1280]{2,1,0:T(8,128)(2,1)S(1)}, u32[]{:S(2)}, u32[]{:S(2)}) collective-permute-start(bf16[2,64,1280]{2,1,0:T(8,128)(2,1)S(1)} %get-tuple-element.64), channel_id=1, source_target_pairs={{0,16},{1,17},{2,18},{3,19},{4,20},{5,21},{6,22},{7,23},{8,24},{9,... | collective-permute-start | bytes 983048 | tf_op jit(solution)/shard_map/ppermute | solution.py:551
  43.4 9.2 %collective-permute-start.4 = (bf16[2,64,1280]{2,1,0:T(8,128)(2,1)}, bf16[2,64,1280]{2,1,0:T(8,128)(2,1)}, u32[]{:S(2)}, u32[]{:S(2)}) collective-permute-start(bf16[2,64,1280]{2,1,0:T(8,128)(2,1)} %get-tuple-element.62), channel_id=1, source_target_pairs={{0,16},{1,17},{2,18},{3,19},{4,20},{5,21},{6,22},{7,23},{8,24},{9,... | collective-permute-start | bytes 983048 | tf_op jit(solution)/shard_map/ppermute | solution.py:551
  48.1 6.3 %collective-permute-start.6 = (bf16[64,1280]{1,0:T(8,128)(2,1)S(1)}, bf16[64,1280]{1,0:T(8,128)(2,1)S(1)}, u32[]{:S(2)}, u32[]{:S(2)}) collective-permute-start(bf16[64,1280]{1,0:T(8,128)(2,1)S(1)} %get-tuple-element.65), channel_id=1, source_target_pairs={{0,3},{1,0},{2,1},{3,2},{4,7},{5,4},{6,5},{7,6},{8,11},{9,8},{10,9... | collective-permute-start | bytes 491528 | tf_op jit(solution)/shard_map/ppermute | solution.py:21
  49.7 7.5 %collective-permute-start.7 = (bf16[64,1280]{1,0:T(8,128)(2,1)S(1)}, bf16[64,1280]{1,0:T(8,128)(2,1)S(1)}, u32[]{:S(2)}, u32[]{:S(2)}) collective-permute-start(bf16[64,1280]{1,0:T(8,128)(2,1)S(1)} %get-tuple-element.66), channel_id=1, source_target_pairs={{0,1},{1,2},{2,3},{3,0},{4,5},{5,6},{6,7},{7,4},{8,9},{9,10},{10,1... | collective-permute-start | bytes 491528 | tf_op jit(solution)/shard_map/ppermute | solution.py:21
  52.5 7.1 %collective-permute-start.10 = (bf16[2,320,1280]{2,1,0:T(8,128)(2,1)S(1)}, bf16[2,320,1280]{2,1,0:T(8,128)(2,1)S(1)}, u32[]{:S(2)}, u32[]{:S(2)}) collective-permute-start(bf16[2,320,1280]{2,1,0:T(8,128)(2,1)S(1)} %get-tuple-element.71), channel_id=1, source_target_pairs={{0,4},{4,0},{8,12},{12,8},{1,5},{5,1},{9,13},{13,9},{2,6},{6,2},{1... | collective-permute-start | bytes 4915208 | tf_op jit(solution)/shard_map/ppermute | solution.py:26
  58.8 9.2 %collective-permute-start.8 = (bf16[64,1280]{1,0:T(8,128)(2,1)S(1)}, bf16[64,1280]{1,0:T(8,128)(2,1)S(1)}, u32[]{:S(2)}, u32[]{:S(2)}) collective-permute-start(bf16[64,1280]{1,0:T(8,128)(2,1)S(1)} %get-tuple-element.68), channel_id=1, source_target_pairs={{0,2},{1,3},{2,0},{3,1},{4,6},{5,7},{6,4},{7,5},{8,10},{9,11},{10,... | collective-permute-start | bytes 491528 | tf_op jit(solution)/shard_map/ppermute | solution.py:21
  61.3 1.7 copy-start.18
  69.3 10.7 %copy-start.22 = (s32[2]{0:T(128)S(1)}, s32[2]{0:T(128)}, u32[]{:S(2)}) copy-start(s32[2]{0:T(128)} %param.9) | copy-start | bytes 28
  69.3 8.5 %collective-permute-start.11 = (bf16[64,1280]{1,0:T(8,128)(2,1)}, bf16[64,1280]{1,0:T(8,128)(2,1)S(1)}, u32[]{:S(2)}, u32[]{:S(2)}) collective-permute-start(bf16[64,1280]{1,0:T(8,128)(2,1)} %get-tuple-element.73.refs_1_), channel_id=1, source_target_pairs={{0,1},{1,2},{2,3},{3,0},{4,5},{5,6},{6,7},{7,4},{8,9},{9,10},{10,1... | collective-permute-start | bytes 491528 | tf_op jit(solution)/shard_map/ppermute | solution.py:21
  69.3 8.5 %collective-permute-start.13 = (bf16[64,1280]{1,0:T(8,128)(2,1)}, bf16[64,1280]{1,0:T(8,128)(2,1)S(1)}, u32[]{:S(2)}, u32[]{:S(2)}) collective-permute-start(bf16[64,1280]{1,0:T(8,128)(2,1)} %get-tuple-element.73.refs_1_), channel_id=1, source_target_pairs={{0,3},{1,0},{2,1},{3,2},{4,7},{5,4},{6,5},{7,6},{8,11},{9,8},{10,9... | collective-permute-start | bytes 491528 | tf_op jit(solution)/shard_map/ppermute | solution.py:21
  77.8 2.2 %copy-start.14 = (bf16[64,1280]{1,0:T(8,128)(2,1)}, bf16[64,1280]{1,0:T(8,128)(2,1)S(1)}, u32[]{:S(2)}) copy-start(bf16[64,1280]{1,0:T(8,128)(2,1)S(1)} %collective-permute-done.11.refs_2_) | copy-start | bytes 491524
  77.8 2.2 %copy-start.16 = (bf16[64,1280]{1,0:T(8,128)(2,1)}, bf16[64,1280]{1,0:T(8,128)(2,1)S(1)}, u32[]{:S(2)}) copy-start(bf16[64,1280]{1,0:T(8,128)(2,1)S(1)} %collective-permute-done.13.refs_3_.refs_4_) | copy-start | bytes 491524
  80.0 4.5 %collective-permute-start.15 = (bf16[1,640,1280]{2,1,0:T(8,128)(2,1)S(1)}, bf16[1,640,1280]{2,1,0:T(8,128)(2,1)S(1)}, u32[]{:S(2)}, u32[]{:S(2)}) collective-permute-start(bf16[1,640,1280]{2,1,0:T(8,128)(2,1)S(1)} %get-tuple-element.76), channel_id=1, source_target_pairs={{0,4},{4,0},{8,12},{12,8},{1,5},{5,1},{9,13},{13,9},{2,6},{6,2},{1... | collective-permute-start | bytes 4915208 | tf_op jit(solution)/shard_map/ppermute | solution.py:26
  82.1 11.3 %copy-start.5 = (bf16[1,1280,1280]{2,1,0:T(8,128)(2,1)S(1)}, bf16[1,1280,1280]{2,1,0:T(8,128)(2,1)}, u32[]{:S(2)}) copy-start(bf16[1,1280,1280]{2,1,0:T(8,128)(2,1)} %param.12) | copy-start | bytes 9830404
  82.1 11.3 %copy-start.7 = (bf16[1,1280,1280]{2,1,0:T(8,128)(2,1)S(1)}, bf16[1,1280,1280]{2,1,0:T(8,128)(2,1)}, u32[]{:S(2)}) copy-start(bf16[1,1280,1280]{2,1,0:T(8,128)(2,1)} %param.13) | copy-start | bytes 9830404
  82.1 11.3 %copy-start.15 = (bf16[64,1280]{1,0:T(8,128)(2,1)S(1)}, bf16[64,1280]{1,0:T(8,128)(2,1)}, u32[]{:S(2)}) copy-start(bf16[64,1280]{1,0:T(8,128)(2,1)} %copy-done.14) | copy-start | bytes 491524
  82.1 11.3 %copy-start.17 = (bf16[64,1280]{1,0:T(8,128)(2,1)S(1)}, bf16[64,1280]{1,0:T(8,128)(2,1)}, u32[]{:S(2)}) copy-start(bf16[64,1280]{1,0:T(8,128)(2,1)} %copy-done.16) | copy-start | bytes 491524
  82.1 11.3 %copy-start.19 = (bf16[1280,1280]{1,0:T(8,128)(2,1)S(1)}, bf16[1280,1280]{1,0:T(8,128)(2,1)}, u32[]{:S(2)}) copy-start(bf16[1280,1280]{1,0:T(8,128)(2,1)} %copy-done.18) | copy-start | bytes 9830404
  82.1 11.2 %collective-permute-start.12 = (bf16[64,1280]{1,0:T(8,128)(2,1)}, bf16[64,1280]{1,0:T(8,128)(2,1)S(1)}, u32[]{:S(2)}, u32[]{:S(2)}) collective-permute-start(bf16[64,1280]{1,0:T(8,128)(2,1)} %get-tuple-element.73.refs_1_), channel_id=1, source_target_pairs={{0,2},{1,3},{2,0},{3,1},{4,6},{5,7},{6,4},{7,5},{8,10},{9,11},{10,... | collective-permute-start | bytes 491528 | tf_op jit(solution)/shard_map/ppermute | solution.py:21
  97.6 8.1 %collective-permute-start.16 = (f32[8,1280]{1,0:T(8,128)S(1)}, f32[8,1280]{1,0:T(8,128)S(1)}, u32[]{:S(2)}, u32[]{:S(2)}) collective-permute-start(f32[8,1280]{1,0:T(8,128)S(1)} %get-tuple-element.78.refs_1_), channel_id=1, source_target_pairs={{0,1},{1,2},{2,3},{3,0},{4,5},{5,6},{6,7},{7,4},{8,9},{9,10},{10,1... | collective-permute-start | bytes 122888 | tf_op jit(solution)/shard_map/ppermute | solution.py:21
  97.6 8.1 %collective-permute-start.17 = (f32[8,1280]{1,0:T(8,128)S(1)}, f32[8,1280]{1,0:T(8,128)S(1)}, u32[]{:S(2)}, u32[]{:S(2)}) collective-permute-start(f32[8,1280]{1,0:T(8,128)S(1)} %get-tuple-element.78.refs_1_), channel_id=1, source_target_pairs={{0,2},{1,3},{2,0},{3,1},{4,6},{5,7},{6,4},{7,5},{8,10},{9,11},{10,... | collective-permute-start | bytes 122888 | tf_op jit(solution)/shard_map/ppermute | solution.py:21
  100.8 4.9 %collective-permute-start.18 = (f32[8,1280]{1,0:T(8,128)S(1)}, f32[8,1280]{1,0:T(8,128)S(1)}, u32[]{:S(2)}, u32[]{:S(2)}) collective-permute-start(f32[8,1280]{1,0:T(8,128)S(1)} %get-tuple-element.78.refs_1_), channel_id=1, source_target_pairs={{0,3},{1,0},{2,1},{3,2},{4,7},{5,4},{6,5},{7,6},{8,11},{9,8},{10,9... | collective-permute-start | bytes 122888 | tf_op jit(solution)/shard_map/ppermute | solution.py:21
  103.2 47.5 %collective-permute-start.28 = (bf16[640,1280]{1,0:T(8,128)(2,1)}, bf16[640,1280]{1,0:T(8,128)(2,1)}, u32[]{:S(2)}, u32[]{:S(2)}) collective-permute-start(bf16[640,1280]{1,0:T(8,128)(2,1)} %get-tuple-element.96), channel_id=1, source_target_pairs={{0,16},{1,17},{2,18},{3,19},{4,20},{5,21},{6,22},{7,23},{8,24},{9,... | collective-permute-start | bytes 4915208 | tf_op jit(solution)/shard_map/ppermute | solution.py:566
  105.7 7.6 %copy-start.2 = (f32[1,1280]{1,0:T(1,128)S(1)}, f32[1,1280]{1,0:T(1,128)}, u32[]{:S(2)}) copy-start(f32[1,1280]{1,0:T(1,128)} %copy-done.1) | copy-start | bytes 15364
  105.7 7.6 %copy-start.9 = (bf16[2,64,1280]{2,1,0:T(8,128)(2,1)S(1)}, bf16[2,64,1280]{2,1,0:T(8,128)(2,1)}, u32[]{:S(2)}) copy-start(bf16[2,64,1280]{2,1,0:T(8,128)(2,1)} %param.7) | copy-start | bytes 983044
  105.7 7.6 %copy-start.11 = (bf16[128,1280]{1,0:T(8,128)(2,1)S(1)}, bf16[128,1280]{1,0:T(8,128)(2,1)}, u32[]{:S(2)}) copy-start(bf16[128,1280]{1,0:T(8,128)(2,1)} %copy-done.10) | copy-start | bytes 983044
  105.7 7.6 %copy-start.13 = (bf16[128,1280]{1,0:T(8,128)(2,1)S(1)}, bf16[128,1280]{1,0:T(8,128)(2,1)}, u32[]{:S(2)}) copy-start(bf16[128,1280]{1,0:T(8,128)(2,1)} %copy-done.12) | copy-start | bytes 983044
  109.3 8.4 %collective-permute-start.19 = (bf16[64,1280]{1,0:T(8,128)(2,1)S(1)}, bf16[64,1280]{1,0:T(8,128)(2,1)S(1)}, u32[]{:S(2)}, u32[]{:S(2)}) collective-permute-start(bf16[64,1280]{1,0:T(8,128)(2,1)S(1)} %get-tuple-element.85), channel_id=1, source_target_pairs={{0,3},{1,0},{2,1},{3,2},{4,7},{5,4},{6,5},{7,6},{8,11},{9,8},{10,9... | collective-permute-start | bytes 491528 | tf_op jit(solution)/shard_map/ppermute | solution.py:21
  110.9 14.7 %collective-permute-start.20 = (bf16[64,1280]{1,0:T(8,128)(2,1)S(1)}, bf16[64,1280]{1,0:T(8,128)(2,1)S(1)}, u32[]{:S(2)}, u32[]{:S(2)}) collective-permute-start(bf16[64,1280]{1,0:T(8,128)(2,1)S(1)} %get-tuple-element.86), channel_id=1, source_target_pairs={{0,2},{1,3},{2,0},{3,1},{4,6},{5,7},{6,4},{7,5},{8,10},{9,11},{10,... | collective-permute-start | bytes 491528 | tf_op jit(solution)/shard_map/ppermute | solution.py:21
  112.1 13.5 %collective-permute-start.21 = (bf16[64,1280]{1,0:T(8,128)(2,1)S(1)}, bf16[64,1280]{1,0:T(8,128)(2,1)S(1)}, u32[]{:S(2)}, u32[]{:S(2)}) collective-permute-start(bf16[64,1280]{1,0:T(8,128)(2,1)S(1)} %get-tuple-element.87), channel_id=1, source_target_pairs={{0,1},{1,2},{2,3},{3,0},{4,5},{5,6},{6,7},{7,4},{8,9},{9,10},{10,1... | collective-permute-start | bytes 491528 | tf_op jit(solution)/shard_map/ppermute | solution.py:21
  127.4 7.5 %collective-permute-start.22 = (bf16[64,1280]{1,0:T(8,128)(2,1)S(1)}, bf16[64,1280]{1,0:T(8,128)(2,1)S(1)}, u32[]{:S(2)}, u32[]{:S(2)}) collective-permute-start(bf16[64,1280]{1,0:T(8,128)(2,1)S(1)} %get-tuple-element.89.refs_1_), channel_id=1, source_target_pairs={{0,1},{1,2},{2,3},{3,0},{4,5},{5,6},{6,7},{7,4},{8,9},{9,10},{10,1... | collective-permute-start | bytes 491528 | tf_op jit(solution)/shard_map/ppermute | solution.py:21
  127.4 9.1 %collective-permute-start.24 = (bf16[64,1280]{1,0:T(8,128)(2,1)S(1)}, bf16[64,1280]{1,0:T(8,128)(2,1)S(1)}, u32[]{:S(2)}, u32[]{:S(2)}) collective-permute-start(bf16[64,1280]{1,0:T(8,128)(2,1)S(1)} %get-tuple-element.89.refs_1_), channel_id=1, source_target_pairs={{0,3},{1,0},{2,1},{3,2},{4,7},{5,4},{6,5},{7,6},{8,11},{9,8},{10,9... | collective-permute-start | bytes 491528 | tf_op jit(solution)/shard_map/ppermute | solution.py:21
  137.6 13.1 %collective-permute-start.26 = (bf16[128,1280]{1,0:T(8,128)(2,1)S(1)}, bf16[128,1280]{1,0:T(8,128)(2,1)S(1)}, u32[]{:S(2)}, u32[]{:S(2)}) collective-permute-start(bf16[128,1280]{1,0:T(8,128)(2,1)S(1)} %get-tuple-element.90), channel_id=1, source_target_pairs={{0,16},{16,0},{1,17},{17,1},{2,18},{18,2},{3,19},{19,3},{4,20},{20... | collective-permute-start | bytes 983048 | tf_op jit(solution)/shard_map/ppermute | solution.py:26
  137.6 9.5 %collective-permute-start.23 = (bf16[64,1280]{1,0:T(8,128)(2,1)S(1)}, bf16[64,1280]{1,0:T(8,128)(2,1)S(1)}, u32[]{:S(2)}, u32[]{:S(2)}) collective-permute-start(bf16[64,1280]{1,0:T(8,128)(2,1)S(1)} %get-tuple-element.89.refs_1_), channel_id=1, source_target_pairs={{0,2},{1,3},{2,0},{3,1},{4,6},{5,7},{6,4},{7,5},{8,10},{9,11},{10,... | collective-permute-start | bytes 491528 | tf_op jit(solution)/shard_map/ppermute | solution.py:21
  139.5 11.3 %collective-permute-start.25 = (bf16[64,1280]{1,0:T(8,128)(2,1)S(1)}, bf16[64,1280]{1,0:T(8,128)(2,1)S(1)}, u32[]{:S(2)}, u32[]{:S(2)}) collective-permute-start(bf16[64,1280]{1,0:T(8,128)(2,1)S(1)} %get-tuple-element.89.refs_1_), channel_id=1, source_target_pairs={{0,16},{16,0},{1,17},{17,1},{2,18},{18,2},{3,19},{19,3},{4,20},{20... | collective-permute-start | bytes 491528 | tf_op jit(solution)/shard_map/ppermute | solution.py:26
  152.8 3.5 %collective-permute-start.29 = (bf16[1,640,1280]{2,1,0:T(8,128)(2,1)S(1)}, bf16[1,640,1280]{2,1,0:T(8,128)(2,1)S(1)}, u32[]{:S(2)}, u32[]{:S(2)}) collective-permute-start(bf16[1,640,1280]{2,1,0:T(8,128)(2,1)S(1)} %get-tuple-element.98), channel_id=1, source_target_pairs={{0,4},{4,0},{8,12},{12,8},{1,5},{5,1},{9,13},{13,9},{2,6},{6,2},{1... | collective-permute-start | bytes 4915208 | tf_op jit(solution)/shard_map/ppermute | solution.py:26
  152.8 6.8 %collective-permute-start.27 = (bf16[64,1280]{1,0:T(8,128)(2,1)S(1)}, bf16[64,1280]{1,0:T(8,128)(2,1)S(1)}, u32[]{:S(2)}, u32[]{:S(2)}) collective-permute-start(bf16[64,1280]{1,0:T(8,128)(2,1)S(1)} %get-tuple-element.91), channel_id=1, source_target_pairs={{0,16},{16,0},{1,17},{17,1},{2,18},{18,2},{3,19},{19,3},{4,20},{20... | collective-permute-start | bytes 491528 | tf_op jit(solution)/shard_map/ppermute | solution.py:26
  165.2 2.3 %collective-permute-start.32 = (bf16[2,160,1280]{2,1,0:T(8,128)(2,1)S(1)}, bf16[2,160,1280]{2,1,0:T(8,128)(2,1)S(1)}, u32[]{:S(2)}, u32[]{:S(2)}) collective-permute-start(bf16[2,160,1280]{2,1,0:T(8,128)(2,1)S(1)} %get-tuple-element.105), channel_id=1, source_target_pairs={{0,4},{4,0},{8,12},{12,8},{1,5},{5,1},{9,13},{13,9},{2,6},{6,2},{1... | collective-permute-start | bytes 2457608 | tf_op jit(solution)/shard_map/ppermute | solution.py:26
  165.2 5.0 %collective-permute-start.30 = (bf16[2,160,1280]{2,1,0:T(8,128)(2,1)S(1)}, bf16[2,160,1280]{2,1,0:T(8,128)(2,1)S(1)}, u32[]{:S(2)}, u32[]{:S(2)}) collective-permute-start(bf16[2,160,1280]{2,1,0:T(8,128)(2,1)S(1)} %get-tuple-element.101), channel_id=1, source_target_pairs={{0,4},{4,0},{8,12},{12,8},{1,5},{5,1},{9,13},{13,9},{2,6},{6,2},{1... | collective-permute-start | bytes 2457608 | tf_op jit(solution)/shard_map/ppermute | solution.py:26
  168.7 12.3 %collective-permute-start.33 = (bf16[160,1280]{1,0:T(8,128)(2,1)S(1)}, bf16[160,1280]{1,0:T(8,128)(2,1)S(1)}, u32[]{:S(2)}, u32[]{:S(2)}) collective-permute-start(bf16[160,1280]{1,0:T(8,128)(2,1)S(1)} %bitcast.30), channel_id=1, source_target_pairs={{0,8},{4,12},{8,0},{12,4},{1,9},{5,13},{9,1},{13,5},{2,10},{6,14},... | collective-permute-start | bytes 1228808 | tf_op jit(solution)/shard_map/ppermute | solution.py:21
  171.3 17.7 %collective-permute-start.31 = (bf16[160,1280]{1,0:T(8,128)(2,1)S(1)}, bf16[160,1280]{1,0:T(8,128)(2,1)S(1)}, u32[]{:S(2)}, u32[]{:S(2)}) collective-permute-start(bf16[160,1280]{1,0:T(8,128)(2,1)S(1)} %bitcast.31), channel_id=1, source_target_pairs={{0,8},{4,12},{8,0},{12,4},{1,9},{5,13},{9,1},{13,5},{2,10},{6,14},... | collective-permute-start | bytes 1228808 | tf_op jit(solution)/shard_map/ppermute | solution.py:21

commit v13 on v12

--- a/solution.py
+++ b/solution.py
@@ -153,11 +153,12 @@
     rows, hidden = pieces[0].shape
     count = len(pieces)
     out = bf16(count, rows, hidden)
-    stacked = run(stack_body, "stack", sel, pieces, [out], [], after, cost)[0]
+    stacked, token = run(stack_body, "stack", sel, pieces, [out], [], after, cost)
     beside = swapped(stacked, "dp", 1)
     body = functools.partial(assemble_body, count)
     out = bf16(2 * count * rows, hidden)
-    return run(body, "assemble", sel, [*pieces, beside], [out], [], (), cost)
+    whole, done = run(body, "assemble", sel, [*pieces, beside], [out], [], (), cost)
+    return whole, token, done
 
 
 def partial_body(count, sel_ref, *refs):
@@ -555,13 +556,12 @@
             else:
                 sums = [rotated(part, "tp", -k) for k, part in zip(ks, chosen)]
                 before = [partial_token, out_token]
-    other_in, in_token = assembled([got_in, across_in], sel, [partial_token])
-    mine_rows, unused = denoised(flat, sigma, alpha, sums, tokens, sel, [in_token])
+    other_in, unused, in_token = assembled([got_in, across_in], sel, [partial_token])
+    other_out, out_token, joined_token = assembled([got_out], sel, [in_token], COST)
+    other = (other_in, other_out)
+    mine_rows, unused = denoised(flat, sigma, alpha, sums, tokens, sel, [in_token, out_token])
 
     seen_parts = gather_parts(mine_rows)
-    near_seen = [seen_parts[k] for k in near]
-    other_out, joined_token = assembled([got_out], sel, near_seen)
-    other = (other_in, other_out)
     late_share, late_token = share(own[1], 2, sel, [joined_token])
     got_late = lax.ppermute(late_share, "sec", [(0, 1)])
     slopes1, pool = reward_forward(

time: 191 us -> 195 us (1.021)
  waiting for transfers between devices: 75 us -> 85.7 us
  Pallas kernels: 55 us -> 52 us
    ppermute x10, waiting for transfers between devices: 12 us -> 27.4 us  [swapped(): return lax.ppermute(value, axis, [(i, i ^ bit) for i in range(count)])]
    ppermute x20, waiting for transfers between devices: 62.9 us -> 58.3 us  [rotated(): lax.ppermute(value, axis, [(i, (i + steps) % count) for i in range(count)])]
    ppermute x20, starting transfers between devices: 31.1 us -> 28 us  [rotated(): lax.ppermute(value, axis, [(i, (i + steps) % count) for i in range(count)])]
    pallas_call x25, Pallas kernels: 55 us -> 52 us  [run(): pl.pallas_call(with_token, in_specs=[IN_SMEM] + [IN_VMEM] * (len(operands...]
  transfers between devices with their start and end apart: 34 -> 34, of which waited for: 19 -> 18; matrix products, arithmetic and copies ran while one was open for 1% -> 1% of each run, Pallas kernels for 22% -> 21%
where the time goes in v13:
time: 195 us; the launch traced here: 194 us
  waiting for transfers between devices  85.7 us (44%)
  Pallas kernels  52 us (27%)
  starting transfers between devices  47.3 us (24%)
  between operations  3.54 us (2%)
  local copies, waits for them, and re-layouts  3.18 us (2%)
  other arithmetic  1.99 us (1%)
    ppermute x20, waiting for transfers between devices, rotated(): lax.ppermute(value, axis, [(i, (i + steps) % count) for i in range(count)])  58.3 us
    pallas_call x25, Pallas kernels, run(): pl.pallas_call(with_token, in_specs=[IN_SMEM] + [IN_VMEM] * (len(operands...  52 us
    ppermute x20, starting transfers between devices, rotated(): lax.ppermute(value, axis, [(i, (i + steps) % count) for i in range(count)])  28 us
    ppermute x10, waiting for transfers between devices, swapped(): return lax.ppermute(value, axis, [(i, i ^ bit) for i in range(count)])  27.4 us
    ppermute x10, starting transfers between devices, swapped(): return lax.ppermute(value, axis, [(i, i ^ bit) for i in range(count)])  8.39 us
    ppermute x2, starting transfers between devices, on_device(): crossed = lax.ppermute(leave, 'sec', [(0, 1)])  6.9 us
  transfers between devices with their start and end apart: 34, of which 18 were waited for; matrix products, arithmetic and copies ran while one was open for 1% of the time, Pallas kernels for 21%

profile of v13, /device:TPU:0, one launch (start us, length us, event | category | flops | bytes accessed | tf_op | source)
XLA Modules:
  0.0 194.0 jit_solution(8527548043378700596)
XLA Ops:
  0.6 3.1 %collective-permute-start = (bf16[128,1280]{1,0:T(8,128)(2,1)}, bf16[128,1280]{1,0:T(8,128)(2,1)S(1)}, u32[]{:S(2)}, u32[]{:S(2)}) collective-permute-start(bf16[128,1280]{1,0:T(8,128)(2,1)} %bitcast.32), channel_id=1, source_target_pairs={{0,1},{1,2},{2,3},{3,0},{4,5},{5,6},{6,7},{7,4},{8,9},{9,10},{10,1... | collective-permute-start | bytes 983048 | tf_op jit(solution)/shard_map/ppermute | solution.py:21
  3.7 2.1 %collective-permute-start.1 = (bf16[128,1280]{1,0:T(8,128)(2,1)}, bf16[128,1280]{1,0:T(8,128)(2,1)S(1)}, u32[]{:S(2)}, u32[]{:S(2)}) collective-permute-start(bf16[128,1280]{1,0:T(8,128)(2,1)} %bitcast.33), channel_id=1, source_target_pairs={{0,3},{1,0},{2,1},{3,2},{4,7},{5,4},{6,5},{7,6},{8,11},{9,8},{10,9... | collective-permute-start | bytes 983048 | tf_op jit(solution)/shard_map/ppermute | solution.py:21
  5.9 1.9 copy-done.1
  7.8 1.5 share.3
  9.3 1.7 collective-permute-start.3
  15.1 5.0 %collective-permute-done.1.refs_3_.refs_2_.refs_4_ = bf16[128,1280]{1,0:T(8,128)(2,1)S(1)} collective-permute-done((bf16[128,1280]{1,0:T(8,128)(2,1)}, bf16[128,1280]{1,0:T(8,128)(2,1)S(1)}, u32[]{:S(2)}, u32[]{:S(2)}) %collective-permute-start.1) | collective-permute-done | bytes 327712 | tf_op jit(solution)/shard_map/ppermute | solution.py:21
  20.1 1.3 relay.2
  21.4 1.3 collective-permute-start.2
  22.7 1.8 share.4
  24.6 1.5 collective-permute-start.11
  26.1 3.9 %collective-permute-done.3.refs_1_ = bf16[320,1280]{1,0:T(8,128)(2,1)} collective-permute-done((bf16[320,1280]{1,0:T(8,128)(2,1)}, bf16[320,1280]{1,0:T(8,128)(2,1)}, u32[]{:S(2)}, u32[]{:S(2)}) %collective-permute-start.3) | collective-permute-done | bytes 819232 | tf_op jit(solution)/shard_map/ppermute | solution.py:26
  30.0 1.2 relay.3
  31.3 2.9 %block0_partial.2 = (bf16[2,64,1280]{2,1,0:T(8,128)(2,1)S(1)}, bf16[2,64,1280]{2,1,0:T(8,128)(2,1)S(1)}, f32[8,128]{1,0:T(8,128)S(1)}) custom-call(s32[4]{0:T(128)S(1)} %pad_add_fusion.refs_0_, bf16[128,1280]{1,0:T(8,128)(2,1)S(1)} %collective-permute-done.refs_2_.refs_1_, bf16[128,1280]{1,0:T(8,128)(2,1)S(1)} %collective-permute-done.1.refs_3_.refs_2_.refs_4_, ...), custom_call_target="tpu_custom_call" | custom-call | flops 99999997952 | bytes 500000000 | tf_op jit(solution)/shard_map/block0_partial/pallas_call | solution.py:74
  34.2 2.8 %collective-permute-start.5 = (bf16[2,64,1280]{2,1,0:T(8,128)(2,1)S(1)}, bf16[2,64,1280]{2,1,0:T(8,128)(2,1)S(1)}, u32[]{:S(2)}, u32[]{:S(2)}) collective-permute-start(bf16[2,64,1280]{2,1,0:T(8,128)(2,1)S(1)} %get-tuple-element.65), channel_id=1, source_target_pairs={{0,16},{1,17},{2,18},{3,19},{4,20},{5,21},{6,22},{7,23},{8,24},{9,... | collective-permute-start | bytes 983048 | tf_op jit(solution)/shard_map/ppermute | solution.py:552
  37.0 1.8 collective-permute-done.2.refs_2_.refs_3_
  38.8 4.1 %block0_partial.3 = (bf16[2,64,1280]{2,1,0:T(8,128)(2,1)S(1)}, bf16[2,64,1280]{2,1,0:T(8,128)(2,1)}, f32[8,128]{1,0:T(8,128)S(1)}) custom-call(s32[4]{0:T(128)S(1)} %pad_add_fusion.refs_0_, bf16[128,1280]{1,0:T(8,128)(2,1)S(1)} %bitcast.35, bf16[128,1280]{1,0:T(8,128)(2,1)} %collective-permute-done.2.refs_2_.refs_3_, ...), custom_call_target="tpu_custom_call" | custom-call | flops 99999997952 | bytes 500000000 | tf_op jit(solution)/shard_map/block0_partial/pallas_call | solution.py:74
  42.9 4.1 %collective-permute-start.4 = (bf16[2,64,1280]{2,1,0:T(8,128)(2,1)}, bf16[2,64,1280]{2,1,0:T(8,128)(2,1)}, u32[]{:S(2)}, u32[]{:S(2)}) collective-permute-start(bf16[2,64,1280]{2,1,0:T(8,128)(2,1)} %get-tuple-element.63), channel_id=1, source_target_pairs={{0,16},{1,17},{2,18},{3,19},{4,20},{5,21},{6,22},{7,23},{8,24},{9,... | collective-permute-start | bytes 983048 | tf_op jit(solution)/shard_map/ppermute | solution.py:552
  47.0 1.5 collective-permute-start.9
  48.5 1.1 pick.2
  49.6 1.6 collective-permute-start.6
  51.7 14.0 %collective-permute-done.9.refs_2_ = bf16[320,1280]{1,0:T(8,128)(2,1)S(1)} collective-permute-done((bf16[320,1280]{1,0:T(8,128)(2,1)S(1)}, bf16[320,1280]{1,0:T(8,128)(2,1)S(1)}, u32[]{:S(2)}, u32[]{:S(2)}) %collective-permute-start.9) | collective-permute-done | bytes 819232 | tf_op jit(solution)/shard_map/ppermute | solution.py:26
  65.6 1.7 stack.23
  67.4 1.7 pick.3
  69.1 1.8 collective-permute-done.10.refs_3_
  70.9 1.4 assemble.3
  72.3 1.5 stack.24
  74.0 6.4 %collective-permute-done.8.refs_5_ = bf16[64,1280]{1,0:T(8,128)(2,1)} collective-permute-done((bf16[64,1280]{1,0:T(8,128)(2,1)}, bf16[64,1280]{1,0:T(8,128)(2,1)}, u32[]{:S(2)}, u32[]{:S(2)}) %collective-permute-start.8) | collective-permute-done | bytes 163872 | tf_op jit(solution)/shard_map/ppermute | solution.py:21
  80.4 1.5 denoise.1
  82.0 1.7 collective-permute-start.13
  83.7 2.1 %collective-permute-start.14 = (bf16[64,1280]{1,0:T(8,128)(2,1)S(1)}, bf16[64,1280]{1,0:T(8,128)(2,1)S(1)}, u32[]{:S(2)}, u32[]{:S(2)}) collective-permute-start(bf16[64,1280]{1,0:T(8,128)(2,1)S(1)} %get-tuple-element.76.refs_1_), channel_id=1, source_target_pairs={{0,3},{1,0},{2,1},{3,2},{4,7},{5,4},{6,5},{7,6},{8,11},{9,8},{10,9... | collective-permute-start | bytes 491528 | tf_op jit(solution)/shard_map/ppermute | solution.py:21
  85.8 1.7 assemble.4
  87.5 3.5 %collective-permute-done.12.refs_2_ = bf16[64,1280]{1,0:T(8,128)(2,1)S(1)} collective-permute-done((bf16[64,1280]{1,0:T(8,128)(2,1)S(1)}, bf16[64,1280]{1,0:T(8,128)(2,1)S(1)}, u32[]{:S(2)}, u32[]{:S(2)}) %collective-permute-start.12) | collective-permute-done | bytes 163872 | tf_op jit(solution)/shard_map/ppermute | solution.py:21
  90.9 6.0 %collective-permute-done.13.refs_3_ = bf16[64,1280]{1,0:T(8,128)(2,1)S(1)} collective-permute-done((bf16[64,1280]{1,0:T(8,128)(2,1)S(1)}, bf16[64,1280]{1,0:T(8,128)(2,1)S(1)}, u32[]{:S(2)}, u32[]{:S(2)}) %collective-permute-start.13) | collective-permute-done | bytes 163872 | tf_op jit(solution)/shard_map/ppermute | solution.py:21
  97.0 3.7 %reward_forward.1 = (bf16[64,1280]{1,0:T(8,128)(2,1)S(1)}, bf16[64,1280]{1,0:T(8,128)(2,1)S(1)}, bf16[64,1280]{1,0:T(8,128)(2,1)S(1)}, bf16[64,1280]{1,0:T(8,128...) custom-call(s32[4]{0:T(128)S(1)} %pad_add_fusion.refs_0_, bf16[64,1280]{1,0:T(8,128)(2,1)S(1)} %get-tuple-element.76.refs_1_, ...), custom_call_target="tpu_custom_call" | custom-call | flops 99999997952 | bytes 500000000 | tf_op jit(solution)/shard_map/reward_forward/pallas_call | solution.py:74
  100.7 3.1 %collective-permute-start.16 = (f32[8,1280]{1,0:T(8,128)S(1)}, f32[8,1280]{1,0:T(8,128)S(1)}, u32[]{:S(2)}, u32[]{:S(2)}) collective-permute-start(f32[8,1280]{1,0:T(8,128)S(1)} %get-tuple-element.80.refs_1_), channel_id=1, source_target_pairs={{0,1},{1,2},{2,3},{3,0},{4,5},{5,6},{6,7},{7,4},{8,9},{9,10},{10,1... | collective-permute-start | bytes 122888 | tf_op jit(solution)/shard_map/ppermute | solution.py:21
  103.9 2.4 %collective-permute-start.18 = (f32[8,1280]{1,0:T(8,128)S(1)}, f32[8,1280]{1,0:T(8,128)S(1)}, u32[]{:S(2)}, u32[]{:S(2)}) collective-permute-start(f32[8,1280]{1,0:T(8,128)S(1)} %get-tuple-element.80.refs_1_), channel_id=1, source_target_pairs={{0,3},{1,0},{2,1},{3,2},{4,7},{5,4},{6,5},{7,6},{8,11},{9,8},{10,9... | collective-permute-start | bytes 122888 | tf_op jit(solution)/shard_map/ppermute | solution.py:21
  106.2 1.9 share.5
  108.1 2.5 %collective-permute-start.28 = (bf16[640,1280]{1,0:T(8,128)(2,1)}, bf16[640,1280]{1,0:T(8,128)(2,1)}, u32[]{:S(2)}, u32[]{:S(2)}) collective-permute-start(bf16[640,1280]{1,0:T(8,128)(2,1)} %get-tuple-element.98), channel_id=1, source_target_pairs={{0,16},{1,17},{2,18},{3,19},{4,20},{5,21},{6,22},{7,23},{8,24},{9,... | collective-permute-start | bytes 4915208 | tf_op jit(solution)/shard_map/ppermute | solution.py:566
  110.6 3.5 %reward_back.1 = (bf16[64,1280]{1,0:T(8,128)(2,1)S(1)}, bf16[64,1280]{1,0:T(8,128)(2,1)S(1)}, bf16[64,1280]{1,0:T(8,128)(2,1)S(1)}, bf16[64,1280]{1,0:T(8,128)(2...) custom-call(s32[4]{0:T(128)S(1)} %pad_add_fusion.refs_0_, f32[8,1280]{1,0:T(8,128)S(1)} %get-tuple-element.80.refs_1_, ...), custom_call_target="tpu_custom_call" | custom-call | flops 99999997952 | bytes 500000000 | tf_op jit(solution)/shard_map/reward_back/pallas_call | solution.py:74
  114.1 2.0 %collective-permute-start.19 = (bf16[64,1280]{1,0:T(8,128)(2,1)S(1)}, bf16[64,1280]{1,0:T(8,128)(2,1)S(1)}, u32[]{:S(2)}, u32[]{:S(2)}) collective-permute-start(bf16[64,1280]{1,0:T(8,128)(2,1)S(1)} %get-tuple-element.87), channel_id=1, source_target_pairs={{0,3},{1,0},{2,1},{3,2},{4,7},{5,4},{6,5},{7,6},{8,11},{9,8},{10,9... | collective-permute-start | bytes 491528 | tf_op jit(solution)/shard_map/ppermute | solution.py:21
  116.7 4.3 %block0_state.1 = (bf16[512,1280]{1,0:T(8,128)(2,1)S(1)}, bf16[512,1280]{1,0:T(8,128)(2,1)S(1)}, bf16[640,512]{1,0:T(8,128)(2,1)S(1)}, f32[8,128]{1,0:T(8,128)S(1)}) custom-call(s32[4]{0:T(128)S(1)} %pad_add_fusion.refs_0_, bf16[128,1280]{1,0:T(8,128)(2,1)S(1)} %bitcast.37, bf16[128,1280]{1,0:T(8,128)(2,1)S(1)} %collective-permute-done.refs_2_.refs_1_, ...), custom_call_target="tpu_custom_call" | custom-call | flops 99999997952 | bytes 500000000 | tf_op jit(solution)/shard_map/block0_state/pallas_call | solution.py:74
  121.0 8.0 %collective-permute-done.20.refs_7_ = bf16[64,1280]{1,0:T(8,128)(2,1)S(1)} collective-permute-done((bf16[64,1280]{1,0:T(8,128)(2,1)S(1)}, bf16[64,1280]{1,0:T(8,128)(2,1)S(1)}, u32[]{:S(2)}, u32[]{:S(2)}) %collective-permute-start.20) | collective-permute-done | bytes 163872 | tf_op jit(solution)/shard_map/ppermute | solution.py:21
  129.1 1.4 eps_gradient.1
  130.6 3.6 %collective-permute-start.24 = (bf16[64,1280]{1,0:T(8,128)(2,1)S(1)}, bf16[64,1280]{1,0:T(8,128)(2,1)S(1)}, u32[]{:S(2)}, u32[]{:S(2)}) collective-permute-start(bf16[64,1280]{1,0:T(8,128)(2,1)S(1)} %get-tuple-element.91.refs_1_), channel_id=1, source_target_pairs={{0,3},{1,0},{2,1},{3,2},{4,7},{5,4},{6,5},{7,6},{8,11},{9,8},{10,9... | collective-permute-start | bytes 491528 | tf_op jit(solution)/shard_map/ppermute | solution.py:21
  134.3 5.0 %collective-permute-done.22.refs_1_.refs_2_ = bf16[64,1280]{1,0:T(8,128)(2,1)S(1)} collective-permute-done((bf16[64,1280]{1,0:T(8,128)(2,1)S(1)}, bf16[64,1280]{1,0:T(8,128)(2,1)S(1)}, u32[]{:S(2)}, u32[]{:S(2)}) %collective-permute-start.22) | collective-permute-done | bytes 163872 | tf_op jit(solution)/shard_map/ppermute | solution.py:21
  139.8 1.1 join.2
  140.9 1.8 collective-permute-start.23
  142.7 2.0 %collective-permute-start.25 = (bf16[64,1280]{1,0:T(8,128)(2,1)S(1)}, bf16[64,1280]{1,0:T(8,128)(2,1)S(1)}, u32[]{:S(2)}, u32[]{:S(2)}) collective-permute-start(bf16[64,1280]{1,0:T(8,128)(2,1)S(1)} %get-tuple-element.91.refs_1_), channel_id=1, source_target_pairs={{0,16},{16,0},{1,17},{17,1},{2,18},{18,2},{3,19},{19,3},{4,20},{20... | collective-permute-start | bytes 491528 | tf_op jit(solution)/shard_map/ppermute | solution.py:26
  144.7 5.9 %collective-permute-done.23.refs_1_.refs_3_ = bf16[64,1280]{1,0:T(8,128)(2,1)S(1)} collective-permute-done((bf16[64,1280]{1,0:T(8,128)(2,1)S(1)}, bf16[64,1280]{1,0:T(8,128)(2,1)S(1)}, u32[]{:S(2)}, u32[]{:S(2)}) %collective-permute-start.23) | collective-permute-done | bytes 163872 | tf_op jit(solution)/shard_map/ppermute | solution.py:21
  151.2 3.1 %collective-permute-done.25.refs_2_.refs_5_ = bf16[64,1280]{1,0:T(8,128)(2,1)S(1)} collective-permute-done((bf16[64,1280]{1,0:T(8,128)(2,1)S(1)}, bf16[64,1280]{1,0:T(8,128)(2,1)S(1)}, u32[]{:S(2)}, u32[]{:S(2)}) %collective-permute-start.25) | collective-permute-done | bytes 163872 | tf_op jit(solution)/shard_map/ppermute | solution.py:26
  154.2 2.0 %stack.25 = (bf16[1,640,1280]{2,1,0:T(8,128)(2,1)S(1)}, f32[8,128]{1,0:T(8,128)}) custom-call(s32[4]{0:T(128)S(1)} %pad_add_fusion.refs_0_, bf16[640,1280]{1,0:T(8,128)(2,1)} %collective-permute-done.28.refs_1_, bf16[64,1280]{1,0:T(8,128)(2,1)S(1)} %collective-permute-done.25.refs_2_.refs_5_, bf16[128,1280]{1,0:T(8,128)(2,1)S(1)} %collective-permute-done.26.refs_3_.refs_6_, ...), custom_call_target="tpu_custom_call" | custom-call | flops 1 | tf_op jit(solution)/shard_map/stack/pallas_call | solution.py:74
  156.3 2.5 %collective-permute-start.27 = (bf16[64,1280]{1,0:T(8,128)(2,1)S(1)}, bf16[64,1280]{1,0:T(8,128)(2,1)S(1)}, u32[]{:S(2)}, u32[]{:S(2)}) collective-permute-start(bf16[64,1280]{1,0:T(8,128)(2,1)S(1)} %get-tuple-element.93), channel_id=1, source_target_pairs={{0,16},{16,0},{1,17},{17,1},{2,18},{18,2},{3,19},{19,3},{4,20},{20... | collective-permute-start | bytes 491528 | tf_op jit(solution)/shard_map/ppermute | solution.py:26
  158.8 1.0 collective-permute-done.29.refs_2_
  159.8 2.0 %assemble.5 = (bf16[1280,1280]{1,0:T(8,128)(2,1)S(1)}, f32[8,128]{1,0:T(8,128)}) custom-call(s32[4]{0:T(128)S(1)} %pad_add_fusion.refs_0_, bf16[640,1280]{1,0:T(8,128)(2,1)} %collective-permute-done.28.refs_1_, bf16[1,640,1280]{2,1,0:T(8,128)(2,1)S(1)} %collective-permute-done.29.refs_2_), custom_call_target="tpu_custom_call" | custom-call | flops 1 | tf_op jit(solution)/shard_map/assemble/pallas_call | solution.py:74
  161.8 1.8 collective-permute-done.27.refs_7_
  163.6 5.6 %gradients.1 = (bf16[2,160,1280]{2,1,0:T(8,128)(2,1)S(1)}, bf16[2,160,1280]{2,1,0:T(8,128)(2,1)S(1)}, bf16[2,160,1280]{2,1,0:T(8,128)(2,1)S(1)}, bf16[2,160,1280]{2,1,0:T(8,128)(2,1)S(1)}, f32[8,128]{1,0:T(8,128)}) custom-call(s32[4]{0:T(128)S(1)} %pad_add_fusion.refs_0_, bf16[64,1280]{1,0:T(8,128)(2,1)S(1)} %get-tuple-element.91.refs_1_, ...), custom_call_target="tpu_custom_call" | custom-call | flops 99999997952 | bytes 500000000 | tf_op jit(solution)/shard_map/gradients/pallas_call | solution.py:74
  169.8 1.8 collective-permute-done.30.refs_2_
  171.6 1.1 chip_sum.2
  172.7 1.5 collective-permute-start.31
  174.2 1.1 chip_sum.3
  175.9 9.1 %collective-permute-done.31 = bf16[160,1280]{1,0:T(8,128)(2,1)S(1)} collective-permute-done((bf16[160,1280]{1,0:T(8,128)(2,1)S(1)}, bf16[160,1280]{1,0:T(8,128)(2,1)S(1)}, u32[]{:S(2)}, u32[]{:S(2)}) %collective-permute-start.31) | collective-permute-done | bytes 409632 | tf_op jit(solution)/shard_map/ppermute | solution.py:21
  185.0 1.0 convert_add_fusion.1
  186.0 7.0 %collective-permute-done.33 = bf16[160,1280]{1,0:T(8,128)(2,1)S(1)} collective-permute-done((bf16[160,1280]{1,0:T(8,128)(2,1)S(1)}, bf16[160,1280]{1,0:T(8,128)(2,1)S(1)}, u32[]{:S(2)}, u32[]{:S(2)}) %collective-permute-start.33) | collective-permute-done | bytes 409632 | tf_op jit(solution)/shard_map/ppermute | solution.py:21
  193.0 1.0 convert_add_fusion
  (59 shorter events, 5.0 us)
Async XLA Ops:
  0.6 14.3 %copy-start = (bf16[64,1280]{1,0:T(8,128)(2,1)S(1)}, bf16[64,1280]{1,0:T(8,128)(2,1)}, u32[]{:S(2)}) copy-start(bf16[64,1280]{1,0:T(8,128)(2,1)} %param.10) | copy-start | bytes 491524
  0.6 14.4 %collective-permute-start = (bf16[128,1280]{1,0:T(8,128)(2,1)}, bf16[128,1280]{1,0:T(8,128)(2,1)S(1)}, u32[]{:S(2)}, u32[]{:S(2)}) collective-permute-start(bf16[128,1280]{1,0:T(8,128)(2,1)} %bitcast.32), channel_id=1, source_target_pairs={{0,1},{1,2},{2,3},{3,0},{4,5},{5,6},{6,7},{7,4},{8,9},{9,10},{10,1... | collective-permute-start | bytes 983048 | tf_op jit(solution)/shard_map/ppermute | solution.py:21
  3.7 16.4 %collective-permute-start.1 = (bf16[128,1280]{1,0:T(8,128)(2,1)}, bf16[128,1280]{1,0:T(8,128)(2,1)S(1)}, u32[]{:S(2)}, u32[]{:S(2)}) collective-permute-start(bf16[128,1280]{1,0:T(8,128)(2,1)} %bitcast.33), channel_id=1, source_target_pairs={{0,3},{1,0},{2,1},{3,2},{4,7},{5,4},{6,5},{7,6},{8,11},{9,8},{10,9... | collective-permute-start | bytes 983048 | tf_op jit(solution)/shard_map/ppermute | solution.py:21
  5.9 1.9 copy-start.1
  7.8 3.2 %copy-start.8 = (s32[2]{0:T(128)S(1)}, s32[2]{0:T(128)}, u32[]{:S(2)}) copy-start(s32[2]{0:T(128)} %param.8) | copy-start | bytes 28
  7.8 5.2 %copy-start.7 = (f32[2,1280]{1,0:T(2,128)S(1)}, f32[2,1280]{1,0:T(2,128)}, u32[]{:S(2)}) copy-start(f32[2,1280]{1,0:T(2,128)} %param.11) | copy-start | bytes 30724
  7.8 5.2 %copy-start.9 = (s32[2]{0:T(128)S(1)}, s32[2]{0:T(128)}, u32[]{:S(2)}) copy-start(s32[2]{0:T(128)} %param.9) | copy-start | bytes 28
  7.8 12.3 %copy-start.6 = (bf16[2,64,1280]{2,1,0:T(8,128)(2,1)S(1)}, bf16[2,64,1280]{2,1,0:T(8,128)(2,1)}, u32[]{:S(2)}) copy-start(bf16[2,64,1280]{2,1,0:T(8,128)(2,1)} %param.7) | copy-start | bytes 983044
  9.3 20.7 %collective-permute-start.3 = (bf16[320,1280]{1,0:T(8,128)(2,1)}, bf16[320,1280]{1,0:T(8,128)(2,1)}, u32[]{:S(2)}, u32[]{:S(2)}) collective-permute-start(bf16[320,1280]{1,0:T(8,128)(2,1)} %get-tuple-element.57), channel_id=1, source_target_pairs={{0,16},{16,0},{1,17},{17,1},{2,18},{18,2},{3,19},{19,3},{4,20},{20... | collective-permute-start | bytes 2457608 | tf_op jit(solution)/shard_map/ppermute | solution.py:26
  15.1 7.6 %copy-start.4 = (bf16[1,1280,1280]{2,1,0:T(8,128)(2,1)S(1)}, bf16[1,1280,1280]{2,1,0:T(8,128)(2,1)}, u32[]{:S(2)}) copy-start(bf16[1,1280,1280]{2,1,0:T(8,128)(2,1)} %param.13) | copy-start | bytes 9830404
  21.4 17.3 %collective-permute-start.2 = (bf16[128,1280]{1,0:T(8,128)(2,1)}, bf16[128,1280]{1,0:T(8,128)(2,1)}, u32[]{:S(2)}, u32[]{:S(2)}) collective-permute-start(bf16[128,1280]{1,0:T(8,128)(2,1)} %get-tuple-element.56), channel_id=1, source_target_pairs={{0,2},{1,3},{2,0},{3,1},{4,6},{5,7},{6,4},{7,5},{8,10},{9,11},{10,... | collective-permute-start | bytes 983048 | tf_op jit(solution)/shard_map/ppermute | solution.py:21
  24.6 6.7 %copy-start.2 = (bf16[1,1280,1280]{2,1,0:T(8,128)(2,1)S(1)}, bf16[1,1280,1280]{2,1,0:T(8,128)(2,1)}, u32[]{:S(2)}) copy-start(bf16[1,1280,1280]{2,1,0:T(8,128)(2,1)} %param.12) | copy-start | bytes 9830404
  24.6 47.7 %collective-permute-start.11 = (bf16[640,1280]{1,0:T(8,128)(2,1)}, bf16[640,1280]{1,0:T(8,128)(2,1)}, u32[]{:S(2)}, u32[]{:S(2)}) collective-permute-start(bf16[640,1280]{1,0:T(8,128)(2,1)} %get-tuple-element.74), channel_id=1, source_target_pairs={{16,0},{17,1},{18,2},{19,3},{20,4},{21,5},{22,6},{23,7},{24,8},{25... | collective-permute-start | bytes 4915208 | tf_op jit(solution)/shard_map/ppermute | solution.py:539
  34.2 14.3 %collective-permute-start.5 = (bf16[2,64,1280]{2,1,0:T(8,128)(2,1)S(1)}, bf16[2,64,1280]{2,1,0:T(8,128)(2,1)S(1)}, u32[]{:S(2)}, u32[]{:S(2)}) collective-permute-start(bf16[2,64,1280]{2,1,0:T(8,128)(2,1)S(1)} %get-tuple-element.65), channel_id=1, source_target_pairs={{0,16},{1,17},{2,18},{3,19},{4,20},{5,21},{6,22},{7,23},{8,24},{9,... | collective-permute-start | bytes 983048 | tf_op jit(solution)/shard_map/ppermute | solution.py:552
  42.9 24.5 %collective-permute-start.4 = (bf16[2,64,1280]{2,1,0:T(8,128)(2,1)}, bf16[2,64,1280]{2,1,0:T(8,128)(2,1)}, u32[]{:S(2)}, u32[]{:S(2)}) collective-permute-start(bf16[2,64,1280]{2,1,0:T(8,128)(2,1)} %get-tuple-element.63), channel_id=1, source_target_pairs={{0,16},{1,17},{2,18},{3,19},{4,20},{5,21},{6,22},{7,23},{8,24},{9,... | collective-permute-start | bytes 983048 | tf_op jit(solution)/shard_map/ppermute | solution.py:552
  47.0 18.6 %collective-permute-start.9 = (bf16[320,1280]{1,0:T(8,128)(2,1)S(1)}, bf16[320,1280]{1,0:T(8,128)(2,1)S(1)}, u32[]{:S(2)}, u32[]{:S(2)}) collective-permute-start(bf16[320,1280]{1,0:T(8,128)(2,1)S(1)} %get-tuple-element.70), channel_id=1, source_target_pairs={{0,8},{4,12},{8,0},{12,4},{1,9},{5,13},{9,1},{13,5},{2,10},{6,14},... | collective-permute-start | bytes 2457608 | tf_op jit(solution)/shard_map/ppermute | solution.py:26
  49.6 17.8 %collective-permute-start.6 = (bf16[64,1280]{1,0:T(8,128)(2,1)S(1)}, bf16[64,1280]{1,0:T(8,128)(2,1)S(1)}, u32[]{:S(2)}, u32[]{:S(2)}) collective-permute-start(bf16[64,1280]{1,0:T(8,128)(2,1)S(1)} %get-tuple-element.66), channel_id=1, source_target_pairs={{0,3},{1,0},{2,1},{3,2},{4,7},{5,4},{6,5},{7,6},{8,11},{9,8},{10,9... | collective-permute-start | bytes 491528 | tf_op jit(solution)/shard_map/ppermute | solution.py:21
  51.2 16.2 %collective-permute-start.7 = (bf16[64,1280]{1,0:T(8,128)(2,1)S(1)}, bf16[64,1280]{1,0:T(8,128)(2,1)S(1)}, u32[]{:S(2)}, u32[]{:S(2)}) collective-permute-start(bf16[64,1280]{1,0:T(8,128)(2,1)S(1)} %get-tuple-element.67), channel_id=1, source_target_pairs={{0,1},{1,2},{2,3},{3,0},{4,5},{5,6},{6,7},{7,4},{8,9},{9,10},{10,1... | collective-permute-start | bytes 491528 | tf_op jit(solution)/shard_map/ppermute | solution.py:21
  67.4 3.5 %collective-permute-start.10 = (bf16[2,320,1280]{2,1,0:T(8,128)(2,1)S(1)}, bf16[2,320,1280]{2,1,0:T(8,128)(2,1)S(1)}, u32[]{:S(2)}, u32[]{:S(2)}) collective-permute-start(bf16[2,320,1280]{2,1,0:T(8,128)(2,1)S(1)} %get-tuple-element.72), channel_id=1, source_target_pairs={{0,4},{4,0},{8,12},{12,8},{1,5},{5,1},{9,13},{13,9},{2,6},{6,2},{1... | collective-permute-start | bytes 4915208 | tf_op jit(solution)/shard_map/ppermute | solution.py:26
  69.1 11.3 %collective-permute-start.8 = (bf16[64,1280]{1,0:T(8,128)(2,1)}, bf16[64,1280]{1,0:T(8,128)(2,1)}, u32[]{:S(2)}, u32[]{:S(2)}) collective-permute-start(bf16[64,1280]{1,0:T(8,128)(2,1)} %get-tuple-element.69), channel_id=1, source_target_pairs={{0,2},{1,3},{2,0},{3,1},{4,6},{5,7},{6,4},{7,5},{8,10},{9,11},{10,... | collective-permute-start | bytes 491528 | tf_op jit(solution)/shard_map/ppermute | solution.py:21
  73.8 12.0 %collective-permute-start.15 = (bf16[1,640,1280]{2,1,0:T(8,128)(2,1)S(1)}, bf16[1,640,1280]{2,1,0:T(8,128)(2,1)S(1)}, u32[]{:S(2)}, u32[]{:S(2)}) collective-permute-start(bf16[1,640,1280]{2,1,0:T(8,128)(2,1)S(1)} %get-tuple-element.78), channel_id=1, source_target_pairs={{0,4},{4,0},{8,12},{12,8},{1,5},{5,1},{9,13},{13,9},{2,6},{6,2},{1... | collective-permute-start | bytes 4915208 | tf_op jit(solution)/shard_map/ppermute | solution.py:26
  82.0 15.0 %copy-start.3 = (bf16[1,1280,1280]{2,1,0:T(8,128)(2,1)S(1)}, bf16[1,1280,1280]{2,1,0:T(8,128)(2,1)}, u32[]{:S(2)}) copy-start(bf16[1,1280,1280]{2,1,0:T(8,128)(2,1)} %param.12) | copy-start | bytes 9830404
  82.0 15.0 %copy-start.5 = (bf16[1,1280,1280]{2,1,0:T(8,128)(2,1)S(1)}, bf16[1,1280,1280]{2,1,0:T(8,128)(2,1)}, u32[]{:S(2)}) copy-start(bf16[1,1280,1280]{2,1,0:T(8,128)(2,1)} %param.13) | copy-start | bytes 9830404
  82.0 9.0 %collective-permute-start.12 = (bf16[64,1280]{1,0:T(8,128)(2,1)S(1)}, bf16[64,1280]{1,0:T(8,128)(2,1)S(1)}, u32[]{:S(2)}, u32[]{:S(2)}) collective-permute-start(bf16[64,1280]{1,0:T(8,128)(2,1)S(1)} %get-tuple-element.76.refs_1_), channel_id=1, source_target_pairs={{0,1},{1,2},{2,3},{3,0},{4,5},{5,6},{6,7},{7,4},{8,9},{9,10},{10,1... | collective-permute-start | bytes 491528 | tf_op jit(solution)/shard_map/ppermute | solution.py:21
  82.0 15.0 %collective-permute-start.13 = (bf16[64,1280]{1,0:T(8,128)(2,1)S(1)}, bf16[64,1280]{1,0:T(8,128)(2,1)S(1)}, u32[]{:S(2)}, u32[]{:S(2)}) collective-permute-start(bf16[64,1280]{1,0:T(8,128)(2,1)S(1)} %get-tuple-element.76.refs_1_), channel_id=1, source_target_pairs={{0,2},{1,3},{2,0},{3,1},{4,6},{5,7},{6,4},{7,5},{8,10},{9,11},{10,... | collective-permute-start | bytes 491528 | tf_op jit(solution)/shard_map/ppermute | solution.py:21
  83.7 13.3 %collective-permute-start.14 = (bf16[64,1280]{1,0:T(8,128)(2,1)S(1)}, bf16[64,1280]{1,0:T(8,128)(2,1)S(1)}, u32[]{:S(2)}, u32[]{:S(2)}) collective-permute-start(bf16[64,1280]{1,0:T(8,128)(2,1)S(1)} %get-tuple-element.76.refs_1_), channel_id=1, source_target_pairs={{0,3},{1,0},{2,1},{3,2},{4,7},{5,4},{6,5},{7,6},{8,11},{9,8},{10,9... | collective-permute-start | bytes 491528 | tf_op jit(solution)/shard_map/ppermute | solution.py:21
  100.7 9.8 %collective-permute-start.16 = (f32[8,1280]{1,0:T(8,128)S(1)}, f32[8,1280]{1,0:T(8,128)S(1)}, u32[]{:S(2)}, u32[]{:S(2)}) collective-permute-start(f32[8,1280]{1,0:T(8,128)S(1)} %get-tuple-element.80.refs_1_), channel_id=1, source_target_pairs={{0,1},{1,2},{2,3},{3,0},{4,5},{5,6},{6,7},{7,4},{8,9},{9,10},{10,1... | collective-permute-start | bytes 122888 | tf_op jit(solution)/shard_map/ppermute | solution.py:21
  103.9 6.7 %collective-permute-start.17 = (f32[8,1280]{1,0:T(8,128)S(1)}, f32[8,1280]{1,0:T(8,128)S(1)}, u32[]{:S(2)}, u32[]{:S(2)}) collective-permute-start(f32[8,1280]{1,0:T(8,128)S(1)} %get-tuple-element.80.refs_1_), channel_id=1, source_target_pairs={{0,2},{1,3},{2,0},{3,1},{4,6},{5,7},{6,4},{7,5},{8,10},{9,11},{10,... | collective-permute-start | bytes 122888 | tf_op jit(solution)/shard_map/ppermute | solution.py:21
  103.9 6.7 %collective-permute-start.18 = (f32[8,1280]{1,0:T(8,128)S(1)}, f32[8,1280]{1,0:T(8,128)S(1)}, u32[]{:S(2)}, u32[]{:S(2)}) collective-permute-start(f32[8,1280]{1,0:T(8,128)S(1)} %get-tuple-element.80.refs_1_), channel_id=1, source_target_pairs={{0,3},{1,0},{2,1},{3,2},{4,7},{5,4},{6,5},{7,6},{8,11},{9,8},{10,9... | collective-permute-start | bytes 122888 | tf_op jit(solution)/shard_map/ppermute | solution.py:21
  108.1 46.2 %collective-permute-start.28 = (bf16[640,1280]{1,0:T(8,128)(2,1)}, bf16[640,1280]{1,0:T(8,128)(2,1)}, u32[]{:S(2)}, u32[]{:S(2)}) collective-permute-start(bf16[640,1280]{1,0:T(8,128)(2,1)} %get-tuple-element.98), channel_id=1, source_target_pairs={{0,16},{1,17},{2,18},{3,19},{4,20},{5,21},{6,22},{7,23},{8,24},{9,... | collective-permute-start | bytes 4915208 | tf_op jit(solution)/shard_map/ppermute | solution.py:566
  114.1 6.9 %collective-permute-start.19 = (bf16[64,1280]{1,0:T(8,128)(2,1)S(1)}, bf16[64,1280]{1,0:T(8,128)(2,1)S(1)}, u32[]{:S(2)}, u32[]{:S(2)}) collective-permute-start(bf16[64,1280]{1,0:T(8,128)(2,1)S(1)} %get-tuple-element.87), channel_id=1, source_target_pairs={{0,3},{1,0},{2,1},{3,2},{4,7},{5,4},{6,5},{7,6},{8,11},{9,8},{10,9... | collective-permute-start | bytes 491528 | tf_op jit(solution)/shard_map/ppermute | solution.py:21
  116.1 12.9 %collective-permute-start.20 = (bf16[64,1280]{1,0:T(8,128)(2,1)S(1)}, bf16[64,1280]{1,0:T(8,128)(2,1)S(1)}, u32[]{:S(2)}, u32[]{:S(2)}) collective-permute-start(bf16[64,1280]{1,0:T(8,128)(2,1)S(1)} %get-tuple-element.88), channel_id=1, source_target_pairs={{0,2},{1,3},{2,0},{3,1},{4,6},{5,7},{6,4},{7,5},{8,10},{9,11},{10,... | collective-permute-start | bytes 491528 | tf_op jit(solution)/shard_map/ppermute | solution.py:21
  116.2 12.9 %collective-permute-start.21 = (bf16[64,1280]{1,0:T(8,128)(2,1)S(1)}, bf16[64,1280]{1,0:T(8,128)(2,1)S(1)}, u32[]{:S(2)}, u32[]{:S(2)}) collective-permute-start(bf16[64,1280]{1,0:T(8,128)(2,1)S(1)} %get-tuple-element.89), channel_id=1, source_target_pairs={{0,1},{1,2},{2,3},{3,0},{4,5},{5,6},{6,7},{7,4},{8,9},{9,10},{10,1... | collective-permute-start | bytes 491528 | tf_op jit(solution)/shard_map/ppermute | solution.py:21
  130.4 8.8 %collective-permute-start.22 = (bf16[64,1280]{1,0:T(8,128)(2,1)S(1)}, bf16[64,1280]{1,0:T(8,128)(2,1)S(1)}, u32[]{:S(2)}, u32[]{:S(2)}) collective-permute-start(bf16[64,1280]{1,0:T(8,128)(2,1)S(1)} %get-tuple-element.91.refs_1_), channel_id=1, source_target_pairs={{0,1},{1,2},{2,3},{3,0},{4,5},{5,6},{6,7},{7,4},{8,9},{9,10},{10,1... | collective-permute-start | bytes 491528 | tf_op jit(solution)/shard_map/ppermute | solution.py:21
  130.6 9.1 %collective-permute-start.24 = (bf16[64,1280]{1,0:T(8,128)(2,1)S(1)}, bf16[64,1280]{1,0:T(8,128)(2,1)S(1)}, u32[]{:S(2)}, u32[]{:S(2)}) collective-permute-start(bf16[64,1280]{1,0:T(8,128)(2,1)S(1)} %get-tuple-element.91.refs_1_), channel_id=1, source_target_pairs={{0,3},{1,0},{2,1},{3,2},{4,7},{5,4},{6,5},{7,6},{8,11},{9,8},{10,9... | collective-permute-start | bytes 491528 | tf_op jit(solution)/shard_map/ppermute | solution.py:21
  140.9 13.3 %collective-permute-start.26 = (bf16[128,1280]{1,0:T(8,128)(2,1)S(1)}, bf16[128,1280]{1,0:T(8,128)(2,1)S(1)}, u32[]{:S(2)}, u32[]{:S(2)}) collective-permute-start(bf16[128,1280]{1,0:T(8,128)(2,1)S(1)} %get-tuple-element.92), channel_id=1, source_target_pairs={{0,16},{16,0},{1,17},{17,1},{2,18},{18,2},{3,19},{19,3},{4,20},{20... | collective-permute-start | bytes 983048 | tf_op jit(solution)/shard_map/ppermute | solution.py:26
  140.9 9.7 %collective-permute-start.23 = (bf16[64,1280]{1,0:T(8,128)(2,1)S(1)}, bf16[64,1280]{1,0:T(8,128)(2,1)S(1)}, u32[]{:S(2)}, u32[]{:S(2)}) collective-permute-start(bf16[64,1280]{1,0:T(8,128)(2,1)S(1)} %get-tuple-element.91.refs_1_), channel_id=1, source_target_pairs={{0,2},{1,3},{2,0},{3,1},{4,6},{5,7},{6,4},{7,5},{8,10},{9,11},{10,... | collective-permute-start | bytes 491528 | tf_op jit(solution)/shard_map/ppermute | solution.py:21
  142.7 11.6 %collective-permute-start.25 = (bf16[64,1280]{1,0:T(8,128)(2,1)S(1)}, bf16[64,1280]{1,0:T(8,128)(2,1)S(1)}, u32[]{:S(2)}, u32[]{:S(2)}) collective-permute-start(bf16[64,1280]{1,0:T(8,128)(2,1)S(1)} %get-tuple-element.91.refs_1_), channel_id=1, source_target_pairs={{0,16},{16,0},{1,17},{17,1},{2,18},{18,2},{3,19},{19,3},{4,20},{20... | collective-permute-start | bytes 491528 | tf_op jit(solution)/shard_map/ppermute | solution.py:26
  156.3 3.5 %collective-permute-start.29 = (bf16[1,640,1280]{2,1,0:T(8,128)(2,1)S(1)}, bf16[1,640,1280]{2,1,0:T(8,128)(2,1)S(1)}, u32[]{:S(2)}, u32[]{:S(2)}) collective-permute-start(bf16[1,640,1280]{2,1,0:T(8,128)(2,1)S(1)} %get-tuple-element.100), channel_id=1, source_target_pairs={{0,4},{4,0},{8,12},{12,8},{1,5},{5,1},{9,13},{13,9},{2,6},{6,2},{1... | collective-permute-start | bytes 4915208 | tf_op jit(solution)/shard_map/ppermute | solution.py:26
  156.3 7.4 %collective-permute-start.27 = (bf16[64,1280]{1,0:T(8,128)(2,1)S(1)}, bf16[64,1280]{1,0:T(8,128)(2,1)S(1)}, u32[]{:S(2)}, u32[]{:S(2)}) collective-permute-start(bf16[64,1280]{1,0:T(8,128)(2,1)S(1)} %get-tuple-element.93), channel_id=1, source_target_pairs={{0,16},{16,0},{1,17},{17,1},{2,18},{18,2},{3,19},{19,3},{4,20},{20... | collective-permute-start | bytes 491528 | tf_op jit(solution)/shard_map/ppermute | solution.py:26
  169.2 2.3 %collective-permute-start.30 = (bf16[2,160,1280]{2,1,0:T(8,128)(2,1)S(1)}, bf16[2,160,1280]{2,1,0:T(8,128)(2,1)S(1)}, u32[]{:S(2)}, u32[]{:S(2)}) collective-permute-start(bf16[2,160,1280]{2,1,0:T(8,128)(2,1)S(1)} %get-tuple-element.103), channel_id=1, source_target_pairs={{0,4},{4,0},{8,12},{12,8},{1,5},{5,1},{9,13},{13,9},{2,6},{6,2},{1... | collective-permute-start | bytes 2457608 | tf_op jit(solution)/shard_map/ppermute | solution.py:26
  169.2 5.0 %collective-permute-start.32 = (bf16[2,160,1280]{2,1,0:T(8,128)(2,1)S(1)}, bf16[2,160,1280]{2,1,0:T(8,128)(2,1)S(1)}, u32[]{:S(2)}, u32[]{:S(2)}) collective-permute-start(bf16[2,160,1280]{2,1,0:T(8,128)(2,1)S(1)} %get-tuple-element.107), channel_id=1, source_target_pairs={{0,4},{4,0},{8,12},{12,8},{1,5},{5,1},{9,13},{13,9},{2,6},{6,2},{1... | collective-permute-start | bytes 2457608 | tf_op jit(solution)/shard_map/ppermute | solution.py:26
  172.7 12.3 %collective-permute-start.31 = (bf16[160,1280]{1,0:T(8,128)(2,1)S(1)}, bf16[160,1280]{1,0:T(8,128)(2,1)S(1)}, u32[]{:S(2)}, u32[]{:S(2)}) collective-permute-start(bf16[160,1280]{1,0:T(8,128)(2,1)S(1)} %bitcast.30), channel_id=1, source_target_pairs={{0,8},{4,12},{8,0},{12,4},{1,9},{5,13},{9,1},{13,5},{2,10},{6,14},... | collective-permute-start | bytes 1228808 | tf_op jit(solution)/shard_map/ppermute | solution.py:21
  175.3 17.7 %collective-permute-start.33 = (bf16[160,1280]{1,0:T(8,128)(2,1)S(1)}, bf16[160,1280]{1,0:T(8,128)(2,1)S(1)}, u32[]{:S(2)}, u32[]{:S(2)}) collective-permute-start(bf16[160,1280]{1,0:T(8,128)(2,1)S(1)} %bitcast.31), channel_id=1, source_target_pairs={{0,8},{4,12},{8,0},{12,4},{1,9},{5,13},{9,1},{13,5},{2,10},{6,14},... | collective-permute-start | bytes 1228808 | tf_op jit(solution)/shard_map/ppermute | solution.py:21

commit v14 on v13

--- a/solution.py
+++ b/solution.py
@@ -178,7 +178,7 @@
         stay[i] = acc[start + late : start + rows, :].astype(jnp.bfloat16)
 
 
-def block0_partials(parts, gain, w_in, w_out, sel, after):
+def block0_partials(parts, gain, w_in, w_out, sel, after, cost):
     rows, width = parts[0].shape
     hidden, n = w_in.shape[1], len(parts)
     return run(
@@ -192,6 +192,7 @@
             pltpu.VMEM((n * rows, width), jnp.float32),
         ],
         after,
+        cost,
     )
 
 
@@ -207,13 +208,13 @@
         out[...] = value
 
 
-def picked(stay, crossed, arrived, sel):
+def picked(stay, crossed, arrived, sel, after):
     count, rows, width = stay.shape
     outs = [bf16(rows, width)] * count
     if arrived:
         outs[0] = jax.ShapeDtypeStruct((rows, width), jnp.float32)
     body = functools.partial(pick_body, len(arrived))
-    *chosen, token = run(body, "pick", sel, [stay, crossed, *arrived], outs, [])
+    *chosen, token = run(body, "pick", sel, [stay, crossed, *arrived], outs, [], after)
     return chosen, token
 
 
@@ -547,10 +548,12 @@
     for ks in (near, rest):
         if ks:
             stay, leave, partial_token = block0_partials(
-                [lat_parts[k] for k in ks], gains[:1], *own, sel, before
+                [lat_parts[k] for k in ks], gains[:1], *own, sel, before, 1 if ks is rest else COST
             )
             crossed = lax.ppermute(leave, "sec", [(0, 1)])
-            chosen, picked_token = picked(stay, crossed, sums if ks is rest else [], sel)
+            chosen, picked_token = picked(
+                stay, crossed, sums if ks is rest else [], sel, [] if ks is rest else [across_in]
+            )
             if ks is rest:
                 sums = [chosen[0]] + [rotated(part, "tp", -k) for k, part in zip(ks[1:], chosen[1:])]
             else:

time: 195 us -> 196 us (level)
  starting transfers between devices: 47.3 us -> 50.7 us
  local copies, waits for them, and re-layouts: 3.18 us -> 5.59 us
  waiting for transfers between devices: 85.7 us -> 83.6 us
  Pallas kernels: 52 us -> 49.9 us
    ppermute x1, waiting for transfers between devices: 0.01 us -> 10.5 us  [on_device(): got_out = lax.ppermute(out_share, 'sec', [(1, 0)])]
    ppermute x10, waiting for transfers between devices: 27.4 us -> 17 us  [swapped(): return lax.ppermute(value, axis, [(i, i ^ bit) for i in range(count)])]
    ppermute x2, starting transfers between devices: 6.9 us -> 9.93 us  [on_device(): crossed = lax.ppermute(leave, 'sec', [(0, 1)])]
    unnamed x20, local copies, waits for them, and re-layouts: 1.97 us -> 4.28 us
    ppermute x20, waiting for transfers between devices: 58.3 us -> 56.1 us  [rotated(): lax.ppermute(value, axis, [(i, (i + steps) % count) for i in range(count)])]
    pallas_call x25, Pallas kernels: 52 us -> 49.9 us  [run(): pl.pallas_call(with_token, in_specs=[IN_SMEM] + [IN_VMEM] * (len(operands...]
  transfers between devices with their start and end apart: 34 -> 34, of which waited for: 18 -> 18; matrix products, arithmetic and copies ran while one was open for 1% -> 1% of each run, Pallas kernels for 21% -> 20%
where the time goes in v14:
time: 196 us; the launch traced here: 195 us
  waiting for transfers between devices  83.6 us (43%)
  starting transfers between devices  50.7 us (26%)
  Pallas kernels  49.9 us (25%)
  local copies, waits for them, and re-layouts  5.59 us (3%)
  between operations  3.59 us (2%)
  other arithmetic  1.99 us (1%)
    ppermute x20, waiting for transfers between devices, rotated(): lax.ppermute(value, axis, [(i, (i + steps) % count) for i in range(count)])  56.1 us
    pallas_call x25, Pallas kernels, run(): pl.pallas_call(with_token, in_specs=[IN_SMEM] + [IN_VMEM] * (len(operands...  49.9 us
    ppermute x20, starting transfers between devices, rotated(): lax.ppermute(value, axis, [(i, (i + steps) % count) for i in range(count)])  28.6 us
    ppermute x10, waiting for transfers between devices, swapped(): return lax.ppermute(value, axis, [(i, i ^ bit) for i in range(count)])  17 us
    ppermute x1, waiting for transfers between devices, on_device(): got_out = lax.ppermute(out_share, 'sec', [(1, 0)])  10.5 us
    ppermute x2, starting transfers between devices, on_device(): crossed = lax.ppermute(leave, 'sec', [(0, 1)])  9.93 us
    ppermute x10, starting transfers between devices, swapped(): return lax.ppermute(value, axis, [(i, i ^ bit) for i in range(count)])  8.32 us
    unnamed x20, local copies, waits for them, and re-layouts  4.28 us
  transfers between devices with their start and end apart: 34, of which 18 were waited for; matrix products, arithmetic and copies ran while one was open for 1% of the time, Pallas kernels for 20%

profile of v14, /device:TPU:0, one launch (start us, length us, event | category | flops | bytes accessed | tf_op | source)
XLA Modules:
  0.0 195.5 jit_solution(9025248936728961604)
XLA Ops:
  0.6 3.1 %collective-permute-start = (bf16[128,1280]{1,0:T(8,128)(2,1)}, bf16[128,1280]{1,0:T(8,128)(2,1)S(1)}, u32[]{:S(2)}, u32[]{:S(2)}) collective-permute-start(bf16[128,1280]{1,0:T(8,128)(2,1)} %bitcast.30), channel_id=1, source_target_pairs={{0,1},{1,2},{2,3},{3,0},{4,5},{5,6},{6,7},{7,4},{8,9},{9,10},{10,1... | collective-permute-start | bytes 983048 | tf_op jit(solution)/shard_map/ppermute | solution.py:21
  3.7 2.1 %collective-permute-start.1 = (bf16[128,1280]{1,0:T(8,128)(2,1)}, bf16[128,1280]{1,0:T(8,128)(2,1)S(1)}, u32[]{:S(2)}, u32[]{:S(2)}) collective-permute-start(bf16[128,1280]{1,0:T(8,128)(2,1)} %bitcast.31), channel_id=1, source_target_pairs={{0,3},{1,0},{2,1},{3,2},{4,7},{5,4},{6,5},{7,6},{8,11},{9,8},{10,9... | collective-permute-start | bytes 983048 | tf_op jit(solution)/shard_map/ppermute | solution.py:21
  5.9 1.9 copy-done.1
  7.8 1.1 share.3
  9.0 1.7 collective-permute-start.3
  14.9 5.3 %collective-permute-done.1.refs_3_.refs_2_.refs_4_ = bf16[128,1280]{1,0:T(8,128)(2,1)S(1)} collective-permute-done((bf16[128,1280]{1,0:T(8,128)(2,1)}, bf16[128,1280]{1,0:T(8,128)(2,1)S(1)}, u32[]{:S(2)}, u32[]{:S(2)}) %collective-permute-start.1) | collective-permute-done | bytes 327712 | tf_op jit(solution)/shard_map/ppermute | solution.py:21
  20.1 1.3 relay.2
  21.4 1.3 collective-permute-start.2
  22.7 6.0 %collective-permute-done.3.refs_1_ = bf16[320,1280]{1,0:T(8,128)(2,1)S(1)} collective-permute-done((bf16[320,1280]{1,0:T(8,128)(2,1)S(1)}, bf16[320,1280]{1,0:T(8,128)(2,1)S(1)}, u32[]{:S(2)}, u32[]{:S(2)}) %collective-permute-start.3) | collective-permute-done | bytes 819232 | tf_op jit(solution)/shard_map/ppermute | solution.py:26
  29.3 1.3 copy-done.2
  30.6 1.0 copy-done.4
  31.6 3.0 %block0_partial.2 = (bf16[2,64,1280]{2,1,0:T(8,128)(2,1)S(1)}, bf16[2,64,1280]{2,1,0:T(8,128)(2,1)S(1)}, f32[8,128]{1,0:T(8,128)S(1)}) custom-call(s32[4]{0:T(128)S(1)} %pad_add_fusion.refs_0_, bf16[128,1280]{1,0:T(8,128)(2,1)S(1)} %collective-permute-done.refs_2_.refs_1_, bf16[128,1280]{1,0:T(8,128)(2,1)S(1)} %collective-permute-done.1.refs_3_.refs_2_.refs_4_, ...), custom_call_target="tpu_custom_call" | custom-call | flops 99999997952 | bytes 500000000 | tf_op jit(solution)/shard_map/block0_partial/pallas_call | solution.py:74
  34.6 3.4 %collective-permute-start.5 = (bf16[2,64,1280]{2,1,0:T(8,128)(2,1)S(1)}, bf16[2,64,1280]{2,1,0:T(8,128)(2,1)S(1)}, u32[]{:S(2)}, u32[]{:S(2)}) collective-permute-start(bf16[2,64,1280]{2,1,0:T(8,128)(2,1)S(1)} %get-tuple-element.65), channel_id=1, source_target_pairs={{0,16},{1,17},{2,18},{3,19},{4,20},{5,21},{6,22},{7,23},{8,24},{9,... | collective-permute-start | bytes 983048 | tf_op jit(solution)/shard_map/ppermute | solution.py:553
  38.0 1.6 collective-permute-start.6
  39.6 1.8 share.4
  41.4 1.3 collective-permute-start.11
  42.7 4.1 %block0_partial.3 = (bf16[2,64,1280]{2,1,0:T(8,128)(2,1)S(1)}, bf16[2,64,1280]{2,1,0:T(8,128)(2,1)}, f32[8,128]{1,0:T(8,128)S(1)}) custom-call(s32[4]{0:T(128)S(1)} %pad_add_fusion.refs_0_, bf16[128,1280]{1,0:T(8,128)(2,1)S(1)} %bitcast.33, bf16[128,1280]{1,0:T(8,128)(2,1)} %collective-permute-done.2.refs_2_.refs_3_, ...), custom_call_target="tpu_custom_call" | custom-call | flops 1 | tf_op jit(solution)/shard_map/block0_partial/pallas_call | solution.py:74
  46.8 6.5 %collective-permute-start.4 = (bf16[2,64,1280]{2,1,0:T(8,128)(2,1)}, bf16[2,64,1280]{2,1,0:T(8,128)(2,1)}, u32[]{:S(2)}, u32[]{:S(2)}) collective-permute-start(bf16[2,64,1280]{2,1,0:T(8,128)(2,1)} %get-tuple-element.63), channel_id=1, source_target_pairs={{0,16},{1,17},{2,18},{3,19},{4,20},{5,21},{6,22},{7,23},{8,24},{9,... | collective-permute-start | bytes 983048 | tf_op jit(solution)/shard_map/ppermute | solution.py:553
  53.3 3.1 %collective-permute-done.6.refs_3_.refs_2_ = bf16[320,1280]{1,0:T(8,128)(2,1)S(1)} collective-permute-done((bf16[320,1280]{1,0:T(8,128)(2,1)S(1)}, bf16[320,1280]{1,0:T(8,128)(2,1)S(1)}, u32[]{:S(2)}, u32[]{:S(2)}) %collective-permute-start.6) | collective-permute-done | bytes 819232 | tf_op jit(solution)/shard_map/ppermute | solution.py:26
  56.4 1.1 pick.2
  57.6 1.6 collective-permute-start.7
  59.6 1.1 stack.23
  60.7 3.4 %collective-permute-done.7.refs_3_ = bf16[64,1280]{1,0:T(8,128)(2,1)S(1)} collective-permute-done((bf16[64,1280]{1,0:T(8,128)(2,1)S(1)}, bf16[64,1280]{1,0:T(8,128)(2,1)S(1)}, u32[]{:S(2)}, u32[]{:S(2)}) %collective-permute-start.7) | collective-permute-done | bytes 163872 | tf_op jit(solution)/shard_map/ppermute | solution.py:21
  64.1 2.1 %collective-permute-done.8.refs_4_ = bf16[64,1280]{1,0:T(8,128)(2,1)S(1)} collective-permute-done((bf16[64,1280]{1,0:T(8,128)(2,1)S(1)}, bf16[64,1280]{1,0:T(8,128)(2,1)S(1)}, u32[]{:S(2)}, u32[]{:S(2)}) %collective-permute-start.8) | collective-permute-done | bytes 163872 | tf_op jit(solution)/shard_map/ppermute | solution.py:21
  66.2 1.7 pick.3
  68.7 10.5 %collective-permute-done.11.refs_1_ = bf16[640,1280]{1,0:T(8,128)(2,1)} collective-permute-done((bf16[640,1280]{1,0:T(8,128)(2,1)}, bf16[640,1280]{1,0:T(8,128)(2,1)}, u32[]{:S(2)}, u32[]{:S(2)}) %collective-permute-start.11) | collective-permute-done | bytes 1638432 | tf_op jit(solution)/shard_map/ppermute | solution.py:540
  79.2 1.5 stack.24
  80.9 1.6 denoise.1
  82.5 2.1 %collective-permute-start.13 = (bf16[64,1280]{1,0:T(8,128)(2,1)S(1)}, bf16[64,1280]{1,0:T(8,128)(2,1)S(1)}, u32[]{:S(2)}, u32[]{:S(2)}) collective-permute-start(bf16[64,1280]{1,0:T(8,128)(2,1)S(1)} %get-tuple-element.76.refs_1_), channel_id=1, source_target_pairs={{0,2},{1,3},{2,0},{3,1},{4,6},{5,7},{6,4},{7,5},{8,10},{9,11},{10,... | collective-permute-start | bytes 491528 | tf_op jit(solution)/shard_map/ppermute | solution.py:21
  84.6 1.7 collective-permute-start.14
  86.3 1.7 assemble.4
  87.9 3.4 %collective-permute-done.12.refs_2_ = bf16[64,1280]{1,0:T(8,128)(2,1)S(1)} collective-permute-done((bf16[64,1280]{1,0:T(8,128)(2,1)S(1)}, bf16[64,1280]{1,0:T(8,128)(2,1)S(1)}, u32[]{:S(2)}, u32[]{:S(2)}) %collective-permute-start.12) | collective-permute-done | bytes 163872 | tf_op jit(solution)/shard_map/ppermute | solution.py:21
  91.4 6.1 %collective-permute-done.13.refs_3_ = bf16[64,1280]{1,0:T(8,128)(2,1)S(1)} collective-permute-done((bf16[64,1280]{1,0:T(8,128)(2,1)S(1)}, bf16[64,1280]{1,0:T(8,128)(2,1)S(1)}, u32[]{:S(2)}, u32[]{:S(2)}) %collective-permute-start.13) | collective-permute-done | bytes 163872 | tf_op jit(solution)/shard_map/ppermute | solution.py:21
  97.5 3.7 %reward_forward.1 = (bf16[64,1280]{1,0:T(8,128)(2,1)S(1)}, bf16[64,1280]{1,0:T(8,128)(2,1)S(1)}, bf16[64,1280]{1,0:T(8,128)(2,1)S(1)}, bf16[64,1280]{1,0:T(8,128...) custom-call(s32[4]{0:T(128)S(1)} %pad_add_fusion.refs_0_, bf16[64,1280]{1,0:T(8,128)(2,1)S(1)} %get-tuple-element.76.refs_1_, ...), custom_call_target="tpu_custom_call" | custom-call | flops 99999997952 | bytes 500000000 | tf_op jit(solution)/shard_map/reward_forward/pallas_call | solution.py:74
  101.2 3.6 %collective-permute-start.16 = (f32[8,1280]{1,0:T(8,128)S(1)}, f32[8,1280]{1,0:T(8,128)S(1)}, u32[]{:S(2)}, u32[]{:S(2)}) collective-permute-start(f32[8,1280]{1,0:T(8,128)S(1)} %get-tuple-element.80.refs_1_), channel_id=1, source_target_pairs={{0,1},{1,2},{2,3},{3,0},{4,5},{5,6},{6,7},{7,4},{8,9},{9,10},{10,1... | collective-permute-start | bytes 122888 | tf_op jit(solution)/shard_map/ppermute | solution.py:21
  105.4 1.8 collective-permute-start.18
  107.2 1.9 share.5
  109.1 2.6 %collective-permute-start.28 = (bf16[640,1280]{1,0:T(8,128)(2,1)}, bf16[640,1280]{1,0:T(8,128)(2,1)}, u32[]{:S(2)}, u32[]{:S(2)}) collective-permute-start(bf16[640,1280]{1,0:T(8,128)(2,1)} %get-tuple-element.98), channel_id=1, source_target_pairs={{0,16},{1,17},{2,18},{3,19},{4,20},{5,21},{6,22},{7,23},{8,24},{9,... | collective-permute-start | bytes 4915208 | tf_op jit(solution)/shard_map/ppermute | solution.py:569
  111.7 3.6 %reward_back.1 = (bf16[64,1280]{1,0:T(8,128)(2,1)S(1)}, bf16[64,1280]{1,0:T(8,128)(2,1)S(1)}, bf16[64,1280]{1,0:T(8,128)(2,1)S(1)}, bf16[64,1280]{1,0:T(8,128)(2...) custom-call(s32[4]{0:T(128)S(1)} %pad_add_fusion.refs_0_, f32[8,1280]{1,0:T(8,128)S(1)} %get-tuple-element.80.refs_1_, ...), custom_call_target="tpu_custom_call" | custom-call | flops 99999997952 | bytes 500000000 | tf_op jit(solution)/shard_map/reward_back/pallas_call | solution.py:74
  115.3 2.0 %collective-permute-start.19 = (bf16[64,1280]{1,0:T(8,128)(2,1)S(1)}, bf16[64,1280]{1,0:T(8,128)(2,1)S(1)}, u32[]{:S(2)}, u32[]{:S(2)}) collective-permute-start(bf16[64,1280]{1,0:T(8,128)(2,1)S(1)} %get-tuple-element.87), channel_id=1, source_target_pairs={{0,3},{1,0},{2,1},{3,2},{4,7},{5,4},{6,5},{7,6},{8,11},{9,8},{10,9... | collective-permute-start | bytes 491528 | tf_op jit(solution)/shard_map/ppermute | solution.py:21
  117.9 4.3 %block0_state.1 = (bf16[512,1280]{1,0:T(8,128)(2,1)S(1)}, bf16[512,1280]{1,0:T(8,128)(2,1)S(1)}, bf16[640,512]{1,0:T(8,128)(2,1)S(1)}, f32[8,128]{1,0:T(8,128)S(1)}) custom-call(s32[4]{0:T(128)S(1)} %pad_add_fusion.refs_0_, bf16[128,1280]{1,0:T(8,128)(2,1)S(1)} %bitcast.35, bf16[128,1280]{1,0:T(8,128)(2,1)S(1)} %collective-permute-done.refs_2_.refs_1_, ...), custom_call_target="tpu_custom_call" | custom-call | flops 99999997952 | bytes 500000000 | tf_op jit(solution)/shard_map/block0_state/pallas_call | solution.py:74
  122.2 8.6 %collective-permute-done.20.refs_7_ = bf16[64,1280]{1,0:T(8,128)(2,1)S(1)} collective-permute-done((bf16[64,1280]{1,0:T(8,128)(2,1)S(1)}, bf16[64,1280]{1,0:T(8,128)(2,1)S(1)}, u32[]{:S(2)}, u32[]{:S(2)}) %collective-permute-start.20) | collective-permute-done | bytes 163872 | tf_op jit(solution)/shard_map/ppermute | solution.py:21
  130.8 1.4 eps_gradient.1
  132.2 3.8 %collective-permute-start.24 = (bf16[64,1280]{1,0:T(8,128)(2,1)S(1)}, bf16[64,1280]{1,0:T(8,128)(2,1)S(1)}, u32[]{:S(2)}, u32[]{:S(2)}) collective-permute-start(bf16[64,1280]{1,0:T(8,128)(2,1)S(1)} %get-tuple-element.91.refs_1_), channel_id=1, source_target_pairs={{0,3},{1,0},{2,1},{3,2},{4,7},{5,4},{6,5},{7,6},{8,11},{9,8},{10,9... | collective-permute-start | bytes 491528 | tf_op jit(solution)/shard_map/ppermute | solution.py:21
  136.0 4.8 %collective-permute-done.22.refs_1_.refs_2_ = bf16[64,1280]{1,0:T(8,128)(2,1)S(1)} collective-permute-done((bf16[64,1280]{1,0:T(8,128)(2,1)S(1)}, bf16[64,1280]{1,0:T(8,128)(2,1)S(1)}, u32[]{:S(2)}, u32[]{:S(2)}) %collective-permute-start.22) | collective-permute-done | bytes 163872 | tf_op jit(solution)/shard_map/ppermute | solution.py:21
  141.3 1.1 join.2
  142.4 1.8 collective-permute-start.23
  144.2 2.0 %collective-permute-start.25 = (bf16[64,1280]{1,0:T(8,128)(2,1)S(1)}, bf16[64,1280]{1,0:T(8,128)(2,1)S(1)}, u32[]{:S(2)}, u32[]{:S(2)}) collective-permute-start(bf16[64,1280]{1,0:T(8,128)(2,1)S(1)} %get-tuple-element.91.refs_1_), channel_id=1, source_target_pairs={{0,16},{16,0},{1,17},{17,1},{2,18},{18,2},{3,19},{19,3},{4,20},{20... | collective-permute-start | bytes 491528 | tf_op jit(solution)/shard_map/ppermute | solution.py:26
  146.2 5.7 %collective-permute-done.23.refs_1_.refs_3_ = bf16[64,1280]{1,0:T(8,128)(2,1)S(1)} collective-permute-done((bf16[64,1280]{1,0:T(8,128)(2,1)S(1)}, bf16[64,1280]{1,0:T(8,128)(2,1)S(1)}, u32[]{:S(2)}, u32[]{:S(2)}) %collective-permute-start.23) | collective-permute-done | bytes 163872 | tf_op jit(solution)/shard_map/ppermute | solution.py:21
  152.5 3.2 %collective-permute-done.25.refs_2_.refs_5_ = bf16[64,1280]{1,0:T(8,128)(2,1)S(1)} collective-permute-done((bf16[64,1280]{1,0:T(8,128)(2,1)S(1)}, bf16[64,1280]{1,0:T(8,128)(2,1)S(1)}, u32[]{:S(2)}, u32[]{:S(2)}) %collective-permute-start.25) | collective-permute-done | bytes 163872 | tf_op jit(solution)/shard_map/ppermute | solution.py:26
  155.8 2.0 %stack.25 = (bf16[1,640,1280]{2,1,0:T(8,128)(2,1)S(1)}, f32[8,128]{1,0:T(8,128)}) custom-call(s32[4]{0:T(128)S(1)} %pad_add_fusion.refs_0_, bf16[640,1280]{1,0:T(8,128)(2,1)} %collective-permute-done.28.refs_1_, bf16[64,1280]{1,0:T(8,128)(2,1)S(1)} %collective-permute-done.25.refs_2_.refs_5_, bf16[128,1280]{1,0:T(8,128)(2,1)S(1)} %collective-permute-done.26.refs_3_.refs_6_, ...), custom_call_target="tpu_custom_call" | custom-call | flops 1 | tf_op jit(solution)/shard_map/stack/pallas_call | solution.py:74
  157.8 2.5 %collective-permute-start.27 = (bf16[64,1280]{1,0:T(8,128)(2,1)S(1)}, bf16[64,1280]{1,0:T(8,128)(2,1)S(1)}, u32[]{:S(2)}, u32[]{:S(2)}) collective-permute-start(bf16[64,1280]{1,0:T(8,128)(2,1)S(1)} %get-tuple-element.93), channel_id=1, source_target_pairs={{0,16},{16,0},{1,17},{17,1},{2,18},{18,2},{3,19},{19,3},{4,20},{20... | collective-permute-start | bytes 491528 | tf_op jit(solution)/shard_map/ppermute | solution.py:26
  160.3 1.0 collective-permute-done.29.refs_2_
  161.3 2.0 %assemble.5 = (bf16[1280,1280]{1,0:T(8,128)(2,1)S(1)}, f32[8,128]{1,0:T(8,128)}) custom-call(s32[4]{0:T(128)S(1)} %pad_add_fusion.refs_0_, bf16[640,1280]{1,0:T(8,128)(2,1)} %collective-permute-done.28.refs_1_, bf16[1,640,1280]{2,1,0:T(8,128)(2,1)S(1)} %collective-permute-done.29.refs_2_), custom_call_target="tpu_custom_call" | custom-call | flops 1 | tf_op jit(solution)/shard_map/assemble/pallas_call | solution.py:74
  163.3 1.8 collective-permute-done.27.refs_7_
  165.1 5.6 %gradients.1 = (bf16[2,160,1280]{2,1,0:T(8,128)(2,1)S(1)}, bf16[2,160,1280]{2,1,0:T(8,128)(2,1)S(1)}, bf16[2,160,1280]{2,1,0:T(8,128)(2,1)S(1)}, bf16[2,160,1280]{2,1,0:T(8,128)(2,1)S(1)}, f32[8,128]{1,0:T(8,128)}) custom-call(s32[4]{0:T(128)S(1)} %pad_add_fusion.refs_0_, bf16[64,1280]{1,0:T(8,128)(2,1)S(1)} %get-tuple-element.91.refs_1_, ...), custom_call_target="tpu_custom_call" | custom-call | flops 99999997952 | bytes 500000000 | tf_op jit(solution)/shard_map/gradients/pallas_call | solution.py:74
  171.3 1.8 collective-permute-done.30.refs_2_
  173.1 1.1 chip_sum.2
  174.8 1.1 chip_sum.3
  175.9 1.5 collective-permute-start.33
  177.4 9.1 %collective-permute-done.31 = bf16[160,1280]{1,0:T(8,128)(2,1)S(1)} collective-permute-done((bf16[160,1280]{1,0:T(8,128)(2,1)S(1)}, bf16[160,1280]{1,0:T(8,128)(2,1)S(1)}, u32[]{:S(2)}, u32[]{:S(2)}) %collective-permute-start.31) | collective-permute-done | bytes 409632 | tf_op jit(solution)/shard_map/ppermute | solution.py:21
  186.5 1.0 convert_add_fusion.1
  187.5 7.0 %collective-permute-done.33 = bf16[160,1280]{1,0:T(8,128)(2,1)S(1)} collective-permute-done((bf16[160,1280]{1,0:T(8,128)(2,1)S(1)}, bf16[160,1280]{1,0:T(8,128)(2,1)S(1)}, u32[]{:S(2)}, u32[]{:S(2)}) %collective-permute-start.33) | collective-permute-done | bytes 409632 | tf_op jit(solution)/shard_map/ppermute | solution.py:21
  194.5 1.0 convert_add_fusion
  (59 shorter events, 6.7 us)
Async XLA Ops:
  0.6 14.1 %copy-start = (bf16[64,1280]{1,0:T(8,128)(2,1)S(1)}, bf16[64,1280]{1,0:T(8,128)(2,1)}, u32[]{:S(2)}) copy-start(bf16[64,1280]{1,0:T(8,128)(2,1)} %param.10) | copy-start | bytes 491524
  0.6 14.2 %collective-permute-start = (bf16[128,1280]{1,0:T(8,128)(2,1)}, bf16[128,1280]{1,0:T(8,128)(2,1)S(1)}, u32[]{:S(2)}, u32[]{:S(2)}) collective-permute-start(bf16[128,1280]{1,0:T(8,128)(2,1)} %bitcast.30), channel_id=1, source_target_pairs={{0,1},{1,2},{2,3},{3,0},{4,5},{5,6},{6,7},{7,4},{8,9},{9,10},{10,1... | collective-permute-start | bytes 983048 | tf_op jit(solution)/shard_map/ppermute | solution.py:21
  3.7 16.4 %collective-permute-start.1 = (bf16[128,1280]{1,0:T(8,128)(2,1)}, bf16[128,1280]{1,0:T(8,128)(2,1)S(1)}, u32[]{:S(2)}, u32[]{:S(2)}) collective-permute-start(bf16[128,1280]{1,0:T(8,128)(2,1)} %bitcast.31), channel_id=1, source_target_pairs={{0,3},{1,0},{2,1},{3,2},{4,7},{5,4},{6,5},{7,6},{8,11},{9,8},{10,9... | collective-permute-start | bytes 983048 | tf_op jit(solution)/shard_map/ppermute | solution.py:21
  5.9 1.9 copy-start.1
  7.8 2.8 %copy-start.8 = (s32[2]{0:T(128)S(1)}, s32[2]{0:T(128)}, u32[]{:S(2)}) copy-start(s32[2]{0:T(128)} %param.8) | copy-start | bytes 28
  7.8 4.9 %copy-start.7 = (f32[2,1280]{1,0:T(2,128)S(1)}, f32[2,1280]{1,0:T(2,128)}, u32[]{:S(2)}) copy-start(f32[2,1280]{1,0:T(2,128)} %param.11) | copy-start | bytes 30724
  7.8 5.0 %copy-start.9 = (s32[2]{0:T(128)S(1)}, s32[2]{0:T(128)}, u32[]{:S(2)}) copy-start(s32[2]{0:T(128)} %param.9) | copy-start | bytes 28
  7.8 12.3 %copy-start.6 = (bf16[2,64,1280]{2,1,0:T(8,128)(2,1)S(1)}, bf16[2,64,1280]{2,1,0:T(8,128)(2,1)}, u32[]{:S(2)}) copy-start(bf16[2,64,1280]{2,1,0:T(8,128)(2,1)} %param.7) | copy-start | bytes 983044
  9.0 19.7 %collective-permute-start.3 = (bf16[320,1280]{1,0:T(8,128)(2,1)S(1)}, bf16[320,1280]{1,0:T(8,128)(2,1)S(1)}, u32[]{:S(2)}, u32[]{:S(2)}) collective-permute-start(bf16[320,1280]{1,0:T(8,128)(2,1)S(1)} %get-tuple-element.57), channel_id=1, source_target_pairs={{0,16},{16,0},{1,17},{17,1},{2,18},{18,2},{3,19},{19,3},{4,20},{20... | collective-permute-start | bytes 2457608 | tf_op jit(solution)/shard_map/ppermute | solution.py:26
  21.4 21.3 %collective-permute-start.2 = (bf16[128,1280]{1,0:T(8,128)(2,1)}, bf16[128,1280]{1,0:T(8,128)(2,1)}, u32[]{:S(2)}, u32[]{:S(2)}) collective-permute-start(bf16[128,1280]{1,0:T(8,128)(2,1)} %get-tuple-element.56), channel_id=1, source_target_pairs={{0,2},{1,3},{2,0},{3,1},{4,6},{5,7},{6,4},{7,5},{8,10},{9,11},{10,... | collective-permute-start | bytes 983048 | tf_op jit(solution)/shard_map/ppermute | solution.py:21
  28.7 1.9 copy-start.2
  28.7 2.9 %copy-start.4 = (bf16[1,1280,1280]{2,1,0:T(8,128)(2,1)S(1)}, bf16[1,1280,1280]{2,1,0:T(8,128)(2,1)}, u32[]{:S(2)}) copy-start(bf16[1,1280,1280]{2,1,0:T(8,128)(2,1)} %param.13) | copy-start | bytes 9830404
  34.6 18.7 %collective-permute-start.5 = (bf16[2,64,1280]{2,1,0:T(8,128)(2,1)S(1)}, bf16[2,64,1280]{2,1,0:T(8,128)(2,1)S(1)}, u32[]{:S(2)}, u32[]{:S(2)}) collective-permute-start(bf16[2,64,1280]{2,1,0:T(8,128)(2,1)S(1)} %get-tuple-element.65), channel_id=1, source_target_pairs={{0,16},{1,17},{2,18},{3,19},{4,20},{5,21},{6,22},{7,23},{8,24},{9,... | collective-permute-start | bytes 983048 | tf_op jit(solution)/shard_map/ppermute | solution.py:553
  38.0 18.4 %collective-permute-start.6 = (bf16[320,1280]{1,0:T(8,128)(2,1)S(1)}, bf16[320,1280]{1,0:T(8,128)(2,1)S(1)}, u32[]{:S(2)}, u32[]{:S(2)}) collective-permute-start(bf16[320,1280]{1,0:T(8,128)(2,1)S(1)} %get-tuple-element.66), channel_id=1, source_target_pairs={{0,8},{4,12},{8,0},{12,4},{1,9},{5,13},{9,1},{13,5},{2,10},{6,14},... | collective-permute-start | bytes 2457608 | tf_op jit(solution)/shard_map/ppermute | solution.py:26
  41.4 37.8 %collective-permute-start.11 = (bf16[640,1280]{1,0:T(8,128)(2,1)}, bf16[640,1280]{1,0:T(8,128)(2,1)}, u32[]{:S(2)}, u32[]{:S(2)}) collective-permute-start(bf16[640,1280]{1,0:T(8,128)(2,1)} %get-tuple-element.74), channel_id=1, source_target_pairs={{16,0},{17,1},{18,2},{19,3},{20,4},{21,5},{22,6},{23,7},{24,8},{25... | collective-permute-start | bytes 4915208 | tf_op jit(solution)/shard_map/ppermute | solution.py:540
  46.8 13.9 %collective-permute-start.4 = (bf16[2,64,1280]{2,1,0:T(8,128)(2,1)}, bf16[2,64,1280]{2,1,0:T(8,128)(2,1)}, u32[]{:S(2)}, u32[]{:S(2)}) collective-permute-start(bf16[2,64,1280]{2,1,0:T(8,128)(2,1)} %get-tuple-element.63), channel_id=1, source_target_pairs={{0,16},{1,17},{2,18},{3,19},{4,20},{5,21},{6,22},{7,23},{8,24},{9,... | collective-permute-start | bytes 983048 | tf_op jit(solution)/shard_map/ppermute | solution.py:553
  57.6 6.5 %collective-permute-start.7 = (bf16[64,1280]{1,0:T(8,128)(2,1)S(1)}, bf16[64,1280]{1,0:T(8,128)(2,1)S(1)}, u32[]{:S(2)}, u32[]{:S(2)}) collective-permute-start(bf16[64,1280]{1,0:T(8,128)(2,1)S(1)} %get-tuple-element.67), channel_id=1, source_target_pairs={{0,3},{1,0},{2,1},{3,2},{4,7},{5,4},{6,5},{7,6},{8,11},{9,8},{10,9... | collective-permute-start | bytes 491528 | tf_op jit(solution)/shard_map/ppermute | solution.py:21
  59.1 7.1 %collective-permute-start.8 = (bf16[64,1280]{1,0:T(8,128)(2,1)S(1)}, bf16[64,1280]{1,0:T(8,128)(2,1)S(1)}, u32[]{:S(2)}, u32[]{:S(2)}) collective-permute-start(bf16[64,1280]{1,0:T(8,128)(2,1)S(1)} %get-tuple-element.68), channel_id=1, source_target_pairs={{0,1},{1,2},{2,3},{3,0},{4,5},{5,6},{6,7},{7,4},{8,9},{9,10},{10,1... | collective-permute-start | bytes 491528 | tf_op jit(solution)/shard_map/ppermute | solution.py:21
  60.7 7.2 %collective-permute-start.10 = (bf16[2,320,1280]{2,1,0:T(8,128)(2,1)S(1)}, bf16[2,320,1280]{2,1,0:T(8,128)(2,1)S(1)}, u32[]{:S(2)}, u32[]{:S(2)}) collective-permute-start(bf16[2,320,1280]{2,1,0:T(8,128)(2,1)S(1)} %get-tuple-element.72), channel_id=1, source_target_pairs={{0,4},{4,0},{8,12},{12,8},{1,5},{5,1},{9,13},{13,9},{2,6},{6,2},{1... | collective-permute-start | bytes 4915208 | tf_op jit(solution)/shard_map/ppermute | solution.py:26
  67.9 13.0 %collective-permute-start.9 = (bf16[64,1280]{1,0:T(8,128)(2,1)}, bf16[64,1280]{1,0:T(8,128)(2,1)}, u32[]{:S(2)}, u32[]{:S(2)}) collective-permute-start(bf16[64,1280]{1,0:T(8,128)(2,1)} %get-tuple-element.70), channel_id=1, source_target_pairs={{0,2},{1,3},{2,0},{3,1},{4,6},{5,7},{6,4},{7,5},{8,10},{9,11},{10,... | collective-permute-start | bytes 491528 | tf_op jit(solution)/shard_map/ppermute | solution.py:21
  80.8 5.5 %collective-permute-start.15 = (bf16[1,640,1280]{2,1,0:T(8,128)(2,1)S(1)}, bf16[1,640,1280]{2,1,0:T(8,128)(2,1)S(1)}, u32[]{:S(2)}, u32[]{:S(2)}) collective-permute-start(bf16[1,640,1280]{2,1,0:T(8,128)(2,1)S(1)} %get-tuple-element.78), channel_id=1, source_target_pairs={{0,4},{4,0},{8,12},{12,8},{1,5},{5,1},{9,13},{13,9},{2,6},{6,2},{1... | collective-permute-start | bytes 4915208 | tf_op jit(solution)/shard_map/ppermute | solution.py:26
  82.4 15.0 %copy-start.3 = (bf16[1,1280,1280]{2,1,0:T(8,128)(2,1)S(1)}, bf16[1,1280,1280]{2,1,0:T(8,128)(2,1)}, u32[]{:S(2)}) copy-start(bf16[1,1280,1280]{2,1,0:T(8,128)(2,1)} %param.12) | copy-start | bytes 9830404
  82.4 15.0 %copy-start.5 = (bf16[1,1280,1280]{2,1,0:T(8,128)(2,1)S(1)}, bf16[1,1280,1280]{2,1,0:T(8,128)(2,1)}, u32[]{:S(2)}) copy-start(bf16[1,1280,1280]{2,1,0:T(8,128)(2,1)} %param.13) | copy-start | bytes 9830404
  82.4 8.9 %collective-permute-start.12 = (bf16[64,1280]{1,0:T(8,128)(2,1)S(1)}, bf16[64,1280]{1,0:T(8,128)(2,1)S(1)}, u32[]{:S(2)}, u32[]{:S(2)}) collective-permute-start(bf16[64,1280]{1,0:T(8,128)(2,1)S(1)} %get-tuple-element.76.refs_1_), channel_id=1, source_target_pairs={{0,1},{1,2},{2,3},{3,0},{4,5},{5,6},{6,7},{7,4},{8,9},{9,10},{10,1... | collective-permute-start | bytes 491528 | tf_op jit(solution)/shard_map/ppermute | solution.py:21
  82.5 15.0 %collective-permute-start.13 = (bf16[64,1280]{1,0:T(8,128)(2,1)S(1)}, bf16[64,1280]{1,0:T(8,128)(2,1)S(1)}, u32[]{:S(2)}, u32[]{:S(2)}) collective-permute-start(bf16[64,1280]{1,0:T(8,128)(2,1)S(1)} %get-tuple-element.76.refs_1_), channel_id=1, source_target_pairs={{0,2},{1,3},{2,0},{3,1},{4,6},{5,7},{6,4},{7,5},{8,10},{9,11},{10,... | collective-permute-start | bytes 491528 | tf_op jit(solution)/shard_map/ppermute | solution.py:21
  84.6 12.9 %collective-permute-start.14 = (bf16[64,1280]{1,0:T(8,128)(2,1)S(1)}, bf16[64,1280]{1,0:T(8,128)(2,1)S(1)}, u32[]{:S(2)}, u32[]{:S(2)}) collective-permute-start(bf16[64,1280]{1,0:T(8,128)(2,1)S(1)} %get-tuple-element.76.refs_1_), channel_id=1, source_target_pairs={{0,3},{1,0},{2,1},{3,2},{4,7},{5,4},{6,5},{7,6},{8,11},{9,8},{10,9... | collective-permute-start | bytes 491528 | tf_op jit(solution)/shard_map/ppermute | solution.py:21
  101.2 10.5 %collective-permute-start.16 = (f32[8,1280]{1,0:T(8,128)S(1)}, f32[8,1280]{1,0:T(8,128)S(1)}, u32[]{:S(2)}, u32[]{:S(2)}) collective-permute-start(f32[8,1280]{1,0:T(8,128)S(1)} %get-tuple-element.80.refs_1_), channel_id=1, source_target_pairs={{0,1},{1,2},{2,3},{3,0},{4,5},{5,6},{6,7},{7,4},{8,9},{9,10},{10,1... | collective-permute-start | bytes 122888 | tf_op jit(solution)/shard_map/ppermute | solution.py:21
  104.9 6.9 %collective-permute-start.17 = (f32[8,1280]{1,0:T(8,128)S(1)}, f32[8,1280]{1,0:T(8,128)S(1)}, u32[]{:S(2)}, u32[]{:S(2)}) collective-permute-start(f32[8,1280]{1,0:T(8,128)S(1)} %get-tuple-element.80.refs_1_), channel_id=1, source_target_pairs={{0,2},{1,3},{2,0},{3,1},{4,6},{5,7},{6,4},{7,5},{8,10},{9,11},{10,... | collective-permute-start | bytes 122888 | tf_op jit(solution)/shard_map/ppermute | solution.py:21
  105.4 6.3 %collective-permute-start.18 = (f32[8,1280]{1,0:T(8,128)S(1)}, f32[8,1280]{1,0:T(8,128)S(1)}, u32[]{:S(2)}, u32[]{:S(2)}) collective-permute-start(f32[8,1280]{1,0:T(8,128)S(1)} %get-tuple-element.80.refs_1_), channel_id=1, source_target_pairs={{0,3},{1,0},{2,1},{3,2},{4,7},{5,4},{6,5},{7,6},{8,11},{9,8},{10,9... | collective-permute-start | bytes 122888 | tf_op jit(solution)/shard_map/ppermute | solution.py:21
  109.1 46.6 %collective-permute-start.28 = (bf16[640,1280]{1,0:T(8,128)(2,1)}, bf16[640,1280]{1,0:T(8,128)(2,1)}, u32[]{:S(2)}, u32[]{:S(2)}) collective-permute-start(bf16[640,1280]{1,0:T(8,128)(2,1)} %get-tuple-element.98), channel_id=1, source_target_pairs={{0,16},{1,17},{2,18},{3,19},{4,20},{5,21},{6,22},{7,23},{8,24},{9,... | collective-permute-start | bytes 4915208 | tf_op jit(solution)/shard_map/ppermute | solution.py:569
  115.3 6.9 %collective-permute-start.19 = (bf16[64,1280]{1,0:T(8,128)(2,1)S(1)}, bf16[64,1280]{1,0:T(8,128)(2,1)S(1)}, u32[]{:S(2)}, u32[]{:S(2)}) collective-permute-start(bf16[64,1280]{1,0:T(8,128)(2,1)S(1)} %get-tuple-element.87), channel_id=1, source_target_pairs={{0,3},{1,0},{2,1},{3,2},{4,7},{5,4},{6,5},{7,6},{8,11},{9,8},{10,9... | collective-permute-start | bytes 491528 | tf_op jit(solution)/shard_map/ppermute | solution.py:21
  117.3 13.5 %collective-permute-start.20 = (bf16[64,1280]{1,0:T(8,128)(2,1)S(1)}, bf16[64,1280]{1,0:T(8,128)(2,1)S(1)}, u32[]{:S(2)}, u32[]{:S(2)}) collective-permute-start(bf16[64,1280]{1,0:T(8,128)(2,1)S(1)} %get-tuple-element.88), channel_id=1, source_target_pairs={{0,2},{1,3},{2,0},{3,1},{4,6},{5,7},{6,4},{7,5},{8,10},{9,11},{10,... | collective-permute-start | bytes 491528 | tf_op jit(solution)/shard_map/ppermute | solution.py:21
  117.3 13.5 %collective-permute-start.21 = (bf16[64,1280]{1,0:T(8,128)(2,1)S(1)}, bf16[64,1280]{1,0:T(8,128)(2,1)S(1)}, u32[]{:S(2)}, u32[]{:S(2)}) collective-permute-start(bf16[64,1280]{1,0:T(8,128)(2,1)S(1)} %get-tuple-element.89), channel_id=1, source_target_pairs={{0,1},{1,2},{2,3},{3,0},{4,5},{5,6},{6,7},{7,4},{8,9},{9,10},{10,1... | collective-permute-start | bytes 491528 | tf_op jit(solution)/shard_map/ppermute | solution.py:21
  132.2 8.6 %collective-permute-start.22 = (bf16[64,1280]{1,0:T(8,128)(2,1)S(1)}, bf16[64,1280]{1,0:T(8,128)(2,1)S(1)}, u32[]{:S(2)}, u32[]{:S(2)}) collective-permute-start(bf16[64,1280]{1,0:T(8,128)(2,1)S(1)} %get-tuple-element.91.refs_1_), channel_id=1, source_target_pairs={{0,1},{1,2},{2,3},{3,0},{4,5},{5,6},{6,7},{7,4},{8,9},{9,10},{10,1... | collective-permute-start | bytes 491528 | tf_op jit(solution)/shard_map/ppermute | solution.py:21
  132.2 9.1 %collective-permute-start.24 = (bf16[64,1280]{1,0:T(8,128)(2,1)S(1)}, bf16[64,1280]{1,0:T(8,128)(2,1)S(1)}, u32[]{:S(2)}, u32[]{:S(2)}) collective-permute-start(bf16[64,1280]{1,0:T(8,128)(2,1)S(1)} %get-tuple-element.91.refs_1_), channel_id=1, source_target_pairs={{0,3},{1,0},{2,1},{3,2},{4,7},{5,4},{6,5},{7,6},{8,11},{9,8},{10,9... | collective-permute-start | bytes 491528 | tf_op jit(solution)/shard_map/ppermute | solution.py:21
  142.4 13.3 %collective-permute-start.26 = (bf16[128,1280]{1,0:T(8,128)(2,1)S(1)}, bf16[128,1280]{1,0:T(8,128)(2,1)S(1)}, u32[]{:S(2)}, u32[]{:S(2)}) collective-permute-start(bf16[128,1280]{1,0:T(8,128)(2,1)S(1)} %get-tuple-element.92), channel_id=1, source_target_pairs={{0,16},{16,0},{1,17},{17,1},{2,18},{18,2},{3,19},{19,3},{4,20},{20... | collective-permute-start | bytes 983048 | tf_op jit(solution)/shard_map/ppermute | solution.py:26
  142.4 9.6 %collective-permute-start.23 = (bf16[64,1280]{1,0:T(8,128)(2,1)S(1)}, bf16[64,1280]{1,0:T(8,128)(2,1)S(1)}, u32[]{:S(2)}, u32[]{:S(2)}) collective-permute-start(bf16[64,1280]{1,0:T(8,128)(2,1)S(1)} %get-tuple-element.91.refs_1_), channel_id=1, source_target_pairs={{0,2},{1,3},{2,0},{3,1},{4,6},{5,7},{6,4},{7,5},{8,10},{9,11},{10,... | collective-permute-start | bytes 491528 | tf_op jit(solution)/shard_map/ppermute | solution.py:21
  144.2 11.5 %collective-permute-start.25 = (bf16[64,1280]{1,0:T(8,128)(2,1)S(1)}, bf16[64,1280]{1,0:T(8,128)(2,1)S(1)}, u32[]{:S(2)}, u32[]{:S(2)}) collective-permute-start(bf16[64,1280]{1,0:T(8,128)(2,1)S(1)} %get-tuple-element.91.refs_1_), channel_id=1, source_target_pairs={{0,16},{16,0},{1,17},{17,1},{2,18},{18,2},{3,19},{19,3},{4,20},{20... | collective-permute-start | bytes 491528 | tf_op jit(solution)/shard_map/ppermute | solution.py:26
  157.8 3.5 %collective-permute-start.29 = (bf16[1,640,1280]{2,1,0:T(8,128)(2,1)S(1)}, bf16[1,640,1280]{2,1,0:T(8,128)(2,1)S(1)}, u32[]{:S(2)}, u32[]{:S(2)}) collective-permute-start(bf16[1,640,1280]{2,1,0:T(8,128)(2,1)S(1)} %get-tuple-element.100), channel_id=1, source_target_pairs={{0,4},{4,0},{8,12},{12,8},{1,5},{5,1},{9,13},{13,9},{2,6},{6,2},{1... | collective-permute-start | bytes 4915208 | tf_op jit(solution)/shard_map/ppermute | solution.py:26
  157.8 7.4 %collective-permute-start.27 = (bf16[64,1280]{1,0:T(8,128)(2,1)S(1)}, bf16[64,1280]{1,0:T(8,128)(2,1)S(1)}, u32[]{:S(2)}, u32[]{:S(2)}) collective-permute-start(bf16[64,1280]{1,0:T(8,128)(2,1)S(1)} %get-tuple-element.93), channel_id=1, source_target_pairs={{0,16},{16,0},{1,17},{17,1},{2,18},{18,2},{3,19},{19,3},{4,20},{20... | collective-permute-start | bytes 491528 | tf_op jit(solution)/shard_map/ppermute | solution.py:26
  170.8 2.3 %collective-permute-start.30 = (bf16[2,160,1280]{2,1,0:T(8,128)(2,1)S(1)}, bf16[2,160,1280]{2,1,0:T(8,128)(2,1)S(1)}, u32[]{:S(2)}, u32[]{:S(2)}) collective-permute-start(bf16[2,160,1280]{2,1,0:T(8,128)(2,1)S(1)} %get-tuple-element.103), channel_id=1, source_target_pairs={{0,4},{4,0},{8,12},{12,8},{1,5},{5,1},{9,13},{13,9},{2,6},{6,2},{1... | collective-permute-start | bytes 2457608 | tf_op jit(solution)/shard_map/ppermute | solution.py:26
  170.8 4.0 %collective-permute-start.32 = (bf16[2,160,1280]{2,1,0:T(8,128)(2,1)S(1)}, bf16[2,160,1280]{2,1,0:T(8,128)(2,1)S(1)}, u32[]{:S(2)}, u32[]{:S(2)}) collective-permute-start(bf16[2,160,1280]{2,1,0:T(8,128)(2,1)S(1)} %get-tuple-element.107), channel_id=1, source_target_pairs={{0,4},{4,0},{8,12},{12,8},{1,5},{5,1},{9,13},{13,9},{2,6},{6,2},{1... | collective-permute-start | bytes 2457608 | tf_op jit(solution)/shard_map/ppermute | solution.py:26
  174.2 12.3 %collective-permute-start.31 = (bf16[160,1280]{1,0:T(8,128)(2,1)S(1)}, bf16[160,1280]{1,0:T(8,128)(2,1)S(1)}, u32[]{:S(2)}, u32[]{:S(2)}) collective-permute-start(bf16[160,1280]{1,0:T(8,128)(2,1)S(1)} %bitcast.36), channel_id=1, source_target_pairs={{0,8},{4,12},{8,0},{12,4},{1,9},{5,13},{9,1},{13,5},{2,10},{6,14},... | collective-permute-start | bytes 1228808 | tf_op jit(solution)/shard_map/ppermute | solution.py:21
  175.9 18.6 %collective-permute-start.33 = (bf16[160,1280]{1,0:T(8,128)(2,1)S(1)}, bf16[160,1280]{1,0:T(8,128)(2,1)S(1)}, u32[]{:S(2)}, u32[]{:S(2)}) collective-permute-start(bf16[160,1280]{1,0:T(8,128)(2,1)S(1)} %bitcast.37), channel_id=1, source_target_pairs={{0,8},{4,12},{8,0},{12,4},{1,9},{5,13},{9,1},{13,5},{2,10},{6,14},... | collective-permute-start | bytes 1228808 | tf_op jit(solution)/shard_map/ppermute | solution.py:21

commit v15 on v12

--- a/solution.py
+++ b/solution.py
@@ -565,7 +565,7 @@
     late_share, late_token = share(own[1], 2, sel, [joined_token])
     got_late = lax.ppermute(late_share, "sec", [(0, 1)])
     slopes1, pool = reward_forward(
-        seen_parts, tokens, gains[1:], text_mine, own, other, sel, ()
+        seen_parts, tokens, gains[1:], text_mine, own, other, sel, [late_token]
     )
     pools = gather_parts(pool)
     g_parts, g_mean = reward_back(pools, slopes1, tokens, own, other, sel)

time: 191 us -> 202 us (1.058)
  local copies, waits for them, and re-layouts: 5 us -> 16.6 us
  waiting for transfers between devices: 75 us -> 79 us
  starting transfers between devices: 49.1 us -> 46 us
    unnamed x46 -> x78, local copies, waits for them, and re-layouts: 3.69 us -> 15.4 us
    ppermute x20, waiting for transfers between devices: 62.9 us -> 66.5 us  [rotated(): lax.ppermute(value, axis, [(i, (i + steps) % count) for i in range(count)])]
  transfers between devices with their start and end apart: 34 -> 34, of which waited for: 19 -> 21; matrix products, arithmetic and copies ran while one was open for 1% -> 1% of each run, Pallas kernels for 22% -> 20%
where the time goes in v15:
time: 202 us; the launch traced here: 201 us
  waiting for transfers between devices  79 us (39%)
  Pallas kernels  53.8 us (27%)
  starting transfers between devices  46 us (23%)
  local copies, waits for them, and re-layouts  16.6 us (8%)
  between operations  3.76 us (2%)
    ppermute x20, waiting for transfers between devices, rotated(): lax.ppermute(value, axis, [(i, (i + steps) % count) for i in range(count)])  66.5 us
    pallas_call x25, Pallas kernels, run(): pl.pallas_call(with_token, in_specs=[IN_SMEM] + [IN_VMEM] * (len(operands...  53.8 us
    ppermute x20, starting transfers between devices, rotated(): lax.ppermute(value, axis, [(i, (i + steps) % count) for i in range(count)])  29.8 us
    unnamed x78, local copies, waits for them, and re-layouts  15.4 us
    ppermute x10, waiting for transfers between devices, swapped(): return lax.ppermute(value, axis, [(i, i ^ bit) for i in range(count)])  12.5 us
    ppermute x10, starting transfers between devices, swapped(): return lax.ppermute(value, axis, [(i, i ^ bit) for i in range(count)])  6.23 us
    ppermute x2, starting transfers between devices, on_device(): crossed = lax.ppermute(leave, 'sec', [(0, 1)])  6.05 us
  transfers between devices with their start and end apart: 34, of which 21 were waited for; matrix products, arithmetic and copies ran while one was open for 1% of the time, Pallas kernels for 20%

profile of v15, /device:TPU:0, one launch (start us, length us, event | category | flops | bytes accessed | tf_op | source)
XLA Modules:
  0.0 201.4 jit_solution(18418115220862814216)
XLA Ops:
  0.6 3.1 %collective-permute-start = (bf16[128,1280]{1,0:T(8,128)(2,1)}, bf16[128,1280]{1,0:T(8,128)(2,1)S(1)}, u32[]{:S(2)}, u32[]{:S(2)}) collective-permute-start(bf16[128,1280]{1,0:T(8,128)(2,1)} %bitcast.32), channel_id=1, source_target_pairs={{0,1},{1,2},{2,3},{3,0},{4,5},{5,6},{6,7},{7,4},{8,9},{9,10},{10,1... | collective-permute-start | bytes 983048 | tf_op jit(solution)/shard_map/ppermute | solution.py:21
  3.7 2.1 %collective-permute-start.1 = (bf16[128,1280]{1,0:T(8,128)(2,1)}, bf16[128,1280]{1,0:T(8,128)(2,1)S(1)}, u32[]{:S(2)}, u32[]{:S(2)}) collective-permute-start(bf16[128,1280]{1,0:T(8,128)(2,1)} %bitcast.33), channel_id=1, source_target_pairs={{0,3},{1,0},{2,1},{3,2},{4,7},{5,4},{6,5},{7,6},{8,11},{9,8},{10,9... | collective-permute-start | bytes 983048 | tf_op jit(solution)/shard_map/ppermute | solution.py:21
  5.9 1.9 copy-done.5
  7.8 1.5 share.3
  9.3 1.7 collective-permute-start.3
  13.1 1.5 collective-permute-done.refs_2_.refs_1_
  14.5 5.6 %collective-permute-done.1.refs_3_.refs_2_.refs_4_ = bf16[128,1280]{1,0:T(8,128)(2,1)S(1)} collective-permute-done((bf16[128,1280]{1,0:T(8,128)(2,1)}, bf16[128,1280]{1,0:T(8,128)(2,1)S(1)}, u32[]{:S(2)}, u32[]{:S(2)}) %collective-permute-start.1) | collective-permute-done | bytes 327712 | tf_op jit(solution)/shard_map/ppermute | solution.py:21
  20.1 1.3 relay.2
  21.4 1.3 collective-permute-start.2
  22.7 1.8 share.4
  24.6 1.5 collective-permute-start.14
  26.1 3.9 %collective-permute-done.3.refs_1_ = bf16[320,1280]{1,0:T(8,128)(2,1)} collective-permute-done((bf16[320,1280]{1,0:T(8,128)(2,1)}, bf16[320,1280]{1,0:T(8,128)(2,1)}, u32[]{:S(2)}, u32[]{:S(2)}) %collective-permute-start.3) | collective-permute-done | bytes 819232 | tf_op jit(solution)/shard_map/ppermute | solution.py:26
  30.0 2.1 %relay.3 = (bf16[320,1280]{1,0:T(8,128)(2,1)}, f32[8,128]{1,0:T(8,128)S(1)}) custom-call(s32[4]{0:T(128)S(1)} %pad_add_fusion.refs_0_, bf16[320,1280]{1,0:T(8,128)(2,1)} %collective-permute-done.3.refs_1_, f32[8,128]{1,0:T(8,128)S(1)} %get-tuple-element.58.refs_2_), custom_call_target="tpu_custom_call" | custom-call | flops 99999997952 | bytes 500000000 | tf_op jit(solution)/shard_map/relay/pallas_call | solution.py:74
  32.1 1.7 collective-permute-start.9
  33.9 3.0 %block0_partial.2 = (bf16[2,64,1280]{2,1,0:T(8,128)(2,1)S(1)}, bf16[2,64,1280]{2,1,0:T(8,128)(2,1)S(1)}, f32[8,128]{1,0:T(8,128)S(1)}) custom-call(s32[4]{0:T(128)S(1)} %pad_add_fusion.refs_0_, bf16[128,1280]{1,0:T(8,128)(2,1)S(1)} %collective-permute-done.refs_2_.refs_1_, bf16[128,1280]{1,0:T(8,128)(2,1)S(1)} %collective-permute-done.1.refs_3_.refs_2_.refs_4_, ...), custom_call_target="tpu_custom_call" | custom-call | flops 99999997952 | bytes 500000000 | tf_op jit(solution)/shard_map/block0_partial/pallas_call | solution.py:74
  36.8 2.5 %collective-permute-start.5 = (bf16[2,64,1280]{2,1,0:T(8,128)(2,1)S(1)}, bf16[2,64,1280]{2,1,0:T(8,128)(2,1)S(1)}, u32[]{:S(2)}, u32[]{:S(2)}) collective-permute-start(bf16[2,64,1280]{2,1,0:T(8,128)(2,1)S(1)} %get-tuple-element.65), channel_id=1, source_target_pairs={{0,16},{1,17},{2,18},{3,19},{4,20},{5,21},{6,22},{7,23},{8,24},{9,... | collective-permute-start | bytes 983048 | tf_op jit(solution)/shard_map/ppermute | solution.py:551
  39.4 4.1 %block0_partial.3 = (bf16[2,64,1280]{2,1,0:T(8,128)(2,1)S(1)}, bf16[2,64,1280]{2,1,0:T(8,128)(2,1)}, f32[8,128]{1,0:T(8,128)S(1)}) custom-call(s32[4]{0:T(128)S(1)} %pad_add_fusion.refs_0_, bf16[128,1280]{1,0:T(8,128)(2,1)S(1)} %bitcast.35, bf16[128,1280]{1,0:T(8,128)(2,1)} %collective-permute-done.2.refs_2_.refs_3_, ...), custom_call_target="tpu_custom_call" | custom-call | flops 99999997952 | bytes 500000000 | tf_op jit(solution)/shard_map/block0_partial/pallas_call | solution.py:74
  43.5 3.5 %collective-permute-start.4 = (bf16[2,64,1280]{2,1,0:T(8,128)(2,1)}, bf16[2,64,1280]{2,1,0:T(8,128)(2,1)}, u32[]{:S(2)}, u32[]{:S(2)}) collective-permute-start(bf16[2,64,1280]{2,1,0:T(8,128)(2,1)} %get-tuple-element.63), channel_id=1, source_target_pairs={{0,16},{1,17},{2,18},{3,19},{4,20},{5,21},{6,22},{7,23},{8,24},{9,... | collective-permute-start | bytes 983048 | tf_op jit(solution)/shard_map/ppermute | solution.py:551
  47.0 1.1 pick.2
  48.2 1.6 collective-permute-start.6
  50.5 2.0 stack.23
  52.5 1.9 collective-permute-done.6.refs_3_
  54.4 2.8 %collective-permute-done.7.refs_4_ = bf16[64,1280]{1,0:T(8,128)(2,1)S(1)} collective-permute-done((bf16[64,1280]{1,0:T(8,128)(2,1)S(1)}, bf16[64,1280]{1,0:T(8,128)(2,1)S(1)}, u32[]{:S(2)}, u32[]{:S(2)}) %collective-permute-start.7) | collective-permute-done | bytes 163872 | tf_op jit(solution)/shard_map/ppermute | solution.py:21
  57.2 1.6 pick.3
  59.7 1.6 assemble.3
  61.3 6.6 %collective-permute-done.8.refs_5_ = bf16[64,1280]{1,0:T(8,128)(2,1)S(1)} collective-permute-done((bf16[64,1280]{1,0:T(8,128)(2,1)S(1)}, bf16[64,1280]{1,0:T(8,128)(2,1)S(1)}, u32[]{:S(2)}, u32[]{:S(2)}) %collective-permute-start.8) | collective-permute-done | bytes 163872 | tf_op jit(solution)/shard_map/ppermute | solution.py:21
  68.0 1.3 denoise.1
  69.3 3.8 %collective-permute-start.13 = (bf16[64,1280]{1,0:T(8,128)(2,1)}, bf16[64,1280]{1,0:T(8,128)(2,1)S(1)}, u32[]{:S(2)}, u32[]{:S(2)}) collective-permute-start(bf16[64,1280]{1,0:T(8,128)(2,1)} %get-tuple-element.74.refs_1_), channel_id=1, source_target_pairs={{0,3},{1,0},{2,1},{3,2},{4,7},{5,4},{6,5},{7,6},{8,11},{9,8},{10,9... | collective-permute-start | bytes 491528 | tf_op jit(solution)/shard_map/ppermute | solution.py:21
  73.1 4.7 %collective-permute-done.11.refs_2_ = bf16[64,1280]{1,0:T(8,128)(2,1)S(1)} collective-permute-done((bf16[64,1280]{1,0:T(8,128)(2,1)}, bf16[64,1280]{1,0:T(8,128)(2,1)S(1)}, u32[]{:S(2)}, u32[]{:S(2)}) %collective-permute-start.11) | collective-permute-done | bytes 163872 | tf_op jit(solution)/shard_map/ppermute | solution.py:21
  77.8 2.1 %stack.24 = (bf16[1,640,1280]{2,1,0:T(8,128)(2,1)S(1)}, f32[8,128]{1,0:T(8,128)}) custom-call(s32[4]{0:T(128)S(1)} %pad_add_fusion.refs_0_, bf16[640,1280]{1,0:T(8,128)(2,1)} %collective-permute-done.14.refs_1_, bf16[64,1280]{1,0:T(8,128)(2,1)S(1)} %collective-permute-done.11.refs_2_, bf16[64,1280]{1,0:T(8,128)(2,1)S(1)} %collective-permute-done.13.refs_3_.refs_4_), custom_call_target="tpu_custom_call" | custom-call | flops 99999997952 | bytes 500000000 | tf_op jit(solution)/shard_map/stack/pallas_call | solution.py:74
  82.1 2.3 %collective-permute-start.12 = (bf16[64,1280]{1,0:T(8,128)(2,1)}, bf16[64,1280]{1,0:T(8,128)(2,1)}, u32[]{:S(2)}, u32[]{:S(2)}) collective-permute-start(bf16[64,1280]{1,0:T(8,128)(2,1)} %get-tuple-element.74.refs_1_), channel_id=1, source_target_pairs={{0,2},{1,3},{2,0},{3,1},{4,6},{5,7},{6,4},{7,5},{8,10},{9,11},{10,... | collective-permute-start | bytes 491528 | tf_op jit(solution)/shard_map/ppermute | solution.py:21
  84.4 1.7 assemble.4
  86.8 1.2 copy-done.12
  88.1 5.4 %collective-permute-done.12.refs_3_ = bf16[64,1280]{1,0:T(8,128)(2,1)} collective-permute-done((bf16[64,1280]{1,0:T(8,128)(2,1)}, bf16[64,1280]{1,0:T(8,128)(2,1)}, u32[]{:S(2)}, u32[]{:S(2)}) %collective-permute-start.12) | collective-permute-done | bytes 163872 | tf_op jit(solution)/shard_map/ppermute | solution.py:21
  93.5 4.2 %reward_forward.1 = (bf16[64,1280]{1,0:T(8,128)(2,1)S(1)}, bf16[64,1280]{1,0:T(8,128)(2,1)S(1)}, bf16[64,1280]{1,0:T(8,128)(2,1)S(1)}, bf16[64,1280]{1,0:T(8,128...) custom-call(s32[4]{0:T(128)S(1)} %pad_add_fusion.refs_0_, bf16[64,1280]{1,0:T(8,128)(2,1)} %get-tuple-element.74.refs_1_, ...), custom_call_target="tpu_custom_call" | custom-call | flops 99999997952 | bytes 500000000 | tf_op jit(solution)/shard_map/reward_forward/pallas_call | solution.py:74
  100.4 3.2 %collective-permute-start.17 = (f32[8,1280]{1,0:T(8,128)S(1)}, f32[8,1280]{1,0:T(8,128)}, u32[]{:S(2)}, u32[]{:S(2)}) collective-permute-start(f32[8,1280]{1,0:T(8,128)S(1)} %get-tuple-element.81.refs_1_), channel_id=1, source_target_pairs={{0,2},{1,3},{2,0},{3,1},{4,6},{5,7},{6,4},{7,5},{8,10},{9,11},{10,... | collective-permute-start | bytes 122888 | tf_op jit(solution)/shard_map/ppermute | solution.py:21
  104.3 2.5 %collective-permute-start.28 = (bf16[640,1280]{1,0:T(8,128)(2,1)}, bf16[640,1280]{1,0:T(8,128)(2,1)}, u32[]{:S(2)}, u32[]{:S(2)}) collective-permute-start(bf16[640,1280]{1,0:T(8,128)(2,1)} %copy-done.12), channel_id=1, source_target_pairs={{0,16},{1,17},{2,18},{3,19},{4,20},{5,21},{6,22},{7,23},{8,24},{9,... | collective-permute-start | bytes 4915208 | tf_op jit(solution)/shard_map/ppermute | solution.py:566
  107.7 1.9 copy-done.10
  109.6 1.9 copy-done.24
  111.6 1.9 copy-done.27
  117.2 4.0 %reward_back.1 = (bf16[64,1280]{1,0:T(8,128)(2,1)S(1)}, bf16[64,1280]{1,0:T(8,128)(2,1)S(1)}, bf16[64,1280]{1,0:T(8,128)(2,1)S(1)}, bf16[64,1280]{1,0:T(8,128)(2...) custom-call(s32[4]{0:T(128)S(1)} %pad_add_fusion.refs_0_, f32[8,1280]{1,0:T(8,128)S(1)} %get-tuple-element.81.refs_1_, ...), custom_call_target="tpu_custom_call" | custom-call | flops 99999997952 | bytes 500000000 | tf_op jit(solution)/shard_map/reward_back/pallas_call | solution.py:74
  121.1 2.5 %collective-permute-start.19 = (bf16[64,1280]{1,0:T(8,128)(2,1)S(1)}, bf16[64,1280]{1,0:T(8,128)(2,1)S(1)}, u32[]{:S(2)}, u32[]{:S(2)}) collective-permute-start(bf16[64,1280]{1,0:T(8,128)(2,1)S(1)} %get-tuple-element.88), channel_id=1, source_target_pairs={{0,3},{1,0},{2,1},{3,2},{4,7},{5,4},{6,5},{7,6},{8,11},{9,8},{10,9... | collective-permute-start | bytes 491528 | tf_op jit(solution)/shard_map/ppermute | solution.py:21
  124.3 4.3 %block0_state.1 = (bf16[512,1280]{1,0:T(8,128)(2,1)S(1)}, bf16[512,1280]{1,0:T(8,128)(2,1)S(1)}, bf16[640,512]{1,0:T(8,128)(2,1)S(1)}, f32[8,128]{1,0:T(8,128)S(1)}) custom-call(s32[4]{0:T(128)S(1)} %pad_add_fusion.refs_0_, bf16[128,1280]{1,0:T(8,128)(2,1)S(1)} %bitcast.37, bf16[128,1280]{1,0:T(8,128)(2,1)S(1)} %copy-done.16, ...), custom_call_target="tpu_custom_call" | custom-call | flops 99999997952 | bytes 500000000 | tf_op jit(solution)/shard_map/block0_state/pallas_call | solution.py:74
  128.6 8.9 %collective-permute-done.20.refs_7_ = bf16[64,1280]{1,0:T(8,128)(2,1)S(1)} collective-permute-done((bf16[64,1280]{1,0:T(8,128)(2,1)S(1)}, bf16[64,1280]{1,0:T(8,128)(2,1)S(1)}, u32[]{:S(2)}, u32[]{:S(2)}) %collective-permute-start.20) | collective-permute-done | bytes 163872 | tf_op jit(solution)/shard_map/ppermute | solution.py:21
  137.5 1.7 eps_gradient.1
  139.2 3.8 %collective-permute-start.24 = (bf16[64,1280]{1,0:T(8,128)(2,1)S(1)}, bf16[64,1280]{1,0:T(8,128)(2,1)S(1)}, u32[]{:S(2)}, u32[]{:S(2)}) collective-permute-start(bf16[64,1280]{1,0:T(8,128)(2,1)S(1)} %get-tuple-element.92.refs_1_), channel_id=1, source_target_pairs={{0,3},{1,0},{2,1},{3,2},{4,7},{5,4},{6,5},{7,6},{8,11},{9,8},{10,9... | collective-permute-start | bytes 491528 | tf_op jit(solution)/shard_map/ppermute | solution.py:21
  143.1 4.4 %collective-permute-done.22.refs_1_.refs_2_ = bf16[64,1280]{1,0:T(8,128)(2,1)S(1)} collective-permute-done((bf16[64,1280]{1,0:T(8,128)(2,1)S(1)}, bf16[64,1280]{1,0:T(8,128)(2,1)S(1)}, u32[]{:S(2)}, u32[]{:S(2)}) %collective-permute-start.22) | collective-permute-done | bytes 163872 | tf_op jit(solution)/shard_map/ppermute | solution.py:21
  147.5 1.2 collective-permute-done.24.refs_2_.refs_4_
  148.6 1.1 join.2
  149.8 1.5 collective-permute-start.23
  151.2 2.0 %collective-permute-start.25 = (bf16[64,1280]{1,0:T(8,128)(2,1)S(1)}, bf16[64,1280]{1,0:T(8,128)(2,1)S(1)}, u32[]{:S(2)}, u32[]{:S(2)}) collective-permute-start(bf16[64,1280]{1,0:T(8,128)(2,1)S(1)} %get-tuple-element.92.refs_1_), channel_id=1, source_target_pairs={{0,16},{16,0},{1,17},{17,1},{2,18},{18,2},{3,19},{19,3},{4,20},{20... | collective-permute-start | bytes 491528 | tf_op jit(solution)/shard_map/ppermute | solution.py:26
  153.3 6.5 %collective-permute-done.23.refs_1_.refs_3_ = bf16[64,1280]{1,0:T(8,128)(2,1)S(1)} collective-permute-done((bf16[64,1280]{1,0:T(8,128)(2,1)S(1)}, bf16[64,1280]{1,0:T(8,128)(2,1)S(1)}, u32[]{:S(2)}, u32[]{:S(2)}) %collective-permute-start.23) | collective-permute-done | bytes 163872 | tf_op jit(solution)/shard_map/ppermute | solution.py:21
  160.4 2.0 %collective-permute-done.25.refs_2_.refs_5_ = bf16[64,1280]{1,0:T(8,128)(2,1)S(1)} collective-permute-done((bf16[64,1280]{1,0:T(8,128)(2,1)S(1)}, bf16[64,1280]{1,0:T(8,128)(2,1)S(1)}, u32[]{:S(2)}, u32[]{:S(2)}) %collective-permute-start.25) | collective-permute-done | bytes 163872 | tf_op jit(solution)/shard_map/ppermute | solution.py:26
  162.4 2.0 %stack.25 = (bf16[1,640,1280]{2,1,0:T(8,128)(2,1)S(1)}, f32[8,128]{1,0:T(8,128)}) custom-call(s32[4]{0:T(128)S(1)} %pad_add_fusion.refs_0_, bf16[640,1280]{1,0:T(8,128)(2,1)} %collective-permute-done.28.refs_1_, bf16[64,1280]{1,0:T(8,128)(2,1)S(1)} %collective-permute-done.25.refs_2_.refs_5_, bf16[128,1280]{1,0:T(8,128)(2,1)S(1)} %collective-permute-done.26.refs_3_.refs_6_, ...), custom_call_target="tpu_custom_call" | custom-call | flops 1 | tf_op jit(solution)/shard_map/stack/pallas_call | solution.py:74
  164.7 3.2 %collective-permute-done.29.refs_2_ = bf16[1,640,1280]{2,1,0:T(8,128)(2,1)S(1)} collective-permute-done((bf16[1,640,1280]{2,1,0:T(8,128)(2,1)S(1)}, bf16[1,640,1280]{2,1,0:T(8,128)(2,1)S(1)}, u32[]{:S(2)}, u32[]{:S(2)}) %collective-permute-start.29) | collective-permute-done | bytes 1638432 | tf_op jit(solution)/shard_map/ppermute | solution.py:26
  168.0 2.0 %assemble.5 = (bf16[1280,1280]{1,0:T(8,128)(2,1)S(1)}, f32[8,128]{1,0:T(8,128)}) custom-call(s32[4]{0:T(128)S(1)} %pad_add_fusion.refs_0_, bf16[640,1280]{1,0:T(8,128)(2,1)} %collective-permute-done.28.refs_1_, bf16[1,640,1280]{2,1,0:T(8,128)(2,1)S(1)} %collective-permute-done.29.refs_2_), custom_call_target="tpu_custom_call" | custom-call | flops 1 | tf_op jit(solution)/shard_map/assemble/pallas_call | solution.py:74
  170.0 1.1 collective-permute-done.27.refs_7_
  171.1 5.6 %gradients.1 = (bf16[2,160,1280]{2,1,0:T(8,128)(2,1)S(1)}, bf16[2,160,1280]{2,1,0:T(8,128)(2,1)S(1)}, bf16[2,160,1280]{2,1,0:T(8,128)(2,1)S(1)}, bf16[2,160,1280]{2,1,0:T(8,128)(2,1)S(1)}, f32[8,128]{1,0:T(8,128)}) custom-call(s32[4]{0:T(128)S(1)} %pad_add_fusion.refs_0_, bf16[64,1280]{1,0:T(8,128)(2,1)S(1)} %get-tuple-element.92.refs_1_, ...), custom_call_target="tpu_custom_call" | custom-call | flops 99999997952 | bytes 500000000 | tf_op jit(solution)/shard_map/gradients/pallas_call | solution.py:74
  177.2 1.8 collective-permute-done.32.refs_2_
  179.0 1.1 chip_sum.3
  180.2 1.5 collective-permute-start.33
  181.7 1.1 chip_sum.2
  183.3 9.1 %collective-permute-done.33 = bf16[160,1280]{1,0:T(8,128)(2,1)S(1)} collective-permute-done((bf16[160,1280]{1,0:T(8,128)(2,1)S(1)}, bf16[160,1280]{1,0:T(8,128)(2,1)S(1)}, u32[]{:S(2)}, u32[]{:S(2)}) %collective-permute-start.33) | collective-permute-done | bytes 409632 | tf_op jit(solution)/shard_map/ppermute | solution.py:21
  193.4 7.0 %collective-permute-done.31 = bf16[160,1280]{1,0:T(8,128)(2,1)S(1)} collective-permute-done((bf16[160,1280]{1,0:T(8,128)(2,1)S(1)}, bf16[160,1280]{1,0:T(8,128)(2,1)S(1)}, u32[]{:S(2)}, u32[]{:S(2)}) %collective-permute-start.31) | collective-permute-done | bytes 409632 | tf_op jit(solution)/shard_map/ppermute | solution.py:21
  (117 shorter events, 16.3 us)
Async XLA Ops:
  0.6 81.4 %copy-start = (bf16[64,1280]{1,0:T(8,128)(2,1)S(1)}, bf16[64,1280]{1,0:T(8,128)(2,1)}, u32[]{:S(2)}) copy-start(bf16[64,1280]{1,0:T(8,128)(2,1)} %param.10) | copy-start | bytes 491524
  0.6 13.9 %collective-permute-start = (bf16[128,1280]{1,0:T(8,128)(2,1)}, bf16[128,1280]{1,0:T(8,128)(2,1)S(1)}, u32[]{:S(2)}, u32[]{:S(2)}) collective-permute-start(bf16[128,1280]{1,0:T(8,128)(2,1)} %bitcast.32), channel_id=1, source_target_pairs={{0,1},{1,2},{2,3},{3,0},{4,5},{5,6},{6,7},{7,4},{8,9},{9,10},{10,1... | collective-permute-start | bytes 983048 | tf_op jit(solution)/shard_map/ppermute | solution.py:21
  3.7 16.4 %collective-permute-start.1 = (bf16[128,1280]{1,0:T(8,128)(2,1)}, bf16[128,1280]{1,0:T(8,128)(2,1)S(1)}, u32[]{:S(2)}, u32[]{:S(2)}) collective-permute-start(bf16[128,1280]{1,0:T(8,128)(2,1)} %bitcast.33), channel_id=1, source_target_pairs={{0,3},{1,0},{2,1},{3,2},{4,7},{5,4},{6,5},{7,6},{8,11},{9,8},{10,9... | collective-permute-start | bytes 983048 | tf_op jit(solution)/shard_map/ppermute | solution.py:21
  5.9 1.9 copy-start.5
  7.8 3.2 %copy-start.37 = (s32[2]{0:T(128)S(1)}, s32[2]{0:T(128)}, u32[]{:S(2)}) copy-start(s32[2]{0:T(128)} %param.8) | copy-start | bytes 28
  7.8 5.2 %copy-start.36 = (f32[2,1280]{1,0:T(2,128)S(1)}, f32[2,1280]{1,0:T(2,128)}, u32[]{:S(2)}) copy-start(f32[2,1280]{1,0:T(2,128)} %param.11) | copy-start | bytes 30724
  7.8 12.3 %copy-start.13 = (bf16[2,64,1280]{2,1,0:T(8,128)(2,1)S(1)}, bf16[2,64,1280]{2,1,0:T(8,128)(2,1)}, u32[]{:S(2)}) copy-start(bf16[2,64,1280]{2,1,0:T(8,128)(2,1)} %param.7) | copy-start | bytes 983044
  9.3 20.7 %collective-permute-start.3 = (bf16[320,1280]{1,0:T(8,128)(2,1)}, bf16[320,1280]{1,0:T(8,128)(2,1)}, u32[]{:S(2)}, u32[]{:S(2)}) collective-permute-start(bf16[320,1280]{1,0:T(8,128)(2,1)} %get-tuple-element.57), channel_id=1, source_target_pairs={{0,16},{16,0},{1,17},{17,1},{2,18},{18,2},{3,19},{19,3},{4,20},{20... | collective-permute-start | bytes 2457608 | tf_op jit(solution)/shard_map/ppermute | solution.py:26
  13.1 26.3 %copy-start.3 = (f32[1,1280]{1,0:T(1,128)}, f32[1,1280]{1,0:T(1,128)S(1)}, u32[]{:S(2)}) copy-start(f32[1,1280]{1,0:T(1,128)S(1)} %get-tuple-element.111.refs_3_.refs_5_) | copy-start | bytes 15364
  13.1 80.4 %copy-start.1 = (f32[1,1280]{1,0:T(1,128)}, f32[1,1280]{1,0:T(1,128)S(1)}, u32[]{:S(2)}) copy-start(f32[1,1280]{1,0:T(1,128)S(1)} %get-tuple-element.110.refs_5_.refs_3_) | copy-start | bytes 15364
  13.1 9.7 %copy-start.8 = (bf16[1,1280,1280]{2,1,0:T(8,128)(2,1)S(1)}, bf16[1,1280,1280]{2,1,0:T(8,128)(2,1)}, u32[]{:S(2)}) copy-start(bf16[1,1280,1280]{2,1,0:T(8,128)(2,1)} %param.13) | copy-start | bytes 9830404
  14.5 19.3 %copy-start.15 = (bf16[128,1280]{1,0:T(8,128)(2,1)}, bf16[128,1280]{1,0:T(8,128)(2,1)S(1)}, u32[]{:S(2)}) copy-start(bf16[128,1280]{1,0:T(8,128)(2,1)S(1)} %collective-permute-done.refs_2_.refs_1_) | copy-start | bytes 983044
  20.1 13.7 %copy-start.17 = (bf16[128,1280]{1,0:T(8,128)(2,1)}, bf16[128,1280]{1,0:T(8,128)(2,1)S(1)}, u32[]{:S(2)}) copy-start(bf16[128,1280]{1,0:T(8,128)(2,1)S(1)} %collective-permute-done.1.refs_3_.refs_2_.refs_4_) | copy-start | bytes 983044
  21.4 17.9 %collective-permute-start.2 = (bf16[128,1280]{1,0:T(8,128)(2,1)}, bf16[128,1280]{1,0:T(8,128)(2,1)}, u32[]{:S(2)}, u32[]{:S(2)}) collective-permute-start(bf16[128,1280]{1,0:T(8,128)(2,1)} %get-tuple-element.56), channel_id=1, source_target_pairs={{0,2},{1,3},{2,0},{3,1},{4,6},{5,7},{6,4},{7,5},{8,10},{9,11},{10,... | collective-permute-start | bytes 983048 | tf_op jit(solution)/shard_map/ppermute | solution.py:21
  24.6 9.3 %copy-start.6 = (bf16[1,1280,1280]{2,1,0:T(8,128)(2,1)S(1)}, bf16[1,1280,1280]{2,1,0:T(8,128)(2,1)}, u32[]{:S(2)}) copy-start(bf16[1,1280,1280]{2,1,0:T(8,128)(2,1)} %param.12) | copy-start | bytes 9830404
  24.6 48.6 %collective-permute-start.14 = (bf16[640,1280]{1,0:T(8,128)(2,1)}, bf16[640,1280]{1,0:T(8,128)(2,1)}, u32[]{:S(2)}, u32[]{:S(2)}) collective-permute-start(bf16[640,1280]{1,0:T(8,128)(2,1)} %get-tuple-element.76), channel_id=1, source_target_pairs={{16,0},{17,1},{18,2},{19,3},{20,4},{21,5},{22,6},{23,7},{24,8},{25... | collective-permute-start | bytes 4915208 | tf_op jit(solution)/shard_map/ppermute | solution.py:538
  32.1 18.4 %collective-permute-start.9 = (bf16[320,1280]{1,0:T(8,128)(2,1)}, bf16[320,1280]{1,0:T(8,128)(2,1)}, u32[]{:S(2)}, u32[]{:S(2)}) collective-permute-start(bf16[320,1280]{1,0:T(8,128)(2,1)} %get-tuple-element.70), channel_id=1, source_target_pairs={{0,8},{4,12},{8,0},{12,4},{1,9},{5,13},{9,1},{13,5},{2,10},{6,14},... | collective-permute-start | bytes 2457608 | tf_op jit(solution)/shard_map/ppermute | solution.py:26
  36.8 10.2 %collective-permute-start.5 = (bf16[2,64,1280]{2,1,0:T(8,128)(2,1)S(1)}, bf16[2,64,1280]{2,1,0:T(8,128)(2,1)S(1)}, u32[]{:S(2)}, u32[]{:S(2)}) collective-permute-start(bf16[2,64,1280]{2,1,0:T(8,128)(2,1)S(1)} %get-tuple-element.65), channel_id=1, source_target_pairs={{0,16},{1,17},{2,18},{3,19},{4,20},{5,21},{6,22},{7,23},{8,24},{9,... | collective-permute-start | bytes 983048 | tf_op jit(solution)/shard_map/ppermute | solution.py:551
  43.5 9.1 %collective-permute-start.4 = (bf16[2,64,1280]{2,1,0:T(8,128)(2,1)}, bf16[2,64,1280]{2,1,0:T(8,128)(2,1)}, u32[]{:S(2)}, u32[]{:S(2)}) collective-permute-start(bf16[2,64,1280]{2,1,0:T(8,128)(2,1)} %get-tuple-element.63), channel_id=1, source_target_pairs={{0,16},{1,17},{2,18},{3,19},{4,20},{5,21},{6,22},{7,23},{8,24},{9,... | collective-permute-start | bytes 983048 | tf_op jit(solution)/shard_map/ppermute | solution.py:551
  48.2 6.3 %collective-permute-start.6 = (bf16[64,1280]{1,0:T(8,128)(2,1)S(1)}, bf16[64,1280]{1,0:T(8,128)(2,1)S(1)}, u32[]{:S(2)}, u32[]{:S(2)}) collective-permute-start(bf16[64,1280]{1,0:T(8,128)(2,1)S(1)} %get-tuple-element.66), channel_id=1, source_target_pairs={{0,3},{1,0},{2,1},{3,2},{4,7},{5,4},{6,5},{7,6},{8,11},{9,8},{10,9... | collective-permute-start | bytes 491528 | tf_op jit(solution)/shard_map/ppermute | solution.py:21
  49.8 7.5 %collective-permute-start.7 = (bf16[64,1280]{1,0:T(8,128)(2,1)S(1)}, bf16[64,1280]{1,0:T(8,128)(2,1)S(1)}, u32[]{:S(2)}, u32[]{:S(2)}) collective-permute-start(bf16[64,1280]{1,0:T(8,128)(2,1)S(1)} %get-tuple-element.67), channel_id=1, source_target_pairs={{0,1},{1,2},{2,3},{3,0},{4,5},{5,6},{6,7},{7,4},{8,9},{9,10},{10,1... | collective-permute-start | bytes 491528 | tf_op jit(solution)/shard_map/ppermute | solution.py:21
  52.5 7.2 %collective-permute-start.10 = (bf16[2,320,1280]{2,1,0:T(8,128)(2,1)S(1)}, bf16[2,320,1280]{2,1,0:T(8,128)(2,1)S(1)}, u32[]{:S(2)}, u32[]{:S(2)}) collective-permute-start(bf16[2,320,1280]{2,1,0:T(8,128)(2,1)S(1)} %get-tuple-element.72), channel_id=1, source_target_pairs={{0,4},{4,0},{8,12},{12,8},{1,5},{5,1},{9,13},{13,9},{2,6},{6,2},{1... | collective-permute-start | bytes 4915208 | tf_op jit(solution)/shard_map/ppermute | solution.py:26
  58.8 9.2 %collective-permute-start.8 = (bf16[64,1280]{1,0:T(8,128)(2,1)S(1)}, bf16[64,1280]{1,0:T(8,128)(2,1)S(1)}, u32[]{:S(2)}, u32[]{:S(2)}) collective-permute-start(bf16[64,1280]{1,0:T(8,128)(2,1)S(1)} %get-tuple-element.69), channel_id=1, source_target_pairs={{0,2},{1,3},{2,0},{3,1},{4,6},{5,7},{6,4},{7,5},{8,10},{9,11},{10,... | collective-permute-start | bytes 491528 | tf_op jit(solution)/shard_map/ppermute | solution.py:21
  61.3 32.1 %copy-start.23 = (bf16[1280,1280]{1,0:T(8,128)(2,1)}, bf16[1280,1280]{1,0:T(8,128)(2,1)S(1)}, u32[]{:S(2)}) copy-start(bf16[1280,1280]{1,0:T(8,128)(2,1)S(1)} %get-tuple-element.75.refs_9_.refs_11_.refs_7_) | copy-start | bytes 9830404
  69.3 10.7 %copy-start.38 = (s32[2]{0:T(128)S(1)}, s32[2]{0:T(128)}, u32[]{:S(2)}) copy-start(s32[2]{0:T(128)} %param.9) | copy-start | bytes 28
  69.3 8.5 %collective-permute-start.11 = (bf16[64,1280]{1,0:T(8,128)(2,1)}, bf16[64,1280]{1,0:T(8,128)(2,1)S(1)}, u32[]{:S(2)}, u32[]{:S(2)}) collective-permute-start(bf16[64,1280]{1,0:T(8,128)(2,1)} %get-tuple-element.74.refs_1_), channel_id=1, source_target_pairs={{0,1},{1,2},{2,3},{3,0},{4,5},{5,6},{6,7},{7,4},{8,9},{9,10},{10,1... | collective-permute-start | bytes 491528 | tf_op jit(solution)/shard_map/ppermute | solution.py:21
  69.3 8.5 %collective-permute-start.13 = (bf16[64,1280]{1,0:T(8,128)(2,1)}, bf16[64,1280]{1,0:T(8,128)(2,1)S(1)}, u32[]{:S(2)}, u32[]{:S(2)}) collective-permute-start(bf16[64,1280]{1,0:T(8,128)(2,1)} %get-tuple-element.74.refs_1_), channel_id=1, source_target_pairs={{0,3},{1,0},{2,1},{3,2},{4,7},{5,4},{6,5},{7,6},{8,11},{9,8},{10,9... | collective-permute-start | bytes 491528 | tf_op jit(solution)/shard_map/ppermute | solution.py:21
  77.8 2.2 %copy-start.19 = (bf16[64,1280]{1,0:T(8,128)(2,1)}, bf16[64,1280]{1,0:T(8,128)(2,1)S(1)}, u32[]{:S(2)}) copy-start(bf16[64,1280]{1,0:T(8,128)(2,1)S(1)} %collective-permute-done.11.refs_2_) | copy-start | bytes 491524
  77.8 2.2 %copy-start.21 = (bf16[64,1280]{1,0:T(8,128)(2,1)}, bf16[64,1280]{1,0:T(8,128)(2,1)S(1)}, u32[]{:S(2)}) copy-start(bf16[64,1280]{1,0:T(8,128)(2,1)S(1)} %collective-permute-done.13.refs_3_.refs_4_) | copy-start | bytes 491524
  80.0 4.4 %collective-permute-start.15 = (bf16[1,640,1280]{2,1,0:T(8,128)(2,1)S(1)}, bf16[1,640,1280]{2,1,0:T(8,128)(2,1)S(1)}, u32[]{:S(2)}, u32[]{:S(2)}) collective-permute-start(bf16[1,640,1280]{2,1,0:T(8,128)(2,1)S(1)} %get-tuple-element.77), channel_id=1, source_target_pairs={{0,4},{4,0},{8,12},{12,8},{1,5},{5,1},{9,13},{13,9},{2,6},{6,2},{1... | collective-permute-start | bytes 4915208 | tf_op jit(solution)/shard_map/ppermute | solution.py:26
  82.1 4.0 %copy-start.9 = (bf16[1,1280,1280]{2,1,0:T(8,128)(2,1)S(1)}, bf16[1,1280,1280]{2,1,0:T(8,128)(2,1)}, u32[]{:S(2)}) copy-start(bf16[1,1280,1280]{2,1,0:T(8,128)(2,1)} %param.13) | copy-start | bytes 9830404
  82.1 11.3 %collective-permute-start.12 = (bf16[64,1280]{1,0:T(8,128)(2,1)}, bf16[64,1280]{1,0:T(8,128)(2,1)}, u32[]{:S(2)}, u32[]{:S(2)}) collective-permute-start(bf16[64,1280]{1,0:T(8,128)(2,1)} %get-tuple-element.74.refs_1_), channel_id=1, source_target_pairs={{0,2},{1,3},{2,0},{3,1},{4,6},{5,7},{6,4},{7,5},{8,10},{9,11},{10,... | collective-permute-start | bytes 491528 | tf_op jit(solution)/shard_map/ppermute | solution.py:21
  86.1 7.4 %copy-start.26 = (bf16[1280,1280]{1,0:T(8,128)(2,1)}, bf16[1280,1280]{1,0:T(8,128)(2,1)S(1)}, u32[]{:S(2)}) copy-start(bf16[1280,1280]{1,0:T(8,128)(2,1)S(1)} %get-tuple-element.78.refs_10_.refs_12_) | copy-start | bytes 9830404
  86.1 7.3 %copy-start.7 = (bf16[1,1280,1280]{2,1,0:T(8,128)(2,1)S(1)}, bf16[1,1280,1280]{2,1,0:T(8,128)(2,1)}, u32[]{:S(2)}) copy-start(bf16[1,1280,1280]{2,1,0:T(8,128)(2,1)} %param.12) | copy-start | bytes 9830404
  86.1 7.3 %copy-start.20 = (bf16[64,1280]{1,0:T(8,128)(2,1)S(1)}, bf16[64,1280]{1,0:T(8,128)(2,1)}, u32[]{:S(2)}) copy-start(bf16[64,1280]{1,0:T(8,128)(2,1)} %copy-done.19) | copy-start | bytes 491524
  86.1 7.3 %copy-start.22 = (bf16[64,1280]{1,0:T(8,128)(2,1)S(1)}, bf16[64,1280]{1,0:T(8,128)(2,1)}, u32[]{:S(2)}) copy-start(bf16[64,1280]{1,0:T(8,128)(2,1)} %copy-done.21) | copy-start | bytes 491524
  100.4 6.3 %collective-permute-start.16 = (f32[8,1280]{1,0:T(8,128)S(1)}, f32[8,1280]{1,0:T(8,128)S(1)}, u32[]{:S(2)}, u32[]{:S(2)}) collective-permute-start(f32[8,1280]{1,0:T(8,128)S(1)} %get-tuple-element.81.refs_1_), channel_id=1, source_target_pairs={{0,1},{1,2},{2,3},{3,0},{4,5},{5,6},{6,7},{7,4},{8,9},{9,10},{10,1... | collective-permute-start | bytes 122888 | tf_op jit(solution)/shard_map/ppermute | solution.py:21
  100.4 6.9 %collective-permute-start.17 = (f32[8,1280]{1,0:T(8,128)S(1)}, f32[8,1280]{1,0:T(8,128)}, u32[]{:S(2)}, u32[]{:S(2)}) collective-permute-start(f32[8,1280]{1,0:T(8,128)S(1)} %get-tuple-element.81.refs_1_), channel_id=1, source_target_pairs={{0,2},{1,3},{2,0},{3,1},{4,6},{5,7},{6,4},{7,5},{8,10},{9,11},{10,... | collective-permute-start | bytes 122888 | tf_op jit(solution)/shard_map/ppermute | solution.py:21
  103.6 4.1 %collective-permute-start.18 = (f32[8,1280]{1,0:T(8,128)S(1)}, f32[8,1280]{1,0:T(8,128)}, u32[]{:S(2)}, u32[]{:S(2)}) collective-permute-start(f32[8,1280]{1,0:T(8,128)S(1)} %get-tuple-element.81.refs_1_), channel_id=1, source_target_pairs={{0,3},{1,0},{2,1},{3,2},{4,7},{5,4},{6,5},{7,6},{8,11},{9,8},{10,9... | collective-permute-start | bytes 122888 | tf_op jit(solution)/shard_map/ppermute | solution.py:21
  104.3 58.2 %collective-permute-start.28 = (bf16[640,1280]{1,0:T(8,128)(2,1)}, bf16[640,1280]{1,0:T(8,128)(2,1)}, u32[]{:S(2)}, u32[]{:S(2)}) collective-permute-start(bf16[640,1280]{1,0:T(8,128)(2,1)} %copy-done.12), channel_id=1, source_target_pairs={{0,16},{1,17},{2,18},{3,19},{4,20},{5,21},{6,22},{7,23},{8,24},{9,... | collective-permute-start | bytes 4915208 | tf_op jit(solution)/shard_map/ppermute | solution.py:566
  107.7 1.9 copy-start.10
  109.6 1.9 copy-start.24
  111.6 1.9 copy-start.27
  117.1 7.1 %copy-start.4 = (f32[1,1280]{1,0:T(1,128)S(1)}, f32[1,1280]{1,0:T(1,128)}, u32[]{:S(2)}) copy-start(f32[1,1280]{1,0:T(1,128)} %copy-done.3) | copy-start | bytes 15364
  117.2 7.1 %copy-start.14 = (bf16[2,64,1280]{2,1,0:T(8,128)(2,1)S(1)}, bf16[2,64,1280]{2,1,0:T(8,128)(2,1)}, u32[]{:S(2)}) copy-start(bf16[2,64,1280]{2,1,0:T(8,128)(2,1)} %param.7) | copy-start | bytes 983044
  117.2 7.1 %copy-start.16 = (bf16[128,1280]{1,0:T(8,128)(2,1)S(1)}, bf16[128,1280]{1,0:T(8,128)(2,1)}, u32[]{:S(2)}) copy-start(bf16[128,1280]{1,0:T(8,128)(2,1)} %copy-done.15) | copy-start | bytes 983044
  117.2 7.1 %copy-start.18 = (bf16[128,1280]{1,0:T(8,128)(2,1)S(1)}, bf16[128,1280]{1,0:T(8,128)(2,1)}, u32[]{:S(2)}) copy-start(bf16[128,1280]{1,0:T(8,128)(2,1)} %copy-done.17) | copy-start | bytes 983044
  117.2 7.1 %copy-start.25 = (bf16[1280,1280]{1,0:T(8,128)(2,1)S(1)}, bf16[1280,1280]{1,0:T(8,128)(2,1)}, u32[]{:S(2)}) copy-start(bf16[1280,1280]{1,0:T(8,128)(2,1)} %copy-done.23) | copy-start | bytes 9830404
  121.1 7.5 %collective-permute-start.19 = (bf16[64,1280]{1,0:T(8,128)(2,1)S(1)}, bf16[64,1280]{1,0:T(8,128)(2,1)S(1)}, u32[]{:S(2)}, u32[]{:S(2)}) collective-permute-start(bf16[64,1280]{1,0:T(8,128)(2,1)S(1)} %get-tuple-element.88), channel_id=1, source_target_pairs={{0,3},{1,0},{2,1},{3,2},{4,7},{5,4},{6,5},{7,6},{8,11},{9,8},{10,9... | collective-permute-start | bytes 491528 | tf_op jit(solution)/shard_map/ppermute | solution.py:21
  123.7 13.8 %collective-permute-start.20 = (bf16[64,1280]{1,0:T(8,128)(2,1)S(1)}, bf16[64,1280]{1,0:T(8,128)(2,1)S(1)}, u32[]{:S(2)}, u32[]{:S(2)}) collective-permute-start(bf16[64,1280]{1,0:T(8,128)(2,1)S(1)} %get-tuple-element.89), channel_id=1, source_target_pairs={{0,2},{1,3},{2,0},{3,1},{4,6},{5,7},{6,4},{7,5},{8,10},{9,11},{10,... | collective-permute-start | bytes 491528 | tf_op jit(solution)/shard_map/ppermute | solution.py:21
  123.8 13.7 %collective-permute-start.21 = (bf16[64,1280]{1,0:T(8,128)(2,1)S(1)}, bf16[64,1280]{1,0:T(8,128)(2,1)S(1)}, u32[]{:S(2)}, u32[]{:S(2)}) collective-permute-start(bf16[64,1280]{1,0:T(8,128)(2,1)S(1)} %get-tuple-element.90), channel_id=1, source_target_pairs={{0,1},{1,2},{2,3},{3,0},{4,5},{5,6},{6,7},{7,4},{8,9},{9,10},{10,1... | collective-permute-start | bytes 491528 | tf_op jit(solution)/shard_map/ppermute | solution.py:21
  124.3 13.2 %copy-start.2 = (f32[1,1280]{1,0:T(1,128)S(1)}, f32[1,1280]{1,0:T(1,128)}, u32[]{:S(2)}) copy-start(f32[1,1280]{1,0:T(1,128)} %copy-done.1) | copy-start | bytes 15364
  139.2 8.2 %collective-permute-start.22 = (bf16[64,1280]{1,0:T(8,128)(2,1)S(1)}, bf16[64,1280]{1,0:T(8,128)(2,1)S(1)}, u32[]{:S(2)}, u32[]{:S(2)}) collective-permute-start(bf16[64,1280]{1,0:T(8,128)(2,1)S(1)} %get-tuple-element.92.refs_1_), channel_id=1, source_target_pairs={{0,1},{1,2},{2,3},{3,0},{4,5},{5,6},{6,7},{7,4},{8,9},{9,10},{10,1... | collective-permute-start | bytes 491528 | tf_op jit(solution)/shard_map/ppermute | solution.py:21
  139.2 9.4 %collective-permute-start.24 = (bf16[64,1280]{1,0:T(8,128)(2,1)S(1)}, bf16[64,1280]{1,0:T(8,128)(2,1)S(1)}, u32[]{:S(2)}, u32[]{:S(2)}) collective-permute-start(bf16[64,1280]{1,0:T(8,128)(2,1)S(1)} %get-tuple-element.92.refs_1_), channel_id=1, source_target_pairs={{0,3},{1,0},{2,1},{3,2},{4,7},{5,4},{6,5},{7,6},{8,11},{9,8},{10,9... | collective-permute-start | bytes 491528 | tf_op jit(solution)/shard_map/ppermute | solution.py:21
  149.8 12.6 %collective-permute-start.26 = (bf16[128,1280]{1,0:T(8,128)(2,1)S(1)}, bf16[128,1280]{1,0:T(8,128)(2,1)S(1)}, u32[]{:S(2)}, u32[]{:S(2)}) collective-permute-start(bf16[128,1280]{1,0:T(8,128)(2,1)S(1)} %get-tuple-element.93), channel_id=1, source_target_pairs={{0,16},{16,0},{1,17},{17,1},{2,18},{18,2},{3,19},{19,3},{4,20},{20... | collective-permute-start | bytes 983048 | tf_op jit(solution)/shard_map/ppermute | solution.py:26
  149.8 10.0 %collective-permute-start.23 = (bf16[64,1280]{1,0:T(8,128)(2,1)S(1)}, bf16[64,1280]{1,0:T(8,128)(2,1)S(1)}, u32[]{:S(2)}, u32[]{:S(2)}) collective-permute-start(bf16[64,1280]{1,0:T(8,128)(2,1)S(1)} %get-tuple-element.92.refs_1_), channel_id=1, source_target_pairs={{0,2},{1,3},{2,0},{3,1},{4,6},{5,7},{6,4},{7,5},{8,10},{9,11},{10,... | collective-permute-start | bytes 491528 | tf_op jit(solution)/shard_map/ppermute | solution.py:21
  151.2 11.2 %collective-permute-start.25 = (bf16[64,1280]{1,0:T(8,128)(2,1)S(1)}, bf16[64,1280]{1,0:T(8,128)(2,1)S(1)}, u32[]{:S(2)}, u32[]{:S(2)}) collective-permute-start(bf16[64,1280]{1,0:T(8,128)(2,1)S(1)} %get-tuple-element.92.refs_1_), channel_id=1, source_target_pairs={{0,16},{16,0},{1,17},{17,1},{2,18},{18,2},{3,19},{19,3},{4,20},{20... | collective-permute-start | bytes 491528 | tf_op jit(solution)/shard_map/ppermute | solution.py:26
  164.5 3.5 %collective-permute-start.29 = (bf16[1,640,1280]{2,1,0:T(8,128)(2,1)S(1)}, bf16[1,640,1280]{2,1,0:T(8,128)(2,1)S(1)}, u32[]{:S(2)}, u32[]{:S(2)}) collective-permute-start(bf16[1,640,1280]{2,1,0:T(8,128)(2,1)S(1)} %get-tuple-element.100), channel_id=1, source_target_pairs={{0,4},{4,0},{8,12},{12,8},{1,5},{5,1},{9,13},{13,9},{2,6},{6,2},{1... | collective-permute-start | bytes 4915208 | tf_op jit(solution)/shard_map/ppermute | solution.py:26
  164.5 6.6 %copy-start.11 = (bf16[1,1280,1280]{2,1,0:T(8,128)(2,1)S(1)}, bf16[1,1280,1280]{2,1,0:T(8,128)(2,1)}, u32[]{:S(2)}) copy-start(bf16[1,1280,1280]{2,1,0:T(8,128)(2,1)} %param.13) | copy-start | bytes 9830404
  164.5 6.6 %collective-permute-start.27 = (bf16[64,1280]{1,0:T(8,128)(2,1)S(1)}, bf16[64,1280]{1,0:T(8,128)(2,1)S(1)}, u32[]{:S(2)}, u32[]{:S(2)}) collective-permute-start(bf16[64,1280]{1,0:T(8,128)(2,1)S(1)} %get-tuple-element.94), channel_id=1, source_target_pairs={{0,16},{16,0},{1,17},{17,1},{2,18},{18,2},{3,19},{19,3},{4,20},{20... | collective-permute-start | bytes 491528 | tf_op jit(solution)/shard_map/ppermute | solution.py:26
  176.7 2.3 %collective-permute-start.32 = (bf16[2,160,1280]{2,1,0:T(8,128)(2,1)S(1)}, bf16[2,160,1280]{2,1,0:T(8,128)(2,1)S(1)}, u32[]{:S(2)}, u32[]{:S(2)}) collective-permute-start(bf16[2,160,1280]{2,1,0:T(8,128)(2,1)S(1)} %get-tuple-element.107), channel_id=1, source_target_pairs={{0,4},{4,0},{8,12},{12,8},{1,5},{5,1},{9,13},{13,9},{2,6},{6,2},{1... | collective-permute-start | bytes 2457608 | tf_op jit(solution)/shard_map/ppermute | solution.py:26
  176.7 5.0 %collective-permute-start.30 = (bf16[2,160,1280]{2,1,0:T(8,128)(2,1)S(1)}, bf16[2,160,1280]{2,1,0:T(8,128)(2,1)S(1)}, u32[]{:S(2)}, u32[]{:S(2)}) collective-permute-start(bf16[2,160,1280]{2,1,0:T(8,128)(2,1)S(1)} %get-tuple-element.103), channel_id=1, source_target_pairs={{0,4},{4,0},{8,12},{12,8},{1,5},{5,1},{9,13},{13,9},{2,6},{6,2},{1... | collective-permute-start | bytes 2457608 | tf_op jit(solution)/shard_map/ppermute | solution.py:26
  180.2 12.3 %collective-permute-start.33 = (bf16[160,1280]{1,0:T(8,128)(2,1)S(1)}, bf16[160,1280]{1,0:T(8,128)(2,1)S(1)}, u32[]{:S(2)}, u32[]{:S(2)}) collective-permute-start(bf16[160,1280]{1,0:T(8,128)(2,1)S(1)} %bitcast.30), channel_id=1, source_target_pairs={{0,8},{4,12},{8,0},{12,4},{1,9},{5,13},{9,1},{13,5},{2,10},{6,14},... | collective-permute-start | bytes 1228808 | tf_op jit(solution)/shard_map/ppermute | solution.py:21
  182.8 17.7 %collective-permute-start.31 = (bf16[160,1280]{1,0:T(8,128)(2,1)S(1)}, bf16[160,1280]{1,0:T(8,128)(2,1)S(1)}, u32[]{:S(2)}, u32[]{:S(2)}) collective-permute-start(bf16[160,1280]{1,0:T(8,128)(2,1)S(1)} %bitcast.31), channel_id=1, source_target_pairs={{0,8},{4,12},{8,0},{12,4},{1,9},{5,13},{9,1},{13,5},{2,10},{6,14},... | collective-permute-start | bytes 1228808 | tf_op jit(solution)/shard_map/ppermute | solution.py:21
  (9 other events, 7.6 us)
